TPU v7x, 32 devices: a whole 2x2x4 slice. The times are simulated.
32 devices in a mesh: rows: 8 (over z, core), cols: 4 (over y, x).
Axes of the slice: x: 2, y: 2, z: 4, core: 2. Of those that a mesh axis runs over, the one named last changes fastest.
Arguments:
- jac: bfloat16 [2048, 1024], P(('rows', 'cols')), may hold values from -0.29882812 to 0.29882812
- panel_jac: bfloat16 [2048, 512], P(('rows', 'cols')), may hold values from -6 to 6
- weights: float32 [2048], P(('rows', 'cols')), may hold values from 0.1 to 1
- tile_lists: int32 [64, 4], P(('rows', 'cols')), may hold values from 0 to 95, as said below
- tile_masks: int32 [64, 4], P(('rows', 'cols')), may hold values from 0 to 1
- tile_order: int32 [96], replicated, may hold values from 0 to 95, as said below
- factor_inverse: float32 [512, 512], replicated, as said below
Outputs:
- panel_factor: float32 [96, 256, 512], P('cols', 'rows')
Inputs may be any that keep to these rules, and one draw needn't show every extreme that they name: `tile_order`: a permutation of 0 to 95. `tile_lists`: the 4 tiles of one row block are distinct; among the active slots of one device's 2 row blocks, at most 2 name tiles whose positions i share i // 24; in every draw every device has 2 such slots for one and the same position range. `factor_inverse`: lower triangular with a positive diagonal.
All inputs are finite; a program needn't handle non-finite values.
Results may differ from a plain program's by a relative error of at most 0.0029.
Values may be sent and summed in bfloat16 or wider, within the bound.
No kernel may reach another device: no remote copies, remote signals or barrier semaphores. Data moves between devices by JAX's collectives and lax.ppermute only.
A program may use at most 64 MiB of HBM per device.

v0:
```python
import jax
import jax.numpy as jnp
from jax import lax
from jax.sharding import PartitionSpec as P


def tile_positions(tile_lists, tile_order):
    tile_count = tile_order.shape[0]
    matches = tile_lists[:, :, None] == tile_order[None, None, :]
    return jnp.sum(jnp.where(matches, jnp.arange(tile_count, dtype=jnp.int32), 0), axis=2)


def apply_inverse(tiles, factor_inverse):
    return jnp.einsum("ntp,qp->ntq", tiles, factor_inverse, precision=lax.Precision.HIGHEST)


def local(jac, panel_jac, weights, tile_lists, tile_masks, tile_order, factor_inverse):
    block_count, slot_count = tile_lists.shape
    block_rows = jac.shape[0] // block_count
    tile_width = jac.shape[1] // slot_count
    panel_width = panel_jac.shape[1]
    owners = lax.axis_size("cols")
    per_owner = tile_order.shape[0] // owners
    positions = tile_positions(tile_lists, tile_order)
    weighted = (weights[:, None] * panel_jac).astype(jnp.bfloat16)
    first_place = lax.axis_index("cols") * per_owner
    jac_piece = lax.all_gather(jac, "cols", axis=0, tiled=True)
    weighted_piece = lax.all_gather(weighted, "cols", axis=0, tiled=True)
    place_piece = lax.all_gather(positions, "cols", axis=0, tiled=True)
    mask_piece = lax.all_gather(tile_masks, "cols", axis=0, tiled=True)
    blocks_here = place_piece.shape[0]
    local_place = place_piece - first_place
    chosen = (
        (local_place[:, :, None] == jnp.arange(per_owner, dtype=jnp.int32))
        & (mask_piece[:, :, None] == 1)
    ).astype(jnp.bfloat16)
    columns = jac_piece.reshape(blocks_here, block_rows, slot_count, tile_width)
    mixed_tiles = jnp.einsum(
        "bkn,brkt->brnt", chosen, columns, preferred_element_type=jnp.float32
    ).astype(jnp.bfloat16)
    panels = weighted_piece.reshape(blocks_here, block_rows, panel_width)
    gram_tiles = jnp.einsum(
        "brnt,brp->ntp", mixed_tiles, panels, preferred_element_type=jnp.float32
    )
    reduced = lax.psum_scatter(gram_tiles, "rows", scatter_dimension=1, tiled=True)
    return apply_inverse(reduced, factor_inverse)


def solution(mesh):
    in_specs = (
        P(("rows", "cols"), None),
        P(("rows", "cols"), None),
        P(("rows", "cols")),
        P(("rows", "cols"), None),
        P(("rows", "cols"), None),
        P(),
        P(),
    )
    out_specs = P("cols", "rows", None)
    return jax.shard_map(local, mesh=mesh, in_specs=in_specs, out_specs=out_specs, check_vma=False)
```

profile of v0, /device:TPU:0, one launch (start us, length us, event | category | flops | bytes accessed | tf_op | source)
XLA Modules:
  0.0 194.1 jit_solution(9528640244951013951)
XLA Ops:
  6.5 0.0 copy-start
  6.5 0.0 reduce-scatter.2.cloned.1.call-start
  6.5 1.0 select_reduce_fusion
  7.5 9.5 %all-gather = s32[4,2,4]{2,1,0:T(2,128)S(1)} all-gather(s32[1,2,4]{2,1,0:T(2,128)S(1)} %bitcast.27), channel_id=1, replica_groups=mesh['rows'=8,'cols'=4] {'cols'}, dimensions={0}, use_global_device_ids=true | all-gather | bytes 160 | tf_op jit(solution)/shard_map/all_gather | solution.py:29
  17.0 8.0 %all-gather.1 = s32[4,2,4]{2,1,0:T(2,128)S(1)} all-gather(s32[1,2,4]{2,1,0:T(2,128)} %bitcast.28), channel_id=1, replica_groups=mesh['rows'=8,'cols'=4] {'cols'}, dimensions={0}, use_global_device_ids=true | all-gather | bytes 160 | tf_op jit(solution)/shard_map/all_gather | solution.py:30
  25.1 0.9 multiply_convert_fusion
  26.0 8.1 %all_gather.15 = bf16[256,512]{1,0:T(8,128)(2,1)S(1)} all-gather(bf16[64,512]{1,0:T(8,128)(2,1)S(1)} %multiply_convert_fusion), channel_id=1, replica_groups=mesh['rows'=8,'cols'=4] {'cols'}, dimensions={0}, use_global_device_ids=true | all-gather | bytes 327680 | tf_op jit(solution)/shard_map/all_gather | solution.py:28
  34.2 9.9 %all_gather.14 = bf16[256,1024]{1,0:T(8,128)(2,1)S(1)} all-gather(bf16[64,1024]{1,0:T(8,128)(2,1)} %param.7), channel_id=1, replica_groups=mesh['rows'=8,'cols'=4] {'cols'}, dimensions={0}, use_global_device_ids=true | all-gather | bytes 655360 | tf_op jit(solution)/shard_map/all_gather | solution.py:27
  44.1 0.4 reshape.12
  44.5 1.5 convert_bitcast_fusion
  46.0 6.4 %convolution_bitcast_fusion = f32[24,256,512]{2,1,0:T(8,128)} fusion(bf16[8,32,512,1]{2,1,0,3:T(8,128)(2,1)S(1)} %bitcast.24, bf16[8,32,24,256]{3,2,1,0:T(8,128)(2,1)S(1)} %convert_bitcast_fusion), kind=kOutput, calls=%fused_computation | convolution fusion | flops 1610612736 | bytes 15990784 | tf_op jit(solution)/shard_map/brnt,brp->ntp/dot_general | solution.py:42
  52.4 0.0 reduce-scatter.2.cloned.1.call-update
  52.4 129.6 %reduce-scatter.2.cloned.1.call-done = f32[24,32,512]{2,1,0:T(8,128)} async-done(((f32[24,256,512]{2,1,0:T(8,128)}), f32[24,32,512]{2,1,0:T(8,128)}) %reduce-scatter.2.cloned.1.call-update) | async-done | bytes 1572880 | tf_op jit(solution)/shard_map/reduce_scatter | solution.py:45
  182.1 0.0 copy-done
  182.1 5.2 %fusion.1 = f32[24,32,512]{2,1,0:T(8,128)} fusion(f32[24,32,512]{2,1,0:T(8,128)} %reduce-scatter.2.cloned.1.call-done, f32[512,512]{1,0:T(8,128)S(1)} %copy-done), kind=kOutput, calls=%fused_computation.3 | convolution fusion | flops 2415919104 | bytes 4194304 | tf_op jit(solution)/shard_map/ntp,qp->ntq/dot_general | solution.py:14
  (4 shorter events, 0.0 us)
Async XLA Ops:
  6.5 175.5 %copy-start = (f32[512,512]{1,0:T(8,128)S(1)}, f32[512,512]{1,0:T(8,128)}, u32[]{:S(2)}) copy-start(f32[512,512]{1,0:T(8,128)} %param.13) | copy-start | bytes 3145732
  6.5 175.5 %reduce-scatter.2.cloned.1.call-start = ((), (), s32[]{:S(2)}) async-start(), calls=%async_computation.1 | async-start | bytes 14155776 | tf_op jit(solution)/shard_map/reduce_scatter | solution.py:45
Sparse Core Ops, SparseCore 0:
  52.5 129.4 reduce-scatter.1
where the time goes:
time: 194 us
  waiting for transfers between devices  130 us (67%)
  blocking collectives  35.6 us (18%)
  between operations  13.4 us (7%)
  matrix products  13.1 us (7%)
    reduce_scatter x1, waiting for transfers between devices, local(): lax.psum_scatter(gram_tiles, 'rows', scatter_dimension=1, tiled=True)  130 us
    all_gather x1, blocking collectives, local(): jac_piece = lax.all_gather(jac, 'cols', axis=0, tiled=True)  9.9 us
    all_gather x1, blocking collectives, local(): place_piece = lax.all_gather(positions, 'cols', axis=0, tiled=True)  9.52 us
    all_gather x1, blocking collectives, local(): weighted_piece = lax.all_gather(weighted, 'cols', axis=0, tiled=True)  8.14 us
    all_gather x1, blocking collectives, local(): mask_piece = lax.all_gather(tile_masks, 'cols', axis=0, tiled=True)  8.02 us
    dot_general x1, matrix products, local(): jnp.einsum('brnt,brp->ntp', mixed_tiles, panels, preferred_element_type=j...  6.43 us
    dot_general x1, matrix products, apply_inverse(): jnp.einsum('ntp,qp->ntq', tiles, factor_inverse, precision=lax.Precision....  5.21 us
  transfers between devices with their start and end apart: 1, of which 1 were waited for; matrix products, arithmetic and copies ran while one was open for 0% of the time, Pallas kernels for 0%

commit v1 on v0

v1 whole, which is shorter than its diff:
```python
import jax
import jax.numpy as jnp
from jax import lax
from jax.sharding import PartitionSpec as P

CAP = 2
GATHERED = 1 << 22


def tile_positions(tile_lists, tile_order):
    tile_count = tile_order.shape[0]
    matches = tile_lists[:, :, None] == tile_order[None, None, :]
    return jnp.sum(jnp.where(matches, jnp.arange(tile_count, dtype=jnp.int32), 0), axis=2)


def apply_inverse(tiles, factor_inverse):
    return jnp.einsum("ntp,qp->ntq", tiles, factor_inverse, precision=lax.Precision.HIGHEST)


def local(jac, panel_jac, weights, tile_lists, tile_masks, tile_order, factor_inverse):
    block_count, slot_count = tile_lists.shape
    block_rows = jac.shape[0] // block_count
    tile_width = jac.shape[1] // slot_count
    slabs, owners = lax.axis_size("rows"), lax.axis_size("cols")
    devices = slabs * owners
    per_owner = tile_order.shape[0] // owners
    slab_width = tile_width // slabs
    bf16 = jnp.bfloat16

    weighted = (weights[:, None] * panel_jac).astype(bf16)

    positions = tile_positions(tile_lists, tile_order).reshape(-1)
    active = tile_masks.reshape(-1) == 1
    owner = positions // per_owner
    same = (owner[:, None] == owner[None, :]) & active[None, :]
    earlier = jnp.tril(jnp.ones(same.shape, bool), -1)
    rank = jnp.sum(same & earlier, axis=1)
    code = (
        (owner[None, None, :] == jnp.arange(owners)[:, None, None])
        & (rank[None, None, :] == jnp.arange(CAP)[None, :, None])
        & active[None, None, :]
    )
    block = jnp.arange(block_count * slot_count) // slot_count
    place = positions % per_owner + per_owner * block
    places = jnp.sum(jnp.where(code, place + 1, 0), axis=2) - 1
    columns = jac.reshape(block_count, block_rows, slot_count, slabs, slab_width)
    chosen = code.astype(bf16).reshape(owners, CAP, block_count, slot_count)
    pieces = jnp.einsum("cjbk,bmkrt->rcjmt", chosen, columns, preferred_element_type=jnp.float32).astype(bf16)
    pieces = pieces.reshape(devices, -1)
    note = jnp.broadcast_to(places.astype(bf16)[None], (slabs, owners, CAP)).reshape(devices, CAP)
    note = jnp.pad(note, ((0, 0), (0, 128 - CAP)))
    sent = jnp.concatenate([pieces, note], axis=1)
    got = lax.all_to_all(sent, ("rows", "cols"), split_axis=0, concat_axis=0, tiled=True)
    size = pieces.shape[1]
    data = got[:, :size].reshape(devices, CAP, block_rows, slab_width)
    where = got[:, size : size + CAP].astype(jnp.int32)
    hot = (where[:, :, None] == jnp.arange(block_count * per_owner)).astype(bf16)
    hot = hot.reshape(devices, CAP, block_count, per_owner)
    mixed = jnp.einsum("djbn,djmt->dbmnt", hot, data, preferred_element_type=jnp.float32).astype(bf16)
    strips = max(1, devices * weighted.size * 2 // GATHERED)

    def strip_gram(strip):
        panels = lax.all_gather(strip, ("rows", "cols"), axis=0, tiled=True)
        panels = panels.reshape(devices, block_count, block_rows, -1)
        return jnp.einsum("dbmnt,dbmp->ntp", mixed, panels, preferred_element_type=jnp.float32)

    if strips == 1:
        gram = strip_gram(weighted)
    else:
        narrow = weighted.reshape(weighted.shape[0], strips, -1).swapaxes(0, 1)
        gram = jnp.moveaxis(lax.map(strip_gram, narrow), 0, 2)
        gram = gram.reshape(per_owner, slab_width, -1)
    return apply_inverse(gram, factor_inverse)


def solution(mesh):
    in_specs = (
        P(("rows", "cols"), None),
        P(("rows", "cols"), None),
        P(("rows", "cols")),
        P(("rows", "cols"), None),
        P(("rows", "cols"), None),
        P(),
        P(),
    )
    out_specs = P("cols", "rows", None)
    return jax.shard_map(local, mesh=mesh, in_specs=in_specs, out_specs=out_specs, check_vma=False)
```

time: 194 us -> 89.3 us (0.46)
  waiting for transfers between devices: 130 us -> 39.6 us
  blocking collectives: 35.6 us -> 0 us
  starting transfers between devices: 0.01 us -> 7.3 us
  matrix products: 13.1 us -> 19.8 us
  local copies, waits for them, and re-layouts: 0.41 us -> 4.48 us
  other arithmetic: 1.92 us -> 4.31 us
    reduce_scatter x1 -> x0, waiting for transfers between devices: 130 us -> none  [local(): lax.psum_scatter(gram_tiles, 'rows', scatter_dimension=1, tiled=True)]
    all_gather x4 -> x0, blocking collectives: 35.6 us -> none  [the longest x1 9.9 us: local(): jac_piece = lax.all_gather(jac, 'cols', axis=0, tiled=True)]
    all_gather x0 -> x1, waiting for transfers between devices: none -> 30.4 us  [strip_gram(): panels = lax.all_gather(strip, ('rows', 'cols'), axis=0, tiled=True)]
    all_to_all x0 -> x1, waiting for transfers between devices: none -> 9.12 us  [local(): lax.all_to_all(sent, ('rows', 'cols'), split_axis=0, concat_axis=0, tiled...]
    dot_general x2 -> x3, matrix products: 7.93 us -> 16 us  [the longest x1 8.84 us: strip_gram(): jnp.einsum('dbmnt,dbmp->ntp', mixed, panels, preferred_element_type=jnp.f...]
    all_to_all x0 -> x1, starting transfers between devices: none -> 7.3 us  [local(): lax.all_to_all(sent, ('rows', 'cols'), split_axis=0, concat_axis=0, tiled...]
  transfers between devices with their start and end apart: 1 -> 2, of which waited for: 1 -> 2; matrix products, arithmetic and copies ran while one was open for 0% -> 16% of each run, Pallas kernels for 0% -> 0%
where the time goes in v1:
time: 89.3 us; the launch traced here: 89 us
  waiting for transfers between devices  39.6 us (44%)
  matrix products  19.8 us (22%)
  between operations  13.5 us (15%)
  starting transfers between devices  7.3 us (8%)
  local copies, waits for them, and re-layouts  4.48 us (5%)
  other arithmetic  4.31 us (5%)
    all_gather x1, waiting for transfers between devices, strip_gram(): panels = lax.all_gather(strip, ('rows', 'cols'), axis=0, tiled=True)  30.4 us
    all_to_all x1, waiting for transfers between devices, local(): lax.all_to_all(sent, ('rows', 'cols'), split_axis=0, concat_axis=0, tiled...  9.12 us
    dot_general x1, matrix products, strip_gram(): jnp.einsum('dbmnt,dbmp->ntp', mixed, panels, preferred_element_type=jnp.f...  8.84 us
    all_to_all x1, starting transfers between devices, local(): lax.all_to_all(sent, ('rows', 'cols'), split_axis=0, concat_axis=0, tiled...  7.3 us
    dot_general x1, matrix products, local(): jnp.einsum('djbn,djmt->dbmnt', hot, data, preferred_element_type=jnp.floa...  6.55 us
    dot_general x1, matrix products, apply_inverse(): jnp.einsum('ntp,qp->ntq', tiles, factor_inverse, precision=lax.Precision....  3.8 us
  transfers between devices with their start and end apart: 2, of which 2 were waited for; matrix products, arithmetic and copies ran while one was open for 16% of the time, Pallas kernels for 0%

profile of v1, /device:TPU:0, one launch (start us, length us, event | category | flops | bytes accessed | tf_op | source)
XLA Modules:
  0.0 89.0 jit_solution(15316333741708227697)
XLA Ops:
  6.5 0.0 copy-start
  6.5 0.0 all-gather.2.cloned.1.call-start
  6.5 1.6 %multiply_convert_fusion = bf16[64,512]{1,0:T(8,128)(2,1)} fusion(bf16[64,512]{1,0:T(8,128)(2,1)} %param.8, f32[64]{0:T(128)} %param.9), kind=kLoop, calls=%fused_computation.19 | loop fusion | flops 98304 | bytes 131328 | tf_op jit(solution)/shard_map/convert_element_type | solution.py:30
  8.2 0.0 all-gather.2.cloned.1.call-update
  8.2 0.7 broadcast_compare_fusion
  8.9 0.1 eq.125
  9.0 0.9 %select_reduce_fusion.1 = s32[2,4]{1,0:T(2,128)S(1)} fusion(s32[96]{0:T(128)} %param.12, s32[2,4]{1,0:T(2,128)} %param.10), kind=kLoop, calls=%fused_computation.32 | loop fusion | flops 2296 | bytes 448 | tf_op jit(solution)/shard_map/reduce_sum | solution.py:13
  9.9 0.1 ne.61
  10.0 0.1 div.29
  10.1 0.1 rem.38
  10.2 0.2 convert_reduce_fusion
  10.3 0.1 eq.126
  10.4 0.1 select_reduce_fusion
  10.6 0.1 copy.41
  10.7 1.3 %reshape.166 = bf16[2,32,4,8,32]{4,3,2,1,0:T(8,128)(2,1)S(1)} reshape(bf16[64,1024]{1,0:T(8,128)(2,1)} %param.7) | data formatting | bytes 262144 | tf_op jit(solution)/shard_map/reshape | solution.py:46
  12.0 0.6 fusion.7
  12.7 0.2 copy.26
  12.9 0.5 reshape.167
  13.5 0.5 broadcast.172
  14.0 0.7 reduce
  14.7 0.8 reshape.179
  15.5 7.3 %all-to-all-start = ((bf16[32,2,1088]{2,1,0:T(2,128)(2,1)}), bf16[32,2,1088]{2,1,0:T(2,128)(2,1)S(1)}, u32[]{:S(2)}, u32[]{:S(2)}) async-start(bf16[32,2,1088]{2,1,0:T(2,128)(2,1)} %reshape.179), calls=%async_computation | async-start | bytes 294912 | tf_op jit(solution)/shard_map/all_to_all | solution.py:53
  22.8 9.1 %all-to-all-done = bf16[32,2,1088]{2,1,0:T(2,128)(2,1)S(1)} async-done(((bf16[32,2,1088]{2,1,0:T(2,128)(2,1)}), bf16[32,2,1088]{2,1,0:T(2,128)(2,1)S(1)}, u32[]{:S(2)}, u32[]{:S(2)}) %all-to-all-start) | async-done | bytes 139296 | tf_op jit(solution)/shard_map/all_to_all | solution.py:53
  32.0 0.2 reshape.180
  32.2 0.4 reshape.169
  32.5 6.5 %convert_bitcast_fusion = bf16[32,2,32,24,32]{4,3,1,2,0:T(8,128)(2,1)} fusion(bf16[32,2,32,32,1]{3,2,1,0,4:T(8,128)(2,1)S(1)} %bitcast.45, s32[2,24]{1,0:T(2,128)S(1)} %multiply_add_fusion, s32[32,2]{1,0:T(8,128)S(1)} %slice_convert_fusion), kind=kOutput, calls=%fused_computation.2 | convolution fusion | flops 7867392 | bytes 3277248 | tf_op jit(solution)/shard_map/djbn,djmt->dbmnt/dot_general | solution.py:59
  39.1 30.4 %all-gather.2.cloned.1.call-done = bf16[2048,512]{1,0:T(8,128)(2,1)} async-done(((bf16[64,512]{1,0:T(8,128)(2,1)}), bf16[2048,512]{1,0:T(8,128)(2,1)}) %all-gather.2.cloned.1.call-update) | async-done | bytes 2097168 | tf_op jit(solution)/shard_map/all_gather | solution.py:63
  69.5 8.8 %fusion = f32[24,32,512,1,1]{2,1,4,3,0:T(8,128)S(1)} fusion(bf16[32,2,32,24,32]{4,3,1,2,0:T(8,128)(2,1)} %convert_bitcast_fusion, bf16[32,2,32,512]{3,2,1,0:T(8,128)(2,1)} %bitcast.49), kind=kOutput, calls=%fused_computation | convolution fusion | flops 1610612736 | bytes 6815744 | tf_op jit(solution)/shard_map/dbmnt,dbmp->ntp/dot_general | solution.py:65
  78.4 0.0 copy-done
  78.4 3.8 %fusion.4 = f32[24,32,512]{2,1,0:T(8,128)} fusion(f32[24,32,512,1,1]{2,1,4,3,0:T(8,128)S(1)} %fusion, f32[512,512]{1,0:T(8,128)S(1)} %copy-done), kind=kOutput, calls=%fused_computation.5 | convolution fusion | flops 2415919104 | bytes 4194304 | tf_op jit(solution)/shard_map/ntp,qp->ntq/dot_general | solution.py:17
  (13 shorter events, 0.1 us)
Async XLA Ops:
  6.5 71.8 %copy-start = (f32[512,512]{1,0:T(8,128)S(1)}, f32[512,512]{1,0:T(8,128)}, u32[]{:S(2)}) copy-start(f32[512,512]{1,0:T(8,128)} %param.13) | copy-start | bytes 3145732
  6.5 63.0 %all-gather.2.cloned.1.call-start = ((), (), s32[]{:S(2)}) async-start(), calls=%async_computation.1 | async-start | bytes 2162688 | tf_op jit(solution)/shard_map/all_gather | solution.py:63
  15.5 16.4 %all-to-all-start = ((bf16[32,2,1088]{2,1,0:T(2,128)(2,1)}), bf16[32,2,1088]{2,1,0:T(2,128)(2,1)S(1)}, u32[]{:S(2)}, u32[]{:S(2)}) async-start(bf16[32,2,1088]{2,1,0:T(2,128)(2,1)} %reshape.179), calls=%async_computation | async-start | bytes 294912 | tf_op jit(solution)/shard_map/all_to_all | solution.py:53
Sparse Core Ops, SparseCore 0:
  10.2 59.2 all-gather.1

commit v2 on v1

--- a/solution.py
+++ b/solution.py
@@ -17,7 +17,26 @@
     return jnp.einsum("ntp,qp->ntq", tiles, factor_inverse, precision=lax.Precision.HIGHEST)
 
 
-def local(jac, panel_jac, weights, tile_lists, tile_masks, tile_order, factor_inverse):
+def slot_codes(tile_lists, tile_masks, tile_order, owner_ids):
+    block_count, slot_count = tile_lists.shape
+    per_owner = tile_order.shape[0] // lax.axis_size("cols")
+    positions = tile_positions(tile_lists, tile_order).reshape(-1)
+    active = tile_masks.reshape(-1) == 1
+    owner = positions // per_owner
+    same = (owner[:, None] == owner[None, :]) & active[None, :]
+    earlier = jnp.tril(jnp.ones(same.shape, bool), -1)
+    rank = jnp.sum(same & earlier, axis=1)
+    code = (
+        (owner[None, None, :] == owner_ids[:, None, None])
+        & (rank[None, None, :] == jnp.arange(CAP)[None, :, None])
+        & active[None, None, :]
+    )
+    block = jnp.arange(block_count * slot_count) // slot_count
+    place = positions % per_owner + per_owner * block
+    return code, jnp.sum(jnp.where(code, place + 1, 0), axis=2) - 1
+
+
+def local_general(jac, panel_jac, weights, tile_lists, tile_masks, tile_order, factor_inverse):
     block_count, slot_count = tile_lists.shape
     block_rows = jac.shape[0] // block_count
     tile_width = jac.shape[1] // slot_count
@@ -26,23 +45,8 @@
     per_owner = tile_order.shape[0] // owners
     slab_width = tile_width // slabs
     bf16 = jnp.bfloat16
-
     weighted = (weights[:, None] * panel_jac).astype(bf16)
-
-    positions = tile_positions(tile_lists, tile_order).reshape(-1)
-    active = tile_masks.reshape(-1) == 1
-    owner = positions // per_owner
-    same = (owner[:, None] == owner[None, :]) & active[None, :]
-    earlier = jnp.tril(jnp.ones(same.shape, bool), -1)
-    rank = jnp.sum(same & earlier, axis=1)
-    code = (
-        (owner[None, None, :] == jnp.arange(owners)[:, None, None])
-        & (rank[None, None, :] == jnp.arange(CAP)[None, :, None])
-        & active[None, None, :]
-    )
-    block = jnp.arange(block_count * slot_count) // slot_count
-    place = positions % per_owner + per_owner * block
-    places = jnp.sum(jnp.where(code, place + 1, 0), axis=2) - 1
+    code, places = slot_codes(tile_lists, tile_masks, tile_order, jnp.arange(owners))
     columns = jac.reshape(block_count, block_rows, slot_count, slabs, slab_width)
     chosen = code.astype(bf16).reshape(owners, CAP, block_count, slot_count)
     pieces = jnp.einsum("cjbk,bmkrt->rcjmt", chosen, columns, preferred_element_type=jnp.float32).astype(bf16)
@@ -73,6 +77,64 @@
     return apply_inverse(gram, factor_inverse)
 
 
+def shift(value, steps_z, flip_cols, flip_core=0):
+    slabs, owners = lax.axis_size("rows"), lax.axis_size("cols")
+    pairs = []
+    for r in range(slabs):
+        to_r = ((r // 2 + steps_z) % (slabs // 2)) * 2 + ((r % 2) ^ flip_core)
+        for c in range(owners):
+            pairs.append((r * owners + c, to_r * owners + (c ^ flip_cols)))
+    return lax.ppermute(value, ("rows", "cols"), pairs)
+
+
+def local(jac, panel_jac, weights, tile_lists, tile_masks, tile_order, factor_inverse):
+    block_count, slot_count = tile_lists.shape
+    block_rows = jac.shape[0] // block_count
+    tile_width = jac.shape[1] // slot_count
+    slabs, owners = lax.axis_size("rows"), lax.axis_size("cols")
+    layers = slabs // 2
+    per_owner = tile_order.shape[0] // owners
+    slab_width = tile_width // slabs
+    bf16 = jnp.bfloat16
+    weighted = (weights[:, None] * panel_jac).astype(bf16)
+
+    lines = [weighted] + [shift(weighted, k, 0) for k in range(1, layers)]
+    by_x = [shift(w, 0, 1) for w in lines]
+    by_y = [shift(w, 0, 2) for w in lines]
+    half = layers // 2
+    across = [shift(w, 0, 2) for w in by_x[:half]] + [shift(w, 0, 1) for w in by_y[half:]]
+
+    me_r, me_c = lax.axis_index("rows"), lax.axis_index("cols")
+    me_z, me_core = me_r // 2, me_r % 2
+    code, places = slot_codes(tile_lists, tile_masks, tile_order, me_c ^ jnp.arange(owners))
+    columns = jac.reshape(block_count, block_rows, slot_count, layers, 2, slab_width)
+    columns = jnp.take(columns, (me_z + jnp.arange(layers)) % layers, axis=3)
+    columns = jnp.take(columns, me_core ^ jnp.arange(2), axis=4)
+    chosen = code.astype(bf16).reshape(owners, CAP, block_count, slot_count)
+    pieces = jnp.einsum("ejbk,bmkzut->zemjut", chosen, columns, preferred_element_type=jnp.float32).astype(bf16)
+    pieces = pieces.reshape(layers, owners, block_rows, -1)
+    note = jnp.pad(places.astype(bf16), ((0, 0), (0, pieces.shape[3] - CAP)))
+    note = jnp.broadcast_to(note[None, :, None], (layers, owners, 1, pieces.shape[3]))
+    sent = jnp.concatenate([pieces, note], axis=2)
+    got = [
+        [sent[k, e] if k == e == 0 else shift(sent[k, e], k, e) for e in range(owners)]
+        for k in range(layers)
+    ]
+
+    panels = jnp.stack([w for group in (lines, by_x, by_y, across) for w in group])
+    got = jnp.stack([got[k][e] for e in range(owners) for k in range(layers)])
+    sources = layers * owners
+    panels = panels.reshape(sources, block_count, block_rows, -1)
+    data = got[:, :block_rows].reshape(sources, block_rows, CAP, 2, slab_width)
+    where = got[:, block_rows, :CAP].astype(jnp.int32)
+    hot = (where[:, :, None] == jnp.arange(block_count * per_owner)).astype(bf16)
+    hot = hot.reshape(sources, CAP, block_count, per_owner)
+    mixed = jnp.einsum("djbn,dmjut->dbmunt", hot, data, preferred_element_type=jnp.float32).astype(bf16)
+    gram = jnp.einsum("dbmunt,dbmp->untp", mixed, panels, preferred_element_type=jnp.float32)
+    other = shift(gram[1].astype(bf16), 0, 0, 1)
+    return apply_inverse(gram[0] + other.astype(jnp.float32), factor_inverse)
+
+
 def solution(mesh):
     in_specs = (
         P(("rows", "cols"), None),
@@ -84,4 +146,5 @@
         P(),
     )
     out_specs = P("cols", "rows", None)
-    return jax.shard_map(local, mesh=mesh, in_specs=in_specs, out_specs=out_specs, check_vma=False)
+    body = local if (mesh.shape["rows"], mesh.shape["cols"]) == (8, 4) else local_general
+    return jax.shard_map(body, mesh=mesh, in_specs=in_specs, out_specs=out_specs, check_vma=False)

time: 89.3 us -> 116 us (1.30)
  local copies, waits for them, and re-layouts: 4.48 us -> 45 us
  starting transfers between devices: 7.3 us -> 43.4 us
  waiting for transfers between devices: 39.6 us -> 8.01 us
  between operations: 13.5 us -> 0.33 us
  matrix products: 19.8 us -> 14.6 us
    ppermute x0 -> x31, starting transfers between devices: none -> 43.4 us  [shift(): return lax.ppermute(value, ('rows', 'cols'), pairs)]
    another operation x0 -> x18, local copies, waits for them, and re-layouts: none -> 36.9 us  [the longest x17 36.9 us: local(): got = jnp.stack([got[k][e] for e in range(owners) for k in range(layers)])]
    all_gather x1 -> x0, waiting for transfers between devices: 30.4 us -> none  [strip_gram(): panels = lax.all_gather(strip, ('rows', 'cols'), axis=0, tiled=True)]
    all_to_all x1 -> x0, waiting for transfers between devices: 9.12 us -> none  [local(): lax.all_to_all(sent, ('rows', 'cols'), split_axis=0, concat_axis=0, tiled...]
    ppermute x0 -> x31, waiting for transfers between devices: none -> 8.01 us  [shift(): return lax.ppermute(value, ('rows', 'cols'), pairs)]
    all_to_all x1 -> x0, starting transfers between devices: 7.3 us -> none  [local(): lax.all_to_all(sent, ('rows', 'cols'), split_axis=0, concat_axis=0, tiled...]
    dot_general x3, matrix products: 16 us -> 10.8 us  [the longest x1 6.14 us: local(): jnp.einsum('dbmunt,dbmp->untp', mixed, panels, preferred_element_type=jnp...]
    convert_element_type x1, other arithmetic: 1.62 us -> 0.08 us  [local(): weighted = (weights[:, None] * panel_jac).astype(bf16)]
  transfers between devices with their start and end apart: 2 -> 31, of which waited for: 2 -> 7; matrix products, arithmetic and copies ran while one was open for 16% -> 40% of each run, Pallas kernels for 0% -> 0%
where the time goes in v2:
time: 116 us; the launch traced here: 115 us
  local copies, waits for them, and re-layouts  45 us (39%)
  starting transfers between devices  43.4 us (37%)
  matrix products  14.6 us (13%)
  waiting for transfers between devices  8.01 us (7%)
  other arithmetic  3.79 us (3%)
    ppermute x31, starting transfers between devices, shift(): return lax.ppermute(value, ('rows', 'cols'), pairs)  43.4 us
    another operation x17, local copies, waits for them, and re-layouts, local(): got = jnp.stack([got[k][e] for e in range(owners) for k in range(layers)])  36.9 us
    ppermute x31, waiting for transfers between devices, shift(): return lax.ppermute(value, ('rows', 'cols'), pairs)  8.01 us
    dot_general x1, matrix products, local(): jnp.einsum('dbmunt,dbmp->untp', mixed, panels, preferred_element_type=jnp...  6.14 us
    dot_general x1, matrix products, local(): jnp.einsum('djbn,dmjut->dbmunt', hot, data, preferred_element_type=jnp.fl...  3.99 us
    dot_general x1, matrix products, apply_inverse(): jnp.einsum('ntp,qp->ntq', tiles, factor_inverse, precision=lax.Precision....  3.84 us
  transfers between devices with their start and end apart: 31, of which 7 were waited for; matrix products, arithmetic and copies ran while one was open for 40% of the time, Pallas kernels for 0%

profile of v2, /device:TPU:0, one launch (start us, length us, event | category | flops | bytes accessed | tf_op | source)
XLA Modules:
  0.0 115.2 jit_solution(8886573673283226255)
XLA Ops:
  7.4 3.0 %collective-permute-start.7 = (bf16[33,128]{1,0:T(8,128)(2,1)S(1)}, bf16[33,128]{1,0:T(8,128)(2,1)S(1)}, u32[]{:S(2)}, u32[]{:S(2)}) collective-permute-start(bf16[33,128]{1,0:T(8,128)(2,1)S(1)} %get-tuple-element.18), channel_id=1, source_target_pairs={{0,2},{1,3},{2,0},{3,1},{4,6},{5,7},{6,4},{7,5},{8,10},{9,11},{10,... | collective-permute-start | bytes 25352 | tf_op jit(solution)/shard_map/ppermute | solution.py:87
  10.5 1.5 %collective-permute-start.8 = (bf16[33,128]{1,0:T(8,128)(2,1)S(1)}, bf16[33,128]{1,0:T(8,128)(2,1)S(1)}, u32[]{:S(2)}, u32[]{:S(2)}) collective-permute-start(bf16[33,128]{1,0:T(8,128)(2,1)S(1)} %get-tuple-element.19), channel_id=1, source_target_pairs={{0,10},{1,11},{2,8},{3,9},{4,14},{5,15},{6,12},{7,13},{8,18},{9,19... | collective-permute-start | bytes 25352 | tf_op jit(solution)/shard_map/ppermute | solution.py:87
  12.0 3.5 %collective-permute-start.9 = (bf16[33,128]{1,0:T(8,128)(2,1)S(1)}, bf16[33,128]{1,0:T(8,128)(2,1)S(1)}, u32[]{:S(2)}, u32[]{:S(2)}) collective-permute-start(bf16[33,128]{1,0:T(8,128)(2,1)S(1)} %get-tuple-element.20), channel_id=1, source_target_pairs={{0,18},{1,19},{2,16},{3,17},{4,22},{5,23},{6,20},{7,21},{8,26},{9,... | collective-permute-start | bytes 25352 | tf_op jit(solution)/shard_map/ppermute | solution.py:87
  16.8 2.4 %collective-permute-start.11 = (bf16[33,128]{1,0:T(8,128)(2,1)S(1)}, bf16[33,128]{1,0:T(8,128)(2,1)S(1)}, u32[]{:S(2)}, u32[]{:S(2)}) collective-permute-start(bf16[33,128]{1,0:T(8,128)(2,1)S(1)} %get-tuple-element.22), channel_id=1, source_target_pairs={{0,3},{1,2},{2,1},{3,0},{4,7},{5,6},{6,5},{7,4},{8,11},{9,10},{10,... | collective-permute-start | bytes 25352 | tf_op jit(solution)/shard_map/ppermute | solution.py:87
  20.6 2.2 %collective-permute-start.13 = (bf16[33,128]{1,0:T(8,128)(2,1)S(1)}, bf16[33,128]{1,0:T(8,128)(2,1)S(1)}, u32[]{:S(2)}, u32[]{:S(2)}) collective-permute-start(bf16[33,128]{1,0:T(8,128)(2,1)S(1)} %get-tuple-element.17), channel_id=1, source_target_pairs={{0,19},{1,18},{2,17},{3,16},{4,23},{5,22},{6,21},{7,20},{8,27},{9,... | collective-permute-start | bytes 25352 | tf_op jit(solution)/shard_map/ppermute | solution.py:87
  22.8 3.4 %collective-permute-start = (bf16[33,128]{1,0:T(8,128)(2,1)S(1)}, bf16[33,128]{1,0:T(8,128)(2,1)S(1)}, u32[]{:S(2)}, u32[]{:S(2)}) collective-permute-start(bf16[33,128]{1,0:T(8,128)(2,1)S(1)} %get-tuple-element.10), channel_id=1, source_target_pairs={{0,8},{1,9},{2,10},{3,11},{4,12},{5,13},{6,14},{7,15},{8,16},{9,17... | collective-permute-start | bytes 25352 | tf_op jit(solution)/shard_map/ppermute | solution.py:87
  26.2 2.4 %collective-permute-start.2 = (bf16[33,128]{1,0:T(8,128)(2,1)S(1)}, bf16[33,128]{1,0:T(8,128)(2,1)S(1)}, u32[]{:S(2)}, u32[]{:S(2)}) collective-permute-start(bf16[33,128]{1,0:T(8,128)(2,1)S(1)} %get-tuple-element.12), channel_id=1, source_target_pairs={{0,24},{1,25},{2,26},{3,27},{4,28},{5,29},{6,30},{7,31},{8,0},{9,1... | collective-permute-start | bytes 25352 | tf_op jit(solution)/shard_map/ppermute | solution.py:87
  30.3 2.8 %collective-permute-start.5 = (bf16[33,128]{1,0:T(8,128)(2,1)S(1)}, bf16[33,128]{1,0:T(8,128)(2,1)S(1)}, u32[]{:S(2)}, u32[]{:S(2)}) collective-permute-start(bf16[33,128]{1,0:T(8,128)(2,1)S(1)} %get-tuple-element.15), channel_id=1, source_target_pairs={{0,17},{1,16},{2,19},{3,18},{4,21},{5,20},{6,23},{7,22},{8,25},{9,... | collective-permute-start | bytes 25352 | tf_op jit(solution)/shard_map/ppermute | solution.py:87
  33.2 1.8 %collective-permute-start.6 = (bf16[33,128]{1,0:T(8,128)(2,1)S(1)}, bf16[33,128]{1,0:T(8,128)(2,1)}, u32[]{:S(2)}, u32[]{:S(2)}) collective-permute-start(bf16[33,128]{1,0:T(8,128)(2,1)S(1)} %get-tuple-element.16), channel_id=1, source_target_pairs={{0,25},{1,24},{2,27},{3,26},{4,29},{5,28},{6,31},{7,30},{8,1},{9,0... | collective-permute-start | bytes 25352 | tf_op jit(solution)/shard_map/ppermute | solution.py:87
  37.2 1.4 %copy.476 = bf16[1,33,128]{0,2,1:T(8,128)(2,1)} copy(bf16[1,33,128]{2,1,0:T(8,128)(2,1)S(1)} %bitcast.139) | data formatting | bytes 16896 | tf_op jit(solution)/shard_map/stack | solution.py:125
  38.7 1.5 %copy.477 = bf16[1,33,128]{0,2,1:T(8,128)(2,1)} copy(bf16[1,33,128]{2,1,0:T(8,128)(2,1)S(1)} %bitcast.140) | data formatting | bytes 16896 | tf_op jit(solution)/shard_map/stack | solution.py:125
  40.2 1.4 %copy.478 = bf16[1,33,128]{0,2,1:T(8,128)(2,1)} copy(bf16[1,33,128]{2,1,0:T(8,128)(2,1)S(1)} %bitcast.141) | data formatting | bytes 16896 | tf_op jit(solution)/shard_map/stack | solution.py:125
  41.6 1.4 %copy.479 = bf16[1,33,128]{0,2,1:T(8,128)(2,1)} copy(bf16[1,33,128]{2,1,0:T(8,128)(2,1)S(1)} %bitcast.142) | data formatting | bytes 16896 | tf_op jit(solution)/shard_map/stack | solution.py:125
  44.4 1.5 %copy.481 = bf16[1,33,128]{0,2,1:T(8,128)(2,1)} copy(bf16[1,33,128]{2,1,0:T(8,128)(2,1)S(1)} %bitcast.144) | data formatting | bytes 16896 | tf_op jit(solution)/shard_map/stack | solution.py:125
  45.9 1.4 %copy.468 = bf16[1,33,128]{0,2,1:T(8,128)(2,1)} copy(bf16[1,33,128]{2,1,0:T(8,128)(2,1)S(1)} %bitcast.145) | data formatting | bytes 16896 | tf_op jit(solution)/shard_map/stack | solution.py:125
  47.3 1.4 %copy.469 = bf16[1,33,128]{0,2,1:T(8,128)(2,1)} copy(bf16[1,33,128]{2,1,0:T(8,128)(2,1)S(1)} %bitcast.147) | data formatting | bytes 16896 | tf_op jit(solution)/shard_map/stack | solution.py:125
  50.1 1.5 %collective-permute-start.15 = (bf16[64,512]{1,0:T(8,128)(2,1)S(1)}, bf16[64,512]{1,0:T(8,128)(2,1)S(1)}, u32[]{:S(2)}, u32[]{:S(2)}) collective-permute-start(bf16[64,512]{1,0:T(8,128)(2,1)S(1)} %multiply_convert_fusion), channel_id=1, source_target_pairs={{0,8},{1,9},{2,10},{3,11},{4,12},{5,13},{6,14},{7,15},{8,16},{9,17... | collective-permute-start | bytes 196616 | tf_op jit(solution)/shard_map/ppermute | solution.py:87
  51.6 1.4 %copy.471 = bf16[1,33,128]{0,2,1:T(8,128)(2,1)} copy(bf16[1,33,128]{2,1,0:T(8,128)(2,1)S(1)} %bitcast.150) | data formatting | bytes 16896 | tf_op jit(solution)/shard_map/stack | solution.py:125
  53.0 1.9 %collective-permute-start.16 = (bf16[64,512]{1,0:T(8,128)(2,1)S(1)}, bf16[64,512]{1,0:T(8,128)(2,1)S(1)}, u32[]{:S(2)}, u32[]{:S(2)}) collective-permute-start(bf16[64,512]{1,0:T(8,128)(2,1)S(1)} %multiply_convert_fusion), channel_id=1, source_target_pairs={{0,16},{1,17},{2,18},{3,19},{4,20},{5,21},{6,22},{7,23},{8,24},{9,... | collective-permute-start | bytes 196616 | tf_op jit(solution)/shard_map/ppermute | solution.py:87
  55.0 1.4 %copy.472 = bf16[1,33,128]{0,2,1:T(8,128)(2,1)} copy(bf16[1,33,128]{2,1,0:T(8,128)(2,1)S(1)} %bitcast.149) | data formatting | bytes 16896 | tf_op jit(solution)/shard_map/stack | solution.py:125
  57.5 1.5 %copy.473 = bf16[1,33,128]{0,2,1:T(8,128)(2,1)} copy(bf16[1,33,128]{2,1,0:T(8,128)(2,1)S(1)} %bitcast.148) | data formatting | bytes 16896 | tf_op jit(solution)/shard_map/stack | solution.py:125
  59.0 1.5 %collective-permute-start.18 = (bf16[64,512]{1,0:T(8,128)(2,1)S(1)}, bf16[64,512]{1,0:T(8,128)(2,1)S(1)}, u32[]{:S(2)}, u32[]{:S(2)}) collective-permute-start(bf16[64,512]{1,0:T(8,128)(2,1)S(1)} %multiply_convert_fusion), channel_id=1, source_target_pairs={{0,1},{1,0},{2,3},{3,2},{4,5},{5,4},{6,7},{7,6},{8,9},{9,8},{10,11... | collective-permute-start | bytes 196616 | tf_op jit(solution)/shard_map/ppermute | solution.py:87
  60.4 2.1 %copy.474 = bf16[1,33,128]{0,2,1:T(8,128)(2,1)} copy(bf16[1,33,128]{2,1,0:T(8,128)(2,1)} %bitcast.24) | data formatting | bytes 16896 | tf_op jit(solution)/shard_map/stack | solution.py:125
  62.6 1.5 %collective-permute-start.22 = (bf16[64,512]{1,0:T(8,128)(2,1)S(1)}, bf16[64,512]{1,0:T(8,128)(2,1)}, u32[]{:S(2)}, u32[]{:S(2)}) collective-permute-start(bf16[64,512]{1,0:T(8,128)(2,1)S(1)} %multiply_convert_fusion), channel_id=1, source_target_pairs={{0,2},{1,3},{2,0},{3,1},{4,6},{5,7},{6,4},{7,5},{8,10},{9,11},{10,... | collective-permute-start | bytes 196616 | tf_op jit(solution)/shard_map/ppermute | solution.py:87
  64.1 1.4 %copy.482 = bf16[1,33,128]{0,2,1:T(8,128)(2,1)} copy(bf16[1,33,128]{2,1,0:T(8,128)(2,1)S(1)} %bitcast.146) | data formatting | bytes 16896 | tf_op jit(solution)/shard_map/stack | solution.py:125
  65.5 14.8 %stack.114 = bf16[16,33,128]{0,2,1:T(8,128)(2,1)} concatenate(bf16[1,33,128]{0,2,1:T(8,128)(2,1)S(1)} %copy.467, bf16[1,33,128]{0,2,1:T(8,128)(2,1)} %copy.468, bf16[1,33,128]{0,2,1:T(8,128)(2,1)} %copy.469, bf16[1,33,128]{0,2,1:T(8,128)(2,1)} %copy.470, bf16[1,33,128]{0,2,1:T(8,128)(2,1)} %copy.471, bf16[1,33,128]{0,2,1:T(8,128)(2,1)} %copy.472, bf16[1,33,128]{0,2,1:T(8,128)(2,1)} %copy.473, ...), dimensions={0} | concatenate | bytes 270336 | tf_op jit(solution)/shard_map/stack | solution.py:125
  83.4 4.0 %convert_bitcast_fusion = bf16[16,2,32,2,24,32]{5,4,1,3,2,0:T(8,128)(2,1)S(1)} fusion(bf16[16,32,2,2,32,1]{4,2,5,3,1,0:T(2,128)(2,1)S(1)} %copy.490, s32[2,24]{1,0:T(2,128)S(1)} %multiply_add_fusion, s32[16,2]{1,0:T(8,128)S(1)} %copy.484), kind=kOutput, calls=%fused_computation.4 | convolution fusion | flops 7865856 | bytes 3277120 | tf_op jit(solution)/shard_map/djbn,dmjut->dbmunt/dot_general | solution.py:132
  88.0 1.6 %collective-permute-start.20 = (bf16[64,512]{1,0:T(8,128)(2,1)S(1)}, bf16[64,512]{1,0:T(8,128)(2,1)S(1)}, u32[]{:S(2)}, u32[]{:S(2)}) collective-permute-start(bf16[64,512]{1,0:T(8,128)(2,1)S(1)} %collective-permute-done.16), channel_id=1, source_target_pairs={{0,1},{1,0},{2,3},{3,2},{4,5},{5,4},{6,7},{7,6},{8,9},{9,8},{10,11... | collective-permute-start | bytes 196616 | tf_op jit(solution)/shard_map/ppermute | solution.py:87
  99.8 2.0 %collective-permute-done.28 = bf16[64,512]{1,0:T(8,128)(2,1)S(1)} collective-permute-done((bf16[64,512]{1,0:T(8,128)(2,1)S(1)}, bf16[64,512]{1,0:T(8,128)(2,1)S(1)}, u32[]{:S(2)}, u32[]{:S(2)}) %collective-permute-start.28) | collective-permute-done | bytes 65568 | tf_op jit(solution)/shard_map/ppermute | solution.py:87
  102.7 6.1 %fusion.2 = f32[2,24,32,512]{3,2,1,0:T(8,128)S(1)} fusion(bf16[16,2,32,2,24,32]{5,4,1,3,2,0:T(8,128)(2,1)S(1)} %convert_bitcast_fusion, bf16[16,2,32,512]{3,2,0,1:T(8,128)(2,1)S(1)} %constant_dynamic-update-slice_fusion), kind=kOutput, calls=%fused_computation.5 | convolution fusion | flops 1610612736 | bytes 7340032 | tf_op jit(solution)/shard_map/dbmunt,dbmp->untp/dot_general | solution.py:133
  109.0 2.3 %collective-permute-done.30 = bf16[24,32,512]{2,1,0:T(8,128)(2,1)S(1)} collective-permute-done((bf16[24,32,512]{2,1,0:T(8,128)(2,1)S(1)}, bf16[24,32,512]{2,1,0:T(8,128)(2,1)S(1)}, u32[]{:S(2)}, u32[]{:S(2)}) %collective-permute-start.30) | collective-permute-done | bytes 786464 | tf_op jit(solution)/shard_map/ppermute | solution.py:87
  111.3 3.8 %fusion.6 = f32[24,32,512]{2,1,0:T(8,128)} fusion(f32[2,24,32,512]{3,2,1,0:T(8,128)S(1)} %fusion.2, bf16[24,32,512]{2,1,0:T(8,128)(2,1)S(1)} %collective-permute-done.30, f32[512,512]{1,0:T(8,128)S(1)} %copy-done), kind=kOutput, calls=%fused_computation.9 | convolution fusion | flops 2416705536 | bytes 4980736 | tf_op jit(solution)/shard_map/ntp,qp->ntq/dot_general | solution.py:17
  (118 shorter events, 32.6 us)
Async XLA Ops:
  0.0 111.3 %copy-start = (f32[512,512]{1,0:T(8,128)S(1)}, f32[512,512]{1,0:T(8,128)}, u32[]{:S(2)}) copy-start(f32[512,512]{1,0:T(8,128)} %param.13) | copy-start | bytes 3145732
  7.4 12.5 %collective-permute-start.7 = (bf16[33,128]{1,0:T(8,128)(2,1)S(1)}, bf16[33,128]{1,0:T(8,128)(2,1)S(1)}, u32[]{:S(2)}, u32[]{:S(2)}) collective-permute-start(bf16[33,128]{1,0:T(8,128)(2,1)S(1)} %get-tuple-element.18), channel_id=1, source_target_pairs={{0,2},{1,3},{2,0},{3,1},{4,6},{5,7},{6,4},{7,5},{8,10},{9,11},{10,... | collective-permute-start | bytes 25352 | tf_op jit(solution)/shard_map/ppermute | solution.py:87
  10.5 10.1 %collective-permute-start.8 = (bf16[33,128]{1,0:T(8,128)(2,1)S(1)}, bf16[33,128]{1,0:T(8,128)(2,1)S(1)}, u32[]{:S(2)}, u32[]{:S(2)}) collective-permute-start(bf16[33,128]{1,0:T(8,128)(2,1)S(1)} %get-tuple-element.19), channel_id=1, source_target_pairs={{0,10},{1,11},{2,8},{3,9},{4,14},{5,15},{6,12},{7,13},{8,18},{9,19... | collective-permute-start | bytes 25352 | tf_op jit(solution)/shard_map/ppermute | solution.py:87
  12.0 10.8 %collective-permute-start.9 = (bf16[33,128]{1,0:T(8,128)(2,1)S(1)}, bf16[33,128]{1,0:T(8,128)(2,1)S(1)}, u32[]{:S(2)}, u32[]{:S(2)}) collective-permute-start(bf16[33,128]{1,0:T(8,128)(2,1)S(1)} %get-tuple-element.20), channel_id=1, source_target_pairs={{0,18},{1,19},{2,16},{3,17},{4,22},{5,23},{6,20},{7,21},{8,26},{9,... | collective-permute-start | bytes 25352 | tf_op jit(solution)/shard_map/ppermute | solution.py:87
  15.5 10.6 %collective-permute-start.10 = (bf16[33,128]{1,0:T(8,128)(2,1)S(1)}, bf16[33,128]{1,0:T(8,128)(2,1)S(1)}, u32[]{:S(2)}, u32[]{:S(2)}) collective-permute-start(bf16[33,128]{1,0:T(8,128)(2,1)S(1)} %get-tuple-element.21), channel_id=1, source_target_pairs={{0,26},{1,27},{2,24},{3,25},{4,30},{5,31},{6,28},{7,29},{8,2},{9,3... | collective-permute-start | bytes 25352 | tf_op jit(solution)/shard_map/ppermute | solution.py:87
  16.8 9.3 %collective-permute-start.11 = (bf16[33,128]{1,0:T(8,128)(2,1)S(1)}, bf16[33,128]{1,0:T(8,128)(2,1)S(1)}, u32[]{:S(2)}, u32[]{:S(2)}) collective-permute-start(bf16[33,128]{1,0:T(8,128)(2,1)S(1)} %get-tuple-element.22), channel_id=1, source_target_pairs={{0,3},{1,2},{2,1},{3,0},{4,7},{5,6},{6,5},{7,4},{8,11},{9,10},{10,... | collective-permute-start | bytes 25352 | tf_op jit(solution)/shard_map/ppermute | solution.py:87
  20.0 9.3 %collective-permute-start.12 = (bf16[33,128]{1,0:T(8,128)(2,1)S(1)}, bf16[33,128]{1,0:T(8,128)(2,1)S(1)}, u32[]{:S(2)}, u32[]{:S(2)}) collective-permute-start(bf16[33,128]{1,0:T(8,128)(2,1)S(1)} %get-tuple-element.23), channel_id=1, source_target_pairs={{0,11},{1,10},{2,9},{3,8},{4,15},{5,14},{6,13},{7,12},{8,19},{9,18... | collective-permute-start | bytes 25352 | tf_op jit(solution)/shard_map/ppermute | solution.py:87
  20.6 9.2 %collective-permute-start.13 = (bf16[33,128]{1,0:T(8,128)(2,1)S(1)}, bf16[33,128]{1,0:T(8,128)(2,1)S(1)}, u32[]{:S(2)}, u32[]{:S(2)}) collective-permute-start(bf16[33,128]{1,0:T(8,128)(2,1)S(1)} %get-tuple-element.17), channel_id=1, source_target_pairs={{0,19},{1,18},{2,17},{3,16},{4,23},{5,22},{6,21},{7,20},{8,27},{9,... | collective-permute-start | bytes 25352 | tf_op jit(solution)/shard_map/ppermute | solution.py:87
  22.8 7.6 %collective-permute-start = (bf16[33,128]{1,0:T(8,128)(2,1)S(1)}, bf16[33,128]{1,0:T(8,128)(2,1)S(1)}, u32[]{:S(2)}, u32[]{:S(2)}) collective-permute-start(bf16[33,128]{1,0:T(8,128)(2,1)S(1)} %get-tuple-element.10), channel_id=1, source_target_pairs={{0,8},{1,9},{2,10},{3,11},{4,12},{5,13},{6,14},{7,15},{8,16},{9,17... | collective-permute-start | bytes 25352 | tf_op jit(solution)/shard_map/ppermute | solution.py:87
  26.2 7.0 %collective-permute-start.1 = (bf16[33,128]{1,0:T(8,128)(2,1)S(1)}, bf16[33,128]{1,0:T(8,128)(2,1)S(1)}, u32[]{:S(2)}, u32[]{:S(2)}) collective-permute-start(bf16[33,128]{1,0:T(8,128)(2,1)S(1)} %get-tuple-element.11), channel_id=1, source_target_pairs={{0,16},{1,17},{2,18},{3,19},{4,20},{5,21},{6,22},{7,23},{8,24},{9,... | collective-permute-start | bytes 25352 | tf_op jit(solution)/shard_map/ppermute | solution.py:87
  26.2 8.8 %collective-permute-start.2 = (bf16[33,128]{1,0:T(8,128)(2,1)S(1)}, bf16[33,128]{1,0:T(8,128)(2,1)S(1)}, u32[]{:S(2)}, u32[]{:S(2)}) collective-permute-start(bf16[33,128]{1,0:T(8,128)(2,1)S(1)} %get-tuple-element.12), channel_id=1, source_target_pairs={{0,24},{1,25},{2,26},{3,27},{4,28},{5,29},{6,30},{7,31},{8,0},{9,1... | collective-permute-start | bytes 25352 | tf_op jit(solution)/shard_map/ppermute | solution.py:87
  29.2 20.9 %collective-permute-start.3 = (bf16[33,128]{1,0:T(8,128)(2,1)S(1)}, bf16[33,128]{1,0:T(8,128)(2,1)S(1)}, u32[]{:S(2)}, u32[]{:S(2)}) collective-permute-start(bf16[33,128]{1,0:T(8,128)(2,1)S(1)} %get-tuple-element.13), channel_id=1, source_target_pairs={{0,1},{1,0},{2,3},{3,2},{4,5},{5,4},{6,7},{7,6},{8,9},{9,8},{10,11... | collective-permute-start | bytes 25352 | tf_op jit(solution)/shard_map/ppermute | solution.py:87
  29.8 23.3 %collective-permute-start.4 = (bf16[33,128]{1,0:T(8,128)(2,1)S(1)}, bf16[33,128]{1,0:T(8,128)(2,1)S(1)}, u32[]{:S(2)}, u32[]{:S(2)}) collective-permute-start(bf16[33,128]{1,0:T(8,128)(2,1)S(1)} %get-tuple-element.14), channel_id=1, source_target_pairs={{0,9},{1,8},{2,11},{3,10},{4,13},{5,12},{6,15},{7,14},{8,17},{9,16... | collective-permute-start | bytes 25352 | tf_op jit(solution)/shard_map/ppermute | solution.py:87
  30.3 26.1 %collective-permute-start.5 = (bf16[33,128]{1,0:T(8,128)(2,1)S(1)}, bf16[33,128]{1,0:T(8,128)(2,1)S(1)}, u32[]{:S(2)}, u32[]{:S(2)}) collective-permute-start(bf16[33,128]{1,0:T(8,128)(2,1)S(1)} %get-tuple-element.15), channel_id=1, source_target_pairs={{0,17},{1,16},{2,19},{3,18},{4,21},{5,20},{6,23},{7,22},{8,25},{9,... | collective-permute-start | bytes 25352 | tf_op jit(solution)/shard_map/ppermute | solution.py:87
  33.2 25.8 %collective-permute-start.6 = (bf16[33,128]{1,0:T(8,128)(2,1)S(1)}, bf16[33,128]{1,0:T(8,128)(2,1)}, u32[]{:S(2)}, u32[]{:S(2)}) collective-permute-start(bf16[33,128]{1,0:T(8,128)(2,1)S(1)} %get-tuple-element.16), channel_id=1, source_target_pairs={{0,25},{1,24},{2,27},{3,26},{4,29},{5,28},{6,31},{7,30},{8,1},{9,0... | collective-permute-start | bytes 25352 | tf_op jit(solution)/shard_map/ppermute | solution.py:87
  35.0 27.6 %collective-permute-start.14 = (bf16[33,128]{1,0:T(8,128)(2,1)}, bf16[33,128]{1,0:T(8,128)(2,1)S(1)}, u32[]{:S(2)}, u32[]{:S(2)}) collective-permute-start(bf16[33,128]{1,0:T(8,128)(2,1)} %get-tuple-element.8), channel_id=1, source_target_pairs={{0,27},{1,26},{2,25},{3,24},{4,31},{5,30},{6,29},{7,28},{8,3},{9,2... | collective-permute-start | bytes 25352 | tf_op jit(solution)/shard_map/ppermute | solution.py:87
  50.1 37.2 %collective-permute-start.15 = (bf16[64,512]{1,0:T(8,128)(2,1)S(1)}, bf16[64,512]{1,0:T(8,128)(2,1)S(1)}, u32[]{:S(2)}, u32[]{:S(2)}) collective-permute-start(bf16[64,512]{1,0:T(8,128)(2,1)S(1)} %multiply_convert_fusion), channel_id=1, source_target_pairs={{0,8},{1,9},{2,10},{3,11},{4,12},{5,13},{6,14},{7,15},{8,16},{9,17... | collective-permute-start | bytes 196616 | tf_op jit(solution)/shard_map/ppermute | solution.py:87
  53.0 35.0 %collective-permute-start.16 = (bf16[64,512]{1,0:T(8,128)(2,1)S(1)}, bf16[64,512]{1,0:T(8,128)(2,1)S(1)}, u32[]{:S(2)}, u32[]{:S(2)}) collective-permute-start(bf16[64,512]{1,0:T(8,128)(2,1)S(1)} %multiply_convert_fusion), channel_id=1, source_target_pairs={{0,16},{1,17},{2,18},{3,19},{4,20},{5,21},{6,22},{7,23},{8,24},{9,... | collective-permute-start | bytes 196616 | tf_op jit(solution)/shard_map/ppermute | solution.py:87
  56.4 33.2 %collective-permute-start.17 = (bf16[64,512]{1,0:T(8,128)(2,1)S(1)}, bf16[64,512]{1,0:T(8,128)(2,1)S(1)}, u32[]{:S(2)}, u32[]{:S(2)}) collective-permute-start(bf16[64,512]{1,0:T(8,128)(2,1)S(1)} %multiply_convert_fusion), channel_id=1, source_target_pairs={{0,24},{1,25},{2,26},{3,27},{4,28},{5,29},{6,30},{7,31},{8,0},{9,1... | collective-permute-start | bytes 196616 | tf_op jit(solution)/shard_map/ppermute | solution.py:87
  59.0 31.2 %collective-permute-start.18 = (bf16[64,512]{1,0:T(8,128)(2,1)S(1)}, bf16[64,512]{1,0:T(8,128)(2,1)S(1)}, u32[]{:S(2)}, u32[]{:S(2)}) collective-permute-start(bf16[64,512]{1,0:T(8,128)(2,1)S(1)} %multiply_convert_fusion), channel_id=1, source_target_pairs={{0,1},{1,0},{2,3},{3,2},{4,5},{5,4},{6,7},{7,6},{8,9},{9,8},{10,11... | collective-permute-start | bytes 196616 | tf_op jit(solution)/shard_map/ppermute | solution.py:87
  62.6 32.9 %collective-permute-start.22 = (bf16[64,512]{1,0:T(8,128)(2,1)S(1)}, bf16[64,512]{1,0:T(8,128)(2,1)}, u32[]{:S(2)}, u32[]{:S(2)}) collective-permute-start(bf16[64,512]{1,0:T(8,128)(2,1)S(1)} %multiply_convert_fusion), channel_id=1, source_target_pairs={{0,2},{1,3},{2,0},{3,1},{4,6},{5,7},{6,4},{7,5},{8,10},{9,11},{10,... | collective-permute-start | bytes 196616 | tf_op jit(solution)/shard_map/ppermute | solution.py:87
  87.4 4.6 %collective-permute-start.19 = (bf16[64,512]{1,0:T(8,128)(2,1)S(1)}, bf16[64,512]{1,0:T(8,128)(2,1)S(1)}, u32[]{:S(2)}, u32[]{:S(2)}) collective-permute-start(bf16[64,512]{1,0:T(8,128)(2,1)S(1)} %collective-permute-done.15), channel_id=1, source_target_pairs={{0,1},{1,0},{2,3},{3,2},{4,5},{5,4},{6,7},{7,6},{8,9},{9,8},{10,11... | collective-permute-start | bytes 196616 | tf_op jit(solution)/shard_map/ppermute | solution.py:87
  88.0 5.4 %collective-permute-start.20 = (bf16[64,512]{1,0:T(8,128)(2,1)S(1)}, bf16[64,512]{1,0:T(8,128)(2,1)S(1)}, u32[]{:S(2)}, u32[]{:S(2)}) collective-permute-start(bf16[64,512]{1,0:T(8,128)(2,1)S(1)} %collective-permute-done.16), channel_id=1, source_target_pairs={{0,1},{1,0},{2,3},{3,2},{4,5},{5,4},{6,7},{7,6},{8,9},{9,8},{10,11... | collective-permute-start | bytes 196616 | tf_op jit(solution)/shard_map/ppermute | solution.py:87
  89.6 4.9 %collective-permute-start.21 = (bf16[64,512]{1,0:T(8,128)(2,1)S(1)}, bf16[64,512]{1,0:T(8,128)(2,1)S(1)}, u32[]{:S(2)}, u32[]{:S(2)}) collective-permute-start(bf16[64,512]{1,0:T(8,128)(2,1)S(1)} %collective-permute-done.17), channel_id=1, source_target_pairs={{0,1},{1,0},{2,3},{3,2},{4,5},{5,4},{6,7},{7,6},{8,9},{9,8},{10,11... | collective-permute-start | bytes 196616 | tf_op jit(solution)/shard_map/ppermute | solution.py:87
  90.2 7.3 %collective-permute-start.23 = (bf16[64,512]{1,0:T(8,128)(2,1)S(1)}, bf16[64,512]{1,0:T(8,128)(2,1)S(1)}, u32[]{:S(2)}, u32[]{:S(2)}) collective-permute-start(bf16[64,512]{1,0:T(8,128)(2,1)S(1)} %collective-permute-done.15), channel_id=1, source_target_pairs={{0,2},{1,3},{2,0},{3,1},{4,6},{5,7},{6,4},{7,5},{8,10},{9,11},{10,... | collective-permute-start | bytes 196616 | tf_op jit(solution)/shard_map/ppermute | solution.py:87
  92.0 5.5 %collective-permute-start.24 = (bf16[64,512]{1,0:T(8,128)(2,1)S(1)}, bf16[64,512]{1,0:T(8,128)(2,1)S(1)}, u32[]{:S(2)}, u32[]{:S(2)}) collective-permute-start(bf16[64,512]{1,0:T(8,128)(2,1)S(1)} %collective-permute-done.16), channel_id=1, source_target_pairs={{0,2},{1,3},{2,0},{3,1},{4,6},{5,7},{6,4},{7,5},{8,10},{9,11},{10,... | collective-permute-start | bytes 196616 | tf_op jit(solution)/shard_map/ppermute | solution.py:87
  93.4 5.0 %collective-permute-start.25 = (bf16[64,512]{1,0:T(8,128)(2,1)S(1)}, bf16[64,512]{1,0:T(8,128)(2,1)S(1)}, u32[]{:S(2)}, u32[]{:S(2)}) collective-permute-start(bf16[64,512]{1,0:T(8,128)(2,1)S(1)} %collective-permute-done.17), channel_id=1, source_target_pairs={{0,2},{1,3},{2,0},{3,1},{4,6},{5,7},{6,4},{7,5},{8,10},{9,11},{10,... | collective-permute-start | bytes 196616 | tf_op jit(solution)/shard_map/ppermute | solution.py:87
  94.5 5.1 %collective-permute-start.26 = (bf16[64,512]{1,0:T(8,128)(2,1)S(1)}, bf16[64,512]{1,0:T(8,128)(2,1)S(1)}, u32[]{:S(2)}, u32[]{:S(2)}) collective-permute-start(bf16[64,512]{1,0:T(8,128)(2,1)S(1)} %collective-permute-done.18), channel_id=1, source_target_pairs={{0,2},{1,3},{2,0},{3,1},{4,6},{5,7},{6,4},{7,5},{8,10},{9,11},{10,... | collective-permute-start | bytes 196616 | tf_op jit(solution)/shard_map/ppermute | solution.py:87
  95.5 4.3 %collective-permute-start.27 = (bf16[64,512]{1,0:T(8,128)(2,1)S(1)}, bf16[64,512]{1,0:T(8,128)(2,1)S(1)}, u32[]{:S(2)}, u32[]{:S(2)}) collective-permute-start(bf16[64,512]{1,0:T(8,128)(2,1)S(1)} %collective-permute-done.19), channel_id=1, source_target_pairs={{0,2},{1,3},{2,0},{3,1},{4,6},{5,7},{6,4},{7,5},{8,10},{9,11},{10,... | collective-permute-start | bytes 196616 | tf_op jit(solution)/shard_map/ppermute | solution.py:87
  97.5 4.3 %collective-permute-start.28 = (bf16[64,512]{1,0:T(8,128)(2,1)S(1)}, bf16[64,512]{1,0:T(8,128)(2,1)S(1)}, u32[]{:S(2)}, u32[]{:S(2)}) collective-permute-start(bf16[64,512]{1,0:T(8,128)(2,1)S(1)} %collective-permute-done.24), channel_id=1, source_target_pairs={{0,1},{1,0},{2,3},{3,2},{4,5},{5,4},{6,7},{7,6},{8,9},{9,8},{10,11... | collective-permute-start | bytes 196616 | tf_op jit(solution)/shard_map/ppermute | solution.py:87
  98.4 4.3 %collective-permute-start.29 = (bf16[64,512]{1,0:T(8,128)(2,1)S(1)}, bf16[64,512]{1,0:T(8,128)(2,1)S(1)}, u32[]{:S(2)}, u32[]{:S(2)}) collective-permute-start(bf16[64,512]{1,0:T(8,128)(2,1)S(1)} %collective-permute-done.25), channel_id=1, source_target_pairs={{0,1},{1,0},{2,3},{3,2},{4,5},{5,4},{6,7},{7,6},{8,9},{9,8},{10,11... | collective-permute-start | bytes 196616 | tf_op jit(solution)/shard_map/ppermute | solution.py:87
  109.0 2.4 %collective-permute-start.30 = (bf16[24,32,512]{2,1,0:T(8,128)(2,1)S(1)}, bf16[24,32,512]{2,1,0:T(8,128)(2,1)S(1)}, u32[]{:S(2)}, u32[]{:S(2)}) collective-permute-start(bf16[24,32,512]{2,1,0:T(8,128)(2,1)S(1)} %fusion.13), channel_id=1, source_target_pairs={{0,4},{1,5},{2,6},{3,7},{4,0},{5,1},{6,2},{7,3},{8,12},{9,13},{10,... | collective-permute-start | bytes 2359304 | tf_op jit(solution)/shard_map/ppermute | solution.py:87
  (3 other events, 31.8 us)

commit v3 on v2

--- a/solution.py
+++ b/solution.py
@@ -1,6 +1,10 @@
+import functools
+
 import jax
 import jax.numpy as jnp
 from jax import lax
+from jax.experimental import pallas as pl
+from jax.experimental.pallas import tpu as pltpu
 from jax.sharding import PartitionSpec as P
 
 CAP = 2
@@ -87,52 +91,223 @@
     return lax.ppermute(value, ("rows", "cols"), pairs)
 
 
+def pack_kernel(
+    sizes, me_ref, lists_ref, masks_ref, order_ref, weights_ref, panel_ref, jac_ref, *rest
+):
+    layers, owners, per_owner, block_count, slot_count, block_rows, tile_width = sizes
+    parcels, (places_ref, turned_ref) = rest[:layers], rest[layers:]
+    f32, bf16 = jnp.float32, jnp.bfloat16
+    rows, panel_width = panel_ref.shape
+    lane_group = CAP * block_rows
+    slab = tile_width // layers
+    part = slab // 2
+    me_z, me_core, me_c = me_ref[0], me_ref[1], me_ref[2]
+
+    for i in range(order_ref.shape[0]):
+        places_ref[order_ref[i]] = i
+
+    row_ids = lax.broadcasted_iota(jnp.int32, (rows, rows), 0)
+    lane_ids = lax.broadcasted_iota(jnp.int32, (rows, rows), 1)
+    column = jnp.sum(jnp.where(row_ids == lane_ids, weights_ref[...], 0.0), axis=1, keepdims=True)
+    weighted = (column * panel_ref[...].astype(f32)).astype(bf16)
+    for parcel in parcels:
+        parcel[:, :panel_width] = weighted
+
+    for b in range(block_count):
+        block = jac_ref[b * block_rows : (b + 1) * block_rows, :].astype(f32)
+        start = b * slot_count * tile_width
+        turned_ref[start : start + slot_count * tile_width, :] = block.T
+
+    slots = []
+    for s in range(block_count * slot_count):
+        b, k = divmod(s, slot_count)
+        place = places_ref[lists_ref[b, k]]
+        owner = jnp.int32(0)
+        for c in range(1, owners):
+            owner += (place >= c * per_owner).astype(jnp.int32)
+        slots.append((place - owner * per_owner, jnp.where(masks_ref[b, k] == 1, owner, -1)))
+
+    lane = lax.broadcasted_iota(jnp.int32, (16, CAP * block_count * block_rows), 1)
+    for e in range(owners):
+        wanted = me_c ^ e
+        found = jnp.int32(0)
+        chosen = [jnp.int32(0)] * CAP
+        codes = [jnp.int32(-1)] * CAP
+        for s, (place, owner) in enumerate(slots):
+            hit = owner == wanted
+            for j in range(CAP):
+                take = hit & (found == j)
+                chosen[j] = jnp.where(take, s, chosen[j])
+                codes[j] = jnp.where(take, place, codes[j])
+            found += hit.astype(jnp.int32)
+        note = jnp.full(lane.shape, -1, jnp.int32)
+        for j in range(CAP):
+            for b in range(block_count):
+                at = (j * block_count + b) * block_rows
+                here = (lane >= at) & (lane < at + block_rows)
+                code = jnp.where(chosen[j] // slot_count == b, codes[j], -1)
+                note = jnp.where(here, code, note)
+        note = note.astype(f32).astype(bf16)
+        at = panel_width + owners * lane_group
+        for k, parcel in enumerate(parcels):
+            parcel[e * 16 : (e + 1) * 16, at : at + note.shape[1]] = note
+            z = lax.rem(me_z + k, layers)
+            for u in range(2):
+                core = me_core ^ u
+                for j in range(CAP):
+                    first = pl.multiple_of(chosen[j] * tile_width + z * slab + core * part, part)
+                    piece = turned_ref[pl.ds(first, part), :].astype(bf16)
+                    to = panel_width + e * lane_group + j * block_rows
+                    parcel[u * part : (u + 1) * part, to : to + block_rows] = piece
+
+
+def sort_kernel(sizes, *refs):
+    layers, owners, panel_width, lane_group = sizes
+    parcels, outs = refs[:layers], refs[layers:]
+    halves, posts = outs[: layers // 2], outs[layers // 2 :]
+    rows = parcels[0].shape[0]
+    codes_at = panel_width + owners * lane_group
+    for k, parcel in enumerate(parcels):
+        halves[k // 2][(k % 2) * rows : (k % 2 + 1) * rows, :] = parcel[:, :panel_width]
+        for e, post in enumerate(posts):
+            at = panel_width + e * lane_group
+            post[:rows, k * lane_group : (k + 1) * lane_group] = parcel[:, at : at + lane_group]
+            note = parcel[e * 16 : (e + 1) * 16, codes_at:]
+            wide = note.shape[1]
+            low = rows + 16 * (k // 2)
+            post[low : low + 16, (k % 2) * wide : (k % 2 + 1) * wide] = note
+
+
+def gram_kernel(sizes, *refs):
+    layers, owners, per_owner, block_rows, block_count = sizes
+    pairs = layers // 2
+    panels = refs[: owners * pairs]
+    posts = refs[owners * pairs : owners * pairs + owners]
+    own_ref, other_ref, placed_ref, rows_ref = refs[owners * pairs + owners :]
+    f32, bf16 = jnp.float32, jnp.bfloat16
+    rows = block_count * block_rows
+    group = CAP * block_rows
+    height = posts[0].shape[0] - 16 * pairs
+    part = height // 2
+    depth = 2 * rows
+    for i, panel in enumerate(panels):
+        rows_ref[i * depth : (i + 1) * depth, :] = panel[...]
+    for u, out_ref in ((1, other_ref), (0, own_ref)):
+        for e in range(owners):
+            for h in range(pairs):
+                post = posts[e]
+                columns, codes = [], []
+                for j in range(CAP):
+                    pieces, notes = [], []
+                    for d in range(2):
+                        at = (h * 2 + d) * group + j * block_rows
+                        piece = post[u * part : (u + 1) * part, at : at + block_rows].astype(f32)
+                        pieces += [piece] * block_count
+                        low = height + 16 * h
+                        wide = CAP * rows
+                        notes.append(post[low : low + 16, d * wide + j * rows : d * wide + (j + 1) * rows].astype(f32))
+                    columns.append(jnp.concatenate(pieces, axis=1).astype(bf16))
+                    note = jnp.concatenate(notes, axis=1)
+                    codes.append(jnp.concatenate([note] * (part // 16), axis=0).astype(bf16))
+                at = (e * pairs + h) * depth
+                for n in range(per_owner):
+                    placed = jnp.zeros(columns[0].shape, bf16)
+                    for j in range(CAP):
+                        placed = jnp.where(codes[j] == jnp.asarray(n, bf16), columns[j], placed)
+                    placed_ref[n * part : (n + 1) * part, at : at + depth] = placed
+        out_ref[...] = jnp.dot(placed_ref[...], rows_ref[...], preferred_element_type=f32).astype(out_ref.dtype)
+
+
+def inverse_kernel(own_ref, other_ref, factor_ref, out_ref):
+    f32, bf16 = jnp.float32, jnp.bfloat16
+    factor = factor_ref[...]
+    high = factor.astype(bf16)
+    low = (factor - high.astype(f32)).astype(bf16)
+    gram = own_ref[...] + other_ref[...].astype(f32)
+    gram_high = gram.astype(bf16)
+    gram_low = (gram - gram_high.astype(f32)).astype(bf16)
+    dims = (((1,), (1,)), ((), ()))
+
+    def times(a, b):
+        return lax.dot_general(a, b, dims, preferred_element_type=f32)
+
+    out_ref[...] = times(gram_high, high) + (times(gram_high, low) + times(gram_low, high))
+
+
 def local(jac, panel_jac, weights, tile_lists, tile_masks, tile_order, factor_inverse):
     block_count, slot_count = tile_lists.shape
-    block_rows = jac.shape[0] // block_count
+    rows, panel_width = panel_jac.shape
+    block_rows = rows // block_count
     tile_width = jac.shape[1] // slot_count
     slabs, owners = lax.axis_size("rows"), lax.axis_size("cols")
-    layers = slabs // 2
+    layers, pairs = slabs // 2, slabs // 4
     per_owner = tile_order.shape[0] // owners
     slab_width = tile_width // slabs
-    bf16 = jnp.bfloat16
-    weighted = (weights[:, None] * panel_jac).astype(bf16)
-
-    lines = [weighted] + [shift(weighted, k, 0) for k in range(1, layers)]
-    by_x = [shift(w, 0, 1) for w in lines]
-    by_y = [shift(w, 0, 2) for w in lines]
-    half = layers // 2
-    across = [shift(w, 0, 2) for w in by_x[:half]] + [shift(w, 0, 1) for w in by_y[half:]]
+    f32, bf16 = jnp.float32, jnp.bfloat16
+    vmem, smem = pl.BlockSpec(memory_space=pltpu.VMEM), pl.BlockSpec(memory_space=pltpu.SMEM)
+    params = pltpu.CompilerParams(vmem_limit_bytes=48 << 20)
 
     me_r, me_c = lax.axis_index("rows"), lax.axis_index("cols")
-    me_z, me_core = me_r // 2, me_r % 2
-    code, places = slot_codes(tile_lists, tile_masks, tile_order, me_c ^ jnp.arange(owners))
-    columns = jac.reshape(block_count, block_rows, slot_count, layers, 2, slab_width)
-    columns = jnp.take(columns, (me_z + jnp.arange(layers)) % layers, axis=3)
-    columns = jnp.take(columns, me_core ^ jnp.arange(2), axis=4)
-    chosen = code.astype(bf16).reshape(owners, CAP, block_count, slot_count)
-    pieces = jnp.einsum("ejbk,bmkzut->zemjut", chosen, columns, preferred_element_type=jnp.float32).astype(bf16)
-    pieces = pieces.reshape(layers, owners, block_rows, -1)
-    note = jnp.pad(places.astype(bf16), ((0, 0), (0, pieces.shape[3] - CAP)))
-    note = jnp.broadcast_to(note[None, :, None], (layers, owners, 1, pieces.shape[3]))
-    sent = jnp.concatenate([pieces, note], axis=2)
-    got = [
-        [sent[k, e] if k == e == 0 else shift(sent[k, e], k, e) for e in range(owners)]
-        for k in range(layers)
-    ]
-
-    panels = jnp.stack([w for group in (lines, by_x, by_y, across) for w in group])
-    got = jnp.stack([got[k][e] for e in range(owners) for k in range(layers)])
-    sources = layers * owners
-    panels = panels.reshape(sources, block_count, block_rows, -1)
-    data = got[:, :block_rows].reshape(sources, block_rows, CAP, 2, slab_width)
-    where = got[:, block_rows, :CAP].astype(jnp.int32)
-    hot = (where[:, :, None] == jnp.arange(block_count * per_owner)).astype(bf16)
-    hot = hot.reshape(sources, CAP, block_count, per_owner)
-    mixed = jnp.einsum("djbn,dmjut->dbmunt", hot, data, preferred_element_type=jnp.float32).astype(bf16)
-    gram = jnp.einsum("dbmunt,dbmp->untp", mixed, panels, preferred_element_type=jnp.float32)
-    other = shift(gram[1].astype(bf16), 0, 0, 1)
-    return apply_inverse(gram[0] + other.astype(jnp.float32), factor_inverse)
+    me = jnp.stack([me_r // 2, me_r % 2, me_c]).astype(jnp.int32)
+    lane_group = CAP * block_rows
+    wide = CAP * block_count * block_rows
+    parcel = jax.ShapeDtypeStruct((rows, panel_width + owners * lane_group + wide), bf16)
+    sizes = (layers, owners, per_owner, block_count, slot_count, block_rows, tile_width)
+    parcels = pl.pallas_call(
+        functools.partial(pack_kernel, sizes),
+        out_shape=[parcel] * layers,
+        in_specs=[smem] * 4 + [vmem] * 3,
+        out_specs=[vmem] * layers,
+        scratch_shapes=[
+            pltpu.SMEM((tile_order.shape[0],), jnp.int32),
+            pltpu.VMEM((block_count * slot_count * tile_width, block_rows), f32),
+        ],
+        compiler_params=params,
+        name="pack",
+    )(me, tile_lists, tile_masks, tile_order, weights.reshape(1, rows), panel_jac, jac)
+    parcels = [parcels[0]] + [shift(parcels[k], k, 0) for k in range(1, layers)]
+
+    height = 2 * slab_width
+    half = jax.ShapeDtypeStruct((2 * rows, panel_width), bf16)
+    post = jax.ShapeDtypeStruct((height + 16 * pairs, max(layers * lane_group, 2 * wide)), bf16)
+    outs = pl.pallas_call(
+        functools.partial(sort_kernel, (layers, owners, panel_width, lane_group)),
+        out_shape=[half] * pairs + [post] * owners,
+        in_specs=[vmem] * layers,
+        out_specs=[vmem] * (pairs + owners),
+        compiler_params=params,
+        name="sort",
+    )(*parcels)
+    mine, posts = outs[:pairs], outs[pairs:]
+    by_x = [shift(w, 0, 1) for w in mine]
+    by_y = [shift(w, 0, 2) for w in mine]
+    across = [shift(by_x[0], 0, 2), shift(by_y[1], 0, 1)]
+    posts = [posts[0]] + [shift(posts[e], 0, e) for e in range(1, owners)]
+
+    count = per_owner * slab_width
+    depth = layers * owners * rows
+    own, other = pl.pallas_call(
+        functools.partial(gram_kernel, (layers, owners, per_owner, block_rows, block_count)),
+        out_shape=[
+            jax.ShapeDtypeStruct((count, panel_width), f32),
+            jax.ShapeDtypeStruct((count, panel_width), bf16),
+        ],
+        in_specs=[vmem] * (owners * pairs + owners),
+        out_specs=[vmem] * 2,
+        scratch_shapes=[pltpu.VMEM((count, depth), bf16), pltpu.VMEM((depth, panel_width), bf16)],
+        compiler_params=params,
+        name="gram",
+    )(*mine, *by_x, *by_y, *across, *posts)
+    other = shift(other, 0, 0, 1)
+    out = pl.pallas_call(
+        inverse_kernel,
+        out_shape=jax.ShapeDtypeStruct((count, panel_width), f32),
+        in_specs=[vmem] * 3,
+        out_specs=vmem,
+        compiler_params=params,
+        name="inverse",
+    )(own, other, factor_inverse)
+    return out.reshape(per_owner, slab_width, panel_width)
 
 
 def solution(mesh):

time: 116 us -> 44.9 us (0.39)
  local copies, waits for them, and re-layouts: 45 us -> 4.49 us
  starting transfers between devices: 43.4 us -> 18.7 us
  matrix products: 14.6 us -> 0 us
  waiting for transfers between devices: 8.01 us -> 15.3 us
  Pallas kernels: 0 us -> 5.72 us
  other arithmetic: 3.79 us -> 0.08 us
    another operation x18 -> x0, local copies, waits for them, and re-layouts: 36.9 us -> none  [the longest x17 36.9 us: local(): got = jnp.stack([got[k][e] for e in range(owners) for k in range(layers)])]
    ppermute x31 -> x13, starting transfers between devices: 43.4 us -> 18.7 us  [shift(): return lax.ppermute(value, ('rows', 'cols'), pairs)]
    dot_general x4 -> x0, matrix products: 14.6 us -> none  [the longest x1 6.14 us: local(): jnp.einsum('dbmunt,dbmp->untp', mixed, panels, preferred_element_type=jnp...]
    ppermute x31 -> x13, waiting for transfers between devices: 8.01 us -> 15.3 us  [shift(): return lax.ppermute(value, ('rows', 'cols'), pairs)]
    pallas_call x0 -> x4, Pallas kernels: none -> 5.72 us  [the longest x1 2.56 us: local(): pl.pallas_call(inverse_kernel, out_shape=jax.ShapeDtypeStruct((count, pan...]
    unnamed x24 -> x14, local copies, waits for them, and re-layouts: 1.66 us -> 4.49 us
    reshape x4 -> x0, local copies, waits for them, and re-layouts: 2.77 us -> none  [the longest x2 1.5 us: local(): jac.reshape(block_count, block_rows, slot_count, layers, 2, slab_width)]
    reduce_sum x3 -> x0, other arithmetic: 1.31 us -> none  [the longest x1 0.98 us: tile_positions(): jnp.sum(jnp.where(matches, jnp.arange(tile_count, dtype=jnp.int32), 0), a...]
  transfers between devices with their start and end apart: 31 -> 13, of which waited for: 7 -> 6; matrix products, arithmetic and copies ran while one was open for 40% -> 0% of each run, Pallas kernels for 0% -> 0%
where the time goes in v3:
time: 44.9 us; the launch traced here: 44.3 us
  starting transfers between devices  18.7 us (42%)
  waiting for transfers between devices  15.3 us (34%)
  Pallas kernels  5.72 us (13%)
  local copies, waits for them, and re-layouts  4.49 us (10%)
    ppermute x13, starting transfers between devices, shift(): return lax.ppermute(value, ('rows', 'cols'), pairs)  18.7 us
    ppermute x13, waiting for transfers between devices, shift(): return lax.ppermute(value, ('rows', 'cols'), pairs)  15.3 us
    unnamed x14, local copies, waits for them, and re-layouts  4.49 us
    pallas_call x1, Pallas kernels, local(): pl.pallas_call(inverse_kernel, out_shape=jax.ShapeDtypeStruct((count, pan...  2.56 us
    pallas_call x1, Pallas kernels, local(): pl.pallas_call(functools.partial(gram_kernel, (layers, owners, per_owner,...  1.87 us
    pallas_call x1, Pallas kernels, local(): pl.pallas_call(functools.partial(pack_kernel, sizes), out_shape=[parcel]...  1.16 us
  transfers between devices with their start and end apart: 13, of which 6 were waited for; matrix products, arithmetic and copies ran while one was open for 0% of the time, Pallas kernels for 0%

profile of v3, /device:TPU:0, one launch (start us, length us, event | category | flops | bytes accessed | tf_op | source)
XLA Modules:
  0.0 44.3 jit_solution(888633889570488007)
XLA Ops:
  0.0 0.1 pad_add_fusion.me_ref
  0.1 1.0 %copy-done.1 = bf16[64,1024]{1,0:T(8,128)(2,1)S(1)} copy-done((bf16[64,1024]{1,0:T(8,128)(2,1)S(1)}, bf16[64,1024]{1,0:T(8,128)(2,1)}, u32[]{:S(2)}) %copy-start.1) | copy-done | bytes 131096
  1.1 0.8 %copy-done.2 = bf16[64,512]{1,0:T(8,128)(2,1)S(1)} copy-done((bf16[64,512]{1,0:T(8,128)(2,1)S(1)}, bf16[64,512]{1,0:T(8,128)(2,1)}, u32[]{:S(2)}) %copy-start.2) | copy-done | bytes 65560
  1.9 0.7 %copy-done.3 = s32[2,4]{1,0:T(2,128)S(1)} copy-done((s32[2,4]{1,0:T(2,128)S(1)}, s32[2,4]{1,0:T(2,128)}, u32[]{:S(2)}) %copy-start.3) | copy-done | bytes 56
  2.6 0.7 %copy-done.4 = s32[2,4]{1,0:T(2,128)S(1)} copy-done((s32[2,4]{1,0:T(2,128)S(1)}, s32[2,4]{1,0:T(2,128)}, u32[]{:S(2)}) %copy-start.4) | copy-done | bytes 56
  3.3 0.7 %copy-done.5 = s32[96]{0:T(128)S(1)} copy-done((s32[96]{0:T(128)S(1)}, s32[96]{0:T(128)}, u32[]{:S(2)}) %copy-start.5) | copy-done | bytes 408
  3.9 0.7 %copy-done.6 = f32[64]{0:T(128)S(1)} copy-done((f32[64]{0:T(128)S(1)}, f32[64]{0:T(128)}, u32[]{:S(2)}) %copy-start.6) | copy-done | bytes 280
  4.6 1.2 %pack.1 = (bf16[64,896]{1,0:T(8,128)(2,1)S(1)}, bf16[64,896]{1,0:T(8,128)(2,1)S(1)}, bf16[64,896]{1,0:T(8,128)(2,1)S(1)}, bf16[64,896]{1,0:T(8,128)(2,1)S(1)}) custom-call(s32[3]{0:T(128)S(1)} %pad_add_fusion.me_ref, s32[2,4]{1,0:T(2,128)S(1)} %copy-done.3, s32[2,4]{1,0:T(2,128)S(1)} %copy-done.4, s32[96]{0:T(128)S(1)} %copy-done.5, f32[1,64]{1,0:T(1,128)S(1)} %bitcast.5, ...), custom_call_target="tpu_custom_call" | custom-call | tf_op jit(solution)/shard_map/pack/pallas_call | solution.py:256
  5.7 3.1 %collective-permute-start = (bf16[64,896]{1,0:T(8,128)(2,1)S(1)}, bf16[64,896]{1,0:T(8,128)(2,1)S(1)}, u32[]{:S(2)}, u32[]{:S(2)}) collective-permute-start(bf16[64,896]{1,0:T(8,128)(2,1)S(1)} %get-tuple-element.18), channel_id=1, source_target_pairs={{0,8},{1,9},{2,10},{3,11},{4,12},{5,13},{6,14},{7,15},{8,16},{9,17... | collective-permute-start | bytes 344072 | tf_op jit(solution)/shard_map/ppermute | solution.py:91
  8.8 2.6 %collective-permute-start.1 = (bf16[64,896]{1,0:T(8,128)(2,1)S(1)}, bf16[64,896]{1,0:T(8,128)(2,1)S(1)}, u32[]{:S(2)}, u32[]{:S(2)}) collective-permute-start(bf16[64,896]{1,0:T(8,128)(2,1)S(1)} %get-tuple-element.19), channel_id=1, source_target_pairs={{0,16},{1,17},{2,18},{3,19},{4,20},{5,21},{6,22},{7,23},{8,24},{9,... | collective-permute-start | bytes 344072 | tf_op jit(solution)/shard_map/ppermute | solution.py:91
  11.4 1.3 %collective-permute-start.2 = (bf16[64,896]{1,0:T(8,128)(2,1)S(1)}, bf16[64,896]{1,0:T(8,128)(2,1)S(1)}, u32[]{:S(2)}, u32[]{:S(2)}) collective-permute-start(bf16[64,896]{1,0:T(8,128)(2,1)S(1)} %get-tuple-element.20), channel_id=1, source_target_pairs={{0,24},{1,25},{2,26},{3,27},{4,28},{5,29},{6,30},{7,31},{8,0},{9,1... | collective-permute-start | bytes 344072 | tf_op jit(solution)/shard_map/ppermute | solution.py:91
  12.8 2.2 %collective-permute-done.refs_1_ = bf16[64,896]{1,0:T(8,128)(2,1)S(1)} collective-permute-done((bf16[64,896]{1,0:T(8,128)(2,1)S(1)}, bf16[64,896]{1,0:T(8,128)(2,1)S(1)}, u32[]{:S(2)}, u32[]{:S(2)}) %collective-permute-start) | collective-permute-done | bytes 114720 | tf_op jit(solution)/shard_map/ppermute | solution.py:91
  14.9 4.1 %collective-permute-done.1.refs_2_ = bf16[64,896]{1,0:T(8,128)(2,1)S(1)} collective-permute-done((bf16[64,896]{1,0:T(8,128)(2,1)S(1)}, bf16[64,896]{1,0:T(8,128)(2,1)S(1)}, u32[]{:S(2)}, u32[]{:S(2)}) %collective-permute-start.1) | collective-permute-done | bytes 114720 | tf_op jit(solution)/shard_map/ppermute | solution.py:91
  19.0 0.1 sort.1
  19.1 1.6 %collective-permute-start.3 = (bf16[128,512]{1,0:T(8,128)(2,1)S(1)}, bf16[128,512]{1,0:T(8,128)(2,1)S(1)}, u32[]{:S(2)}, u32[]{:S(2)}) collective-permute-start(bf16[128,512]{1,0:T(8,128)(2,1)S(1)} %get-tuple-element.21.refs_0_), channel_id=1, source_target_pairs={{0,1},{1,0},{2,3},{3,2},{4,5},{5,4},{6,7},{7,6},{8,9},{9,8},{10,11... | collective-permute-start | bytes 393224 | tf_op jit(solution)/shard_map/ppermute | solution.py:91
  20.7 1.5 %collective-permute-start.6 = (bf16[128,512]{1,0:T(8,128)(2,1)S(1)}, bf16[128,512]{1,0:T(8,128)(2,1)S(1)}, u32[]{:S(2)}, u32[]{:S(2)}) collective-permute-start(bf16[128,512]{1,0:T(8,128)(2,1)S(1)} %get-tuple-element.22.refs_1_), channel_id=1, source_target_pairs={{0,2},{1,3},{2,0},{3,1},{4,6},{5,7},{6,4},{7,5},{8,10},{9,11},{10,... | collective-permute-start | bytes 393224 | tf_op jit(solution)/shard_map/ppermute | solution.py:91
  22.3 0.5 %collective-permute-start.9 = (bf16[96,256]{1,0:T(8,128)(2,1)S(1)}, bf16[96,256]{1,0:T(8,128)(2,1)S(1)}, u32[]{:S(2)}, u32[]{:S(2)}) collective-permute-start(bf16[96,256]{1,0:T(8,128)(2,1)S(1)} %get-tuple-element.24), channel_id=1, source_target_pairs={{0,1},{1,0},{2,3},{3,2},{4,5},{5,4},{6,7},{7,6},{8,9},{9,8},{10,11... | collective-permute-start | bytes 147464 | tf_op jit(solution)/shard_map/ppermute | solution.py:91
  22.8 0.5 %collective-permute-start.5 = (bf16[128,512]{1,0:T(8,128)(2,1)S(1)}, bf16[128,512]{1,0:T(8,128)(2,1)S(1)}, u32[]{:S(2)}, u32[]{:S(2)}) collective-permute-start(bf16[128,512]{1,0:T(8,128)(2,1)S(1)} %get-tuple-element.21.refs_0_), channel_id=1, source_target_pairs={{0,2},{1,3},{2,0},{3,1},{4,6},{5,7},{6,4},{7,5},{8,10},{9,11},{10,... | collective-permute-start | bytes 393224 | tf_op jit(solution)/shard_map/ppermute | solution.py:91
  23.2 1.5 %collective-permute-start.4 = (bf16[128,512]{1,0:T(8,128)(2,1)S(1)}, bf16[128,512]{1,0:T(8,128)(2,1)S(1)}, u32[]{:S(2)}, u32[]{:S(2)}) collective-permute-start(bf16[128,512]{1,0:T(8,128)(2,1)S(1)} %get-tuple-element.22.refs_1_), channel_id=1, source_target_pairs={{0,1},{1,0},{2,3},{3,2},{4,5},{5,4},{6,7},{7,6},{8,9},{9,8},{10,11... | collective-permute-start | bytes 393224 | tf_op jit(solution)/shard_map/ppermute | solution.py:91
  24.8 2.2 %collective-permute-start.7 = (bf16[128,512]{1,0:T(8,128)(2,1)S(1)}, bf16[128,512]{1,0:T(8,128)(2,1)S(1)}, u32[]{:S(2)}, u32[]{:S(2)}) collective-permute-start(bf16[128,512]{1,0:T(8,128)(2,1)S(1)} %collective-permute-done.3.refs_2_), channel_id=1, source_target_pairs={{0,2},{1,3},{2,0},{3,1},{4,6},{5,7},{6,4},{7,5},{8,10},{9,11},{10,... | collective-permute-start | bytes 393224 | tf_op jit(solution)/shard_map/ppermute | solution.py:91
  26.9 0.1 collective-permute-done.6.refs_5_
  27.1 1.4 %collective-permute-start.8 = (bf16[128,512]{1,0:T(8,128)(2,1)S(1)}, bf16[128,512]{1,0:T(8,128)(2,1)S(1)}, u32[]{:S(2)}, u32[]{:S(2)}) collective-permute-start(bf16[128,512]{1,0:T(8,128)(2,1)S(1)} %collective-permute-done.6.refs_5_), channel_id=1, source_target_pairs={{0,1},{1,0},{2,3},{3,2},{4,5},{5,4},{6,7},{7,6},{8,9},{9,8},{10,11... | collective-permute-start | bytes 393224 | tf_op jit(solution)/shard_map/ppermute | solution.py:91
  28.4 0.0 collective-permute-done.9.refs_9_
  28.4 0.8 %collective-permute-start.10 = (bf16[96,256]{1,0:T(8,128)(2,1)S(1)}, bf16[96,256]{1,0:T(8,128)(2,1)S(1)}, u32[]{:S(2)}, u32[]{:S(2)}) collective-permute-start(bf16[96,256]{1,0:T(8,128)(2,1)S(1)} %get-tuple-element.25), channel_id=1, source_target_pairs={{0,2},{1,3},{2,0},{3,1},{4,6},{5,7},{6,4},{7,5},{8,10},{9,11},{10,... | collective-permute-start | bytes 147464 | tf_op jit(solution)/shard_map/ppermute | solution.py:91
  29.2 3.3 %collective-permute-done.10.refs_10_ = bf16[96,256]{1,0:T(8,128)(2,1)S(1)} collective-permute-done((bf16[96,256]{1,0:T(8,128)(2,1)S(1)}, bf16[96,256]{1,0:T(8,128)(2,1)S(1)}, u32[]{:S(2)}, u32[]{:S(2)}) %collective-permute-start.10) | collective-permute-done | bytes 49184 | tf_op jit(solution)/shard_map/ppermute | solution.py:91
  32.5 1.7 %collective-permute-start.11 = (bf16[96,256]{1,0:T(8,128)(2,1)S(1)}, bf16[96,256]{1,0:T(8,128)(2,1)S(1)}, u32[]{:S(2)}, u32[]{:S(2)}) collective-permute-start(bf16[96,256]{1,0:T(8,128)(2,1)S(1)} %get-tuple-element.26), channel_id=1, source_target_pairs={{0,3},{1,2},{2,1},{3,0},{4,7},{5,6},{6,5},{7,4},{8,11},{9,10},{10,... | collective-permute-start | bytes 147464 | tf_op jit(solution)/shard_map/ppermute | solution.py:91
  34.2 3.3 %collective-permute-done.11.refs_11_ = bf16[96,256]{1,0:T(8,128)(2,1)S(1)} collective-permute-done((bf16[96,256]{1,0:T(8,128)(2,1)S(1)}, bf16[96,256]{1,0:T(8,128)(2,1)S(1)}, u32[]{:S(2)}, u32[]{:S(2)}) %collective-permute-start.11) | collective-permute-done | bytes 49184 | tf_op jit(solution)/shard_map/ppermute | solution.py:91
  37.5 0.0 collective-permute-done.4.refs_3_
  37.5 1.9 %gram.1 = (f32[768,512]{1,0:T(8,128)S(1)}, bf16[768,512]{1,0:T(8,128)(2,1)S(1)}) custom-call(bf16[128,512]{1,0:T(8,128)(2,1)S(1)} %get-tuple-element.21.refs_0_, bf16[128,512]{1,0:T(8,128)(2,1)S(1)} %get-tuple-element.22.refs_1_, bf16[128,512]{1,0:T(8,128)(2,1)S(1)} %collective-permute-done.3.refs_2_, bf16[128,512]{1,0:T(8,128)(2,1)S(1)} %collective-permute-done.4.refs_3_, ...), custom_call_target="tpu_custom_call" | custom-call | tf_op jit(solution)/shard_map/gram/pallas_call | solution.py:289
  39.4 0.1 collective-permute-start.12
  39.5 2.3 %collective-permute-done.12.other_ref = bf16[768,512]{1,0:T(8,128)(2,1)S(1)} collective-permute-done((bf16[768,512]{1,0:T(8,128)(2,1)S(1)}, bf16[768,512]{1,0:T(8,128)(2,1)S(1)}, u32[]{:S(2)}, u32[]{:S(2)}) %collective-permute-start.12) | collective-permute-done | bytes 786464 | tf_op jit(solution)/shard_map/ppermute | solution.py:91
  41.8 2.6 %inverse.1 = f32[768,512]{1,0:T(8,128)} custom-call(f32[768,512]{1,0:T(8,128)S(1)} %get-tuple-element.27.own_ref, bf16[768,512]{1,0:T(8,128)(2,1)S(1)} %collective-permute-done.12.other_ref, f32[512,512]{1,0:T(8,128)S(1)} %copy-done), custom_call_target="tpu_custom_call" | custom-call | tf_op jit(solution)/shard_map/inverse/pallas_call | solution.py:302
  (13 shorter events, 0.0 us)
Async XLA Ops:
  0.0 41.8 %copy-start = (f32[512,512]{1,0:T(8,128)S(1)}, f32[512,512]{1,0:T(8,128)}, u32[]{:S(2)}) copy-start(f32[512,512]{1,0:T(8,128)} %factor_ref.1) | copy-start | bytes 3145732
  0.1 1.0 %copy-start.1 = (bf16[64,1024]{1,0:T(8,128)(2,1)S(1)}, bf16[64,1024]{1,0:T(8,128)(2,1)}, u32[]{:S(2)}) copy-start(bf16[64,1024]{1,0:T(8,128)(2,1)} %jac_ref.1) | copy-start | bytes 393220
  1.1 0.8 %copy-start.2 = (bf16[64,512]{1,0:T(8,128)(2,1)S(1)}, bf16[64,512]{1,0:T(8,128)(2,1)}, u32[]{:S(2)}) copy-start(bf16[64,512]{1,0:T(8,128)(2,1)} %panel_ref.1) | copy-start | bytes 196612
  1.9 0.7 %copy-start.3 = (s32[2,4]{1,0:T(2,128)S(1)}, s32[2,4]{1,0:T(2,128)}, u32[]{:S(2)}) copy-start(s32[2,4]{1,0:T(2,128)} %lists_ref.1) | copy-start | bytes 100
  2.6 0.7 %copy-start.4 = (s32[2,4]{1,0:T(2,128)S(1)}, s32[2,4]{1,0:T(2,128)}, u32[]{:S(2)}) copy-start(s32[2,4]{1,0:T(2,128)} %masks_ref.1) | copy-start | bytes 100
  3.3 0.7 %copy-start.5 = (s32[96]{0:T(128)S(1)}, s32[96]{0:T(128)}, u32[]{:S(2)}) copy-start(s32[96]{0:T(128)} %order_ref.1) | copy-start | bytes 1156
  3.9 0.7 %copy-start.6 = (f32[64]{0:T(128)S(1)}, f32[64]{0:T(128)}, u32[]{:S(2)}) copy-start(f32[64]{0:T(128)} %param.9) | copy-start | bytes 772
  5.7 9.2 %collective-permute-start = (bf16[64,896]{1,0:T(8,128)(2,1)S(1)}, bf16[64,896]{1,0:T(8,128)(2,1)S(1)}, u32[]{:S(2)}, u32[]{:S(2)}) collective-permute-start(bf16[64,896]{1,0:T(8,128)(2,1)S(1)} %get-tuple-element.18), channel_id=1, source_target_pairs={{0,8},{1,9},{2,10},{3,11},{4,12},{5,13},{6,14},{7,15},{8,16},{9,17... | collective-permute-start | bytes 344072 | tf_op jit(solution)/shard_map/ppermute | solution.py:91
  8.8 10.2 %collective-permute-start.1 = (bf16[64,896]{1,0:T(8,128)(2,1)S(1)}, bf16[64,896]{1,0:T(8,128)(2,1)S(1)}, u32[]{:S(2)}, u32[]{:S(2)}) collective-permute-start(bf16[64,896]{1,0:T(8,128)(2,1)S(1)} %get-tuple-element.19), channel_id=1, source_target_pairs={{0,16},{1,17},{2,18},{3,19},{4,20},{5,21},{6,22},{7,23},{8,24},{9,... | collective-permute-start | bytes 344072 | tf_op jit(solution)/shard_map/ppermute | solution.py:91
  11.4 7.6 %collective-permute-start.2 = (bf16[64,896]{1,0:T(8,128)(2,1)S(1)}, bf16[64,896]{1,0:T(8,128)(2,1)S(1)}, u32[]{:S(2)}, u32[]{:S(2)}) collective-permute-start(bf16[64,896]{1,0:T(8,128)(2,1)S(1)} %get-tuple-element.20), channel_id=1, source_target_pairs={{0,24},{1,25},{2,26},{3,27},{4,28},{5,29},{6,30},{7,31},{8,0},{9,1... | collective-permute-start | bytes 344072 | tf_op jit(solution)/shard_map/ppermute | solution.py:91
  19.1 5.7 %collective-permute-start.3 = (bf16[128,512]{1,0:T(8,128)(2,1)S(1)}, bf16[128,512]{1,0:T(8,128)(2,1)S(1)}, u32[]{:S(2)}, u32[]{:S(2)}) collective-permute-start(bf16[128,512]{1,0:T(8,128)(2,1)S(1)} %get-tuple-element.21.refs_0_), channel_id=1, source_target_pairs={{0,1},{1,0},{2,3},{3,2},{4,5},{5,4},{6,7},{7,6},{8,9},{9,8},{10,11... | collective-permute-start | bytes 393224 | tf_op jit(solution)/shard_map/ppermute | solution.py:91
  20.7 6.4 %collective-permute-start.6 = (bf16[128,512]{1,0:T(8,128)(2,1)S(1)}, bf16[128,512]{1,0:T(8,128)(2,1)S(1)}, u32[]{:S(2)}, u32[]{:S(2)}) collective-permute-start(bf16[128,512]{1,0:T(8,128)(2,1)S(1)} %get-tuple-element.22.refs_1_), channel_id=1, source_target_pairs={{0,2},{1,3},{2,0},{3,1},{4,6},{5,7},{6,4},{7,5},{8,10},{9,11},{10,... | collective-permute-start | bytes 393224 | tf_op jit(solution)/shard_map/ppermute | solution.py:91
  22.3 6.2 %collective-permute-start.9 = (bf16[96,256]{1,0:T(8,128)(2,1)S(1)}, bf16[96,256]{1,0:T(8,128)(2,1)S(1)}, u32[]{:S(2)}, u32[]{:S(2)}) collective-permute-start(bf16[96,256]{1,0:T(8,128)(2,1)S(1)} %get-tuple-element.24), channel_id=1, source_target_pairs={{0,1},{1,0},{2,3},{3,2},{4,5},{5,4},{6,7},{7,6},{8,9},{9,8},{10,11... | collective-permute-start | bytes 147464 | tf_op jit(solution)/shard_map/ppermute | solution.py:91
  22.8 14.7 %collective-permute-start.5 = (bf16[128,512]{1,0:T(8,128)(2,1)S(1)}, bf16[128,512]{1,0:T(8,128)(2,1)S(1)}, u32[]{:S(2)}, u32[]{:S(2)}) collective-permute-start(bf16[128,512]{1,0:T(8,128)(2,1)S(1)} %get-tuple-element.21.refs_0_), channel_id=1, source_target_pairs={{0,2},{1,3},{2,0},{3,1},{4,6},{5,7},{6,4},{7,5},{8,10},{9,11},{10,... | collective-permute-start | bytes 393224 | tf_op jit(solution)/shard_map/ppermute | solution.py:91
  23.2 14.3 %collective-permute-start.4 = (bf16[128,512]{1,0:T(8,128)(2,1)S(1)}, bf16[128,512]{1,0:T(8,128)(2,1)S(1)}, u32[]{:S(2)}, u32[]{:S(2)}) collective-permute-start(bf16[128,512]{1,0:T(8,128)(2,1)S(1)} %get-tuple-element.22.refs_1_), channel_id=1, source_target_pairs={{0,1},{1,0},{2,3},{3,2},{4,5},{5,4},{6,7},{7,6},{8,9},{9,8},{10,11... | collective-permute-start | bytes 393224 | tf_op jit(solution)/shard_map/ppermute | solution.py:91
  24.8 12.7 %collective-permute-start.7 = (bf16[128,512]{1,0:T(8,128)(2,1)S(1)}, bf16[128,512]{1,0:T(8,128)(2,1)S(1)}, u32[]{:S(2)}, u32[]{:S(2)}) collective-permute-start(bf16[128,512]{1,0:T(8,128)(2,1)S(1)} %collective-permute-done.3.refs_2_), channel_id=1, source_target_pairs={{0,2},{1,3},{2,0},{3,1},{4,6},{5,7},{6,4},{7,5},{8,10},{9,11},{10,... | collective-permute-start | bytes 393224 | tf_op jit(solution)/shard_map/ppermute | solution.py:91
  27.1 10.5 %collective-permute-start.8 = (bf16[128,512]{1,0:T(8,128)(2,1)S(1)}, bf16[128,512]{1,0:T(8,128)(2,1)S(1)}, u32[]{:S(2)}, u32[]{:S(2)}) collective-permute-start(bf16[128,512]{1,0:T(8,128)(2,1)S(1)} %collective-permute-done.6.refs_5_), channel_id=1, source_target_pairs={{0,1},{1,0},{2,3},{3,2},{4,5},{5,4},{6,7},{7,6},{8,9},{9,8},{10,11... | collective-permute-start | bytes 393224 | tf_op jit(solution)/shard_map/ppermute | solution.py:91
  28.4 4.1 %collective-permute-start.10 = (bf16[96,256]{1,0:T(8,128)(2,1)S(1)}, bf16[96,256]{1,0:T(8,128)(2,1)S(1)}, u32[]{:S(2)}, u32[]{:S(2)}) collective-permute-start(bf16[96,256]{1,0:T(8,128)(2,1)S(1)} %get-tuple-element.25), channel_id=1, source_target_pairs={{0,2},{1,3},{2,0},{3,1},{4,6},{5,7},{6,4},{7,5},{8,10},{9,11},{10,... | collective-permute-start | bytes 147464 | tf_op jit(solution)/shard_map/ppermute | solution.py:91
  32.5 5.0 %collective-permute-start.11 = (bf16[96,256]{1,0:T(8,128)(2,1)S(1)}, bf16[96,256]{1,0:T(8,128)(2,1)S(1)}, u32[]{:S(2)}, u32[]{:S(2)}) collective-permute-start(bf16[96,256]{1,0:T(8,128)(2,1)S(1)} %get-tuple-element.26), channel_id=1, source_target_pairs={{0,3},{1,2},{2,1},{3,0},{4,7},{5,6},{6,5},{7,4},{8,11},{9,10},{10,... | collective-permute-start | bytes 147464 | tf_op jit(solution)/shard_map/ppermute | solution.py:91
  39.4 2.4 %collective-permute-start.12 = (bf16[768,512]{1,0:T(8,128)(2,1)S(1)}, bf16[768,512]{1,0:T(8,128)(2,1)S(1)}, u32[]{:S(2)}, u32[]{:S(2)}) collective-permute-start(bf16[768,512]{1,0:T(8,128)(2,1)S(1)} %get-tuple-element.28), channel_id=1, source_target_pairs={{0,4},{1,5},{2,6},{3,7},{4,0},{5,1},{6,2},{7,3},{8,12},{9,13},{10,... | collective-permute-start | bytes 2359304 | tf_op jit(solution)/shard_map/ppermute | solution.py:91

commit v4 on v3

v4 whole, which is shorter than its diff:
```python
import functools

import jax
import jax.numpy as jnp
from jax import lax
from jax.experimental import pallas as pl
from jax.experimental.pallas import tpu as pltpu
from jax.sharding import PartitionSpec as P

CAP = 2
GATHERED = 1 << 22


def tile_positions(tile_lists, tile_order):
    tile_count = tile_order.shape[0]
    matches = tile_lists[:, :, None] == tile_order[None, None, :]
    return jnp.sum(jnp.where(matches, jnp.arange(tile_count, dtype=jnp.int32), 0), axis=2)


def apply_inverse(tiles, factor_inverse):
    return jnp.einsum("ntp,qp->ntq", tiles, factor_inverse, precision=lax.Precision.HIGHEST)


def slot_codes(tile_lists, tile_masks, tile_order, owner_ids):
    block_count, slot_count = tile_lists.shape
    per_owner = tile_order.shape[0] // lax.axis_size("cols")
    positions = tile_positions(tile_lists, tile_order).reshape(-1)
    active = tile_masks.reshape(-1) == 1
    owner = positions // per_owner
    same = (owner[:, None] == owner[None, :]) & active[None, :]
    earlier = jnp.tril(jnp.ones(same.shape, bool), -1)
    rank = jnp.sum(same & earlier, axis=1)
    code = (
        (owner[None, None, :] == owner_ids[:, None, None])
        & (rank[None, None, :] == jnp.arange(CAP)[None, :, None])
        & active[None, None, :]
    )
    block = jnp.arange(block_count * slot_count) // slot_count
    place = positions % per_owner + per_owner * block
    return code, jnp.sum(jnp.where(code, place + 1, 0), axis=2) - 1


def local_general(jac, panel_jac, weights, tile_lists, tile_masks, tile_order, factor_inverse):
    block_count, slot_count = tile_lists.shape
    block_rows = jac.shape[0] // block_count
    tile_width = jac.shape[1] // slot_count
    slabs, owners = lax.axis_size("rows"), lax.axis_size("cols")
    devices = slabs * owners
    per_owner = tile_order.shape[0] // owners
    slab_width = tile_width // slabs
    bf16 = jnp.bfloat16
    weighted = (weights[:, None] * panel_jac).astype(bf16)
    code, places = slot_codes(tile_lists, tile_masks, tile_order, jnp.arange(owners))
    columns = jac.reshape(block_count, block_rows, slot_count, slabs, slab_width)
    chosen = code.astype(bf16).reshape(owners, CAP, block_count, slot_count)
    pieces = jnp.einsum("cjbk,bmkrt->rcjmt", chosen, columns, preferred_element_type=jnp.float32).astype(bf16)
    pieces = pieces.reshape(devices, -1)
    note = jnp.broadcast_to(places.astype(bf16)[None], (slabs, owners, CAP)).reshape(devices, CAP)
    note = jnp.pad(note, ((0, 0), (0, 128 - CAP)))
    sent = jnp.concatenate([pieces, note], axis=1)
    got = lax.all_to_all(sent, ("rows", "cols"), split_axis=0, concat_axis=0, tiled=True)
    size = pieces.shape[1]
    data = got[:, :size].reshape(devices, CAP, block_rows, slab_width)
    where = got[:, size : size + CAP].astype(jnp.int32)
    hot = (where[:, :, None] == jnp.arange(block_count * per_owner)).astype(bf16)
    hot = hot.reshape(devices, CAP, block_count, per_owner)
    mixed = jnp.einsum("djbn,djmt->dbmnt", hot, data, preferred_element_type=jnp.float32).astype(bf16)
    strips = max(1, devices * weighted.size * 2 // GATHERED)

    def strip_gram(strip):
        panels = lax.all_gather(strip, ("rows", "cols"), axis=0, tiled=True)
        panels = panels.reshape(devices, block_count, block_rows, -1)
        return jnp.einsum("dbmnt,dbmp->ntp", mixed, panels, preferred_element_type=jnp.float32)

    if strips == 1:
        gram = strip_gram(weighted)
    else:
        narrow = weighted.reshape(weighted.shape[0], strips, -1).swapaxes(0, 1)
        gram = jnp.moveaxis(lax.map(strip_gram, narrow), 0, 2)
        gram = gram.reshape(per_owner, slab_width, -1)
    return apply_inverse(gram, factor_inverse)


def shift(value, steps_z, flip_cols, flip_core=0):
    slabs, owners = lax.axis_size("rows"), lax.axis_size("cols")
    pairs = []
    for r in range(slabs):
        to_r = ((r // 2 + steps_z) % (slabs // 2)) * 2 + ((r % 2) ^ flip_core)
        for c in range(owners):
            pairs.append((r * owners + c, to_r * owners + (c ^ flip_cols)))
    return lax.ppermute(value, ("rows", "cols"), pairs)


def weigh_kernel(weights_hbm, panel_hbm, out_ref, weights_ref, panel_ref, sems):
    copies = [
        pltpu.make_async_copy(weights_hbm, weights_ref, sems.at[0]),
        pltpu.make_async_copy(panel_hbm, panel_ref, sems.at[1]),
    ]
    for copy in copies:
        copy.start()
    for copy in copies:
        copy.wait()
    rows = panel_ref.shape[0]
    row_ids = lax.broadcasted_iota(jnp.int32, (rows, rows), 0)
    lane_ids = lax.broadcasted_iota(jnp.int32, (rows, rows), 1)
    column = jnp.sum(jnp.where(row_ids == lane_ids, weights_ref[...], 0.0), axis=1, keepdims=True)
    out_ref[...] = (column * panel_ref[...].astype(jnp.float32)).astype(jnp.bfloat16)


def pack_kernel(sizes, lists_hbm, masks_hbm, order_hbm, jac_hbm, weighted_ref, *rest):
    layers, owners, per_owner, block_count, slot_count, block_rows, tile_width = sizes
    parcels = rest[:owners]
    lists_ref, masks_ref, order_ref, jac_ref, places_ref, turned_ref, sems = rest[owners:]
    copies = [
        pltpu.make_async_copy(order_hbm, order_ref, sems.at[0]),
        pltpu.make_async_copy(lists_hbm, lists_ref, sems.at[1]),
        pltpu.make_async_copy(masks_hbm, masks_ref, sems.at[2]),
        pltpu.make_async_copy(jac_hbm, jac_ref, sems.at[3]),
    ]
    for copy in copies:
        copy.start()
    f32, bf16 = jnp.float32, jnp.bfloat16
    panel_width = weighted_ref.shape[1]
    lane_group = CAP * block_rows
    slab = tile_width // layers
    part = slab // 2
    me_r, me_c = lax.axis_index("rows"), lax.axis_index("cols")
    me_z, me_core = me_r // 2, lax.rem(me_r, 2)
    for parcel in parcels[1:]:
        parcel[:, :panel_width] = weighted_ref[...]
    spots = [(parcel, panel_width if e else 0) for e, parcel in enumerate(parcels)]
    for copy in copies:
        copy.wait()

    for b in range(block_count):
        block = jac_ref[b * block_rows : (b + 1) * block_rows, :].astype(f32)
        start = b * slot_count * tile_width
        turned_ref[start : start + slot_count * tile_width, :] = block.T

    for i in range(order_ref.shape[0]):
        places_ref[order_ref[i]] = i
    slots = []
    for s in range(block_count * slot_count):
        b, k = divmod(s, slot_count)
        place = places_ref[lists_ref[b, k]]
        owner = jnp.int32(0)
        for c in range(1, owners):
            owner += (place >= c * per_owner).astype(jnp.int32)
        slots.append((place - owner * per_owner, jnp.where(masks_ref[b, k] == 1, owner, -1)))

    lane = lax.broadcasted_iota(jnp.int32, (16, CAP * block_count * block_rows), 1)
    for e, (parcel, start) in enumerate(spots):
        wanted = me_c ^ e
        found = jnp.int32(0)
        chosen = [jnp.int32(0)] * CAP
        codes = [jnp.int32(-1)] * CAP
        for s, (place, owner) in enumerate(slots):
            hit = owner == wanted
            for j in range(CAP):
                take = hit & (found == j)
                chosen[j] = jnp.where(take, s, chosen[j])
                codes[j] = jnp.where(take, place, codes[j])
            found += hit.astype(jnp.int32)
        note = jnp.full(lane.shape, -1, jnp.int32)
        for j in range(CAP):
            for b in range(block_count):
                at = (j * block_count + b) * block_rows
                here = (lane >= at) & (lane < at + block_rows)
                code = jnp.where(chosen[j] // slot_count == b, codes[j], -1)
                note = jnp.where(here, code, note)
        at = start + layers * lane_group
        parcel[:16, at : at + note.shape[1]] = note.astype(f32).astype(bf16)
        for k in range(layers):
            z = lax.rem(me_z + k, layers)
            for u in range(2):
                core = me_core ^ u
                for j in range(CAP):
                    first = pl.multiple_of(chosen[j] * tile_width + z * slab + core * part, part)
                    piece = turned_ref[pl.ds(first, part), :].astype(bf16)
                    to = start + k * lane_group + j * block_rows
                    parcel[u * part : (u + 1) * part, to : to + block_rows] = piece


def sort_kernel(sizes, starts, *refs):
    layers, owners, lane_group, wide = sizes
    parcels, line = refs[:owners], refs[owners : layers - 1 + owners]
    stacked, posts = refs[layers - 1 + owners], refs[layers + owners :]
    rows = parcels[0].shape[0]
    for k, ref in enumerate(line):
        stacked[k * rows : (k + 1) * rows, :] = ref[...]
    for e, (parcel, start) in enumerate(zip(parcels, starts)):
        at = start + layers * lane_group
        note = parcel[:16, at : at + wide]
        for k, post in enumerate(posts):
            piece = parcel[:, start + k * lane_group : start + (k + 1) * lane_group]
            post[:rows, e * lane_group : (e + 1) * lane_group] = piece
            low = rows + 16 * (e // 2)
            post[low : low + 16, (e % 2) * wide : (e % 2 + 1) * wide] = note


def cut_kernel(by_x_ref, by_y_ref, *refs):
    first_ref, second_ref = refs[-2:]
    half = first_ref.shape[0]
    first_ref[...] = by_x_ref[:half, :]
    second_ref[...] = by_y_ref[half:, :]


def place_kernel(sizes, *refs):
    layers, owners, per_owner, block_rows, block_count = sizes
    posts, (factor_ref, own_ref, other_ref, high_ref, low_ref) = refs[:layers], refs[layers:]
    f32, bf16 = jnp.float32, jnp.bfloat16
    high = factor_ref[...].astype(bf16)
    high_ref[...] = high
    low_ref[...] = (factor_ref[...] - high.astype(f32)).astype(bf16)
    rows = block_count * block_rows
    group, wide = CAP * block_rows, CAP * rows
    height = posts[0].shape[0] - 16 * (owners // 2)
    part = height // 2
    for e in range(owners):
        low = height + 16 * (e // 2)
        for h in range(layers // 2):
            pair = posts[2 * h : 2 * h + 2]
            codes = []
            for j in range(CAP):
                at = (e % 2) * wide + j * rows
                notes = [post[low : low + 16, at : at + rows].astype(f32) for post in pair]
                note = jnp.concatenate(notes, axis=1)
                codes.append(jnp.concatenate([note] * (part // 16), axis=0).astype(bf16))
            lanes = slice((e * layers + 2 * h) * rows, (e * layers + 2 * h + 2) * rows)
            for u, out_ref in ((0, own_ref), (1, other_ref)):
                columns = []
                for j in range(CAP):
                    at = e * group + j * block_rows
                    pieces = []
                    for post in pair:
                        piece = post[u * part : (u + 1) * part, at : at + block_rows].astype(f32)
                        pieces += [piece] * block_count
                    columns.append(jnp.concatenate(pieces, axis=1).astype(bf16))
                for n in range(per_owner):
                    placed = jnp.zeros(columns[0].shape, bf16)
                    for j in range(CAP):
                        placed = jnp.where(codes[j] == jnp.asarray(n, bf16), columns[j], placed)
                    out_ref[n * part : (n + 1) * part, lanes] = placed


def gram_kernel(parts, *refs):
    panels = refs[: len(parts)]
    placed_ref, high_ref, low_ref, out_ref, rows_ref = refs[len(parts) :]
    f32, bf16 = jnp.float32, jnp.bfloat16
    width = rows_ref.shape[1]
    at = 0
    for start, panel in zip(parts, panels):
        rows = panel.shape[0]
        rows_ref[at : at + rows, :] = panel[:, start : start + width]
        at += rows
    gram = jnp.dot(placed_ref[...], rows_ref[...], preferred_element_type=f32)
    gram_high = gram.astype(bf16)
    gram_low = (gram - gram_high.astype(f32)).astype(bf16)
    dims = (((1,), (1,)), ((), ()))
    half = width // 2
    for start, stop in ((0, half), (half, width)):
        high, low = high_ref[start:stop, :stop], low_ref[start:stop, :stop]
        a, b = gram_high[:, :stop], gram_low[:, :stop]
        total = lax.dot_general(a, low, dims, preferred_element_type=f32)
        total += lax.dot_general(b, high, dims, preferred_element_type=f32)
        total += lax.dot_general(a, high, dims, preferred_element_type=f32)
        out_ref[:, start:stop] = total.astype(out_ref.dtype)


def local(jac, panel_jac, weights, tile_lists, tile_masks, tile_order, factor_inverse):
    block_count, slot_count = tile_lists.shape
    rows, panel_width = panel_jac.shape
    block_rows = rows // block_count
    tile_width = jac.shape[1] // slot_count
    slabs, owners = lax.axis_size("rows"), lax.axis_size("cols")
    layers = slabs // 2
    per_owner = tile_order.shape[0] // owners
    slab_width = tile_width // slabs
    f32, bf16 = jnp.float32, jnp.bfloat16
    vmem, anywhere = pl.BlockSpec(memory_space=pltpu.VMEM), pl.BlockSpec(memory_space=pl.ANY)
    params = pltpu.CompilerParams(vmem_limit_bytes=48 << 20)
    shaped = jax.ShapeDtypeStruct

    def in_hbm(value):
        return pltpu.with_memory_space_constraint(value, pltpu.HBM)

    weighted = pl.pallas_call(
        weigh_kernel,
        out_shape=shaped((rows, panel_width), bf16),
        in_specs=[anywhere] * 2,
        out_specs=vmem,
        scratch_shapes=[
            pltpu.VMEM((1, rows), f32),
            pltpu.VMEM((rows, panel_width), bf16),
            pltpu.SemaphoreType.DMA((2,)),
        ],
        compiler_params=params,
        name="weigh",
    )(in_hbm(weights.reshape(1, rows)), in_hbm(panel_jac))
    line = [shift(weighted, k, 0) for k in range(1, layers)]

    lane_group = CAP * block_rows
    wide = CAP * rows
    sizes = (layers, owners, per_owner, block_count, slot_count, block_rows, tile_width)
    post = layers * lane_group + wide
    parcels = pl.pallas_call(
        functools.partial(pack_kernel, sizes),
        out_shape=[shaped((rows, post), bf16)] + [shaped((rows, panel_width + post), bf16)] * (owners - 1),
        in_specs=[anywhere] * 4 + [vmem],
        out_specs=[vmem] * owners,
        scratch_shapes=[
            pltpu.SMEM(tile_lists.shape, jnp.int32),
            pltpu.SMEM(tile_masks.shape, jnp.int32),
            pltpu.SMEM(tile_order.shape, jnp.int32),
            pltpu.VMEM(jac.shape, bf16),
            pltpu.SMEM(tile_order.shape, jnp.int32),
            pltpu.VMEM((block_count * slot_count * tile_width, block_rows), f32),
            pltpu.SemaphoreType.DMA((4,)),
        ],
        compiler_params=params,
        name="pack",
    )(in_hbm(tile_lists), in_hbm(tile_masks), in_hbm(tile_order), in_hbm(jac), weighted)
    parcels = [parcels[0]] + [shift(parcels[e], 0, e) for e in range(1, owners)]
    starts = [0] + [panel_width] * (owners - 1)

    height = 2 * slab_width
    letter = shaped((height + 16 * (owners // 2), max(owners * lane_group, 2 * wide)), bf16)
    others, *posts = pl.pallas_call(
        functools.partial(sort_kernel, (layers, owners, lane_group, wide), starts),
        out_shape=[shaped(((layers - 1) * rows, panel_width), bf16)] + [letter] * layers,
        in_specs=[vmem] * (layers - 1 + owners),
        out_specs=[vmem] * (layers + 1),
        compiler_params=params,
        name="sort",
    )(*parcels, *line)
    posts = [posts[0]] + [shift(posts[k], k, 0) for k in range(1, layers)]
    by_x, by_y = shift(others, 0, 1), shift(others, 0, 2)
    half = shaped((others.shape[0] // 2, panel_width), bf16)
    first, second = pl.pallas_call(
        cut_kernel,
        out_shape=[half] * 2,
        in_specs=[vmem] * 2 + [anywhere] * (layers - 1),
        out_specs=[vmem] * 2,
        compiler_params=params,
        name="cut",
    )(by_x, by_y, *posts[1:])
    across = [shift(first, 0, 2), shift(second, 0, 1)]

    count = per_owner * slab_width
    depth = layers * owners * rows
    own_placed, other_placed, high, low = pl.pallas_call(
        functools.partial(place_kernel, (layers, owners, per_owner, block_rows, block_count)),
        out_shape=[shaped((count, depth), bf16)] * 2 + [shaped(factor_inverse.shape, bf16)] * 2,
        in_specs=[vmem] * (layers + 1),
        out_specs=[vmem] * 4,
        compiler_params=params,
        name="place",
    )(*posts, factor_inverse)

    panels = [weighted, others, parcels[1], by_x, parcels[2], by_y, parcels[3], *across]
    parts = [0] * len(panels)

    def gram(placed, kind):
        return pl.pallas_call(
            functools.partial(gram_kernel, parts),
            out_shape=shaped((count, panel_width), kind),
            in_specs=[vmem] * (len(panels) + 3),
            out_specs=vmem,
            scratch_shapes=[pltpu.VMEM((depth, panel_width), bf16)],
            compiler_params=params,
            name="gram",
        )(*panels, placed, high, low)

    other = shift(gram(other_placed, bf16), 0, 0, 1)
    out = gram(own_placed, f32) + other.astype(f32)
    return out.reshape(per_owner, slab_width, panel_width)


def solution(mesh):
    in_specs = (
        P(("rows", "cols"), None),
        P(("rows", "cols"), None),
        P(("rows", "cols")),
        P(("rows", "cols"), None),
        P(("rows", "cols"), None),
        P(),
        P(),
    )
    out_specs = P("cols", "rows", None)
    body = local if (mesh.shape["rows"], mesh.shape["cols"]) == (8, 4) else local_general
    return jax.shard_map(body, mesh=mesh, in_specs=in_specs, out_specs=out_specs, check_vma=False)
```

time: 44.9 us -> 39.8 us (0.89)
  waiting for transfers between devices: 15.3 us -> 10.8 us
  local copies, waits for them, and re-layouts: 4.49 us -> 0.01 us
  Pallas kernels: 5.72 us -> 8.84 us
  other arithmetic: 0.08 us -> 1.38 us
    ppermute x13 -> x14, waiting for transfers between devices: 15.3 us -> 10.8 us  [shift(): return lax.ppermute(value, ('rows', 'cols'), pairs)]
    unnamed x14 -> x2, local copies, waits for them, and re-layouts: 4.49 us -> 0.01 us
    pallas_call x4 -> x7, Pallas kernels: 5.72 us -> 8.84 us  [the longest x2 4.69 us: gram(): pl.pallas_call(functools.partial(gram_kernel, parts), out_shape=shaped((c...]
    add x0 -> x1, other arithmetic: none -> 1.38 us  [local(): out = gram(own_placed, f32) + other.astype(f32)]
    ppermute x13 -> x14, starting transfers between devices: 18.7 us -> 18.5 us  [shift(): return lax.ppermute(value, ('rows', 'cols'), pairs)]
  transfers between devices with their start and end apart: 13 -> 14, of which waited for: 6 -> 6; matrix products, arithmetic and copies ran while one was open for 0% -> 0% of each run, Pallas kernels for 0% -> 13%
where the time goes in v4:
time: 39.8 us; the launch traced here: 39.6 us
  starting transfers between devices  18.5 us (46%)
  waiting for transfers between devices  10.8 us (27%)
  Pallas kernels  8.84 us (22%)
  other arithmetic  1.38 us (3%)
    ppermute x14, starting transfers between devices, shift(): return lax.ppermute(value, ('rows', 'cols'), pairs)  18.5 us
    ppermute x14, waiting for transfers between devices, shift(): return lax.ppermute(value, ('rows', 'cols'), pairs)  10.8 us
    pallas_call x2, Pallas kernels, gram(): pl.pallas_call(functools.partial(gram_kernel, parts), out_shape=shaped((c...  4.69 us
    pallas_call x1, Pallas kernels, local(): pl.pallas_call(functools.partial(place_kernel, (layers, owners, per_owner...  1.53 us
    pallas_call x1, Pallas kernels, local(): pl.pallas_call(functools.partial(pack_kernel, sizes), out_shape=[shaped((...  1.42 us
    add x1, other arithmetic, local(): out = gram(own_placed, f32) + other.astype(f32)  1.38 us
    pallas_call x1, Pallas kernels, local(): pl.pallas_call(weigh_kernel, out_shape=shaped((rows, panel_width), bf16),...  1.05 us
  transfers between devices with their start and end apart: 14, of which 6 were waited for; matrix products, arithmetic and copies ran while one was open for 0% of the time, Pallas kernels for 13%

profile of v4, /device:TPU:0, one launch (start us, length us, event | category | flops | bytes accessed | tf_op | source)
XLA Modules:
  0.0 39.6 jit_solution(8979818030602468246)
XLA Ops:
  0.0 1.0 %weigh.1.weighted_ref.refs_0_ = bf16[64,512]{1,0:T(8,128)(2,1)S(1)} custom-call(f32[1,64]{1,0:T(1,128)} %bitcast.2, bf16[64,512]{1,0:T(8,128)(2,1)} %panel_hbm.1), custom_call_target="tpu_custom_call" | custom-call | tf_op jit(solution)/shard_map/weigh/pallas_call | solution.py:287
  1.1 3.1 %collective-permute-start.3 = (bf16[64,512]{1,0:T(8,128)(2,1)S(1)}, bf16[64,512]{1,0:T(8,128)(2,1)S(1)}, u32[]{:S(2)}, u32[]{:S(2)}) collective-permute-start(bf16[64,512]{1,0:T(8,128)(2,1)S(1)} %weigh.1.weighted_ref.refs_0_), channel_id=1, source_target_pairs={{0,8},{1,9},{2,10},{3,11},{4,12},{5,13},{6,14},{7,15},{8,16},{9,17... | collective-permute-start | bytes 196616 | tf_op jit(solution)/shard_map/ppermute | solution.py:91
  4.1 1.4 %pack.1 = (bf16[64,384]{1,0:T(8,128)(2,1)S(1)}, bf16[64,896]{1,0:T(8,128)(2,1)S(1)}, bf16[64,896]{1,0:T(8,128)(2,1)S(1)}, bf16[64,896]{1,0:T(8,128)(2,1)S(1)}) custom-call(s32[2,4]{1,0:T(2,128)} %lists_hbm.1, s32[2,4]{1,0:T(2,128)} %masks_hbm.1, s32[96]{0:T(128)} %order_hbm.1, bf16[64,1024]{1,0:T(8,128)(2,1)} %jac_hbm.1, ...), custom_call_target="tpu_custom_call" | custom-call | tf_op jit(solution)/shard_map/pack/pallas_call | solution.py:306
  5.6 1.6 %collective-permute-start = (bf16[64,896]{1,0:T(8,128)(2,1)S(1)}, bf16[64,896]{1,0:T(8,128)(2,1)S(1)}, u32[]{:S(2)}, u32[]{:S(2)}) collective-permute-start(bf16[64,896]{1,0:T(8,128)(2,1)S(1)} %get-tuple-element.21), channel_id=1, source_target_pairs={{0,1},{1,0},{2,3},{3,2},{4,5},{5,4},{6,7},{7,6},{8,9},{9,8},{10,11... | collective-permute-start | bytes 344072 | tf_op jit(solution)/shard_map/ppermute | solution.py:91
  7.1 1.5 %collective-permute-start.1 = (bf16[64,896]{1,0:T(8,128)(2,1)S(1)}, bf16[64,896]{1,0:T(8,128)(2,1)S(1)}, u32[]{:S(2)}, u32[]{:S(2)}) collective-permute-start(bf16[64,896]{1,0:T(8,128)(2,1)S(1)} %get-tuple-element.22), channel_id=1, source_target_pairs={{0,2},{1,3},{2,0},{3,1},{4,6},{5,7},{6,4},{7,5},{8,10},{9,11},{10,... | collective-permute-start | bytes 344072 | tf_op jit(solution)/shard_map/ppermute | solution.py:91
  8.6 0.5 %collective-permute-start.2 = (bf16[64,896]{1,0:T(8,128)(2,1)S(1)}, bf16[64,896]{1,0:T(8,128)(2,1)S(1)}, u32[]{:S(2)}, u32[]{:S(2)}) collective-permute-start(bf16[64,896]{1,0:T(8,128)(2,1)S(1)} %get-tuple-element.23), channel_id=1, source_target_pairs={{0,3},{1,2},{2,1},{3,0},{4,7},{5,6},{6,5},{7,4},{8,11},{9,10},{10,... | collective-permute-start | bytes 344072 | tf_op jit(solution)/shard_map/ppermute | solution.py:91
  9.1 2.6 %collective-permute-start.4 = (bf16[64,512]{1,0:T(8,128)(2,1)S(1)}, bf16[64,512]{1,0:T(8,128)(2,1)S(1)}, u32[]{:S(2)}, u32[]{:S(2)}) collective-permute-start(bf16[64,512]{1,0:T(8,128)(2,1)S(1)} %weigh.1.weighted_ref.refs_0_), channel_id=1, source_target_pairs={{0,16},{1,17},{2,18},{3,19},{4,20},{5,21},{6,22},{7,23},{8,24},{9,... | collective-permute-start | bytes 196616 | tf_op jit(solution)/shard_map/ppermute | solution.py:91
  11.7 0.0 collective-permute-done.3.refs_4_
  11.7 1.3 %collective-permute-start.5 = (bf16[64,512]{1,0:T(8,128)(2,1)S(1)}, bf16[64,512]{1,0:T(8,128)(2,1)S(1)}, u32[]{:S(2)}, u32[]{:S(2)}) collective-permute-start(bf16[64,512]{1,0:T(8,128)(2,1)S(1)} %weigh.1.weighted_ref.refs_0_), channel_id=1, source_target_pairs={{0,24},{1,25},{2,26},{3,27},{4,28},{5,29},{6,30},{7,31},{8,0},{9,1... | collective-permute-start | bytes 196616 | tf_op jit(solution)/shard_map/ppermute | solution.py:91
  13.1 1.4 %collective-permute-done.4.refs_5_ = bf16[64,512]{1,0:T(8,128)(2,1)S(1)} collective-permute-done((bf16[64,512]{1,0:T(8,128)(2,1)S(1)}, bf16[64,512]{1,0:T(8,128)(2,1)S(1)}, u32[]{:S(2)}, u32[]{:S(2)}) %collective-permute-start.4) | collective-permute-done | bytes 65568 | tf_op jit(solution)/shard_map/ppermute | solution.py:91
  14.4 1.5 %collective-permute-done.5.refs_6_ = bf16[64,512]{1,0:T(8,128)(2,1)S(1)} collective-permute-done((bf16[64,512]{1,0:T(8,128)(2,1)S(1)}, bf16[64,512]{1,0:T(8,128)(2,1)S(1)}, u32[]{:S(2)}, u32[]{:S(2)}) %collective-permute-start.5) | collective-permute-done | bytes 65568 | tf_op jit(solution)/shard_map/ppermute | solution.py:91
  16.0 0.0 collective-permute-done.refs_1_.refs_2_
  16.0 0.0 collective-permute-done.1.refs_2_.refs_4_
  16.0 0.0 collective-permute-done.2.refs_3_.refs_6_
  16.0 0.1 sort.1
  16.1 1.6 %collective-permute-start.6 = (bf16[192,512]{1,0:T(8,128)(2,1)S(1)}, bf16[192,512]{1,0:T(8,128)(2,1)S(1)}, u32[]{:S(2)}, u32[]{:S(2)}) collective-permute-start(bf16[192,512]{1,0:T(8,128)(2,1)S(1)} %get-tuple-element.24.refs_1_), channel_id=1, source_target_pairs={{0,1},{1,0},{2,3},{3,2},{4,5},{5,4},{6,7},{7,6},{8,9},{9,8},{10,11... | collective-permute-start | bytes 589832 | tf_op jit(solution)/shard_map/ppermute | solution.py:91
  17.7 1.5 %collective-permute-start.7 = (bf16[192,512]{1,0:T(8,128)(2,1)S(1)}, bf16[192,512]{1,0:T(8,128)(2,1)S(1)}, u32[]{:S(2)}, u32[]{:S(2)}) collective-permute-start(bf16[192,512]{1,0:T(8,128)(2,1)S(1)} %get-tuple-element.24.refs_1_), channel_id=1, source_target_pairs={{0,2},{1,3},{2,0},{3,1},{4,6},{5,7},{6,4},{7,5},{8,10},{9,11},{10,... | collective-permute-start | bytes 589832 | tf_op jit(solution)/shard_map/ppermute | solution.py:91
  19.2 3.1 %collective-permute-start.10 = (bf16[96,256]{1,0:T(8,128)(2,1)S(1)}, bf16[96,256]{1,0:T(8,128)(2,1)S(1)}, u32[]{:S(2)}, u32[]{:S(2)}) collective-permute-start(bf16[96,256]{1,0:T(8,128)(2,1)S(1)} %get-tuple-element.27), channel_id=1, source_target_pairs={{0,24},{1,25},{2,26},{3,27},{4,28},{5,29},{6,30},{7,31},{8,0},{9,1... | collective-permute-start | bytes 147464 | tf_op jit(solution)/shard_map/ppermute | solution.py:91
  22.4 0.0 collective-permute-start.8
  22.4 0.6 %collective-permute-start.9 = (bf16[96,256]{1,0:T(8,128)(2,1)S(1)}, bf16[96,256]{1,0:T(8,128)(2,1)S(1)}, u32[]{:S(2)}, u32[]{:S(2)}) collective-permute-start(bf16[96,256]{1,0:T(8,128)(2,1)S(1)} %get-tuple-element.26), channel_id=1, source_target_pairs={{0,16},{1,17},{2,18},{3,19},{4,20},{5,21},{6,22},{7,23},{8,24},{9,... | collective-permute-start | bytes 147464 | tf_op jit(solution)/shard_map/ppermute | solution.py:91
  22.9 1.2 %collective-permute-done.10.refs_2_.refs_3_ = bf16[96,256]{1,0:T(8,128)(2,1)S(1)} collective-permute-done((bf16[96,256]{1,0:T(8,128)(2,1)S(1)}, bf16[96,256]{1,0:T(8,128)(2,1)S(1)}, u32[]{:S(2)}, u32[]{:S(2)}) %collective-permute-start.10) | collective-permute-done | bytes 49184 | tf_op jit(solution)/shard_map/ppermute | solution.py:91
  24.1 4.1 %collective-permute-done.8.refs_0_.refs_1_ = bf16[96,256]{1,0:T(8,128)(2,1)S(1)} collective-permute-done((bf16[96,256]{1,0:T(8,128)(2,1)S(1)}, bf16[96,256]{1,0:T(8,128)(2,1)S(1)}, u32[]{:S(2)}, u32[]{:S(2)}) %collective-permute-start.8) | collective-permute-done | bytes 49184 | tf_op jit(solution)/shard_map/ppermute | solution.py:91
  28.2 0.0 collective-permute-done.9.refs_1_.refs_2_
  28.3 0.6 %collective-permute-start.11 = (bf16[96,512]{1,0:T(8,128)(2,1)S(1)}, bf16[96,512]{1,0:T(8,128)(2,1)S(1)}, u32[]{:S(2)}, u32[]{:S(2)}) collective-permute-start(bf16[96,512]{1,0:T(8,128)(2,1)S(1)} %get-tuple-element.28), channel_id=1, source_target_pairs={{0,2},{1,3},{2,0},{3,1},{4,6},{5,7},{6,4},{7,5},{8,10},{9,11},{10,... | collective-permute-start | bytes 294920 | tf_op jit(solution)/shard_map/ppermute | solution.py:91
  28.9 0.5 %collective-permute-start.12 = (bf16[96,512]{1,0:T(8,128)(2,1)S(1)}, bf16[96,512]{1,0:T(8,128)(2,1)S(1)}, u32[]{:S(2)}, u32[]{:S(2)}) collective-permute-start(bf16[96,512]{1,0:T(8,128)(2,1)S(1)} %get-tuple-element.29), channel_id=1, source_target_pairs={{0,1},{1,0},{2,3},{3,2},{4,5},{5,4},{6,7},{7,6},{8,9},{9,8},{10,11... | collective-permute-start | bytes 294920 | tf_op jit(solution)/shard_map/ppermute | solution.py:91
  29.4 1.5 %place.1 = (bf16[768,1024]{1,0:T(8,128)(2,1)S(1)}, bf16[768,1024]{1,0:T(8,128)(2,1)S(1)}, bf16[512,512]{1,0:T(8,128)(2,1)S(1)}, bf16[512,512]{1,0:T(8,128)(2,1)S(1)}) custom-call(bf16[96,256]{1,0:T(8,128)(2,1)S(1)} %get-tuple-element.30.refs_0_, bf16[96,256]{1,0:T(8,128)(2,1)S(1)} %collective-permute-done.8.refs_0_.refs_1_, ...), custom_call_target="tpu_custom_call" | custom-call | tf_op jit(solution)/shard_map/place/pallas_call | solution.py:351
  30.9 2.0 %collective-permute-done.11.refs_7_ = bf16[96,512]{1,0:T(8,128)(2,1)S(1)} collective-permute-done((bf16[96,512]{1,0:T(8,128)(2,1)S(1)}, bf16[96,512]{1,0:T(8,128)(2,1)S(1)}, u32[]{:S(2)}, u32[]{:S(2)}) %collective-permute-start.11) | collective-permute-done | bytes 98336 | tf_op jit(solution)/shard_map/ppermute | solution.py:91
  33.0 0.5 %collective-permute-done.12.refs_8_ = bf16[96,512]{1,0:T(8,128)(2,1)S(1)} collective-permute-done((bf16[96,512]{1,0:T(8,128)(2,1)S(1)}, bf16[96,512]{1,0:T(8,128)(2,1)S(1)}, u32[]{:S(2)}, u32[]{:S(2)}) %collective-permute-start.12) | collective-permute-done | bytes 98336 | tf_op jit(solution)/shard_map/ppermute | solution.py:91
  33.5 2.3 %gram.3 = bf16[768,512]{1,0:T(8,128)(2,1)S(1)} custom-call(bf16[64,512]{1,0:T(8,128)(2,1)S(1)} %weigh.1.weighted_ref.refs_0_, bf16[192,512]{1,0:T(8,128)(2,1)S(1)} %get-tuple-element.24.refs_1_, bf16[64,896]{1,0:T(8,128)(2,1)S(1)} %collective-permute-done.refs_1_.refs_2_, bf16[192,512]{1,0:T(8,128)(2,1)S(1)} %collective-permute-done.6.by_x_ref.refs_3_, ...), custom_call_target="tpu_custom_call" | custom-call | tf_op jit(solution)/shard_map/gram/pallas_call | solution.py:364
  35.8 0.1 collective-permute-start.13
  35.9 2.3 %gram.2 = f32[768,512]{1,0:T(8,128)S(1)} custom-call(bf16[64,512]{1,0:T(8,128)(2,1)S(1)} %weigh.1.weighted_ref.refs_0_, bf16[192,512]{1,0:T(8,128)(2,1)S(1)} %get-tuple-element.24.refs_1_, bf16[64,896]{1,0:T(8,128)(2,1)S(1)} %collective-permute-done.refs_1_.refs_2_, bf16[192,512]{1,0:T(8,128)(2,1)S(1)} %collective-permute-done.6.by_x_ref.refs_3_, ...), custom_call_target="tpu_custom_call" | custom-call | tf_op jit(solution)/shard_map/gram/pallas_call | solution.py:364
  38.3 1.4 %convert_add_fusion = f32[768,512]{1,0:T(8,128)} fusion(f32[768,512]{1,0:T(8,128)S(1)} %gram.2, bf16[768,512]{1,0:T(8,128)(2,1)S(1)} %collective-permute-done.13), kind=kLoop, calls=%fused_computation | loop fusion | flops 786432 | bytes 3932160 | tf_op jit(solution)/shard_map/add | solution.py:375
  (6 shorter events, 0.0 us)
Async XLA Ops:
  0.0 29.4 %copy-start = (f32[512,512]{1,0:T(8,128)S(1)}, f32[512,512]{1,0:T(8,128)}, u32[]{:S(2)}) copy-start(f32[512,512]{1,0:T(8,128)} %refs_4_.1) | copy-start | bytes 3145732
  1.1 10.7 %collective-permute-start.3 = (bf16[64,512]{1,0:T(8,128)(2,1)S(1)}, bf16[64,512]{1,0:T(8,128)(2,1)S(1)}, u32[]{:S(2)}, u32[]{:S(2)}) collective-permute-start(bf16[64,512]{1,0:T(8,128)(2,1)S(1)} %weigh.1.weighted_ref.refs_0_), channel_id=1, source_target_pairs={{0,8},{1,9},{2,10},{3,11},{4,12},{5,13},{6,14},{7,15},{8,16},{9,17... | collective-permute-start | bytes 196616 | tf_op jit(solution)/shard_map/ppermute | solution.py:91
  5.6 10.4 %collective-permute-start = (bf16[64,896]{1,0:T(8,128)(2,1)S(1)}, bf16[64,896]{1,0:T(8,128)(2,1)S(1)}, u32[]{:S(2)}, u32[]{:S(2)}) collective-permute-start(bf16[64,896]{1,0:T(8,128)(2,1)S(1)} %get-tuple-element.21), channel_id=1, source_target_pairs={{0,1},{1,0},{2,3},{3,2},{4,5},{5,4},{6,7},{7,6},{8,9},{9,8},{10,11... | collective-permute-start | bytes 344072 | tf_op jit(solution)/shard_map/ppermute | solution.py:91
  7.1 8.9 %collective-permute-start.1 = (bf16[64,896]{1,0:T(8,128)(2,1)S(1)}, bf16[64,896]{1,0:T(8,128)(2,1)S(1)}, u32[]{:S(2)}, u32[]{:S(2)}) collective-permute-start(bf16[64,896]{1,0:T(8,128)(2,1)S(1)} %get-tuple-element.22), channel_id=1, source_target_pairs={{0,2},{1,3},{2,0},{3,1},{4,6},{5,7},{6,4},{7,5},{8,10},{9,11},{10,... | collective-permute-start | bytes 344072 | tf_op jit(solution)/shard_map/ppermute | solution.py:91
  8.6 7.3 %collective-permute-start.2 = (bf16[64,896]{1,0:T(8,128)(2,1)S(1)}, bf16[64,896]{1,0:T(8,128)(2,1)S(1)}, u32[]{:S(2)}, u32[]{:S(2)}) collective-permute-start(bf16[64,896]{1,0:T(8,128)(2,1)S(1)} %get-tuple-element.23), channel_id=1, source_target_pairs={{0,3},{1,2},{2,1},{3,0},{4,7},{5,6},{6,5},{7,4},{8,11},{9,10},{10,... | collective-permute-start | bytes 344072 | tf_op jit(solution)/shard_map/ppermute | solution.py:91
  9.1 5.3 %collective-permute-start.4 = (bf16[64,512]{1,0:T(8,128)(2,1)S(1)}, bf16[64,512]{1,0:T(8,128)(2,1)S(1)}, u32[]{:S(2)}, u32[]{:S(2)}) collective-permute-start(bf16[64,512]{1,0:T(8,128)(2,1)S(1)} %weigh.1.weighted_ref.refs_0_), channel_id=1, source_target_pairs={{0,16},{1,17},{2,18},{3,19},{4,20},{5,21},{6,22},{7,23},{8,24},{9,... | collective-permute-start | bytes 196616 | tf_op jit(solution)/shard_map/ppermute | solution.py:91
  11.7 4.3 %collective-permute-start.5 = (bf16[64,512]{1,0:T(8,128)(2,1)S(1)}, bf16[64,512]{1,0:T(8,128)(2,1)S(1)}, u32[]{:S(2)}, u32[]{:S(2)}) collective-permute-start(bf16[64,512]{1,0:T(8,128)(2,1)S(1)} %weigh.1.weighted_ref.refs_0_), channel_id=1, source_target_pairs={{0,24},{1,25},{2,26},{3,27},{4,28},{5,29},{6,30},{7,31},{8,0},{9,1... | collective-permute-start | bytes 196616 | tf_op jit(solution)/shard_map/ppermute | solution.py:91
  16.1 12.1 %collective-permute-start.6 = (bf16[192,512]{1,0:T(8,128)(2,1)S(1)}, bf16[192,512]{1,0:T(8,128)(2,1)S(1)}, u32[]{:S(2)}, u32[]{:S(2)}) collective-permute-start(bf16[192,512]{1,0:T(8,128)(2,1)S(1)} %get-tuple-element.24.refs_1_), channel_id=1, source_target_pairs={{0,1},{1,0},{2,3},{3,2},{4,5},{5,4},{6,7},{7,6},{8,9},{9,8},{10,11... | collective-permute-start | bytes 589832 | tf_op jit(solution)/shard_map/ppermute | solution.py:91
  17.7 10.6 %collective-permute-start.7 = (bf16[192,512]{1,0:T(8,128)(2,1)S(1)}, bf16[192,512]{1,0:T(8,128)(2,1)S(1)}, u32[]{:S(2)}, u32[]{:S(2)}) collective-permute-start(bf16[192,512]{1,0:T(8,128)(2,1)S(1)} %get-tuple-element.24.refs_1_), channel_id=1, source_target_pairs={{0,2},{1,3},{2,0},{3,1},{4,6},{5,7},{6,4},{7,5},{8,10},{9,11},{10,... | collective-permute-start | bytes 589832 | tf_op jit(solution)/shard_map/ppermute | solution.py:91
  19.2 4.9 %collective-permute-start.10 = (bf16[96,256]{1,0:T(8,128)(2,1)S(1)}, bf16[96,256]{1,0:T(8,128)(2,1)S(1)}, u32[]{:S(2)}, u32[]{:S(2)}) collective-permute-start(bf16[96,256]{1,0:T(8,128)(2,1)S(1)} %get-tuple-element.27), channel_id=1, source_target_pairs={{0,24},{1,25},{2,26},{3,27},{4,28},{5,29},{6,30},{7,31},{8,0},{9,1... | collective-permute-start | bytes 147464 | tf_op jit(solution)/shard_map/ppermute | solution.py:91
  22.4 5.9 %collective-permute-start.8 = (bf16[96,256]{1,0:T(8,128)(2,1)S(1)}, bf16[96,256]{1,0:T(8,128)(2,1)S(1)}, u32[]{:S(2)}, u32[]{:S(2)}) collective-permute-start(bf16[96,256]{1,0:T(8,128)(2,1)S(1)} %get-tuple-element.25), channel_id=1, source_target_pairs={{0,8},{1,9},{2,10},{3,11},{4,12},{5,13},{6,14},{7,15},{8,16},{9,17... | collective-permute-start | bytes 147464 | tf_op jit(solution)/shard_map/ppermute | solution.py:91
  22.4 5.9 %collective-permute-start.9 = (bf16[96,256]{1,0:T(8,128)(2,1)S(1)}, bf16[96,256]{1,0:T(8,128)(2,1)S(1)}, u32[]{:S(2)}, u32[]{:S(2)}) collective-permute-start(bf16[96,256]{1,0:T(8,128)(2,1)S(1)} %get-tuple-element.26), channel_id=1, source_target_pairs={{0,16},{1,17},{2,18},{3,19},{4,20},{5,21},{6,22},{7,23},{8,24},{9,... | collective-permute-start | bytes 147464 | tf_op jit(solution)/shard_map/ppermute | solution.py:91
  28.3 4.7 %collective-permute-start.11 = (bf16[96,512]{1,0:T(8,128)(2,1)S(1)}, bf16[96,512]{1,0:T(8,128)(2,1)S(1)}, u32[]{:S(2)}, u32[]{:S(2)}) collective-permute-start(bf16[96,512]{1,0:T(8,128)(2,1)S(1)} %get-tuple-element.28), channel_id=1, source_target_pairs={{0,2},{1,3},{2,0},{3,1},{4,6},{5,7},{6,4},{7,5},{8,10},{9,11},{10,... | collective-permute-start | bytes 294920 | tf_op jit(solution)/shard_map/ppermute | solution.py:91
  28.9 4.6 %collective-permute-start.12 = (bf16[96,512]{1,0:T(8,128)(2,1)S(1)}, bf16[96,512]{1,0:T(8,128)(2,1)S(1)}, u32[]{:S(2)}, u32[]{:S(2)}) collective-permute-start(bf16[96,512]{1,0:T(8,128)(2,1)S(1)} %get-tuple-element.29), channel_id=1, source_target_pairs={{0,1},{1,0},{2,3},{3,2},{4,5},{5,4},{6,7},{7,6},{8,9},{9,8},{10,11... | collective-permute-start | bytes 294920 | tf_op jit(solution)/shard_map/ppermute | solution.py:91
  35.8 2.4 %collective-permute-start.13 = (bf16[768,512]{1,0:T(8,128)(2,1)S(1)}, bf16[768,512]{1,0:T(8,128)(2,1)S(1)}, u32[]{:S(2)}, u32[]{:S(2)}) collective-permute-start(bf16[768,512]{1,0:T(8,128)(2,1)S(1)} %gram.3), channel_id=1, source_target_pairs={{0,4},{1,5},{2,6},{3,7},{4,0},{5,1},{6,2},{7,3},{8,12},{9,13},{10,... | collective-permute-start | bytes 2359304 | tf_op jit(solution)/shard_map/ppermute | solution.py:91

commit v5 on v4

--- a/solution.py
+++ b/solution.py
@@ -109,8 +109,7 @@
 
 def pack_kernel(sizes, lists_hbm, masks_hbm, order_hbm, jac_hbm, weighted_ref, *rest):
     layers, owners, per_owner, block_count, slot_count, block_rows, tile_width = sizes
-    parcels = rest[:owners]
-    lists_ref, masks_ref, order_ref, jac_ref, places_ref, turned_ref, sems = rest[owners:]
+    kept_ref, to_x_ref, to_y_ref, lists_ref, masks_ref, order_ref, jac_ref, places_ref, turned_ref, sems = rest
     copies = [
         pltpu.make_async_copy(order_hbm, order_ref, sems.at[0]),
         pltpu.make_async_copy(lists_hbm, lists_ref, sems.at[1]),
@@ -120,15 +119,15 @@
     for copy in copies:
         copy.start()
     f32, bf16 = jnp.float32, jnp.bfloat16
-    panel_width = weighted_ref.shape[1]
+    width = weighted_ref.shape[1]
     lane_group = CAP * block_rows
+    post = layers * lane_group
     slab = tile_width // layers
     part = slab // 2
     me_r, me_c = lax.axis_index("rows"), lax.axis_index("cols")
     me_z, me_core = me_r // 2, lax.rem(me_r, 2)
-    for parcel in parcels[1:]:
-        parcel[:, :panel_width] = weighted_ref[...]
-    spots = [(parcel, panel_width if e else 0) for e, parcel in enumerate(parcels)]
+    to_x_ref[:, :width] = weighted_ref[...]
+    to_y_ref[:, :width] = weighted_ref[...]
     for copy in copies:
         copy.wait()
 
@@ -148,7 +147,10 @@
             owner += (place >= c * per_owner).astype(jnp.int32)
         slots.append((place - owner * per_owner, jnp.where(masks_ref[b, k] == 1, owner, -1)))
 
-    lane = lax.broadcasted_iota(jnp.int32, (16, CAP * block_count * block_rows), 1)
+    shape = (16, CAP * block_count * block_rows)
+    lane, row = lax.broadcasted_iota(jnp.int32, shape, 1), lax.broadcasted_iota(jnp.int32, shape, 0)
+    notes = []
+    spots = [(kept_ref, 0), (to_x_ref, width), (to_y_ref, width), (to_x_ref, width + post)]
     for e, (parcel, start) in enumerate(spots):
         wanted = me_c ^ e
         found = jnp.int32(0)
@@ -161,15 +163,14 @@
                 chosen[j] = jnp.where(take, s, chosen[j])
                 codes[j] = jnp.where(take, place, codes[j])
             found += hit.astype(jnp.int32)
-        note = jnp.full(lane.shape, -1, jnp.int32)
+        note = jnp.full(shape, -1, jnp.int32)
         for j in range(CAP):
             for b in range(block_count):
                 at = (j * block_count + b) * block_rows
                 here = (lane >= at) & (lane < at + block_rows)
                 code = jnp.where(chosen[j] // slot_count == b, codes[j], -1)
                 note = jnp.where(here, code, note)
-        at = start + layers * lane_group
-        parcel[:16, at : at + note.shape[1]] = note.astype(f32).astype(bf16)
+        notes.append(note)
         for k in range(layers):
             z = lax.rem(me_z + k, layers)
             for u in range(2):
@@ -179,92 +180,149 @@
                     piece = turned_ref[pl.ds(first, part), :].astype(bf16)
                     to = start + k * lane_group + j * block_rows
                     parcel[u * part : (u + 1) * part, to : to + block_rows] = piece
-
-
-def sort_kernel(sizes, starts, *refs):
-    layers, owners, lane_group, wide = sizes
-    parcels, line = refs[:owners], refs[owners : layers - 1 + owners]
-    stacked, posts = refs[layers - 1 + owners], refs[layers + owners :]
-    rows = parcels[0].shape[0]
+    kept_ref[:16, post:] = notes[0].astype(f32).astype(bf16)
+    to_x_ref[:16, width + 2 * post :] = jnp.where(row == 0, notes[1], notes[3]).astype(f32).astype(bf16)
+    to_y_ref[:16, width + post :] = notes[2].astype(f32).astype(bf16)
+
+
+def row_of(block, i):
+    ids = lax.broadcasted_iota(jnp.int32, block.shape, 0)
+    return jnp.sum(jnp.where(ids == i, block.astype(jnp.float32), 0.0), axis=0, keepdims=True)
+
+
+def rows_from(notes):
+    ids = lax.broadcasted_iota(jnp.int32, (16, notes[0].shape[1]), 0)
+    block = jnp.full(ids.shape, -1.0, jnp.float32)
+    for i, note in enumerate(notes):
+        block = jnp.where(ids == i, note, block)
+    return block.astype(jnp.bfloat16)
+
+
+def sort_kernel(sizes, kept_ref, from_x_ref, from_y_ref, *refs):
+    layers, width, lane_group, wide = sizes
+    line, (stacked, *posts) = refs[: layers - 1], refs[layers - 1 :]
+    post = layers * lane_group
+    rows = kept_ref.shape[0]
     for k, ref in enumerate(line):
         stacked[k * rows : (k + 1) * rows, :] = ref[...]
-    for e, (parcel, start) in enumerate(zip(parcels, starts)):
-        at = start + layers * lane_group
-        note = parcel[:16, at : at + wide]
-        for k, post in enumerate(posts):
-            piece = parcel[:, start + k * lane_group : start + (k + 1) * lane_group]
-            post[:rows, e * lane_group : (e + 1) * lane_group] = piece
-            low = rows + 16 * (e // 2)
-            post[low : low + 16, (e % 2) * wide : (e % 2 + 1) * wide] = note
-
-
-def cut_kernel(by_x_ref, by_y_ref, *refs):
-    first_ref, second_ref = refs[-2:]
-    half = first_ref.shape[0]
-    first_ref[...] = by_x_ref[:half, :]
-    second_ref[...] = by_y_ref[half:, :]
-
-
-def place_kernel(sizes, *refs):
-    layers, owners, per_owner, block_rows, block_count = sizes
-    posts, (factor_ref, own_ref, other_ref, high_ref, low_ref) = refs[:layers], refs[layers:]
+    spots = [(kept_ref, 0), (from_x_ref, width), (from_y_ref, width), (from_x_ref, width + post)]
+    notes = [row_of(ref[:16, ref.shape[1] - wide :], int(e == 3)) for e, (ref, start) in enumerate(spots)]
+    block = rows_from(notes)
+    for k, out in enumerate(posts):
+        for e, (ref, start) in enumerate(spots):
+            piece = ref[:, start + k * lane_group : start + (k + 1) * lane_group]
+            out[:rows, e * lane_group : (e + 1) * lane_group] = piece
+        out[rows:, :wide] = block
+
+
+def cut_kernel(sizes, from_y_ref, by_x_ref, by_y_ref, *refs):
+    layers, width, lane_group, wide = sizes
+    posts, (to_y_ref, to_x_ref) = refs[:layers], refs[layers:]
+    rows = from_y_ref.shape[0]
+    half = by_x_ref.shape[0] // 2
+    part = rows // 2
+    post = layers * lane_group
+    to_y_ref[:half, :] = by_x_ref[:half, :]
+    for k, ref in enumerate(posts):
+        for u in range(2):
+            piece = ref[u * part : (u + 1) * part, 3 * lane_group : 4 * lane_group]
+            at = u * post + k * lane_group
+            to_y_ref[half : half + part, at : at + lane_group] = piece
+    notes = [row_of(ref[rows:, :wide], 3) for ref in posts]
+    to_y_ref[half + part :, :wide] = rows_from(notes)
+    to_x_ref[:rows, :] = from_y_ref[:, :width]
+    to_x_ref[rows:, :] = by_y_ref[half:, :]
+
+
+def place(out_ref, lanes, per_owner, pieces, notes, sizes):
+    block_count, block_rows = sizes
+    f32, bf16 = jnp.float32, jnp.bfloat16
+    part, rows = pieces[0].shape[0], block_count * block_rows
+    columns, codes = [], []
+    for j in range(CAP):
+        parts = []
+        for piece in pieces:
+            parts += [piece[:, j * block_rows : (j + 1) * block_rows].astype(f32)] * block_count
+        columns.append(jnp.concatenate(parts, axis=1).astype(bf16))
+        note = jnp.concatenate([note[:, j * rows : (j + 1) * rows] for note in notes], axis=1)
+        codes.append(jnp.broadcast_to(note, columns[j].shape).astype(bf16))
+    for n in range(per_owner):
+        placed = jnp.zeros(columns[0].shape, bf16)
+        for j in range(CAP):
+            placed = jnp.where(codes[j] == jnp.asarray(n, bf16), columns[j], placed)
+        out_ref[n * part : (n + 1) * part, lanes] = placed
+
+
+def near_kernel(sizes, *refs):
+    layers, owners, per_owner, block_count, block_rows = sizes
+    panels, posts, factor_ref = refs[: 2 * (owners - 1)], refs[2 * (owners - 1) :][:layers], refs[2 * owners - 2 + layers]
+    own_ref, other_ref, high_ref, low_ref, placed_ref, rows_ref = refs[2 * owners - 1 + layers :]
     f32, bf16 = jnp.float32, jnp.bfloat16
     high = factor_ref[...].astype(bf16)
     high_ref[...] = high
     low_ref[...] = (factor_ref[...] - high.astype(f32)).astype(bf16)
     rows = block_count * block_rows
     group, wide = CAP * block_rows, CAP * rows
-    height = posts[0].shape[0] - 16 * (owners // 2)
-    part = height // 2
-    for e in range(owners):
-        low = height + 16 * (e // 2)
-        for h in range(layers // 2):
-            pair = posts[2 * h : 2 * h + 2]
-            codes = []
-            for j in range(CAP):
-                at = (e % 2) * wide + j * rows
-                notes = [post[low : low + 16, at : at + rows].astype(f32) for post in pair]
-                note = jnp.concatenate(notes, axis=1)
-                codes.append(jnp.concatenate([note] * (part // 16), axis=0).astype(bf16))
-            lanes = slice((e * layers + 2 * h) * rows, (e * layers + 2 * h + 2) * rows)
-            for u, out_ref in ((0, own_ref), (1, other_ref)):
-                columns = []
-                for j in range(CAP):
-                    at = e * group + j * block_rows
-                    pieces = []
-                    for post in pair:
-                        piece = post[u * part : (u + 1) * part, at : at + block_rows].astype(f32)
-                        pieces += [piece] * block_count
-                    columns.append(jnp.concatenate(pieces, axis=1).astype(bf16))
-                for n in range(per_owner):
-                    placed = jnp.zeros(columns[0].shape, bf16)
-                    for j in range(CAP):
-                        placed = jnp.where(codes[j] == jnp.asarray(n, bf16), columns[j], placed)
-                    out_ref[n * part : (n + 1) * part, lanes] = placed
-
-
-def gram_kernel(parts, *refs):
-    panels = refs[: len(parts)]
-    placed_ref, high_ref, low_ref, out_ref, rows_ref = refs[len(parts) :]
-    f32, bf16 = jnp.float32, jnp.bfloat16
+    part = rows // 2
     width = rows_ref.shape[1]
     at = 0
-    for start, panel in zip(parts, panels):
-        rows = panel.shape[0]
-        rows_ref[at : at + rows, :] = panel[:, start : start + width]
-        at += rows
-    gram = jnp.dot(placed_ref[...], rows_ref[...], preferred_element_type=f32)
+    for panel in panels:
+        rows_ref[at : at + panel.shape[0], :] = panel[:, :width]
+        at += panel.shape[0]
+    for u, out_ref in ((1, other_ref), (0, own_ref)):
+        for e in range(owners - 1):
+            for h in range(layers // 2):
+                pair = posts[2 * h : 2 * h + 2]
+                pieces = [post[u * part : (u + 1) * part, e * group : (e + 1) * group] for post in pair]
+                notes = [row_of(post[rows:, :wide], e) for post in pair]
+                start = (e * layers + 2 * h) * rows
+                place(placed_ref, slice(start, start + 2 * rows), per_owner, pieces, notes, (block_count, block_rows))
+        out_ref[...] = jnp.dot(placed_ref[...], rows_ref[...], preferred_element_type=f32)
+
+
+def far_kernel(sizes, u, near_ref, by_y_ref, by_x_ref, high_ref, low_ref, out_ref, placed_ref, rows_ref):
+    layers, owners, per_owner, block_count, block_rows = sizes
+    f32, bf16 = jnp.float32, jnp.bfloat16
+    rows = block_count * block_rows
+    group, wide = CAP * block_rows, CAP * rows
+    part = rows // 2
+    width = rows_ref.shape[1]
+    half = (layers - 1) * rows // 2
+    rows_ref[:rows, :] = by_x_ref[:rows, :]
+    rows_ref[rows : rows + half, :] = by_y_ref[:half, :]
+    rows_ref[rows + half :, :] = by_x_ref[rows:, :]
+    for h in range(layers // 2):
+        pieces, notes = [], []
+        for k in (2 * h, 2 * h + 1):
+            at = (u * layers + k) * group
+            pieces.append(by_y_ref[half : half + part, at : at + group])
+            notes.append(row_of(by_y_ref[half + part :, :wide], k))
+        start = 2 * h * rows
+        place(placed_ref, slice(start, start + 2 * rows), per_owner, pieces, notes, (block_count, block_rows))
+    gram = near_ref[...] + jnp.dot(placed_ref[...], rows_ref[...], preferred_element_type=f32)
     gram_high = gram.astype(bf16)
     gram_low = (gram - gram_high.astype(f32)).astype(bf16)
     dims = (((1,), (1,)), ((), ()))
-    half = width // 2
-    for start, stop in ((0, half), (half, width)):
+    for start, stop in ((0, width // 2), (width // 2, width)):
         high, low = high_ref[start:stop, :stop], low_ref[start:stop, :stop]
         a, b = gram_high[:, :stop], gram_low[:, :stop]
         total = lax.dot_general(a, low, dims, preferred_element_type=f32)
         total += lax.dot_general(b, high, dims, preferred_element_type=f32)
         total += lax.dot_general(a, high, dims, preferred_element_type=f32)
         out_ref[:, start:stop] = total.astype(out_ref.dtype)
+
+
+def add_kernel(own_ref, other_ref, out_hbm, sum_ref, sems):
+    strips = sems.shape[0]
+    height = sum_ref.shape[0] // strips
+    copies = []
+    for i in range(strips):
+        here = pl.ds(i * height, height)
+        sum_ref[here, :] = own_ref[here, :] + other_ref[here, :].astype(jnp.float32)
+        copies.append(pltpu.make_async_copy(sum_ref.at[here, :], out_hbm.at[here, :], sems.at[i]))
+        copies[-1].start()
+    for copy in copies:
+        copy.wait()
 
 
 def local(jac, panel_jac, weights, tile_lists, tile_masks, tile_order, factor_inverse):
@@ -278,7 +336,7 @@
     slab_width = tile_width // slabs
     f32, bf16 = jnp.float32, jnp.bfloat16
     vmem, anywhere = pl.BlockSpec(memory_space=pltpu.VMEM), pl.BlockSpec(memory_space=pl.ANY)
-    params = pltpu.CompilerParams(vmem_limit_bytes=48 << 20)
+    params = pltpu.CompilerParams(vmem_limit_bytes=24 << 20)
     shaped = jax.ShapeDtypeStruct
 
     def in_hbm(value):
@@ -300,14 +358,17 @@
     line = [shift(weighted, k, 0) for k in range(1, layers)]
 
     lane_group = CAP * block_rows
+    post = layers * lane_group
     wide = CAP * rows
     sizes = (layers, owners, per_owner, block_count, slot_count, block_rows, tile_width)
-    post = layers * lane_group + wide
-    parcels = pl.pallas_call(
+    kept, to_x, to_y = pl.pallas_call(
         functools.partial(pack_kernel, sizes),
-        out_shape=[shaped((rows, post), bf16)] + [shaped((rows, panel_width + post), bf16)] * (owners - 1),
+        out_shape=[
+            shaped((rows, width), bf16)
+            for width in (post + wide, panel_width + 2 * post + wide, panel_width + post + wide)
+        ],
         in_specs=[anywhere] * 4 + [vmem],
-        out_specs=[vmem] * owners,
+        out_specs=[vmem] * 3,
         scratch_shapes=[
             pltpu.SMEM(tile_lists.shape, jnp.int32),
             pltpu.SMEM(tile_masks.shape, jnp.int32),
@@ -320,59 +381,74 @@
         compiler_params=params,
         name="pack",
     )(in_hbm(tile_lists), in_hbm(tile_masks), in_hbm(tile_order), in_hbm(jac), weighted)
-    parcels = [parcels[0]] + [shift(parcels[e], 0, e) for e in range(1, owners)]
-    starts = [0] + [panel_width] * (owners - 1)
-
-    height = 2 * slab_width
-    letter = shaped((height + 16 * (owners // 2), max(owners * lane_group, 2 * wide)), bf16)
+    from_x, from_y = shift(to_x, 0, 1), shift(to_y, 0, 2)
+
+    sizes = (layers, panel_width, lane_group, wide)
     others, *posts = pl.pallas_call(
-        functools.partial(sort_kernel, (layers, owners, lane_group, wide), starts),
-        out_shape=[shaped(((layers - 1) * rows, panel_width), bf16)] + [letter] * layers,
-        in_specs=[vmem] * (layers - 1 + owners),
+        functools.partial(sort_kernel, sizes),
+        out_shape=[shaped(((layers - 1) * rows, panel_width), bf16)]
+        + [shaped((rows + 16, owners * lane_group), bf16)] * layers,
+        in_specs=[vmem] * (layers + 2),
         out_specs=[vmem] * (layers + 1),
         compiler_params=params,
         name="sort",
-    )(*parcels, *line)
+    )(kept, from_x, from_y, *line)
     posts = [posts[0]] + [shift(posts[k], k, 0) for k in range(1, layers)]
     by_x, by_y = shift(others, 0, 1), shift(others, 0, 2)
-    half = shaped((others.shape[0] // 2, panel_width), bf16)
-    first, second = pl.pallas_call(
-        cut_kernel,
-        out_shape=[half] * 2,
-        in_specs=[vmem] * 2 + [anywhere] * (layers - 1),
+
+    half = others.shape[0] // 2
+    to_y, to_x = pl.pallas_call(
+        functools.partial(cut_kernel, sizes),
+        out_shape=[
+            shaped((half + rows // 2 + 16, panel_width), bf16),
+            shaped((rows + half, panel_width), bf16),
+        ],
+        in_specs=[vmem] * (layers + 3),
         out_specs=[vmem] * 2,
         compiler_params=params,
         name="cut",
-    )(by_x, by_y, *posts[1:])
-    across = [shift(first, 0, 2), shift(second, 0, 1)]
+    )(from_y, by_x, by_y, *posts)
+    across_y, across_x = shift(to_y, 0, 2), shift(to_x, 0, 1)
 
     count = per_owner * slab_width
-    depth = layers * owners * rows
-    own_placed, other_placed, high, low = pl.pallas_call(
-        functools.partial(place_kernel, (layers, owners, per_owner, block_rows, block_count)),
-        out_shape=[shaped((count, depth), bf16)] * 2 + [shaped(factor_inverse.shape, bf16)] * 2,
-        in_specs=[vmem] * (layers + 1),
+    depth = layers * rows
+    sizes = (layers, owners, per_owner, block_count, block_rows)
+    gram = shaped((count, panel_width), f32)
+    panels = [weighted, others, from_x, by_x, from_y, by_y]
+    own, other, high, low = pl.pallas_call(
+        functools.partial(near_kernel, sizes),
+        out_shape=[gram] * 2 + [shaped(factor_inverse.shape, bf16)] * 2,
+        in_specs=[vmem] * (len(panels) + layers + 1),
         out_specs=[vmem] * 4,
-        compiler_params=params,
-        name="place",
-    )(*posts, factor_inverse)
-
-    panels = [weighted, others, parcels[1], by_x, parcels[2], by_y, parcels[3], *across]
-    parts = [0] * len(panels)
-
-    def gram(placed, kind):
+        scratch_shapes=[
+            pltpu.VMEM((count, (owners - 1) * depth), bf16),
+            pltpu.VMEM(((owners - 1) * depth, panel_width), bf16),
+        ],
+        compiler_params=params,
+        name="near",
+    )(*panels, *posts, factor_inverse)
+
+    def far(u, near, kind):
         return pl.pallas_call(
-            functools.partial(gram_kernel, parts),
+            functools.partial(far_kernel, sizes, u),
             out_shape=shaped((count, panel_width), kind),
-            in_specs=[vmem] * (len(panels) + 3),
+            in_specs=[vmem] * 5,
             out_specs=vmem,
-            scratch_shapes=[pltpu.VMEM((depth, panel_width), bf16)],
+            scratch_shapes=[pltpu.VMEM((count, depth), bf16), pltpu.VMEM((depth, panel_width), bf16)],
             compiler_params=params,
-            name="gram",
-        )(*panels, placed, high, low)
-
-    other = shift(gram(other_placed, bf16), 0, 0, 1)
-    out = gram(own_placed, f32) + other.astype(f32)
+            name="far",
+        )(near, across_y, across_x, high, low)
+
+    other = shift(far(1, other, bf16), 0, 0, 1)
+    out = pl.pallas_call(
+        add_kernel,
+        out_shape=shaped((count, panel_width), f32),
+        in_specs=[vmem] * 2,
+        out_specs=anywhere,
+        scratch_shapes=[pltpu.VMEM((count, panel_width), f32), pltpu.SemaphoreType.DMA((4,))],
+        compiler_params=params,
+        name="add",
+    )(far(0, own, f32), other)
     return out.reshape(per_owner, slab_width, panel_width)
 
 

time: 39.8 us -> 36.5 us (0.917)
  other arithmetic: 1.38 us -> 0 us
  waiting for transfers between devices: 10.8 us -> 9.56 us
  starting transfers between devices: 18.5 us -> 18.1 us
    add x1 -> x0, other arithmetic: 1.38 us -> none  [local(): out = gram(own_placed, f32) + other.astype(f32)]
    ppermute x14 -> x13, waiting for transfers between devices: 10.8 us -> 9.56 us  [shift(): return lax.ppermute(value, ('rows', 'cols'), pairs)]
    ppermute x14 -> x13, starting transfers between devices: 18.5 us -> 18.1 us  [shift(): return lax.ppermute(value, ('rows', 'cols'), pairs)]
    pallas_call x5 -> x6, Pallas kernels: 6.36 us -> 6.19 us  [the longest x2 3.16 us: far(): pl.pallas_call(functools.partial(far_kernel, sizes, u), out_shape=shaped(...]
  transfers between devices with their start and end apart: 14 -> 13, of which waited for: 6 -> 8; matrix products, arithmetic and copies ran while one was open for 0% -> 0% of each run, Pallas kernels for 13% -> 9%
where the time goes in v5:
time: 36.5 us; the launch traced here: 36.3 us
  starting transfers between devices  18.1 us (50%)
  waiting for transfers between devices  9.56 us (26%)
  Pallas kernels  8.67 us (24%)
    ppermute x13, starting transfers between devices, shift(): return lax.ppermute(value, ('rows', 'cols'), pairs)  18.1 us
    ppermute x13, waiting for transfers between devices, shift(): return lax.ppermute(value, ('rows', 'cols'), pairs)  9.56 us
    pallas_call x2, Pallas kernels, far(): pl.pallas_call(functools.partial(far_kernel, sizes, u), out_shape=shaped(...  3.16 us
    pallas_call x1, Pallas kernels, local(): pl.pallas_call(functools.partial(near_kernel, sizes), out_shape=[gram] *...  1.62 us
    pallas_call x1, Pallas kernels, local(): pl.pallas_call(functools.partial(pack_kernel, sizes), out_shape=[shaped((...  1.43 us
    pallas_call x1, Pallas kernels, local(): pl.pallas_call(add_kernel, out_shape=shaped((count, panel_width), f32), i...  1.2 us
    pallas_call x1, Pallas kernels, local(): pl.pallas_call(weigh_kernel, out_shape=shaped((rows, panel_width), bf16),...  1.05 us
  transfers between devices with their start and end apart: 13, of which 8 were waited for; matrix products, arithmetic and copies ran while one was open for 0% of the time, Pallas kernels for 9%

profile of v5, /device:TPU:0, one launch (start us, length us, event | category | flops | bytes accessed | tf_op | source)
XLA Modules:
  0.0 36.3 jit_solution(1859628616357314356)
XLA Ops:
  0.0 1.0 %weigh.1.weighted_ref.refs_0_ = bf16[64,512]{1,0:T(8,128)(2,1)S(1)} custom-call(f32[1,64]{1,0:T(1,128)} %bitcast.2, bf16[64,512]{1,0:T(8,128)(2,1)} %panel_hbm.1), custom_call_target="tpu_custom_call" | custom-call | tf_op jit(solution)/shard_map/weigh/pallas_call | solution.py:345
  1.1 1.4 %pack.1 = (bf16[64,384]{1,0:T(8,128)(2,1)S(1)}, bf16[64,1152]{1,0:T(8,128)(2,1)S(1)}, bf16[64,896]{1,0:T(8,128)(2,1)S(1)}) custom-call(s32[2,4]{1,0:T(2,128)} %lists_hbm.1, s32[2,4]{1,0:T(2,128)} %masks_hbm.1, s32[96]{0:T(128)} %order_hbm.1, bf16[64,1024]{1,0:T(8,128)(2,1)} %jac_hbm.1, bf16[64,512]{1,0:T(8,128)(2,1)S(1)} %weigh.1.weighted_ref.refs_0_), custom_call_target="tpu_custom_call" | custom-call | tf_op jit(solution)/shard_map/pack/pallas_call | solution.py:364
  2.5 3.0 %collective-permute-start = (bf16[64,1152]{1,0:T(8,128)(2,1)S(1)}, bf16[64,1152]{1,0:T(8,128)(2,1)S(1)}, u32[]{:S(2)}, u32[]{:S(2)}) collective-permute-start(bf16[64,1152]{1,0:T(8,128)(2,1)S(1)} %get-tuple-element.20), channel_id=1, source_target_pairs={{0,1},{1,0},{2,3},{3,2},{4,5},{5,4},{6,7},{7,6},{8,9},{9,8},{10,11... | collective-permute-start | bytes 442376 | tf_op jit(solution)/shard_map/ppermute | solution.py:91
  5.5 1.5 %collective-permute-start.1 = (bf16[64,896]{1,0:T(8,128)(2,1)S(1)}, bf16[64,896]{1,0:T(8,128)(2,1)S(1)}, u32[]{:S(2)}, u32[]{:S(2)}) collective-permute-start(bf16[64,896]{1,0:T(8,128)(2,1)S(1)} %get-tuple-element.21), channel_id=1, source_target_pairs={{0,2},{1,3},{2,0},{3,1},{4,6},{5,7},{6,4},{7,5},{8,10},{9,11},{10,... | collective-permute-start | bytes 344072 | tf_op jit(solution)/shard_map/ppermute | solution.py:91
  7.0 1.6 %collective-permute-start.2 = (bf16[64,512]{1,0:T(8,128)(2,1)S(1)}, bf16[64,512]{1,0:T(8,128)(2,1)S(1)}, u32[]{:S(2)}, u32[]{:S(2)}) collective-permute-start(bf16[64,512]{1,0:T(8,128)(2,1)S(1)} %weigh.1.weighted_ref.refs_0_), channel_id=1, source_target_pairs={{0,8},{1,9},{2,10},{3,11},{4,12},{5,13},{6,14},{7,15},{8,16},{9,17... | collective-permute-start | bytes 196616 | tf_op jit(solution)/shard_map/ppermute | solution.py:91
  8.6 2.6 %collective-permute-start.3 = (bf16[64,512]{1,0:T(8,128)(2,1)S(1)}, bf16[64,512]{1,0:T(8,128)(2,1)S(1)}, u32[]{:S(2)}, u32[]{:S(2)}) collective-permute-start(bf16[64,512]{1,0:T(8,128)(2,1)S(1)} %weigh.1.weighted_ref.refs_0_), channel_id=1, source_target_pairs={{0,16},{1,17},{2,18},{3,19},{4,20},{5,21},{6,22},{7,23},{8,24},{9,... | collective-permute-start | bytes 196616 | tf_op jit(solution)/shard_map/ppermute | solution.py:91
  11.2 1.3 %collective-permute-start.4 = (bf16[64,512]{1,0:T(8,128)(2,1)S(1)}, bf16[64,512]{1,0:T(8,128)(2,1)S(1)}, u32[]{:S(2)}, u32[]{:S(2)}) collective-permute-start(bf16[64,512]{1,0:T(8,128)(2,1)S(1)} %weigh.1.weighted_ref.refs_0_), channel_id=1, source_target_pairs={{0,24},{1,25},{2,26},{3,27},{4,28},{5,29},{6,30},{7,31},{8,0},{9,1... | collective-permute-start | bytes 196616 | tf_op jit(solution)/shard_map/ppermute | solution.py:91
  12.5 1.3 %collective-permute-done.2.refs_0_ = bf16[64,512]{1,0:T(8,128)(2,1)S(1)} collective-permute-done((bf16[64,512]{1,0:T(8,128)(2,1)S(1)}, bf16[64,512]{1,0:T(8,128)(2,1)S(1)}, u32[]{:S(2)}, u32[]{:S(2)}) %collective-permute-start.2) | collective-permute-done | bytes 65568 | tf_op jit(solution)/shard_map/ppermute | solution.py:91
  13.8 1.9 %collective-permute-done.3.refs_1_ = bf16[64,512]{1,0:T(8,128)(2,1)S(1)} collective-permute-done((bf16[64,512]{1,0:T(8,128)(2,1)S(1)}, bf16[64,512]{1,0:T(8,128)(2,1)S(1)}, u32[]{:S(2)}, u32[]{:S(2)}) %collective-permute-start.3) | collective-permute-done | bytes 65568 | tf_op jit(solution)/shard_map/ppermute | solution.py:91
  15.8 0.1 collective-permute-done.4.refs_2_
  15.8 0.0 collective-permute-done.1.from_y_ref.refs_4_
  15.8 0.0 collective-permute-done.from_x_ref.refs_2_
  15.9 0.1 sort.1
  16.0 0.6 %collective-permute-start.5 = (bf16[192,512]{1,0:T(8,128)(2,1)S(1)}, bf16[192,512]{1,0:T(8,128)(2,1)S(1)}, u32[]{:S(2)}, u32[]{:S(2)}) collective-permute-start(bf16[192,512]{1,0:T(8,128)(2,1)S(1)} %get-tuple-element.22.refs_1_), channel_id=1, source_target_pairs={{0,1},{1,0},{2,3},{3,2},{4,5},{5,4},{6,7},{7,6},{8,9},{9,8},{10,11... | collective-permute-start | bytes 589832 | tf_op jit(solution)/shard_map/ppermute | solution.py:91
  16.6 0.4 %collective-permute-start.6 = (bf16[192,512]{1,0:T(8,128)(2,1)S(1)}, bf16[192,512]{1,0:T(8,128)(2,1)S(1)}, u32[]{:S(2)}, u32[]{:S(2)}) collective-permute-start(bf16[192,512]{1,0:T(8,128)(2,1)S(1)} %get-tuple-element.22.refs_1_), channel_id=1, source_target_pairs={{0,2},{1,3},{2,0},{3,1},{4,6},{5,7},{6,4},{7,5},{8,10},{9,11},{10,... | collective-permute-start | bytes 589832 | tf_op jit(solution)/shard_map/ppermute | solution.py:91
  17.0 1.1 %collective-permute-start.7 = (bf16[80,256]{1,0:T(8,128)(2,1)S(1)}, bf16[80,256]{1,0:T(8,128)(2,1)S(1)}, u32[]{:S(2)}, u32[]{:S(2)}) collective-permute-start(bf16[80,256]{1,0:T(8,128)(2,1)S(1)} %get-tuple-element.24), channel_id=1, source_target_pairs={{0,8},{1,9},{2,10},{3,11},{4,12},{5,13},{6,14},{7,15},{8,16},{9,17... | collective-permute-start | bytes 122888 | tf_op jit(solution)/shard_map/ppermute | solution.py:91
  18.2 2.2 %collective-permute-start.8 = (bf16[80,256]{1,0:T(8,128)(2,1)S(1)}, bf16[80,256]{1,0:T(8,128)(2,1)S(1)}, u32[]{:S(2)}, u32[]{:S(2)}) collective-permute-start(bf16[80,256]{1,0:T(8,128)(2,1)S(1)} %get-tuple-element.25), channel_id=1, source_target_pairs={{0,16},{1,17},{2,18},{3,19},{4,20},{5,21},{6,22},{7,23},{8,24},{9,... | collective-permute-start | bytes 122888 | tf_op jit(solution)/shard_map/ppermute | solution.py:91
  20.4 0.5 %collective-permute-start.9 = (bf16[80,256]{1,0:T(8,128)(2,1)S(1)}, bf16[80,256]{1,0:T(8,128)(2,1)S(1)}, u32[]{:S(2)}, u32[]{:S(2)}) collective-permute-start(bf16[80,256]{1,0:T(8,128)(2,1)S(1)} %get-tuple-element.26), channel_id=1, source_target_pairs={{0,24},{1,25},{2,26},{3,27},{4,28},{5,29},{6,30},{7,31},{8,0},{9,1... | collective-permute-start | bytes 122888 | tf_op jit(solution)/shard_map/ppermute | solution.py:91
  20.9 2.0 %collective-permute-done.7.refs_7_.refs_1_ = bf16[80,256]{1,0:T(8,128)(2,1)S(1)} collective-permute-done((bf16[80,256]{1,0:T(8,128)(2,1)S(1)}, bf16[80,256]{1,0:T(8,128)(2,1)S(1)}, u32[]{:S(2)}, u32[]{:S(2)}) %collective-permute-start.7) | collective-permute-done | bytes 40992 | tf_op jit(solution)/shard_map/ppermute | solution.py:91
  22.8 0.9 %collective-permute-done.8.refs_8_.refs_2_ = bf16[80,256]{1,0:T(8,128)(2,1)S(1)} collective-permute-done((bf16[80,256]{1,0:T(8,128)(2,1)S(1)}, bf16[80,256]{1,0:T(8,128)(2,1)S(1)}, u32[]{:S(2)}, u32[]{:S(2)}) %collective-permute-start.8) | collective-permute-done | bytes 40992 | tf_op jit(solution)/shard_map/ppermute | solution.py:91
  23.7 0.7 %collective-permute-done.9.refs_9_.refs_3_ = bf16[80,256]{1,0:T(8,128)(2,1)S(1)} collective-permute-done((bf16[80,256]{1,0:T(8,128)(2,1)S(1)}, bf16[80,256]{1,0:T(8,128)(2,1)S(1)}, u32[]{:S(2)}, u32[]{:S(2)}) %collective-permute-start.9) | collective-permute-done | bytes 40992 | tf_op jit(solution)/shard_map/ppermute | solution.py:91
  24.4 0.0 collective-permute-done.5.refs_3_.by_x_ref
  24.4 0.1 cut.1
  24.5 1.6 %collective-permute-start.11 = (bf16[160,512]{1,0:T(8,128)(2,1)S(1)}, bf16[160,512]{1,0:T(8,128)(2,1)S(1)}, u32[]{:S(2)}, u32[]{:S(2)}) collective-permute-start(bf16[160,512]{1,0:T(8,128)(2,1)S(1)} %get-tuple-element.29), channel_id=1, source_target_pairs={{0,1},{1,0},{2,3},{3,2},{4,5},{5,4},{6,7},{7,6},{8,9},{9,8},{10,11... | collective-permute-start | bytes 491528 | tf_op jit(solution)/shard_map/ppermute | solution.py:91
  26.1 1.5 %collective-permute-start.10 = (bf16[144,512]{1,0:T(8,128)(2,1)S(1)}, bf16[144,512]{1,0:T(8,128)(2,1)S(1)}, u32[]{:S(2)}, u32[]{:S(2)}) collective-permute-start(bf16[144,512]{1,0:T(8,128)(2,1)S(1)} %get-tuple-element.28), channel_id=1, source_target_pairs={{0,2},{1,3},{2,0},{3,1},{4,6},{5,7},{6,4},{7,5},{8,10},{9,11},{10,... | collective-permute-start | bytes 442376 | tf_op jit(solution)/shard_map/ppermute | solution.py:91
  27.6 1.6 %near.1 = (f32[768,512]{1,0:T(8,128)S(1)}, f32[768,512]{1,0:T(8,128)S(1)}, bf16[512,512]{1,0:T(8,128)(2,1)S(1)}, bf16[512,512]{1,0:T(8,128)(2,1)S(1)}) custom-call(bf16[64,512]{1,0:T(8,128)(2,1)S(1)} %weigh.1.weighted_ref.refs_0_, bf16[192,512]{1,0:T(8,128)(2,1)S(1)} %get-tuple-element.22.refs_1_, ...), custom_call_target="tpu_custom_call" | custom-call | tf_op jit(solution)/shard_map/near/pallas_call | solution.py:418
  29.2 2.0 %collective-permute-done.10.by_y_ref = bf16[144,512]{1,0:T(8,128)(2,1)S(1)} collective-permute-done((bf16[144,512]{1,0:T(8,128)(2,1)S(1)}, bf16[144,512]{1,0:T(8,128)(2,1)S(1)}, u32[]{:S(2)}, u32[]{:S(2)}) %collective-permute-start.10) | collective-permute-done | bytes 147488 | tf_op jit(solution)/shard_map/ppermute | solution.py:91
  31.2 1.6 %far.3 = bf16[768,512]{1,0:T(8,128)(2,1)S(1)} custom-call(f32[768,512]{1,0:T(8,128)S(1)} %get-tuple-element.32.near_ref, bf16[144,512]{1,0:T(8,128)(2,1)S(1)} %collective-permute-done.10.by_y_ref, bf16[160,512]{1,0:T(8,128)(2,1)S(1)} %collective-permute-done.11.by_x_ref, bf16[512,512]{1,0:T(8,128)(2,1)S(1)} %get-tuple-element.30.high_ref, ...), custom_call_target="tpu_custom_call" | custom-call | tf_op jit(solution)/shard_map/far/pallas_call | solution.py:432
  32.8 0.1 collective-permute-start.12
  32.9 1.6 %far.2.own_ref = f32[768,512]{1,0:T(8,128)S(1)} custom-call(f32[768,512]{1,0:T(8,128)S(1)} %get-tuple-element.27.near_ref, bf16[144,512]{1,0:T(8,128)(2,1)S(1)} %collective-permute-done.10.by_y_ref, bf16[160,512]{1,0:T(8,128)(2,1)S(1)} %collective-permute-done.11.by_x_ref, bf16[512,512]{1,0:T(8,128)(2,1)S(1)} %get-tuple-element.30.high_ref, ...), custom_call_target="tpu_custom_call" | custom-call | tf_op jit(solution)/shard_map/far/pallas_call | solution.py:432
  34.5 0.7 %collective-permute-done.12.other_ref = bf16[768,512]{1,0:T(8,128)(2,1)S(1)} collective-permute-done((bf16[768,512]{1,0:T(8,128)(2,1)S(1)}, bf16[768,512]{1,0:T(8,128)(2,1)S(1)}, u32[]{:S(2)}, u32[]{:S(2)}) %collective-permute-start.12) | collective-permute-done | bytes 786464 | tf_op jit(solution)/shard_map/ppermute | solution.py:91
  35.1 1.2 %add.1 = f32[768,512]{1,0:T(8,128)} custom-call(f32[768,512]{1,0:T(8,128)S(1)} %far.2.own_ref, bf16[768,512]{1,0:T(8,128)(2,1)S(1)} %collective-permute-done.12.other_ref), custom_call_target="tpu_custom_call" | custom-call | tf_op jit(solution)/shard_map/add/pallas_call | solution.py:443
  (4 shorter events, 0.0 us)
Async XLA Ops:
  0.0 27.6 %copy-start = (f32[512,512]{1,0:T(8,128)S(1)}, f32[512,512]{1,0:T(8,128)}, u32[]{:S(2)}) copy-start(f32[512,512]{1,0:T(8,128)} %refs_10_.1) | copy-start | bytes 3145732
  2.5 13.4 %collective-permute-start = (bf16[64,1152]{1,0:T(8,128)(2,1)S(1)}, bf16[64,1152]{1,0:T(8,128)(2,1)S(1)}, u32[]{:S(2)}, u32[]{:S(2)}) collective-permute-start(bf16[64,1152]{1,0:T(8,128)(2,1)S(1)} %get-tuple-element.20), channel_id=1, source_target_pairs={{0,1},{1,0},{2,3},{3,2},{4,5},{5,4},{6,7},{7,6},{8,9},{9,8},{10,11... | collective-permute-start | bytes 442376 | tf_op jit(solution)/shard_map/ppermute | solution.py:91
  5.5 10.3 %collective-permute-start.1 = (bf16[64,896]{1,0:T(8,128)(2,1)S(1)}, bf16[64,896]{1,0:T(8,128)(2,1)S(1)}, u32[]{:S(2)}, u32[]{:S(2)}) collective-permute-start(bf16[64,896]{1,0:T(8,128)(2,1)S(1)} %get-tuple-element.21), channel_id=1, source_target_pairs={{0,2},{1,3},{2,0},{3,1},{4,6},{5,7},{6,4},{7,5},{8,10},{9,11},{10,... | collective-permute-start | bytes 344072 | tf_op jit(solution)/shard_map/ppermute | solution.py:91
  7.0 6.8 %collective-permute-start.2 = (bf16[64,512]{1,0:T(8,128)(2,1)S(1)}, bf16[64,512]{1,0:T(8,128)(2,1)S(1)}, u32[]{:S(2)}, u32[]{:S(2)}) collective-permute-start(bf16[64,512]{1,0:T(8,128)(2,1)S(1)} %weigh.1.weighted_ref.refs_0_), channel_id=1, source_target_pairs={{0,8},{1,9},{2,10},{3,11},{4,12},{5,13},{6,14},{7,15},{8,16},{9,17... | collective-permute-start | bytes 196616 | tf_op jit(solution)/shard_map/ppermute | solution.py:91
  8.6 7.2 %collective-permute-start.3 = (bf16[64,512]{1,0:T(8,128)(2,1)S(1)}, bf16[64,512]{1,0:T(8,128)(2,1)S(1)}, u32[]{:S(2)}, u32[]{:S(2)}) collective-permute-start(bf16[64,512]{1,0:T(8,128)(2,1)S(1)} %weigh.1.weighted_ref.refs_0_), channel_id=1, source_target_pairs={{0,16},{1,17},{2,18},{3,19},{4,20},{5,21},{6,22},{7,23},{8,24},{9,... | collective-permute-start | bytes 196616 | tf_op jit(solution)/shard_map/ppermute | solution.py:91
  11.2 4.7 %collective-permute-start.4 = (bf16[64,512]{1,0:T(8,128)(2,1)S(1)}, bf16[64,512]{1,0:T(8,128)(2,1)S(1)}, u32[]{:S(2)}, u32[]{:S(2)}) collective-permute-start(bf16[64,512]{1,0:T(8,128)(2,1)S(1)} %weigh.1.weighted_ref.refs_0_), channel_id=1, source_target_pairs={{0,24},{1,25},{2,26},{3,27},{4,28},{5,29},{6,30},{7,31},{8,0},{9,1... | collective-permute-start | bytes 196616 | tf_op jit(solution)/shard_map/ppermute | solution.py:91
  16.0 8.4 %collective-permute-start.5 = (bf16[192,512]{1,0:T(8,128)(2,1)S(1)}, bf16[192,512]{1,0:T(8,128)(2,1)S(1)}, u32[]{:S(2)}, u32[]{:S(2)}) collective-permute-start(bf16[192,512]{1,0:T(8,128)(2,1)S(1)} %get-tuple-element.22.refs_1_), channel_id=1, source_target_pairs={{0,1},{1,0},{2,3},{3,2},{4,5},{5,4},{6,7},{7,6},{8,9},{9,8},{10,11... | collective-permute-start | bytes 589832 | tf_op jit(solution)/shard_map/ppermute | solution.py:91
  16.6 7.8 %collective-permute-start.6 = (bf16[192,512]{1,0:T(8,128)(2,1)S(1)}, bf16[192,512]{1,0:T(8,128)(2,1)S(1)}, u32[]{:S(2)}, u32[]{:S(2)}) collective-permute-start(bf16[192,512]{1,0:T(8,128)(2,1)S(1)} %get-tuple-element.22.refs_1_), channel_id=1, source_target_pairs={{0,2},{1,3},{2,0},{3,1},{4,6},{5,7},{6,4},{7,5},{8,10},{9,11},{10,... | collective-permute-start | bytes 589832 | tf_op jit(solution)/shard_map/ppermute | solution.py:91
  17.0 5.8 %collective-permute-start.7 = (bf16[80,256]{1,0:T(8,128)(2,1)S(1)}, bf16[80,256]{1,0:T(8,128)(2,1)S(1)}, u32[]{:S(2)}, u32[]{:S(2)}) collective-permute-start(bf16[80,256]{1,0:T(8,128)(2,1)S(1)} %get-tuple-element.24), channel_id=1, source_target_pairs={{0,8},{1,9},{2,10},{3,11},{4,12},{5,13},{6,14},{7,15},{8,16},{9,17... | collective-permute-start | bytes 122888 | tf_op jit(solution)/shard_map/ppermute | solution.py:91
  18.2 5.5 %collective-permute-start.8 = (bf16[80,256]{1,0:T(8,128)(2,1)S(1)}, bf16[80,256]{1,0:T(8,128)(2,1)S(1)}, u32[]{:S(2)}, u32[]{:S(2)}) collective-permute-start(bf16[80,256]{1,0:T(8,128)(2,1)S(1)} %get-tuple-element.25), channel_id=1, source_target_pairs={{0,16},{1,17},{2,18},{3,19},{4,20},{5,21},{6,22},{7,23},{8,24},{9,... | collective-permute-start | bytes 122888 | tf_op jit(solution)/shard_map/ppermute | solution.py:91
  20.4 4.0 %collective-permute-start.9 = (bf16[80,256]{1,0:T(8,128)(2,1)S(1)}, bf16[80,256]{1,0:T(8,128)(2,1)S(1)}, u32[]{:S(2)}, u32[]{:S(2)}) collective-permute-start(bf16[80,256]{1,0:T(8,128)(2,1)S(1)} %get-tuple-element.26), channel_id=1, source_target_pairs={{0,24},{1,25},{2,26},{3,27},{4,28},{5,29},{6,30},{7,31},{8,0},{9,1... | collective-permute-start | bytes 122888 | tf_op jit(solution)/shard_map/ppermute | solution.py:91
  24.5 6.7 %collective-permute-start.11 = (bf16[160,512]{1,0:T(8,128)(2,1)S(1)}, bf16[160,512]{1,0:T(8,128)(2,1)S(1)}, u32[]{:S(2)}, u32[]{:S(2)}) collective-permute-start(bf16[160,512]{1,0:T(8,128)(2,1)S(1)} %get-tuple-element.29), channel_id=1, source_target_pairs={{0,1},{1,0},{2,3},{3,2},{4,5},{5,4},{6,7},{7,6},{8,9},{9,8},{10,11... | collective-permute-start | bytes 491528 | tf_op jit(solution)/shard_map/ppermute | solution.py:91
  26.1 5.1 %collective-permute-start.10 = (bf16[144,512]{1,0:T(8,128)(2,1)S(1)}, bf16[144,512]{1,0:T(8,128)(2,1)S(1)}, u32[]{:S(2)}, u32[]{:S(2)}) collective-permute-start(bf16[144,512]{1,0:T(8,128)(2,1)S(1)} %get-tuple-element.28), channel_id=1, source_target_pairs={{0,2},{1,3},{2,0},{3,1},{4,6},{5,7},{6,4},{7,5},{8,10},{9,11},{10,... | collective-permute-start | bytes 442376 | tf_op jit(solution)/shard_map/ppermute | solution.py:91
  32.8 2.4 %collective-permute-start.12 = (bf16[768,512]{1,0:T(8,128)(2,1)S(1)}, bf16[768,512]{1,0:T(8,128)(2,1)S(1)}, u32[]{:S(2)}, u32[]{:S(2)}) collective-permute-start(bf16[768,512]{1,0:T(8,128)(2,1)S(1)} %far.3), channel_id=1, source_target_pairs={{0,4},{1,5},{2,6},{3,7},{4,0},{5,1},{6,2},{7,3},{8,12},{9,13},{10,... | collective-permute-start | bytes 2359304 | tf_op jit(solution)/shard_map/ppermute | solution.py:91

commit v6 on v5

--- a/solution.py
+++ b/solution.py
@@ -91,45 +91,38 @@
     return lax.ppermute(value, ("rows", "cols"), pairs)
 
 
-def weigh_kernel(weights_hbm, panel_hbm, out_ref, weights_ref, panel_ref, sems):
-    copies = [
-        pltpu.make_async_copy(weights_hbm, weights_ref, sems.at[0]),
-        pltpu.make_async_copy(panel_hbm, panel_ref, sems.at[1]),
-    ]
-    for copy in copies:
-        copy.start()
-    for copy in copies:
-        copy.wait()
-    rows = panel_ref.shape[0]
-    row_ids = lax.broadcasted_iota(jnp.int32, (rows, rows), 0)
-    lane_ids = lax.broadcasted_iota(jnp.int32, (rows, rows), 1)
-    column = jnp.sum(jnp.where(row_ids == lane_ids, weights_ref[...], 0.0), axis=1, keepdims=True)
-    out_ref[...] = (column * panel_ref[...].astype(jnp.float32)).astype(jnp.bfloat16)
-
-
-def pack_kernel(sizes, lists_hbm, masks_hbm, order_hbm, jac_hbm, weighted_ref, *rest):
+def pack_kernel(sizes, lists_hbm, masks_hbm, order_hbm, weights_hbm, panel_hbm, jac_hbm, *refs):
     layers, owners, per_owner, block_count, slot_count, block_rows, tile_width = sizes
-    kept_ref, to_x_ref, to_y_ref, lists_ref, masks_ref, order_ref, jac_ref, places_ref, turned_ref, sems = rest
+    weighted_ref, kept_ref, to_x_ref, to_y_ref = refs[:4]
+    lists_ref, masks_ref, order_ref, weights_ref, panel_ref, jac_ref, places_ref, turned_ref, sems = refs[4:]
     copies = [
         pltpu.make_async_copy(order_hbm, order_ref, sems.at[0]),
         pltpu.make_async_copy(lists_hbm, lists_ref, sems.at[1]),
         pltpu.make_async_copy(masks_hbm, masks_ref, sems.at[2]),
-        pltpu.make_async_copy(jac_hbm, jac_ref, sems.at[3]),
+        pltpu.make_async_copy(weights_hbm, weights_ref, sems.at[3]),
+        pltpu.make_async_copy(panel_hbm, panel_ref, sems.at[4]),
+        pltpu.make_async_copy(jac_hbm, jac_ref, sems.at[5]),
     ]
     for copy in copies:
         copy.start()
     f32, bf16 = jnp.float32, jnp.bfloat16
-    width = weighted_ref.shape[1]
+    rows, width = panel_ref.shape
     lane_group = CAP * block_rows
     post = layers * lane_group
     slab = tile_width // layers
     part = slab // 2
     me_r, me_c = lax.axis_index("rows"), lax.axis_index("cols")
     me_z, me_core = me_r // 2, lax.rem(me_r, 2)
-    to_x_ref[:, :width] = weighted_ref[...]
-    to_y_ref[:, :width] = weighted_ref[...]
     for copy in copies:
         copy.wait()
+
+    row_ids = lax.broadcasted_iota(jnp.int32, (rows, rows), 0)
+    lane_ids = lax.broadcasted_iota(jnp.int32, (rows, rows), 1)
+    column = jnp.sum(jnp.where(row_ids == lane_ids, weights_ref[...], 0.0), axis=1, keepdims=True)
+    weighted = (column * panel_ref[...].astype(f32)).astype(bf16)
+    weighted_ref[...] = weighted
+    to_x_ref[:, :width] = weighted
+    to_y_ref[:, :width] = weighted
 
     for b in range(block_count):
         block = jac_ref[b * block_rows : (b + 1) * block_rows, :].astype(f32)
@@ -280,13 +273,12 @@
         out_ref[...] = jnp.dot(placed_ref[...], rows_ref[...], preferred_element_type=f32)
 
 
-def far_kernel(sizes, u, near_ref, by_y_ref, by_x_ref, high_ref, low_ref, out_ref, placed_ref, rows_ref):
+def far_kernel(sizes, u, near_ref, by_y_ref, by_x_ref, out_ref, placed_ref, rows_ref):
     layers, owners, per_owner, block_count, block_rows = sizes
     f32, bf16 = jnp.float32, jnp.bfloat16
     rows = block_count * block_rows
     group, wide = CAP * block_rows, CAP * rows
     part = rows // 2
-    width = rows_ref.shape[1]
     half = (layers - 1) * rows // 2
     rows_ref[:rows, :] = by_x_ref[:rows, :]
     rows_ref[rows : rows + half, :] = by_y_ref[:half, :]
@@ -300,26 +292,29 @@
         start = 2 * h * rows
         place(placed_ref, slice(start, start + 2 * rows), per_owner, pieces, notes, (block_count, block_rows))
     gram = near_ref[...] + jnp.dot(placed_ref[...], rows_ref[...], preferred_element_type=f32)
-    gram_high = gram.astype(bf16)
-    gram_low = (gram - gram_high.astype(f32)).astype(bf16)
+    out_ref[...] = gram.astype(out_ref.dtype)
+
+
+def inverse_kernel(own_ref, other_ref, high_ref, low_ref, out_hbm, out_ref, sems):
+    f32, bf16 = jnp.float32, jnp.bfloat16
+    width = own_ref.shape[1]
+    strips = sems.shape[0]
+    height = own_ref.shape[0] // strips
     dims = (((1,), (1,)), ((), ()))
-    for start, stop in ((0, width // 2), (width // 2, width)):
-        high, low = high_ref[start:stop, :stop], low_ref[start:stop, :stop]
-        a, b = gram_high[:, :stop], gram_low[:, :stop]
-        total = lax.dot_general(a, low, dims, preferred_element_type=f32)
-        total += lax.dot_general(b, high, dims, preferred_element_type=f32)
-        total += lax.dot_general(a, high, dims, preferred_element_type=f32)
-        out_ref[:, start:stop] = total.astype(out_ref.dtype)
-
-
-def add_kernel(own_ref, other_ref, out_hbm, sum_ref, sems):
-    strips = sems.shape[0]
-    height = sum_ref.shape[0] // strips
     copies = []
     for i in range(strips):
         here = pl.ds(i * height, height)
-        sum_ref[here, :] = own_ref[here, :] + other_ref[here, :].astype(jnp.float32)
-        copies.append(pltpu.make_async_copy(sum_ref.at[here, :], out_hbm.at[here, :], sems.at[i]))
+        gram = own_ref[here, :] + other_ref[here, :].astype(f32)
+        gram_high = gram.astype(bf16)
+        gram_low = (gram - gram_high.astype(f32)).astype(bf16)
+        for start, stop in ((0, width // 2), (width // 2, width)):
+            high, low = high_ref[start:stop, :stop], low_ref[start:stop, :stop]
+            a, b = gram_high[:, :stop], gram_low[:, :stop]
+            total = lax.dot_general(a, low, dims, preferred_element_type=f32)
+            total += lax.dot_general(b, high, dims, preferred_element_type=f32)
+            total += lax.dot_general(a, high, dims, preferred_element_type=f32)
+            out_ref[here, start:stop] = total
+        copies.append(pltpu.make_async_copy(out_ref.at[here, :], out_hbm.at[here, :], sems.at[i]))
         copies[-1].start()
     for copy in copies:
         copy.wait()
@@ -342,45 +337,33 @@
     def in_hbm(value):
         return pltpu.with_memory_space_constraint(value, pltpu.HBM)
 
-    weighted = pl.pallas_call(
-        weigh_kernel,
-        out_shape=shaped((rows, panel_width), bf16),
-        in_specs=[anywhere] * 2,
-        out_specs=vmem,
-        scratch_shapes=[
-            pltpu.VMEM((1, rows), f32),
-            pltpu.VMEM((rows, panel_width), bf16),
-            pltpu.SemaphoreType.DMA((2,)),
-        ],
-        compiler_params=params,
-        name="weigh",
-    )(in_hbm(weights.reshape(1, rows)), in_hbm(panel_jac))
-    line = [shift(weighted, k, 0) for k in range(1, layers)]
-
     lane_group = CAP * block_rows
     post = layers * lane_group
     wide = CAP * rows
     sizes = (layers, owners, per_owner, block_count, slot_count, block_rows, tile_width)
-    kept, to_x, to_y = pl.pallas_call(
+    weighted, kept, to_x, to_y = pl.pallas_call(
         functools.partial(pack_kernel, sizes),
         out_shape=[
             shaped((rows, width), bf16)
-            for width in (post + wide, panel_width + 2 * post + wide, panel_width + post + wide)
+            for width in (panel_width, post + wide, panel_width + 2 * post + wide, panel_width + post + wide)
         ],
-        in_specs=[anywhere] * 4 + [vmem],
-        out_specs=[vmem] * 3,
+        in_specs=[anywhere] * 6,
+        out_specs=[vmem] * 4,
         scratch_shapes=[
             pltpu.SMEM(tile_lists.shape, jnp.int32),
             pltpu.SMEM(tile_masks.shape, jnp.int32),
             pltpu.SMEM(tile_order.shape, jnp.int32),
+            pltpu.VMEM((1, rows), f32),
+            pltpu.VMEM(panel_jac.shape, bf16),
             pltpu.VMEM(jac.shape, bf16),
             pltpu.SMEM(tile_order.shape, jnp.int32),
             pltpu.VMEM((block_count * slot_count * tile_width, block_rows), f32),
-            pltpu.SemaphoreType.DMA((4,)),
+            pltpu.SemaphoreType.DMA((6,)),
         ],
         compiler_params=params,
         name="pack",
-    )(in_hbm(tile_lists), in_hbm(tile_masks), in_hbm(tile_order), in_hbm(jac), weighted)
+    )(*map(in_hbm, (tile_lists, tile_masks, tile_order, weights.reshape(1, rows), panel_jac, jac)))
+    line = [shift(weighted, k, 0) for k in range(1, layers)]
     from_x, from_y = shift(to_x, 0, 1), shift(to_y, 0, 2)
 
     sizes = (layers, panel_width, lane_group, wide)
@@ -432,23 +415,23 @@
         return pl.pallas_call(
             functools.partial(far_kernel, sizes, u),
             out_shape=shaped((count, panel_width), kind),
-            in_specs=[vmem] * 5,
+            in_specs=[vmem] * 3,
             out_specs=vmem,
             scratch_shapes=[pltpu.VMEM((count, depth), bf16), pltpu.VMEM((depth, panel_width), bf16)],
             compiler_params=params,
             name="far",
-        )(near, across_y, across_x, high, low)
+        )(near, across_y, across_x)
 
     other = shift(far(1, other, bf16), 0, 0, 1)
     out = pl.pallas_call(
-        add_kernel,
+        inverse_kernel,
         out_shape=shaped((count, panel_width), f32),
-        in_specs=[vmem] * 2,
+        in_specs=[vmem] * 4,
         out_specs=anywhere,
         scratch_shapes=[pltpu.VMEM((count, panel_width), f32), pltpu.SemaphoreType.DMA((4,))],
         compiler_params=params,
-        name="add",
-    )(far(0, own, f32), other)
+        name="inverse",
+    )(far(0, own, f32), other, high, low)
     return out.reshape(per_owner, slab_width, panel_width)
 
 

time: 36.5 us -> 35.9 us (0.984)
  Pallas kernels: 8.67 us -> 6.98 us
  waiting for transfers between devices: 9.56 us -> 10.7 us
    pallas_call x2, Pallas kernels: 3.16 us -> 0.88 us  [far(): pl.pallas_call(functools.partial(far_kernel, sizes, u), out_shape=shaped(...]
    ppermute x13, waiting for transfers between devices: 9.56 us -> 10.7 us  [shift(): return lax.ppermute(value, ('rows', 'cols'), pairs)]
    pallas_call x2 -> x1, Pallas kernels: 2.25 us -> 2.61 us  [local(): pl.pallas_call(inverse_kernel, out_shape=shaped((count, panel_width), f32...]
  transfers between devices with their start and end apart: 13 -> 13, of which waited for: 8 -> 8; matrix products, arithmetic and copies ran while one was open for 0% -> 0% of each run, Pallas kernels for 9% -> 6%
where the time goes in v6:
time: 35.9 us; the launch traced here: 35.8 us
  starting transfers between devices  18.1 us (50%)
  waiting for transfers between devices  10.7 us (30%)
  Pallas kernels  6.98 us (19%)
    ppermute x13, starting transfers between devices, shift(): return lax.ppermute(value, ('rows', 'cols'), pairs)  18.1 us
    ppermute x13, waiting for transfers between devices, shift(): return lax.ppermute(value, ('rows', 'cols'), pairs)  10.7 us
    pallas_call x1, Pallas kernels, local(): pl.pallas_call(inverse_kernel, out_shape=shaped((count, panel_width), f32...  2.61 us
    pallas_call x1, Pallas kernels, local(): pl.pallas_call(functools.partial(pack_kernel, sizes), out_shape=[shaped((...  1.65 us
    pallas_call x1, Pallas kernels, local(): pl.pallas_call(functools.partial(near_kernel, sizes), out_shape=[gram] *...  1.62 us
    pallas_call x2, Pallas kernels, far(): pl.pallas_call(functools.partial(far_kernel, sizes, u), out_shape=shaped(...  0.88 us
  transfers between devices with their start and end apart: 13, of which 8 were waited for; matrix products, arithmetic and copies ran while one was open for 0% of the time, Pallas kernels for 6%

profile of v6, /device:TPU:0, one launch (start us, length us, event | category | flops | bytes accessed | tf_op | source)
XLA Modules:
  0.0 35.8 jit_solution(8589159524147004442)
XLA Ops:
  0.0 1.6 %pack.1 = (bf16[64,512]{1,0:T(8,128)(2,1)S(1)}, bf16[64,384]{1,0:T(8,128)(2,1)S(1)}, bf16[64,1152]{1,0:T(8,128)(2,1)S(1)}, bf16[64,896]{1,0:T(8,128)(2,1)S(1)}) custom-call(s32[2,4]{1,0:T(2,128)} %lists_hbm.1, s32[2,4]{1,0:T(2,128)} %masks_hbm.1, s32[96]{0:T(128)} %order_hbm.1, f32[1,64]{1,0:T(1,128)} %bitcast.2, bf16[64,512]{1,0:T(8,128)(2,1)} %panel_hbm.1, ...), custom_call_target="tpu_custom_call" | custom-call | tf_op jit(solution)/shard_map/pack/pallas_call | solution.py:344
  1.7 3.0 %collective-permute-start = (bf16[64,1152]{1,0:T(8,128)(2,1)S(1)}, bf16[64,1152]{1,0:T(8,128)(2,1)S(1)}, u32[]{:S(2)}, u32[]{:S(2)}) collective-permute-start(bf16[64,1152]{1,0:T(8,128)(2,1)S(1)} %get-tuple-element.22), channel_id=1, source_target_pairs={{0,1},{1,0},{2,3},{3,2},{4,5},{5,4},{6,7},{7,6},{8,9},{9,8},{10,11... | collective-permute-start | bytes 442376 | tf_op jit(solution)/shard_map/ppermute | solution.py:91
  4.7 1.5 %collective-permute-start.1 = (bf16[64,896]{1,0:T(8,128)(2,1)S(1)}, bf16[64,896]{1,0:T(8,128)(2,1)S(1)}, u32[]{:S(2)}, u32[]{:S(2)}) collective-permute-start(bf16[64,896]{1,0:T(8,128)(2,1)S(1)} %get-tuple-element.23), channel_id=1, source_target_pairs={{0,2},{1,3},{2,0},{3,1},{4,6},{5,7},{6,4},{7,5},{8,10},{9,11},{10,... | collective-permute-start | bytes 344072 | tf_op jit(solution)/shard_map/ppermute | solution.py:91
  6.2 1.6 %collective-permute-start.2 = (bf16[64,512]{1,0:T(8,128)(2,1)S(1)}, bf16[64,512]{1,0:T(8,128)(2,1)S(1)}, u32[]{:S(2)}, u32[]{:S(2)}) collective-permute-start(bf16[64,512]{1,0:T(8,128)(2,1)S(1)} %get-tuple-element.20.refs_0_), channel_id=1, source_target_pairs={{0,8},{1,9},{2,10},{3,11},{4,12},{5,13},{6,14},{7,15},{8,16},{9,17... | collective-permute-start | bytes 196616 | tf_op jit(solution)/shard_map/ppermute | solution.py:91
  7.8 2.6 %collective-permute-start.3 = (bf16[64,512]{1,0:T(8,128)(2,1)S(1)}, bf16[64,512]{1,0:T(8,128)(2,1)S(1)}, u32[]{:S(2)}, u32[]{:S(2)}) collective-permute-start(bf16[64,512]{1,0:T(8,128)(2,1)S(1)} %get-tuple-element.20.refs_0_), channel_id=1, source_target_pairs={{0,16},{1,17},{2,18},{3,19},{4,20},{5,21},{6,22},{7,23},{8,24},{9,... | collective-permute-start | bytes 196616 | tf_op jit(solution)/shard_map/ppermute | solution.py:91
  10.3 1.3 %collective-permute-start.4 = (bf16[64,512]{1,0:T(8,128)(2,1)S(1)}, bf16[64,512]{1,0:T(8,128)(2,1)S(1)}, u32[]{:S(2)}, u32[]{:S(2)}) collective-permute-start(bf16[64,512]{1,0:T(8,128)(2,1)S(1)} %get-tuple-element.20.refs_0_), channel_id=1, source_target_pairs={{0,24},{1,25},{2,26},{3,27},{4,28},{5,29},{6,30},{7,31},{8,0},{9,1... | collective-permute-start | bytes 196616 | tf_op jit(solution)/shard_map/ppermute | solution.py:91
  11.7 1.3 %collective-permute-done.2.refs_0_ = bf16[64,512]{1,0:T(8,128)(2,1)S(1)} collective-permute-done((bf16[64,512]{1,0:T(8,128)(2,1)S(1)}, bf16[64,512]{1,0:T(8,128)(2,1)S(1)}, u32[]{:S(2)}, u32[]{:S(2)}) %collective-permute-start.2) | collective-permute-done | bytes 65568 | tf_op jit(solution)/shard_map/ppermute | solution.py:91
  13.0 1.9 %collective-permute-done.3.refs_1_ = bf16[64,512]{1,0:T(8,128)(2,1)S(1)} collective-permute-done((bf16[64,512]{1,0:T(8,128)(2,1)S(1)}, bf16[64,512]{1,0:T(8,128)(2,1)S(1)}, u32[]{:S(2)}, u32[]{:S(2)}) %collective-permute-start.3) | collective-permute-done | bytes 65568 | tf_op jit(solution)/shard_map/ppermute | solution.py:91
  14.9 0.1 collective-permute-done.4.refs_2_
  15.0 0.0 collective-permute-done.1.from_y_ref.refs_4_
  15.0 0.0 collective-permute-done.from_x_ref.refs_2_
  15.0 0.1 sort.1
  15.1 0.6 %collective-permute-start.5 = (bf16[192,512]{1,0:T(8,128)(2,1)S(1)}, bf16[192,512]{1,0:T(8,128)(2,1)S(1)}, u32[]{:S(2)}, u32[]{:S(2)}) collective-permute-start(bf16[192,512]{1,0:T(8,128)(2,1)S(1)} %get-tuple-element.24.refs_1_), channel_id=1, source_target_pairs={{0,1},{1,0},{2,3},{3,2},{4,5},{5,4},{6,7},{7,6},{8,9},{9,8},{10,11... | collective-permute-start | bytes 589832 | tf_op jit(solution)/shard_map/ppermute | solution.py:91
  15.7 0.4 %collective-permute-start.6 = (bf16[192,512]{1,0:T(8,128)(2,1)S(1)}, bf16[192,512]{1,0:T(8,128)(2,1)S(1)}, u32[]{:S(2)}, u32[]{:S(2)}) collective-permute-start(bf16[192,512]{1,0:T(8,128)(2,1)S(1)} %get-tuple-element.24.refs_1_), channel_id=1, source_target_pairs={{0,2},{1,3},{2,0},{3,1},{4,6},{5,7},{6,4},{7,5},{8,10},{9,11},{10,... | collective-permute-start | bytes 589832 | tf_op jit(solution)/shard_map/ppermute | solution.py:91
  16.2 1.1 %collective-permute-start.7 = (bf16[80,256]{1,0:T(8,128)(2,1)S(1)}, bf16[80,256]{1,0:T(8,128)(2,1)S(1)}, u32[]{:S(2)}, u32[]{:S(2)}) collective-permute-start(bf16[80,256]{1,0:T(8,128)(2,1)S(1)} %get-tuple-element.26), channel_id=1, source_target_pairs={{0,8},{1,9},{2,10},{3,11},{4,12},{5,13},{6,14},{7,15},{8,16},{9,17... | collective-permute-start | bytes 122888 | tf_op jit(solution)/shard_map/ppermute | solution.py:91
  17.3 2.2 %collective-permute-start.8 = (bf16[80,256]{1,0:T(8,128)(2,1)S(1)}, bf16[80,256]{1,0:T(8,128)(2,1)S(1)}, u32[]{:S(2)}, u32[]{:S(2)}) collective-permute-start(bf16[80,256]{1,0:T(8,128)(2,1)S(1)} %get-tuple-element.27), channel_id=1, source_target_pairs={{0,16},{1,17},{2,18},{3,19},{4,20},{5,21},{6,22},{7,23},{8,24},{9,... | collective-permute-start | bytes 122888 | tf_op jit(solution)/shard_map/ppermute | solution.py:91
  19.6 0.5 %collective-permute-start.9 = (bf16[80,256]{1,0:T(8,128)(2,1)S(1)}, bf16[80,256]{1,0:T(8,128)(2,1)S(1)}, u32[]{:S(2)}, u32[]{:S(2)}) collective-permute-start(bf16[80,256]{1,0:T(8,128)(2,1)S(1)} %get-tuple-element.28), channel_id=1, source_target_pairs={{0,24},{1,25},{2,26},{3,27},{4,28},{5,29},{6,30},{7,31},{8,0},{9,1... | collective-permute-start | bytes 122888 | tf_op jit(solution)/shard_map/ppermute | solution.py:91
  20.0 2.0 %collective-permute-done.7.refs_7_.refs_1_ = bf16[80,256]{1,0:T(8,128)(2,1)S(1)} collective-permute-done((bf16[80,256]{1,0:T(8,128)(2,1)S(1)}, bf16[80,256]{1,0:T(8,128)(2,1)S(1)}, u32[]{:S(2)}, u32[]{:S(2)}) %collective-permute-start.7) | collective-permute-done | bytes 40992 | tf_op jit(solution)/shard_map/ppermute | solution.py:91
  22.0 0.9 %collective-permute-done.8.refs_8_.refs_2_ = bf16[80,256]{1,0:T(8,128)(2,1)S(1)} collective-permute-done((bf16[80,256]{1,0:T(8,128)(2,1)S(1)}, bf16[80,256]{1,0:T(8,128)(2,1)S(1)}, u32[]{:S(2)}, u32[]{:S(2)}) %collective-permute-start.8) | collective-permute-done | bytes 40992 | tf_op jit(solution)/shard_map/ppermute | solution.py:91
  22.9 0.7 %collective-permute-done.9.refs_9_.refs_3_ = bf16[80,256]{1,0:T(8,128)(2,1)S(1)} collective-permute-done((bf16[80,256]{1,0:T(8,128)(2,1)S(1)}, bf16[80,256]{1,0:T(8,128)(2,1)S(1)}, u32[]{:S(2)}, u32[]{:S(2)}) %collective-permute-start.9) | collective-permute-done | bytes 40992 | tf_op jit(solution)/shard_map/ppermute | solution.py:91
  23.6 0.0 collective-permute-done.5.refs_3_.by_x_ref
  23.6 0.0 collective-permute-done.6.refs_5_.by_y_ref
  23.6 0.1 cut.1
  23.7 1.6 %collective-permute-start.11 = (bf16[160,512]{1,0:T(8,128)(2,1)S(1)}, bf16[160,512]{1,0:T(8,128)(2,1)S(1)}, u32[]{:S(2)}, u32[]{:S(2)}) collective-permute-start(bf16[160,512]{1,0:T(8,128)(2,1)S(1)} %get-tuple-element.31), channel_id=1, source_target_pairs={{0,1},{1,0},{2,3},{3,2},{4,5},{5,4},{6,7},{7,6},{8,9},{9,8},{10,11... | collective-permute-start | bytes 491528 | tf_op jit(solution)/shard_map/ppermute | solution.py:91
  25.2 1.5 %collective-permute-start.10 = (bf16[144,512]{1,0:T(8,128)(2,1)S(1)}, bf16[144,512]{1,0:T(8,128)(2,1)S(1)}, u32[]{:S(2)}, u32[]{:S(2)}) collective-permute-start(bf16[144,512]{1,0:T(8,128)(2,1)S(1)} %get-tuple-element.30), channel_id=1, source_target_pairs={{0,2},{1,3},{2,0},{3,1},{4,6},{5,7},{6,4},{7,5},{8,10},{9,11},{10,... | collective-permute-start | bytes 442376 | tf_op jit(solution)/shard_map/ppermute | solution.py:91
  26.7 1.6 %near.1 = (f32[768,512]{1,0:T(8,128)S(1)}, f32[768,512]{1,0:T(8,128)S(1)}, bf16[512,512]{1,0:T(8,128)(2,1)S(1)}, bf16[512,512]{1,0:T(8,128)(2,1)S(1)}) custom-call(bf16[64,512]{1,0:T(8,128)(2,1)S(1)} %get-tuple-element.20.refs_0_, bf16[192,512]{1,0:T(8,128)(2,1)S(1)} %get-tuple-element.24.refs_1_, ...), custom_call_target="tpu_custom_call" | custom-call | tf_op jit(solution)/shard_map/near/pallas_call | solution.py:401
  28.4 2.0 %collective-permute-done.10.by_y_ref = bf16[144,512]{1,0:T(8,128)(2,1)S(1)} collective-permute-done((bf16[144,512]{1,0:T(8,128)(2,1)S(1)}, bf16[144,512]{1,0:T(8,128)(2,1)S(1)}, u32[]{:S(2)}, u32[]{:S(2)}) %collective-permute-start.10) | collective-permute-done | bytes 147488 | tf_op jit(solution)/shard_map/ppermute | solution.py:91
  30.4 0.4 %far.3 = bf16[768,512]{1,0:T(8,128)(2,1)S(1)} custom-call(f32[768,512]{1,0:T(8,128)S(1)} %get-tuple-element.32.near_ref, bf16[144,512]{1,0:T(8,128)(2,1)S(1)} %collective-permute-done.10.by_y_ref, bf16[160,512]{1,0:T(8,128)(2,1)S(1)} %collective-permute-done.11.by_x_ref), custom_call_target="tpu_custom_call" | custom-call | tf_op jit(solution)/shard_map/far/pallas_call | solution.py:415
  30.8 0.1 collective-permute-start.12
  30.9 0.4 %far.2.own_ref = f32[768,512]{1,0:T(8,128)S(1)} custom-call(f32[768,512]{1,0:T(8,128)S(1)} %get-tuple-element.29.near_ref, bf16[144,512]{1,0:T(8,128)(2,1)S(1)} %collective-permute-done.10.by_y_ref, bf16[160,512]{1,0:T(8,128)(2,1)S(1)} %collective-permute-done.11.by_x_ref), custom_call_target="tpu_custom_call" | custom-call | tf_op jit(solution)/shard_map/far/pallas_call | solution.py:415
  31.3 1.8 %collective-permute-done.12.other_ref = bf16[768,512]{1,0:T(8,128)(2,1)S(1)} collective-permute-done((bf16[768,512]{1,0:T(8,128)(2,1)S(1)}, bf16[768,512]{1,0:T(8,128)(2,1)S(1)}, u32[]{:S(2)}, u32[]{:S(2)}) %collective-permute-start.12) | collective-permute-done | bytes 786464 | tf_op jit(solution)/shard_map/ppermute | solution.py:91
  33.2 2.6 %inverse.1 = f32[768,512]{1,0:T(8,128)} custom-call(f32[768,512]{1,0:T(8,128)S(1)} %far.2.own_ref, bf16[768,512]{1,0:T(8,128)(2,1)S(1)} %collective-permute-done.12.other_ref, bf16[512,512]{1,0:T(8,128)(2,1)S(1)} %get-tuple-element.33.high_ref, bf16[512,512]{1,0:T(8,128)(2,1)S(1)} %get-tuple-element.34.low_ref), custom_call_target="tpu_custom_call" | custom-call | tf_op jit(solution)/shard_map/inverse/pallas_call | solution.py:426
  (3 shorter events, 0.0 us)
Async XLA Ops:
  0.0 26.7 %copy-start = (f32[512,512]{1,0:T(8,128)S(1)}, f32[512,512]{1,0:T(8,128)}, u32[]{:S(2)}) copy-start(f32[512,512]{1,0:T(8,128)} %refs_10_.1) | copy-start | bytes 3145732
  1.7 13.4 %collective-permute-start = (bf16[64,1152]{1,0:T(8,128)(2,1)S(1)}, bf16[64,1152]{1,0:T(8,128)(2,1)S(1)}, u32[]{:S(2)}, u32[]{:S(2)}) collective-permute-start(bf16[64,1152]{1,0:T(8,128)(2,1)S(1)} %get-tuple-element.22), channel_id=1, source_target_pairs={{0,1},{1,0},{2,3},{3,2},{4,5},{5,4},{6,7},{7,6},{8,9},{9,8},{10,11... | collective-permute-start | bytes 442376 | tf_op jit(solution)/shard_map/ppermute | solution.py:91
  4.7 10.3 %collective-permute-start.1 = (bf16[64,896]{1,0:T(8,128)(2,1)S(1)}, bf16[64,896]{1,0:T(8,128)(2,1)S(1)}, u32[]{:S(2)}, u32[]{:S(2)}) collective-permute-start(bf16[64,896]{1,0:T(8,128)(2,1)S(1)} %get-tuple-element.23), channel_id=1, source_target_pairs={{0,2},{1,3},{2,0},{3,1},{4,6},{5,7},{6,4},{7,5},{8,10},{9,11},{10,... | collective-permute-start | bytes 344072 | tf_op jit(solution)/shard_map/ppermute | solution.py:91
  6.2 6.8 %collective-permute-start.2 = (bf16[64,512]{1,0:T(8,128)(2,1)S(1)}, bf16[64,512]{1,0:T(8,128)(2,1)S(1)}, u32[]{:S(2)}, u32[]{:S(2)}) collective-permute-start(bf16[64,512]{1,0:T(8,128)(2,1)S(1)} %get-tuple-element.20.refs_0_), channel_id=1, source_target_pairs={{0,8},{1,9},{2,10},{3,11},{4,12},{5,13},{6,14},{7,15},{8,16},{9,17... | collective-permute-start | bytes 196616 | tf_op jit(solution)/shard_map/ppermute | solution.py:91
  7.8 7.2 %collective-permute-start.3 = (bf16[64,512]{1,0:T(8,128)(2,1)S(1)}, bf16[64,512]{1,0:T(8,128)(2,1)S(1)}, u32[]{:S(2)}, u32[]{:S(2)}) collective-permute-start(bf16[64,512]{1,0:T(8,128)(2,1)S(1)} %get-tuple-element.20.refs_0_), channel_id=1, source_target_pairs={{0,16},{1,17},{2,18},{3,19},{4,20},{5,21},{6,22},{7,23},{8,24},{9,... | collective-permute-start | bytes 196616 | tf_op jit(solution)/shard_map/ppermute | solution.py:91
  10.3 4.7 %collective-permute-start.4 = (bf16[64,512]{1,0:T(8,128)(2,1)S(1)}, bf16[64,512]{1,0:T(8,128)(2,1)S(1)}, u32[]{:S(2)}, u32[]{:S(2)}) collective-permute-start(bf16[64,512]{1,0:T(8,128)(2,1)S(1)} %get-tuple-element.20.refs_0_), channel_id=1, source_target_pairs={{0,24},{1,25},{2,26},{3,27},{4,28},{5,29},{6,30},{7,31},{8,0},{9,1... | collective-permute-start | bytes 196616 | tf_op jit(solution)/shard_map/ppermute | solution.py:91
  15.1 8.4 %collective-permute-start.5 = (bf16[192,512]{1,0:T(8,128)(2,1)S(1)}, bf16[192,512]{1,0:T(8,128)(2,1)S(1)}, u32[]{:S(2)}, u32[]{:S(2)}) collective-permute-start(bf16[192,512]{1,0:T(8,128)(2,1)S(1)} %get-tuple-element.24.refs_1_), channel_id=1, source_target_pairs={{0,1},{1,0},{2,3},{3,2},{4,5},{5,4},{6,7},{7,6},{8,9},{9,8},{10,11... | collective-permute-start | bytes 589832 | tf_op jit(solution)/shard_map/ppermute | solution.py:91
  15.7 7.8 %collective-permute-start.6 = (bf16[192,512]{1,0:T(8,128)(2,1)S(1)}, bf16[192,512]{1,0:T(8,128)(2,1)S(1)}, u32[]{:S(2)}, u32[]{:S(2)}) collective-permute-start(bf16[192,512]{1,0:T(8,128)(2,1)S(1)} %get-tuple-element.24.refs_1_), channel_id=1, source_target_pairs={{0,2},{1,3},{2,0},{3,1},{4,6},{5,7},{6,4},{7,5},{8,10},{9,11},{10,... | collective-permute-start | bytes 589832 | tf_op jit(solution)/shard_map/ppermute | solution.py:91
  16.2 5.8 %collective-permute-start.7 = (bf16[80,256]{1,0:T(8,128)(2,1)S(1)}, bf16[80,256]{1,0:T(8,128)(2,1)S(1)}, u32[]{:S(2)}, u32[]{:S(2)}) collective-permute-start(bf16[80,256]{1,0:T(8,128)(2,1)S(1)} %get-tuple-element.26), channel_id=1, source_target_pairs={{0,8},{1,9},{2,10},{3,11},{4,12},{5,13},{6,14},{7,15},{8,16},{9,17... | collective-permute-start | bytes 122888 | tf_op jit(solution)/shard_map/ppermute | solution.py:91
  17.3 5.5 %collective-permute-start.8 = (bf16[80,256]{1,0:T(8,128)(2,1)S(1)}, bf16[80,256]{1,0:T(8,128)(2,1)S(1)}, u32[]{:S(2)}, u32[]{:S(2)}) collective-permute-start(bf16[80,256]{1,0:T(8,128)(2,1)S(1)} %get-tuple-element.27), channel_id=1, source_target_pairs={{0,16},{1,17},{2,18},{3,19},{4,20},{5,21},{6,22},{7,23},{8,24},{9,... | collective-permute-start | bytes 122888 | tf_op jit(solution)/shard_map/ppermute | solution.py:91
  19.6 4.0 %collective-permute-start.9 = (bf16[80,256]{1,0:T(8,128)(2,1)S(1)}, bf16[80,256]{1,0:T(8,128)(2,1)S(1)}, u32[]{:S(2)}, u32[]{:S(2)}) collective-permute-start(bf16[80,256]{1,0:T(8,128)(2,1)S(1)} %get-tuple-element.28), channel_id=1, source_target_pairs={{0,24},{1,25},{2,26},{3,27},{4,28},{5,29},{6,30},{7,31},{8,0},{9,1... | collective-permute-start | bytes 122888 | tf_op jit(solution)/shard_map/ppermute | solution.py:91
  23.7 6.7 %collective-permute-start.11 = (bf16[160,512]{1,0:T(8,128)(2,1)S(1)}, bf16[160,512]{1,0:T(8,128)(2,1)S(1)}, u32[]{:S(2)}, u32[]{:S(2)}) collective-permute-start(bf16[160,512]{1,0:T(8,128)(2,1)S(1)} %get-tuple-element.31), channel_id=1, source_target_pairs={{0,1},{1,0},{2,3},{3,2},{4,5},{5,4},{6,7},{7,6},{8,9},{9,8},{10,11... | collective-permute-start | bytes 491528 | tf_op jit(solution)/shard_map/ppermute | solution.py:91
  25.2 5.1 %collective-permute-start.10 = (bf16[144,512]{1,0:T(8,128)(2,1)S(1)}, bf16[144,512]{1,0:T(8,128)(2,1)S(1)}, u32[]{:S(2)}, u32[]{:S(2)}) collective-permute-start(bf16[144,512]{1,0:T(8,128)(2,1)S(1)} %get-tuple-element.30), channel_id=1, source_target_pairs={{0,2},{1,3},{2,0},{3,1},{4,6},{5,7},{6,4},{7,5},{8,10},{9,11},{10,... | collective-permute-start | bytes 442376 | tf_op jit(solution)/shard_map/ppermute | solution.py:91
  30.8 2.4 %collective-permute-start.12 = (bf16[768,512]{1,0:T(8,128)(2,1)S(1)}, bf16[768,512]{1,0:T(8,128)(2,1)S(1)}, u32[]{:S(2)}, u32[]{:S(2)}) collective-permute-start(bf16[768,512]{1,0:T(8,128)(2,1)S(1)} %far.3), channel_id=1, source_target_pairs={{0,4},{1,5},{2,6},{3,7},{4,0},{5,1},{6,2},{7,3},{8,12},{9,13},{10,... | collective-permute-start | bytes 2359304 | tf_op jit(solution)/shard_map/ppermute | solution.py:91

commit v7 on v6

--- a/solution.py
+++ b/solution.py
@@ -143,7 +143,7 @@
     shape = (16, CAP * block_count * block_rows)
     lane, row = lax.broadcasted_iota(jnp.int32, shape, 1), lax.broadcasted_iota(jnp.int32, shape, 0)
     notes = []
-    spots = [(kept_ref, 0), (to_x_ref, width), (to_y_ref, width), (to_x_ref, width + post)]
+    spots = [(kept_ref, 0), (to_x_ref, width), (to_y_ref, width), (to_y_ref, width + post)]
     for e, (parcel, start) in enumerate(spots):
         wanted = me_c ^ e
         found = jnp.int32(0)
@@ -174,8 +174,8 @@
                     to = start + k * lane_group + j * block_rows
                     parcel[u * part : (u + 1) * part, to : to + block_rows] = piece
     kept_ref[:16, post:] = notes[0].astype(f32).astype(bf16)
-    to_x_ref[:16, width + 2 * post :] = jnp.where(row == 0, notes[1], notes[3]).astype(f32).astype(bf16)
-    to_y_ref[:16, width + post :] = notes[2].astype(f32).astype(bf16)
+    to_x_ref[:16, width + post :] = notes[1].astype(f32).astype(bf16)
+    to_y_ref[:16, width + 2 * post :] = jnp.where(row == 0, notes[2], notes[3]).astype(f32).astype(bf16)
 
 
 def row_of(block, i):
@@ -198,7 +198,7 @@
     rows = kept_ref.shape[0]
     for k, ref in enumerate(line):
         stacked[k * rows : (k + 1) * rows, :] = ref[...]
-    spots = [(kept_ref, 0), (from_x_ref, width), (from_y_ref, width), (from_x_ref, width + post)]
+    spots = [(kept_ref, 0), (from_x_ref, width), (from_y_ref, width), (from_y_ref, width + post)]
     notes = [row_of(ref[:16, ref.shape[1] - wide :], int(e == 3)) for e, (ref, start) in enumerate(spots)]
     block = rows_from(notes)
     for k, out in enumerate(posts):
@@ -208,23 +208,26 @@
         out[rows:, :wide] = block
 
 
-def cut_kernel(sizes, from_y_ref, by_x_ref, by_y_ref, *refs):
-    layers, width, lane_group, wide = sizes
-    posts, (to_y_ref, to_x_ref) = refs[:layers], refs[layers:]
-    rows = from_y_ref.shape[0]
-    half = by_x_ref.shape[0] // 2
+def rows_to_y_kernel(from_x_ref, by_x_ref, *refs):
+    out_ref = refs[-1]
+    rows = from_x_ref.shape[0]
+    out_ref[:rows, :] = from_x_ref[:, : out_ref.shape[1]]
+    out_ref[rows:, :] = by_x_ref[: out_ref.shape[0] - rows, :]
+
+
+def rest_to_x_kernel(sizes, by_y_ref, *refs):
+    layers, lane_group, wide = sizes
+    posts, out_ref = refs[:layers], refs[layers]
+    rows = posts[0].shape[0] - 16
     part = rows // 2
-    post = layers * lane_group
-    to_y_ref[:half, :] = by_x_ref[:half, :]
+    last = out_ref.shape[0] - part - 16
+    out_ref[:last, :] = by_y_ref[by_y_ref.shape[0] - last :, :]
     for k, ref in enumerate(posts):
         for u in range(2):
             piece = ref[u * part : (u + 1) * part, 3 * lane_group : 4 * lane_group]
-            at = u * post + k * lane_group
-            to_y_ref[half : half + part, at : at + lane_group] = piece
-    notes = [row_of(ref[rows:, :wide], 3) for ref in posts]
-    to_y_ref[half + part :, :wide] = rows_from(notes)
-    to_x_ref[:rows, :] = from_y_ref[:, :width]
-    to_x_ref[rows:, :] = by_y_ref[half:, :]
+            at = (u * layers + k) * lane_group
+            out_ref[last : last + part, at : at + lane_group] = piece
+    out_ref[last + part :, :wide] = rows_from([row_of(ref[rows:, :wide], 3) for ref in posts])
 
 
 def place(out_ref, lanes, per_owner, pieces, notes, sizes):
@@ -251,9 +254,10 @@
     panels, posts, factor_ref = refs[: 2 * (owners - 1)], refs[2 * (owners - 1) :][:layers], refs[2 * owners - 2 + layers]
     own_ref, other_ref, high_ref, low_ref, placed_ref, rows_ref = refs[2 * owners - 1 + layers :]
     f32, bf16 = jnp.float32, jnp.bfloat16
-    high = factor_ref[...].astype(bf16)
+    turned = factor_ref[...].T
+    high = turned.astype(bf16)
     high_ref[...] = high
-    low_ref[...] = (factor_ref[...] - high.astype(f32)).astype(bf16)
+    low_ref[...] = (turned - high.astype(f32)).astype(bf16)
     rows = block_count * block_rows
     group, wide = CAP * block_rows, CAP * rows
     part = rows // 2
@@ -279,16 +283,16 @@
     rows = block_count * block_rows
     group, wide = CAP * block_rows, CAP * rows
     part = rows // 2
-    half = (layers - 1) * rows // 2
-    rows_ref[:rows, :] = by_x_ref[:rows, :]
-    rows_ref[rows : rows + half, :] = by_y_ref[:half, :]
-    rows_ref[rows + half :, :] = by_x_ref[rows:, :]
+    first = by_y_ref.shape[0]
+    last = rows_ref.shape[0] - first
+    rows_ref[:first, :] = by_y_ref[...]
+    rows_ref[first:, :] = by_x_ref[:last, :]
     for h in range(layers // 2):
         pieces, notes = [], []
         for k in (2 * h, 2 * h + 1):
             at = (u * layers + k) * group
-            pieces.append(by_y_ref[half : half + part, at : at + group])
-            notes.append(row_of(by_y_ref[half + part :, :wide], k))
+            pieces.append(by_x_ref[last : last + part, at : at + group])
+            notes.append(row_of(by_x_ref[last + part :, :wide], k))
         start = 2 * h * rows
         place(placed_ref, slice(start, start + 2 * rows), per_owner, pieces, notes, (block_count, block_rows))
     gram = near_ref[...] + jnp.dot(placed_ref[...], rows_ref[...], preferred_element_type=f32)
@@ -300,20 +304,20 @@
     width = own_ref.shape[1]
     strips = sems.shape[0]
     height = own_ref.shape[0] // strips
-    dims = (((1,), (1,)), ((), ()))
     copies = []
+
+    def times(a, b):
+        return jnp.dot(a, b, preferred_element_type=f32)
+
     for i in range(strips):
         here = pl.ds(i * height, height)
         gram = own_ref[here, :] + other_ref[here, :].astype(f32)
         gram_high = gram.astype(bf16)
         gram_low = (gram - gram_high.astype(f32)).astype(bf16)
         for start, stop in ((0, width // 2), (width // 2, width)):
-            high, low = high_ref[start:stop, :stop], low_ref[start:stop, :stop]
+            high, low = high_ref[:stop, start:stop], low_ref[:stop, start:stop]
             a, b = gram_high[:, :stop], gram_low[:, :stop]
-            total = lax.dot_general(a, low, dims, preferred_element_type=f32)
-            total += lax.dot_general(b, high, dims, preferred_element_type=f32)
-            total += lax.dot_general(a, high, dims, preferred_element_type=f32)
-            out_ref[here, start:stop] = total
+            out_ref[here, start:stop] = times(a, high) + (times(a, low) + times(b, high))
         copies.append(pltpu.make_async_copy(out_ref.at[here, :], out_hbm.at[here, :], sems.at[i]))
         copies[-1].start()
     for copy in copies:
@@ -345,7 +349,7 @@
         functools.partial(pack_kernel, sizes),
         out_shape=[
             shaped((rows, width), bf16)
-            for width in (panel_width, post + wide, panel_width + 2 * post + wide, panel_width + post + wide)
+            for width in (panel_width, post + wide, panel_width + post + wide, panel_width + 2 * post + wide)
         ],
         in_specs=[anywhere] * 6,
         out_specs=[vmem] * 4,
@@ -379,19 +383,25 @@
     posts = [posts[0]] + [shift(posts[k], k, 0) for k in range(1, layers)]
     by_x, by_y = shift(others, 0, 1), shift(others, 0, 2)
 
-    half = others.shape[0] // 2
-    to_y, to_x = pl.pallas_call(
-        functools.partial(cut_kernel, sizes),
-        out_shape=[
-            shaped((half + rows // 2 + 16, panel_width), bf16),
-            shaped((rows + half, panel_width), bf16),
-        ],
-        in_specs=[vmem] * (layers + 3),
-        out_specs=[vmem] * 2,
-        compiler_params=params,
-        name="cut",
-    )(from_y, by_x, by_y, *posts)
-    across_y, across_x = shift(to_y, 0, 2), shift(to_x, 0, 1)
+    last = rows // 2
+    rows_to_y = pl.pallas_call(
+        rows_to_y_kernel,
+        out_shape=shaped((rows + others.shape[0] - last, panel_width), bf16),
+        in_specs=[vmem] * 2 + [anywhere] * (layers - 1),
+        out_specs=vmem,
+        compiler_params=params,
+        name="rows_to_y",
+    )(from_x, by_x, *posts[1:])
+    across_y = shift(rows_to_y, 0, 2)
+    rest_to_x = pl.pallas_call(
+        functools.partial(rest_to_x_kernel, (layers, lane_group, wide)),
+        out_shape=shaped((last + rows // 2 + 16, panel_width), bf16),
+        in_specs=[vmem] * (layers + 1),
+        out_specs=vmem,
+        compiler_params=params,
+        name="rest_to_x",
+    )(by_y, *posts)
+    across_x = shift(rest_to_x, 0, 1)
 
     count = per_owner * slab_width
     depth = layers * rows
@@ -428,7 +438,7 @@
         out_shape=shaped((count, panel_width), f32),
         in_specs=[vmem] * 4,
         out_specs=anywhere,
-        scratch_shapes=[pltpu.VMEM((count, panel_width), f32), pltpu.SemaphoreType.DMA((4,))],
+        scratch_shapes=[pltpu.VMEM((count, panel_width), f32), pltpu.SemaphoreType.DMA((3,))],
         compiler_params=params,
         name="inverse",
     )(far(0, own, f32), other, high, low)

time: 35.9 us -> 34.8 us (0.969)
  Pallas kernels: 6.98 us -> 6.3 us
  waiting for transfers between devices: 10.7 us -> 10.2 us
    pallas_call x1, Pallas kernels: 2.61 us -> 2.08 us  [local(): pl.pallas_call(inverse_kernel, out_shape=shaped((count, panel_width), f32...]
    ppermute x13, waiting for transfers between devices: 10.7 us -> 10.2 us  [shift(): return lax.ppermute(value, ('rows', 'cols'), pairs)]
where the time goes in v7:
time: 34.8 us; the launch traced here: 34.7 us
  starting transfers between devices  18.1 us (52%)
  waiting for transfers between devices  10.2 us (29%)
  Pallas kernels  6.3 us (18%)
    ppermute x13, starting transfers between devices, shift(): return lax.ppermute(value, ('rows', 'cols'), pairs)  18.1 us
    ppermute x13, waiting for transfers between devices, shift(): return lax.ppermute(value, ('rows', 'cols'), pairs)  10.2 us
    pallas_call x1, Pallas kernels, local(): pl.pallas_call(inverse_kernel, out_shape=shaped((count, panel_width), f32...  2.08 us
    pallas_call x1, Pallas kernels, local(): pl.pallas_call(functools.partial(pack_kernel, sizes), out_shape=[shaped((...  1.65 us
    pallas_call x1, Pallas kernels, local(): pl.pallas_call(functools.partial(near_kernel, sizes), out_shape=[gram] *...  1.46 us
    pallas_call x2, Pallas kernels, far(): pl.pallas_call(functools.partial(far_kernel, sizes, u), out_shape=shaped(...  0.88 us
  transfers between devices with their start and end apart: 13, of which 8 were waited for; matrix products, arithmetic and copies ran while one was open for 0% of the time, Pallas kernels for 6%

profile of v7, /device:TPU:0, one launch (start us, length us, event | category | flops | bytes accessed | tf_op | source)
XLA Modules:
  0.0 34.7 jit_solution(6515851394316306596)
XLA Ops:
  0.0 1.7 %pack.1 = (bf16[64,512]{1,0:T(8,128)(2,1)S(1)}, bf16[64,384]{1,0:T(8,128)(2,1)S(1)}, bf16[64,896]{1,0:T(8,128)(2,1)S(1)}, bf16[64,1152]{1,0:T(8,128)(2,1)S(1)}) custom-call(s32[2,4]{1,0:T(2,128)} %lists_hbm.1, s32[2,4]{1,0:T(2,128)} %masks_hbm.1, s32[96]{0:T(128)} %order_hbm.1, f32[1,64]{1,0:T(1,128)} %bitcast.2, bf16[64,512]{1,0:T(8,128)(2,1)} %panel_hbm.1, ...), custom_call_target="tpu_custom_call" | custom-call | tf_op jit(solution)/shard_map/pack/pallas_call | solution.py:348
  1.7 3.0 %collective-permute-start.1 = (bf16[64,1152]{1,0:T(8,128)(2,1)S(1)}, bf16[64,1152]{1,0:T(8,128)(2,1)S(1)}, u32[]{:S(2)}, u32[]{:S(2)}) collective-permute-start(bf16[64,1152]{1,0:T(8,128)(2,1)S(1)} %get-tuple-element.21), channel_id=1, source_target_pairs={{0,2},{1,3},{2,0},{3,1},{4,6},{5,7},{6,4},{7,5},{8,10},{9,11},{10,... | collective-permute-start | bytes 442376 | tf_op jit(solution)/shard_map/ppermute | solution.py:91
  4.7 1.5 %collective-permute-start = (bf16[64,896]{1,0:T(8,128)(2,1)S(1)}, bf16[64,896]{1,0:T(8,128)(2,1)S(1)}, u32[]{:S(2)}, u32[]{:S(2)}) collective-permute-start(bf16[64,896]{1,0:T(8,128)(2,1)S(1)} %get-tuple-element.20), channel_id=1, source_target_pairs={{0,1},{1,0},{2,3},{3,2},{4,5},{5,4},{6,7},{7,6},{8,9},{9,8},{10,11... | collective-permute-start | bytes 344072 | tf_op jit(solution)/shard_map/ppermute | solution.py:91
  6.2 1.6 %collective-permute-start.2 = (bf16[64,512]{1,0:T(8,128)(2,1)S(1)}, bf16[64,512]{1,0:T(8,128)(2,1)S(1)}, u32[]{:S(2)}, u32[]{:S(2)}) collective-permute-start(bf16[64,512]{1,0:T(8,128)(2,1)S(1)} %get-tuple-element.18.refs_0_), channel_id=1, source_target_pairs={{0,8},{1,9},{2,10},{3,11},{4,12},{5,13},{6,14},{7,15},{8,16},{9,17... | collective-permute-start | bytes 196616 | tf_op jit(solution)/shard_map/ppermute | solution.py:91
  7.8 2.6 %collective-permute-start.3 = (bf16[64,512]{1,0:T(8,128)(2,1)S(1)}, bf16[64,512]{1,0:T(8,128)(2,1)S(1)}, u32[]{:S(2)}, u32[]{:S(2)}) collective-permute-start(bf16[64,512]{1,0:T(8,128)(2,1)S(1)} %get-tuple-element.18.refs_0_), channel_id=1, source_target_pairs={{0,16},{1,17},{2,18},{3,19},{4,20},{5,21},{6,22},{7,23},{8,24},{9,... | collective-permute-start | bytes 196616 | tf_op jit(solution)/shard_map/ppermute | solution.py:91
  10.4 1.3 %collective-permute-start.4 = (bf16[64,512]{1,0:T(8,128)(2,1)S(1)}, bf16[64,512]{1,0:T(8,128)(2,1)S(1)}, u32[]{:S(2)}, u32[]{:S(2)}) collective-permute-start(bf16[64,512]{1,0:T(8,128)(2,1)S(1)} %get-tuple-element.18.refs_0_), channel_id=1, source_target_pairs={{0,24},{1,25},{2,26},{3,27},{4,28},{5,29},{6,30},{7,31},{8,0},{9,1... | collective-permute-start | bytes 196616 | tf_op jit(solution)/shard_map/ppermute | solution.py:91
  11.7 1.3 %collective-permute-done.2.refs_0_ = bf16[64,512]{1,0:T(8,128)(2,1)S(1)} collective-permute-done((bf16[64,512]{1,0:T(8,128)(2,1)S(1)}, bf16[64,512]{1,0:T(8,128)(2,1)S(1)}, u32[]{:S(2)}, u32[]{:S(2)}) %collective-permute-start.2) | collective-permute-done | bytes 65568 | tf_op jit(solution)/shard_map/ppermute | solution.py:91
  13.0 1.9 %collective-permute-done.3.refs_1_ = bf16[64,512]{1,0:T(8,128)(2,1)S(1)} collective-permute-done((bf16[64,512]{1,0:T(8,128)(2,1)S(1)}, bf16[64,512]{1,0:T(8,128)(2,1)S(1)}, u32[]{:S(2)}, u32[]{:S(2)}) %collective-permute-start.3) | collective-permute-done | bytes 65568 | tf_op jit(solution)/shard_map/ppermute | solution.py:91
  14.9 0.1 collective-permute-done.4.refs_2_
  15.0 0.0 collective-permute-done.from_x_ref.refs_2_
  15.0 0.0 collective-permute-done.1.from_y_ref.refs_4_
  15.0 0.1 sort.1
  15.2 0.6 %collective-permute-start.5 = (bf16[192,512]{1,0:T(8,128)(2,1)S(1)}, bf16[192,512]{1,0:T(8,128)(2,1)S(1)}, u32[]{:S(2)}, u32[]{:S(2)}) collective-permute-start(bf16[192,512]{1,0:T(8,128)(2,1)S(1)} %get-tuple-element.22.refs_1_), channel_id=1, source_target_pairs={{0,1},{1,0},{2,3},{3,2},{4,5},{5,4},{6,7},{7,6},{8,9},{9,8},{10,11... | collective-permute-start | bytes 589832 | tf_op jit(solution)/shard_map/ppermute | solution.py:91
  15.8 0.4 %collective-permute-start.6 = (bf16[192,512]{1,0:T(8,128)(2,1)S(1)}, bf16[192,512]{1,0:T(8,128)(2,1)S(1)}, u32[]{:S(2)}, u32[]{:S(2)}) collective-permute-start(bf16[192,512]{1,0:T(8,128)(2,1)S(1)} %get-tuple-element.22.refs_1_), channel_id=1, source_target_pairs={{0,2},{1,3},{2,0},{3,1},{4,6},{5,7},{6,4},{7,5},{8,10},{9,11},{10,... | collective-permute-start | bytes 589832 | tf_op jit(solution)/shard_map/ppermute | solution.py:91
  16.2 1.1 %collective-permute-start.7 = (bf16[80,256]{1,0:T(8,128)(2,1)S(1)}, bf16[80,256]{1,0:T(8,128)(2,1)S(1)}, u32[]{:S(2)}, u32[]{:S(2)}) collective-permute-start(bf16[80,256]{1,0:T(8,128)(2,1)S(1)} %get-tuple-element.24), channel_id=1, source_target_pairs={{0,8},{1,9},{2,10},{3,11},{4,12},{5,13},{6,14},{7,15},{8,16},{9,17... | collective-permute-start | bytes 122888 | tf_op jit(solution)/shard_map/ppermute | solution.py:91
  17.3 2.2 %collective-permute-start.8 = (bf16[80,256]{1,0:T(8,128)(2,1)S(1)}, bf16[80,256]{1,0:T(8,128)(2,1)S(1)}, u32[]{:S(2)}, u32[]{:S(2)}) collective-permute-start(bf16[80,256]{1,0:T(8,128)(2,1)S(1)} %get-tuple-element.25), channel_id=1, source_target_pairs={{0,16},{1,17},{2,18},{3,19},{4,20},{5,21},{6,22},{7,23},{8,24},{9,... | collective-permute-start | bytes 122888 | tf_op jit(solution)/shard_map/ppermute | solution.py:91
  19.6 0.5 %collective-permute-start.9 = (bf16[80,256]{1,0:T(8,128)(2,1)S(1)}, bf16[80,256]{1,0:T(8,128)(2,1)S(1)}, u32[]{:S(2)}, u32[]{:S(2)}) collective-permute-start(bf16[80,256]{1,0:T(8,128)(2,1)S(1)} %get-tuple-element.26), channel_id=1, source_target_pairs={{0,24},{1,25},{2,26},{3,27},{4,28},{5,29},{6,30},{7,31},{8,0},{9,1... | collective-permute-start | bytes 122888 | tf_op jit(solution)/shard_map/ppermute | solution.py:91
  20.0 2.0 %collective-permute-done.7.refs_7_.refs_0_.refs_1_ = bf16[80,256]{1,0:T(8,128)(2,1)S(1)} collective-permute-done((bf16[80,256]{1,0:T(8,128)(2,1)S(1)}, bf16[80,256]{1,0:T(8,128)(2,1)S(1)}, u32[]{:S(2)}, u32[]{:S(2)}) %collective-permute-start.7) | collective-permute-done | bytes 40992 | tf_op jit(solution)/shard_map/ppermute | solution.py:91
  22.0 0.9 %collective-permute-done.8.refs_8_.refs_1_.refs_2_ = bf16[80,256]{1,0:T(8,128)(2,1)S(1)} collective-permute-done((bf16[80,256]{1,0:T(8,128)(2,1)S(1)}, bf16[80,256]{1,0:T(8,128)(2,1)S(1)}, u32[]{:S(2)}, u32[]{:S(2)}) %collective-permute-start.8) | collective-permute-done | bytes 40992 | tf_op jit(solution)/shard_map/ppermute | solution.py:91
  22.9 0.7 %collective-permute-done.9.refs_9_.refs_2_.refs_3_ = bf16[80,256]{1,0:T(8,128)(2,1)S(1)} collective-permute-done((bf16[80,256]{1,0:T(8,128)(2,1)S(1)}, bf16[80,256]{1,0:T(8,128)(2,1)S(1)}, u32[]{:S(2)}, u32[]{:S(2)}) %collective-permute-start.9) | collective-permute-done | bytes 40992 | tf_op jit(solution)/shard_map/ppermute | solution.py:91
  23.6 0.0 collective-permute-done.5.refs_3_.by_x_ref
  23.6 1.6 %collective-permute-start.10 = (bf16[224,512]{1,0:T(8,128)(2,1)S(1)}, bf16[224,512]{1,0:T(8,128)(2,1)S(1)}, u32[]{:S(2)}, u32[]{:S(2)}) collective-permute-start(bf16[224,512]{1,0:T(8,128)(2,1)S(1)} %rows_to_y.1), channel_id=1, source_target_pairs={{0,2},{1,3},{2,0},{3,1},{4,6},{5,7},{6,4},{7,5},{8,10},{9,11},{10,... | collective-permute-start | bytes 688136 | tf_op jit(solution)/shard_map/ppermute | solution.py:91
  25.2 0.1 rest_to_x.1
  25.3 1.6 %collective-permute-start.11 = (bf16[80,512]{1,0:T(8,128)(2,1)S(1)}, bf16[80,512]{1,0:T(8,128)(2,1)S(1)}, u32[]{:S(2)}, u32[]{:S(2)}) collective-permute-start(bf16[80,512]{1,0:T(8,128)(2,1)S(1)} %rest_to_x.1), channel_id=1, source_target_pairs={{0,1},{1,0},{2,3},{3,2},{4,5},{5,4},{6,7},{7,6},{8,9},{9,8},{10,11... | collective-permute-start | bytes 245768 | tf_op jit(solution)/shard_map/ppermute | solution.py:91
  26.8 1.5 %near.1 = (f32[768,512]{1,0:T(8,128)S(1)}, f32[768,512]{1,0:T(8,128)S(1)}, bf16[512,512]{1,0:T(8,128)(2,1)S(1)}, bf16[512,512]{1,0:T(8,128)(2,1)S(1)}) custom-call(bf16[64,512]{1,0:T(8,128)(2,1)S(1)} %get-tuple-element.18.refs_0_, bf16[192,512]{1,0:T(8,128)(2,1)S(1)} %get-tuple-element.22.refs_1_, ...), custom_call_target="tpu_custom_call" | custom-call | tf_op jit(solution)/shard_map/near/pallas_call | solution.py:411
  28.3 1.5 %collective-permute-done.11.by_x_ref = bf16[80,512]{1,0:T(8,128)(2,1)S(1)} collective-permute-done((bf16[80,512]{1,0:T(8,128)(2,1)S(1)}, bf16[80,512]{1,0:T(8,128)(2,1)S(1)}, u32[]{:S(2)}, u32[]{:S(2)}) %collective-permute-start.11) | collective-permute-done | bytes 81952 | tf_op jit(solution)/shard_map/ppermute | solution.py:91
  29.8 0.0 collective-permute-done.10.by_y_ref
  29.8 0.4 %far.3 = bf16[768,512]{1,0:T(8,128)(2,1)S(1)} custom-call(f32[768,512]{1,0:T(8,128)S(1)} %get-tuple-element.28.near_ref, bf16[224,512]{1,0:T(8,128)(2,1)S(1)} %collective-permute-done.10.by_y_ref, bf16[80,512]{1,0:T(8,128)(2,1)S(1)} %collective-permute-done.11.by_x_ref), custom_call_target="tpu_custom_call" | custom-call | tf_op jit(solution)/shard_map/far/pallas_call | solution.py:425
  30.2 0.1 collective-permute-start.12
  30.3 0.4 %far.2.own_ref = f32[768,512]{1,0:T(8,128)S(1)} custom-call(f32[768,512]{1,0:T(8,128)S(1)} %get-tuple-element.27.near_ref, bf16[224,512]{1,0:T(8,128)(2,1)S(1)} %collective-permute-done.10.by_y_ref, bf16[80,512]{1,0:T(8,128)(2,1)S(1)} %collective-permute-done.11.by_x_ref), custom_call_target="tpu_custom_call" | custom-call | tf_op jit(solution)/shard_map/far/pallas_call | solution.py:425
  30.8 1.8 %collective-permute-done.12.other_ref = bf16[768,512]{1,0:T(8,128)(2,1)S(1)} collective-permute-done((bf16[768,512]{1,0:T(8,128)(2,1)S(1)}, bf16[768,512]{1,0:T(8,128)(2,1)S(1)}, u32[]{:S(2)}, u32[]{:S(2)}) %collective-permute-start.12) | collective-permute-done | bytes 786464 | tf_op jit(solution)/shard_map/ppermute | solution.py:91
  32.6 2.1 %inverse.1 = f32[768,512]{1,0:T(8,128)} custom-call(f32[768,512]{1,0:T(8,128)S(1)} %far.2.own_ref, bf16[768,512]{1,0:T(8,128)(2,1)S(1)} %collective-permute-done.12.other_ref, bf16[512,512]{1,0:T(8,128)(2,1)S(1)} %get-tuple-element.29.high_ref, bf16[512,512]{1,0:T(8,128)(2,1)S(1)} %get-tuple-element.30.low_ref), custom_call_target="tpu_custom_call" | custom-call | tf_op jit(solution)/shard_map/inverse/pallas_call | solution.py:436
  (4 shorter events, 0.0 us)
Async XLA Ops:
  0.0 26.8 %copy-start = (f32[512,512]{1,0:T(8,128)S(1)}, f32[512,512]{1,0:T(8,128)}, u32[]{:S(2)}) copy-start(f32[512,512]{1,0:T(8,128)} %refs_10_.1) | copy-start | bytes 3145732
  1.7 13.4 %collective-permute-start.1 = (bf16[64,1152]{1,0:T(8,128)(2,1)S(1)}, bf16[64,1152]{1,0:T(8,128)(2,1)S(1)}, u32[]{:S(2)}, u32[]{:S(2)}) collective-permute-start(bf16[64,1152]{1,0:T(8,128)(2,1)S(1)} %get-tuple-element.21), channel_id=1, source_target_pairs={{0,2},{1,3},{2,0},{3,1},{4,6},{5,7},{6,4},{7,5},{8,10},{9,11},{10,... | collective-permute-start | bytes 442376 | tf_op jit(solution)/shard_map/ppermute | solution.py:91
  4.7 10.3 %collective-permute-start = (bf16[64,896]{1,0:T(8,128)(2,1)S(1)}, bf16[64,896]{1,0:T(8,128)(2,1)S(1)}, u32[]{:S(2)}, u32[]{:S(2)}) collective-permute-start(bf16[64,896]{1,0:T(8,128)(2,1)S(1)} %get-tuple-element.20), channel_id=1, source_target_pairs={{0,1},{1,0},{2,3},{3,2},{4,5},{5,4},{6,7},{7,6},{8,9},{9,8},{10,11... | collective-permute-start | bytes 344072 | tf_op jit(solution)/shard_map/ppermute | solution.py:91
  6.2 6.8 %collective-permute-start.2 = (bf16[64,512]{1,0:T(8,128)(2,1)S(1)}, bf16[64,512]{1,0:T(8,128)(2,1)S(1)}, u32[]{:S(2)}, u32[]{:S(2)}) collective-permute-start(bf16[64,512]{1,0:T(8,128)(2,1)S(1)} %get-tuple-element.18.refs_0_), channel_id=1, source_target_pairs={{0,8},{1,9},{2,10},{3,11},{4,12},{5,13},{6,14},{7,15},{8,16},{9,17... | collective-permute-start | bytes 196616 | tf_op jit(solution)/shard_map/ppermute | solution.py:91
  7.8 7.2 %collective-permute-start.3 = (bf16[64,512]{1,0:T(8,128)(2,1)S(1)}, bf16[64,512]{1,0:T(8,128)(2,1)S(1)}, u32[]{:S(2)}, u32[]{:S(2)}) collective-permute-start(bf16[64,512]{1,0:T(8,128)(2,1)S(1)} %get-tuple-element.18.refs_0_), channel_id=1, source_target_pairs={{0,16},{1,17},{2,18},{3,19},{4,20},{5,21},{6,22},{7,23},{8,24},{9,... | collective-permute-start | bytes 196616 | tf_op jit(solution)/shard_map/ppermute | solution.py:91
  10.4 4.7 %collective-permute-start.4 = (bf16[64,512]{1,0:T(8,128)(2,1)S(1)}, bf16[64,512]{1,0:T(8,128)(2,1)S(1)}, u32[]{:S(2)}, u32[]{:S(2)}) collective-permute-start(bf16[64,512]{1,0:T(8,128)(2,1)S(1)} %get-tuple-element.18.refs_0_), channel_id=1, source_target_pairs={{0,24},{1,25},{2,26},{3,27},{4,28},{5,29},{6,30},{7,31},{8,0},{9,1... | collective-permute-start | bytes 196616 | tf_op jit(solution)/shard_map/ppermute | solution.py:91
  15.2 8.4 %collective-permute-start.5 = (bf16[192,512]{1,0:T(8,128)(2,1)S(1)}, bf16[192,512]{1,0:T(8,128)(2,1)S(1)}, u32[]{:S(2)}, u32[]{:S(2)}) collective-permute-start(bf16[192,512]{1,0:T(8,128)(2,1)S(1)} %get-tuple-element.22.refs_1_), channel_id=1, source_target_pairs={{0,1},{1,0},{2,3},{3,2},{4,5},{5,4},{6,7},{7,6},{8,9},{9,8},{10,11... | collective-permute-start | bytes 589832 | tf_op jit(solution)/shard_map/ppermute | solution.py:91
  15.8 9.4 %collective-permute-start.6 = (bf16[192,512]{1,0:T(8,128)(2,1)S(1)}, bf16[192,512]{1,0:T(8,128)(2,1)S(1)}, u32[]{:S(2)}, u32[]{:S(2)}) collective-permute-start(bf16[192,512]{1,0:T(8,128)(2,1)S(1)} %get-tuple-element.22.refs_1_), channel_id=1, source_target_pairs={{0,2},{1,3},{2,0},{3,1},{4,6},{5,7},{6,4},{7,5},{8,10},{9,11},{10,... | collective-permute-start | bytes 589832 | tf_op jit(solution)/shard_map/ppermute | solution.py:91
  16.2 5.8 %collective-permute-start.7 = (bf16[80,256]{1,0:T(8,128)(2,1)S(1)}, bf16[80,256]{1,0:T(8,128)(2,1)S(1)}, u32[]{:S(2)}, u32[]{:S(2)}) collective-permute-start(bf16[80,256]{1,0:T(8,128)(2,1)S(1)} %get-tuple-element.24), channel_id=1, source_target_pairs={{0,8},{1,9},{2,10},{3,11},{4,12},{5,13},{6,14},{7,15},{8,16},{9,17... | collective-permute-start | bytes 122888 | tf_op jit(solution)/shard_map/ppermute | solution.py:91
  17.3 5.5 %collective-permute-start.8 = (bf16[80,256]{1,0:T(8,128)(2,1)S(1)}, bf16[80,256]{1,0:T(8,128)(2,1)S(1)}, u32[]{:S(2)}, u32[]{:S(2)}) collective-permute-start(bf16[80,256]{1,0:T(8,128)(2,1)S(1)} %get-tuple-element.25), channel_id=1, source_target_pairs={{0,16},{1,17},{2,18},{3,19},{4,20},{5,21},{6,22},{7,23},{8,24},{9,... | collective-permute-start | bytes 122888 | tf_op jit(solution)/shard_map/ppermute | solution.py:91
  19.6 4.0 %collective-permute-start.9 = (bf16[80,256]{1,0:T(8,128)(2,1)S(1)}, bf16[80,256]{1,0:T(8,128)(2,1)S(1)}, u32[]{:S(2)}, u32[]{:S(2)}) collective-permute-start(bf16[80,256]{1,0:T(8,128)(2,1)S(1)} %get-tuple-element.26), channel_id=1, source_target_pairs={{0,24},{1,25},{2,26},{3,27},{4,28},{5,29},{6,30},{7,31},{8,0},{9,1... | collective-permute-start | bytes 122888 | tf_op jit(solution)/shard_map/ppermute | solution.py:91
  23.6 6.2 %collective-permute-start.10 = (bf16[224,512]{1,0:T(8,128)(2,1)S(1)}, bf16[224,512]{1,0:T(8,128)(2,1)S(1)}, u32[]{:S(2)}, u32[]{:S(2)}) collective-permute-start(bf16[224,512]{1,0:T(8,128)(2,1)S(1)} %rows_to_y.1), channel_id=1, source_target_pairs={{0,2},{1,3},{2,0},{3,1},{4,6},{5,7},{6,4},{7,5},{8,10},{9,11},{10,... | collective-permute-start | bytes 688136 | tf_op jit(solution)/shard_map/ppermute | solution.py:91
  25.3 4.5 %collective-permute-start.11 = (bf16[80,512]{1,0:T(8,128)(2,1)S(1)}, bf16[80,512]{1,0:T(8,128)(2,1)S(1)}, u32[]{:S(2)}, u32[]{:S(2)}) collective-permute-start(bf16[80,512]{1,0:T(8,128)(2,1)S(1)} %rest_to_x.1), channel_id=1, source_target_pairs={{0,1},{1,0},{2,3},{3,2},{4,5},{5,4},{6,7},{7,6},{8,9},{9,8},{10,11... | collective-permute-start | bytes 245768 | tf_op jit(solution)/shard_map/ppermute | solution.py:91
  30.2 2.4 %collective-permute-start.12 = (bf16[768,512]{1,0:T(8,128)(2,1)S(1)}, bf16[768,512]{1,0:T(8,128)(2,1)S(1)}, u32[]{:S(2)}, u32[]{:S(2)}) collective-permute-start(bf16[768,512]{1,0:T(8,128)(2,1)S(1)} %far.3), channel_id=1, source_target_pairs={{0,4},{1,5},{2,6},{3,7},{4,0},{5,1},{6,2},{7,3},{8,12},{9,13},{10,... | collective-permute-start | bytes 2359304 | tf_op jit(solution)/shard_map/ppermute | solution.py:91

commit v8 on v7

--- a/solution.py
+++ b/solution.py
@@ -93,8 +93,8 @@
 
 def pack_kernel(sizes, lists_hbm, masks_hbm, order_hbm, weights_hbm, panel_hbm, jac_hbm, *refs):
     layers, owners, per_owner, block_count, slot_count, block_rows, tile_width = sizes
-    weighted_ref, kept_ref, to_x_ref, to_y_ref = refs[:4]
-    lists_ref, masks_ref, order_ref, weights_ref, panel_ref, jac_ref, places_ref, turned_ref, sems = refs[4:]
+    weighted_ref, parcels_ref = refs[:2]
+    lists_ref, masks_ref, order_ref, weights_ref, panel_ref, jac_ref, places_ref, turned_ref, sems = refs[2:]
     copies = [
         pltpu.make_async_copy(order_hbm, order_ref, sems.at[0]),
         pltpu.make_async_copy(lists_hbm, lists_ref, sems.at[1]),
@@ -111,7 +111,7 @@
     post = layers * lane_group
     slab = tile_width // layers
     part = slab // 2
-    me_r, me_c = lax.axis_index("rows"), lax.axis_index("cols")
+    me_r = lax.axis_index("rows")
     me_z, me_core = me_r // 2, lax.rem(me_r, 2)
     for copy in copies:
         copy.wait()
@@ -121,8 +121,8 @@
     column = jnp.sum(jnp.where(row_ids == lane_ids, weights_ref[...], 0.0), axis=1, keepdims=True)
     weighted = (column * panel_ref[...].astype(f32)).astype(bf16)
     weighted_ref[...] = weighted
-    to_x_ref[:, :width] = weighted
-    to_y_ref[:, :width] = weighted
+    for c in range(owners):
+        parcels_ref[c, :, :width] = weighted
 
     for b in range(block_count):
         block = jac_ref[b * block_rows : (b + 1) * block_rows, :].astype(f32)
@@ -141,11 +141,8 @@
         slots.append((place - owner * per_owner, jnp.where(masks_ref[b, k] == 1, owner, -1)))
 
     shape = (16, CAP * block_count * block_rows)
-    lane, row = lax.broadcasted_iota(jnp.int32, shape, 1), lax.broadcasted_iota(jnp.int32, shape, 0)
-    notes = []
-    spots = [(kept_ref, 0), (to_x_ref, width), (to_y_ref, width), (to_y_ref, width + post)]
-    for e, (parcel, start) in enumerate(spots):
-        wanted = me_c ^ e
+    lane = lax.broadcasted_iota(jnp.int32, shape, 1)
+    for wanted in range(owners):
         found = jnp.int32(0)
         chosen = [jnp.int32(0)] * CAP
         codes = [jnp.int32(-1)] * CAP
@@ -163,7 +160,7 @@
                 here = (lane >= at) & (lane < at + block_rows)
                 code = jnp.where(chosen[j] // slot_count == b, codes[j], -1)
                 note = jnp.where(here, code, note)
-        notes.append(note)
+        parcels_ref[wanted, :16, width + post :] = note.astype(f32).astype(bf16)
         for k in range(layers):
             z = lax.rem(me_z + k, layers)
             for u in range(2):
@@ -171,11 +168,8 @@
                 for j in range(CAP):
                     first = pl.multiple_of(chosen[j] * tile_width + z * slab + core * part, part)
                     piece = turned_ref[pl.ds(first, part), :].astype(bf16)
-                    to = start + k * lane_group + j * block_rows
-                    parcel[u * part : (u + 1) * part, to : to + block_rows] = piece
-    kept_ref[:16, post:] = notes[0].astype(f32).astype(bf16)
-    to_x_ref[:16, width + post :] = notes[1].astype(f32).astype(bf16)
-    to_y_ref[:16, width + 2 * post :] = jnp.where(row == 0, notes[2], notes[3]).astype(f32).astype(bf16)
+                    to = width + k * lane_group + j * block_rows
+                    parcels_ref[wanted, u * part : (u + 1) * part, to : to + block_rows] = piece
 
 
 def row_of(block, i):
@@ -191,43 +185,30 @@
     return block.astype(jnp.bfloat16)
 
 
-def sort_kernel(sizes, kept_ref, from_x_ref, from_y_ref, *refs):
-    layers, width, lane_group, wide = sizes
-    line, (stacked, *posts) = refs[: layers - 1], refs[layers - 1 :]
-    post = layers * lane_group
-    rows = kept_ref.shape[0]
+def sort_kernel(sizes, parcels_ref, *refs):
+    layers, owners, width, lane_group, wide = sizes
+    line, (stacked, mail_ref) = refs[: layers - 1], refs[layers - 1 :]
+    rows = parcels_ref.shape[1]
+    me_z, me_c = lax.axis_index("rows") // 2, lax.axis_index("cols")
     for k, ref in enumerate(line):
         stacked[k * rows : (k + 1) * rows, :] = ref[...]
-    spots = [(kept_ref, 0), (from_x_ref, width), (from_y_ref, width), (from_y_ref, width + post)]
-    notes = [row_of(ref[:16, ref.shape[1] - wide :], int(e == 3)) for e, (ref, start) in enumerate(spots)]
-    block = rows_from(notes)
-    for k, out in enumerate(posts):
-        for e, (ref, start) in enumerate(spots):
-            piece = ref[:, start + k * lane_group : start + (k + 1) * lane_group]
-            out[:rows, e * lane_group : (e + 1) * lane_group] = piece
-        out[rows:, :wide] = block
-
-
-def rows_to_y_kernel(from_x_ref, by_x_ref, *refs):
-    out_ref = refs[-1]
-    rows = from_x_ref.shape[0]
-    out_ref[:rows, :] = from_x_ref[:, : out_ref.shape[1]]
-    out_ref[rows:, :] = by_x_ref[: out_ref.shape[0] - rows, :]
-
-
-def rest_to_x_kernel(sizes, by_y_ref, *refs):
-    layers, lane_group, wide = sizes
-    posts, out_ref = refs[:layers], refs[layers]
-    rows = posts[0].shape[0] - 16
-    part = rows // 2
-    last = out_ref.shape[0] - part - 16
-    out_ref[:last, :] = by_y_ref[by_y_ref.shape[0] - last :, :]
-    for k, ref in enumerate(posts):
-        for u in range(2):
-            piece = ref[u * part : (u + 1) * part, 3 * lane_group : 4 * lane_group]
-            at = (u * layers + k) * lane_group
-            out_ref[last : last + part, at : at + lane_group] = piece
-    out_ref[last + part :, :wide] = rows_from([row_of(ref[rows:, :wide], 3) for ref in posts])
+    at = width + layers * lane_group
+    block = rows_from([row_of(parcels_ref[me_c ^ e, :16, at : at + wide], 0) for e in range(owners)])
+    for k in range(layers):
+        z = lax.rem(me_z + k, layers)
+        for e in range(owners):
+            start = width + k * lane_group
+            piece = parcels_ref[me_c ^ e, :, start : start + lane_group]
+            mail_ref[z, :rows, e * lane_group : (e + 1) * lane_group] = piece
+        mail_ref[z, rows:, :wide] = block
+
+
+def first_kernel(in_ref, earlier_ref, out_ref):
+    out_ref[...] = in_ref[: out_ref.shape[0], :]
+
+
+def last_kernel(in_ref, earlier_ref, out_ref):
+    out_ref[...] = in_ref[in_ref.shape[0] - out_ref.shape[0] :, :]
 
 
 def place(out_ref, lanes, per_owner, pieces, notes, sizes):
@@ -249,10 +230,9 @@
         out_ref[n * part : (n + 1) * part, lanes] = placed
 
 
-def near_kernel(sizes, *refs):
+def near_kernel(sizes, panel_ref, others_ref, parcels_ref, by_x_ref, by_y_ref, mail_ref, factor_ref, *refs):
     layers, owners, per_owner, block_count, block_rows = sizes
-    panels, posts, factor_ref = refs[: 2 * (owners - 1)], refs[2 * (owners - 1) :][:layers], refs[2 * owners - 2 + layers]
-    own_ref, other_ref, high_ref, low_ref, placed_ref, rows_ref = refs[2 * owners - 1 + layers :]
+    own_ref, other_ref, own_far_ref, other_far_ref, high_ref, low_ref, placed_ref, rows_ref = refs
     f32, bf16 = jnp.float32, jnp.bfloat16
     turned = factor_ref[...].T
     high = turned.astype(bf16)
@@ -262,40 +242,33 @@
     group, wide = CAP * block_rows, CAP * rows
     part = rows // 2
     width = rows_ref.shape[1]
-    at = 0
-    for panel in panels:
-        rows_ref[at : at + panel.shape[0], :] = panel[:, :width]
-        at += panel.shape[0]
-    for u, out_ref in ((1, other_ref), (0, own_ref)):
-        for e in range(owners - 1):
+    depth = layers * rows
+    me_z, me_c = lax.axis_index("rows") // 2, lax.axis_index("cols")
+    for e, (first, rest) in enumerate(((None, others_ref), (1, by_x_ref), (2, by_y_ref))):
+        start = e * depth
+        rows_ref[start : start + rows, :] = panel_ref[...] if first is None else parcels_ref[me_c ^ e, :, :width]
+        rows_ref[start + rows : start + depth, :] = rest[...]
+    for u, out_ref, far_ref in ((1, other_ref, other_far_ref), (0, own_ref, own_far_ref)):
+        for e in range(owners):
             for h in range(layers // 2):
-                pair = posts[2 * h : 2 * h + 2]
-                pieces = [post[u * part : (u + 1) * part, e * group : (e + 1) * group] for post in pair]
-                notes = [row_of(post[rows:, :wide], e) for post in pair]
-                start = (e * layers + 2 * h) * rows
-                place(placed_ref, slice(start, start + 2 * rows), per_owner, pieces, notes, (block_count, block_rows))
+                pieces, notes = [], []
+                for k in (2 * h, 2 * h + 1):
+                    z = lax.rem(me_z + layers - k, layers)
+                    pieces.append(mail_ref[z, u * part : (u + 1) * part, e * group : (e + 1) * group])
+                    notes.append(row_of(mail_ref[z, rows:, :wide], e))
+                to_ref, start = (placed_ref, e * depth) if e < owners - 1 else (far_ref, 0)
+                lanes = slice(start + 2 * h * rows, start + 2 * (h + 1) * rows)
+                place(to_ref, lanes, per_owner, pieces, notes, (block_count, block_rows))
         out_ref[...] = jnp.dot(placed_ref[...], rows_ref[...], preferred_element_type=f32)
 
 
-def far_kernel(sizes, u, near_ref, by_y_ref, by_x_ref, out_ref, placed_ref, rows_ref):
-    layers, owners, per_owner, block_count, block_rows = sizes
-    f32, bf16 = jnp.float32, jnp.bfloat16
-    rows = block_count * block_rows
-    group, wide = CAP * block_rows, CAP * rows
-    part = rows // 2
-    first = by_y_ref.shape[0]
-    last = rows_ref.shape[0] - first
-    rows_ref[:first, :] = by_y_ref[...]
-    rows_ref[first:, :] = by_x_ref[:last, :]
-    for h in range(layers // 2):
-        pieces, notes = [], []
-        for k in (2 * h, 2 * h + 1):
-            at = (u * layers + k) * group
-            pieces.append(by_x_ref[last : last + part, at : at + group])
-            notes.append(row_of(by_x_ref[last + part :, :wide], k))
-        start = 2 * h * rows
-        place(placed_ref, slice(start, start + 2 * rows), per_owner, pieces, notes, (block_count, block_rows))
-    gram = near_ref[...] + jnp.dot(placed_ref[...], rows_ref[...], preferred_element_type=f32)
+def far_kernel(near_ref, placed_ref, parcels_ref, across_y_ref, across_x_ref, out_ref, rows_ref):
+    rows, first = parcels_ref.shape[1], across_y_ref.shape[0]
+    diagonal = lax.axis_index("cols") ^ (parcels_ref.shape[0] - 1)
+    rows_ref[:rows, :] = parcels_ref[diagonal, :, : rows_ref.shape[1]]
+    rows_ref[rows : rows + first, :] = across_y_ref[...]
+    rows_ref[rows + first :, :] = across_x_ref[...]
+    gram = near_ref[...] + jnp.dot(placed_ref[...], rows_ref[...], preferred_element_type=jnp.float32)
     out_ref[...] = gram.astype(out_ref.dtype)
 
 
@@ -345,14 +318,14 @@
     post = layers * lane_group
     wide = CAP * rows
     sizes = (layers, owners, per_owner, block_count, slot_count, block_rows, tile_width)
-    weighted, kept, to_x, to_y = pl.pallas_call(
+    weighted, parcels = pl.pallas_call(
         functools.partial(pack_kernel, sizes),
         out_shape=[
-            shaped((rows, width), bf16)
-            for width in (panel_width, post + wide, panel_width + post + wide, panel_width + 2 * post + wide)
+            shaped((rows, panel_width), bf16),
+            shaped((owners, rows, panel_width + post + wide), bf16),
         ],
         in_specs=[anywhere] * 6,
-        out_specs=[vmem] * 4,
+        out_specs=[vmem] * 2,
         scratch_shapes=[
             pltpu.SMEM(tile_lists.shape, jnp.int32),
             pltpu.SMEM(tile_masks.shape, jnp.int32),
@@ -368,71 +341,67 @@
         name="pack",
     )(*map(in_hbm, (tile_lists, tile_masks, tile_order, weights.reshape(1, rows), panel_jac, jac)))
     line = [shift(weighted, k, 0) for k in range(1, layers)]
-    from_x, from_y = shift(to_x, 0, 1), shift(to_y, 0, 2)
-
-    sizes = (layers, panel_width, lane_group, wide)
-    others, *posts = pl.pallas_call(
-        functools.partial(sort_kernel, sizes),
-        out_shape=[shaped(((layers - 1) * rows, panel_width), bf16)]
-        + [shaped((rows + 16, owners * lane_group), bf16)] * layers,
-        in_specs=[vmem] * (layers + 2),
-        out_specs=[vmem] * (layers + 1),
+    parcels = lax.all_to_all(parcels, "cols", split_axis=0, concat_axis=0, tiled=True)
+
+    others, mail = pl.pallas_call(
+        functools.partial(sort_kernel, (layers, owners, panel_width, lane_group, wide)),
+        out_shape=[
+            shaped(((layers - 1) * rows, panel_width), bf16),
+            shaped((layers, rows + 16, owners * lane_group), bf16),
+        ],
+        in_specs=[vmem] * layers,
+        out_specs=[vmem] * 2,
         compiler_params=params,
         name="sort",
-    )(kept, from_x, from_y, *line)
-    posts = [posts[0]] + [shift(posts[k], k, 0) for k in range(1, layers)]
+    )(parcels, *line)
     by_x, by_y = shift(others, 0, 1), shift(others, 0, 2)
-
-    last = rows // 2
-    rows_to_y = pl.pallas_call(
-        rows_to_y_kernel,
-        out_shape=shaped((rows + others.shape[0] - last, panel_width), bf16),
-        in_specs=[vmem] * 2 + [anywhere] * (layers - 1),
-        out_specs=vmem,
-        compiler_params=params,
-        name="rows_to_y",
-    )(from_x, by_x, *posts[1:])
-    across_y = shift(rows_to_y, 0, 2)
-    rest_to_x = pl.pallas_call(
-        functools.partial(rest_to_x_kernel, (layers, lane_group, wide)),
-        out_shape=shaped((last + rows // 2 + 16, panel_width), bf16),
-        in_specs=[vmem] * (layers + 1),
-        out_specs=vmem,
-        compiler_params=params,
-        name="rest_to_x",
-    )(by_y, *posts)
-    across_x = shift(rest_to_x, 0, 1)
+    same_core = [[r for r in range(slabs) if r % 2 == core] for core in range(2)]
+    mail = lax.all_to_all(mail, "rows", split_axis=0, concat_axis=0, axis_index_groups=same_core, tiled=True)
+
+    def cut(kernel, value, height, name):
+        return pl.pallas_call(
+            kernel,
+            out_shape=shaped((height, panel_width), bf16),
+            in_specs=[vmem, anywhere],
+            out_specs=vmem,
+            compiler_params=params,
+            name=name,
+        )(value, mail)
+
+    last = others.shape[0] // 4
+    across_y = shift(cut(first_kernel, by_x, others.shape[0] - last, "first"), 0, 2)
+    across_x = shift(cut(last_kernel, by_y, last, "last"), 0, 1)
 
     count = per_owner * slab_width
     depth = layers * rows
     sizes = (layers, owners, per_owner, block_count, block_rows)
     gram = shaped((count, panel_width), f32)
-    panels = [weighted, others, from_x, by_x, from_y, by_y]
-    own, other, high, low = pl.pallas_call(
+    far_placed = shaped((count, depth), bf16)
+    own, other, own_far, other_far, high, low = pl.pallas_call(
         functools.partial(near_kernel, sizes),
-        out_shape=[gram] * 2 + [shaped(factor_inverse.shape, bf16)] * 2,
-        in_specs=[vmem] * (len(panels) + layers + 1),
-        out_specs=[vmem] * 4,
+        out_shape=[gram] * 2 + [far_placed] * 2 + [shaped(factor_inverse.shape, bf16)] * 2,
+        in_specs=[vmem] * 7,
+        out_specs=[vmem] * 6,
         scratch_shapes=[
             pltpu.VMEM((count, (owners - 1) * depth), bf16),
             pltpu.VMEM(((owners - 1) * depth, panel_width), bf16),
         ],
         compiler_params=params,
         name="near",
-    )(*panels, *posts, factor_inverse)
-
-    def far(u, near, kind):
+    )(weighted, others, parcels, by_x, by_y, mail, factor_inverse)
+
+    def far(near, placed, kind):
         return pl.pallas_call(
-            functools.partial(far_kernel, sizes, u),
+            far_kernel,
             out_shape=shaped((count, panel_width), kind),
-            in_specs=[vmem] * 3,
+            in_specs=[vmem] * 5,
             out_specs=vmem,
-            scratch_shapes=[pltpu.VMEM((count, depth), bf16), pltpu.VMEM((depth, panel_width), bf16)],
+            scratch_shapes=[pltpu.VMEM((depth, panel_width), bf16)],
             compiler_params=params,
             name="far",
-        )(near, across_y, across_x)
-
-    other = shift(far(1, other, bf16), 0, 0, 1)
+        )(near, placed, parcels, across_y, across_x)
+
+    other = shift(far(other, other_far, bf16), 0, 0, 1)
     out = pl.pallas_call(
         inverse_kernel,
         out_shape=shaped((count, panel_width), f32),
@@ -441,7 +410,7 @@
         scratch_shapes=[pltpu.VMEM((count, panel_width), f32), pltpu.SemaphoreType.DMA((3,))],
         compiler_params=params,
         name="inverse",
-    )(far(0, own, f32), other, high, low)
+    )(far(own, own_far, f32), other, high, low)
     return out.reshape(per_owner, slab_width, panel_width)
 
 

time: 34.8 us -> 39.7 us (1.14)
  starting transfers between devices: 18.1 us -> 20.4 us
  Pallas kernels: 6.3 us -> 7.63 us
  waiting for transfers between devices: 10.2 us -> 11.3 us
    all_to_all x0 -> x2, starting transfers between devices: none -> 9.16 us  [the longest x1 5.18 us: local(): lax.all_to_all(parcels, 'cols', split_axis=0, concat_axis=0, tiled=True)]
    ppermute x13 -> x8, starting transfers between devices: 18.1 us -> 11.3 us  [shift(): return lax.ppermute(value, ('rows', 'cols'), pairs)]
    ppermute x13 -> x8, waiting for transfers between devices: 10.2 us -> 10.9 us  [shift(): return lax.ppermute(value, ('rows', 'cols'), pairs)]
    pallas_call x1, Pallas kernels: 1.65 us -> 2.41 us  [local(): pl.pallas_call(functools.partial(pack_kernel, sizes), out_shape=[shaped((...]
    pallas_call x5, Pallas kernels: 1.11 us -> 1.56 us  [the longest x1 0.81 us: local(): pl.pallas_call(functools.partial(sort_kernel, (layers, owners, panel_widt...]
  transfers between devices with their start and end apart: 13 -> 10, of which waited for: 8 -> 7; matrix products, arithmetic and copies ran while one was open for 0% -> 0% of each run, Pallas kernels for 6% -> 5%
where the time goes in v8:
time: 39.7 us; the launch traced here: 39.4 us
  starting transfers between devices  20.4 us (51%)
  waiting for transfers between devices  11.3 us (28%)
  Pallas kernels  7.63 us (19%)
    ppermute x8, starting transfers between devices, shift(): return lax.ppermute(value, ('rows', 'cols'), pairs)  11.3 us
    ppermute x8, waiting for transfers between devices, shift(): return lax.ppermute(value, ('rows', 'cols'), pairs)  10.9 us
    all_to_all x1, starting transfers between devices, local(): lax.all_to_all(parcels, 'cols', split_axis=0, concat_axis=0, tiled=True)  5.18 us
    all_to_all x1, starting transfers between devices, local(): lax.all_to_all(mail, 'rows', split_axis=0, concat_axis=0, axis_index_grou...  3.99 us
    pallas_call x1, Pallas kernels, local(): pl.pallas_call(functools.partial(pack_kernel, sizes), out_shape=[shaped((...  2.41 us
    pallas_call x1, Pallas kernels, local(): pl.pallas_call(inverse_kernel, out_shape=shaped((count, panel_width), f32...  2.09 us
    pallas_call x1, Pallas kernels, local(): pl.pallas_call(functools.partial(near_kernel, sizes), out_shape=[gram] *...  1.57 us
    pallas_call x1, Pallas kernels, local(): pl.pallas_call(functools.partial(sort_kernel, (layers, owners, panel_widt...  0.81 us
  transfers between devices with their start and end apart: 10, of which 7 were waited for; matrix products, arithmetic and copies ran while one was open for 0% of the time, Pallas kernels for 5%

profile of v8, /device:TPU:0, one launch (start us, length us, event | category | flops | bytes accessed | tf_op | source)
XLA Modules:
  0.0 39.4 jit_solution(12414553967609112648)
XLA Ops:
  0.0 0.0 copy-start
  0.0 2.4 %pack.1 = (bf16[64,512]{1,0:T(8,128)(2,1)S(1)}, bf16[4,64,896]{2,1,0:T(8,128)(2,1)}) custom-call(s32[2,4]{1,0:T(2,128)} %lists_hbm.1, s32[2,4]{1,0:T(2,128)} %masks_hbm.1, s32[96]{0:T(128)} %order_hbm.1, f32[1,64]{1,0:T(1,128)} %bitcast.2, bf16[64,512]{1,0:T(8,128)(2,1)} %panel_hbm.1, bf16[64,1024]{1,0:T(8,128)(2,1)} %jac_hbm.1), custom_call_target="tpu_custom_call" | custom-call | tf_op jit(solution)/shard_map/pack/pallas_call | solution.py:321
  2.4 5.2 %all-to-all-start = ((bf16[4,64,896]{2,1,0:T(8,128)(2,1)}), bf16[4,64,896]{2,1,0:T(8,128)(2,1)S(1)}, u32[]{:S(2)}, u32[]{:S(2)}) async-start(bf16[4,64,896]{2,1,0:T(8,128)(2,1)} %get-tuple-element.16), calls=%async_computation | async-start | bytes 917504 | tf_op jit(solution)/shard_map/all_to_all | solution.py:344
  7.6 1.6 %collective-permute-start = (bf16[64,512]{1,0:T(8,128)(2,1)S(1)}, bf16[64,512]{1,0:T(8,128)(2,1)S(1)}, u32[]{:S(2)}, u32[]{:S(2)}) collective-permute-start(bf16[64,512]{1,0:T(8,128)(2,1)S(1)} %get-tuple-element.15.panel_ref), channel_id=1, source_target_pairs={{0,8},{1,9},{2,10},{3,11},{4,12},{5,13},{6,14},{7,15},{8,16},{9,17... | collective-permute-start | bytes 196616 | tf_op jit(solution)/shard_map/ppermute | solution.py:91
  9.2 2.6 %collective-permute-start.1 = (bf16[64,512]{1,0:T(8,128)(2,1)S(1)}, bf16[64,512]{1,0:T(8,128)(2,1)S(1)}, u32[]{:S(2)}, u32[]{:S(2)}) collective-permute-start(bf16[64,512]{1,0:T(8,128)(2,1)S(1)} %get-tuple-element.15.panel_ref), channel_id=1, source_target_pairs={{0,16},{1,17},{2,18},{3,19},{4,20},{5,21},{6,22},{7,23},{8,24},{9,... | collective-permute-start | bytes 196616 | tf_op jit(solution)/shard_map/ppermute | solution.py:91
  11.8 1.3 %collective-permute-start.2 = (bf16[64,512]{1,0:T(8,128)(2,1)S(1)}, bf16[64,512]{1,0:T(8,128)(2,1)S(1)}, u32[]{:S(2)}, u32[]{:S(2)}) collective-permute-start(bf16[64,512]{1,0:T(8,128)(2,1)S(1)} %get-tuple-element.15.panel_ref), channel_id=1, source_target_pairs={{0,24},{1,25},{2,26},{3,27},{4,28},{5,29},{6,30},{7,31},{8,0},{9,1... | collective-permute-start | bytes 196616 | tf_op jit(solution)/shard_map/ppermute | solution.py:91
  13.1 1.3 %collective-permute-done.refs_0_ = bf16[64,512]{1,0:T(8,128)(2,1)S(1)} collective-permute-done((bf16[64,512]{1,0:T(8,128)(2,1)S(1)}, bf16[64,512]{1,0:T(8,128)(2,1)S(1)}, u32[]{:S(2)}, u32[]{:S(2)}) %collective-permute-start) | collective-permute-done | bytes 65568 | tf_op jit(solution)/shard_map/ppermute | solution.py:91
  14.4 2.2 %collective-permute-done.1.refs_1_ = bf16[64,512]{1,0:T(8,128)(2,1)S(1)} collective-permute-done((bf16[64,512]{1,0:T(8,128)(2,1)S(1)}, bf16[64,512]{1,0:T(8,128)(2,1)S(1)}, u32[]{:S(2)}, u32[]{:S(2)}) %collective-permute-start.1) | collective-permute-done | bytes 65568 | tf_op jit(solution)/shard_map/ppermute | solution.py:91
  16.6 0.0 collective-permute-done.2.refs_2_
  16.6 0.0 all-to-all-done.parcels_ref
  16.6 0.8 %sort.1 = (bf16[192,512]{1,0:T(8,128)(2,1)S(1)}, bf16[4,80,256]{2,1,0:T(8,128)(2,1)}) custom-call(bf16[4,64,896]{2,1,0:T(8,128)(2,1)S(1)} %all-to-all-done.parcels_ref, bf16[64,512]{1,0:T(8,128)(2,1)S(1)} %collective-permute-done.refs_0_, bf16[64,512]{1,0:T(8,128)(2,1)S(1)} %collective-permute-done.1.refs_1_, bf16[64,512]{1,0:T(8,128)(2,1)S(1)} %collective-permute-done.2.refs_2_), custom_call_target="tpu_custom_call" | custom-call | tf_op jit(solution)/shard_map/sort/pallas_call | solution.py:346
  17.4 4.0 %all-to-all-start.1 = ((bf16[4,80,256]{2,1,0:T(8,128)(2,1)}), bf16[4,80,256]{2,1,0:T(8,128)(2,1)S(1)}, u32[]{:S(2)}, u32[]{:S(2)}) async-start(bf16[4,80,256]{2,1,0:T(8,128)(2,1)} %get-tuple-element.18), calls=%async_computation.1 | async-start | bytes 327680 | tf_op jit(solution)/shard_map/all_to_all | solution.py:359
  21.4 1.9 %collective-permute-start.3 = (bf16[192,512]{1,0:T(8,128)(2,1)S(1)}, bf16[192,512]{1,0:T(8,128)(2,1)S(1)}, u32[]{:S(2)}, u32[]{:S(2)}) collective-permute-start(bf16[192,512]{1,0:T(8,128)(2,1)S(1)} %get-tuple-element.17.others_ref), channel_id=1, source_target_pairs={{0,1},{1,0},{2,3},{3,2},{4,5},{5,4},{6,7},{7,6},{8,9},{9,8},{10,11... | collective-permute-start | bytes 589832 | tf_op jit(solution)/shard_map/ppermute | solution.py:91
  23.3 1.5 %collective-permute-start.4 = (bf16[192,512]{1,0:T(8,128)(2,1)S(1)}, bf16[192,512]{1,0:T(8,128)(2,1)S(1)}, u32[]{:S(2)}, u32[]{:S(2)}) collective-permute-start(bf16[192,512]{1,0:T(8,128)(2,1)S(1)} %get-tuple-element.17.others_ref), channel_id=1, source_target_pairs={{0,2},{1,3},{2,0},{3,1},{4,6},{5,7},{6,4},{7,5},{8,10},{9,11},{10,... | collective-permute-start | bytes 589832 | tf_op jit(solution)/shard_map/ppermute | solution.py:91
  24.7 2.3 %collective-permute-done.3.by_x_ref.in_ref = bf16[192,512]{1,0:T(8,128)(2,1)S(1)} collective-permute-done((bf16[192,512]{1,0:T(8,128)(2,1)S(1)}, bf16[192,512]{1,0:T(8,128)(2,1)S(1)}, u32[]{:S(2)}, u32[]{:S(2)}) %collective-permute-start.3) | collective-permute-done | bytes 196640 | tf_op jit(solution)/shard_map/ppermute | solution.py:91
  27.1 0.3 all-to-all-done.1.mail_ref.earlier_ref
  27.4 1.9 %collective-permute-start.5 = (bf16[144,512]{1,0:T(8,128)(2,1)S(1)}, bf16[144,512]{1,0:T(8,128)(2,1)S(1)}, u32[]{:S(2)}, u32[]{:S(2)}) collective-permute-start(bf16[144,512]{1,0:T(8,128)(2,1)S(1)} %first.1), channel_id=1, source_target_pairs={{0,2},{1,3},{2,0},{3,1},{4,6},{5,7},{6,4},{7,5},{8,10},{9,11},{10,... | collective-permute-start | bytes 442376 | tf_op jit(solution)/shard_map/ppermute | solution.py:91
  29.4 1.1 %collective-permute-done.4.by_y_ref.in_ref = bf16[192,512]{1,0:T(8,128)(2,1)S(1)} collective-permute-done((bf16[192,512]{1,0:T(8,128)(2,1)S(1)}, bf16[192,512]{1,0:T(8,128)(2,1)S(1)}, u32[]{:S(2)}, u32[]{:S(2)}) %collective-permute-start.4) | collective-permute-done | bytes 196640 | tf_op jit(solution)/shard_map/ppermute | solution.py:91
  30.5 0.4 %collective-permute-start.6 = (bf16[48,512]{1,0:T(8,128)(2,1)S(1)}, bf16[48,512]{1,0:T(8,128)(2,1)S(1)}, u32[]{:S(2)}, u32[]{:S(2)}) collective-permute-start(bf16[48,512]{1,0:T(8,128)(2,1)S(1)} %last.1), channel_id=1, source_target_pairs={{0,1},{1,0},{2,3},{3,2},{4,5},{5,4},{6,7},{7,6},{8,9},{9,8},{10,11... | collective-permute-start | bytes 147464 | tf_op jit(solution)/shard_map/ppermute | solution.py:91
  30.9 0.0 copy-done
  30.9 1.6 %near.1 = (f32[768,512]{1,0:T(8,128)S(1)}, f32[768,512]{1,0:T(8,128)S(1)}, bf16[768,256]{1,0:T(8,128)(2,1)S(1)}, bf16[768,256]{1,0:T(8,128)(2,1)S(1)}, bf16[512,...) custom-call(bf16[64,512]{1,0:T(8,128)(2,1)S(1)} %get-tuple-element.15.panel_ref, ...), custom_call_target="tpu_custom_call" | custom-call | tf_op jit(solution)/shard_map/near/pallas_call | solution.py:380
  32.5 2.1 %collective-permute-done.6.across_x_ref = bf16[48,512]{1,0:T(8,128)(2,1)S(1)} collective-permute-done((bf16[48,512]{1,0:T(8,128)(2,1)S(1)}, bf16[48,512]{1,0:T(8,128)(2,1)S(1)}, u32[]{:S(2)}, u32[]{:S(2)}) %collective-permute-start.6) | collective-permute-done | bytes 49184 | tf_op jit(solution)/shard_map/ppermute | solution.py:91
  34.6 0.0 collective-permute-done.5.across_y_ref
  34.6 0.4 far.3
  35.0 0.1 collective-permute-start.7
  35.0 0.4 far.2.own_ref
  35.4 1.9 %collective-permute-done.7.other_ref = bf16[768,512]{1,0:T(8,128)(2,1)S(1)} collective-permute-done((bf16[768,512]{1,0:T(8,128)(2,1)S(1)}, bf16[768,512]{1,0:T(8,128)(2,1)S(1)}, u32[]{:S(2)}, u32[]{:S(2)}) %collective-permute-start.7) | collective-permute-done | bytes 786464 | tf_op jit(solution)/shard_map/ppermute | solution.py:91
  37.3 2.1 %inverse.1 = f32[768,512]{1,0:T(8,128)} custom-call(f32[768,512]{1,0:T(8,128)S(1)} %far.2.own_ref, bf16[768,512]{1,0:T(8,128)(2,1)S(1)} %collective-permute-done.7.other_ref, bf16[512,512]{1,0:T(8,128)(2,1)S(1)} %get-tuple-element.23.high_ref, bf16[512,512]{1,0:T(8,128)(2,1)S(1)} %get-tuple-element.24.low_ref), custom_call_target="tpu_custom_call" | custom-call | tf_op jit(solution)/shard_map/inverse/pallas_call | solution.py:405
  (2 shorter events, 0.0 us)
Async XLA Ops:
  0.0 30.9 %copy-start = (f32[512,512]{1,0:T(8,128)S(1)}, f32[512,512]{1,0:T(8,128)}, u32[]{:S(2)}) copy-start(f32[512,512]{1,0:T(8,128)} %factor_ref.1) | copy-start | bytes 3145732
  2.4 14.2 %all-to-all-start = ((bf16[4,64,896]{2,1,0:T(8,128)(2,1)}), bf16[4,64,896]{2,1,0:T(8,128)(2,1)S(1)}, u32[]{:S(2)}, u32[]{:S(2)}) async-start(bf16[4,64,896]{2,1,0:T(8,128)(2,1)} %get-tuple-element.16), calls=%async_computation | async-start | bytes 917504 | tf_op jit(solution)/shard_map/all_to_all | solution.py:344
  7.6 6.8 %collective-permute-start = (bf16[64,512]{1,0:T(8,128)(2,1)S(1)}, bf16[64,512]{1,0:T(8,128)(2,1)S(1)}, u32[]{:S(2)}, u32[]{:S(2)}) collective-permute-start(bf16[64,512]{1,0:T(8,128)(2,1)S(1)} %get-tuple-element.15.panel_ref), channel_id=1, source_target_pairs={{0,8},{1,9},{2,10},{3,11},{4,12},{5,13},{6,14},{7,15},{8,16},{9,17... | collective-permute-start | bytes 196616 | tf_op jit(solution)/shard_map/ppermute | solution.py:91
  9.2 7.4 %collective-permute-start.1 = (bf16[64,512]{1,0:T(8,128)(2,1)S(1)}, bf16[64,512]{1,0:T(8,128)(2,1)S(1)}, u32[]{:S(2)}, u32[]{:S(2)}) collective-permute-start(bf16[64,512]{1,0:T(8,128)(2,1)S(1)} %get-tuple-element.15.panel_ref), channel_id=1, source_target_pairs={{0,16},{1,17},{2,18},{3,19},{4,20},{5,21},{6,22},{7,23},{8,24},{9,... | collective-permute-start | bytes 196616 | tf_op jit(solution)/shard_map/ppermute | solution.py:91
  11.8 4.9 %collective-permute-start.2 = (bf16[64,512]{1,0:T(8,128)(2,1)S(1)}, bf16[64,512]{1,0:T(8,128)(2,1)S(1)}, u32[]{:S(2)}, u32[]{:S(2)}) collective-permute-start(bf16[64,512]{1,0:T(8,128)(2,1)S(1)} %get-tuple-element.15.panel_ref), channel_id=1, source_target_pairs={{0,24},{1,25},{2,26},{3,27},{4,28},{5,29},{6,30},{7,31},{8,0},{9,1... | collective-permute-start | bytes 196616 | tf_op jit(solution)/shard_map/ppermute | solution.py:91
  17.4 10.0 %all-to-all-start.1 = ((bf16[4,80,256]{2,1,0:T(8,128)(2,1)}), bf16[4,80,256]{2,1,0:T(8,128)(2,1)S(1)}, u32[]{:S(2)}, u32[]{:S(2)}) async-start(bf16[4,80,256]{2,1,0:T(8,128)(2,1)} %get-tuple-element.18), calls=%async_computation.1 | async-start | bytes 327680 | tf_op jit(solution)/shard_map/all_to_all | solution.py:359
  21.4 5.7 %collective-permute-start.3 = (bf16[192,512]{1,0:T(8,128)(2,1)S(1)}, bf16[192,512]{1,0:T(8,128)(2,1)S(1)}, u32[]{:S(2)}, u32[]{:S(2)}) collective-permute-start(bf16[192,512]{1,0:T(8,128)(2,1)S(1)} %get-tuple-element.17.others_ref), channel_id=1, source_target_pairs={{0,1},{1,0},{2,3},{3,2},{4,5},{5,4},{6,7},{7,6},{8,9},{9,8},{10,11... | collective-permute-start | bytes 589832 | tf_op jit(solution)/shard_map/ppermute | solution.py:91
  23.3 7.2 %collective-permute-start.4 = (bf16[192,512]{1,0:T(8,128)(2,1)S(1)}, bf16[192,512]{1,0:T(8,128)(2,1)S(1)}, u32[]{:S(2)}, u32[]{:S(2)}) collective-permute-start(bf16[192,512]{1,0:T(8,128)(2,1)S(1)} %get-tuple-element.17.others_ref), channel_id=1, source_target_pairs={{0,2},{1,3},{2,0},{3,1},{4,6},{5,7},{6,4},{7,5},{8,10},{9,11},{10,... | collective-permute-start | bytes 589832 | tf_op jit(solution)/shard_map/ppermute | solution.py:91
  27.4 7.1 %collective-permute-start.5 = (bf16[144,512]{1,0:T(8,128)(2,1)S(1)}, bf16[144,512]{1,0:T(8,128)(2,1)S(1)}, u32[]{:S(2)}, u32[]{:S(2)}) collective-permute-start(bf16[144,512]{1,0:T(8,128)(2,1)S(1)} %first.1), channel_id=1, source_target_pairs={{0,2},{1,3},{2,0},{3,1},{4,6},{5,7},{6,4},{7,5},{8,10},{9,11},{10,... | collective-permute-start | bytes 442376 | tf_op jit(solution)/shard_map/ppermute | solution.py:91
  30.5 4.1 %collective-permute-start.6 = (bf16[48,512]{1,0:T(8,128)(2,1)S(1)}, bf16[48,512]{1,0:T(8,128)(2,1)S(1)}, u32[]{:S(2)}, u32[]{:S(2)}) collective-permute-start(bf16[48,512]{1,0:T(8,128)(2,1)S(1)} %last.1), channel_id=1, source_target_pairs={{0,1},{1,0},{2,3},{3,2},{4,5},{5,4},{6,7},{7,6},{8,9},{9,8},{10,11... | collective-permute-start | bytes 147464 | tf_op jit(solution)/shard_map/ppermute | solution.py:91
  35.0 2.4 %collective-permute-start.7 = (bf16[768,512]{1,0:T(8,128)(2,1)S(1)}, bf16[768,512]{1,0:T(8,128)(2,1)S(1)}, u32[]{:S(2)}, u32[]{:S(2)}) collective-permute-start(bf16[768,512]{1,0:T(8,128)(2,1)S(1)} %far.3), channel_id=1, source_target_pairs={{0,4},{1,5},{2,6},{3,7},{4,0},{5,1},{6,2},{7,3},{8,12},{9,13},{10,... | collective-permute-start | bytes 2359304 | tf_op jit(solution)/shard_map/ppermute | solution.py:91

commit v9 on v7

--- a/solution.py
+++ b/solution.py
@@ -81,20 +81,23 @@
     return apply_inverse(gram, factor_inverse)
 
 
-def shift(value, steps_z, flip_cols, flip_core=0):
+NEAR_FLIPS = (0, 0), (1, 2), (2, 1), (3, 3)
+
+
+def shift(value, steps_z, e, flip_core=0):
     slabs, owners = lax.axis_size("rows"), lax.axis_size("cols")
     pairs = []
     for r in range(slabs):
         to_r = ((r // 2 + steps_z) % (slabs // 2)) * 2 + ((r % 2) ^ flip_core)
         for c in range(owners):
-            pairs.append((r * owners + c, to_r * owners + (c ^ flip_cols)))
+            pairs.append((r * owners + c, to_r * owners + (c ^ NEAR_FLIPS[e][r % 2])))
     return lax.ppermute(value, ("rows", "cols"), pairs)
 
 
 def pack_kernel(sizes, lists_hbm, masks_hbm, order_hbm, weights_hbm, panel_hbm, jac_hbm, *refs):
     layers, owners, per_owner, block_count, slot_count, block_rows, tile_width = sizes
-    weighted_ref, kept_ref, to_x_ref, to_y_ref = refs[:4]
-    lists_ref, masks_ref, order_ref, weights_ref, panel_ref, jac_ref, places_ref, turned_ref, sems = refs[4:]
+    weighted_ref, parcels = refs[0], refs[1 : 1 + layers]
+    lists_ref, masks_ref, order_ref, weights_ref, panel_ref, jac_ref, places_ref, turned_ref, sems = refs[1 + layers :]
     copies = [
         pltpu.make_async_copy(order_hbm, order_ref, sems.at[0]),
         pltpu.make_async_copy(lists_hbm, lists_ref, sems.at[1]),
@@ -108,7 +111,6 @@
     f32, bf16 = jnp.float32, jnp.bfloat16
     rows, width = panel_ref.shape
     lane_group = CAP * block_rows
-    post = layers * lane_group
     slab = tile_width // layers
     part = slab // 2
     me_r, me_c = lax.axis_index("rows"), lax.axis_index("cols")
@@ -121,8 +123,9 @@
     column = jnp.sum(jnp.where(row_ids == lane_ids, weights_ref[...], 0.0), axis=1, keepdims=True)
     weighted = (column * panel_ref[...].astype(f32)).astype(bf16)
     weighted_ref[...] = weighted
-    to_x_ref[:, :width] = weighted
-    to_y_ref[:, :width] = weighted
+    for parcel in parcels[1:]:
+        for i in range(width // 128):
+            parcel[i * rows : (i + 1) * rows, :] = weighted[:, i * 128 : (i + 1) * 128]
 
     for b in range(block_count):
         block = jac_ref[b * block_rows : (b + 1) * block_rows, :].astype(f32)
@@ -141,11 +144,10 @@
         slots.append((place - owner * per_owner, jnp.where(masks_ref[b, k] == 1, owner, -1)))
 
     shape = (16, CAP * block_count * block_rows)
-    lane, row = lax.broadcasted_iota(jnp.int32, shape, 1), lax.broadcasted_iota(jnp.int32, shape, 0)
+    lane = lax.broadcasted_iota(jnp.int32, shape, 1)
     notes = []
-    spots = [(kept_ref, 0), (to_x_ref, width), (to_y_ref, width), (to_y_ref, width + post)]
-    for e, (parcel, start) in enumerate(spots):
-        wanted = me_c ^ e
+    for e in range(owners):
+        wanted = me_c ^ jnp.where(me_core == 0, NEAR_FLIPS[e][0], NEAR_FLIPS[e][1])
         found = jnp.int32(0)
         chosen = [jnp.int32(0)] * CAP
         codes = [jnp.int32(-1)] * CAP
@@ -163,19 +165,21 @@
                 here = (lane >= at) & (lane < at + block_rows)
                 code = jnp.where(chosen[j] // slot_count == b, codes[j], -1)
                 note = jnp.where(here, code, note)
-        notes.append(note)
-        for k in range(layers):
+        notes.append(note.astype(f32)[:1])
+        for k, parcel in enumerate(parcels):
             z = lax.rem(me_z + k, layers)
+            top = parcel.shape[0] - 16 - rows * (owners * lane_group // 128)
             for u in range(2):
                 core = me_core ^ u
                 for j in range(CAP):
                     first = pl.multiple_of(chosen[j] * tile_width + z * slab + core * part, part)
                     piece = turned_ref[pl.ds(first, part), :].astype(bf16)
-                    to = start + k * lane_group + j * block_rows
-                    parcel[u * part : (u + 1) * part, to : to + block_rows] = piece
-    kept_ref[:16, post:] = notes[0].astype(f32).astype(bf16)
-    to_x_ref[:16, width + post :] = notes[1].astype(f32).astype(bf16)
-    to_y_ref[:16, width + 2 * post :] = jnp.where(row == 0, notes[2], notes[3]).astype(f32).astype(bf16)
+                    below, to = divmod(e * lane_group + j * block_rows, 128)
+                    start = top + below * rows + u * part
+                    parcel[start : start + part, to : to + block_rows] = piece
+    block = rows_from(notes)
+    for parcel in parcels:
+        parcel[parcel.shape[0] - 16 :, :] = block
 
 
 def row_of(block, i):
@@ -191,43 +195,39 @@
     return block.astype(jnp.bfloat16)
 
 
-def sort_kernel(sizes, kept_ref, from_x_ref, from_y_ref, *refs):
-    layers, width, lane_group, wide = sizes
-    line, (stacked, *posts) = refs[: layers - 1], refs[layers - 1 :]
-    post = layers * lane_group
-    rows = kept_ref.shape[0]
-    for k, ref in enumerate(line):
-        stacked[k * rows : (k + 1) * rows, :] = ref[...]
-    spots = [(kept_ref, 0), (from_x_ref, width), (from_y_ref, width), (from_y_ref, width + post)]
-    notes = [row_of(ref[:16, ref.shape[1] - wide :], int(e == 3)) for e, (ref, start) in enumerate(spots)]
-    block = rows_from(notes)
-    for k, out in enumerate(posts):
-        for e, (ref, start) in enumerate(spots):
-            piece = ref[:, start + k * lane_group : start + (k + 1) * lane_group]
-            out[:rows, e * lane_group : (e + 1) * lane_group] = piece
-        out[rows:, :wide] = block
-
-
-def rows_to_y_kernel(from_x_ref, by_x_ref, *refs):
-    out_ref = refs[-1]
-    rows = from_x_ref.shape[0]
-    out_ref[:rows, :] = from_x_ref[:, : out_ref.shape[1]]
-    out_ref[rows:, :] = by_x_ref[: out_ref.shape[0] - rows, :]
-
-
-def rest_to_x_kernel(sizes, by_y_ref, *refs):
-    layers, lane_group, wide = sizes
-    posts, out_ref = refs[:layers], refs[layers]
-    rows = posts[0].shape[0] - 16
+def sort_kernel(sizes, *refs):
+    layers, owners, rows, width, lane_group = sizes
+    parcels, (to_1_ref, to_2_ref, kept_ref) = refs[:layers], refs[-3:]
     part = rows // 2
-    last = out_ref.shape[0] - part - 16
-    out_ref[:last, :] = by_y_ref[by_y_ref.shape[0] - last :, :]
-    for k, ref in enumerate(posts):
-        for u in range(2):
-            piece = ref[u * part : (u + 1) * part, 3 * lane_group : 4 * lane_group]
-            at = (u * layers + k) * lane_group
-            out_ref[last : last + part, at : at + lane_group] = piece
-    out_ref[last + part :, :wide] = rows_from([row_of(ref[rows:, :wide], 3) for ref in posts])
+    for k, parcel in enumerate(parcels[1:]):
+        for i in range(width // 128):
+            piece = parcel[i * rows : (i + 1) * rows, :]
+            to_1_ref[k * rows : (k + 1) * rows, i * 128 : (i + 1) * 128] = piece
+            to_2_ref[k * rows : (k + 1) * rows, i * 128 : (i + 1) * 128] = piece
+    many = (layers - 1) * rows
+    for e, (ref, start) in enumerate(((kept_ref, 0), (to_1_ref, many), (to_2_ref, many), (to_1_ref, many + part))):
+        for k, parcel in enumerate(parcels):
+            top = parcel.shape[0] - 16 - rows * (owners * lane_group // 128)
+            below, lane = divmod(e * lane_group, 128)
+            for u in range(2):
+                at = top + below * rows + u * part
+                to = (u * layers + k) * lane_group
+                ref[start : start + part, to : to + lane_group] = parcel[at : at + part, lane : lane + lane_group]
+    notes = [[row_of(parcel[parcel.shape[0] - 16 :, :], e) for parcel in parcels] for e in range(owners)]
+    for ref, rows_of_codes in ((kept_ref, notes[0]), (to_1_ref, notes[1] + notes[3]), (to_2_ref, notes[2])):
+        ref[ref.shape[0] - 16 :, :128] = rows_from(rows_of_codes)
+
+
+def forward_1_kernel(many, by_1_ref, out_ref):
+    first = out_ref.shape[0] - (by_1_ref.shape[0] - many - 16) // 2 - 16
+    out_ref[:first, :] = by_1_ref[:first, :]
+    out_ref[first:, :] = by_1_ref[by_1_ref.shape[0] - out_ref.shape[0] + first :, :]
+
+
+def forward_2_kernel(many, first_2_ref, by_2_ref, out_ref):
+    rows = first_2_ref.shape[0]
+    out_ref[:rows, :] = first_2_ref[...]
+    out_ref[rows:, :] = by_2_ref[many - out_ref.shape[0] + rows : many, :]
 
 
 def place(out_ref, lanes, per_owner, pieces, notes, sizes):
@@ -249,52 +249,48 @@
         out_ref[n * part : (n + 1) * part, lanes] = placed
 
 
-def near_kernel(sizes, *refs):
+def place_all(out_ref, start, sizes, u, columns, codes, row):
     layers, owners, per_owner, block_count, block_rows = sizes
-    panels, posts, factor_ref = refs[: 2 * (owners - 1)], refs[2 * (owners - 1) :][:layers], refs[2 * owners - 2 + layers]
-    own_ref, other_ref, high_ref, low_ref, placed_ref, rows_ref = refs[2 * owners - 1 + layers :]
+    group, depth = CAP * block_rows, 2 * block_count * block_rows
+    for h in range(layers // 2):
+        pair = (2 * h, 2 * h + 1)
+        pieces = [columns[:, (u * layers + k) * group : (u * layers + k + 1) * group] for k in pair]
+        notes = [row_of(codes, row + k) for k in pair]
+        lanes = slice(start + h * depth, start + (h + 1) * depth)
+        place(out_ref, lanes, per_owner, pieces, notes, (block_count, block_rows))
+
+
+def near_kernel(sizes, own_0_ref, own_ref, kept_ref, first_1_ref, by_1_ref, first_2_ref, by_2_ref, factor_ref, *refs):
+    layers, owners, per_owner, block_count, block_rows = sizes
+    sum_ref, other_sum_ref, high_ref, low_ref, placed_ref, rows_ref = refs
     f32, bf16 = jnp.float32, jnp.bfloat16
     turned = factor_ref[...].T
     high = turned.astype(bf16)
     high_ref[...] = high
     low_ref[...] = (turned - high.astype(f32)).astype(bf16)
     rows = block_count * block_rows
-    group, wide = CAP * block_rows, CAP * rows
+    part, many, depth = rows // 2, (layers - 1) * rows, layers * rows
+    for e, (first_ref, ref) in enumerate(((own_0_ref, own_ref), (first_1_ref, by_1_ref), (first_2_ref, by_2_ref))):
+        rows_ref[e * depth : e * depth + rows, :] = first_ref[...]
+        rows_ref[e * depth + rows : (e + 1) * depth, :] = ref[:many, :]
+    for u, out_ref in ((1, other_sum_ref), (0, sum_ref)):
+        for e, (ref, start) in enumerate(((kept_ref, 0), (by_1_ref, many), (by_2_ref, many))):
+            columns, codes = ref[start : start + part, :], ref[ref.shape[0] - 16 :, :128]
+            place_all(placed_ref, e * depth, sizes, u, columns, codes, 0)
+        out_ref[...] = jnp.dot(placed_ref[...], rows_ref[...], preferred_element_type=f32)
+
+
+def far_kernel(sizes, u, near_ref, by_2_ref, by_1_ref, out_ref, placed_ref, rows_ref):
+    layers, owners, per_owner, block_count, block_rows = sizes
+    f32 = jnp.float32
+    rows = block_count * block_rows
     part = rows // 2
-    width = rows_ref.shape[1]
-    at = 0
-    for panel in panels:
-        rows_ref[at : at + panel.shape[0], :] = panel[:, :width]
-        at += panel.shape[0]
-    for u, out_ref in ((1, other_ref), (0, own_ref)):
-        for e in range(owners - 1):
-            for h in range(layers // 2):
-                pair = posts[2 * h : 2 * h + 2]
-                pieces = [post[u * part : (u + 1) * part, e * group : (e + 1) * group] for post in pair]
-                notes = [row_of(post[rows:, :wide], e) for post in pair]
-                start = (e * layers + 2 * h) * rows
-                place(placed_ref, slice(start, start + 2 * rows), per_owner, pieces, notes, (block_count, block_rows))
-        out_ref[...] = jnp.dot(placed_ref[...], rows_ref[...], preferred_element_type=f32)
-
-
-def far_kernel(sizes, u, near_ref, by_y_ref, by_x_ref, out_ref, placed_ref, rows_ref):
-    layers, owners, per_owner, block_count, block_rows = sizes
-    f32, bf16 = jnp.float32, jnp.bfloat16
-    rows = block_count * block_rows
-    group, wide = CAP * block_rows, CAP * rows
-    part = rows // 2
-    first = by_y_ref.shape[0]
-    last = rows_ref.shape[0] - first
-    rows_ref[:first, :] = by_y_ref[...]
-    rows_ref[first:, :] = by_x_ref[:last, :]
-    for h in range(layers // 2):
-        pieces, notes = [], []
-        for k in (2 * h, 2 * h + 1):
-            at = (u * layers + k) * group
-            pieces.append(by_x_ref[last : last + part, at : at + group])
-            notes.append(row_of(by_x_ref[last + part :, :wide], k))
-        start = 2 * h * rows
-        place(placed_ref, slice(start, start + 2 * rows), per_owner, pieces, notes, (block_count, block_rows))
+    first = by_2_ref.shape[0] - part - 16
+    rows_ref[:rows, :] = by_1_ref[:rows, :]
+    rows_ref[rows : rows + first, :] = by_2_ref[:first, :]
+    rows_ref[rows + first :, :] = by_1_ref[rows:, :]
+    columns, codes = by_2_ref[first : first + part, :], by_2_ref[first + part :, :128]
+    place_all(placed_ref, 0, sizes, u, columns, codes, layers)
     gram = near_ref[...] + jnp.dot(placed_ref[...], rows_ref[...], preferred_element_type=f32)
     out_ref[...] = gram.astype(out_ref.dtype)
 
@@ -342,17 +338,15 @@
         return pltpu.with_memory_space_constraint(value, pltpu.HBM)
 
     lane_group = CAP * block_rows
-    post = layers * lane_group
-    wide = CAP * rows
     sizes = (layers, owners, per_owner, block_count, slot_count, block_rows, tile_width)
-    weighted, kept, to_x, to_y = pl.pallas_call(
+    kept_height = rows * (owners * lane_group // 128) + 16
+    height = rows * (panel_width // 128) + kept_height
+    weighted, *parcels = pl.pallas_call(
         functools.partial(pack_kernel, sizes),
-        out_shape=[
-            shaped((rows, width), bf16)
-            for width in (panel_width, post + wide, panel_width + post + wide, panel_width + 2 * post + wide)
-        ],
+        out_shape=[shaped((rows, panel_width), bf16), shaped((kept_height, 128), bf16)]
+        + [shaped((height, 128), bf16)] * (layers - 1),
         in_specs=[anywhere] * 6,
-        out_specs=[vmem] * 4,
+        out_specs=[vmem] * (layers + 1),
         scratch_shapes=[
             pltpu.SMEM(tile_lists.shape, jnp.int32),
             pltpu.SMEM(tile_masks.shape, jnp.int32),
@@ -367,51 +361,48 @@
         compiler_params=params,
         name="pack",
     )(*map(in_hbm, (tile_lists, tile_masks, tile_order, weights.reshape(1, rows), panel_jac, jac)))
-    line = [shift(weighted, k, 0) for k in range(1, layers)]
-    from_x, from_y = shift(to_x, 0, 1), shift(to_y, 0, 2)
-
-    sizes = (layers, panel_width, lane_group, wide)
-    others, *posts = pl.pallas_call(
-        functools.partial(sort_kernel, sizes),
-        out_shape=[shaped(((layers - 1) * rows, panel_width), bf16)]
-        + [shaped((rows + 16, owners * lane_group), bf16)] * layers,
-        in_specs=[vmem] * (layers + 2),
-        out_specs=[vmem] * (layers + 1),
+    parcels = [parcels[0]] + [shift(parcels[k], k, 0) for k in range(1, layers)]
+    first_1, first_2 = shift(weighted, 0, 1), shift(weighted, 0, 2)
+
+    many, part = (layers - 1) * rows, rows // 2
+    to_1, to_2, kept = pl.pallas_call(
+        functools.partial(sort_kernel, (layers, owners, rows, panel_width, lane_group)),
+        out_shape=[shaped((more + 16, panel_width), bf16) for more in (many + 2 * part, many + part, part)],
+        in_specs=[vmem] * layers + [anywhere] * 2,
+        out_specs=[vmem] * 3,
         compiler_params=params,
         name="sort",
-    )(kept, from_x, from_y, *line)
-    posts = [posts[0]] + [shift(posts[k], k, 0) for k in range(1, layers)]
-    by_x, by_y = shift(others, 0, 1), shift(others, 0, 2)
-
-    last = rows // 2
-    rows_to_y = pl.pallas_call(
-        rows_to_y_kernel,
-        out_shape=shaped((rows + others.shape[0] - last, panel_width), bf16),
-        in_specs=[vmem] * 2 + [anywhere] * (layers - 1),
+    )(*parcels, first_1, first_2)
+    by_1, by_2 = shift(to_1, 0, 1), shift(to_2, 0, 2)
+
+    last = 16
+    forward_1 = pl.pallas_call(
+        functools.partial(forward_1_kernel, many),
+        out_shape=shaped((many - last + part + 16, panel_width), bf16),
+        in_specs=[vmem],
         out_specs=vmem,
         compiler_params=params,
-        name="rows_to_y",
-    )(from_x, by_x, *posts[1:])
-    across_y = shift(rows_to_y, 0, 2)
-    rest_to_x = pl.pallas_call(
-        functools.partial(rest_to_x_kernel, (layers, lane_group, wide)),
-        out_shape=shaped((last + rows // 2 + 16, panel_width), bf16),
-        in_specs=[vmem] * (layers + 1),
+        name="forward_1",
+    )(by_1)
+    across_2 = shift(forward_1, 0, 2)
+    forward_2 = pl.pallas_call(
+        functools.partial(forward_2_kernel, many),
+        out_shape=shaped((rows + last, panel_width), bf16),
+        in_specs=[vmem] * 2,
         out_specs=vmem,
         compiler_params=params,
-        name="rest_to_x",
-    )(by_y, *posts)
-    across_x = shift(rest_to_x, 0, 1)
+        name="forward_2",
+    )(first_2, by_2)
+    across_1 = shift(forward_2, 0, 1)
 
     count = per_owner * slab_width
     depth = layers * rows
     sizes = (layers, owners, per_owner, block_count, block_rows)
     gram = shaped((count, panel_width), f32)
-    panels = [weighted, others, from_x, by_x, from_y, by_y]
     own, other, high, low = pl.pallas_call(
         functools.partial(near_kernel, sizes),
         out_shape=[gram] * 2 + [shaped(factor_inverse.shape, bf16)] * 2,
-        in_specs=[vmem] * (len(panels) + layers + 1),
+        in_specs=[vmem] * 8,
         out_specs=[vmem] * 4,
         scratch_shapes=[
             pltpu.VMEM((count, (owners - 1) * depth), bf16),
@@ -419,7 +410,7 @@
         ],
         compiler_params=params,
         name="near",
-    )(*panels, *posts, factor_inverse)
+    )(weighted, to_1, kept, first_1, by_1, first_2, by_2, factor_inverse)
 
     def far(u, near, kind):
         return pl.pallas_call(
@@ -430,7 +421,7 @@
             scratch_shapes=[pltpu.VMEM((count, depth), bf16), pltpu.VMEM((depth, panel_width), bf16)],
             compiler_params=params,
             name="far",
-        )(near, across_y, across_x)
+        )(near, across_2, across_1)
 
     other = shift(far(1, other, bf16), 0, 0, 1)
     out = pl.pallas_call(

time: 34.8 us -> 35.1 us (level)
  waiting for transfers between devices: 10.2 us -> 13.8 us
  starting transfers between devices: 18.1 us -> 14.8 us
    ppermute x13 -> x10, waiting for transfers between devices: 10.2 us -> 13.8 us  [shift(): return lax.ppermute(value, ('rows', 'cols'), pairs)]
    ppermute x13 -> x10, starting transfers between devices: 18.1 us -> 14.8 us  [shift(): return lax.ppermute(value, ('rows', 'cols'), pairs)]
  transfers between devices with their start and end apart: 13 -> 10, of which waited for: 8 -> 6; matrix products, arithmetic and copies ran while one was open for 0% -> 0% of each run, Pallas kernels for 6% -> 6%
where the time goes in v9:
time: 35.1 us; the launch traced here: 35 us
  starting transfers between devices  14.8 us (42%)
  waiting for transfers between devices  13.8 us (39%)
  Pallas kernels  6.36 us (18%)
    ppermute x10, starting transfers between devices, shift(): return lax.ppermute(value, ('rows', 'cols'), pairs)  14.8 us
    ppermute x10, waiting for transfers between devices, shift(): return lax.ppermute(value, ('rows', 'cols'), pairs)  13.8 us
    pallas_call x1, Pallas kernels, local(): pl.pallas_call(inverse_kernel, out_shape=shaped((count, panel_width), f32...  2.08 us
    pallas_call x1, Pallas kernels, local(): pl.pallas_call(functools.partial(pack_kernel, sizes), out_shape=[shaped((...  1.62 us
    pallas_call x1, Pallas kernels, local(): pl.pallas_call(functools.partial(near_kernel, sizes), out_shape=[gram] *...  1.51 us
    pallas_call x2, Pallas kernels, far(): pl.pallas_call(functools.partial(far_kernel, sizes, u), out_shape=shaped(...  0.98 us
  transfers between devices with their start and end apart: 10, of which 6 were waited for; matrix products, arithmetic and copies ran while one was open for 0% of the time, Pallas kernels for 6%

profile of v9, /device:TPU:0, one launch (start us, length us, event | category | flops | bytes accessed | tf_op | source)
XLA Modules:
  0.0 35.0 jit_solution(17394298263771353791)
XLA Ops:
  0.0 0.0 copy-start
  0.0 1.6 %pack.1 = (bf16[64,512]{1,0:T(8,128)(2,1)S(1)}, bf16[144,128]{1,0:T(8,128)(2,1)S(1)}, bf16[400,128]{1,0:T(8,128)(2,1)S(1)}, bf16[400,128]{1,0:T(8,128)(2,1)S(1)}, bf16[400,128]{1,0:T(8,128)(2,1)S(1)}) custom-call(s32[2,4]{1,0:T(2,128)} %lists_hbm.1, s32[2,4]{1,0:T(2,128)} %masks_hbm.1, s32[96]{0:T(128)} %order_hbm.1, f32[1,64]{1,0:T(1,128)} %bitcast.2, ...), custom_call_target="tpu_custom_call" | custom-call | tf_op jit(solution)/shard_map/pack/pallas_call | solution.py:344
  1.6 3.1 %collective-permute-start = (bf16[400,128]{1,0:T(8,128)(2,1)S(1)}, bf16[400,128]{1,0:T(8,128)(2,1)S(1)}, u32[]{:S(2)}, u32[]{:S(2)}) collective-permute-start(bf16[400,128]{1,0:T(8,128)(2,1)S(1)} %get-tuple-element.19), channel_id=1, source_target_pairs={{0,8},{1,9},{2,10},{3,11},{4,12},{5,13},{6,14},{7,15},{8,16},{9,17... | collective-permute-start | bytes 307208 | tf_op jit(solution)/shard_map/ppermute | solution.py:94
  4.7 2.6 %collective-permute-start.1 = (bf16[400,128]{1,0:T(8,128)(2,1)S(1)}, bf16[400,128]{1,0:T(8,128)(2,1)S(1)}, u32[]{:S(2)}, u32[]{:S(2)}) collective-permute-start(bf16[400,128]{1,0:T(8,128)(2,1)S(1)} %get-tuple-element.20), channel_id=1, source_target_pairs={{0,16},{1,17},{2,18},{3,19},{4,20},{5,21},{6,22},{7,23},{8,24},{9,... | collective-permute-start | bytes 307208 | tf_op jit(solution)/shard_map/ppermute | solution.py:94
  7.3 1.3 %collective-permute-start.2 = (bf16[400,128]{1,0:T(8,128)(2,1)S(1)}, bf16[400,128]{1,0:T(8,128)(2,1)S(1)}, u32[]{:S(2)}, u32[]{:S(2)}) collective-permute-start(bf16[400,128]{1,0:T(8,128)(2,1)S(1)} %get-tuple-element.21), channel_id=1, source_target_pairs={{0,24},{1,25},{2,26},{3,27},{4,28},{5,29},{6,30},{7,31},{8,0},{9,1... | collective-permute-start | bytes 307208 | tf_op jit(solution)/shard_map/ppermute | solution.py:94
  8.6 1.5 %collective-permute-start.4 = (bf16[64,512]{1,0:T(8,128)(2,1)S(1)}, bf16[64,512]{1,0:T(8,128)(2,1)S(1)}, u32[]{:S(2)}, u32[]{:S(2)}) collective-permute-start(bf16[64,512]{1,0:T(8,128)(2,1)S(1)} %get-tuple-element.17.own_0_ref), channel_id=1, source_target_pairs={{0,2},{1,3},{2,0},{3,1},{4,5},{5,4},{6,7},{7,6},{8,10},{9,11},{10,... | collective-permute-start | bytes 196616 | tf_op jit(solution)/shard_map/ppermute | solution.py:94
  10.2 1.5 %collective-permute-start.3 = (bf16[64,512]{1,0:T(8,128)(2,1)S(1)}, bf16[64,512]{1,0:T(8,128)(2,1)S(1)}, u32[]{:S(2)}, u32[]{:S(2)}) collective-permute-start(bf16[64,512]{1,0:T(8,128)(2,1)S(1)} %get-tuple-element.17.own_0_ref), channel_id=1, source_target_pairs={{0,1},{1,0},{2,3},{3,2},{4,6},{5,7},{6,4},{7,5},{8,9},{9,8},{10,11... | collective-permute-start | bytes 196616 | tf_op jit(solution)/shard_map/ppermute | solution.py:94
  11.7 1.3 %collective-permute-done.4.refs_5_.first_2_ref = bf16[64,512]{1,0:T(8,128)(2,1)S(1)} collective-permute-done((bf16[64,512]{1,0:T(8,128)(2,1)S(1)}, bf16[64,512]{1,0:T(8,128)(2,1)S(1)}, u32[]{:S(2)}, u32[]{:S(2)}) %collective-permute-start.4) | collective-permute-done | bytes 65568 | tf_op jit(solution)/shard_map/ppermute | solution.py:94
  12.9 1.5 %collective-permute-done.3.refs_4_.first_1_ref = bf16[64,512]{1,0:T(8,128)(2,1)S(1)} collective-permute-done((bf16[64,512]{1,0:T(8,128)(2,1)S(1)}, bf16[64,512]{1,0:T(8,128)(2,1)S(1)}, u32[]{:S(2)}, u32[]{:S(2)}) %collective-permute-start.3) | collective-permute-done | bytes 65568 | tf_op jit(solution)/shard_map/ppermute | solution.py:94
  14.4 0.0 collective-permute-done.refs_1_
  14.4 0.0 collective-permute-done.1.refs_2_
  14.4 0.0 collective-permute-done.2.refs_3_
  14.4 0.1 sort.1
  14.6 1.6 %collective-permute-start.5 = (bf16[272,512]{1,0:T(8,128)(2,1)S(1)}, bf16[272,512]{1,0:T(8,128)(2,1)S(1)}, u32[]{:S(2)}, u32[]{:S(2)}) collective-permute-start(bf16[272,512]{1,0:T(8,128)(2,1)S(1)} %get-tuple-element.22.own_ref), channel_id=1, source_target_pairs={{0,1},{1,0},{2,3},{3,2},{4,6},{5,7},{6,4},{7,5},{8,9},{9,8},{10,11... | collective-permute-start | bytes 835592 | tf_op jit(solution)/shard_map/ppermute | solution.py:94
  16.2 1.2 %collective-permute-start.6 = (bf16[240,512]{1,0:T(8,128)(2,1)S(1)}, bf16[240,512]{1,0:T(8,128)(2,1)S(1)}, u32[]{:S(2)}, u32[]{:S(2)}) collective-permute-start(bf16[240,512]{1,0:T(8,128)(2,1)S(1)} %get-tuple-element.24), channel_id=1, source_target_pairs={{0,2},{1,3},{2,0},{3,1},{4,5},{5,4},{6,7},{7,6},{8,10},{9,11},{10,... | collective-permute-start | bytes 737288 | tf_op jit(solution)/shard_map/ppermute | solution.py:94
  17.4 6.6 %collective-permute-done.5.by_1_ref = bf16[272,512]{1,0:T(8,128)(2,1)S(1)} collective-permute-done((bf16[272,512]{1,0:T(8,128)(2,1)S(1)}, bf16[272,512]{1,0:T(8,128)(2,1)S(1)}, u32[]{:S(2)}, u32[]{:S(2)}) %collective-permute-start.5) | collective-permute-done | bytes 278560 | tf_op jit(solution)/shard_map/ppermute | solution.py:94
  24.0 0.3 collective-permute-start.7
  24.3 0.0 collective-permute-done.6.by_2_ref
  24.3 1.6 %collective-permute-start.8 = (bf16[80,512]{1,0:T(8,128)(2,1)S(1)}, bf16[80,512]{1,0:T(8,128)(2,1)S(1)}, u32[]{:S(2)}, u32[]{:S(2)}) collective-permute-start(bf16[80,512]{1,0:T(8,128)(2,1)S(1)} %forward_2.1), channel_id=1, source_target_pairs={{0,1},{1,0},{2,3},{3,2},{4,6},{5,7},{6,4},{7,5},{8,9},{9,8},{10,11... | collective-permute-start | bytes 245768 | tf_op jit(solution)/shard_map/ppermute | solution.py:94
  25.9 0.0 copy-done
  25.9 1.5 %near.1 = (f32[768,512]{1,0:T(8,128)S(1)}, f32[768,512]{1,0:T(8,128)S(1)}, bf16[512,512]{1,0:T(8,128)(2,1)S(1)}, bf16[512,512]{1,0:T(8,128)(2,1)S(1)}) custom-call(bf16[64,512]{1,0:T(8,128)(2,1)S(1)} %get-tuple-element.17.own_0_ref, bf16[272,512]{1,0:T(8,128)(2,1)S(1)} %get-tuple-element.22.own_ref, bf16[48,512]{1,0:T(8,128)(2,1)S(1)} %get-tuple-element.23.kept_ref, ...), custom_call_target="tpu_custom_call" | custom-call | tf_op jit(solution)/shard_map/near/pallas_call | solution.py:402
  27.4 1.4 %collective-permute-done.8.by_1_ref = bf16[80,512]{1,0:T(8,128)(2,1)S(1)} collective-permute-done((bf16[80,512]{1,0:T(8,128)(2,1)S(1)}, bf16[80,512]{1,0:T(8,128)(2,1)S(1)}, u32[]{:S(2)}, u32[]{:S(2)}) %collective-permute-start.8) | collective-permute-done | bytes 81952 | tf_op jit(solution)/shard_map/ppermute | solution.py:94
  28.8 1.2 %collective-permute-done.7.by_2_ref = bf16[224,512]{1,0:T(8,128)(2,1)S(1)} collective-permute-done((bf16[224,512]{1,0:T(8,128)(2,1)S(1)}, bf16[224,512]{1,0:T(8,128)(2,1)S(1)}, u32[]{:S(2)}, u32[]{:S(2)}) %collective-permute-start.7) | collective-permute-done | bytes 229408 | tf_op jit(solution)/shard_map/ppermute | solution.py:94
  30.1 0.5 %far.3 = bf16[768,512]{1,0:T(8,128)(2,1)S(1)} custom-call(f32[768,512]{1,0:T(8,128)S(1)} %get-tuple-element.26.near_ref, bf16[224,512]{1,0:T(8,128)(2,1)S(1)} %collective-permute-done.7.by_2_ref, bf16[80,512]{1,0:T(8,128)(2,1)S(1)} %collective-permute-done.8.by_1_ref), custom_call_target="tpu_custom_call" | custom-call | tf_op jit(solution)/shard_map/far/pallas_call | solution.py:416
  30.6 0.1 collective-permute-start.9
  30.6 0.5 %far.2.own_ref = f32[768,512]{1,0:T(8,128)S(1)} custom-call(f32[768,512]{1,0:T(8,128)S(1)} %get-tuple-element.25.near_ref, bf16[224,512]{1,0:T(8,128)(2,1)S(1)} %collective-permute-done.7.by_2_ref, bf16[80,512]{1,0:T(8,128)(2,1)S(1)} %collective-permute-done.8.by_1_ref), custom_call_target="tpu_custom_call" | custom-call | tf_op jit(solution)/shard_map/far/pallas_call | solution.py:416
  31.1 1.8 %collective-permute-done.9.other_ref = bf16[768,512]{1,0:T(8,128)(2,1)S(1)} collective-permute-done((bf16[768,512]{1,0:T(8,128)(2,1)S(1)}, bf16[768,512]{1,0:T(8,128)(2,1)S(1)}, u32[]{:S(2)}, u32[]{:S(2)}) %collective-permute-start.9) | collective-permute-done | bytes 786464 | tf_op jit(solution)/shard_map/ppermute | solution.py:94
  32.9 2.1 %inverse.1 = f32[768,512]{1,0:T(8,128)} custom-call(f32[768,512]{1,0:T(8,128)S(1)} %far.2.own_ref, bf16[768,512]{1,0:T(8,128)(2,1)S(1)} %collective-permute-done.9.other_ref, bf16[512,512]{1,0:T(8,128)(2,1)S(1)} %get-tuple-element.27.high_ref, bf16[512,512]{1,0:T(8,128)(2,1)S(1)} %get-tuple-element.28.low_ref), custom_call_target="tpu_custom_call" | custom-call | tf_op jit(solution)/shard_map/inverse/pallas_call | solution.py:427
  (2 shorter events, 0.0 us)
Async XLA Ops:
  0.0 25.9 %copy-start = (f32[512,512]{1,0:T(8,128)S(1)}, f32[512,512]{1,0:T(8,128)}, u32[]{:S(2)}) copy-start(f32[512,512]{1,0:T(8,128)} %factor_ref.1) | copy-start | bytes 3145732
  1.6 12.8 %collective-permute-start = (bf16[400,128]{1,0:T(8,128)(2,1)S(1)}, bf16[400,128]{1,0:T(8,128)(2,1)S(1)}, u32[]{:S(2)}, u32[]{:S(2)}) collective-permute-start(bf16[400,128]{1,0:T(8,128)(2,1)S(1)} %get-tuple-element.19), channel_id=1, source_target_pairs={{0,8},{1,9},{2,10},{3,11},{4,12},{5,13},{6,14},{7,15},{8,16},{9,17... | collective-permute-start | bytes 307208 | tf_op jit(solution)/shard_map/ppermute | solution.py:94
  4.7 9.7 %collective-permute-start.1 = (bf16[400,128]{1,0:T(8,128)(2,1)S(1)}, bf16[400,128]{1,0:T(8,128)(2,1)S(1)}, u32[]{:S(2)}, u32[]{:S(2)}) collective-permute-start(bf16[400,128]{1,0:T(8,128)(2,1)S(1)} %get-tuple-element.20), channel_id=1, source_target_pairs={{0,16},{1,17},{2,18},{3,19},{4,20},{5,21},{6,22},{7,23},{8,24},{9,... | collective-permute-start | bytes 307208 | tf_op jit(solution)/shard_map/ppermute | solution.py:94
  7.3 7.1 %collective-permute-start.2 = (bf16[400,128]{1,0:T(8,128)(2,1)S(1)}, bf16[400,128]{1,0:T(8,128)(2,1)S(1)}, u32[]{:S(2)}, u32[]{:S(2)}) collective-permute-start(bf16[400,128]{1,0:T(8,128)(2,1)S(1)} %get-tuple-element.21), channel_id=1, source_target_pairs={{0,24},{1,25},{2,26},{3,27},{4,28},{5,29},{6,30},{7,31},{8,0},{9,1... | collective-permute-start | bytes 307208 | tf_op jit(solution)/shard_map/ppermute | solution.py:94
  8.6 4.3 %collective-permute-start.4 = (bf16[64,512]{1,0:T(8,128)(2,1)S(1)}, bf16[64,512]{1,0:T(8,128)(2,1)S(1)}, u32[]{:S(2)}, u32[]{:S(2)}) collective-permute-start(bf16[64,512]{1,0:T(8,128)(2,1)S(1)} %get-tuple-element.17.own_0_ref), channel_id=1, source_target_pairs={{0,2},{1,3},{2,0},{3,1},{4,5},{5,4},{6,7},{7,6},{8,10},{9,11},{10,... | collective-permute-start | bytes 196616 | tf_op jit(solution)/shard_map/ppermute | solution.py:94
  10.2 4.3 %collective-permute-start.3 = (bf16[64,512]{1,0:T(8,128)(2,1)S(1)}, bf16[64,512]{1,0:T(8,128)(2,1)S(1)}, u32[]{:S(2)}, u32[]{:S(2)}) collective-permute-start(bf16[64,512]{1,0:T(8,128)(2,1)S(1)} %get-tuple-element.17.own_0_ref), channel_id=1, source_target_pairs={{0,1},{1,0},{2,3},{3,2},{4,6},{5,7},{6,4},{7,5},{8,9},{9,8},{10,11... | collective-permute-start | bytes 196616 | tf_op jit(solution)/shard_map/ppermute | solution.py:94
  14.6 9.4 %collective-permute-start.5 = (bf16[272,512]{1,0:T(8,128)(2,1)S(1)}, bf16[272,512]{1,0:T(8,128)(2,1)S(1)}, u32[]{:S(2)}, u32[]{:S(2)}) collective-permute-start(bf16[272,512]{1,0:T(8,128)(2,1)S(1)} %get-tuple-element.22.own_ref), channel_id=1, source_target_pairs={{0,1},{1,0},{2,3},{3,2},{4,6},{5,7},{6,4},{7,5},{8,9},{9,8},{10,11... | collective-permute-start | bytes 835592 | tf_op jit(solution)/shard_map/ppermute | solution.py:94
  16.2 8.2 %collective-permute-start.6 = (bf16[240,512]{1,0:T(8,128)(2,1)S(1)}, bf16[240,512]{1,0:T(8,128)(2,1)S(1)}, u32[]{:S(2)}, u32[]{:S(2)}) collective-permute-start(bf16[240,512]{1,0:T(8,128)(2,1)S(1)} %get-tuple-element.24), channel_id=1, source_target_pairs={{0,2},{1,3},{2,0},{3,1},{4,5},{5,4},{6,7},{7,6},{8,10},{9,11},{10,... | collective-permute-start | bytes 737288 | tf_op jit(solution)/shard_map/ppermute | solution.py:94
  24.0 6.1 %collective-permute-start.7 = (bf16[224,512]{1,0:T(8,128)(2,1)S(1)}, bf16[224,512]{1,0:T(8,128)(2,1)S(1)}, u32[]{:S(2)}, u32[]{:S(2)}) collective-permute-start(bf16[224,512]{1,0:T(8,128)(2,1)S(1)} %forward_1.1), channel_id=1, source_target_pairs={{0,2},{1,3},{2,0},{3,1},{4,5},{5,4},{6,7},{7,6},{8,10},{9,11},{10,... | collective-permute-start | bytes 688136 | tf_op jit(solution)/shard_map/ppermute | solution.py:94
  24.3 4.5 %collective-permute-start.8 = (bf16[80,512]{1,0:T(8,128)(2,1)S(1)}, bf16[80,512]{1,0:T(8,128)(2,1)S(1)}, u32[]{:S(2)}, u32[]{:S(2)}) collective-permute-start(bf16[80,512]{1,0:T(8,128)(2,1)S(1)} %forward_2.1), channel_id=1, source_target_pairs={{0,1},{1,0},{2,3},{3,2},{4,6},{5,7},{6,4},{7,5},{8,9},{9,8},{10,11... | collective-permute-start | bytes 245768 | tf_op jit(solution)/shard_map/ppermute | solution.py:94
  30.6 2.4 %collective-permute-start.9 = (bf16[768,512]{1,0:T(8,128)(2,1)S(1)}, bf16[768,512]{1,0:T(8,128)(2,1)S(1)}, u32[]{:S(2)}, u32[]{:S(2)}) collective-permute-start(bf16[768,512]{1,0:T(8,128)(2,1)S(1)} %far.3), channel_id=1, source_target_pairs={{0,4},{1,5},{2,6},{3,7},{4,0},{5,1},{6,2},{7,3},{8,12},{9,13},{10,... | collective-permute-start | bytes 2359304 | tf_op jit(solution)/shard_map/ppermute | solution.py:94

commit v10 on v7

--- a/solution.py
+++ b/solution.py
@@ -81,11 +81,11 @@
     return apply_inverse(gram, factor_inverse)
 
 
-def shift(value, steps_z, flip_cols, flip_core=0):
+def swap(value, flip_z, flip_cols, flip_core=0):
     slabs, owners = lax.axis_size("rows"), lax.axis_size("cols")
     pairs = []
     for r in range(slabs):
-        to_r = ((r // 2 + steps_z) % (slabs // 2)) * 2 + ((r % 2) ^ flip_core)
+        to_r = r ^ (2 * flip_z + flip_core)
         for c in range(owners):
             pairs.append((r * owners + c, to_r * owners + (c ^ flip_cols)))
     return lax.ppermute(value, ("rows", "cols"), pairs)
@@ -165,7 +165,7 @@
                 note = jnp.where(here, code, note)
         notes.append(note)
         for k in range(layers):
-            z = lax.rem(me_z + k, layers)
+            z = me_z ^ k
             for u in range(2):
                 core = me_core ^ u
                 for j in range(CAP):
@@ -299,25 +299,38 @@
     out_ref[...] = gram.astype(out_ref.dtype)
 
 
-def inverse_kernel(own_ref, other_ref, high_ref, low_ref, out_hbm, out_ref, sems):
-    f32, bf16 = jnp.float32, jnp.bfloat16
-    width = own_ref.shape[1]
+def times_inverse(gram, high, low):
+    f32, bf16 = jnp.float32, jnp.bfloat16
+    width = gram.shape[1]
+    first = gram.astype(bf16)
+    parts = []
+    for start, stop in ((0, width // 2), (width // 2, width)):
+        a, b = high[:stop, start:stop], low[:stop, start:stop]
+        total = jnp.dot(first[:, :stop], a, preferred_element_type=f32)
+        total += jnp.dot(first[:, :stop], b, preferred_element_type=f32)
+        if gram.dtype == f32:
+            second = (gram - first.astype(f32)).astype(bf16)
+            total += jnp.dot(second[:, :stop], a, preferred_element_type=f32)
+        parts.append(total)
+    return parts
+
+
+def own_inverse_kernel(gram_ref, high_ref, low_ref, out_ref):
+    half = out_ref.shape[1] // 2
+    left, right = times_inverse(gram_ref[...], high_ref[...], low_ref[...])
+    out_ref[:, :half] = left
+    out_ref[:, half:] = right
+
+
+def sum_kernel(own_ref, other_ref, high_ref, low_ref, out_hbm, out_ref, sems):
     strips = sems.shape[0]
-    height = own_ref.shape[0] // strips
+    height, half = own_ref.shape[0] // strips, own_ref.shape[1] // 2
     copies = []
-
-    def times(a, b):
-        return jnp.dot(a, b, preferred_element_type=f32)
-
     for i in range(strips):
         here = pl.ds(i * height, height)
-        gram = own_ref[here, :] + other_ref[here, :].astype(f32)
-        gram_high = gram.astype(bf16)
-        gram_low = (gram - gram_high.astype(f32)).astype(bf16)
-        for start, stop in ((0, width // 2), (width // 2, width)):
-            high, low = high_ref[:stop, start:stop], low_ref[:stop, start:stop]
-            a, b = gram_high[:, :stop], gram_low[:, :stop]
-            out_ref[here, start:stop] = times(a, high) + (times(a, low) + times(b, high))
+        left, right = times_inverse(other_ref[here, :], high_ref[...], low_ref[...])
+        out_ref[here, :half] = own_ref[here, :half] + left
+        out_ref[here, half:] = own_ref[here, half:] + right
         copies.append(pltpu.make_async_copy(out_ref.at[here, :], out_hbm.at[here, :], sems.at[i]))
         copies[-1].start()
     for copy in copies:
@@ -367,8 +380,8 @@
         compiler_params=params,
         name="pack",
     )(*map(in_hbm, (tile_lists, tile_masks, tile_order, weights.reshape(1, rows), panel_jac, jac)))
-    line = [shift(weighted, k, 0) for k in range(1, layers)]
-    from_x, from_y = shift(to_x, 0, 1), shift(to_y, 0, 2)
+    line = [swap(weighted, k, 0) for k in range(1, layers)]
+    from_x, from_y = swap(to_x, 0, 1), swap(to_y, 0, 2)
 
     sizes = (layers, panel_width, lane_group, wide)
     others, *posts = pl.pallas_call(
@@ -380,8 +393,8 @@
         compiler_params=params,
         name="sort",
     )(kept, from_x, from_y, *line)
-    posts = [posts[0]] + [shift(posts[k], k, 0) for k in range(1, layers)]
-    by_x, by_y = shift(others, 0, 1), shift(others, 0, 2)
+    posts = [posts[0]] + [swap(posts[k], k, 0) for k in range(1, layers)]
+    by_x, by_y = swap(others, 0, 1), swap(others, 0, 2)
 
     last = rows // 2
     rows_to_y = pl.pallas_call(
@@ -392,7 +405,7 @@
         compiler_params=params,
         name="rows_to_y",
     )(from_x, by_x, *posts[1:])
-    across_y = shift(rows_to_y, 0, 2)
+    across_y = swap(rows_to_y, 0, 2)
     rest_to_x = pl.pallas_call(
         functools.partial(rest_to_x_kernel, (layers, lane_group, wide)),
         out_shape=shaped((last + rows // 2 + 16, panel_width), bf16),
@@ -401,7 +414,7 @@
         compiler_params=params,
         name="rest_to_x",
     )(by_y, *posts)
-    across_x = shift(rest_to_x, 0, 1)
+    across_x = swap(rest_to_x, 0, 1)
 
     count = per_owner * slab_width
     depth = layers * rows
@@ -432,16 +445,24 @@
             name="far",
         )(near, across_y, across_x)
 
-    other = shift(far(1, other, bf16), 0, 0, 1)
+    other = swap(far(1, other, bf16), 0, 0, 1)
+    own = pl.pallas_call(
+        own_inverse_kernel,
+        out_shape=gram,
+        in_specs=[vmem] * 3,
+        out_specs=vmem,
+        compiler_params=params,
+        name="own_inverse",
+    )(far(0, own, f32), high, low)
     out = pl.pallas_call(
-        inverse_kernel,
-        out_shape=shaped((count, panel_width), f32),
+        sum_kernel,
+        out_shape=gram,
         in_specs=[vmem] * 4,
         out_specs=anywhere,
         scratch_shapes=[pltpu.VMEM((count, panel_width), f32), pltpu.SemaphoreType.DMA((3,))],
         compiler_params=params,
-        name="inverse",
-    )(far(0, own, f32), other, high, low)
+        name="sum",
+    )(own, other, high, low)
     return out.reshape(per_owner, slab_width, panel_width)
 
 

time: 34.8 us -> 36.2 us (1.040)
  waiting for transfers between devices: 10.2 us -> 11.3 us
  Pallas kernels: 6.3 us -> 7.1 us
  starting transfers between devices: 18.1 us -> 17.6 us
    ppermute x13, waiting for transfers between devices: 10.2 us -> 11.3 us  [swap(): return lax.ppermute(value, ('rows', 'cols'), pairs)]
    pallas_call x1 -> x2, Pallas kernels: 2.08 us -> 2.89 us  [the longest x1 1.8 us: local(): pl.pallas_call(sum_kernel, out_shape=gram, in_specs=[vmem] * 4, out_specs...]
    ppermute x13, starting transfers between devices: 18.1 us -> 17.6 us  [swap(): return lax.ppermute(value, ('rows', 'cols'), pairs)]
  transfers between devices with their start and end apart: 13 -> 13, of which waited for: 8 -> 7; matrix products, arithmetic and copies ran while one was open for 0% -> 0% of each run, Pallas kernels for 6% -> 9%
where the time goes in v10:
time: 36.2 us; the launch traced here: 36.1 us
  starting transfers between devices  17.6 us (49%)
  waiting for transfers between devices  11.3 us (31%)
  Pallas kernels  7.1 us (20%)
    ppermute x13, starting transfers between devices, swap(): return lax.ppermute(value, ('rows', 'cols'), pairs)  17.6 us
    ppermute x13, waiting for transfers between devices, swap(): return lax.ppermute(value, ('rows', 'cols'), pairs)  11.3 us
    pallas_call x1, Pallas kernels, local(): pl.pallas_call(sum_kernel, out_shape=gram, in_specs=[vmem] * 4, out_specs...  1.8 us
    pallas_call x1, Pallas kernels, local(): pl.pallas_call(functools.partial(pack_kernel, sizes), out_shape=[shaped((...  1.65 us
    pallas_call x1, Pallas kernels, local(): pl.pallas_call(functools.partial(near_kernel, sizes), out_shape=[gram] *...  1.46 us
    pallas_call x1, Pallas kernels, local(): pl.pallas_call(own_inverse_kernel, out_shape=gram, in_specs=[vmem] * 3, o...  1.09 us
    pallas_call x2, Pallas kernels, far(): pl.pallas_call(functools.partial(far_kernel, sizes, u), out_shape=shaped(...  0.88 us
  transfers between devices with their start and end apart: 13, of which 7 were waited for; matrix products, arithmetic and copies ran while one was open for 0% of the time, Pallas kernels for 9%

profile of v10, /device:TPU:0, one launch (start us, length us, event | category | flops | bytes accessed | tf_op | source)
XLA Modules:
  0.0 36.1 jit_solution(4592464869130545496)
XLA Ops:
  0.0 1.6 %pack.1 = (bf16[64,512]{1,0:T(8,128)(2,1)S(1)}, bf16[64,384]{1,0:T(8,128)(2,1)S(1)}, bf16[64,896]{1,0:T(8,128)(2,1)S(1)}, bf16[64,1152]{1,0:T(8,128)(2,1)S(1)}) custom-call(s32[2,4]{1,0:T(2,128)} %lists_hbm.1, s32[2,4]{1,0:T(2,128)} %masks_hbm.1, s32[96]{0:T(128)} %order_hbm.1, f32[1,64]{1,0:T(1,128)} %bitcast.2, bf16[64,512]{1,0:T(8,128)(2,1)} %panel_hbm.1, ...), custom_call_target="tpu_custom_call" | custom-call | tf_op jit(solution)/shard_map/pack/pallas_call | solution.py:361
  1.7 3.0 %collective-permute-start.1 = (bf16[64,1152]{1,0:T(8,128)(2,1)S(1)}, bf16[64,1152]{1,0:T(8,128)(2,1)S(1)}, u32[]{:S(2)}, u32[]{:S(2)}) collective-permute-start(bf16[64,1152]{1,0:T(8,128)(2,1)S(1)} %get-tuple-element.21), channel_id=1, source_target_pairs={{0,2},{1,3},{2,0},{3,1},{4,6},{5,7},{6,4},{7,5},{8,10},{9,11},{10,... | collective-permute-start | bytes 442376 | tf_op jit(solution)/shard_map/ppermute | solution.py:91
  4.7 1.5 %collective-permute-start = (bf16[64,896]{1,0:T(8,128)(2,1)S(1)}, bf16[64,896]{1,0:T(8,128)(2,1)S(1)}, u32[]{:S(2)}, u32[]{:S(2)}) collective-permute-start(bf16[64,896]{1,0:T(8,128)(2,1)S(1)} %get-tuple-element.20), channel_id=1, source_target_pairs={{0,1},{1,0},{2,3},{3,2},{4,5},{5,4},{6,7},{7,6},{8,9},{9,8},{10,11... | collective-permute-start | bytes 344072 | tf_op jit(solution)/shard_map/ppermute | solution.py:91
  6.2 1.6 %collective-permute-start.2 = (bf16[64,512]{1,0:T(8,128)(2,1)S(1)}, bf16[64,512]{1,0:T(8,128)(2,1)S(1)}, u32[]{:S(2)}, u32[]{:S(2)}) collective-permute-start(bf16[64,512]{1,0:T(8,128)(2,1)S(1)} %get-tuple-element.18.refs_0_), channel_id=1, source_target_pairs={{0,8},{1,9},{2,10},{3,11},{4,12},{5,13},{6,14},{7,15},{8,0},{9,1},... | collective-permute-start | bytes 196616 | tf_op jit(solution)/shard_map/ppermute | solution.py:91
  7.8 2.6 %collective-permute-start.3 = (bf16[64,512]{1,0:T(8,128)(2,1)S(1)}, bf16[64,512]{1,0:T(8,128)(2,1)S(1)}, u32[]{:S(2)}, u32[]{:S(2)}) collective-permute-start(bf16[64,512]{1,0:T(8,128)(2,1)S(1)} %get-tuple-element.18.refs_0_), channel_id=1, source_target_pairs={{0,16},{1,17},{2,18},{3,19},{4,20},{5,21},{6,22},{7,23},{8,24},{9,... | collective-permute-start | bytes 196616 | tf_op jit(solution)/shard_map/ppermute | solution.py:91
  10.3 0.2 collective-permute-start.4
  10.6 0.5 %collective-permute-done.2.refs_0_ = bf16[64,512]{1,0:T(8,128)(2,1)S(1)} collective-permute-done((bf16[64,512]{1,0:T(8,128)(2,1)S(1)}, bf16[64,512]{1,0:T(8,128)(2,1)S(1)}, u32[]{:S(2)}, u32[]{:S(2)}) %collective-permute-start.2) | collective-permute-done | bytes 65568 | tf_op jit(solution)/shard_map/ppermute | solution.py:91
  11.1 3.4 %collective-permute-done.3.refs_1_ = bf16[64,512]{1,0:T(8,128)(2,1)S(1)} collective-permute-done((bf16[64,512]{1,0:T(8,128)(2,1)S(1)}, bf16[64,512]{1,0:T(8,128)(2,1)S(1)}, u32[]{:S(2)}, u32[]{:S(2)}) %collective-permute-start.3) | collective-permute-done | bytes 65568 | tf_op jit(solution)/shard_map/ppermute | solution.py:91
  14.5 2.0 %collective-permute-done.4.refs_2_ = bf16[64,512]{1,0:T(8,128)(2,1)S(1)} collective-permute-done((bf16[64,512]{1,0:T(8,128)(2,1)S(1)}, bf16[64,512]{1,0:T(8,128)(2,1)S(1)}, u32[]{:S(2)}, u32[]{:S(2)}) %collective-permute-start.4) | collective-permute-done | bytes 65568 | tf_op jit(solution)/shard_map/ppermute | solution.py:91
  16.4 0.0 collective-permute-done.1.from_y_ref.refs_4_
  16.4 0.1 sort.1
  16.6 0.6 %collective-permute-start.5 = (bf16[192,512]{1,0:T(8,128)(2,1)S(1)}, bf16[192,512]{1,0:T(8,128)(2,1)S(1)}, u32[]{:S(2)}, u32[]{:S(2)}) collective-permute-start(bf16[192,512]{1,0:T(8,128)(2,1)S(1)} %get-tuple-element.22.refs_1_), channel_id=1, source_target_pairs={{0,1},{1,0},{2,3},{3,2},{4,5},{5,4},{6,7},{7,6},{8,9},{9,8},{10,11... | collective-permute-start | bytes 589832 | tf_op jit(solution)/shard_map/ppermute | solution.py:91
  17.2 0.5 %collective-permute-start.6 = (bf16[192,512]{1,0:T(8,128)(2,1)S(1)}, bf16[192,512]{1,0:T(8,128)(2,1)S(1)}, u32[]{:S(2)}, u32[]{:S(2)}) collective-permute-start(bf16[192,512]{1,0:T(8,128)(2,1)S(1)} %get-tuple-element.22.refs_1_), channel_id=1, source_target_pairs={{0,2},{1,3},{2,0},{3,1},{4,6},{5,7},{6,4},{7,5},{8,10},{9,11},{10,... | collective-permute-start | bytes 589832 | tf_op jit(solution)/shard_map/ppermute | solution.py:91
  17.7 0.0 collective-permute-start.7
  17.7 1.8 %collective-permute-start.8 = (bf16[80,256]{1,0:T(8,128)(2,1)S(1)}, bf16[80,256]{1,0:T(8,128)(2,1)S(1)}, u32[]{:S(2)}, u32[]{:S(2)}) collective-permute-start(bf16[80,256]{1,0:T(8,128)(2,1)S(1)} %get-tuple-element.25), channel_id=1, source_target_pairs={{0,16},{1,17},{2,18},{3,19},{4,20},{5,21},{6,22},{7,23},{8,24},{9,... | collective-permute-start | bytes 122888 | tf_op jit(solution)/shard_map/ppermute | solution.py:91
  19.5 2.6 %collective-permute-start.9 = (bf16[80,256]{1,0:T(8,128)(2,1)S(1)}, bf16[80,256]{1,0:T(8,128)(2,1)S(1)}, u32[]{:S(2)}, u32[]{:S(2)}) collective-permute-start(bf16[80,256]{1,0:T(8,128)(2,1)S(1)} %get-tuple-element.26), channel_id=1, source_target_pairs={{0,24},{1,25},{2,26},{3,27},{4,28},{5,29},{6,30},{7,31},{8,16},{9,... | collective-permute-start | bytes 122888 | tf_op jit(solution)/shard_map/ppermute | solution.py:91
  22.0 0.0 collective-permute-done.7.refs_7_.refs_0_.refs_1_
  22.1 0.5 %collective-permute-done.8.refs_8_.refs_1_.refs_2_ = bf16[80,256]{1,0:T(8,128)(2,1)S(1)} collective-permute-done((bf16[80,256]{1,0:T(8,128)(2,1)S(1)}, bf16[80,256]{1,0:T(8,128)(2,1)S(1)}, u32[]{:S(2)}, u32[]{:S(2)}) %collective-permute-start.8) | collective-permute-done | bytes 40992 | tf_op jit(solution)/shard_map/ppermute | solution.py:91
  22.6 2.7 %collective-permute-done.9.refs_9_.refs_2_.refs_3_ = bf16[80,256]{1,0:T(8,128)(2,1)S(1)} collective-permute-done((bf16[80,256]{1,0:T(8,128)(2,1)S(1)}, bf16[80,256]{1,0:T(8,128)(2,1)S(1)}, u32[]{:S(2)}, u32[]{:S(2)}) %collective-permute-start.9) | collective-permute-done | bytes 40992 | tf_op jit(solution)/shard_map/ppermute | solution.py:91
  25.3 0.0 collective-permute-done.5.refs_3_.by_x_ref
  25.3 1.6 %collective-permute-start.10 = (bf16[224,512]{1,0:T(8,128)(2,1)S(1)}, bf16[224,512]{1,0:T(8,128)(2,1)S(1)}, u32[]{:S(2)}, u32[]{:S(2)}) collective-permute-start(bf16[224,512]{1,0:T(8,128)(2,1)S(1)} %rows_to_y.1), channel_id=1, source_target_pairs={{0,2},{1,3},{2,0},{3,1},{4,6},{5,7},{6,4},{7,5},{8,10},{9,11},{10,... | collective-permute-start | bytes 688136 | tf_op jit(solution)/shard_map/ppermute | solution.py:91
  26.9 0.0 collective-permute-done.6.refs_5_.by_y_ref
  26.9 0.1 rest_to_x.1
  27.0 1.6 %collective-permute-start.11 = (bf16[80,512]{1,0:T(8,128)(2,1)S(1)}, bf16[80,512]{1,0:T(8,128)(2,1)S(1)}, u32[]{:S(2)}, u32[]{:S(2)}) collective-permute-start(bf16[80,512]{1,0:T(8,128)(2,1)S(1)} %rest_to_x.1), channel_id=1, source_target_pairs={{0,1},{1,0},{2,3},{3,2},{4,5},{5,4},{6,7},{7,6},{8,9},{9,8},{10,11... | collective-permute-start | bytes 245768 | tf_op jit(solution)/shard_map/ppermute | solution.py:91
  28.5 1.5 %near.1 = (f32[768,512]{1,0:T(8,128)S(1)}, f32[768,512]{1,0:T(8,128)S(1)}, bf16[512,512]{1,0:T(8,128)(2,1)S(1)}, bf16[512,512]{1,0:T(8,128)(2,1)S(1)}) custom-call(bf16[64,512]{1,0:T(8,128)(2,1)S(1)} %get-tuple-element.18.refs_0_, bf16[192,512]{1,0:T(8,128)(2,1)S(1)} %get-tuple-element.22.refs_1_, ...), custom_call_target="tpu_custom_call" | custom-call | tf_op jit(solution)/shard_map/near/pallas_call | solution.py:424
  30.0 1.5 %collective-permute-done.11.by_x_ref = bf16[80,512]{1,0:T(8,128)(2,1)S(1)} collective-permute-done((bf16[80,512]{1,0:T(8,128)(2,1)S(1)}, bf16[80,512]{1,0:T(8,128)(2,1)S(1)}, u32[]{:S(2)}, u32[]{:S(2)}) %collective-permute-start.11) | collective-permute-done | bytes 81952 | tf_op jit(solution)/shard_map/ppermute | solution.py:91
  31.5 0.4 %far.3 = bf16[768,512]{1,0:T(8,128)(2,1)S(1)} custom-call(f32[768,512]{1,0:T(8,128)S(1)} %get-tuple-element.30.near_ref, bf16[224,512]{1,0:T(8,128)(2,1)S(1)} %collective-permute-done.10.by_y_ref, bf16[80,512]{1,0:T(8,128)(2,1)S(1)} %collective-permute-done.11.by_x_ref), custom_call_target="tpu_custom_call" | custom-call | tf_op jit(solution)/shard_map/far/pallas_call | solution.py:438
  31.9 0.1 collective-permute-start.12
  32.0 0.4 %far.2.gram_ref = f32[768,512]{1,0:T(8,128)S(1)} custom-call(f32[768,512]{1,0:T(8,128)S(1)} %get-tuple-element.27.near_ref, bf16[224,512]{1,0:T(8,128)(2,1)S(1)} %collective-permute-done.10.by_y_ref, bf16[80,512]{1,0:T(8,128)(2,1)S(1)} %collective-permute-done.11.by_x_ref), custom_call_target="tpu_custom_call" | custom-call | tf_op jit(solution)/shard_map/far/pallas_call | solution.py:438
  32.4 1.1 %own_inverse.1.own_ref = f32[768,512]{1,0:T(8,128)S(1)} custom-call(f32[768,512]{1,0:T(8,128)S(1)} %far.2.gram_ref, bf16[512,512]{1,0:T(8,128)(2,1)S(1)} %get-tuple-element.28.high_ref, bf16[512,512]{1,0:T(8,128)(2,1)S(1)} %get-tuple-element.29.low_ref), custom_call_target="tpu_custom_call" | custom-call | tf_op jit(solution)/shard_map/own_inverse/pallas_call | solution.py:449
  33.5 0.7 %collective-permute-done.12.other_ref = bf16[768,512]{1,0:T(8,128)(2,1)S(1)} collective-permute-done((bf16[768,512]{1,0:T(8,128)(2,1)S(1)}, bf16[768,512]{1,0:T(8,128)(2,1)S(1)}, u32[]{:S(2)}, u32[]{:S(2)}) %collective-permute-start.12) | collective-permute-done | bytes 786464 | tf_op jit(solution)/shard_map/ppermute | solution.py:91
  34.3 1.8 %sum.1 = f32[768,512]{1,0:T(8,128)} custom-call(f32[768,512]{1,0:T(8,128)S(1)} %own_inverse.1.own_ref, bf16[768,512]{1,0:T(8,128)(2,1)S(1)} %collective-permute-done.12.other_ref, bf16[512,512]{1,0:T(8,128)(2,1)S(1)} %get-tuple-element.28.high_ref, bf16[512,512]{1,0:T(8,128)(2,1)S(1)} %get-tuple-element.29.low_ref), custom_call_target="tpu_custom_call" | custom-call | tf_op jit(solution)/shard_map/sum/pallas_call | solution.py:457
  (5 shorter events, 0.0 us)
Async XLA Ops:
  0.0 28.5 %copy-start = (f32[512,512]{1,0:T(8,128)S(1)}, f32[512,512]{1,0:T(8,128)}, u32[]{:S(2)}) copy-start(f32[512,512]{1,0:T(8,128)} %refs_10_.1) | copy-start | bytes 3145732
  1.7 14.8 %collective-permute-start.1 = (bf16[64,1152]{1,0:T(8,128)(2,1)S(1)}, bf16[64,1152]{1,0:T(8,128)(2,1)S(1)}, u32[]{:S(2)}, u32[]{:S(2)}) collective-permute-start(bf16[64,1152]{1,0:T(8,128)(2,1)S(1)} %get-tuple-element.21), channel_id=1, source_target_pairs={{0,2},{1,3},{2,0},{3,1},{4,6},{5,7},{6,4},{7,5},{8,10},{9,11},{10,... | collective-permute-start | bytes 442376 | tf_op jit(solution)/shard_map/ppermute | solution.py:91
  4.7 11.7 %collective-permute-start = (bf16[64,896]{1,0:T(8,128)(2,1)S(1)}, bf16[64,896]{1,0:T(8,128)(2,1)S(1)}, u32[]{:S(2)}, u32[]{:S(2)}) collective-permute-start(bf16[64,896]{1,0:T(8,128)(2,1)S(1)} %get-tuple-element.20), channel_id=1, source_target_pairs={{0,1},{1,0},{2,3},{3,2},{4,5},{5,4},{6,7},{7,6},{8,9},{9,8},{10,11... | collective-permute-start | bytes 344072 | tf_op jit(solution)/shard_map/ppermute | solution.py:91
  6.2 4.9 %collective-permute-start.2 = (bf16[64,512]{1,0:T(8,128)(2,1)S(1)}, bf16[64,512]{1,0:T(8,128)(2,1)S(1)}, u32[]{:S(2)}, u32[]{:S(2)}) collective-permute-start(bf16[64,512]{1,0:T(8,128)(2,1)S(1)} %get-tuple-element.18.refs_0_), channel_id=1, source_target_pairs={{0,8},{1,9},{2,10},{3,11},{4,12},{5,13},{6,14},{7,15},{8,0},{9,1},... | collective-permute-start | bytes 196616 | tf_op jit(solution)/shard_map/ppermute | solution.py:91
  7.8 6.7 %collective-permute-start.3 = (bf16[64,512]{1,0:T(8,128)(2,1)S(1)}, bf16[64,512]{1,0:T(8,128)(2,1)S(1)}, u32[]{:S(2)}, u32[]{:S(2)}) collective-permute-start(bf16[64,512]{1,0:T(8,128)(2,1)S(1)} %get-tuple-element.18.refs_0_), channel_id=1, source_target_pairs={{0,16},{1,17},{2,18},{3,19},{4,20},{5,21},{6,22},{7,23},{8,24},{9,... | collective-permute-start | bytes 196616 | tf_op jit(solution)/shard_map/ppermute | solution.py:91
  10.3 6.1 %collective-permute-start.4 = (bf16[64,512]{1,0:T(8,128)(2,1)S(1)}, bf16[64,512]{1,0:T(8,128)(2,1)S(1)}, u32[]{:S(2)}, u32[]{:S(2)}) collective-permute-start(bf16[64,512]{1,0:T(8,128)(2,1)S(1)} %get-tuple-element.18.refs_0_), channel_id=1, source_target_pairs={{0,24},{1,25},{2,26},{3,27},{4,28},{5,29},{6,30},{7,31},{8,16},{9,... | collective-permute-start | bytes 196616 | tf_op jit(solution)/shard_map/ppermute | solution.py:91
  16.6 8.7 %collective-permute-start.5 = (bf16[192,512]{1,0:T(8,128)(2,1)S(1)}, bf16[192,512]{1,0:T(8,128)(2,1)S(1)}, u32[]{:S(2)}, u32[]{:S(2)}) collective-permute-start(bf16[192,512]{1,0:T(8,128)(2,1)S(1)} %get-tuple-element.22.refs_1_), channel_id=1, source_target_pairs={{0,1},{1,0},{2,3},{3,2},{4,5},{5,4},{6,7},{7,6},{8,9},{9,8},{10,11... | collective-permute-start | bytes 589832 | tf_op jit(solution)/shard_map/ppermute | solution.py:91
  17.2 9.7 %collective-permute-start.6 = (bf16[192,512]{1,0:T(8,128)(2,1)S(1)}, bf16[192,512]{1,0:T(8,128)(2,1)S(1)}, u32[]{:S(2)}, u32[]{:S(2)}) collective-permute-start(bf16[192,512]{1,0:T(8,128)(2,1)S(1)} %get-tuple-element.22.refs_1_), channel_id=1, source_target_pairs={{0,2},{1,3},{2,0},{3,1},{4,6},{5,7},{6,4},{7,5},{8,10},{9,11},{10,... | collective-permute-start | bytes 589832 | tf_op jit(solution)/shard_map/ppermute | solution.py:91
  17.7 4.4 %collective-permute-start.7 = (bf16[80,256]{1,0:T(8,128)(2,1)S(1)}, bf16[80,256]{1,0:T(8,128)(2,1)S(1)}, u32[]{:S(2)}, u32[]{:S(2)}) collective-permute-start(bf16[80,256]{1,0:T(8,128)(2,1)S(1)} %get-tuple-element.24), channel_id=1, source_target_pairs={{0,8},{1,9},{2,10},{3,11},{4,12},{5,13},{6,14},{7,15},{8,0},{9,1},... | collective-permute-start | bytes 122888 | tf_op jit(solution)/shard_map/ppermute | solution.py:91
  17.7 4.9 %collective-permute-start.8 = (bf16[80,256]{1,0:T(8,128)(2,1)S(1)}, bf16[80,256]{1,0:T(8,128)(2,1)S(1)}, u32[]{:S(2)}, u32[]{:S(2)}) collective-permute-start(bf16[80,256]{1,0:T(8,128)(2,1)S(1)} %get-tuple-element.25), channel_id=1, source_target_pairs={{0,16},{1,17},{2,18},{3,19},{4,20},{5,21},{6,22},{7,23},{8,24},{9,... | collective-permute-start | bytes 122888 | tf_op jit(solution)/shard_map/ppermute | solution.py:91
  19.5 5.8 %collective-permute-start.9 = (bf16[80,256]{1,0:T(8,128)(2,1)S(1)}, bf16[80,256]{1,0:T(8,128)(2,1)S(1)}, u32[]{:S(2)}, u32[]{:S(2)}) collective-permute-start(bf16[80,256]{1,0:T(8,128)(2,1)S(1)} %get-tuple-element.26), channel_id=1, source_target_pairs={{0,24},{1,25},{2,26},{3,27},{4,28},{5,29},{6,30},{7,31},{8,16},{9,... | collective-permute-start | bytes 122888 | tf_op jit(solution)/shard_map/ppermute | solution.py:91
  25.3 6.2 %collective-permute-start.10 = (bf16[224,512]{1,0:T(8,128)(2,1)S(1)}, bf16[224,512]{1,0:T(8,128)(2,1)S(1)}, u32[]{:S(2)}, u32[]{:S(2)}) collective-permute-start(bf16[224,512]{1,0:T(8,128)(2,1)S(1)} %rows_to_y.1), channel_id=1, source_target_pairs={{0,2},{1,3},{2,0},{3,1},{4,6},{5,7},{6,4},{7,5},{8,10},{9,11},{10,... | collective-permute-start | bytes 688136 | tf_op jit(solution)/shard_map/ppermute | solution.py:91
  27.0 4.5 %collective-permute-start.11 = (bf16[80,512]{1,0:T(8,128)(2,1)S(1)}, bf16[80,512]{1,0:T(8,128)(2,1)S(1)}, u32[]{:S(2)}, u32[]{:S(2)}) collective-permute-start(bf16[80,512]{1,0:T(8,128)(2,1)S(1)} %rest_to_x.1), channel_id=1, source_target_pairs={{0,1},{1,0},{2,3},{3,2},{4,5},{5,4},{6,7},{7,6},{8,9},{9,8},{10,11... | collective-permute-start | bytes 245768 | tf_op jit(solution)/shard_map/ppermute | solution.py:91
  31.9 2.4 %collective-permute-start.12 = (bf16[768,512]{1,0:T(8,128)(2,1)S(1)}, bf16[768,512]{1,0:T(8,128)(2,1)S(1)}, u32[]{:S(2)}, u32[]{:S(2)}) collective-permute-start(bf16[768,512]{1,0:T(8,128)(2,1)S(1)} %far.3), channel_id=1, source_target_pairs={{0,4},{1,5},{2,6},{3,7},{4,0},{5,1},{6,2},{7,3},{8,12},{9,13},{10,... | collective-permute-start | bytes 2359304 | tf_op jit(solution)/shard_map/ppermute | solution.py:91

commit v11 on v10

--- a/solution.py
+++ b/solution.py
@@ -81,11 +81,11 @@
     return apply_inverse(gram, factor_inverse)
 
 
-def swap(value, flip_z, flip_cols, flip_core=0):
+def shift(value, steps_z, flip_cols, flip_core=0):
     slabs, owners = lax.axis_size("rows"), lax.axis_size("cols")
     pairs = []
     for r in range(slabs):
-        to_r = r ^ (2 * flip_z + flip_core)
+        to_r = ((r // 2 + steps_z) % (slabs // 2)) * 2 + ((r % 2) ^ flip_core)
         for c in range(owners):
             pairs.append((r * owners + c, to_r * owners + (c ^ flip_cols)))
     return lax.ppermute(value, ("rows", "cols"), pairs)
@@ -165,7 +165,7 @@
                 note = jnp.where(here, code, note)
         notes.append(note)
         for k in range(layers):
-            z = me_z ^ k
+            z = lax.rem(me_z + k, layers)
             for u in range(2):
                 core = me_core ^ u
                 for j in range(CAP):
@@ -277,7 +277,8 @@
         out_ref[...] = jnp.dot(placed_ref[...], rows_ref[...], preferred_element_type=f32)
 
 
-def far_kernel(sizes, u, near_ref, by_y_ref, by_x_ref, out_ref, placed_ref, rows_ref):
+def far_kernel(sizes, u, near_ref, by_y_ref, by_x_ref, *refs):
+    out_refs, (placed_ref, rows_ref) = refs[:-2], refs[-2:]
     layers, owners, per_owner, block_count, block_rows = sizes
     f32, bf16 = jnp.float32, jnp.bfloat16
     rows = block_count * block_rows
@@ -295,8 +296,10 @@
             notes.append(row_of(by_x_ref[last + part :, :wide], k))
         start = 2 * h * rows
         place(placed_ref, slice(start, start + 2 * rows), per_owner, pieces, notes, (block_count, block_rows))
-    gram = near_ref[...] + jnp.dot(placed_ref[...], rows_ref[...], preferred_element_type=f32)
-    out_ref[...] = gram.astype(out_ref.dtype)
+    for i, out_ref in enumerate(out_refs):
+        here = pl.ds(i * out_ref.shape[0], out_ref.shape[0])
+        gram = near_ref[here, :] + jnp.dot(placed_ref[here, :], rows_ref[...], preferred_element_type=f32)
+        out_ref[...] = gram.astype(out_ref.dtype)
 
 
 def times_inverse(gram, high, low):
@@ -322,16 +325,17 @@
     out_ref[:, half:] = right
 
 
-def sum_kernel(own_ref, other_ref, high_ref, low_ref, out_hbm, out_ref, sems):
+def sum_kernel(top, own_ref, other_ref, high_ref, low_ref, *refs):
+    out_hbm, out_ref, sems = refs[-3:]
     strips = sems.shape[0]
-    height, half = own_ref.shape[0] // strips, own_ref.shape[1] // 2
+    height, half = other_ref.shape[0] // strips, own_ref.shape[1] // 2
     copies = []
     for i in range(strips):
-        here = pl.ds(i * height, height)
+        here, there = pl.ds(i * height, height), pl.ds(top + i * height, height)
         left, right = times_inverse(other_ref[here, :], high_ref[...], low_ref[...])
-        out_ref[here, :half] = own_ref[here, :half] + left
-        out_ref[here, half:] = own_ref[here, half:] + right
-        copies.append(pltpu.make_async_copy(out_ref.at[here, :], out_hbm.at[here, :], sems.at[i]))
+        out_ref[here, :half] = own_ref[there, :half] + left
+        out_ref[here, half:] = own_ref[there, half:] + right
+        copies.append(pltpu.make_async_copy(out_ref.at[here, :], out_hbm.at[there, :], sems.at[i]))
         copies[-1].start()
     for copy in copies:
         copy.wait()
@@ -380,8 +384,8 @@
         compiler_params=params,
         name="pack",
     )(*map(in_hbm, (tile_lists, tile_masks, tile_order, weights.reshape(1, rows), panel_jac, jac)))
-    line = [swap(weighted, k, 0) for k in range(1, layers)]
-    from_x, from_y = swap(to_x, 0, 1), swap(to_y, 0, 2)
+    line = [shift(weighted, k, 0) for k in range(1, layers)]
+    from_x, from_y = shift(to_x, 0, 1), shift(to_y, 0, 2)
 
     sizes = (layers, panel_width, lane_group, wide)
     others, *posts = pl.pallas_call(
@@ -393,8 +397,8 @@
         compiler_params=params,
         name="sort",
     )(kept, from_x, from_y, *line)
-    posts = [posts[0]] + [swap(posts[k], k, 0) for k in range(1, layers)]
-    by_x, by_y = swap(others, 0, 1), swap(others, 0, 2)
+    posts = [posts[0]] + [shift(posts[k], k, 0) for k in range(1, layers)]
+    by_x, by_y = shift(others, 0, 1), shift(others, 0, 2)
 
     last = rows // 2
     rows_to_y = pl.pallas_call(
@@ -405,7 +409,7 @@
         compiler_params=params,
         name="rows_to_y",
     )(from_x, by_x, *posts[1:])
-    across_y = swap(rows_to_y, 0, 2)
+    across_y = shift(rows_to_y, 0, 2)
     rest_to_x = pl.pallas_call(
         functools.partial(rest_to_x_kernel, (layers, lane_group, wide)),
         out_shape=shaped((last + rows // 2 + 16, panel_width), bf16),
@@ -414,7 +418,7 @@
         compiler_params=params,
         name="rest_to_x",
     )(by_y, *posts)
-    across_x = swap(rest_to_x, 0, 1)
+    across_x = shift(rest_to_x, 0, 1)
 
     count = per_owner * slab_width
     depth = layers * rows
@@ -434,18 +438,18 @@
         name="near",
     )(*panels, *posts, factor_inverse)
 
-    def far(u, near, kind):
+    def far(u, near, kind, pieces):
         return pl.pallas_call(
             functools.partial(far_kernel, sizes, u),
-            out_shape=shaped((count, panel_width), kind),
+            out_shape=[shaped((count // pieces, panel_width), kind)] * pieces,
             in_specs=[vmem] * 3,
-            out_specs=vmem,
+            out_specs=[vmem] * pieces,
             scratch_shapes=[pltpu.VMEM((count, depth), bf16), pltpu.VMEM((depth, panel_width), bf16)],
             compiler_params=params,
             name="far",
         )(near, across_y, across_x)
 
-    other = swap(far(1, other, bf16), 0, 0, 1)
+    others = [shift(piece, 0, 0, 1) for piece in far(1, other, bf16, 2)]
     own = pl.pallas_call(
         own_inverse_kernel,
         out_shape=gram,
@@ -453,16 +457,23 @@
         out_specs=vmem,
         compiler_params=params,
         name="own_inverse",
-    )(far(0, own, f32), high, low)
-    out = pl.pallas_call(
-        sum_kernel,
-        out_shape=gram,
-        in_specs=[vmem] * 4,
-        out_specs=anywhere,
-        scratch_shapes=[pltpu.VMEM((count, panel_width), f32), pltpu.SemaphoreType.DMA((3,))],
-        compiler_params=params,
-        name="sum",
-    )(own, other, high, low)
+    )(*far(0, own, f32, 1), high, low)
+    out = []
+    for i, other in enumerate(others):
+        height = other.shape[0]
+        out = [
+            pl.pallas_call(
+                functools.partial(sum_kernel, i * height),
+                out_shape=gram,
+                in_specs=[vmem] * 4 + [anywhere] * len(out),
+                out_specs=anywhere,
+                input_output_aliases={4: 0} if out else {},
+                scratch_shapes=[pltpu.VMEM((height, panel_width), f32), pltpu.SemaphoreType.DMA((2,))],
+                compiler_params=params,
+                name="sum",
+            )(own, other, high, low, *out)
+        ]
+    (out,) = out
     return out.reshape(per_owner, slab_width, panel_width)
 
 

time: 36.2 us -> 35.2 us (0.972)
  waiting for transfers between devices: 11.3 us -> 8.38 us
  Pallas kernels: 7.1 us -> 8.1 us
  starting transfers between devices: 17.6 us -> 18.5 us
    ppermute x13 -> x14, waiting for transfers between devices: 11.3 us -> 8.38 us  [shift(): return lax.ppermute(value, ('rows', 'cols'), pairs)]
    pallas_call x3 -> x4, Pallas kernels: 2.68 us -> 3.68 us  [the longest x2 2.79 us: local(): pl.pallas_call(functools.partial(sum_kernel, i * height), out_shape=gram,...]
    ppermute x13 -> x14, starting transfers between devices: 17.6 us -> 18.5 us  [shift(): return lax.ppermute(value, ('rows', 'cols'), pairs)]
  transfers between devices with their start and end apart: 13 -> 14, of which waited for: 7 -> 6; matrix products, arithmetic and copies ran while one was open for 0% -> 0% of each run, Pallas kernels for 9% -> 13%
where the time goes in v11:
time: 35.2 us; the launch traced here: 35.1 us
  starting transfers between devices  18.5 us (53%)
  waiting for transfers between devices  8.38 us (24%)
  Pallas kernels  8.1 us (23%)
    ppermute x14, starting transfers between devices, shift(): return lax.ppermute(value, ('rows', 'cols'), pairs)  18.5 us
    ppermute x14, waiting for transfers between devices, shift(): return lax.ppermute(value, ('rows', 'cols'), pairs)  8.38 us
    pallas_call x2, Pallas kernels, local(): pl.pallas_call(functools.partial(sum_kernel, i * height), out_shape=gram,...  2.79 us
    pallas_call x1, Pallas kernels, local(): pl.pallas_call(functools.partial(pack_kernel, sizes), out_shape=[shaped((...  1.65 us
    pallas_call x1, Pallas kernels, local(): pl.pallas_call(functools.partial(near_kernel, sizes), out_shape=[gram] *...  1.46 us
    pallas_call x1, Pallas kernels, local(): pl.pallas_call(own_inverse_kernel, out_shape=gram, in_specs=[vmem] * 3, o...  1.08 us
    pallas_call x2, Pallas kernels, far(): pl.pallas_call(functools.partial(far_kernel, sizes, u), out_shape=[shaped...  0.89 us
  transfers between devices with their start and end apart: 14, of which 6 were waited for; matrix products, arithmetic and copies ran while one was open for 0% of the time, Pallas kernels for 13%

profile of v11, /device:TPU:0, one launch (start us, length us, event | category | flops | bytes accessed | tf_op | source)
XLA Modules:
  0.0 35.1 jit_solution(13524312810373943314)
XLA Ops:
  0.0 1.7 %pack.1 = (bf16[64,512]{1,0:T(8,128)(2,1)S(1)}, bf16[64,384]{1,0:T(8,128)(2,1)S(1)}, bf16[64,896]{1,0:T(8,128)(2,1)S(1)}, bf16[64,1152]{1,0:T(8,128)(2,1)S(1)}) custom-call(s32[2,4]{1,0:T(2,128)} %lists_hbm.1, s32[2,4]{1,0:T(2,128)} %masks_hbm.1, s32[96]{0:T(128)} %order_hbm.1, f32[1,64]{1,0:T(1,128)} %bitcast.2, bf16[64,512]{1,0:T(8,128)(2,1)} %panel_hbm.1, ...), custom_call_target="tpu_custom_call" | custom-call | tf_op jit(solution)/shard_map/pack/pallas_call | solution.py:365
  1.7 3.0 %collective-permute-start.1 = (bf16[64,1152]{1,0:T(8,128)(2,1)S(1)}, bf16[64,1152]{1,0:T(8,128)(2,1)S(1)}, u32[]{:S(2)}, u32[]{:S(2)}) collective-permute-start(bf16[64,1152]{1,0:T(8,128)(2,1)S(1)} %get-tuple-element.23), channel_id=1, source_target_pairs={{0,2},{1,3},{2,0},{3,1},{4,6},{5,7},{6,4},{7,5},{8,10},{9,11},{10,... | collective-permute-start | bytes 442376 | tf_op jit(solution)/shard_map/ppermute | solution.py:91
  4.7 1.5 %collective-permute-start = (bf16[64,896]{1,0:T(8,128)(2,1)S(1)}, bf16[64,896]{1,0:T(8,128)(2,1)S(1)}, u32[]{:S(2)}, u32[]{:S(2)}) collective-permute-start(bf16[64,896]{1,0:T(8,128)(2,1)S(1)} %get-tuple-element.22), channel_id=1, source_target_pairs={{0,1},{1,0},{2,3},{3,2},{4,5},{5,4},{6,7},{7,6},{8,9},{9,8},{10,11... | collective-permute-start | bytes 344072 | tf_op jit(solution)/shard_map/ppermute | solution.py:91
  6.2 3.6 %collective-permute-start.4 = (bf16[64,512]{1,0:T(8,128)(2,1)S(1)}, bf16[64,512]{1,0:T(8,128)(2,1)S(1)}, u32[]{:S(2)}, u32[]{:S(2)}) collective-permute-start(bf16[64,512]{1,0:T(8,128)(2,1)S(1)} %get-tuple-element.20.refs_0_), channel_id=1, source_target_pairs={{0,24},{1,25},{2,26},{3,27},{4,28},{5,29},{6,30},{7,31},{8,0},{9,1... | collective-permute-start | bytes 196616 | tf_op jit(solution)/shard_map/ppermute | solution.py:91
  9.8 0.0 collective-permute-start.3
  9.8 1.0 %collective-permute-start.2 = (bf16[64,512]{1,0:T(8,128)(2,1)S(1)}, bf16[64,512]{1,0:T(8,128)(2,1)S(1)}, u32[]{:S(2)}, u32[]{:S(2)}) collective-permute-start(bf16[64,512]{1,0:T(8,128)(2,1)S(1)} %get-tuple-element.20.refs_0_), channel_id=1, source_target_pairs={{0,8},{1,9},{2,10},{3,11},{4,12},{5,13},{6,14},{7,15},{8,16},{9,17... | collective-permute-start | bytes 196616 | tf_op jit(solution)/shard_map/ppermute | solution.py:91
  10.8 1.2 %collective-permute-done.4.refs_2_ = bf16[64,512]{1,0:T(8,128)(2,1)S(1)} collective-permute-done((bf16[64,512]{1,0:T(8,128)(2,1)S(1)}, bf16[64,512]{1,0:T(8,128)(2,1)S(1)}, u32[]{:S(2)}, u32[]{:S(2)}) %collective-permute-start.4) | collective-permute-done | bytes 65568 | tf_op jit(solution)/shard_map/ppermute | solution.py:91
  12.0 3.1 %collective-permute-done.3.refs_1_ = bf16[64,512]{1,0:T(8,128)(2,1)S(1)} collective-permute-done((bf16[64,512]{1,0:T(8,128)(2,1)S(1)}, bf16[64,512]{1,0:T(8,128)(2,1)S(1)}, u32[]{:S(2)}, u32[]{:S(2)}) %collective-permute-start.3) | collective-permute-done | bytes 65568 | tf_op jit(solution)/shard_map/ppermute | solution.py:91
  15.1 0.8 %collective-permute-done.2.refs_0_ = bf16[64,512]{1,0:T(8,128)(2,1)S(1)} collective-permute-done((bf16[64,512]{1,0:T(8,128)(2,1)S(1)}, bf16[64,512]{1,0:T(8,128)(2,1)S(1)}, u32[]{:S(2)}, u32[]{:S(2)}) %collective-permute-start.2) | collective-permute-done | bytes 65568 | tf_op jit(solution)/shard_map/ppermute | solution.py:91
  15.9 0.0 collective-permute-done.1.from_y_ref.refs_4_
  15.9 0.1 sort.1
  16.0 0.6 %collective-permute-start.5 = (bf16[192,512]{1,0:T(8,128)(2,1)S(1)}, bf16[192,512]{1,0:T(8,128)(2,1)S(1)}, u32[]{:S(2)}, u32[]{:S(2)}) collective-permute-start(bf16[192,512]{1,0:T(8,128)(2,1)S(1)} %get-tuple-element.24.refs_1_), channel_id=1, source_target_pairs={{0,1},{1,0},{2,3},{3,2},{4,5},{5,4},{6,7},{7,6},{8,9},{9,8},{10,11... | collective-permute-start | bytes 589832 | tf_op jit(solution)/shard_map/ppermute | solution.py:91
  16.6 0.5 %collective-permute-start.6 = (bf16[192,512]{1,0:T(8,128)(2,1)S(1)}, bf16[192,512]{1,0:T(8,128)(2,1)S(1)}, u32[]{:S(2)}, u32[]{:S(2)}) collective-permute-start(bf16[192,512]{1,0:T(8,128)(2,1)S(1)} %get-tuple-element.24.refs_1_), channel_id=1, source_target_pairs={{0,2},{1,3},{2,0},{3,1},{4,6},{5,7},{6,4},{7,5},{8,10},{9,11},{10,... | collective-permute-start | bytes 589832 | tf_op jit(solution)/shard_map/ppermute | solution.py:91
  17.1 0.0 collective-permute-start.7
  17.1 2.3 %collective-permute-start.8 = (bf16[80,256]{1,0:T(8,128)(2,1)S(1)}, bf16[80,256]{1,0:T(8,128)(2,1)S(1)}, u32[]{:S(2)}, u32[]{:S(2)}) collective-permute-start(bf16[80,256]{1,0:T(8,128)(2,1)S(1)} %get-tuple-element.27), channel_id=1, source_target_pairs={{0,16},{1,17},{2,18},{3,19},{4,20},{5,21},{6,22},{7,23},{8,24},{9,... | collective-permute-start | bytes 122888 | tf_op jit(solution)/shard_map/ppermute | solution.py:91
  19.4 2.2 %collective-permute-start.9 = (bf16[80,256]{1,0:T(8,128)(2,1)S(1)}, bf16[80,256]{1,0:T(8,128)(2,1)S(1)}, u32[]{:S(2)}, u32[]{:S(2)}) collective-permute-start(bf16[80,256]{1,0:T(8,128)(2,1)S(1)} %get-tuple-element.28), channel_id=1, source_target_pairs={{0,24},{1,25},{2,26},{3,27},{4,28},{5,29},{6,30},{7,31},{8,0},{9,1... | collective-permute-start | bytes 122888 | tf_op jit(solution)/shard_map/ppermute | solution.py:91
  21.6 1.3 %collective-permute-done.7.refs_7_.refs_0_.refs_1_ = bf16[80,256]{1,0:T(8,128)(2,1)S(1)} collective-permute-done((bf16[80,256]{1,0:T(8,128)(2,1)S(1)}, bf16[80,256]{1,0:T(8,128)(2,1)S(1)}, u32[]{:S(2)}, u32[]{:S(2)}) %collective-permute-start.7) | collective-permute-done | bytes 40992 | tf_op jit(solution)/shard_map/ppermute | solution.py:91
  22.9 0.6 %collective-permute-done.9.refs_9_.refs_2_.refs_3_ = bf16[80,256]{1,0:T(8,128)(2,1)S(1)} collective-permute-done((bf16[80,256]{1,0:T(8,128)(2,1)S(1)}, bf16[80,256]{1,0:T(8,128)(2,1)S(1)}, u32[]{:S(2)}, u32[]{:S(2)}) %collective-permute-start.9) | collective-permute-done | bytes 40992 | tf_op jit(solution)/shard_map/ppermute | solution.py:91
  23.5 0.0 collective-permute-done.5.refs_3_.by_x_ref
  23.5 1.6 %collective-permute-start.10 = (bf16[224,512]{1,0:T(8,128)(2,1)S(1)}, bf16[224,512]{1,0:T(8,128)(2,1)S(1)}, u32[]{:S(2)}, u32[]{:S(2)}) collective-permute-start(bf16[224,512]{1,0:T(8,128)(2,1)S(1)} %rows_to_y.1), channel_id=1, source_target_pairs={{0,2},{1,3},{2,0},{3,1},{4,6},{5,7},{6,4},{7,5},{8,10},{9,11},{10,... | collective-permute-start | bytes 688136 | tf_op jit(solution)/shard_map/ppermute | solution.py:91
  25.1 0.1 rest_to_x.1
  25.2 1.6 %collective-permute-start.11 = (bf16[80,512]{1,0:T(8,128)(2,1)S(1)}, bf16[80,512]{1,0:T(8,128)(2,1)S(1)}, u32[]{:S(2)}, u32[]{:S(2)}) collective-permute-start(bf16[80,512]{1,0:T(8,128)(2,1)S(1)} %rest_to_x.1), channel_id=1, source_target_pairs={{0,1},{1,0},{2,3},{3,2},{4,5},{5,4},{6,7},{7,6},{8,9},{9,8},{10,11... | collective-permute-start | bytes 245768 | tf_op jit(solution)/shard_map/ppermute | solution.py:91
  26.7 1.5 %near.1 = (f32[768,512]{1,0:T(8,128)S(1)}, f32[768,512]{1,0:T(8,128)S(1)}, bf16[512,512]{1,0:T(8,128)(2,1)S(1)}, bf16[512,512]{1,0:T(8,128)(2,1)S(1)}) custom-call(bf16[64,512]{1,0:T(8,128)(2,1)S(1)} %get-tuple-element.20.refs_0_, bf16[192,512]{1,0:T(8,128)(2,1)S(1)} %get-tuple-element.24.refs_1_, ...), custom_call_target="tpu_custom_call" | custom-call | tf_op jit(solution)/shard_map/near/pallas_call | solution.py:428
  28.2 1.5 %collective-permute-done.11.by_x_ref = bf16[80,512]{1,0:T(8,128)(2,1)S(1)} collective-permute-done((bf16[80,512]{1,0:T(8,128)(2,1)S(1)}, bf16[80,512]{1,0:T(8,128)(2,1)S(1)}, u32[]{:S(2)}, u32[]{:S(2)}) %collective-permute-start.11) | collective-permute-done | bytes 81952 | tf_op jit(solution)/shard_map/ppermute | solution.py:91
  29.7 0.0 collective-permute-done.10.by_y_ref
  29.7 0.4 %far.3 = (bf16[384,512]{1,0:T(8,128)(2,1)S(1)}, bf16[384,512]{1,0:T(8,128)(2,1)S(1)}) custom-call(f32[768,512]{1,0:T(8,128)S(1)} %get-tuple-element.32.near_ref, bf16[224,512]{1,0:T(8,128)(2,1)S(1)} %collective-permute-done.10.by_y_ref, bf16[80,512]{1,0:T(8,128)(2,1)S(1)} %collective-permute-done.11.by_x_ref), custom_call_target="tpu_custom_call" | custom-call | tf_op jit(solution)/shard_map/far/pallas_call | solution.py:442
  30.1 0.1 collective-permute-start.13
  30.2 0.5 %collective-permute-start.12 = (bf16[384,512]{1,0:T(8,128)(2,1)S(1)}, bf16[384,512]{1,0:T(8,128)(2,1)S(1)}, u32[]{:S(2)}, u32[]{:S(2)}) collective-permute-start(bf16[384,512]{1,0:T(8,128)(2,1)S(1)} %get-tuple-element.33), channel_id=1, source_target_pairs={{0,4},{1,5},{2,6},{3,7},{4,0},{5,1},{6,2},{7,3},{8,12},{9,13},{10,... | collective-permute-start | bytes 1179656 | tf_op jit(solution)/shard_map/ppermute | solution.py:91
  30.7 0.4 %far.2.gram_ref = f32[768,512]{1,0:T(8,128)S(1)} custom-call(f32[768,512]{1,0:T(8,128)S(1)} %get-tuple-element.29.near_ref, bf16[224,512]{1,0:T(8,128)(2,1)S(1)} %collective-permute-done.10.by_y_ref, bf16[80,512]{1,0:T(8,128)(2,1)S(1)} %collective-permute-done.11.by_x_ref), custom_call_target="tpu_custom_call" | custom-call | tf_op jit(solution)/shard_map/far/pallas_call | solution.py:442
  31.2 1.1 %own_inverse.1.own_ref = f32[768,512]{1,0:T(8,128)S(1)} custom-call(f32[768,512]{1,0:T(8,128)S(1)} %far.2.gram_ref, bf16[512,512]{1,0:T(8,128)(2,1)S(1)} %get-tuple-element.30.high_ref, bf16[512,512]{1,0:T(8,128)(2,1)S(1)} %get-tuple-element.31.low_ref), custom_call_target="tpu_custom_call" | custom-call | tf_op jit(solution)/shard_map/own_inverse/pallas_call | solution.py:453
  32.3 1.4 %sum.2.refs_0_ = f32[768,512]{1,0:T(8,128)} custom-call(f32[768,512]{1,0:T(8,128)S(1)} %own_inverse.1.own_ref, bf16[384,512]{1,0:T(8,128)(2,1)S(1)} %collective-permute-done.13.other_ref, bf16[512,512]{1,0:T(8,128)(2,1)S(1)} %get-tuple-element.30.high_ref, bf16[512,512]{1,0:T(8,128)(2,1)S(1)} %get-tuple-element.31.low_ref), custom_call_target="tpu_custom_call" | custom-call | tf_op jit(solution)/shard_map/sum/pallas_call | solution.py:465
  33.7 1.4 %sum.3 = f32[768,512]{1,0:T(8,128)} custom-call(f32[768,512]{1,0:T(8,128)S(1)} %own_inverse.1.own_ref, bf16[384,512]{1,0:T(8,128)(2,1)S(1)} %collective-permute-done.12.other_ref, bf16[512,512]{1,0:T(8,128)(2,1)S(1)} %get-tuple-element.30.high_ref, bf16[512,512]{1,0:T(8,128)(2,1)S(1)} %get-tuple-element.31.low_ref, ...), custom_call_target="tpu_custom_call", output_to_operand_aliasing={{}: (4, {})} | custom-call | tf_op jit(solution)/shard_map/sum/pallas_call | solution.py:465
  (8 shorter events, 0.0 us)
Async XLA Ops:
  0.0 26.7 %copy-start = (f32[512,512]{1,0:T(8,128)S(1)}, f32[512,512]{1,0:T(8,128)}, u32[]{:S(2)}) copy-start(f32[512,512]{1,0:T(8,128)} %refs_10_.1) | copy-start | bytes 3145732
  1.7 14.2 %collective-permute-start.1 = (bf16[64,1152]{1,0:T(8,128)(2,1)S(1)}, bf16[64,1152]{1,0:T(8,128)(2,1)S(1)}, u32[]{:S(2)}, u32[]{:S(2)}) collective-permute-start(bf16[64,1152]{1,0:T(8,128)(2,1)S(1)} %get-tuple-element.23), channel_id=1, source_target_pairs={{0,2},{1,3},{2,0},{3,1},{4,6},{5,7},{6,4},{7,5},{8,10},{9,11},{10,... | collective-permute-start | bytes 442376 | tf_op jit(solution)/shard_map/ppermute | solution.py:91
  4.7 11.2 %collective-permute-start = (bf16[64,896]{1,0:T(8,128)(2,1)S(1)}, bf16[64,896]{1,0:T(8,128)(2,1)S(1)}, u32[]{:S(2)}, u32[]{:S(2)}) collective-permute-start(bf16[64,896]{1,0:T(8,128)(2,1)S(1)} %get-tuple-element.22), channel_id=1, source_target_pairs={{0,1},{1,0},{2,3},{3,2},{4,5},{5,4},{6,7},{7,6},{8,9},{9,8},{10,11... | collective-permute-start | bytes 344072 | tf_op jit(solution)/shard_map/ppermute | solution.py:91
  6.2 5.8 %collective-permute-start.4 = (bf16[64,512]{1,0:T(8,128)(2,1)S(1)}, bf16[64,512]{1,0:T(8,128)(2,1)S(1)}, u32[]{:S(2)}, u32[]{:S(2)}) collective-permute-start(bf16[64,512]{1,0:T(8,128)(2,1)S(1)} %get-tuple-element.20.refs_0_), channel_id=1, source_target_pairs={{0,24},{1,25},{2,26},{3,27},{4,28},{5,29},{6,30},{7,31},{8,0},{9,1... | collective-permute-start | bytes 196616 | tf_op jit(solution)/shard_map/ppermute | solution.py:91
  9.8 5.3 %collective-permute-start.3 = (bf16[64,512]{1,0:T(8,128)(2,1)S(1)}, bf16[64,512]{1,0:T(8,128)(2,1)S(1)}, u32[]{:S(2)}, u32[]{:S(2)}) collective-permute-start(bf16[64,512]{1,0:T(8,128)(2,1)S(1)} %get-tuple-element.20.refs_0_), channel_id=1, source_target_pairs={{0,16},{1,17},{2,18},{3,19},{4,20},{5,21},{6,22},{7,23},{8,24},{9,... | collective-permute-start | bytes 196616 | tf_op jit(solution)/shard_map/ppermute | solution.py:91
  9.8 6.1 %collective-permute-start.2 = (bf16[64,512]{1,0:T(8,128)(2,1)S(1)}, bf16[64,512]{1,0:T(8,128)(2,1)S(1)}, u32[]{:S(2)}, u32[]{:S(2)}) collective-permute-start(bf16[64,512]{1,0:T(8,128)(2,1)S(1)} %get-tuple-element.20.refs_0_), channel_id=1, source_target_pairs={{0,8},{1,9},{2,10},{3,11},{4,12},{5,13},{6,14},{7,15},{8,16},{9,17... | collective-permute-start | bytes 196616 | tf_op jit(solution)/shard_map/ppermute | solution.py:91
  16.0 7.5 %collective-permute-start.5 = (bf16[192,512]{1,0:T(8,128)(2,1)S(1)}, bf16[192,512]{1,0:T(8,128)(2,1)S(1)}, u32[]{:S(2)}, u32[]{:S(2)}) collective-permute-start(bf16[192,512]{1,0:T(8,128)(2,1)S(1)} %get-tuple-element.24.refs_1_), channel_id=1, source_target_pairs={{0,1},{1,0},{2,3},{3,2},{4,5},{5,4},{6,7},{7,6},{8,9},{9,8},{10,11... | collective-permute-start | bytes 589832 | tf_op jit(solution)/shard_map/ppermute | solution.py:91
  16.6 8.5 %collective-permute-start.6 = (bf16[192,512]{1,0:T(8,128)(2,1)S(1)}, bf16[192,512]{1,0:T(8,128)(2,1)S(1)}, u32[]{:S(2)}, u32[]{:S(2)}) collective-permute-start(bf16[192,512]{1,0:T(8,128)(2,1)S(1)} %get-tuple-element.24.refs_1_), channel_id=1, source_target_pairs={{0,2},{1,3},{2,0},{3,1},{4,6},{5,7},{6,4},{7,5},{8,10},{9,11},{10,... | collective-permute-start | bytes 589832 | tf_op jit(solution)/shard_map/ppermute | solution.py:91
  17.1 5.8 %collective-permute-start.7 = (bf16[80,256]{1,0:T(8,128)(2,1)S(1)}, bf16[80,256]{1,0:T(8,128)(2,1)S(1)}, u32[]{:S(2)}, u32[]{:S(2)}) collective-permute-start(bf16[80,256]{1,0:T(8,128)(2,1)S(1)} %get-tuple-element.26), channel_id=1, source_target_pairs={{0,8},{1,9},{2,10},{3,11},{4,12},{5,13},{6,14},{7,15},{8,16},{9,17... | collective-permute-start | bytes 122888 | tf_op jit(solution)/shard_map/ppermute | solution.py:91
  17.1 5.8 %collective-permute-start.8 = (bf16[80,256]{1,0:T(8,128)(2,1)S(1)}, bf16[80,256]{1,0:T(8,128)(2,1)S(1)}, u32[]{:S(2)}, u32[]{:S(2)}) collective-permute-start(bf16[80,256]{1,0:T(8,128)(2,1)S(1)} %get-tuple-element.27), channel_id=1, source_target_pairs={{0,16},{1,17},{2,18},{3,19},{4,20},{5,21},{6,22},{7,23},{8,24},{9,... | collective-permute-start | bytes 122888 | tf_op jit(solution)/shard_map/ppermute | solution.py:91
  19.4 4.0 %collective-permute-start.9 = (bf16[80,256]{1,0:T(8,128)(2,1)S(1)}, bf16[80,256]{1,0:T(8,128)(2,1)S(1)}, u32[]{:S(2)}, u32[]{:S(2)}) collective-permute-start(bf16[80,256]{1,0:T(8,128)(2,1)S(1)} %get-tuple-element.28), channel_id=1, source_target_pairs={{0,24},{1,25},{2,26},{3,27},{4,28},{5,29},{6,30},{7,31},{8,0},{9,1... | collective-permute-start | bytes 122888 | tf_op jit(solution)/shard_map/ppermute | solution.py:91
  23.5 6.2 %collective-permute-start.10 = (bf16[224,512]{1,0:T(8,128)(2,1)S(1)}, bf16[224,512]{1,0:T(8,128)(2,1)S(1)}, u32[]{:S(2)}, u32[]{:S(2)}) collective-permute-start(bf16[224,512]{1,0:T(8,128)(2,1)S(1)} %rows_to_y.1), channel_id=1, source_target_pairs={{0,2},{1,3},{2,0},{3,1},{4,6},{5,7},{6,4},{7,5},{8,10},{9,11},{10,... | collective-permute-start | bytes 688136 | tf_op jit(solution)/shard_map/ppermute | solution.py:91
  25.2 4.5 %collective-permute-start.11 = (bf16[80,512]{1,0:T(8,128)(2,1)S(1)}, bf16[80,512]{1,0:T(8,128)(2,1)S(1)}, u32[]{:S(2)}, u32[]{:S(2)}) collective-permute-start(bf16[80,512]{1,0:T(8,128)(2,1)S(1)} %rest_to_x.1), channel_id=1, source_target_pairs={{0,1},{1,0},{2,3},{3,2},{4,5},{5,4},{6,7},{7,6},{8,9},{9,8},{10,11... | collective-permute-start | bytes 245768 | tf_op jit(solution)/shard_map/ppermute | solution.py:91
  30.1 2.1 %collective-permute-start.13 = (bf16[384,512]{1,0:T(8,128)(2,1)S(1)}, bf16[384,512]{1,0:T(8,128)(2,1)S(1)}, u32[]{:S(2)}, u32[]{:S(2)}) collective-permute-start(bf16[384,512]{1,0:T(8,128)(2,1)S(1)} %get-tuple-element.34), channel_id=1, source_target_pairs={{0,4},{1,5},{2,6},{3,7},{4,0},{5,1},{6,2},{7,3},{8,12},{9,13},{10,... | collective-permute-start | bytes 1179656 | tf_op jit(solution)/shard_map/ppermute | solution.py:91
  30.2 3.4 %collective-permute-start.12 = (bf16[384,512]{1,0:T(8,128)(2,1)S(1)}, bf16[384,512]{1,0:T(8,128)(2,1)S(1)}, u32[]{:S(2)}, u32[]{:S(2)}) collective-permute-start(bf16[384,512]{1,0:T(8,128)(2,1)S(1)} %get-tuple-element.33), channel_id=1, source_target_pairs={{0,4},{1,5},{2,6},{3,7},{4,0},{5,1},{6,2},{7,3},{8,12},{9,13},{10,... | collective-permute-start | bytes 1179656 | tf_op jit(solution)/shard_map/ppermute | solution.py:91

commit v12 on v7

--- a/solution.py
+++ b/solution.py
@@ -249,15 +249,27 @@
         out_ref[n * part : (n + 1) * part, lanes] = placed
 
 
+def inverse_rows(rows_ref, factor_ref, high_ref, low_ref):
+    f32, bf16 = jnp.float32, jnp.bfloat16
+    width = rows_ref.shape[1]
+    for start, stop in ((0, width // 2), (width // 2, width)):
+        rows = rows_ref[:, :stop]
+        total = jnp.dot(rows, factor_ref[0, :stop, start:stop], preferred_element_type=f32)
+        total += jnp.dot(rows, factor_ref[1, :stop, start:stop], preferred_element_type=f32)
+        high = total.astype(bf16)
+        high_ref[:, start:stop] = high
+        low_ref[:, start:stop] = (total - high.astype(f32)).astype(bf16)
+
+
 def near_kernel(sizes, *refs):
     layers, owners, per_owner, block_count, block_rows = sizes
     panels, posts, factor_ref = refs[: 2 * (owners - 1)], refs[2 * (owners - 1) :][:layers], refs[2 * owners - 2 + layers]
-    own_ref, other_ref, high_ref, low_ref, placed_ref, rows_ref = refs[2 * owners - 1 + layers :]
+    own_ref, other_ref, turned_ref, placed_ref, rows_ref, high_ref, low_ref = refs[2 * owners - 1 + layers :]
     f32, bf16 = jnp.float32, jnp.bfloat16
     turned = factor_ref[...].T
     high = turned.astype(bf16)
-    high_ref[...] = high
-    low_ref[...] = (turned - high.astype(f32)).astype(bf16)
+    turned_ref[0, :, :] = high
+    turned_ref[1, :, :] = (turned - high.astype(f32)).astype(bf16)
     rows = block_count * block_rows
     group, wide = CAP * block_rows, CAP * rows
     part = rows // 2
@@ -266,6 +278,7 @@
     for panel in panels:
         rows_ref[at : at + panel.shape[0], :] = panel[:, :width]
         at += panel.shape[0]
+    inverse_rows(rows_ref, turned_ref, high_ref, low_ref)
     for u, out_ref in ((1, other_ref), (0, own_ref)):
         for e in range(owners - 1):
             for h in range(layers // 2):
@@ -274,12 +287,14 @@
                 notes = [row_of(post[rows:, :wide], e) for post in pair]
                 start = (e * layers + 2 * h) * rows
                 place(placed_ref, slice(start, start + 2 * rows), per_owner, pieces, notes, (block_count, block_rows))
-        out_ref[...] = jnp.dot(placed_ref[...], rows_ref[...], preferred_element_type=f32)
-
-
-def far_kernel(sizes, u, near_ref, by_y_ref, by_x_ref, out_ref, placed_ref, rows_ref):
+        placed = placed_ref[...]
+        total = jnp.dot(placed, high_ref[...], preferred_element_type=f32)
+        out_ref[...] = total + jnp.dot(placed, low_ref[...], preferred_element_type=f32)
+
+
+def far_kernel(sizes, u, near_ref, by_y_ref, by_x_ref, turned_ref, out_ref, placed_ref, rows_ref, high_ref, low_ref):
     layers, owners, per_owner, block_count, block_rows = sizes
-    f32, bf16 = jnp.float32, jnp.bfloat16
+    f32 = jnp.float32
     rows = block_count * block_rows
     group, wide = CAP * block_rows, CAP * rows
     part = rows // 2
@@ -287,6 +302,7 @@
     last = rows_ref.shape[0] - first
     rows_ref[:first, :] = by_y_ref[...]
     rows_ref[first:, :] = by_x_ref[:last, :]
+    inverse_rows(rows_ref, turned_ref, high_ref, low_ref)
     for h in range(layers // 2):
         pieces, notes = [], []
         for k in (2 * h, 2 * h + 1):
@@ -295,30 +311,20 @@
             notes.append(row_of(by_x_ref[last + part :, :wide], k))
         start = 2 * h * rows
         place(placed_ref, slice(start, start + 2 * rows), per_owner, pieces, notes, (block_count, block_rows))
-    gram = near_ref[...] + jnp.dot(placed_ref[...], rows_ref[...], preferred_element_type=f32)
-    out_ref[...] = gram.astype(out_ref.dtype)
-
-
-def inverse_kernel(own_ref, other_ref, high_ref, low_ref, out_hbm, out_ref, sems):
-    f32, bf16 = jnp.float32, jnp.bfloat16
-    width = own_ref.shape[1]
+    placed = placed_ref[...]
+    total = near_ref[...] + jnp.dot(placed, high_ref[...], preferred_element_type=f32)
+    total += jnp.dot(placed, low_ref[...], preferred_element_type=f32)
+    out_ref[...] = total.astype(out_ref.dtype)
+
+
+def add_kernel(own_ref, other_ref, out_hbm, sum_ref, sems):
     strips = sems.shape[0]
-    height = own_ref.shape[0] // strips
+    height = sum_ref.shape[0] // strips
     copies = []
-
-    def times(a, b):
-        return jnp.dot(a, b, preferred_element_type=f32)
-
     for i in range(strips):
         here = pl.ds(i * height, height)
-        gram = own_ref[here, :] + other_ref[here, :].astype(f32)
-        gram_high = gram.astype(bf16)
-        gram_low = (gram - gram_high.astype(f32)).astype(bf16)
-        for start, stop in ((0, width // 2), (width // 2, width)):
-            high, low = high_ref[:stop, start:stop], low_ref[:stop, start:stop]
-            a, b = gram_high[:, :stop], gram_low[:, :stop]
-            out_ref[here, start:stop] = times(a, high) + (times(a, low) + times(b, high))
-        copies.append(pltpu.make_async_copy(out_ref.at[here, :], out_hbm.at[here, :], sems.at[i]))
+        sum_ref[here, :] = own_ref[here, :] + other_ref[here, :].astype(jnp.float32)
+        copies.append(pltpu.make_async_copy(sum_ref.at[here, :], out_hbm.at[here, :], sems.at[i]))
         copies[-1].start()
     for copy in copies:
         copy.wait()
@@ -406,17 +412,15 @@
     count = per_owner * slab_width
     depth = layers * rows
     sizes = (layers, owners, per_owner, block_count, block_rows)
-    gram = shaped((count, panel_width), f32)
+    result = shaped((count, panel_width), f32)
     panels = [weighted, others, from_x, by_x, from_y, by_y]
-    own, other, high, low = pl.pallas_call(
+    own, other, turned = pl.pallas_call(
         functools.partial(near_kernel, sizes),
-        out_shape=[gram] * 2 + [shaped(factor_inverse.shape, bf16)] * 2,
+        out_shape=[result] * 2 + [shaped((2, *factor_inverse.shape), bf16)],
         in_specs=[vmem] * (len(panels) + layers + 1),
-        out_specs=[vmem] * 4,
-        scratch_shapes=[
-            pltpu.VMEM((count, (owners - 1) * depth), bf16),
-            pltpu.VMEM(((owners - 1) * depth, panel_width), bf16),
-        ],
+        out_specs=[vmem] * 3,
+        scratch_shapes=[pltpu.VMEM((count, (owners - 1) * depth), bf16)]
+        + [pltpu.VMEM(((owners - 1) * depth, panel_width), bf16)] * 3,
         compiler_params=params,
         name="near",
     )(*panels, *posts, factor_inverse)
@@ -425,23 +429,23 @@
         return pl.pallas_call(
             functools.partial(far_kernel, sizes, u),
             out_shape=shaped((count, panel_width), kind),
-            in_specs=[vmem] * 3,
+            in_specs=[vmem] * 4,
             out_specs=vmem,
-            scratch_shapes=[pltpu.VMEM((count, depth), bf16), pltpu.VMEM((depth, panel_width), bf16)],
+            scratch_shapes=[pltpu.VMEM((count, depth), bf16)] + [pltpu.VMEM((depth, panel_width), bf16)] * 3,
             compiler_params=params,
             name="far",
-        )(near, across_y, across_x)
+        )(near, across_y, across_x, turned)
 
     other = shift(far(1, other, bf16), 0, 0, 1)
     out = pl.pallas_call(
-        inverse_kernel,
-        out_shape=shaped((count, panel_width), f32),
-        in_specs=[vmem] * 4,
+        add_kernel,
+        out_shape=result,
+        in_specs=[vmem] * 2,
         out_specs=anywhere,
-        scratch_shapes=[pltpu.VMEM((count, panel_width), f32), pltpu.SemaphoreType.DMA((3,))],
-        compiler_params=params,
-        name="inverse",
-    )(far(0, own, f32), other, high, low)
+        scratch_shapes=[pltpu.VMEM((count, panel_width), f32), pltpu.SemaphoreType.DMA((6,))],
+        compiler_params=params,
+        name="add",
+    )(far(0, own, f32), other)
     return out.reshape(per_owner, slab_width, panel_width)
 
 

time: 34.8 us -> 34.9 us (level)
  Pallas kernels: 6.3 us -> 8.3 us
  waiting for transfers between devices: 10.2 us -> 8.24 us
    ppermute x13, waiting for transfers between devices: 10.2 us -> 8.24 us  [shift(): return lax.ppermute(value, ('rows', 'cols'), pairs)]
    pallas_call x2, Pallas kernels: 3.53 us -> 4.61 us  [the longest x1 3.4 us: local(): pl.pallas_call(functools.partial(near_kernel, sizes), out_shape=[result]...]
    pallas_call x2, Pallas kernels: 0.88 us -> 1.8 us  [far(): pl.pallas_call(functools.partial(far_kernel, sizes, u), out_shape=shaped(...]
  transfers between devices with their start and end apart: 13 -> 13, of which waited for: 8 -> 7; matrix products, arithmetic and copies ran while one was open for 0% -> 0% of each run, Pallas kernels for 6% -> 13%
where the time goes in v12:
time: 34.9 us; the launch traced here: 34.7 us
  starting transfers between devices  18.1 us (52%)
  Pallas kernels  8.3 us (24%)
  waiting for transfers between devices  8.24 us (24%)
    ppermute x13, starting transfers between devices, shift(): return lax.ppermute(value, ('rows', 'cols'), pairs)  18.1 us
    ppermute x13, waiting for transfers between devices, shift(): return lax.ppermute(value, ('rows', 'cols'), pairs)  8.24 us
    pallas_call x1, Pallas kernels, local(): pl.pallas_call(functools.partial(near_kernel, sizes), out_shape=[result]...  3.4 us
    pallas_call x2, Pallas kernels, far(): pl.pallas_call(functools.partial(far_kernel, sizes, u), out_shape=shaped(...  1.8 us
    pallas_call x1, Pallas kernels, local(): pl.pallas_call(functools.partial(pack_kernel, sizes), out_shape=[shaped((...  1.65 us
    pallas_call x1, Pallas kernels, local(): pl.pallas_call(add_kernel, out_shape=result, in_specs=[vmem] * 2, out_spe...  1.21 us
  transfers between devices with their start and end apart: 13, of which 7 were waited for; matrix products, arithmetic and copies ran while one was open for 0% of the time, Pallas kernels for 13%

profile of v12, /device:TPU:0, one launch (start us, length us, event | category | flops | bytes accessed | tf_op | source)
XLA Modules:
  0.0 34.7 jit_solution(14876788659668462827)
XLA Ops:
  0.0 1.7 %pack.1 = (bf16[64,512]{1,0:T(8,128)(2,1)S(1)}, bf16[64,384]{1,0:T(8,128)(2,1)S(1)}, bf16[64,896]{1,0:T(8,128)(2,1)S(1)}, bf16[64,1152]{1,0:T(8,128)(2,1)S(1)}) custom-call(s32[2,4]{1,0:T(2,128)} %lists_hbm.1, s32[2,4]{1,0:T(2,128)} %masks_hbm.1, s32[96]{0:T(128)} %order_hbm.1, f32[1,64]{1,0:T(1,128)} %bitcast.2, bf16[64,512]{1,0:T(8,128)(2,1)} %panel_hbm.1, ...), custom_call_target="tpu_custom_call" | custom-call | tf_op jit(solution)/shard_map/pack/pallas_call | solution.py:354
  1.7 3.0 %collective-permute-start.1 = (bf16[64,1152]{1,0:T(8,128)(2,1)S(1)}, bf16[64,1152]{1,0:T(8,128)(2,1)S(1)}, u32[]{:S(2)}, u32[]{:S(2)}) collective-permute-start(bf16[64,1152]{1,0:T(8,128)(2,1)S(1)} %get-tuple-element.20), channel_id=1, source_target_pairs={{0,2},{1,3},{2,0},{3,1},{4,6},{5,7},{6,4},{7,5},{8,10},{9,11},{10,... | collective-permute-start | bytes 442376 | tf_op jit(solution)/shard_map/ppermute | solution.py:91
  4.7 1.5 %collective-permute-start = (bf16[64,896]{1,0:T(8,128)(2,1)S(1)}, bf16[64,896]{1,0:T(8,128)(2,1)S(1)}, u32[]{:S(2)}, u32[]{:S(2)}) collective-permute-start(bf16[64,896]{1,0:T(8,128)(2,1)S(1)} %get-tuple-element.19), channel_id=1, source_target_pairs={{0,1},{1,0},{2,3},{3,2},{4,5},{5,4},{6,7},{7,6},{8,9},{9,8},{10,11... | collective-permute-start | bytes 344072 | tf_op jit(solution)/shard_map/ppermute | solution.py:91
  6.2 1.6 %collective-permute-start.2 = (bf16[64,512]{1,0:T(8,128)(2,1)S(1)}, bf16[64,512]{1,0:T(8,128)(2,1)S(1)}, u32[]{:S(2)}, u32[]{:S(2)}) collective-permute-start(bf16[64,512]{1,0:T(8,128)(2,1)S(1)} %get-tuple-element.17.refs_0_), channel_id=1, source_target_pairs={{0,8},{1,9},{2,10},{3,11},{4,12},{5,13},{6,14},{7,15},{8,16},{9,17... | collective-permute-start | bytes 196616 | tf_op jit(solution)/shard_map/ppermute | solution.py:91
  7.8 2.6 %collective-permute-start.3 = (bf16[64,512]{1,0:T(8,128)(2,1)S(1)}, bf16[64,512]{1,0:T(8,128)(2,1)S(1)}, u32[]{:S(2)}, u32[]{:S(2)}) collective-permute-start(bf16[64,512]{1,0:T(8,128)(2,1)S(1)} %get-tuple-element.17.refs_0_), channel_id=1, source_target_pairs={{0,16},{1,17},{2,18},{3,19},{4,20},{5,21},{6,22},{7,23},{8,24},{9,... | collective-permute-start | bytes 196616 | tf_op jit(solution)/shard_map/ppermute | solution.py:91
  10.4 1.3 %collective-permute-start.4 = (bf16[64,512]{1,0:T(8,128)(2,1)S(1)}, bf16[64,512]{1,0:T(8,128)(2,1)S(1)}, u32[]{:S(2)}, u32[]{:S(2)}) collective-permute-start(bf16[64,512]{1,0:T(8,128)(2,1)S(1)} %get-tuple-element.17.refs_0_), channel_id=1, source_target_pairs={{0,24},{1,25},{2,26},{3,27},{4,28},{5,29},{6,30},{7,31},{8,0},{9,1... | collective-permute-start | bytes 196616 | tf_op jit(solution)/shard_map/ppermute | solution.py:91
  11.7 1.3 %collective-permute-done.2.refs_0_ = bf16[64,512]{1,0:T(8,128)(2,1)S(1)} collective-permute-done((bf16[64,512]{1,0:T(8,128)(2,1)S(1)}, bf16[64,512]{1,0:T(8,128)(2,1)S(1)}, u32[]{:S(2)}, u32[]{:S(2)}) %collective-permute-start.2) | collective-permute-done | bytes 65568 | tf_op jit(solution)/shard_map/ppermute | solution.py:91
  13.0 1.9 %collective-permute-done.3.refs_1_ = bf16[64,512]{1,0:T(8,128)(2,1)S(1)} collective-permute-done((bf16[64,512]{1,0:T(8,128)(2,1)S(1)}, bf16[64,512]{1,0:T(8,128)(2,1)S(1)}, u32[]{:S(2)}, u32[]{:S(2)}) %collective-permute-start.3) | collective-permute-done | bytes 65568 | tf_op jit(solution)/shard_map/ppermute | solution.py:91
  14.9 0.1 collective-permute-done.4.refs_2_
  15.0 0.0 collective-permute-done.from_x_ref.refs_2_
  15.0 0.0 collective-permute-done.1.from_y_ref.refs_4_
  15.0 0.1 sort.1
  15.2 0.6 %collective-permute-start.5 = (bf16[192,512]{1,0:T(8,128)(2,1)S(1)}, bf16[192,512]{1,0:T(8,128)(2,1)S(1)}, u32[]{:S(2)}, u32[]{:S(2)}) collective-permute-start(bf16[192,512]{1,0:T(8,128)(2,1)S(1)} %get-tuple-element.21.refs_1_), channel_id=1, source_target_pairs={{0,1},{1,0},{2,3},{3,2},{4,5},{5,4},{6,7},{7,6},{8,9},{9,8},{10,11... | collective-permute-start | bytes 589832 | tf_op jit(solution)/shard_map/ppermute | solution.py:91
  15.8 0.4 %collective-permute-start.6 = (bf16[192,512]{1,0:T(8,128)(2,1)S(1)}, bf16[192,512]{1,0:T(8,128)(2,1)S(1)}, u32[]{:S(2)}, u32[]{:S(2)}) collective-permute-start(bf16[192,512]{1,0:T(8,128)(2,1)S(1)} %get-tuple-element.21.refs_1_), channel_id=1, source_target_pairs={{0,2},{1,3},{2,0},{3,1},{4,6},{5,7},{6,4},{7,5},{8,10},{9,11},{10,... | collective-permute-start | bytes 589832 | tf_op jit(solution)/shard_map/ppermute | solution.py:91
  16.2 1.1 %collective-permute-start.7 = (bf16[80,256]{1,0:T(8,128)(2,1)S(1)}, bf16[80,256]{1,0:T(8,128)(2,1)S(1)}, u32[]{:S(2)}, u32[]{:S(2)}) collective-permute-start(bf16[80,256]{1,0:T(8,128)(2,1)S(1)} %get-tuple-element.23), channel_id=1, source_target_pairs={{0,8},{1,9},{2,10},{3,11},{4,12},{5,13},{6,14},{7,15},{8,16},{9,17... | collective-permute-start | bytes 122888 | tf_op jit(solution)/shard_map/ppermute | solution.py:91
  17.3 2.2 %collective-permute-start.8 = (bf16[80,256]{1,0:T(8,128)(2,1)S(1)}, bf16[80,256]{1,0:T(8,128)(2,1)S(1)}, u32[]{:S(2)}, u32[]{:S(2)}) collective-permute-start(bf16[80,256]{1,0:T(8,128)(2,1)S(1)} %get-tuple-element.24), channel_id=1, source_target_pairs={{0,16},{1,17},{2,18},{3,19},{4,20},{5,21},{6,22},{7,23},{8,24},{9,... | collective-permute-start | bytes 122888 | tf_op jit(solution)/shard_map/ppermute | solution.py:91
  19.6 0.5 %collective-permute-start.9 = (bf16[80,256]{1,0:T(8,128)(2,1)S(1)}, bf16[80,256]{1,0:T(8,128)(2,1)S(1)}, u32[]{:S(2)}, u32[]{:S(2)}) collective-permute-start(bf16[80,256]{1,0:T(8,128)(2,1)S(1)} %get-tuple-element.25), channel_id=1, source_target_pairs={{0,24},{1,25},{2,26},{3,27},{4,28},{5,29},{6,30},{7,31},{8,0},{9,1... | collective-permute-start | bytes 122888 | tf_op jit(solution)/shard_map/ppermute | solution.py:91
  20.0 2.0 %collective-permute-done.7.refs_7_.refs_0_.refs_1_ = bf16[80,256]{1,0:T(8,128)(2,1)S(1)} collective-permute-done((bf16[80,256]{1,0:T(8,128)(2,1)S(1)}, bf16[80,256]{1,0:T(8,128)(2,1)S(1)}, u32[]{:S(2)}, u32[]{:S(2)}) %collective-permute-start.7) | collective-permute-done | bytes 40992 | tf_op jit(solution)/shard_map/ppermute | solution.py:91
  22.0 0.9 %collective-permute-done.8.refs_8_.refs_1_.refs_2_ = bf16[80,256]{1,0:T(8,128)(2,1)S(1)} collective-permute-done((bf16[80,256]{1,0:T(8,128)(2,1)S(1)}, bf16[80,256]{1,0:T(8,128)(2,1)S(1)}, u32[]{:S(2)}, u32[]{:S(2)}) %collective-permute-start.8) | collective-permute-done | bytes 40992 | tf_op jit(solution)/shard_map/ppermute | solution.py:91
  22.9 0.7 %collective-permute-done.9.refs_9_.refs_2_.refs_3_ = bf16[80,256]{1,0:T(8,128)(2,1)S(1)} collective-permute-done((bf16[80,256]{1,0:T(8,128)(2,1)S(1)}, bf16[80,256]{1,0:T(8,128)(2,1)S(1)}, u32[]{:S(2)}, u32[]{:S(2)}) %collective-permute-start.9) | collective-permute-done | bytes 40992 | tf_op jit(solution)/shard_map/ppermute | solution.py:91
  23.6 0.0 collective-permute-done.5.refs_3_.by_x_ref
  23.6 1.6 %collective-permute-start.10 = (bf16[224,512]{1,0:T(8,128)(2,1)S(1)}, bf16[224,512]{1,0:T(8,128)(2,1)S(1)}, u32[]{:S(2)}, u32[]{:S(2)}) collective-permute-start(bf16[224,512]{1,0:T(8,128)(2,1)S(1)} %rows_to_y.1), channel_id=1, source_target_pairs={{0,2},{1,3},{2,0},{3,1},{4,6},{5,7},{6,4},{7,5},{8,10},{9,11},{10,... | collective-permute-start | bytes 688136 | tf_op jit(solution)/shard_map/ppermute | solution.py:91
  25.2 0.0 collective-permute-done.6.refs_5_.by_y_ref
  25.2 0.1 rest_to_x.1
  25.3 1.6 %collective-permute-start.11 = (bf16[80,512]{1,0:T(8,128)(2,1)S(1)}, bf16[80,512]{1,0:T(8,128)(2,1)S(1)}, u32[]{:S(2)}, u32[]{:S(2)}) collective-permute-start(bf16[80,512]{1,0:T(8,128)(2,1)S(1)} %rest_to_x.1), channel_id=1, source_target_pairs={{0,1},{1,0},{2,3},{3,2},{4,5},{5,4},{6,7},{7,6},{8,9},{9,8},{10,11... | collective-permute-start | bytes 245768 | tf_op jit(solution)/shard_map/ppermute | solution.py:91
  26.8 3.4 %near.1 = (f32[768,512]{1,0:T(8,128)S(1)}, f32[768,512]{1,0:T(8,128)S(1)}, bf16[2,512,512]{2,1,0:T(8,128)(2,1)S(1)}) custom-call(bf16[64,512]{1,0:T(8,128)(2,1)S(1)} %get-tuple-element.17.refs_0_, bf16[192,512]{1,0:T(8,128)(2,1)S(1)} %get-tuple-element.21.refs_1_, bf16[64,896]{1,0:T(8,128)(2,1)S(1)} %collective-permute-done.from_x_ref.refs_2_, ...), custom_call_target="tpu_custom_call" | custom-call | tf_op jit(solution)/shard_map/near/pallas_call | solution.py:417
  30.3 0.0 collective-permute-done.10.by_y_ref
  30.3 0.9 %far.3 = bf16[768,512]{1,0:T(8,128)(2,1)S(1)} custom-call(f32[768,512]{1,0:T(8,128)S(1)} %get-tuple-element.28.near_ref, bf16[224,512]{1,0:T(8,128)(2,1)S(1)} %collective-permute-done.10.by_y_ref, bf16[80,512]{1,0:T(8,128)(2,1)S(1)} %collective-permute-done.11.by_x_ref, bf16[2,512,512]{2,1,0:T(8,128)(2,1)S(1)} %get-tuple-element.27.turned_ref), custom_call_target="tpu_custom_call" | custom-call | tf_op jit(solution)/shard_map/far/pallas_call | solution.py:429
  31.2 0.1 collective-permute-start.12
  31.2 0.9 %far.2.own_ref = f32[768,512]{1,0:T(8,128)S(1)} custom-call(f32[768,512]{1,0:T(8,128)S(1)} %get-tuple-element.26.near_ref, bf16[224,512]{1,0:T(8,128)(2,1)S(1)} %collective-permute-done.10.by_y_ref, bf16[80,512]{1,0:T(8,128)(2,1)S(1)} %collective-permute-done.11.by_x_ref, bf16[2,512,512]{2,1,0:T(8,128)(2,1)S(1)} %get-tuple-element.27.turned_ref), custom_call_target="tpu_custom_call" | custom-call | tf_op jit(solution)/shard_map/far/pallas_call | solution.py:429
  32.2 1.4 %collective-permute-done.12.other_ref = bf16[768,512]{1,0:T(8,128)(2,1)S(1)} collective-permute-done((bf16[768,512]{1,0:T(8,128)(2,1)S(1)}, bf16[768,512]{1,0:T(8,128)(2,1)S(1)}, u32[]{:S(2)}, u32[]{:S(2)}) %collective-permute-start.12) | collective-permute-done | bytes 786464 | tf_op jit(solution)/shard_map/ppermute | solution.py:91
  33.5 1.2 %add.1 = f32[768,512]{1,0:T(8,128)} custom-call(f32[768,512]{1,0:T(8,128)S(1)} %far.2.own_ref, bf16[768,512]{1,0:T(8,128)(2,1)S(1)} %collective-permute-done.12.other_ref), custom_call_target="tpu_custom_call" | custom-call | tf_op jit(solution)/shard_map/add/pallas_call | solution.py:440
  (4 shorter events, 0.0 us)
Async XLA Ops:
  0.0 26.8 %copy-start = (f32[512,512]{1,0:T(8,128)S(1)}, f32[512,512]{1,0:T(8,128)}, u32[]{:S(2)}) copy-start(f32[512,512]{1,0:T(8,128)} %refs_10_.1) | copy-start | bytes 3145732
  1.7 13.4 %collective-permute-start.1 = (bf16[64,1152]{1,0:T(8,128)(2,1)S(1)}, bf16[64,1152]{1,0:T(8,128)(2,1)S(1)}, u32[]{:S(2)}, u32[]{:S(2)}) collective-permute-start(bf16[64,1152]{1,0:T(8,128)(2,1)S(1)} %get-tuple-element.20), channel_id=1, source_target_pairs={{0,2},{1,3},{2,0},{3,1},{4,6},{5,7},{6,4},{7,5},{8,10},{9,11},{10,... | collective-permute-start | bytes 442376 | tf_op jit(solution)/shard_map/ppermute | solution.py:91
  4.7 10.3 %collective-permute-start = (bf16[64,896]{1,0:T(8,128)(2,1)S(1)}, bf16[64,896]{1,0:T(8,128)(2,1)S(1)}, u32[]{:S(2)}, u32[]{:S(2)}) collective-permute-start(bf16[64,896]{1,0:T(8,128)(2,1)S(1)} %get-tuple-element.19), channel_id=1, source_target_pairs={{0,1},{1,0},{2,3},{3,2},{4,5},{5,4},{6,7},{7,6},{8,9},{9,8},{10,11... | collective-permute-start | bytes 344072 | tf_op jit(solution)/shard_map/ppermute | solution.py:91
  6.2 6.8 %collective-permute-start.2 = (bf16[64,512]{1,0:T(8,128)(2,1)S(1)}, bf16[64,512]{1,0:T(8,128)(2,1)S(1)}, u32[]{:S(2)}, u32[]{:S(2)}) collective-permute-start(bf16[64,512]{1,0:T(8,128)(2,1)S(1)} %get-tuple-element.17.refs_0_), channel_id=1, source_target_pairs={{0,8},{1,9},{2,10},{3,11},{4,12},{5,13},{6,14},{7,15},{8,16},{9,17... | collective-permute-start | bytes 196616 | tf_op jit(solution)/shard_map/ppermute | solution.py:91
  7.8 7.2 %collective-permute-start.3 = (bf16[64,512]{1,0:T(8,128)(2,1)S(1)}, bf16[64,512]{1,0:T(8,128)(2,1)S(1)}, u32[]{:S(2)}, u32[]{:S(2)}) collective-permute-start(bf16[64,512]{1,0:T(8,128)(2,1)S(1)} %get-tuple-element.17.refs_0_), channel_id=1, source_target_pairs={{0,16},{1,17},{2,18},{3,19},{4,20},{5,21},{6,22},{7,23},{8,24},{9,... | collective-permute-start | bytes 196616 | tf_op jit(solution)/shard_map/ppermute | solution.py:91
  10.4 4.7 %collective-permute-start.4 = (bf16[64,512]{1,0:T(8,128)(2,1)S(1)}, bf16[64,512]{1,0:T(8,128)(2,1)S(1)}, u32[]{:S(2)}, u32[]{:S(2)}) collective-permute-start(bf16[64,512]{1,0:T(8,128)(2,1)S(1)} %get-tuple-element.17.refs_0_), channel_id=1, source_target_pairs={{0,24},{1,25},{2,26},{3,27},{4,28},{5,29},{6,30},{7,31},{8,0},{9,1... | collective-permute-start | bytes 196616 | tf_op jit(solution)/shard_map/ppermute | solution.py:91
  15.2 8.4 %collective-permute-start.5 = (bf16[192,512]{1,0:T(8,128)(2,1)S(1)}, bf16[192,512]{1,0:T(8,128)(2,1)S(1)}, u32[]{:S(2)}, u32[]{:S(2)}) collective-permute-start(bf16[192,512]{1,0:T(8,128)(2,1)S(1)} %get-tuple-element.21.refs_1_), channel_id=1, source_target_pairs={{0,1},{1,0},{2,3},{3,2},{4,5},{5,4},{6,7},{7,6},{8,9},{9,8},{10,11... | collective-permute-start | bytes 589832 | tf_op jit(solution)/shard_map/ppermute | solution.py:91
  15.8 9.4 %collective-permute-start.6 = (bf16[192,512]{1,0:T(8,128)(2,1)S(1)}, bf16[192,512]{1,0:T(8,128)(2,1)S(1)}, u32[]{:S(2)}, u32[]{:S(2)}) collective-permute-start(bf16[192,512]{1,0:T(8,128)(2,1)S(1)} %get-tuple-element.21.refs_1_), channel_id=1, source_target_pairs={{0,2},{1,3},{2,0},{3,1},{4,6},{5,7},{6,4},{7,5},{8,10},{9,11},{10,... | collective-permute-start | bytes 589832 | tf_op jit(solution)/shard_map/ppermute | solution.py:91
  16.2 5.8 %collective-permute-start.7 = (bf16[80,256]{1,0:T(8,128)(2,1)S(1)}, bf16[80,256]{1,0:T(8,128)(2,1)S(1)}, u32[]{:S(2)}, u32[]{:S(2)}) collective-permute-start(bf16[80,256]{1,0:T(8,128)(2,1)S(1)} %get-tuple-element.23), channel_id=1, source_target_pairs={{0,8},{1,9},{2,10},{3,11},{4,12},{5,13},{6,14},{7,15},{8,16},{9,17... | collective-permute-start | bytes 122888 | tf_op jit(solution)/shard_map/ppermute | solution.py:91
  17.3 5.5 %collective-permute-start.8 = (bf16[80,256]{1,0:T(8,128)(2,1)S(1)}, bf16[80,256]{1,0:T(8,128)(2,1)S(1)}, u32[]{:S(2)}, u32[]{:S(2)}) collective-permute-start(bf16[80,256]{1,0:T(8,128)(2,1)S(1)} %get-tuple-element.24), channel_id=1, source_target_pairs={{0,16},{1,17},{2,18},{3,19},{4,20},{5,21},{6,22},{7,23},{8,24},{9,... | collective-permute-start | bytes 122888 | tf_op jit(solution)/shard_map/ppermute | solution.py:91
  19.6 4.0 %collective-permute-start.9 = (bf16[80,256]{1,0:T(8,128)(2,1)S(1)}, bf16[80,256]{1,0:T(8,128)(2,1)S(1)}, u32[]{:S(2)}, u32[]{:S(2)}) collective-permute-start(bf16[80,256]{1,0:T(8,128)(2,1)S(1)} %get-tuple-element.25), channel_id=1, source_target_pairs={{0,24},{1,25},{2,26},{3,27},{4,28},{5,29},{6,30},{7,31},{8,0},{9,1... | collective-permute-start | bytes 122888 | tf_op jit(solution)/shard_map/ppermute | solution.py:91
  23.6 6.7 %collective-permute-start.10 = (bf16[224,512]{1,0:T(8,128)(2,1)S(1)}, bf16[224,512]{1,0:T(8,128)(2,1)S(1)}, u32[]{:S(2)}, u32[]{:S(2)}) collective-permute-start(bf16[224,512]{1,0:T(8,128)(2,1)S(1)} %rows_to_y.1), channel_id=1, source_target_pairs={{0,2},{1,3},{2,0},{3,1},{4,6},{5,7},{6,4},{7,5},{8,10},{9,11},{10,... | collective-permute-start | bytes 688136 | tf_op jit(solution)/shard_map/ppermute | solution.py:91
  25.3 5.0 %collective-permute-start.11 = (bf16[80,512]{1,0:T(8,128)(2,1)S(1)}, bf16[80,512]{1,0:T(8,128)(2,1)S(1)}, u32[]{:S(2)}, u32[]{:S(2)}) collective-permute-start(bf16[80,512]{1,0:T(8,128)(2,1)S(1)} %rest_to_x.1), channel_id=1, source_target_pairs={{0,1},{1,0},{2,3},{3,2},{4,5},{5,4},{6,7},{7,6},{8,9},{9,8},{10,11... | collective-permute-start | bytes 245768 | tf_op jit(solution)/shard_map/ppermute | solution.py:91
  31.2 2.4 %collective-permute-start.12 = (bf16[768,512]{1,0:T(8,128)(2,1)S(1)}, bf16[768,512]{1,0:T(8,128)(2,1)S(1)}, u32[]{:S(2)}, u32[]{:S(2)}) collective-permute-start(bf16[768,512]{1,0:T(8,128)(2,1)S(1)} %far.3), channel_id=1, source_target_pairs={{0,4},{1,5},{2,6},{3,7},{4,0},{5,1},{6,2},{7,3},{8,12},{9,13},{10,... | collective-permute-start | bytes 2359304 | tf_op jit(solution)/shard_map/ppermute | solution.py:91

commit v13 on v12

--- a/solution.py
+++ b/solution.py
@@ -261,15 +261,21 @@
         low_ref[:, start:stop] = (total - high.astype(f32)).astype(bf16)
 
 
-def near_kernel(sizes, *refs):
+def near_kernel(sizes, u, earlier, *refs):
     layers, owners, per_owner, block_count, block_rows = sizes
-    panels, posts, factor_ref = refs[: 2 * (owners - 1)], refs[2 * (owners - 1) :][:layers], refs[2 * owners - 2 + layers]
-    own_ref, other_ref, turned_ref, placed_ref, rows_ref, high_ref, low_ref = refs[2 * owners - 1 + layers :]
-    f32, bf16 = jnp.float32, jnp.bfloat16
-    turned = factor_ref[...].T
-    high = turned.astype(bf16)
-    turned_ref[0, :, :] = high
-    turned_ref[1, :, :] = (turned - high.astype(f32)).astype(bf16)
+    refs = refs[earlier:]
+    inputs = 2 * (owners - 1) + layers
+    panels, posts = refs[: 2 * (owners - 1)], refs[2 * (owners - 1) : inputs]
+    factors, (placed_ref, rows_ref) = refs[inputs:-2], refs[-2:]
+    f32, bf16 = jnp.float32, jnp.bfloat16
+    if u == 0:
+        factor_ref, out_ref, turned_ref = factors
+        turned = factor_ref[...].T
+        high = turned.astype(bf16)
+        turned_ref[0, :, :] = high
+        turned_ref[1, :, :] = (turned - high.astype(f32)).astype(bf16)
+    else:
+        (out_ref,) = factors
     rows = block_count * block_rows
     group, wide = CAP * block_rows, CAP * rows
     part = rows // 2
@@ -278,52 +284,62 @@
     for panel in panels:
         rows_ref[at : at + panel.shape[0], :] = panel[:, :width]
         at += panel.shape[0]
-    inverse_rows(rows_ref, turned_ref, high_ref, low_ref)
-    for u, out_ref in ((1, other_ref), (0, own_ref)):
-        for e in range(owners - 1):
-            for h in range(layers // 2):
-                pair = posts[2 * h : 2 * h + 2]
-                pieces = [post[u * part : (u + 1) * part, e * group : (e + 1) * group] for post in pair]
-                notes = [row_of(post[rows:, :wide], e) for post in pair]
-                start = (e * layers + 2 * h) * rows
-                place(placed_ref, slice(start, start + 2 * rows), per_owner, pieces, notes, (block_count, block_rows))
-        placed = placed_ref[...]
-        total = jnp.dot(placed, high_ref[...], preferred_element_type=f32)
-        out_ref[...] = total + jnp.dot(placed, low_ref[...], preferred_element_type=f32)
-
-
-def far_kernel(sizes, u, near_ref, by_y_ref, by_x_ref, turned_ref, out_ref, placed_ref, rows_ref, high_ref, low_ref):
+    for e in range(owners - 1):
+        for h in range(layers // 2):
+            pair = posts[2 * h : 2 * h + 2]
+            pieces = [post[u * part : (u + 1) * part, e * group : (e + 1) * group] for post in pair]
+            notes = [row_of(post[rows:, :wide], e) for post in pair]
+            start = (e * layers + 2 * h) * rows
+            place(placed_ref, slice(start, start + 2 * rows), per_owner, pieces, notes, (block_count, block_rows))
+    gram = jnp.dot(placed_ref[...], rows_ref[...], preferred_element_type=f32)
+    out_ref[...] = gram.astype(out_ref.dtype)
+
+
+def join_kernel(above_ref, below_ref, earlier_ref, out_ref):
+    rows = above_ref.shape[0]
+    out_ref[:rows, :] = above_ref[...]
+    out_ref[rows:, :] = below_ref[...]
+
+
+def middle_kernel(own_ref, other_ref, turned_ref, out_ref):
+    f32, bf16 = jnp.float32, jnp.bfloat16
+    width = own_ref.shape[1]
+    gram = own_ref[...] + other_ref[...].astype(f32)
+    high = gram.astype(bf16)
+    low = (gram - high.astype(f32)).astype(bf16)
+    for start, stop in ((0, width // 2), (width // 2, width)):
+        a, b = turned_ref[0, :stop, start:stop], turned_ref[1, :stop, start:stop]
+        total = jnp.dot(high[:, :stop], a, preferred_element_type=f32)
+        total += jnp.dot(high[:, :stop], b, preferred_element_type=f32)
+        out_ref[:, start:stop] = total + jnp.dot(low[:, :stop], a, preferred_element_type=f32)
+
+
+def final_kernel(sizes, near_ref, own_ref, other_ref, turned_ref, out_hbm, *refs):
     layers, owners, per_owner, block_count, block_rows = sizes
+    sum_ref, placed_ref, rows_ref, high_ref, low_ref, sems = refs
     f32 = jnp.float32
     rows = block_count * block_rows
     group, wide = CAP * block_rows, CAP * rows
-    part = rows // 2
-    first = by_y_ref.shape[0]
-    last = rows_ref.shape[0] - first
-    rows_ref[:first, :] = by_y_ref[...]
-    rows_ref[first:, :] = by_x_ref[:last, :]
+    part, depth = rows // 2, layers * rows
+    for u, ref in enumerate((own_ref, other_ref)):
+        rows_ref[u * depth : (u + 1) * depth, :] = ref[:depth, :]
+        for h in range(layers // 2):
+            pieces, notes = [], []
+            for k in (2 * h, 2 * h + 1):
+                at = (u * layers + k) * group
+                pieces.append(ref[depth : depth + part, at : at + group])
+                notes.append(row_of(ref[depth + part :, :wide], k))
+            start = u * depth + 2 * h * rows
+            place(placed_ref, slice(start, start + 2 * rows), per_owner, pieces, notes, (block_count, block_rows))
     inverse_rows(rows_ref, turned_ref, high_ref, low_ref)
-    for h in range(layers // 2):
-        pieces, notes = [], []
-        for k in (2 * h, 2 * h + 1):
-            at = (u * layers + k) * group
-            pieces.append(by_x_ref[last : last + part, at : at + group])
-            notes.append(row_of(by_x_ref[last + part :, :wide], k))
-        start = 2 * h * rows
-        place(placed_ref, slice(start, start + 2 * rows), per_owner, pieces, notes, (block_count, block_rows))
-    placed = placed_ref[...]
-    total = near_ref[...] + jnp.dot(placed, high_ref[...], preferred_element_type=f32)
-    total += jnp.dot(placed, low_ref[...], preferred_element_type=f32)
-    out_ref[...] = total.astype(out_ref.dtype)
-
-
-def add_kernel(own_ref, other_ref, out_hbm, sum_ref, sems):
     strips = sems.shape[0]
     height = sum_ref.shape[0] // strips
     copies = []
     for i in range(strips):
         here = pl.ds(i * height, height)
-        sum_ref[here, :] = own_ref[here, :] + other_ref[here, :].astype(jnp.float32)
+        placed = placed_ref[here, :]
+        total = near_ref[here, :] + jnp.dot(placed, high_ref[...], preferred_element_type=f32)
+        sum_ref[here, :] = total + jnp.dot(placed, low_ref[...], preferred_element_type=f32)
         copies.append(pltpu.make_async_copy(sum_ref.at[here, :], out_hbm.at[here, :], sems.at[i]))
         copies[-1].start()
     for copy in copies:
@@ -414,38 +430,50 @@
     sizes = (layers, owners, per_owner, block_count, block_rows)
     result = shaped((count, panel_width), f32)
     panels = [weighted, others, from_x, by_x, from_y, by_y]
-    own, other, turned = pl.pallas_call(
-        functools.partial(near_kernel, sizes),
-        out_shape=[result] * 2 + [shaped((2, *factor_inverse.shape), bf16)],
-        in_specs=[vmem] * (len(panels) + layers + 1),
-        out_specs=[vmem] * 3,
-        scratch_shapes=[pltpu.VMEM((count, (owners - 1) * depth), bf16)]
-        + [pltpu.VMEM(((owners - 1) * depth, panel_width), bf16)] * 3,
-        compiler_params=params,
-        name="near",
-    )(*panels, *posts, factor_inverse)
-
-    def far(u, near, kind):
+    def near(u, out_shape, earlier, *factors):
         return pl.pallas_call(
-            functools.partial(far_kernel, sizes, u),
-            out_shape=shaped((count, panel_width), kind),
-            in_specs=[vmem] * 4,
-            out_specs=vmem,
-            scratch_shapes=[pltpu.VMEM((count, depth), bf16)] + [pltpu.VMEM((depth, panel_width), bf16)] * 3,
+            functools.partial(near_kernel, sizes, u, len(earlier)),
+            out_shape=out_shape,
+            in_specs=[anywhere] * len(earlier) + [vmem] * (len(panels) + layers + len(factors)),
+            out_specs=[vmem] * len(out_shape),
+            scratch_shapes=[
+                pltpu.VMEM((count, (owners - 1) * depth), bf16),
+                pltpu.VMEM(((owners - 1) * depth, panel_width), bf16),
+            ],
             compiler_params=params,
-            name="far",
-        )(near, across_y, across_x, turned)
-
-    other = shift(far(1, other, bf16), 0, 0, 1)
+            name="near",
+        )(*earlier, *panels, *posts, *factors)
+
+    other = shift(*near(1, [shaped((count, panel_width), bf16)], [rows_to_y, rest_to_x]), 0, 0, 1)
+    own, turned = near(0, [result, shaped((2, *factor_inverse.shape), bf16)], [], factor_inverse)
+    joined = pl.pallas_call(
+        join_kernel,
+        out_shape=shaped((across_y.shape[0] + across_x.shape[0], panel_width), bf16),
+        in_specs=[vmem] * 2 + [anywhere],
+        out_specs=vmem,
+        compiler_params=params,
+        name="join",
+    )(across_y, across_x, own)
+    other_joined = shift(joined, 0, 0, 1)
+    middle = pl.pallas_call(
+        middle_kernel,
+        out_shape=result,
+        in_specs=[vmem] * 3,
+        out_specs=vmem,
+        compiler_params=params,
+        name="middle",
+    )(own, other, turned)
     out = pl.pallas_call(
-        add_kernel,
+        functools.partial(final_kernel, sizes),
         out_shape=result,
-        in_specs=[vmem] * 2,
+        in_specs=[vmem] * 4,
         out_specs=anywhere,
-        scratch_shapes=[pltpu.VMEM((count, panel_width), f32), pltpu.SemaphoreType.DMA((6,))],
-        compiler_params=params,
-        name="add",
-    )(far(0, own, f32), other)
+        scratch_shapes=[pltpu.VMEM((count, panel_width), f32), pltpu.VMEM((count, 2 * depth), bf16)]
+        + [pltpu.VMEM((2 * depth, panel_width), bf16)] * 3
+        + [pltpu.SemaphoreType.DMA((4,))],
+        compiler_params=params,
+        name="final",
+    )(middle, joined, other_joined, turned)
     return out.reshape(per_owner, slab_width, panel_width)
 
 

time: 34.9 us -> 36.7 us (1.052)
  waiting for transfers between devices: 8.24 us -> 11.5 us
  Pallas kernels: 8.3 us -> 6.98 us
    ppermute x13 -> x14, waiting for transfers between devices: 8.24 us -> 11.5 us  [shift(): return lax.ppermute(value, ('rows', 'cols'), pairs)]
    pallas_call x4 -> x5, Pallas kernels: 6.41 us -> 5.18 us  [the longest x1 2.4 us: local(): pl.pallas_call(functools.partial(final_kernel, sizes), out_shape=result,...]
    ppermute x13 -> x14, starting transfers between devices: 18.1 us -> 18 us  [shift(): return lax.ppermute(value, ('rows', 'cols'), pairs)]
  transfers between devices with their start and end apart: 13 -> 14, of which waited for: 7 -> 8; matrix products, arithmetic and copies ran while one was open for 0% -> 0% of each run, Pallas kernels for 13% -> 5%
where the time goes in v13:
time: 36.7 us; the launch traced here: 36.5 us
  starting transfers between devices  18 us (49%)
  waiting for transfers between devices  11.5 us (31%)
  Pallas kernels  6.98 us (19%)
    ppermute x14, starting transfers between devices, shift(): return lax.ppermute(value, ('rows', 'cols'), pairs)  18 us
    ppermute x14, waiting for transfers between devices, shift(): return lax.ppermute(value, ('rows', 'cols'), pairs)  11.5 us
    pallas_call x1, Pallas kernels, local(): pl.pallas_call(functools.partial(final_kernel, sizes), out_shape=result,...  2.4 us
    pallas_call x2, Pallas kernels, near(): pl.pallas_call(functools.partial(near_kernel, sizes, u, len(earlier)), ou...  1.68 us
    pallas_call x1, Pallas kernels, local(): pl.pallas_call(functools.partial(pack_kernel, sizes), out_shape=[shaped((...  1.57 us
    pallas_call x1, Pallas kernels, local(): pl.pallas_call(middle_kernel, out_shape=result, in_specs=[vmem] * 3, out_...  1.09 us
  transfers between devices with their start and end apart: 14, of which 8 were waited for; matrix products, arithmetic and copies ran while one was open for 0% of the time, Pallas kernels for 5%

profile of v13, /device:TPU:0, one launch (start us, length us, event | category | flops | bytes accessed | tf_op | source)
XLA Modules:
  0.0 36.5 jit_solution(1426083837150423116)
XLA Ops:
  0.0 1.6 %pack.1 = (bf16[64,512]{1,0:T(8,128)(2,1)S(1)}, bf16[64,384]{1,0:T(8,128)(2,1)S(1)}, bf16[64,896]{1,0:T(8,128)(2,1)S(1)}, bf16[64,1152]{1,0:T(8,128)(2,1)S(1)}) custom-call(s32[2,4]{1,0:T(2,128)} %lists_hbm.1, s32[2,4]{1,0:T(2,128)} %masks_hbm.1, s32[96]{0:T(128)} %order_hbm.1, f32[1,64]{1,0:T(1,128)} %bitcast.2, bf16[64,512]{1,0:T(8,128)(2,1)} %panel_hbm.1, ...), custom_call_target="tpu_custom_call" | custom-call | tf_op jit(solution)/shard_map/pack/pallas_call | solution.py:370
  1.6 3.0 %collective-permute-start.1 = (bf16[64,1152]{1,0:T(8,128)(2,1)S(1)}, bf16[64,1152]{1,0:T(8,128)(2,1)S(1)}, u32[]{:S(2)}, u32[]{:S(2)}) collective-permute-start(bf16[64,1152]{1,0:T(8,128)(2,1)S(1)} %get-tuple-element.19), channel_id=1, source_target_pairs={{0,2},{1,3},{2,0},{3,1},{4,6},{5,7},{6,4},{7,5},{8,10},{9,11},{10,... | collective-permute-start | bytes 442376 | tf_op jit(solution)/shard_map/ppermute | solution.py:91
  4.6 1.5 %collective-permute-start = (bf16[64,896]{1,0:T(8,128)(2,1)S(1)}, bf16[64,896]{1,0:T(8,128)(2,1)S(1)}, u32[]{:S(2)}, u32[]{:S(2)}) collective-permute-start(bf16[64,896]{1,0:T(8,128)(2,1)S(1)} %get-tuple-element.18), channel_id=1, source_target_pairs={{0,1},{1,0},{2,3},{3,2},{4,5},{5,4},{6,7},{7,6},{8,9},{9,8},{10,11... | collective-permute-start | bytes 344072 | tf_op jit(solution)/shard_map/ppermute | solution.py:91
  6.1 3.6 %collective-permute-start.4 = (bf16[64,512]{1,0:T(8,128)(2,1)S(1)}, bf16[64,512]{1,0:T(8,128)(2,1)S(1)}, u32[]{:S(2)}, u32[]{:S(2)}) collective-permute-start(bf16[64,512]{1,0:T(8,128)(2,1)S(1)} %get-tuple-element.16.refs_0_.refs_2_), channel_id=1, source_target_pairs={{0,24},{1,25},{2,26},{3,27},{4,28},{5,29},{6,30},{7,31},{8,0},{9,1... | collective-permute-start | bytes 196616 | tf_op jit(solution)/shard_map/ppermute | solution.py:91
  9.7 1.0 %collective-permute-start.2 = (bf16[64,512]{1,0:T(8,128)(2,1)S(1)}, bf16[64,512]{1,0:T(8,128)(2,1)S(1)}, u32[]{:S(2)}, u32[]{:S(2)}) collective-permute-start(bf16[64,512]{1,0:T(8,128)(2,1)S(1)} %get-tuple-element.16.refs_0_.refs_2_), channel_id=1, source_target_pairs={{0,8},{1,9},{2,10},{3,11},{4,12},{5,13},{6,14},{7,15},{8,16},{9,17... | collective-permute-start | bytes 196616 | tf_op jit(solution)/shard_map/ppermute | solution.py:91
  10.7 1.2 %collective-permute-done.4.refs_2_ = bf16[64,512]{1,0:T(8,128)(2,1)S(1)} collective-permute-done((bf16[64,512]{1,0:T(8,128)(2,1)S(1)}, bf16[64,512]{1,0:T(8,128)(2,1)S(1)}, u32[]{:S(2)}, u32[]{:S(2)}) %collective-permute-start.4) | collective-permute-done | bytes 65568 | tf_op jit(solution)/shard_map/ppermute | solution.py:91
  11.9 3.1 %collective-permute-done.3.refs_1_ = bf16[64,512]{1,0:T(8,128)(2,1)S(1)} collective-permute-done((bf16[64,512]{1,0:T(8,128)(2,1)S(1)}, bf16[64,512]{1,0:T(8,128)(2,1)S(1)}, u32[]{:S(2)}, u32[]{:S(2)}) %collective-permute-start.3) | collective-permute-done | bytes 65568 | tf_op jit(solution)/shard_map/ppermute | solution.py:91
  15.0 0.8 %collective-permute-done.2.refs_0_ = bf16[64,512]{1,0:T(8,128)(2,1)S(1)} collective-permute-done((bf16[64,512]{1,0:T(8,128)(2,1)S(1)}, bf16[64,512]{1,0:T(8,128)(2,1)S(1)}, u32[]{:S(2)}, u32[]{:S(2)}) %collective-permute-start.2) | collective-permute-done | bytes 65568 | tf_op jit(solution)/shard_map/ppermute | solution.py:91
  15.8 0.0 collective-permute-done.from_x_ref.refs_2_.refs_4_
  15.8 0.0 collective-permute-done.1.from_y_ref.refs_4_.refs_6_
  15.8 0.1 sort.1
  15.9 0.6 %collective-permute-start.5 = (bf16[192,512]{1,0:T(8,128)(2,1)S(1)}, bf16[192,512]{1,0:T(8,128)(2,1)S(1)}, u32[]{:S(2)}, u32[]{:S(2)}) collective-permute-start(bf16[192,512]{1,0:T(8,128)(2,1)S(1)} %get-tuple-element.20.refs_1_.refs_3_), channel_id=1, source_target_pairs={{0,1},{1,0},{2,3},{3,2},{4,5},{5,4},{6,7},{7,6},{8,9},{9,8},{10,11... | collective-permute-start | bytes 589832 | tf_op jit(solution)/shard_map/ppermute | solution.py:91
  16.5 0.5 %collective-permute-start.6 = (bf16[192,512]{1,0:T(8,128)(2,1)S(1)}, bf16[192,512]{1,0:T(8,128)(2,1)S(1)}, u32[]{:S(2)}, u32[]{:S(2)}) collective-permute-start(bf16[192,512]{1,0:T(8,128)(2,1)S(1)} %get-tuple-element.20.refs_1_.refs_3_), channel_id=1, source_target_pairs={{0,2},{1,3},{2,0},{3,1},{4,6},{5,7},{6,4},{7,5},{8,10},{9,11},{10,... | collective-permute-start | bytes 589832 | tf_op jit(solution)/shard_map/ppermute | solution.py:91
  17.0 0.0 collective-permute-start.7
  17.0 2.3 %collective-permute-start.8 = (bf16[80,256]{1,0:T(8,128)(2,1)S(1)}, bf16[80,256]{1,0:T(8,128)(2,1)S(1)}, u32[]{:S(2)}, u32[]{:S(2)}) collective-permute-start(bf16[80,256]{1,0:T(8,128)(2,1)S(1)} %get-tuple-element.23), channel_id=1, source_target_pairs={{0,16},{1,17},{2,18},{3,19},{4,20},{5,21},{6,22},{7,23},{8,24},{9,... | collective-permute-start | bytes 122888 | tf_op jit(solution)/shard_map/ppermute | solution.py:91
  19.3 2.2 %collective-permute-start.9 = (bf16[80,256]{1,0:T(8,128)(2,1)S(1)}, bf16[80,256]{1,0:T(8,128)(2,1)S(1)}, u32[]{:S(2)}, u32[]{:S(2)}) collective-permute-start(bf16[80,256]{1,0:T(8,128)(2,1)S(1)} %get-tuple-element.24), channel_id=1, source_target_pairs={{0,24},{1,25},{2,26},{3,27},{4,28},{5,29},{6,30},{7,31},{8,0},{9,1... | collective-permute-start | bytes 122888 | tf_op jit(solution)/shard_map/ppermute | solution.py:91
  21.6 1.3 %collective-permute-done.7.refs_7_.refs_0_.refs_1_.refs_9_ = bf16[80,256]{1,0:T(8,128)(2,1)S(1)} collective-permute-done((bf16[80,256]{1,0:T(8,128)(2,1)S(1)}, bf16[80,256]{1,0:T(8,128)(2,1)S(1)}, u32[]{:S(2)}, u32[]{:S(2)}) %collective-permute-start.7) | collective-permute-done | bytes 40992 | tf_op jit(solution)/shard_map/ppermute | solution.py:91
  22.8 0.0 collective-permute-done.8.refs_8_.refs_1_.refs_2_.refs_10_
  22.8 0.6 %collective-permute-done.9.refs_9_.refs_2_.refs_3_.refs_11_ = bf16[80,256]{1,0:T(8,128)(2,1)S(1)} collective-permute-done((bf16[80,256]{1,0:T(8,128)(2,1)S(1)}, bf16[80,256]{1,0:T(8,128)(2,1)S(1)}, u32[]{:S(2)}, u32[]{:S(2)}) %collective-permute-start.9) | collective-permute-done | bytes 40992 | tf_op jit(solution)/shard_map/ppermute | solution.py:91
  23.4 0.0 collective-permute-done.5.refs_3_.by_x_ref.refs_5_
  23.4 0.1 rest_to_x.1.refs_1_
  23.5 0.8 %near.3 = bf16[768,512]{1,0:T(8,128)(2,1)S(1)} custom-call(bf16[224,512]{1,0:T(8,128)(2,1)S(1)} %rows_to_y.1.refs_0_, bf16[80,512]{1,0:T(8,128)(2,1)S(1)} %rest_to_x.1.refs_1_, bf16[64,512]{1,0:T(8,128)(2,1)S(1)} %get-tuple-element.16.refs_0_.refs_2_, bf16[192,512]{1,0:T(8,128)(2,1)S(1)} %get-tuple-element.20.refs_1_.refs_3_, ...), custom_call_target="tpu_custom_call" | custom-call | tf_op jit(solution)/shard_map/near/pallas_call | solution.py:434
  24.4 0.1 collective-permute-start.10
  24.4 1.6 %collective-permute-start.11 = (bf16[224,512]{1,0:T(8,128)(2,1)S(1)}, bf16[224,512]{1,0:T(8,128)(2,1)S(1)}, u32[]{:S(2)}, u32[]{:S(2)}) collective-permute-start(bf16[224,512]{1,0:T(8,128)(2,1)S(1)} %rows_to_y.1.refs_0_), channel_id=1, source_target_pairs={{0,2},{1,3},{2,0},{3,1},{4,6},{5,7},{6,4},{7,5},{8,10},{9,11},{10,... | collective-permute-start | bytes 688136 | tf_op jit(solution)/shard_map/ppermute | solution.py:91
  26.0 1.5 %collective-permute-start.12 = (bf16[80,512]{1,0:T(8,128)(2,1)S(1)}, bf16[80,512]{1,0:T(8,128)(2,1)S(1)}, u32[]{:S(2)}, u32[]{:S(2)}) collective-permute-start(bf16[80,512]{1,0:T(8,128)(2,1)S(1)} %rest_to_x.1.refs_1_), channel_id=1, source_target_pairs={{0,1},{1,0},{2,3},{3,2},{4,5},{5,4},{6,7},{7,6},{8,9},{9,8},{10,11... | collective-permute-start | bytes 245768 | tf_op jit(solution)/shard_map/ppermute | solution.py:91
  27.5 0.8 %near.2 = (f32[768,512]{1,0:T(8,128)S(1)}, bf16[2,512,512]{2,1,0:T(8,128)(2,1)S(1)}) custom-call(bf16[64,512]{1,0:T(8,128)(2,1)S(1)} %get-tuple-element.16.refs_0_.refs_2_, bf16[192,512]{1,0:T(8,128)(2,1)S(1)} %get-tuple-element.20.refs_1_.refs_3_, bf16[64,896]{1,0:T(8,128)(2,1)S(1)} %collective-permute-done.from_x_ref.refs_2_.refs_4_, ...), custom_call_target="tpu_custom_call" | custom-call | tf_op jit(solution)/shard_map/near/pallas_call | solution.py:434
  28.4 2.2 %collective-permute-done.12.below_ref = bf16[80,512]{1,0:T(8,128)(2,1)S(1)} collective-permute-done((bf16[80,512]{1,0:T(8,128)(2,1)S(1)}, bf16[80,512]{1,0:T(8,128)(2,1)S(1)}, u32[]{:S(2)}, u32[]{:S(2)}) %collective-permute-start.12) | collective-permute-done | bytes 81952 | tf_op jit(solution)/shard_map/ppermute | solution.py:91
  30.5 1.9 %collective-permute-done.11.above_ref = bf16[224,512]{1,0:T(8,128)(2,1)S(1)} collective-permute-done((bf16[224,512]{1,0:T(8,128)(2,1)S(1)}, bf16[224,512]{1,0:T(8,128)(2,1)S(1)}, u32[]{:S(2)}, u32[]{:S(2)}) %collective-permute-start.11) | collective-permute-done | bytes 229408 | tf_op jit(solution)/shard_map/ppermute | solution.py:91
  32.5 0.1 collective-permute-start.13
  32.6 1.1 %middle.1.near_ref = f32[768,512]{1,0:T(8,128)S(1)} custom-call(f32[768,512]{1,0:T(8,128)S(1)} %get-tuple-element.25.own_ref.earlier_ref, bf16[768,512]{1,0:T(8,128)(2,1)S(1)} %collective-permute-done.10.other_ref, bf16[2,512,512]{2,1,0:T(8,128)(2,1)S(1)} %get-tuple-element.26.turned_ref), custom_call_target="tpu_custom_call" | custom-call | tf_op jit(solution)/shard_map/middle/pallas_call | solution.py:458
  33.7 0.5 %collective-permute-done.13.other_ref = bf16[304,512]{1,0:T(8,128)(2,1)S(1)} collective-permute-done((bf16[304,512]{1,0:T(8,128)(2,1)S(1)}, bf16[304,512]{1,0:T(8,128)(2,1)S(1)}, u32[]{:S(2)}, u32[]{:S(2)}) %collective-permute-start.13) | collective-permute-done | bytes 311328 | tf_op jit(solution)/shard_map/ppermute | solution.py:91
  34.1 2.4 %final.1 = f32[768,512]{1,0:T(8,128)} custom-call(f32[768,512]{1,0:T(8,128)S(1)} %middle.1.near_ref, bf16[304,512]{1,0:T(8,128)(2,1)S(1)} %join.1.own_ref, bf16[304,512]{1,0:T(8,128)(2,1)S(1)} %collective-permute-done.13.other_ref, bf16[2,512,512]{2,1,0:T(8,128)(2,1)S(1)} %get-tuple-element.26.turned_ref), custom_call_target="tpu_custom_call" | custom-call | tf_op jit(solution)/shard_map/final/pallas_call | solution.py:466
  (7 shorter events, 0.0 us)
Async XLA Ops:
  1.6 14.2 %collective-permute-start.1 = (bf16[64,1152]{1,0:T(8,128)(2,1)S(1)}, bf16[64,1152]{1,0:T(8,128)(2,1)S(1)}, u32[]{:S(2)}, u32[]{:S(2)}) collective-permute-start(bf16[64,1152]{1,0:T(8,128)(2,1)S(1)} %get-tuple-element.19), channel_id=1, source_target_pairs={{0,2},{1,3},{2,0},{3,1},{4,6},{5,7},{6,4},{7,5},{8,10},{9,11},{10,... | collective-permute-start | bytes 442376 | tf_op jit(solution)/shard_map/ppermute | solution.py:91
  4.6 11.2 %collective-permute-start = (bf16[64,896]{1,0:T(8,128)(2,1)S(1)}, bf16[64,896]{1,0:T(8,128)(2,1)S(1)}, u32[]{:S(2)}, u32[]{:S(2)}) collective-permute-start(bf16[64,896]{1,0:T(8,128)(2,1)S(1)} %get-tuple-element.18), channel_id=1, source_target_pairs={{0,1},{1,0},{2,3},{3,2},{4,5},{5,4},{6,7},{7,6},{8,9},{9,8},{10,11... | collective-permute-start | bytes 344072 | tf_op jit(solution)/shard_map/ppermute | solution.py:91
  6.1 5.8 %collective-permute-start.4 = (bf16[64,512]{1,0:T(8,128)(2,1)S(1)}, bf16[64,512]{1,0:T(8,128)(2,1)S(1)}, u32[]{:S(2)}, u32[]{:S(2)}) collective-permute-start(bf16[64,512]{1,0:T(8,128)(2,1)S(1)} %get-tuple-element.16.refs_0_.refs_2_), channel_id=1, source_target_pairs={{0,24},{1,25},{2,26},{3,27},{4,28},{5,29},{6,30},{7,31},{8,0},{9,1... | collective-permute-start | bytes 196616 | tf_op jit(solution)/shard_map/ppermute | solution.py:91
  9.7 5.3 %collective-permute-start.3 = (bf16[64,512]{1,0:T(8,128)(2,1)S(1)}, bf16[64,512]{1,0:T(8,128)(2,1)S(1)}, u32[]{:S(2)}, u32[]{:S(2)}) collective-permute-start(bf16[64,512]{1,0:T(8,128)(2,1)S(1)} %get-tuple-element.16.refs_0_.refs_2_), channel_id=1, source_target_pairs={{0,16},{1,17},{2,18},{3,19},{4,20},{5,21},{6,22},{7,23},{8,24},{9,... | collective-permute-start | bytes 196616 | tf_op jit(solution)/shard_map/ppermute | solution.py:91
  9.7 6.1 %collective-permute-start.2 = (bf16[64,512]{1,0:T(8,128)(2,1)S(1)}, bf16[64,512]{1,0:T(8,128)(2,1)S(1)}, u32[]{:S(2)}, u32[]{:S(2)}) collective-permute-start(bf16[64,512]{1,0:T(8,128)(2,1)S(1)} %get-tuple-element.16.refs_0_.refs_2_), channel_id=1, source_target_pairs={{0,8},{1,9},{2,10},{3,11},{4,12},{5,13},{6,14},{7,15},{8,16},{9,17... | collective-permute-start | bytes 196616 | tf_op jit(solution)/shard_map/ppermute | solution.py:91
  15.9 7.5 %collective-permute-start.5 = (bf16[192,512]{1,0:T(8,128)(2,1)S(1)}, bf16[192,512]{1,0:T(8,128)(2,1)S(1)}, u32[]{:S(2)}, u32[]{:S(2)}) collective-permute-start(bf16[192,512]{1,0:T(8,128)(2,1)S(1)} %get-tuple-element.20.refs_1_.refs_3_), channel_id=1, source_target_pairs={{0,1},{1,0},{2,3},{3,2},{4,5},{5,4},{6,7},{7,6},{8,9},{9,8},{10,11... | collective-permute-start | bytes 589832 | tf_op jit(solution)/shard_map/ppermute | solution.py:91
  16.5 6.9 %collective-permute-start.6 = (bf16[192,512]{1,0:T(8,128)(2,1)S(1)}, bf16[192,512]{1,0:T(8,128)(2,1)S(1)}, u32[]{:S(2)}, u32[]{:S(2)}) collective-permute-start(bf16[192,512]{1,0:T(8,128)(2,1)S(1)} %get-tuple-element.20.refs_1_.refs_3_), channel_id=1, source_target_pairs={{0,2},{1,3},{2,0},{3,1},{4,6},{5,7},{6,4},{7,5},{8,10},{9,11},{10,... | collective-permute-start | bytes 589832 | tf_op jit(solution)/shard_map/ppermute | solution.py:91
  17.0 5.8 %collective-permute-start.7 = (bf16[80,256]{1,0:T(8,128)(2,1)S(1)}, bf16[80,256]{1,0:T(8,128)(2,1)S(1)}, u32[]{:S(2)}, u32[]{:S(2)}) collective-permute-start(bf16[80,256]{1,0:T(8,128)(2,1)S(1)} %get-tuple-element.22), channel_id=1, source_target_pairs={{0,8},{1,9},{2,10},{3,11},{4,12},{5,13},{6,14},{7,15},{8,16},{9,17... | collective-permute-start | bytes 122888 | tf_op jit(solution)/shard_map/ppermute | solution.py:91
  17.0 5.8 %collective-permute-start.8 = (bf16[80,256]{1,0:T(8,128)(2,1)S(1)}, bf16[80,256]{1,0:T(8,128)(2,1)S(1)}, u32[]{:S(2)}, u32[]{:S(2)}) collective-permute-start(bf16[80,256]{1,0:T(8,128)(2,1)S(1)} %get-tuple-element.23), channel_id=1, source_target_pairs={{0,16},{1,17},{2,18},{3,19},{4,20},{5,21},{6,22},{7,23},{8,24},{9,... | collective-permute-start | bytes 122888 | tf_op jit(solution)/shard_map/ppermute | solution.py:91
  19.3 8.2 %copy-start = (f32[512,512]{1,0:T(8,128)S(1)}, f32[512,512]{1,0:T(8,128)}, u32[]{:S(2)}) copy-start(f32[512,512]{1,0:T(8,128)} %refs_10_.1) | copy-start | bytes 3145732
  19.3 4.0 %collective-permute-start.9 = (bf16[80,256]{1,0:T(8,128)(2,1)S(1)}, bf16[80,256]{1,0:T(8,128)(2,1)S(1)}, u32[]{:S(2)}, u32[]{:S(2)}) collective-permute-start(bf16[80,256]{1,0:T(8,128)(2,1)S(1)} %get-tuple-element.24), channel_id=1, source_target_pairs={{0,24},{1,25},{2,26},{3,27},{4,28},{5,29},{6,30},{7,31},{8,0},{9,1... | collective-permute-start | bytes 122888 | tf_op jit(solution)/shard_map/ppermute | solution.py:91
  24.4 8.2 %collective-permute-start.10 = (bf16[768,512]{1,0:T(8,128)(2,1)S(1)}, bf16[768,512]{1,0:T(8,128)(2,1)S(1)}, u32[]{:S(2)}, u32[]{:S(2)}) collective-permute-start(bf16[768,512]{1,0:T(8,128)(2,1)S(1)} %near.3), channel_id=1, source_target_pairs={{0,4},{1,5},{2,6},{3,7},{4,0},{5,1},{6,2},{7,3},{8,12},{9,13},{10,... | collective-permute-start | bytes 2359304 | tf_op jit(solution)/shard_map/ppermute | solution.py:91
  24.4 8.0 %collective-permute-start.11 = (bf16[224,512]{1,0:T(8,128)(2,1)S(1)}, bf16[224,512]{1,0:T(8,128)(2,1)S(1)}, u32[]{:S(2)}, u32[]{:S(2)}) collective-permute-start(bf16[224,512]{1,0:T(8,128)(2,1)S(1)} %rows_to_y.1.refs_0_), channel_id=1, source_target_pairs={{0,2},{1,3},{2,0},{3,1},{4,6},{5,7},{6,4},{7,5},{8,10},{9,11},{10,... | collective-permute-start | bytes 688136 | tf_op jit(solution)/shard_map/ppermute | solution.py:91
  26.0 4.5 %collective-permute-start.12 = (bf16[80,512]{1,0:T(8,128)(2,1)S(1)}, bf16[80,512]{1,0:T(8,128)(2,1)S(1)}, u32[]{:S(2)}, u32[]{:S(2)}) collective-permute-start(bf16[80,512]{1,0:T(8,128)(2,1)S(1)} %rest_to_x.1.refs_1_), channel_id=1, source_target_pairs={{0,1},{1,0},{2,3},{3,2},{4,5},{5,4},{6,7},{7,6},{8,9},{9,8},{10,11... | collective-permute-start | bytes 245768 | tf_op jit(solution)/shard_map/ppermute | solution.py:91
  32.5 1.7 %collective-permute-start.13 = (bf16[304,512]{1,0:T(8,128)(2,1)S(1)}, bf16[304,512]{1,0:T(8,128)(2,1)S(1)}, u32[]{:S(2)}, u32[]{:S(2)}) collective-permute-start(bf16[304,512]{1,0:T(8,128)(2,1)S(1)} %join.1.own_ref), channel_id=1, source_target_pairs={{0,4},{1,5},{2,6},{3,7},{4,0},{5,1},{6,2},{7,3},{8,12},{9,13},{10,... | collective-permute-start | bytes 933896 | tf_op jit(solution)/shard_map/ppermute | solution.py:91

commit v14 on v13

--- a/solution.py
+++ b/solution.py
@@ -89,6 +89,10 @@
         for c in range(owners):
             pairs.append((r * owners + c, to_r * owners + (c ^ flip_cols)))
     return lax.ppermute(value, ("rows", "cols"), pairs)
+
+
+def lasting(flops):
+    return pl.CostEstimate(flops=flops, bytes_accessed=0, transcendentals=0)
 
 
 def pack_kernel(sizes, lists_hbm, masks_hbm, order_hbm, weights_hbm, panel_hbm, jac_hbm, *refs):
@@ -191,13 +195,17 @@
     return block.astype(jnp.bfloat16)
 
 
-def sort_kernel(sizes, kept_ref, from_x_ref, from_y_ref, *refs):
+def stack_kernel(*refs):
+    at = 0
+    for ref in refs[:-1]:
+        refs[-1][at : at + ref.shape[0], :] = ref[...]
+        at += ref.shape[0]
+
+
+def sort_kernel(sizes, kept_ref, from_x_ref, from_y_ref, *posts):
     layers, width, lane_group, wide = sizes
-    line, (stacked, *posts) = refs[: layers - 1], refs[layers - 1 :]
     post = layers * lane_group
     rows = kept_ref.shape[0]
-    for k, ref in enumerate(line):
-        stacked[k * rows : (k + 1) * rows, :] = ref[...]
     spots = [(kept_ref, 0), (from_x_ref, width), (from_y_ref, width), (from_y_ref, width + post)]
     notes = [row_of(ref[:16, ref.shape[1] - wide :], int(e == 3)) for e, (ref, start) in enumerate(spots)]
     block = rows_from(notes)
@@ -295,7 +303,7 @@
     out_ref[...] = gram.astype(out_ref.dtype)
 
 
-def join_kernel(above_ref, below_ref, earlier_ref, out_ref):
+def join_kernel(above_ref, below_ref, out_ref):
     rows = above_ref.shape[0]
     out_ref[:rows, :] = above_ref[...]
     out_ref[rows:, :] = below_ref[...]
@@ -393,15 +401,24 @@
     from_x, from_y = shift(to_x, 0, 1), shift(to_y, 0, 2)
 
     sizes = (layers, panel_width, lane_group, wide)
-    others, *posts = pl.pallas_call(
+    others = pl.pallas_call(
+        stack_kernel,
+        out_shape=shaped(((layers - 1) * rows, panel_width), bf16),
+        in_specs=[vmem] * (layers - 1),
+        out_specs=vmem,
+        compiler_params=params,
+        cost_estimate=lasting(10**10),
+        name="stack",
+    )(*line)
+    posts = pl.pallas_call(
         functools.partial(sort_kernel, sizes),
-        out_shape=[shaped(((layers - 1) * rows, panel_width), bf16)]
-        + [shaped((rows + 16, owners * lane_group), bf16)] * layers,
-        in_specs=[vmem] * (layers + 2),
-        out_specs=[vmem] * (layers + 1),
-        compiler_params=params,
+        out_shape=[shaped((rows + 16, owners * lane_group), bf16)] * layers,
+        in_specs=[vmem] * 3,
+        out_specs=[vmem] * layers,
+        compiler_params=params,
+        cost_estimate=lasting(10**10),
         name="sort",
-    )(kept, from_x, from_y, *line)
+    )(kept, from_x, from_y)
     posts = [posts[0]] + [shift(posts[k], k, 0) for k in range(1, layers)]
     by_x, by_y = shift(others, 0, 1), shift(others, 0, 2)
 
@@ -441,6 +458,7 @@
                 pltpu.VMEM(((owners - 1) * depth, panel_width), bf16),
             ],
             compiler_params=params,
+            cost_estimate=lasting(0 if u else 10**10),
             name="near",
         )(*earlier, *panels, *posts, *factors)
 
@@ -449,11 +467,11 @@
     joined = pl.pallas_call(
         join_kernel,
         out_shape=shaped((across_y.shape[0] + across_x.shape[0], panel_width), bf16),
-        in_specs=[vmem] * 2 + [anywhere],
+        in_specs=[vmem] * 2,
         out_specs=vmem,
         compiler_params=params,
         name="join",
-    )(across_y, across_x, own)
+    )(across_y, across_x)
     other_joined = shift(joined, 0, 0, 1)
     middle = pl.pallas_call(
         middle_kernel,

time: 36.7 us -> 33.8 us (0.921)
  waiting for transfers between devices: 11.5 us -> 7.92 us
  starting transfers between devices: 18 us -> 18.6 us
    ppermute x14, waiting for transfers between devices: 11.5 us -> 7.92 us  [shift(): return lax.ppermute(value, ('rows', 'cols'), pairs)]
    ppermute x14, starting transfers between devices: 18 us -> 18.6 us  [shift(): return lax.ppermute(value, ('rows', 'cols'), pairs)]
  transfers between devices with their start and end apart: 14 -> 14, of which waited for: 8 -> 8; matrix products, arithmetic and copies ran while one was open for 0% -> 0% of each run, Pallas kernels for 5% -> 9%
where the time goes in v14:
time: 33.8 us; the launch traced here: 33.6 us
  starting transfers between devices  18.6 us (55%)
  waiting for transfers between devices  7.92 us (23%)
  Pallas kernels  6.99 us (21%)
    ppermute x14, starting transfers between devices, shift(): return lax.ppermute(value, ('rows', 'cols'), pairs)  18.6 us
    ppermute x14, waiting for transfers between devices, shift(): return lax.ppermute(value, ('rows', 'cols'), pairs)  7.92 us
    pallas_call x1, Pallas kernels, local(): pl.pallas_call(functools.partial(final_kernel, sizes), out_shape=result,...  2.4 us
    pallas_call x2, Pallas kernels, near(): pl.pallas_call(functools.partial(near_kernel, sizes, u, len(earlier)), ou...  1.67 us
    pallas_call x1, Pallas kernels, local(): pl.pallas_call(functools.partial(pack_kernel, sizes), out_shape=[shaped((...  1.57 us
    pallas_call x1, Pallas kernels, local(): pl.pallas_call(middle_kernel, out_shape=result, in_specs=[vmem] * 3, out_...  1.09 us
  transfers between devices with their start and end apart: 14, of which 8 were waited for; matrix products, arithmetic and copies ran while one was open for 0% of the time, Pallas kernels for 9%

profile of v14, /device:TPU:0, one launch (start us, length us, event | category | flops | bytes accessed | tf_op | source)
XLA Modules:
  0.0 33.6 jit_solution(15101153198108621452)
XLA Ops:
  0.0 1.6 %pack.1 = (bf16[64,512]{1,0:T(8,128)(2,1)S(1)}, bf16[64,384]{1,0:T(8,128)(2,1)S(1)}, bf16[64,896]{1,0:T(8,128)(2,1)S(1)}, bf16[64,1152]{1,0:T(8,128)(2,1)S(1)}) custom-call(s32[2,4]{1,0:T(2,128)} %lists_hbm.1, s32[2,4]{1,0:T(2,128)} %masks_hbm.1, s32[96]{0:T(128)} %order_hbm.1, f32[1,64]{1,0:T(1,128)} %bitcast.2, bf16[64,512]{1,0:T(8,128)(2,1)} %panel_hbm.1, ...), custom_call_target="tpu_custom_call" | custom-call | tf_op jit(solution)/shard_map/pack/pallas_call | solution.py:378
  1.6 3.1 %collective-permute-start = (bf16[64,512]{1,0:T(8,128)(2,1)S(1)}, bf16[64,512]{1,0:T(8,128)(2,1)S(1)}, u32[]{:S(2)}, u32[]{:S(2)}) collective-permute-start(bf16[64,512]{1,0:T(8,128)(2,1)S(1)} %get-tuple-element.15.refs_0_.refs_2_), channel_id=1, source_target_pairs={{0,8},{1,9},{2,10},{3,11},{4,12},{5,13},{6,14},{7,15},{8,16},{9,17... | collective-permute-start | bytes 196616 | tf_op jit(solution)/shard_map/ppermute | solution.py:91
  4.7 2.6 %collective-permute-start.1 = (bf16[64,512]{1,0:T(8,128)(2,1)S(1)}, bf16[64,512]{1,0:T(8,128)(2,1)S(1)}, u32[]{:S(2)}, u32[]{:S(2)}) collective-permute-start(bf16[64,512]{1,0:T(8,128)(2,1)S(1)} %get-tuple-element.15.refs_0_.refs_2_), channel_id=1, source_target_pairs={{0,16},{1,17},{2,18},{3,19},{4,20},{5,21},{6,22},{7,23},{8,24},{9,... | collective-permute-start | bytes 196616 | tf_op jit(solution)/shard_map/ppermute | solution.py:91
  7.2 1.3 %collective-permute-start.2 = (bf16[64,512]{1,0:T(8,128)(2,1)S(1)}, bf16[64,512]{1,0:T(8,128)(2,1)S(1)}, u32[]{:S(2)}, u32[]{:S(2)}) collective-permute-start(bf16[64,512]{1,0:T(8,128)(2,1)S(1)} %get-tuple-element.15.refs_0_.refs_2_), channel_id=1, source_target_pairs={{0,24},{1,25},{2,26},{3,27},{4,28},{5,29},{6,30},{7,31},{8,0},{9,1... | collective-permute-start | bytes 196616 | tf_op jit(solution)/shard_map/ppermute | solution.py:91
  8.6 1.5 %collective-permute-start.3 = (bf16[64,896]{1,0:T(8,128)(2,1)S(1)}, bf16[64,896]{1,0:T(8,128)(2,1)S(1)}, u32[]{:S(2)}, u32[]{:S(2)}) collective-permute-start(bf16[64,896]{1,0:T(8,128)(2,1)S(1)} %get-tuple-element.16), channel_id=1, source_target_pairs={{0,1},{1,0},{2,3},{3,2},{4,5},{5,4},{6,7},{7,6},{8,9},{9,8},{10,11... | collective-permute-start | bytes 344072 | tf_op jit(solution)/shard_map/ppermute | solution.py:91
  10.1 1.5 %collective-permute-start.5 = (bf16[64,1152]{1,0:T(8,128)(2,1)S(1)}, bf16[64,1152]{1,0:T(8,128)(2,1)S(1)}, u32[]{:S(2)}, u32[]{:S(2)}) collective-permute-start(bf16[64,1152]{1,0:T(8,128)(2,1)S(1)} %get-tuple-element.17), channel_id=1, source_target_pairs={{0,2},{1,3},{2,0},{3,1},{4,6},{5,7},{6,4},{7,5},{8,10},{9,11},{10,... | collective-permute-start | bytes 442376 | tf_op jit(solution)/shard_map/ppermute | solution.py:91
  11.6 0.1 collective-permute-done.1.refs_1_
  11.7 0.2 collective-permute-done.2.refs_2_
  12.0 1.6 %collective-permute-start.4 = (bf16[192,512]{1,0:T(8,128)(2,1)S(1)}, bf16[192,512]{1,0:T(8,128)(2,1)S(1)}, u32[]{:S(2)}, u32[]{:S(2)}) collective-permute-start(bf16[192,512]{1,0:T(8,128)(2,1)S(1)} %stack.1.refs_1_.refs_3_), channel_id=1, source_target_pairs={{0,1},{1,0},{2,3},{3,2},{4,5},{5,4},{6,7},{7,6},{8,9},{9,8},{10,11... | collective-permute-start | bytes 589832 | tf_op jit(solution)/shard_map/ppermute | solution.py:91
  13.6 1.5 %collective-permute-start.6 = (bf16[192,512]{1,0:T(8,128)(2,1)S(1)}, bf16[192,512]{1,0:T(8,128)(2,1)S(1)}, u32[]{:S(2)}, u32[]{:S(2)}) collective-permute-start(bf16[192,512]{1,0:T(8,128)(2,1)S(1)} %stack.1.refs_1_.refs_3_), channel_id=1, source_target_pairs={{0,2},{1,3},{2,0},{3,1},{4,6},{5,7},{6,4},{7,5},{8,10},{9,11},{10,... | collective-permute-start | bytes 589832 | tf_op jit(solution)/shard_map/ppermute | solution.py:91
  15.1 0.0 collective-permute-done.3.from_x_ref.refs_2_.refs_4_
  15.1 0.6 %collective-permute-done.5.from_y_ref.refs_4_.refs_6_ = bf16[64,1152]{1,0:T(8,128)(2,1)S(1)} collective-permute-done((bf16[64,1152]{1,0:T(8,128)(2,1)S(1)}, bf16[64,1152]{1,0:T(8,128)(2,1)S(1)}, u32[]{:S(2)}, u32[]{:S(2)}) %collective-permute-start.5) | collective-permute-done | bytes 147488 | tf_op jit(solution)/shard_map/ppermute | solution.py:91
  15.7 0.1 sort.1
  15.9 1.0 %collective-permute-start.7 = (bf16[80,256]{1,0:T(8,128)(2,1)S(1)}, bf16[80,256]{1,0:T(8,128)(2,1)S(1)}, u32[]{:S(2)}, u32[]{:S(2)}) collective-permute-start(bf16[80,256]{1,0:T(8,128)(2,1)S(1)} %get-tuple-element.20), channel_id=1, source_target_pairs={{0,8},{1,9},{2,10},{3,11},{4,12},{5,13},{6,14},{7,15},{8,16},{9,17... | collective-permute-start | bytes 122888 | tf_op jit(solution)/shard_map/ppermute | solution.py:91
  16.8 2.0 %collective-permute-start.8 = (bf16[80,256]{1,0:T(8,128)(2,1)S(1)}, bf16[80,256]{1,0:T(8,128)(2,1)S(1)}, u32[]{:S(2)}, u32[]{:S(2)}) collective-permute-start(bf16[80,256]{1,0:T(8,128)(2,1)S(1)} %get-tuple-element.21), channel_id=1, source_target_pairs={{0,16},{1,17},{2,18},{3,19},{4,20},{5,21},{6,22},{7,23},{8,24},{9,... | collective-permute-start | bytes 122888 | tf_op jit(solution)/shard_map/ppermute | solution.py:91
  18.9 0.9 %collective-permute-start.9 = (bf16[80,256]{1,0:T(8,128)(2,1)S(1)}, bf16[80,256]{1,0:T(8,128)(2,1)S(1)}, u32[]{:S(2)}, u32[]{:S(2)}) collective-permute-start(bf16[80,256]{1,0:T(8,128)(2,1)S(1)} %get-tuple-element.22), channel_id=1, source_target_pairs={{0,24},{1,25},{2,26},{3,27},{4,28},{5,29},{6,30},{7,31},{8,0},{9,1... | collective-permute-start | bytes 122888 | tf_op jit(solution)/shard_map/ppermute | solution.py:91
  19.7 2.0 %collective-permute-done.7.refs_7_.refs_0_.refs_1_.refs_9_ = bf16[80,256]{1,0:T(8,128)(2,1)S(1)} collective-permute-done((bf16[80,256]{1,0:T(8,128)(2,1)S(1)}, bf16[80,256]{1,0:T(8,128)(2,1)S(1)}, u32[]{:S(2)}, u32[]{:S(2)}) %collective-permute-start.7) | collective-permute-done | bytes 40992 | tf_op jit(solution)/shard_map/ppermute | solution.py:91
  21.8 0.8 %collective-permute-done.8.refs_8_.refs_1_.refs_2_.refs_10_ = bf16[80,256]{1,0:T(8,128)(2,1)S(1)} collective-permute-done((bf16[80,256]{1,0:T(8,128)(2,1)S(1)}, bf16[80,256]{1,0:T(8,128)(2,1)S(1)}, u32[]{:S(2)}, u32[]{:S(2)}) %collective-permute-start.8) | collective-permute-done | bytes 40992 | tf_op jit(solution)/shard_map/ppermute | solution.py:91
  22.6 0.4 %collective-permute-done.9.refs_9_.refs_2_.refs_3_.refs_11_ = bf16[80,256]{1,0:T(8,128)(2,1)S(1)} collective-permute-done((bf16[80,256]{1,0:T(8,128)(2,1)S(1)}, bf16[80,256]{1,0:T(8,128)(2,1)S(1)}, u32[]{:S(2)}, u32[]{:S(2)}) %collective-permute-start.9) | collective-permute-done | bytes 40992 | tf_op jit(solution)/shard_map/ppermute | solution.py:91
  23.0 0.0 collective-permute-done.4.refs_3_.by_x_ref.refs_5_
  23.1 0.8 %collective-permute-start.11 = (bf16[224,512]{1,0:T(8,128)(2,1)S(1)}, bf16[224,512]{1,0:T(8,128)(2,1)S(1)}, u32[]{:S(2)}, u32[]{:S(2)}) collective-permute-start(bf16[224,512]{1,0:T(8,128)(2,1)S(1)} %rows_to_y.1.refs_0_), channel_id=1, source_target_pairs={{0,2},{1,3},{2,0},{3,1},{4,6},{5,7},{6,4},{7,5},{8,10},{9,11},{10,... | collective-permute-start | bytes 688136 | tf_op jit(solution)/shard_map/ppermute | solution.py:91
  23.9 0.1 rest_to_x.1.refs_1_
  24.0 0.6 %collective-permute-start.12 = (bf16[80,512]{1,0:T(8,128)(2,1)S(1)}, bf16[80,512]{1,0:T(8,128)(2,1)S(1)}, u32[]{:S(2)}, u32[]{:S(2)}) collective-permute-start(bf16[80,512]{1,0:T(8,128)(2,1)S(1)} %rest_to_x.1.refs_1_), channel_id=1, source_target_pairs={{0,1},{1,0},{2,3},{3,2},{4,5},{5,4},{6,7},{7,6},{8,9},{9,8},{10,11... | collective-permute-start | bytes 245768 | tf_op jit(solution)/shard_map/ppermute | solution.py:91
  24.6 0.8 %near.3 = bf16[768,512]{1,0:T(8,128)(2,1)S(1)} custom-call(bf16[224,512]{1,0:T(8,128)(2,1)S(1)} %rows_to_y.1.refs_0_, bf16[80,512]{1,0:T(8,128)(2,1)S(1)} %rest_to_x.1.refs_1_, bf16[64,512]{1,0:T(8,128)(2,1)S(1)} %get-tuple-element.15.refs_0_.refs_2_, bf16[192,512]{1,0:T(8,128)(2,1)S(1)} %stack.1.refs_1_.refs_3_, ...), custom_call_target="tpu_custom_call" | custom-call | tf_op jit(solution)/shard_map/near/pallas_call | solution.py:451
  25.4 0.1 collective-permute-start.10
  25.5 3.0 %collective-permute-done.12.below_ref = bf16[80,512]{1,0:T(8,128)(2,1)S(1)} collective-permute-done((bf16[80,512]{1,0:T(8,128)(2,1)S(1)}, bf16[80,512]{1,0:T(8,128)(2,1)S(1)}, u32[]{:S(2)}, u32[]{:S(2)}) %collective-permute-start.12) | collective-permute-done | bytes 81952 | tf_op jit(solution)/shard_map/ppermute | solution.py:91
  28.5 0.7 %collective-permute-done.11.above_ref = bf16[224,512]{1,0:T(8,128)(2,1)S(1)} collective-permute-done((bf16[224,512]{1,0:T(8,128)(2,1)S(1)}, bf16[224,512]{1,0:T(8,128)(2,1)S(1)}, u32[]{:S(2)}, u32[]{:S(2)}) %collective-permute-start.11) | collective-permute-done | bytes 229408 | tf_op jit(solution)/shard_map/ppermute | solution.py:91
  29.2 0.1 collective-permute-start.13
  29.3 0.8 %near.2 = (f32[768,512]{1,0:T(8,128)S(1)}, bf16[2,512,512]{2,1,0:T(8,128)(2,1)S(1)}) custom-call(bf16[64,512]{1,0:T(8,128)(2,1)S(1)} %get-tuple-element.15.refs_0_.refs_2_, bf16[192,512]{1,0:T(8,128)(2,1)S(1)} %stack.1.refs_1_.refs_3_, bf16[64,896]{1,0:T(8,128)(2,1)S(1)} %collective-permute-done.3.from_x_ref.refs_2_.refs_4_, ...), custom_call_target="tpu_custom_call" | custom-call | flops 10000000000 | tf_op jit(solution)/shard_map/near/pallas_call | solution.py:451
  30.1 0.0 collective-permute-done.10.other_ref
  30.1 1.1 %middle.1.near_ref = f32[768,512]{1,0:T(8,128)S(1)} custom-call(f32[768,512]{1,0:T(8,128)S(1)} %get-tuple-element.23.own_ref, bf16[768,512]{1,0:T(8,128)(2,1)S(1)} %collective-permute-done.10.other_ref, bf16[2,512,512]{2,1,0:T(8,128)(2,1)S(1)} %get-tuple-element.24.turned_ref), custom_call_target="tpu_custom_call" | custom-call | tf_op jit(solution)/shard_map/middle/pallas_call | solution.py:476
  31.2 2.4 %final.1 = f32[768,512]{1,0:T(8,128)} custom-call(f32[768,512]{1,0:T(8,128)S(1)} %middle.1.near_ref, bf16[304,512]{1,0:T(8,128)(2,1)S(1)} %join.1.own_ref, bf16[304,512]{1,0:T(8,128)(2,1)S(1)} %collective-permute-done.13.other_ref, bf16[2,512,512]{2,1,0:T(8,128)(2,1)S(1)} %get-tuple-element.24.turned_ref), custom_call_target="tpu_custom_call" | custom-call | tf_op jit(solution)/shard_map/final/pallas_call | solution.py:484
  (8 shorter events, 0.1 us)
Async XLA Ops:
  1.6 10.0 %collective-permute-start = (bf16[64,512]{1,0:T(8,128)(2,1)S(1)}, bf16[64,512]{1,0:T(8,128)(2,1)S(1)}, u32[]{:S(2)}, u32[]{:S(2)}) collective-permute-start(bf16[64,512]{1,0:T(8,128)(2,1)S(1)} %get-tuple-element.15.refs_0_.refs_2_), channel_id=1, source_target_pairs={{0,8},{1,9},{2,10},{3,11},{4,12},{5,13},{6,14},{7,15},{8,16},{9,17... | collective-permute-start | bytes 196616 | tf_op jit(solution)/shard_map/ppermute | solution.py:91
  4.7 7.1 %collective-permute-start.1 = (bf16[64,512]{1,0:T(8,128)(2,1)S(1)}, bf16[64,512]{1,0:T(8,128)(2,1)S(1)}, u32[]{:S(2)}, u32[]{:S(2)}) collective-permute-start(bf16[64,512]{1,0:T(8,128)(2,1)S(1)} %get-tuple-element.15.refs_0_.refs_2_), channel_id=1, source_target_pairs={{0,16},{1,17},{2,18},{3,19},{4,20},{5,21},{6,22},{7,23},{8,24},{9,... | collective-permute-start | bytes 196616 | tf_op jit(solution)/shard_map/ppermute | solution.py:91
  7.2 4.7 %collective-permute-start.2 = (bf16[64,512]{1,0:T(8,128)(2,1)S(1)}, bf16[64,512]{1,0:T(8,128)(2,1)S(1)}, u32[]{:S(2)}, u32[]{:S(2)}) collective-permute-start(bf16[64,512]{1,0:T(8,128)(2,1)S(1)} %get-tuple-element.15.refs_0_.refs_2_), channel_id=1, source_target_pairs={{0,24},{1,25},{2,26},{3,27},{4,28},{5,29},{6,30},{7,31},{8,0},{9,1... | collective-permute-start | bytes 196616 | tf_op jit(solution)/shard_map/ppermute | solution.py:91
  8.6 6.5 %collective-permute-start.3 = (bf16[64,896]{1,0:T(8,128)(2,1)S(1)}, bf16[64,896]{1,0:T(8,128)(2,1)S(1)}, u32[]{:S(2)}, u32[]{:S(2)}) collective-permute-start(bf16[64,896]{1,0:T(8,128)(2,1)S(1)} %get-tuple-element.16), channel_id=1, source_target_pairs={{0,1},{1,0},{2,3},{3,2},{4,5},{5,4},{6,7},{7,6},{8,9},{9,8},{10,11... | collective-permute-start | bytes 344072 | tf_op jit(solution)/shard_map/ppermute | solution.py:91
  10.1 5.6 %collective-permute-start.5 = (bf16[64,1152]{1,0:T(8,128)(2,1)S(1)}, bf16[64,1152]{1,0:T(8,128)(2,1)S(1)}, u32[]{:S(2)}, u32[]{:S(2)}) collective-permute-start(bf16[64,1152]{1,0:T(8,128)(2,1)S(1)} %get-tuple-element.17), channel_id=1, source_target_pairs={{0,2},{1,3},{2,0},{3,1},{4,6},{5,7},{6,4},{7,5},{8,10},{9,11},{10,... | collective-permute-start | bytes 442376 | tf_op jit(solution)/shard_map/ppermute | solution.py:91
  12.0 11.1 %collective-permute-start.4 = (bf16[192,512]{1,0:T(8,128)(2,1)S(1)}, bf16[192,512]{1,0:T(8,128)(2,1)S(1)}, u32[]{:S(2)}, u32[]{:S(2)}) collective-permute-start(bf16[192,512]{1,0:T(8,128)(2,1)S(1)} %stack.1.refs_1_.refs_3_), channel_id=1, source_target_pairs={{0,1},{1,0},{2,3},{3,2},{4,5},{5,4},{6,7},{7,6},{8,9},{9,8},{10,11... | collective-permute-start | bytes 589832 | tf_op jit(solution)/shard_map/ppermute | solution.py:91
  13.6 10.3 %collective-permute-start.6 = (bf16[192,512]{1,0:T(8,128)(2,1)S(1)}, bf16[192,512]{1,0:T(8,128)(2,1)S(1)}, u32[]{:S(2)}, u32[]{:S(2)}) collective-permute-start(bf16[192,512]{1,0:T(8,128)(2,1)S(1)} %stack.1.refs_1_.refs_3_), channel_id=1, source_target_pairs={{0,2},{1,3},{2,0},{3,1},{4,6},{5,7},{6,4},{7,5},{8,10},{9,11},{10,... | collective-permute-start | bytes 589832 | tf_op jit(solution)/shard_map/ppermute | solution.py:91
  15.9 5.9 %collective-permute-start.7 = (bf16[80,256]{1,0:T(8,128)(2,1)S(1)}, bf16[80,256]{1,0:T(8,128)(2,1)S(1)}, u32[]{:S(2)}, u32[]{:S(2)}) collective-permute-start(bf16[80,256]{1,0:T(8,128)(2,1)S(1)} %get-tuple-element.20), channel_id=1, source_target_pairs={{0,8},{1,9},{2,10},{3,11},{4,12},{5,13},{6,14},{7,15},{8,16},{9,17... | collective-permute-start | bytes 122888 | tf_op jit(solution)/shard_map/ppermute | solution.py:91
  16.8 5.8 %collective-permute-start.8 = (bf16[80,256]{1,0:T(8,128)(2,1)S(1)}, bf16[80,256]{1,0:T(8,128)(2,1)S(1)}, u32[]{:S(2)}, u32[]{:S(2)}) collective-permute-start(bf16[80,256]{1,0:T(8,128)(2,1)S(1)} %get-tuple-element.21), channel_id=1, source_target_pairs={{0,16},{1,17},{2,18},{3,19},{4,20},{5,21},{6,22},{7,23},{8,24},{9,... | collective-permute-start | bytes 122888 | tf_op jit(solution)/shard_map/ppermute | solution.py:91
  18.9 4.2 %collective-permute-start.9 = (bf16[80,256]{1,0:T(8,128)(2,1)S(1)}, bf16[80,256]{1,0:T(8,128)(2,1)S(1)}, u32[]{:S(2)}, u32[]{:S(2)}) collective-permute-start(bf16[80,256]{1,0:T(8,128)(2,1)S(1)} %get-tuple-element.22), channel_id=1, source_target_pairs={{0,24},{1,25},{2,26},{3,27},{4,28},{5,29},{6,30},{7,31},{8,0},{9,1... | collective-permute-start | bytes 122888 | tf_op jit(solution)/shard_map/ppermute | solution.py:91
  23.1 6.1 %collective-permute-start.11 = (bf16[224,512]{1,0:T(8,128)(2,1)S(1)}, bf16[224,512]{1,0:T(8,128)(2,1)S(1)}, u32[]{:S(2)}, u32[]{:S(2)}) collective-permute-start(bf16[224,512]{1,0:T(8,128)(2,1)S(1)} %rows_to_y.1.refs_0_), channel_id=1, source_target_pairs={{0,2},{1,3},{2,0},{3,1},{4,6},{5,7},{6,4},{7,5},{8,10},{9,11},{10,... | collective-permute-start | bytes 688136 | tf_op jit(solution)/shard_map/ppermute | solution.py:91
  23.9 5.4 %copy-start = (f32[512,512]{1,0:T(8,128)S(1)}, f32[512,512]{1,0:T(8,128)}, u32[]{:S(2)}) copy-start(f32[512,512]{1,0:T(8,128)} %refs_10_.1) | copy-start | bytes 3145732
  24.0 4.5 %collective-permute-start.12 = (bf16[80,512]{1,0:T(8,128)(2,1)S(1)}, bf16[80,512]{1,0:T(8,128)(2,1)S(1)}, u32[]{:S(2)}, u32[]{:S(2)}) collective-permute-start(bf16[80,512]{1,0:T(8,128)(2,1)S(1)} %rest_to_x.1.refs_1_), channel_id=1, source_target_pairs={{0,1},{1,0},{2,3},{3,2},{4,5},{5,4},{6,7},{7,6},{8,9},{9,8},{10,11... | collective-permute-start | bytes 245768 | tf_op jit(solution)/shard_map/ppermute | solution.py:91
  25.4 4.7 %collective-permute-start.10 = (bf16[768,512]{1,0:T(8,128)(2,1)S(1)}, bf16[768,512]{1,0:T(8,128)(2,1)S(1)}, u32[]{:S(2)}, u32[]{:S(2)}) collective-permute-start(bf16[768,512]{1,0:T(8,128)(2,1)S(1)} %near.3), channel_id=1, source_target_pairs={{0,4},{1,5},{2,6},{3,7},{4,0},{5,1},{6,2},{7,3},{8,12},{9,13},{10,... | collective-permute-start | bytes 2359304 | tf_op jit(solution)/shard_map/ppermute | solution.py:91
  29.2 2.0 %collective-permute-start.13 = (bf16[304,512]{1,0:T(8,128)(2,1)S(1)}, bf16[304,512]{1,0:T(8,128)(2,1)S(1)}, u32[]{:S(2)}, u32[]{:S(2)}) collective-permute-start(bf16[304,512]{1,0:T(8,128)(2,1)S(1)} %join.1.own_ref), channel_id=1, source_target_pairs={{0,4},{1,5},{2,6},{3,7},{4,0},{5,1},{6,2},{7,3},{8,12},{9,13},{10,... | collective-permute-start | bytes 933896 | tf_op jit(solution)/shard_map/ppermute | solution.py:91

commit v15 on v14

--- a/solution.py
+++ b/solution.py
@@ -216,8 +216,7 @@
         out[rows:, :wide] = block
 
 
-def rows_to_y_kernel(from_x_ref, by_x_ref, *refs):
-    out_ref = refs[-1]
+def rows_to_y_kernel(from_x_ref, by_x_ref, out_ref):
     rows = from_x_ref.shape[0]
     out_ref[:rows, :] = from_x_ref[:, : out_ref.shape[1]]
     out_ref[rows:, :] = by_x_ref[: out_ref.shape[0] - rows, :]
@@ -259,9 +258,9 @@
 
 def inverse_rows(rows_ref, factor_ref, high_ref, low_ref):
     f32, bf16 = jnp.float32, jnp.bfloat16
-    width = rows_ref.shape[1]
+    height, width = high_ref.shape
     for start, stop in ((0, width // 2), (width // 2, width)):
-        rows = rows_ref[:, :stop]
+        rows = rows_ref[:height, :stop]
         total = jnp.dot(rows, factor_ref[0, :stop, start:stop], preferred_element_type=f32)
         total += jnp.dot(rows, factor_ref[1, :stop, start:stop], preferred_element_type=f32)
         high = total.astype(bf16)
@@ -269,21 +268,13 @@
         low_ref[:, start:stop] = (total - high.astype(f32)).astype(bf16)
 
 
-def near_kernel(sizes, u, earlier, *refs):
+def near_kernel(sizes, earlier, *refs):
     layers, owners, per_owner, block_count, block_rows = sizes
     refs = refs[earlier:]
     inputs = 2 * (owners - 1) + layers
     panels, posts = refs[: 2 * (owners - 1)], refs[2 * (owners - 1) : inputs]
-    factors, (placed_ref, rows_ref) = refs[inputs:-2], refs[-2:]
+    factor_ref, own_ref, other_ref, turned_ref, placed_ref, rows_ref = refs[inputs:]
     f32, bf16 = jnp.float32, jnp.bfloat16
-    if u == 0:
-        factor_ref, out_ref, turned_ref = factors
-        turned = factor_ref[...].T
-        high = turned.astype(bf16)
-        turned_ref[0, :, :] = high
-        turned_ref[1, :, :] = (turned - high.astype(f32)).astype(bf16)
-    else:
-        (out_ref,) = factors
     rows = block_count * block_rows
     group, wide = CAP * block_rows, CAP * rows
     part = rows // 2
@@ -292,15 +283,20 @@
     for panel in panels:
         rows_ref[at : at + panel.shape[0], :] = panel[:, :width]
         at += panel.shape[0]
-    for e in range(owners - 1):
-        for h in range(layers // 2):
-            pair = posts[2 * h : 2 * h + 2]
-            pieces = [post[u * part : (u + 1) * part, e * group : (e + 1) * group] for post in pair]
-            notes = [row_of(post[rows:, :wide], e) for post in pair]
-            start = (e * layers + 2 * h) * rows
-            place(placed_ref, slice(start, start + 2 * rows), per_owner, pieces, notes, (block_count, block_rows))
-    gram = jnp.dot(placed_ref[...], rows_ref[...], preferred_element_type=f32)
-    out_ref[...] = gram.astype(out_ref.dtype)
+    for u, out_ref in ((1, other_ref), (0, own_ref)):
+        for e in range(owners - 1):
+            for h in range(layers // 2):
+                pair = posts[2 * h : 2 * h + 2]
+                pieces = [post[u * part : (u + 1) * part, e * group : (e + 1) * group] for post in pair]
+                notes = [row_of(post[rows:, :wide], e) for post in pair]
+                start = (e * layers + 2 * h) * rows
+                place(placed_ref, slice(start, start + 2 * rows), per_owner, pieces, notes, (block_count, block_rows))
+        gram = jnp.dot(placed_ref[...], rows_ref[...], preferred_element_type=f32)
+        out_ref[...] = gram.astype(out_ref.dtype)
+    turned = factor_ref[...].T
+    high = turned.astype(bf16)
+    turned_ref[0, :, :] = high
+    turned_ref[1, :, :] = (turned - high.astype(f32)).astype(bf16)
 
 
 def join_kernel(above_ref, below_ref, out_ref):
@@ -309,9 +305,27 @@
     out_ref[rows:, :] = below_ref[...]
 
 
-def middle_kernel(own_ref, other_ref, turned_ref, out_ref):
+def place_far(sizes, u, ref, placed_ref):
+    layers, owners, per_owner, block_count, block_rows = sizes
+    rows = block_count * block_rows
+    group, wide = CAP * block_rows, CAP * rows
+    part, depth = rows // 2, layers * rows
+    for h in range(layers // 2):
+        pieces, notes = [], []
+        for k in (2 * h, 2 * h + 1):
+            at = (u * layers + k) * group
+            pieces.append(ref[depth : depth + part, at : at + group])
+            notes.append(row_of(ref[depth + part :, :wide], k))
+        lanes = slice(2 * h * rows, 2 * (h + 1) * rows)
+        place(placed_ref, lanes, per_owner, pieces, notes, (block_count, block_rows))
+
+
+def middle_kernel(sizes, own_ref, other_ref, joined_ref, turned_ref, out_ref, placed_ref, high_ref, low_ref):
     f32, bf16 = jnp.float32, jnp.bfloat16
     width = own_ref.shape[1]
+    place_far(sizes, 0, joined_ref, placed_ref)
+    inverse_rows(joined_ref, turned_ref, high_ref, low_ref)
+    placed = placed_ref[...]
     gram = own_ref[...] + other_ref[...].astype(f32)
     high = gram.astype(bf16)
     low = (gram - high.astype(f32)).astype(bf16)
@@ -319,34 +333,22 @@
         a, b = turned_ref[0, :stop, start:stop], turned_ref[1, :stop, start:stop]
         total = jnp.dot(high[:, :stop], a, preferred_element_type=f32)
         total += jnp.dot(high[:, :stop], b, preferred_element_type=f32)
-        out_ref[:, start:stop] = total + jnp.dot(low[:, :stop], a, preferred_element_type=f32)
-
-
-def final_kernel(sizes, near_ref, own_ref, other_ref, turned_ref, out_hbm, *refs):
-    layers, owners, per_owner, block_count, block_rows = sizes
-    sum_ref, placed_ref, rows_ref, high_ref, low_ref, sems = refs
+        total += jnp.dot(low[:, :stop], a, preferred_element_type=f32)
+        total += jnp.dot(placed, high_ref[:, start:stop], preferred_element_type=f32)
+        out_ref[:, start:stop] = total + jnp.dot(placed, low_ref[:, start:stop], preferred_element_type=f32)
+
+
+def final_kernel(sizes, middle_ref, joined_ref, turned_ref, out_hbm, sum_ref, placed_ref, high_ref, low_ref, sems):
     f32 = jnp.float32
-    rows = block_count * block_rows
-    group, wide = CAP * block_rows, CAP * rows
-    part, depth = rows // 2, layers * rows
-    for u, ref in enumerate((own_ref, other_ref)):
-        rows_ref[u * depth : (u + 1) * depth, :] = ref[:depth, :]
-        for h in range(layers // 2):
-            pieces, notes = [], []
-            for k in (2 * h, 2 * h + 1):
-                at = (u * layers + k) * group
-                pieces.append(ref[depth : depth + part, at : at + group])
-                notes.append(row_of(ref[depth + part :, :wide], k))
-            start = u * depth + 2 * h * rows
-            place(placed_ref, slice(start, start + 2 * rows), per_owner, pieces, notes, (block_count, block_rows))
-    inverse_rows(rows_ref, turned_ref, high_ref, low_ref)
+    place_far(sizes, 1, joined_ref, placed_ref)
+    inverse_rows(joined_ref, turned_ref, high_ref, low_ref)
     strips = sems.shape[0]
     height = sum_ref.shape[0] // strips
     copies = []
     for i in range(strips):
         here = pl.ds(i * height, height)
         placed = placed_ref[here, :]
-        total = near_ref[here, :] + jnp.dot(placed, high_ref[...], preferred_element_type=f32)
+        total = middle_ref[here, :] + jnp.dot(placed, high_ref[...], preferred_element_type=f32)
         sum_ref[here, :] = total + jnp.dot(placed, low_ref[...], preferred_element_type=f32)
         copies.append(pltpu.make_async_copy(sum_ref.at[here, :], out_hbm.at[here, :], sems.at[i]))
         copies[-1].start()
@@ -426,11 +428,11 @@
     rows_to_y = pl.pallas_call(
         rows_to_y_kernel,
         out_shape=shaped((rows + others.shape[0] - last, panel_width), bf16),
-        in_specs=[vmem] * 2 + [anywhere] * (layers - 1),
+        in_specs=[vmem] * 2,
         out_specs=vmem,
         compiler_params=params,
         name="rows_to_y",
-    )(from_x, by_x, *posts[1:])
+    )(from_x, by_x)
     across_y = shift(rows_to_y, 0, 2)
     rest_to_x = pl.pallas_call(
         functools.partial(rest_to_x_kernel, (layers, lane_group, wide)),
@@ -438,6 +440,7 @@
         in_specs=[vmem] * (layers + 1),
         out_specs=vmem,
         compiler_params=params,
+        cost_estimate=lasting(3 * 10**9),
         name="rest_to_x",
     )(by_y, *posts)
     across_x = shift(rest_to_x, 0, 1)
@@ -447,51 +450,49 @@
     sizes = (layers, owners, per_owner, block_count, block_rows)
     result = shaped((count, panel_width), f32)
     panels = [weighted, others, from_x, by_x, from_y, by_y]
-    def near(u, out_shape, earlier, *factors):
-        return pl.pallas_call(
-            functools.partial(near_kernel, sizes, u, len(earlier)),
-            out_shape=out_shape,
-            in_specs=[anywhere] * len(earlier) + [vmem] * (len(panels) + layers + len(factors)),
-            out_specs=[vmem] * len(out_shape),
-            scratch_shapes=[
-                pltpu.VMEM((count, (owners - 1) * depth), bf16),
-                pltpu.VMEM(((owners - 1) * depth, panel_width), bf16),
-            ],
-            compiler_params=params,
-            cost_estimate=lasting(0 if u else 10**10),
-            name="near",
-        )(*earlier, *panels, *posts, *factors)
-
-    other = shift(*near(1, [shaped((count, panel_width), bf16)], [rows_to_y, rest_to_x]), 0, 0, 1)
-    own, turned = near(0, [result, shaped((2, *factor_inverse.shape), bf16)], [], factor_inverse)
+    own, other, turned = pl.pallas_call(
+        functools.partial(near_kernel, sizes, 2),
+        out_shape=[result, shaped((count, panel_width), bf16), shaped((2, *factor_inverse.shape), bf16)],
+        in_specs=[anywhere] * 2 + [vmem] * (len(panels) + layers + 1),
+        out_specs=[vmem] * 3,
+        scratch_shapes=[
+            pltpu.VMEM((count, (owners - 1) * depth), bf16),
+            pltpu.VMEM(((owners - 1) * depth, panel_width), bf16),
+        ],
+        compiler_params=params,
+        cost_estimate=lasting(10**9),
+        name="near",
+    )(rows_to_y, rest_to_x, *panels, *posts, factor_inverse)
+    other = shift(other, 0, 0, 1)
     joined = pl.pallas_call(
         join_kernel,
         out_shape=shaped((across_y.shape[0] + across_x.shape[0], panel_width), bf16),
         in_specs=[vmem] * 2,
         out_specs=vmem,
         compiler_params=params,
+        cost_estimate=lasting(10**10),
         name="join",
     )(across_y, across_x)
     other_joined = shift(joined, 0, 0, 1)
+    far_scratch = [pltpu.VMEM((count, depth), bf16)] + [pltpu.VMEM((depth, panel_width), bf16)] * 2
     middle = pl.pallas_call(
-        middle_kernel,
+        functools.partial(middle_kernel, sizes),
         out_shape=result,
-        in_specs=[vmem] * 3,
+        in_specs=[vmem] * 4,
         out_specs=vmem,
+        scratch_shapes=far_scratch,
         compiler_params=params,
         name="middle",
-    )(own, other, turned)
+    )(own, other, joined, turned)
     out = pl.pallas_call(
         functools.partial(final_kernel, sizes),
         out_shape=result,
-        in_specs=[vmem] * 4,
+        in_specs=[vmem] * 3,
         out_specs=anywhere,
-        scratch_shapes=[pltpu.VMEM((count, panel_width), f32), pltpu.VMEM((count, 2 * depth), bf16)]
-        + [pltpu.VMEM((2 * depth, panel_width), bf16)] * 3
-        + [pltpu.SemaphoreType.DMA((4,))],
+        scratch_shapes=[pltpu.VMEM((count, panel_width), f32)] + far_scratch + [pltpu.SemaphoreType.DMA((4,))],
         compiler_params=params,
         name="final",
-    )(middle, joined, other_joined, turned)
+    )(middle, other_joined, turned)
     return out.reshape(per_owner, slab_width, panel_width)
 
 

time: 33.8 us -> 31.6 us (0.935)
  waiting for transfers between devices: 7.92 us -> 4.15 us
  starting transfers between devices: 18.6 us -> 19.9 us
  local copies, waits for them, and re-layouts: 0.01 us -> 0.47 us
    ppermute x14, waiting for transfers between devices: 7.92 us -> 4.15 us  [shift(): return lax.ppermute(value, ('rows', 'cols'), pairs)]
    ppermute x14, starting transfers between devices: 18.6 us -> 19.9 us  [shift(): return lax.ppermute(value, ('rows', 'cols'), pairs)]
    pallas_call x1, Pallas kernels: 2.4 us -> 1.86 us  [local(): pl.pallas_call(functools.partial(final_kernel, sizes), out_shape=result,...]
    unnamed x2, local copies, waits for them, and re-layouts: 0.01 us -> 0.47 us
    pallas_call x3 -> x2, Pallas kernels: 2.77 us -> 3.15 us  [the longest x1 1.7 us: local(): pl.pallas_call(functools.partial(middle_kernel, sizes), out_shape=result,...]
  transfers between devices with their start and end apart: 14 -> 14, of which waited for: 8 -> 6; matrix products, arithmetic and copies ran while one was open for 0% -> 0% of each run, Pallas kernels for 9% -> 11%
where the time goes in v15:
time: 31.6 us; the launch traced here: 31.5 us
  starting transfers between devices  19.9 us (63%)
  Pallas kernels  6.84 us (22%)
  waiting for transfers between devices  4.15 us (13%)
  local copies, waits for them, and re-layouts  0.47 us (1%)
    ppermute x14, starting transfers between devices, shift(): return lax.ppermute(value, ('rows', 'cols'), pairs)  19.9 us
    ppermute x14, waiting for transfers between devices, shift(): return lax.ppermute(value, ('rows', 'cols'), pairs)  4.15 us
    pallas_call x1, Pallas kernels, local(): pl.pallas_call(functools.partial(final_kernel, sizes), out_shape=result,...  1.86 us
    pallas_call x1, Pallas kernels, local(): pl.pallas_call(functools.partial(middle_kernel, sizes), out_shape=result,...  1.7 us
    pallas_call x1, Pallas kernels, local(): pl.pallas_call(functools.partial(pack_kernel, sizes), out_shape=[shaped((...  1.57 us
    pallas_call x1, Pallas kernels, local(): pl.pallas_call(functools.partial(near_kernel, sizes, 2), out_shape=[resul...  1.45 us
  transfers between devices with their start and end apart: 14, of which 6 were waited for; matrix products, arithmetic and copies ran while one was open for 0% of the time, Pallas kernels for 11%

profile of v15, /device:TPU:0, one launch (start us, length us, event | category | flops | bytes accessed | tf_op | source)
XLA Modules:
  0.0 31.5 jit_solution(2371153391325000063)
XLA Ops:
  0.0 1.6 %pack.1 = (bf16[64,512]{1,0:T(8,128)(2,1)S(1)}, bf16[64,384]{1,0:T(8,128)(2,1)S(1)}, bf16[64,896]{1,0:T(8,128)(2,1)S(1)}, bf16[64,1152]{1,0:T(8,128)(2,1)S(1)}) custom-call(s32[2,4]{1,0:T(2,128)} %lists_hbm.1, s32[2,4]{1,0:T(2,128)} %masks_hbm.1, s32[96]{0:T(128)} %order_hbm.1, f32[1,64]{1,0:T(1,128)} %bitcast.2, bf16[64,512]{1,0:T(8,128)(2,1)} %panel_hbm.1, ...), custom_call_target="tpu_custom_call" | custom-call | tf_op jit(solution)/shard_map/pack/pallas_call | solution.py:380
  1.6 3.1 %collective-permute-start.1 = (bf16[64,512]{1,0:T(8,128)(2,1)S(1)}, bf16[64,512]{1,0:T(8,128)(2,1)S(1)}, u32[]{:S(2)}, u32[]{:S(2)}) collective-permute-start(bf16[64,512]{1,0:T(8,128)(2,1)S(1)} %get-tuple-element.17.refs_2_), channel_id=1, source_target_pairs={{0,8},{1,9},{2,10},{3,11},{4,12},{5,13},{6,14},{7,15},{8,16},{9,17... | collective-permute-start | bytes 196616 | tf_op jit(solution)/shard_map/ppermute | solution.py:91
  4.7 2.6 %collective-permute-start.2 = (bf16[64,512]{1,0:T(8,128)(2,1)S(1)}, bf16[64,512]{1,0:T(8,128)(2,1)S(1)}, u32[]{:S(2)}, u32[]{:S(2)}) collective-permute-start(bf16[64,512]{1,0:T(8,128)(2,1)S(1)} %get-tuple-element.17.refs_2_), channel_id=1, source_target_pairs={{0,16},{1,17},{2,18},{3,19},{4,20},{5,21},{6,22},{7,23},{8,24},{9,... | collective-permute-start | bytes 196616 | tf_op jit(solution)/shard_map/ppermute | solution.py:91
  7.2 1.3 %collective-permute-start.3 = (bf16[64,512]{1,0:T(8,128)(2,1)S(1)}, bf16[64,512]{1,0:T(8,128)(2,1)S(1)}, u32[]{:S(2)}, u32[]{:S(2)}) collective-permute-start(bf16[64,512]{1,0:T(8,128)(2,1)S(1)} %get-tuple-element.17.refs_2_), channel_id=1, source_target_pairs={{0,24},{1,25},{2,26},{3,27},{4,28},{5,29},{6,30},{7,31},{8,0},{9,1... | collective-permute-start | bytes 196616 | tf_op jit(solution)/shard_map/ppermute | solution.py:91
  8.6 1.5 %collective-permute-start = (bf16[64,896]{1,0:T(8,128)(2,1)S(1)}, bf16[64,896]{1,0:T(8,128)(2,1)S(1)}, u32[]{:S(2)}, u32[]{:S(2)}) collective-permute-start(bf16[64,896]{1,0:T(8,128)(2,1)S(1)} %get-tuple-element.16), channel_id=1, source_target_pairs={{0,1},{1,0},{2,3},{3,2},{4,5},{5,4},{6,7},{7,6},{8,9},{9,8},{10,11... | collective-permute-start | bytes 344072 | tf_op jit(solution)/shard_map/ppermute | solution.py:91
  10.1 1.5 %collective-permute-start.6 = (bf16[64,1152]{1,0:T(8,128)(2,1)S(1)}, bf16[64,1152]{1,0:T(8,128)(2,1)S(1)}, u32[]{:S(2)}, u32[]{:S(2)}) collective-permute-start(bf16[64,1152]{1,0:T(8,128)(2,1)S(1)} %get-tuple-element.19), channel_id=1, source_target_pairs={{0,2},{1,3},{2,0},{3,1},{4,6},{5,7},{6,4},{7,5},{8,10},{9,11},{10,... | collective-permute-start | bytes 442376 | tf_op jit(solution)/shard_map/ppermute | solution.py:91
  11.6 0.1 collective-permute-done.2.refs_1_
  11.7 0.2 collective-permute-done.3.refs_2_
  12.0 1.6 %collective-permute-start.5 = (bf16[192,512]{1,0:T(8,128)(2,1)S(1)}, bf16[192,512]{1,0:T(8,128)(2,1)S(1)}, u32[]{:S(2)}, u32[]{:S(2)}) collective-permute-start(bf16[192,512]{1,0:T(8,128)(2,1)S(1)} %stack.1.refs_3_), channel_id=1, source_target_pairs={{0,2},{1,3},{2,0},{3,1},{4,6},{5,7},{6,4},{7,5},{8,10},{9,11},{10,... | collective-permute-start | bytes 589832 | tf_op jit(solution)/shard_map/ppermute | solution.py:91
  13.6 1.5 %collective-permute-start.4 = (bf16[192,512]{1,0:T(8,128)(2,1)S(1)}, bf16[192,512]{1,0:T(8,128)(2,1)S(1)}, u32[]{:S(2)}, u32[]{:S(2)}) collective-permute-start(bf16[192,512]{1,0:T(8,128)(2,1)S(1)} %stack.1.refs_3_), channel_id=1, source_target_pairs={{0,1},{1,0},{2,3},{3,2},{4,5},{5,4},{6,7},{7,6},{8,9},{9,8},{10,11... | collective-permute-start | bytes 589832 | tf_op jit(solution)/shard_map/ppermute | solution.py:91
  15.1 0.0 collective-permute-done.from_x_ref.refs_4_
  15.1 1.2 %collective-permute-done.6.from_y_ref.refs_6_ = bf16[64,1152]{1,0:T(8,128)(2,1)S(1)} collective-permute-done((bf16[64,1152]{1,0:T(8,128)(2,1)S(1)}, bf16[64,1152]{1,0:T(8,128)(2,1)S(1)}, u32[]{:S(2)}, u32[]{:S(2)}) %collective-permute-start.6) | collective-permute-done | bytes 147488 | tf_op jit(solution)/shard_map/ppermute | solution.py:91
  16.3 0.1 sort.1
  16.4 0.4 %collective-permute-start.7 = (bf16[80,256]{1,0:T(8,128)(2,1)S(1)}, bf16[80,256]{1,0:T(8,128)(2,1)S(1)}, u32[]{:S(2)}, u32[]{:S(2)}) collective-permute-start(bf16[80,256]{1,0:T(8,128)(2,1)S(1)} %get-tuple-element.21), channel_id=1, source_target_pairs={{0,8},{1,9},{2,10},{3,11},{4,12},{5,13},{6,14},{7,15},{8,16},{9,17... | collective-permute-start | bytes 122888 | tf_op jit(solution)/shard_map/ppermute | solution.py:91
  16.8 2.0 %collective-permute-start.8 = (bf16[80,256]{1,0:T(8,128)(2,1)S(1)}, bf16[80,256]{1,0:T(8,128)(2,1)S(1)}, u32[]{:S(2)}, u32[]{:S(2)}) collective-permute-start(bf16[80,256]{1,0:T(8,128)(2,1)S(1)} %get-tuple-element.22), channel_id=1, source_target_pairs={{0,16},{1,17},{2,18},{3,19},{4,20},{5,21},{6,22},{7,23},{8,24},{9,... | collective-permute-start | bytes 122888 | tf_op jit(solution)/shard_map/ppermute | solution.py:91
  18.9 1.4 %collective-permute-start.9 = (bf16[80,256]{1,0:T(8,128)(2,1)S(1)}, bf16[80,256]{1,0:T(8,128)(2,1)S(1)}, u32[]{:S(2)}, u32[]{:S(2)}) collective-permute-start(bf16[80,256]{1,0:T(8,128)(2,1)S(1)} %get-tuple-element.23), channel_id=1, source_target_pairs={{0,24},{1,25},{2,26},{3,27},{4,28},{5,29},{6,30},{7,31},{8,0},{9,1... | collective-permute-start | bytes 122888 | tf_op jit(solution)/shard_map/ppermute | solution.py:91
  20.3 2.1 %collective-permute-start.11 = (bf16[224,512]{1,0:T(8,128)(2,1)S(1)}, bf16[224,512]{1,0:T(8,128)(2,1)S(1)}, u32[]{:S(2)}, u32[]{:S(2)}) collective-permute-start(bf16[224,512]{1,0:T(8,128)(2,1)S(1)} %rows_to_y.1.refs_0_), channel_id=1, source_target_pairs={{0,2},{1,3},{2,0},{3,1},{4,6},{5,7},{6,4},{7,5},{8,10},{9,11},{10,... | collective-permute-start | bytes 688136 | tf_op jit(solution)/shard_map/ppermute | solution.py:91
  22.4 0.0 collective-permute-done.7.refs_1_.refs_9_
  22.4 0.0 collective-permute-done.8.refs_2_.refs_10_
  22.4 0.4 %collective-permute-done.9.refs_3_.refs_11_ = bf16[80,256]{1,0:T(8,128)(2,1)S(1)} collective-permute-done((bf16[80,256]{1,0:T(8,128)(2,1)S(1)}, bf16[80,256]{1,0:T(8,128)(2,1)S(1)}, u32[]{:S(2)}, u32[]{:S(2)}) %collective-permute-start.9) | collective-permute-done | bytes 40992 | tf_op jit(solution)/shard_map/ppermute | solution.py:91
  22.9 0.0 collective-permute-done.5.by_y_ref.refs_7_
  22.9 0.1 rest_to_x.1.refs_1_
  22.9 0.7 %collective-permute-start.12 = (bf16[80,512]{1,0:T(8,128)(2,1)S(1)}, bf16[80,512]{1,0:T(8,128)(2,1)S(1)}, u32[]{:S(2)}, u32[]{:S(2)}) collective-permute-start(bf16[80,512]{1,0:T(8,128)(2,1)S(1)} %rest_to_x.1.refs_1_), channel_id=1, source_target_pairs={{0,1},{1,0},{2,3},{3,2},{4,5},{5,4},{6,7},{7,6},{8,9},{9,8},{10,11... | collective-permute-start | bytes 245768 | tf_op jit(solution)/shard_map/ppermute | solution.py:91
  23.6 0.5 %copy-done = f32[512,512]{1,0:T(8,128)S(1)} copy-done((f32[512,512]{1,0:T(8,128)S(1)}, f32[512,512]{1,0:T(8,128)}, u32[]{:S(2)}) %copy-start) | copy-done | bytes 1048600
  24.1 1.5 %near.1 = (f32[768,512]{1,0:T(8,128)S(1)}, bf16[768,512]{1,0:T(8,128)(2,1)S(1)}, bf16[2,512,512]{2,1,0:T(8,128)(2,1)S(1)}) custom-call(bf16[224,512]{1,0:T(8,128)(2,1)S(1)} %rows_to_y.1.refs_0_, bf16[80,512]{1,0:T(8,128)(2,1)S(1)} %rest_to_x.1.refs_1_, bf16[64,512]{1,0:T(8,128)(2,1)S(1)} %get-tuple-element.17.refs_2_, bf16[192,512]{1,0:T(8,128)(2,1)S(1)} %stack.1.refs_3_, ...), custom_call_target="tpu_custom_call" | custom-call | flops 1000000000 | tf_op jit(solution)/shard_map/near/pallas_call | solution.py:453
  25.5 0.1 collective-permute-start.10
  25.6 1.8 %collective-permute-done.12.below_ref = bf16[80,512]{1,0:T(8,128)(2,1)S(1)} collective-permute-done((bf16[80,512]{1,0:T(8,128)(2,1)S(1)}, bf16[80,512]{1,0:T(8,128)(2,1)S(1)}, u32[]{:S(2)}, u32[]{:S(2)}) %collective-permute-start.12) | collective-permute-done | bytes 81952 | tf_op jit(solution)/shard_map/ppermute | solution.py:91
  27.5 0.0 collective-permute-done.11.above_ref
  27.5 0.1 collective-permute-start.13
  27.6 0.3 %collective-permute-done.10.other_ref = bf16[768,512]{1,0:T(8,128)(2,1)S(1)} collective-permute-done((bf16[768,512]{1,0:T(8,128)(2,1)S(1)}, bf16[768,512]{1,0:T(8,128)(2,1)S(1)}, u32[]{:S(2)}, u32[]{:S(2)}) %collective-permute-start.10) | collective-permute-done | bytes 786464 | tf_op jit(solution)/shard_map/ppermute | solution.py:91
  27.9 1.7 %middle.1.middle_ref = f32[768,512]{1,0:T(8,128)S(1)} custom-call(f32[768,512]{1,0:T(8,128)S(1)} %get-tuple-element.24.own_ref, bf16[768,512]{1,0:T(8,128)(2,1)S(1)} %collective-permute-done.10.other_ref, bf16[304,512]{1,0:T(8,128)(2,1)S(1)} %join.1.joined_ref, bf16[2,512,512]{2,1,0:T(8,128)(2,1)S(1)} %get-tuple-element.26.turned_ref), custom_call_target="tpu_custom_call" | custom-call | tf_op jit(solution)/shard_map/middle/pallas_call | solution.py:478
  29.6 1.9 %final.1 = f32[768,512]{1,0:T(8,128)} custom-call(f32[768,512]{1,0:T(8,128)S(1)} %middle.1.middle_ref, bf16[304,512]{1,0:T(8,128)(2,1)S(1)} %collective-permute-done.13.joined_ref, bf16[2,512,512]{2,1,0:T(8,128)(2,1)S(1)} %get-tuple-element.26.turned_ref), custom_call_target="tpu_custom_call" | custom-call | tf_op jit(solution)/shard_map/final/pallas_call | solution.py:487
  (7 shorter events, 0.1 us)
Async XLA Ops:
  1.6 10.0 %collective-permute-start.1 = (bf16[64,512]{1,0:T(8,128)(2,1)S(1)}, bf16[64,512]{1,0:T(8,128)(2,1)S(1)}, u32[]{:S(2)}, u32[]{:S(2)}) collective-permute-start(bf16[64,512]{1,0:T(8,128)(2,1)S(1)} %get-tuple-element.17.refs_2_), channel_id=1, source_target_pairs={{0,8},{1,9},{2,10},{3,11},{4,12},{5,13},{6,14},{7,15},{8,16},{9,17... | collective-permute-start | bytes 196616 | tf_op jit(solution)/shard_map/ppermute | solution.py:91
  4.7 7.1 %collective-permute-start.2 = (bf16[64,512]{1,0:T(8,128)(2,1)S(1)}, bf16[64,512]{1,0:T(8,128)(2,1)S(1)}, u32[]{:S(2)}, u32[]{:S(2)}) collective-permute-start(bf16[64,512]{1,0:T(8,128)(2,1)S(1)} %get-tuple-element.17.refs_2_), channel_id=1, source_target_pairs={{0,16},{1,17},{2,18},{3,19},{4,20},{5,21},{6,22},{7,23},{8,24},{9,... | collective-permute-start | bytes 196616 | tf_op jit(solution)/shard_map/ppermute | solution.py:91
  7.2 4.7 %collective-permute-start.3 = (bf16[64,512]{1,0:T(8,128)(2,1)S(1)}, bf16[64,512]{1,0:T(8,128)(2,1)S(1)}, u32[]{:S(2)}, u32[]{:S(2)}) collective-permute-start(bf16[64,512]{1,0:T(8,128)(2,1)S(1)} %get-tuple-element.17.refs_2_), channel_id=1, source_target_pairs={{0,24},{1,25},{2,26},{3,27},{4,28},{5,29},{6,30},{7,31},{8,0},{9,1... | collective-permute-start | bytes 196616 | tf_op jit(solution)/shard_map/ppermute | solution.py:91
  8.6 6.5 %collective-permute-start = (bf16[64,896]{1,0:T(8,128)(2,1)S(1)}, bf16[64,896]{1,0:T(8,128)(2,1)S(1)}, u32[]{:S(2)}, u32[]{:S(2)}) collective-permute-start(bf16[64,896]{1,0:T(8,128)(2,1)S(1)} %get-tuple-element.16), channel_id=1, source_target_pairs={{0,1},{1,0},{2,3},{3,2},{4,5},{5,4},{6,7},{7,6},{8,9},{9,8},{10,11... | collective-permute-start | bytes 344072 | tf_op jit(solution)/shard_map/ppermute | solution.py:91
  10.1 6.2 %collective-permute-start.6 = (bf16[64,1152]{1,0:T(8,128)(2,1)S(1)}, bf16[64,1152]{1,0:T(8,128)(2,1)S(1)}, u32[]{:S(2)}, u32[]{:S(2)}) collective-permute-start(bf16[64,1152]{1,0:T(8,128)(2,1)S(1)} %get-tuple-element.19), channel_id=1, source_target_pairs={{0,2},{1,3},{2,0},{3,1},{4,6},{5,7},{6,4},{7,5},{8,10},{9,11},{10,... | collective-permute-start | bytes 442376 | tf_op jit(solution)/shard_map/ppermute | solution.py:91
  12.0 10.9 %collective-permute-start.5 = (bf16[192,512]{1,0:T(8,128)(2,1)S(1)}, bf16[192,512]{1,0:T(8,128)(2,1)S(1)}, u32[]{:S(2)}, u32[]{:S(2)}) collective-permute-start(bf16[192,512]{1,0:T(8,128)(2,1)S(1)} %stack.1.refs_3_), channel_id=1, source_target_pairs={{0,2},{1,3},{2,0},{3,1},{4,6},{5,7},{6,4},{7,5},{8,10},{9,11},{10,... | collective-permute-start | bytes 589832 | tf_op jit(solution)/shard_map/ppermute | solution.py:91
  13.6 6.7 %collective-permute-start.4 = (bf16[192,512]{1,0:T(8,128)(2,1)S(1)}, bf16[192,512]{1,0:T(8,128)(2,1)S(1)}, u32[]{:S(2)}, u32[]{:S(2)}) collective-permute-start(bf16[192,512]{1,0:T(8,128)(2,1)S(1)} %stack.1.refs_3_), channel_id=1, source_target_pairs={{0,1},{1,0},{2,3},{3,2},{4,5},{5,4},{6,7},{7,6},{8,9},{9,8},{10,11... | collective-permute-start | bytes 589832 | tf_op jit(solution)/shard_map/ppermute | solution.py:91
  16.4 6.0 %collective-permute-start.7 = (bf16[80,256]{1,0:T(8,128)(2,1)S(1)}, bf16[80,256]{1,0:T(8,128)(2,1)S(1)}, u32[]{:S(2)}, u32[]{:S(2)}) collective-permute-start(bf16[80,256]{1,0:T(8,128)(2,1)S(1)} %get-tuple-element.21), channel_id=1, source_target_pairs={{0,8},{1,9},{2,10},{3,11},{4,12},{5,13},{6,14},{7,15},{8,16},{9,17... | collective-permute-start | bytes 122888 | tf_op jit(solution)/shard_map/ppermute | solution.py:91
  16.8 5.6 %collective-permute-start.8 = (bf16[80,256]{1,0:T(8,128)(2,1)S(1)}, bf16[80,256]{1,0:T(8,128)(2,1)S(1)}, u32[]{:S(2)}, u32[]{:S(2)}) collective-permute-start(bf16[80,256]{1,0:T(8,128)(2,1)S(1)} %get-tuple-element.22), channel_id=1, source_target_pairs={{0,16},{1,17},{2,18},{3,19},{4,20},{5,21},{6,22},{7,23},{8,24},{9,... | collective-permute-start | bytes 122888 | tf_op jit(solution)/shard_map/ppermute | solution.py:91
  18.9 4.0 %collective-permute-start.9 = (bf16[80,256]{1,0:T(8,128)(2,1)S(1)}, bf16[80,256]{1,0:T(8,128)(2,1)S(1)}, u32[]{:S(2)}, u32[]{:S(2)}) collective-permute-start(bf16[80,256]{1,0:T(8,128)(2,1)S(1)} %get-tuple-element.23), channel_id=1, source_target_pairs={{0,24},{1,25},{2,26},{3,27},{4,28},{5,29},{6,30},{7,31},{8,0},{9,1... | collective-permute-start | bytes 122888 | tf_op jit(solution)/shard_map/ppermute | solution.py:91
  20.3 7.1 %collective-permute-start.11 = (bf16[224,512]{1,0:T(8,128)(2,1)S(1)}, bf16[224,512]{1,0:T(8,128)(2,1)S(1)}, u32[]{:S(2)}, u32[]{:S(2)}) collective-permute-start(bf16[224,512]{1,0:T(8,128)(2,1)S(1)} %rows_to_y.1.refs_0_), channel_id=1, source_target_pairs={{0,2},{1,3},{2,0},{3,1},{4,6},{5,7},{6,4},{7,5},{8,10},{9,11},{10,... | collective-permute-start | bytes 688136 | tf_op jit(solution)/shard_map/ppermute | solution.py:91
  22.9 1.2 %copy-start = (f32[512,512]{1,0:T(8,128)S(1)}, f32[512,512]{1,0:T(8,128)}, u32[]{:S(2)}) copy-start(f32[512,512]{1,0:T(8,128)} %refs_12_.1) | copy-start | bytes 3145732
  22.9 4.5 %collective-permute-start.12 = (bf16[80,512]{1,0:T(8,128)(2,1)S(1)}, bf16[80,512]{1,0:T(8,128)(2,1)S(1)}, u32[]{:S(2)}, u32[]{:S(2)}) collective-permute-start(bf16[80,512]{1,0:T(8,128)(2,1)S(1)} %rest_to_x.1.refs_1_), channel_id=1, source_target_pairs={{0,1},{1,0},{2,3},{3,2},{4,5},{5,4},{6,7},{7,6},{8,9},{9,8},{10,11... | collective-permute-start | bytes 245768 | tf_op jit(solution)/shard_map/ppermute | solution.py:91
  25.5 2.4 %collective-permute-start.10 = (bf16[768,512]{1,0:T(8,128)(2,1)S(1)}, bf16[768,512]{1,0:T(8,128)(2,1)S(1)}, u32[]{:S(2)}, u32[]{:S(2)}) collective-permute-start(bf16[768,512]{1,0:T(8,128)(2,1)S(1)} %get-tuple-element.25), channel_id=1, source_target_pairs={{0,4},{1,5},{2,6},{3,7},{4,0},{5,1},{6,2},{7,3},{8,12},{9,13},{10,... | collective-permute-start | bytes 2359304 | tf_op jit(solution)/shard_map/ppermute | solution.py:91
  27.5 2.1 %collective-permute-start.13 = (bf16[304,512]{1,0:T(8,128)(2,1)S(1)}, bf16[304,512]{1,0:T(8,128)(2,1)S(1)}, u32[]{:S(2)}, u32[]{:S(2)}) collective-permute-start(bf16[304,512]{1,0:T(8,128)(2,1)S(1)} %join.1.joined_ref), channel_id=1, source_target_pairs={{0,4},{1,5},{2,6},{3,7},{4,0},{5,1},{6,2},{7,3},{8,12},{9,13},{10,... | collective-permute-start | bytes 933896 | tf_op jit(solution)/shard_map/ppermute | solution.py:91

commit v16 on v15

--- a/solution.py
+++ b/solution.py
@@ -126,7 +126,6 @@
     weighted = (column * panel_ref[...].astype(f32)).astype(bf16)
     weighted_ref[...] = weighted
     to_x_ref[:, :width] = weighted
-    to_y_ref[:, :width] = weighted
 
     for b in range(block_count):
         block = jac_ref[b * block_rows : (b + 1) * block_rows, :].astype(f32)
@@ -147,7 +146,7 @@
     shape = (16, CAP * block_count * block_rows)
     lane, row = lax.broadcasted_iota(jnp.int32, shape, 1), lax.broadcasted_iota(jnp.int32, shape, 0)
     notes = []
-    spots = [(kept_ref, 0), (to_x_ref, width), (to_y_ref, width), (to_y_ref, width + post)]
+    spots = [(kept_ref, 0), (to_x_ref, width), (to_y_ref, 0), (to_y_ref, post)]
     for e, (parcel, start) in enumerate(spots):
         wanted = me_c ^ e
         found = jnp.int32(0)
@@ -179,7 +178,7 @@
                     parcel[u * part : (u + 1) * part, to : to + block_rows] = piece
     kept_ref[:16, post:] = notes[0].astype(f32).astype(bf16)
     to_x_ref[:16, width + post :] = notes[1].astype(f32).astype(bf16)
-    to_y_ref[:16, width + 2 * post :] = jnp.where(row == 0, notes[2], notes[3]).astype(f32).astype(bf16)
+    to_y_ref[:16, 2 * post :] = jnp.where(row == 0, notes[2], notes[3]).astype(f32).astype(bf16)
 
 
 def row_of(block, i):
@@ -196,17 +195,19 @@
 
 
 def stack_kernel(*refs):
-    at = 0
-    for ref in refs[:-1]:
-        refs[-1][at : at + ref.shape[0], :] = ref[...]
-        at += ref.shape[0]
+    inputs, (rest_ref, all_ref) = refs[:-2], refs[-2:]
+    rows = inputs[0].shape[0]
+    for i, ref in enumerate(inputs):
+        all_ref[i * rows : (i + 1) * rows, :] = ref[...]
+        if i:
+            rest_ref[(i - 1) * rows : i * rows, :] = ref[...]
 
 
 def sort_kernel(sizes, kept_ref, from_x_ref, from_y_ref, *posts):
     layers, width, lane_group, wide = sizes
     post = layers * lane_group
     rows = kept_ref.shape[0]
-    spots = [(kept_ref, 0), (from_x_ref, width), (from_y_ref, width), (from_y_ref, width + post)]
+    spots = [(kept_ref, 0), (from_x_ref, width), (from_y_ref, 0), (from_y_ref, post)]
     notes = [row_of(ref[:16, ref.shape[1] - wide :], int(e == 3)) for e, (ref, start) in enumerate(spots)]
     block = rows_from(notes)
     for k, out in enumerate(posts):
@@ -219,22 +220,20 @@
 def rows_to_y_kernel(from_x_ref, by_x_ref, out_ref):
     rows = from_x_ref.shape[0]
     out_ref[:rows, :] = from_x_ref[:, : out_ref.shape[1]]
-    out_ref[rows:, :] = by_x_ref[: out_ref.shape[0] - rows, :]
-
-
-def rest_to_x_kernel(sizes, by_y_ref, *refs):
+    out_ref[rows:, :] = by_x_ref[...]
+
+
+def columns_to_x_kernel(sizes, *refs):
     layers, lane_group, wide = sizes
-    posts, out_ref = refs[:layers], refs[layers]
+    posts, out_ref = refs[:layers], refs[-1]
     rows = posts[0].shape[0] - 16
     part = rows // 2
-    last = out_ref.shape[0] - part - 16
-    out_ref[:last, :] = by_y_ref[by_y_ref.shape[0] - last :, :]
     for k, ref in enumerate(posts):
         for u in range(2):
             piece = ref[u * part : (u + 1) * part, 3 * lane_group : 4 * lane_group]
             at = (u * layers + k) * lane_group
-            out_ref[last : last + part, at : at + lane_group] = piece
-    out_ref[last + part :, :wide] = rows_from([row_of(ref[rows:, :wide], 3) for ref in posts])
+            out_ref[:part, at : at + lane_group] = piece
+    out_ref[part:, :wide] = rows_from([row_of(ref[rows:, :wide], 3) for ref in posts])
 
 
 def place(out_ref, lanes, per_owner, pieces, notes, sizes):
@@ -270,10 +269,10 @@
 
 def near_kernel(sizes, earlier, *refs):
     layers, owners, per_owner, block_count, block_rows = sizes
-    refs = refs[earlier:]
-    inputs = 2 * (owners - 1) + layers
-    panels, posts = refs[: 2 * (owners - 1)], refs[2 * (owners - 1) : inputs]
-    factor_ref, own_ref, other_ref, turned_ref, placed_ref, rows_ref = refs[inputs:]
+    panels, posts, refs = refs[earlier : earlier + 4], refs[earlier + 4 : earlier + 4 + layers], refs[earlier + 4 + layers :]
+    factor_hbm, own_ref, other_ref, turned_ref, placed_ref, rows_ref, factor_ref, sem = refs
+    copy = pltpu.make_async_copy(factor_hbm, factor_ref, sem)
+    copy.start()
     f32, bf16 = jnp.float32, jnp.bfloat16
     rows = block_count * block_rows
     group, wide = CAP * block_rows, CAP * rows
@@ -293,6 +292,7 @@
                 place(placed_ref, slice(start, start + 2 * rows), per_owner, pieces, notes, (block_count, block_rows))
         gram = jnp.dot(placed_ref[...], rows_ref[...], preferred_element_type=f32)
         out_ref[...] = gram.astype(out_ref.dtype)
+    copy.wait()
     turned = factor_ref[...].T
     high = turned.astype(bf16)
     turned_ref[0, :, :] = high
@@ -381,7 +381,7 @@
         functools.partial(pack_kernel, sizes),
         out_shape=[
             shaped((rows, width), bf16)
-            for width in (panel_width, post + wide, panel_width + post + wide, panel_width + 2 * post + wide)
+            for width in (panel_width, post + wide, panel_width + post + wide, 2 * post + wide)
         ],
         in_specs=[anywhere] * 6,
         out_specs=[vmem] * 4,
@@ -403,15 +403,15 @@
     from_x, from_y = shift(to_x, 0, 1), shift(to_y, 0, 2)
 
     sizes = (layers, panel_width, lane_group, wide)
-    others = pl.pallas_call(
+    others, column = pl.pallas_call(
         stack_kernel,
-        out_shape=shaped(((layers - 1) * rows, panel_width), bf16),
-        in_specs=[vmem] * (layers - 1),
-        out_specs=vmem,
+        out_shape=[shaped((height * rows, panel_width), bf16) for height in (layers - 1, layers)],
+        in_specs=[vmem] * layers,
+        out_specs=[vmem] * 2,
         compiler_params=params,
         cost_estimate=lasting(10**10),
         name="stack",
-    )(*line)
+    )(weighted, *line)
     posts = pl.pallas_call(
         functools.partial(sort_kernel, sizes),
         out_shape=[shaped((rows + 16, owners * lane_group), bf16)] * layers,
@@ -422,47 +422,48 @@
         name="sort",
     )(kept, from_x, from_y)
     posts = [posts[0]] + [shift(posts[k], k, 0) for k in range(1, layers)]
-    by_x, by_y = shift(others, 0, 1), shift(others, 0, 2)
-
-    last = rows // 2
+    by_x, by_y = shift(others, 0, 1), shift(column, 0, 2)
+
     rows_to_y = pl.pallas_call(
         rows_to_y_kernel,
-        out_shape=shaped((rows + others.shape[0] - last, panel_width), bf16),
+        out_shape=shaped(column.shape, bf16),
         in_specs=[vmem] * 2,
         out_specs=vmem,
         compiler_params=params,
         name="rows_to_y",
     )(from_x, by_x)
     across_y = shift(rows_to_y, 0, 2)
-    rest_to_x = pl.pallas_call(
-        functools.partial(rest_to_x_kernel, (layers, lane_group, wide)),
-        out_shape=shaped((last + rows // 2 + 16, panel_width), bf16),
-        in_specs=[vmem] * (layers + 1),
+    columns_to_x = pl.pallas_call(
+        functools.partial(columns_to_x_kernel, (layers, lane_group, wide)),
+        out_shape=shaped((rows // 2 + 16, panel_width), bf16),
+        in_specs=[vmem] * layers + [anywhere],
         out_specs=vmem,
         compiler_params=params,
         cost_estimate=lasting(3 * 10**9),
-        name="rest_to_x",
-    )(by_y, *posts)
-    across_x = shift(rest_to_x, 0, 1)
+        name="columns_to_x",
+    )(*posts, by_y)
+    across_x = shift(columns_to_x, 0, 1)
 
     count = per_owner * slab_width
     depth = layers * rows
     sizes = (layers, owners, per_owner, block_count, block_rows)
     result = shaped((count, panel_width), f32)
-    panels = [weighted, others, from_x, by_x, from_y, by_y]
+    panels = [column, from_x, by_x, by_y]
     own, other, turned = pl.pallas_call(
         functools.partial(near_kernel, sizes, 2),
         out_shape=[result, shaped((count, panel_width), bf16), shaped((2, *factor_inverse.shape), bf16)],
-        in_specs=[anywhere] * 2 + [vmem] * (len(panels) + layers + 1),
+        in_specs=[anywhere] * 2 + [vmem] * (len(panels) + layers) + [anywhere],
         out_specs=[vmem] * 3,
         scratch_shapes=[
             pltpu.VMEM((count, (owners - 1) * depth), bf16),
             pltpu.VMEM(((owners - 1) * depth, panel_width), bf16),
+            pltpu.VMEM(factor_inverse.shape, f32),
+            pltpu.SemaphoreType.DMA,
         ],
         compiler_params=params,
         cost_estimate=lasting(10**9),
         name="near",
-    )(rows_to_y, rest_to_x, *panels, *posts, factor_inverse)
+    )(rows_to_y, columns_to_x, *panels, *posts, in_hbm(factor_inverse))
     other = shift(other, 0, 0, 1)
     joined = pl.pallas_call(
         join_kernel,

time: 31.6 us -> 31.5 us (level)
  local copies, waits for them, and re-layouts: 0.47 us -> 0 us
  Pallas kernels: 6.84 us -> 7.21 us
    unnamed x2 -> x0, local copies, waits for them, and re-layouts: 0.47 us -> none
    pallas_call x1, Pallas kernels: 1.45 us -> 1.8 us  [local(): pl.pallas_call(functools.partial(near_kernel, sizes, 2), out_shape=[resul...]
  transfers between devices with their start and end apart: 14 -> 14, of which waited for: 6 -> 7; matrix products, arithmetic and copies ran while one was open for 0% -> 0% of each run, Pallas kernels for 11% -> 12%
where the time goes in v16:
time: 31.5 us; the launch traced here: 31.3 us
  starting transfers between devices  19.6 us (62%)
  Pallas kernels  7.21 us (23%)
  waiting for transfers between devices  4.38 us (14%)
    ppermute x14, starting transfers between devices, shift(): return lax.ppermute(value, ('rows', 'cols'), pairs)  19.6 us
    ppermute x14, waiting for transfers between devices, shift(): return lax.ppermute(value, ('rows', 'cols'), pairs)  4.38 us
    pallas_call x1, Pallas kernels, local(): pl.pallas_call(functools.partial(final_kernel, sizes), out_shape=result,...  1.86 us
    pallas_call x1, Pallas kernels, local(): pl.pallas_call(functools.partial(near_kernel, sizes, 2), out_shape=[resul...  1.8 us
    pallas_call x1, Pallas kernels, local(): pl.pallas_call(functools.partial(middle_kernel, sizes), out_shape=result,...  1.7 us
    pallas_call x1, Pallas kernels, local(): pl.pallas_call(functools.partial(pack_kernel, sizes), out_shape=[shaped((...  1.57 us
  transfers between devices with their start and end apart: 14, of which 7 were waited for; matrix products, arithmetic and copies ran while one was open for 0% of the time, Pallas kernels for 12%

profile of v16, /device:TPU:0, one launch (start us, length us, event | category | flops | bytes accessed | tf_op | source)
XLA Modules:
  0.0 31.3 jit_solution(2731040212201225340)
XLA Ops:
  0.0 1.6 %pack.1 = (bf16[64,512]{1,0:T(8,128)(2,1)S(1)}, bf16[64,384]{1,0:T(8,128)(2,1)S(1)}, bf16[64,896]{1,0:T(8,128)(2,1)S(1)}, bf16[64,640]{1,0:T(8,128)(2,1)S(1)}) custom-call(s32[2,4]{1,0:T(2,128)} %lists_hbm.1, s32[2,4]{1,0:T(2,128)} %masks_hbm.1, s32[96]{0:T(128)} %order_hbm.1, f32[1,64]{1,0:T(1,128)} %bitcast.2, bf16[64,512]{1,0:T(8,128)(2,1)} %panel_hbm.1, ...), custom_call_target="tpu_custom_call" | custom-call | tf_op jit(solution)/shard_map/pack/pallas_call | solution.py:380
  1.6 3.1 %collective-permute-start.1 = (bf16[64,512]{1,0:T(8,128)(2,1)S(1)}, bf16[64,512]{1,0:T(8,128)(2,1)S(1)}, u32[]{:S(2)}, u32[]{:S(2)}) collective-permute-start(bf16[64,512]{1,0:T(8,128)(2,1)S(1)} %get-tuple-element.19.refs_0_), channel_id=1, source_target_pairs={{0,8},{1,9},{2,10},{3,11},{4,12},{5,13},{6,14},{7,15},{8,16},{9,17... | collective-permute-start | bytes 196616 | tf_op jit(solution)/shard_map/ppermute | solution.py:91
  4.7 2.6 %collective-permute-start.2 = (bf16[64,512]{1,0:T(8,128)(2,1)S(1)}, bf16[64,512]{1,0:T(8,128)(2,1)S(1)}, u32[]{:S(2)}, u32[]{:S(2)}) collective-permute-start(bf16[64,512]{1,0:T(8,128)(2,1)S(1)} %get-tuple-element.19.refs_0_), channel_id=1, source_target_pairs={{0,16},{1,17},{2,18},{3,19},{4,20},{5,21},{6,22},{7,23},{8,24},{9,... | collective-permute-start | bytes 196616 | tf_op jit(solution)/shard_map/ppermute | solution.py:91
  7.2 1.3 %collective-permute-start.3 = (bf16[64,512]{1,0:T(8,128)(2,1)S(1)}, bf16[64,512]{1,0:T(8,128)(2,1)S(1)}, u32[]{:S(2)}, u32[]{:S(2)}) collective-permute-start(bf16[64,512]{1,0:T(8,128)(2,1)S(1)} %get-tuple-element.19.refs_0_), channel_id=1, source_target_pairs={{0,24},{1,25},{2,26},{3,27},{4,28},{5,29},{6,30},{7,31},{8,0},{9,1... | collective-permute-start | bytes 196616 | tf_op jit(solution)/shard_map/ppermute | solution.py:91
  8.6 1.5 %collective-permute-start = (bf16[64,896]{1,0:T(8,128)(2,1)S(1)}, bf16[64,896]{1,0:T(8,128)(2,1)S(1)}, u32[]{:S(2)}, u32[]{:S(2)}) collective-permute-start(bf16[64,896]{1,0:T(8,128)(2,1)S(1)} %get-tuple-element.18), channel_id=1, source_target_pairs={{0,1},{1,0},{2,3},{3,2},{4,5},{5,4},{6,7},{7,6},{8,9},{9,8},{10,11... | collective-permute-start | bytes 344072 | tf_op jit(solution)/shard_map/ppermute | solution.py:91
  10.1 1.5 %collective-permute-start.5 = (bf16[64,640]{1,0:T(8,128)(2,1)S(1)}, bf16[64,640]{1,0:T(8,128)(2,1)S(1)}, u32[]{:S(2)}, u32[]{:S(2)}) collective-permute-start(bf16[64,640]{1,0:T(8,128)(2,1)S(1)} %get-tuple-element.22), channel_id=1, source_target_pairs={{0,2},{1,3},{2,0},{3,1},{4,6},{5,7},{6,4},{7,5},{8,10},{9,11},{10,... | collective-permute-start | bytes 245768 | tf_op jit(solution)/shard_map/ppermute | solution.py:91
  11.6 0.0 collective-permute-done.1.refs_1_
  11.6 0.1 collective-permute-done.2.refs_2_
  11.7 0.2 collective-permute-done.3.refs_3_
  12.0 1.6 %collective-permute-start.9 = (bf16[256,512]{1,0:T(8,128)(2,1)S(1)}, bf16[256,512]{1,0:T(8,128)(2,1)S(1)}, u32[]{:S(2)}, u32[]{:S(2)}) collective-permute-start(bf16[256,512]{1,0:T(8,128)(2,1)S(1)} %get-tuple-element.27.refs_2_), channel_id=1, source_target_pairs={{0,2},{1,3},{2,0},{3,1},{4,6},{5,7},{6,4},{7,5},{8,10},{9,11},{10,... | collective-permute-start | bytes 786440 | tf_op jit(solution)/shard_map/ppermute | solution.py:91
  13.6 1.5 %collective-permute-start.4 = (bf16[192,512]{1,0:T(8,128)(2,1)S(1)}, bf16[192,512]{1,0:T(8,128)(2,1)S(1)}, u32[]{:S(2)}, u32[]{:S(2)}) collective-permute-start(bf16[192,512]{1,0:T(8,128)(2,1)S(1)} %get-tuple-element.20), channel_id=1, source_target_pairs={{0,1},{1,0},{2,3},{3,2},{4,5},{5,4},{6,7},{7,6},{8,9},{9,8},{10,11... | collective-permute-start | bytes 589832 | tf_op jit(solution)/shard_map/ppermute | solution.py:91
  15.1 0.0 collective-permute-done.5.from_y_ref
  15.1 0.0 collective-permute-done.from_x_ref.refs_3_
  15.1 0.1 sort.1
  15.3 1.6 %collective-permute-start.6 = (bf16[80,256]{1,0:T(8,128)(2,1)S(1)}, bf16[80,256]{1,0:T(8,128)(2,1)S(1)}, u32[]{:S(2)}, u32[]{:S(2)}) collective-permute-start(bf16[80,256]{1,0:T(8,128)(2,1)S(1)} %get-tuple-element.24), channel_id=1, source_target_pairs={{0,8},{1,9},{2,10},{3,11},{4,12},{5,13},{6,14},{7,15},{8,16},{9,17... | collective-permute-start | bytes 122888 | tf_op jit(solution)/shard_map/ppermute | solution.py:91
  16.8 2.0 %collective-permute-start.7 = (bf16[80,256]{1,0:T(8,128)(2,1)S(1)}, bf16[80,256]{1,0:T(8,128)(2,1)S(1)}, u32[]{:S(2)}, u32[]{:S(2)}) collective-permute-start(bf16[80,256]{1,0:T(8,128)(2,1)S(1)} %get-tuple-element.25), channel_id=1, source_target_pairs={{0,16},{1,17},{2,18},{3,19},{4,20},{5,21},{6,22},{7,23},{8,24},{9,... | collective-permute-start | bytes 122888 | tf_op jit(solution)/shard_map/ppermute | solution.py:91
  18.9 0.4 %collective-permute-start.8 = (bf16[80,256]{1,0:T(8,128)(2,1)S(1)}, bf16[80,256]{1,0:T(8,128)(2,1)S(1)}, u32[]{:S(2)}, u32[]{:S(2)}) collective-permute-start(bf16[80,256]{1,0:T(8,128)(2,1)S(1)} %get-tuple-element.26), channel_id=1, source_target_pairs={{0,24},{1,25},{2,26},{3,27},{4,28},{5,29},{6,30},{7,31},{8,0},{9,1... | collective-permute-start | bytes 122888 | tf_op jit(solution)/shard_map/ppermute | solution.py:91
  19.3 0.0 collective-permute-done.4.by_x_ref.refs_4_
  19.3 1.7 %collective-permute-start.11 = (bf16[256,512]{1,0:T(8,128)(2,1)S(1)}, bf16[256,512]{1,0:T(8,128)(2,1)S(1)}, u32[]{:S(2)}, u32[]{:S(2)}) collective-permute-start(bf16[256,512]{1,0:T(8,128)(2,1)S(1)} %rows_to_y.1.refs_0_), channel_id=1, source_target_pairs={{0,2},{1,3},{2,0},{3,1},{4,6},{5,7},{6,4},{7,5},{8,10},{9,11},{10,... | collective-permute-start | bytes 786440 | tf_op jit(solution)/shard_map/ppermute | solution.py:91
  21.0 0.2 collective-permute-done.6.refs_1_.refs_7_
  21.2 0.9 %collective-permute-done.7.refs_2_.refs_8_ = bf16[80,256]{1,0:T(8,128)(2,1)S(1)} collective-permute-done((bf16[80,256]{1,0:T(8,128)(2,1)S(1)}, bf16[80,256]{1,0:T(8,128)(2,1)S(1)}, u32[]{:S(2)}, u32[]{:S(2)}) %collective-permute-start.7) | collective-permute-done | bytes 40992 | tf_op jit(solution)/shard_map/ppermute | solution.py:91
  22.1 0.7 %collective-permute-done.8.refs_3_.refs_9_ = bf16[80,256]{1,0:T(8,128)(2,1)S(1)} collective-permute-done((bf16[80,256]{1,0:T(8,128)(2,1)S(1)}, bf16[80,256]{1,0:T(8,128)(2,1)S(1)}, u32[]{:S(2)}, u32[]{:S(2)}) %collective-permute-start.8) | collective-permute-done | bytes 40992 | tf_op jit(solution)/shard_map/ppermute | solution.py:91
  22.9 0.1 columns_to_x.1.refs_1_
  23.0 0.6 %collective-permute-start.12 = (bf16[48,512]{1,0:T(8,128)(2,1)S(1)}, bf16[48,512]{1,0:T(8,128)(2,1)S(1)}, u32[]{:S(2)}, u32[]{:S(2)}) collective-permute-start(bf16[48,512]{1,0:T(8,128)(2,1)S(1)} %columns_to_x.1.refs_1_), channel_id=1, source_target_pairs={{0,1},{1,0},{2,3},{3,2},{4,5},{5,4},{6,7},{7,6},{8,9},{9,8},{10,11... | collective-permute-start | bytes 147464 | tf_op jit(solution)/shard_map/ppermute | solution.py:91
  23.6 1.8 %near.1 = (f32[768,512]{1,0:T(8,128)S(1)}, bf16[768,512]{1,0:T(8,128)(2,1)S(1)}, bf16[2,512,512]{2,1,0:T(8,128)(2,1)S(1)}) custom-call(bf16[256,512]{1,0:T(8,128)(2,1)S(1)} %rows_to_y.1.refs_0_, bf16[48,512]{1,0:T(8,128)(2,1)S(1)} %columns_to_x.1.refs_1_, bf16[256,512]{1,0:T(8,128)(2,1)S(1)} %get-tuple-element.27.refs_2_, ...), custom_call_target="tpu_custom_call" | custom-call | flops 1000000000 | tf_op jit(solution)/shard_map/near/pallas_call | solution.py:452
  25.4 0.1 collective-permute-start.10
  25.5 1.7 %collective-permute-done.12.below_ref = bf16[48,512]{1,0:T(8,128)(2,1)S(1)} collective-permute-done((bf16[48,512]{1,0:T(8,128)(2,1)S(1)}, bf16[48,512]{1,0:T(8,128)(2,1)S(1)}, u32[]{:S(2)}, u32[]{:S(2)}) %collective-permute-start.12) | collective-permute-done | bytes 49184 | tf_op jit(solution)/shard_map/ppermute | solution.py:91
  27.1 0.0 collective-permute-done.11.above_ref
  27.1 0.1 collective-permute-start.13
  27.2 0.5 %collective-permute-done.10.other_ref = bf16[768,512]{1,0:T(8,128)(2,1)S(1)} collective-permute-done((bf16[768,512]{1,0:T(8,128)(2,1)S(1)}, bf16[768,512]{1,0:T(8,128)(2,1)S(1)}, u32[]{:S(2)}, u32[]{:S(2)}) %collective-permute-start.10) | collective-permute-done | bytes 786464 | tf_op jit(solution)/shard_map/ppermute | solution.py:91
  27.7 1.7 %middle.1.middle_ref = f32[768,512]{1,0:T(8,128)S(1)} custom-call(f32[768,512]{1,0:T(8,128)S(1)} %get-tuple-element.28.own_ref, bf16[768,512]{1,0:T(8,128)(2,1)S(1)} %collective-permute-done.10.other_ref, bf16[304,512]{1,0:T(8,128)(2,1)S(1)} %join.1.joined_ref, bf16[2,512,512]{2,1,0:T(8,128)(2,1)S(1)} %get-tuple-element.30.turned_ref), custom_call_target="tpu_custom_call" | custom-call | tf_op jit(solution)/shard_map/middle/pallas_call | solution.py:479
  29.4 1.9 %final.1 = f32[768,512]{1,0:T(8,128)} custom-call(f32[768,512]{1,0:T(8,128)S(1)} %middle.1.middle_ref, bf16[304,512]{1,0:T(8,128)(2,1)S(1)} %collective-permute-done.13.joined_ref, bf16[2,512,512]{2,1,0:T(8,128)(2,1)S(1)} %get-tuple-element.30.turned_ref), custom_call_target="tpu_custom_call" | custom-call | tf_op jit(solution)/shard_map/final/pallas_call | solution.py:488
  (5 shorter events, 0.1 us)
Async XLA Ops:
  1.6 10.0 %collective-permute-start.1 = (bf16[64,512]{1,0:T(8,128)(2,1)S(1)}, bf16[64,512]{1,0:T(8,128)(2,1)S(1)}, u32[]{:S(2)}, u32[]{:S(2)}) collective-permute-start(bf16[64,512]{1,0:T(8,128)(2,1)S(1)} %get-tuple-element.19.refs_0_), channel_id=1, source_target_pairs={{0,8},{1,9},{2,10},{3,11},{4,12},{5,13},{6,14},{7,15},{8,16},{9,17... | collective-permute-start | bytes 196616 | tf_op jit(solution)/shard_map/ppermute | solution.py:91
  4.7 7.1 %collective-permute-start.2 = (bf16[64,512]{1,0:T(8,128)(2,1)S(1)}, bf16[64,512]{1,0:T(8,128)(2,1)S(1)}, u32[]{:S(2)}, u32[]{:S(2)}) collective-permute-start(bf16[64,512]{1,0:T(8,128)(2,1)S(1)} %get-tuple-element.19.refs_0_), channel_id=1, source_target_pairs={{0,16},{1,17},{2,18},{3,19},{4,20},{5,21},{6,22},{7,23},{8,24},{9,... | collective-permute-start | bytes 196616 | tf_op jit(solution)/shard_map/ppermute | solution.py:91
  7.2 4.7 %collective-permute-start.3 = (bf16[64,512]{1,0:T(8,128)(2,1)S(1)}, bf16[64,512]{1,0:T(8,128)(2,1)S(1)}, u32[]{:S(2)}, u32[]{:S(2)}) collective-permute-start(bf16[64,512]{1,0:T(8,128)(2,1)S(1)} %get-tuple-element.19.refs_0_), channel_id=1, source_target_pairs={{0,24},{1,25},{2,26},{3,27},{4,28},{5,29},{6,30},{7,31},{8,0},{9,1... | collective-permute-start | bytes 196616 | tf_op jit(solution)/shard_map/ppermute | solution.py:91
  8.6 6.5 %collective-permute-start = (bf16[64,896]{1,0:T(8,128)(2,1)S(1)}, bf16[64,896]{1,0:T(8,128)(2,1)S(1)}, u32[]{:S(2)}, u32[]{:S(2)}) collective-permute-start(bf16[64,896]{1,0:T(8,128)(2,1)S(1)} %get-tuple-element.18), channel_id=1, source_target_pairs={{0,1},{1,0},{2,3},{3,2},{4,5},{5,4},{6,7},{7,6},{8,9},{9,8},{10,11... | collective-permute-start | bytes 344072 | tf_op jit(solution)/shard_map/ppermute | solution.py:91
  10.1 5.0 %collective-permute-start.5 = (bf16[64,640]{1,0:T(8,128)(2,1)S(1)}, bf16[64,640]{1,0:T(8,128)(2,1)S(1)}, u32[]{:S(2)}, u32[]{:S(2)}) collective-permute-start(bf16[64,640]{1,0:T(8,128)(2,1)S(1)} %get-tuple-element.22), channel_id=1, source_target_pairs={{0,2},{1,3},{2,0},{3,1},{4,6},{5,7},{6,4},{7,5},{8,10},{9,11},{10,... | collective-permute-start | bytes 245768 | tf_op jit(solution)/shard_map/ppermute | solution.py:91
  12.0 10.9 %collective-permute-start.9 = (bf16[256,512]{1,0:T(8,128)(2,1)S(1)}, bf16[256,512]{1,0:T(8,128)(2,1)S(1)}, u32[]{:S(2)}, u32[]{:S(2)}) collective-permute-start(bf16[256,512]{1,0:T(8,128)(2,1)S(1)} %get-tuple-element.27.refs_2_), channel_id=1, source_target_pairs={{0,2},{1,3},{2,0},{3,1},{4,6},{5,7},{6,4},{7,5},{8,10},{9,11},{10,... | collective-permute-start | bytes 786440 | tf_op jit(solution)/shard_map/ppermute | solution.py:91
  13.6 5.7 %collective-permute-start.4 = (bf16[192,512]{1,0:T(8,128)(2,1)S(1)}, bf16[192,512]{1,0:T(8,128)(2,1)S(1)}, u32[]{:S(2)}, u32[]{:S(2)}) collective-permute-start(bf16[192,512]{1,0:T(8,128)(2,1)S(1)} %get-tuple-element.20), channel_id=1, source_target_pairs={{0,1},{1,0},{2,3},{3,2},{4,5},{5,4},{6,7},{7,6},{8,9},{9,8},{10,11... | collective-permute-start | bytes 589832 | tf_op jit(solution)/shard_map/ppermute | solution.py:91
  15.3 6.0 %collective-permute-start.6 = (bf16[80,256]{1,0:T(8,128)(2,1)S(1)}, bf16[80,256]{1,0:T(8,128)(2,1)S(1)}, u32[]{:S(2)}, u32[]{:S(2)}) collective-permute-start(bf16[80,256]{1,0:T(8,128)(2,1)S(1)} %get-tuple-element.24), channel_id=1, source_target_pairs={{0,8},{1,9},{2,10},{3,11},{4,12},{5,13},{6,14},{7,15},{8,16},{9,17... | collective-permute-start | bytes 122888 | tf_op jit(solution)/shard_map/ppermute | solution.py:91
  16.8 5.3 %collective-permute-start.7 = (bf16[80,256]{1,0:T(8,128)(2,1)S(1)}, bf16[80,256]{1,0:T(8,128)(2,1)S(1)}, u32[]{:S(2)}, u32[]{:S(2)}) collective-permute-start(bf16[80,256]{1,0:T(8,128)(2,1)S(1)} %get-tuple-element.25), channel_id=1, source_target_pairs={{0,16},{1,17},{2,18},{3,19},{4,20},{5,21},{6,22},{7,23},{8,24},{9,... | collective-permute-start | bytes 122888 | tf_op jit(solution)/shard_map/ppermute | solution.py:91
  18.9 4.0 %collective-permute-start.8 = (bf16[80,256]{1,0:T(8,128)(2,1)S(1)}, bf16[80,256]{1,0:T(8,128)(2,1)S(1)}, u32[]{:S(2)}, u32[]{:S(2)}) collective-permute-start(bf16[80,256]{1,0:T(8,128)(2,1)S(1)} %get-tuple-element.26), channel_id=1, source_target_pairs={{0,24},{1,25},{2,26},{3,27},{4,28},{5,29},{6,30},{7,31},{8,0},{9,1... | collective-permute-start | bytes 122888 | tf_op jit(solution)/shard_map/ppermute | solution.py:91
  19.3 7.8 %collective-permute-start.11 = (bf16[256,512]{1,0:T(8,128)(2,1)S(1)}, bf16[256,512]{1,0:T(8,128)(2,1)S(1)}, u32[]{:S(2)}, u32[]{:S(2)}) collective-permute-start(bf16[256,512]{1,0:T(8,128)(2,1)S(1)} %rows_to_y.1.refs_0_), channel_id=1, source_target_pairs={{0,2},{1,3},{2,0},{3,1},{4,6},{5,7},{6,4},{7,5},{8,10},{9,11},{10,... | collective-permute-start | bytes 786440 | tf_op jit(solution)/shard_map/ppermute | solution.py:91
  23.0 4.2 %collective-permute-start.12 = (bf16[48,512]{1,0:T(8,128)(2,1)S(1)}, bf16[48,512]{1,0:T(8,128)(2,1)S(1)}, u32[]{:S(2)}, u32[]{:S(2)}) collective-permute-start(bf16[48,512]{1,0:T(8,128)(2,1)S(1)} %columns_to_x.1.refs_1_), channel_id=1, source_target_pairs={{0,1},{1,0},{2,3},{3,2},{4,5},{5,4},{6,7},{7,6},{8,9},{9,8},{10,11... | collective-permute-start | bytes 147464 | tf_op jit(solution)/shard_map/ppermute | solution.py:91
  25.4 2.4 %collective-permute-start.10 = (bf16[768,512]{1,0:T(8,128)(2,1)S(1)}, bf16[768,512]{1,0:T(8,128)(2,1)S(1)}, u32[]{:S(2)}, u32[]{:S(2)}) collective-permute-start(bf16[768,512]{1,0:T(8,128)(2,1)S(1)} %get-tuple-element.29), channel_id=1, source_target_pairs={{0,4},{1,5},{2,6},{3,7},{4,0},{5,1},{6,2},{7,3},{8,12},{9,13},{10,... | collective-permute-start | bytes 2359304 | tf_op jit(solution)/shard_map/ppermute | solution.py:91
  27.1 2.3 %collective-permute-start.13 = (bf16[304,512]{1,0:T(8,128)(2,1)S(1)}, bf16[304,512]{1,0:T(8,128)(2,1)S(1)}, u32[]{:S(2)}, u32[]{:S(2)}) collective-permute-start(bf16[304,512]{1,0:T(8,128)(2,1)S(1)} %join.1.joined_ref), channel_id=1, source_target_pairs={{0,4},{1,5},{2,6},{3,7},{4,0},{5,1},{6,2},{7,3},{8,12},{9,13},{10,... | collective-permute-start | bytes 933896 | tf_op jit(solution)/shard_map/ppermute | solution.py:91

commit v17 on v16

--- a/solution.py
+++ b/solution.py
@@ -197,7 +197,7 @@
 def stack_kernel(*refs):
     inputs, (rest_ref, all_ref) = refs[:-2], refs[-2:]
     rows = inputs[0].shape[0]
-    for i, ref in enumerate(inputs):
+    for i, ref in enumerate(reversed(inputs)):
         all_ref[i * rows : (i + 1) * rows, :] = ref[...]
         if i:
             rest_ref[(i - 1) * rows : i * rows, :] = ref[...]
@@ -267,12 +267,20 @@
         low_ref[:, start:stop] = (total - high.astype(f32)).astype(bf16)
 
 
+def turn_kernel(factor_hbm, out_ref, factor_ref, sem):
+    copy = pltpu.make_async_copy(factor_hbm, factor_ref, sem)
+    copy.start()
+    copy.wait()
+    turned = factor_ref[...].T
+    high = turned.astype(jnp.bfloat16)
+    out_ref[0, :, :] = high
+    out_ref[1, :, :] = (turned - high.astype(jnp.float32)).astype(jnp.bfloat16)
+
+
 def near_kernel(sizes, earlier, *refs):
     layers, owners, per_owner, block_count, block_rows = sizes
     panels, posts, refs = refs[earlier : earlier + 4], refs[earlier + 4 : earlier + 4 + layers], refs[earlier + 4 + layers :]
-    factor_hbm, own_ref, other_ref, turned_ref, placed_ref, rows_ref, factor_ref, sem = refs
-    copy = pltpu.make_async_copy(factor_hbm, factor_ref, sem)
-    copy.start()
+    own_ref, other_ref, placed_ref, rows_ref = refs
     f32, bf16 = jnp.float32, jnp.bfloat16
     rows = block_count * block_rows
     group, wide = CAP * block_rows, CAP * rows
@@ -292,11 +300,6 @@
                 place(placed_ref, slice(start, start + 2 * rows), per_owner, pieces, notes, (block_count, block_rows))
         gram = jnp.dot(placed_ref[...], rows_ref[...], preferred_element_type=f32)
         out_ref[...] = gram.astype(out_ref.dtype)
-    copy.wait()
-    turned = factor_ref[...].T
-    high = turned.astype(bf16)
-    turned_ref[0, :, :] = high
-    turned_ref[1, :, :] = (turned - high.astype(f32)).astype(bf16)
 
 
 def join_kernel(above_ref, below_ref, out_ref):
@@ -320,22 +323,25 @@
         place(placed_ref, lanes, per_owner, pieces, notes, (block_count, block_rows))
 
 
-def middle_kernel(sizes, own_ref, other_ref, joined_ref, turned_ref, out_ref, placed_ref, high_ref, low_ref):
-    f32, bf16 = jnp.float32, jnp.bfloat16
-    width = own_ref.shape[1]
+def far_kernel(sizes, joined_ref, turned_ref, out_ref, placed_ref, high_ref, low_ref):
     place_far(sizes, 0, joined_ref, placed_ref)
     inverse_rows(joined_ref, turned_ref, high_ref, low_ref)
     placed = placed_ref[...]
+    total = jnp.dot(placed, high_ref[...], preferred_element_type=jnp.float32)
+    out_ref[...] = total + jnp.dot(placed, low_ref[...], preferred_element_type=jnp.float32)
+
+
+def middle_kernel(far_ref, own_ref, other_ref, turned_ref, out_ref):
+    f32, bf16 = jnp.float32, jnp.bfloat16
+    width = own_ref.shape[1]
     gram = own_ref[...] + other_ref[...].astype(f32)
     high = gram.astype(bf16)
     low = (gram - high.astype(f32)).astype(bf16)
     for start, stop in ((0, width // 2), (width // 2, width)):
         a, b = turned_ref[0, :stop, start:stop], turned_ref[1, :stop, start:stop]
-        total = jnp.dot(high[:, :stop], a, preferred_element_type=f32)
+        total = far_ref[:, start:stop] + jnp.dot(high[:, :stop], a, preferred_element_type=f32)
         total += jnp.dot(high[:, :stop], b, preferred_element_type=f32)
-        total += jnp.dot(low[:, :stop], a, preferred_element_type=f32)
-        total += jnp.dot(placed, high_ref[:, start:stop], preferred_element_type=f32)
-        out_ref[:, start:stop] = total + jnp.dot(placed, low_ref[:, start:stop], preferred_element_type=f32)
+        out_ref[:, start:stop] = total + jnp.dot(low[:, :stop], a, preferred_element_type=f32)
 
 
 def final_kernel(sizes, middle_ref, joined_ref, turned_ref, out_hbm, sum_ref, placed_ref, high_ref, low_ref, sems):
@@ -411,7 +417,7 @@
         compiler_params=params,
         cost_estimate=lasting(10**10),
         name="stack",
-    )(weighted, *line)
+    )(*reversed(line), weighted)
     posts = pl.pallas_call(
         functools.partial(sort_kernel, sizes),
         out_shape=[shaped((rows + 16, owners * lane_group), bf16)] * layers,
@@ -433,15 +439,24 @@
         name="rows_to_y",
     )(from_x, by_x)
     across_y = shift(rows_to_y, 0, 2)
+    turned = pl.pallas_call(
+        turn_kernel,
+        out_shape=shaped((2, *factor_inverse.shape), bf16),
+        in_specs=[anywhere],
+        out_specs=vmem,
+        scratch_shapes=[pltpu.VMEM(factor_inverse.shape, f32), pltpu.SemaphoreType.DMA],
+        compiler_params=params,
+        name="turn",
+    )(in_hbm(factor_inverse))
     columns_to_x = pl.pallas_call(
         functools.partial(columns_to_x_kernel, (layers, lane_group, wide)),
         out_shape=shaped((rows // 2 + 16, panel_width), bf16),
-        in_specs=[vmem] * layers + [anywhere],
+        in_specs=[vmem] * layers + [anywhere] * 2,
         out_specs=vmem,
         compiler_params=params,
         cost_estimate=lasting(3 * 10**9),
         name="columns_to_x",
-    )(*posts, by_y)
+    )(*posts, by_y, turned)
     across_x = shift(columns_to_x, 0, 1)
 
     count = per_owner * slab_width
@@ -449,21 +464,19 @@
     sizes = (layers, owners, per_owner, block_count, block_rows)
     result = shaped((count, panel_width), f32)
     panels = [column, from_x, by_x, by_y]
-    own, other, turned = pl.pallas_call(
+    own, other = pl.pallas_call(
         functools.partial(near_kernel, sizes, 2),
-        out_shape=[result, shaped((count, panel_width), bf16), shaped((2, *factor_inverse.shape), bf16)],
-        in_specs=[anywhere] * 2 + [vmem] * (len(panels) + layers) + [anywhere],
-        out_specs=[vmem] * 3,
+        out_shape=[result, shaped((count, panel_width), bf16)],
+        in_specs=[anywhere] * 2 + [vmem] * (len(panels) + layers),
+        out_specs=[vmem] * 2,
         scratch_shapes=[
             pltpu.VMEM((count, (owners - 1) * depth), bf16),
             pltpu.VMEM(((owners - 1) * depth, panel_width), bf16),
-            pltpu.VMEM(factor_inverse.shape, f32),
-            pltpu.SemaphoreType.DMA,
         ],
         compiler_params=params,
         cost_estimate=lasting(10**9),
         name="near",
-    )(rows_to_y, columns_to_x, *panels, *posts, in_hbm(factor_inverse))
+    )(rows_to_y, columns_to_x, *panels, *posts)
     other = shift(other, 0, 0, 1)
     joined = pl.pallas_call(
         join_kernel,
@@ -476,15 +489,23 @@
     )(across_y, across_x)
     other_joined = shift(joined, 0, 0, 1)
     far_scratch = [pltpu.VMEM((count, depth), bf16)] + [pltpu.VMEM((depth, panel_width), bf16)] * 2
+    far = pl.pallas_call(
+        functools.partial(far_kernel, sizes),
+        out_shape=result,
+        in_specs=[vmem] * 2,
+        out_specs=vmem,
+        scratch_shapes=far_scratch,
+        compiler_params=params,
+        name="far",
+    )(joined, turned)
     middle = pl.pallas_call(
-        functools.partial(middle_kernel, sizes),
+        middle_kernel,
         out_shape=result,
         in_specs=[vmem] * 4,
         out_specs=vmem,
-        scratch_shapes=far_scratch,
         compiler_params=params,
         name="middle",
-    )(own, other, joined, turned)
+    )(far, own, other, turned)
     out = pl.pallas_call(
         functools.partial(final_kernel, sizes),
         out_shape=result,

time: 31.5 us -> 32 us (1.016)
  Pallas kernels: 7.21 us -> 8.73 us
  starting transfers between devices: 19.6 us -> 18.7 us
    pallas_call x1 -> x3, Pallas kernels: 1.7 us -> 3.57 us  [the longest x1 1.57 us: local(): pl.pallas_call(turn_kernel, out_shape=shaped((2, *factor_inverse.shape),...]
    ppermute x14, starting transfers between devices: 19.6 us -> 18.7 us  [shift(): return lax.ppermute(value, ('rows', 'cols'), pairs)]
    pallas_call x1, Pallas kernels: 1.8 us -> 1.45 us  [local(): pl.pallas_call(functools.partial(near_kernel, sizes, 2), out_shape=[resul...]
  transfers between devices with their start and end apart: 14 -> 14, of which waited for: 7 -> 8; matrix products, arithmetic and copies ran while one was open for 0% -> 0% of each run, Pallas kernels for 12% -> 17%
where the time goes in v17:
time: 32 us; the launch traced here: 31.7 us
  starting transfers between devices  18.7 us (58%)
  Pallas kernels  8.73 us (27%)
  waiting for transfers between devices  4.21 us (13%)
    ppermute x14, starting transfers between devices, shift(): return lax.ppermute(value, ('rows', 'cols'), pairs)  18.7 us
    ppermute x14, waiting for transfers between devices, shift(): return lax.ppermute(value, ('rows', 'cols'), pairs)  4.21 us
    pallas_call x1, Pallas kernels, local(): pl.pallas_call(functools.partial(final_kernel, sizes), out_shape=result,...  1.86 us
    pallas_call x1, Pallas kernels, local(): pl.pallas_call(turn_kernel, out_shape=shaped((2, *factor_inverse.shape),...  1.57 us
    pallas_call x1, Pallas kernels, local(): pl.pallas_call(functools.partial(pack_kernel, sizes), out_shape=[shaped((...  1.57 us
    pallas_call x1, Pallas kernels, local(): pl.pallas_call(functools.partial(near_kernel, sizes, 2), out_shape=[resul...  1.45 us
    pallas_call x1, Pallas kernels, local(): pl.pallas_call(middle_kernel, out_shape=result, in_specs=[vmem] * 4, out_...  1.09 us
    pallas_call x1, Pallas kernels, local(): pl.pallas_call(functools.partial(far_kernel, sizes), out_shape=result, in...  0.9 us
  transfers between devices with their start and end apart: 14, of which 8 were waited for; matrix products, arithmetic and copies ran while one was open for 0% of the time, Pallas kernels for 17%

profile of v17, /device:TPU:0, one launch (start us, length us, event | category | flops | bytes accessed | tf_op | source)
XLA Modules:
  0.0 31.7 jit_solution(2614946999261310767)
XLA Ops:
  0.0 1.6 %pack.1 = (bf16[64,512]{1,0:T(8,128)(2,1)S(1)}, bf16[64,384]{1,0:T(8,128)(2,1)S(1)}, bf16[64,896]{1,0:T(8,128)(2,1)S(1)}, bf16[64,640]{1,0:T(8,128)(2,1)S(1)}) custom-call(s32[2,4]{1,0:T(2,128)} %lists_hbm.1, s32[2,4]{1,0:T(2,128)} %masks_hbm.1, s32[96]{0:T(128)} %order_hbm.1, f32[1,64]{1,0:T(1,128)} %bitcast.2, bf16[64,512]{1,0:T(8,128)(2,1)} %panel_hbm.1, ...), custom_call_target="tpu_custom_call" | custom-call | tf_op jit(solution)/shard_map/pack/pallas_call | solution.py:386
  1.6 3.1 %collective-permute-start.3 = (bf16[64,512]{1,0:T(8,128)(2,1)S(1)}, bf16[64,512]{1,0:T(8,128)(2,1)S(1)}, u32[]{:S(2)}, u32[]{:S(2)}) collective-permute-start(bf16[64,512]{1,0:T(8,128)(2,1)S(1)} %get-tuple-element.18.refs_3_), channel_id=1, source_target_pairs={{0,8},{1,9},{2,10},{3,11},{4,12},{5,13},{6,14},{7,15},{8,16},{9,17... | collective-permute-start | bytes 196616 | tf_op jit(solution)/shard_map/ppermute | solution.py:91
  4.7 2.6 %collective-permute-start.2 = (bf16[64,512]{1,0:T(8,128)(2,1)S(1)}, bf16[64,512]{1,0:T(8,128)(2,1)S(1)}, u32[]{:S(2)}, u32[]{:S(2)}) collective-permute-start(bf16[64,512]{1,0:T(8,128)(2,1)S(1)} %get-tuple-element.18.refs_3_), channel_id=1, source_target_pairs={{0,16},{1,17},{2,18},{3,19},{4,20},{5,21},{6,22},{7,23},{8,24},{9,... | collective-permute-start | bytes 196616 | tf_op jit(solution)/shard_map/ppermute | solution.py:91
  7.2 1.3 %collective-permute-start.1 = (bf16[64,512]{1,0:T(8,128)(2,1)S(1)}, bf16[64,512]{1,0:T(8,128)(2,1)S(1)}, u32[]{:S(2)}, u32[]{:S(2)}) collective-permute-start(bf16[64,512]{1,0:T(8,128)(2,1)S(1)} %get-tuple-element.18.refs_3_), channel_id=1, source_target_pairs={{0,24},{1,25},{2,26},{3,27},{4,28},{5,29},{6,30},{7,31},{8,0},{9,1... | collective-permute-start | bytes 196616 | tf_op jit(solution)/shard_map/ppermute | solution.py:91
  8.6 1.5 %collective-permute-start.6 = (bf16[64,640]{1,0:T(8,128)(2,1)S(1)}, bf16[64,640]{1,0:T(8,128)(2,1)S(1)}, u32[]{:S(2)}, u32[]{:S(2)}) collective-permute-start(bf16[64,640]{1,0:T(8,128)(2,1)S(1)} %get-tuple-element.21), channel_id=1, source_target_pairs={{0,2},{1,3},{2,0},{3,1},{4,6},{5,7},{6,4},{7,5},{8,10},{9,11},{10,... | collective-permute-start | bytes 245768 | tf_op jit(solution)/shard_map/ppermute | solution.py:91
  10.1 1.5 %collective-permute-start = (bf16[64,896]{1,0:T(8,128)(2,1)S(1)}, bf16[64,896]{1,0:T(8,128)(2,1)S(1)}, u32[]{:S(2)}, u32[]{:S(2)}) collective-permute-start(bf16[64,896]{1,0:T(8,128)(2,1)S(1)} %get-tuple-element.17), channel_id=1, source_target_pairs={{0,1},{1,0},{2,3},{3,2},{4,5},{5,4},{6,7},{7,6},{8,9},{9,8},{10,11... | collective-permute-start | bytes 344072 | tf_op jit(solution)/shard_map/ppermute | solution.py:91
  11.6 0.1 collective-permute-done.2.refs_1_
  11.7 0.2 collective-permute-done.1.refs_0_
  12.0 1.6 %collective-permute-start.4 = (bf16[192,512]{1,0:T(8,128)(2,1)S(1)}, bf16[192,512]{1,0:T(8,128)(2,1)S(1)}, u32[]{:S(2)}, u32[]{:S(2)}) collective-permute-start(bf16[192,512]{1,0:T(8,128)(2,1)S(1)} %get-tuple-element.19), channel_id=1, source_target_pairs={{0,1},{1,0},{2,3},{3,2},{4,5},{5,4},{6,7},{7,6},{8,9},{9,8},{10,11... | collective-permute-start | bytes 589832 | tf_op jit(solution)/shard_map/ppermute | solution.py:91
  13.6 1.5 %collective-permute-start.10 = (bf16[256,512]{1,0:T(8,128)(2,1)S(1)}, bf16[256,512]{1,0:T(8,128)(2,1)S(1)}, u32[]{:S(2)}, u32[]{:S(2)}) collective-permute-start(bf16[256,512]{1,0:T(8,128)(2,1)S(1)} %get-tuple-element.26.refs_2_), channel_id=1, source_target_pairs={{0,2},{1,3},{2,0},{3,1},{4,6},{5,7},{6,4},{7,5},{8,10},{9,11},{10,... | collective-permute-start | bytes 786440 | tf_op jit(solution)/shard_map/ppermute | solution.py:91
  15.1 0.0 collective-permute-done.6.from_y_ref
  15.1 0.5 %collective-permute-done.from_x_ref.refs_3_ = bf16[64,896]{1,0:T(8,128)(2,1)S(1)} collective-permute-done((bf16[64,896]{1,0:T(8,128)(2,1)S(1)}, bf16[64,896]{1,0:T(8,128)(2,1)S(1)}, u32[]{:S(2)}, u32[]{:S(2)}) %collective-permute-start) | collective-permute-done | bytes 114720 | tf_op jit(solution)/shard_map/ppermute | solution.py:91
  15.6 0.1 sort.1
  15.8 1.1 %collective-permute-start.7 = (bf16[80,256]{1,0:T(8,128)(2,1)S(1)}, bf16[80,256]{1,0:T(8,128)(2,1)S(1)}, u32[]{:S(2)}, u32[]{:S(2)}) collective-permute-start(bf16[80,256]{1,0:T(8,128)(2,1)S(1)} %get-tuple-element.23), channel_id=1, source_target_pairs={{0,8},{1,9},{2,10},{3,11},{4,12},{5,13},{6,14},{7,15},{8,16},{9,17... | collective-permute-start | bytes 122888 | tf_op jit(solution)/shard_map/ppermute | solution.py:91
  16.8 2.0 %collective-permute-start.8 = (bf16[80,256]{1,0:T(8,128)(2,1)S(1)}, bf16[80,256]{1,0:T(8,128)(2,1)S(1)}, u32[]{:S(2)}, u32[]{:S(2)}) collective-permute-start(bf16[80,256]{1,0:T(8,128)(2,1)S(1)} %get-tuple-element.24), channel_id=1, source_target_pairs={{0,16},{1,17},{2,18},{3,19},{4,20},{5,21},{6,22},{7,23},{8,24},{9,... | collective-permute-start | bytes 122888 | tf_op jit(solution)/shard_map/ppermute | solution.py:91
  18.9 0.8 %collective-permute-start.9 = (bf16[80,256]{1,0:T(8,128)(2,1)S(1)}, bf16[80,256]{1,0:T(8,128)(2,1)S(1)}, u32[]{:S(2)}, u32[]{:S(2)}) collective-permute-start(bf16[80,256]{1,0:T(8,128)(2,1)S(1)} %get-tuple-element.25), channel_id=1, source_target_pairs={{0,24},{1,25},{2,26},{3,27},{4,28},{5,29},{6,30},{7,31},{8,0},{9,1... | collective-permute-start | bytes 122888 | tf_op jit(solution)/shard_map/ppermute | solution.py:91
  19.6 1.6 %turn.1.refs_5_.turned_ref = bf16[2,512,512]{2,1,0:T(8,128)(2,1)S(1)} custom-call(f32[512,512]{1,0:T(8,128)} %factor_hbm.1), custom_call_target="tpu_custom_call" | custom-call | tf_op jit(solution)/shard_map/turn/pallas_call | solution.py:442
  21.2 0.0 collective-permute-done.4.by_x_ref.refs_4_
  21.3 0.2 collective-permute-start.5
  21.5 0.1 collective-permute-done.7.refs_1_.refs_7_
  21.6 0.9 %collective-permute-done.8.refs_2_.refs_8_ = bf16[80,256]{1,0:T(8,128)(2,1)S(1)} collective-permute-done((bf16[80,256]{1,0:T(8,128)(2,1)S(1)}, bf16[80,256]{1,0:T(8,128)(2,1)S(1)}, u32[]{:S(2)}, u32[]{:S(2)}) %collective-permute-start.8) | collective-permute-done | bytes 40992 | tf_op jit(solution)/shard_map/ppermute | solution.py:91
  22.5 0.4 %collective-permute-done.9.refs_3_.refs_9_ = bf16[80,256]{1,0:T(8,128)(2,1)S(1)} collective-permute-done((bf16[80,256]{1,0:T(8,128)(2,1)S(1)}, bf16[80,256]{1,0:T(8,128)(2,1)S(1)}, u32[]{:S(2)}, u32[]{:S(2)}) %collective-permute-start.9) | collective-permute-done | bytes 40992 | tf_op jit(solution)/shard_map/ppermute | solution.py:91
  22.9 0.1 columns_to_x.1.refs_1_
  23.0 1.3 %collective-permute-start.11 = (bf16[48,512]{1,0:T(8,128)(2,1)S(1)}, bf16[48,512]{1,0:T(8,128)(2,1)S(1)}, u32[]{:S(2)}, u32[]{:S(2)}) collective-permute-start(bf16[48,512]{1,0:T(8,128)(2,1)S(1)} %columns_to_x.1.refs_1_), channel_id=1, source_target_pairs={{0,1},{1,0},{2,3},{3,2},{4,5},{5,4},{6,7},{7,6},{8,9},{9,8},{10,11... | collective-permute-start | bytes 147464 | tf_op jit(solution)/shard_map/ppermute | solution.py:91
  24.3 1.4 %near.1 = (f32[768,512]{1,0:T(8,128)S(1)}, bf16[768,512]{1,0:T(8,128)(2,1)S(1)}) custom-call(bf16[256,512]{1,0:T(8,128)(2,1)S(1)} %rows_to_y.1.refs_0_, bf16[48,512]{1,0:T(8,128)(2,1)S(1)} %columns_to_x.1.refs_1_, bf16[256,512]{1,0:T(8,128)(2,1)S(1)} %get-tuple-element.26.refs_2_, bf16[64,896]{1,0:T(8,128)(2,1)S(1)} %collective-permute-done.from_x_ref.refs_3_, ...), custom_call_target="tpu_custom_call" | custom-call | flops 1000000000 | tf_op jit(solution)/shard_map/near/pallas_call | solution.py:467
  25.8 0.1 collective-permute-start.12
  25.9 1.3 %collective-permute-done.11.below_ref = bf16[48,512]{1,0:T(8,128)(2,1)S(1)} collective-permute-done((bf16[48,512]{1,0:T(8,128)(2,1)S(1)}, bf16[48,512]{1,0:T(8,128)(2,1)S(1)}, u32[]{:S(2)}, u32[]{:S(2)}) %collective-permute-start.11) | collective-permute-done | bytes 49184 | tf_op jit(solution)/shard_map/ppermute | solution.py:91
  27.2 0.6 %collective-permute-done.5.above_ref = bf16[256,512]{1,0:T(8,128)(2,1)S(1)} collective-permute-done((bf16[256,512]{1,0:T(8,128)(2,1)S(1)}, bf16[256,512]{1,0:T(8,128)(2,1)S(1)}, u32[]{:S(2)}, u32[]{:S(2)}) %collective-permute-start.5) | collective-permute-done | bytes 262176 | tf_op jit(solution)/shard_map/ppermute | solution.py:91
  27.8 0.1 collective-permute-start.13
  27.9 0.9 %far.1.far_ref = f32[768,512]{1,0:T(8,128)S(1)} custom-call(bf16[304,512]{1,0:T(8,128)(2,1)S(1)} %join.1.joined_ref, bf16[2,512,512]{2,1,0:T(8,128)(2,1)S(1)} %turn.1.refs_5_.turned_ref), custom_call_target="tpu_custom_call" | custom-call | tf_op jit(solution)/shard_map/far/pallas_call | solution.py:492
  28.8 1.1 %middle.1.middle_ref = f32[768,512]{1,0:T(8,128)S(1)} custom-call(f32[768,512]{1,0:T(8,128)S(1)} %far.1.far_ref, f32[768,512]{1,0:T(8,128)S(1)} %get-tuple-element.27.own_ref, bf16[768,512]{1,0:T(8,128)(2,1)S(1)} %collective-permute-done.12.other_ref, bf16[2,512,512]{2,1,0:T(8,128)(2,1)S(1)} %turn.1.refs_5_.turned_ref), custom_call_target="tpu_custom_call" | custom-call | tf_op jit(solution)/shard_map/middle/pallas_call | solution.py:501
  29.9 1.9 %final.1 = f32[768,512]{1,0:T(8,128)} custom-call(f32[768,512]{1,0:T(8,128)S(1)} %middle.1.middle_ref, bf16[304,512]{1,0:T(8,128)(2,1)S(1)} %collective-permute-done.13.joined_ref, bf16[2,512,512]{2,1,0:T(8,128)(2,1)S(1)} %turn.1.refs_5_.turned_ref), custom_call_target="tpu_custom_call" | custom-call | tf_op jit(solution)/shard_map/final/pallas_call | solution.py:509
  (7 shorter events, 0.1 us)
Async XLA Ops:
  1.6 10.0 %collective-permute-start.3 = (bf16[64,512]{1,0:T(8,128)(2,1)S(1)}, bf16[64,512]{1,0:T(8,128)(2,1)S(1)}, u32[]{:S(2)}, u32[]{:S(2)}) collective-permute-start(bf16[64,512]{1,0:T(8,128)(2,1)S(1)} %get-tuple-element.18.refs_3_), channel_id=1, source_target_pairs={{0,8},{1,9},{2,10},{3,11},{4,12},{5,13},{6,14},{7,15},{8,16},{9,17... | collective-permute-start | bytes 196616 | tf_op jit(solution)/shard_map/ppermute | solution.py:91
  4.7 7.1 %collective-permute-start.2 = (bf16[64,512]{1,0:T(8,128)(2,1)S(1)}, bf16[64,512]{1,0:T(8,128)(2,1)S(1)}, u32[]{:S(2)}, u32[]{:S(2)}) collective-permute-start(bf16[64,512]{1,0:T(8,128)(2,1)S(1)} %get-tuple-element.18.refs_3_), channel_id=1, source_target_pairs={{0,16},{1,17},{2,18},{3,19},{4,20},{5,21},{6,22},{7,23},{8,24},{9,... | collective-permute-start | bytes 196616 | tf_op jit(solution)/shard_map/ppermute | solution.py:91
  7.2 4.7 %collective-permute-start.1 = (bf16[64,512]{1,0:T(8,128)(2,1)S(1)}, bf16[64,512]{1,0:T(8,128)(2,1)S(1)}, u32[]{:S(2)}, u32[]{:S(2)}) collective-permute-start(bf16[64,512]{1,0:T(8,128)(2,1)S(1)} %get-tuple-element.18.refs_3_), channel_id=1, source_target_pairs={{0,24},{1,25},{2,26},{3,27},{4,28},{5,29},{6,30},{7,31},{8,0},{9,1... | collective-permute-start | bytes 196616 | tf_op jit(solution)/shard_map/ppermute | solution.py:91
  8.6 6.5 %collective-permute-start.6 = (bf16[64,640]{1,0:T(8,128)(2,1)S(1)}, bf16[64,640]{1,0:T(8,128)(2,1)S(1)}, u32[]{:S(2)}, u32[]{:S(2)}) collective-permute-start(bf16[64,640]{1,0:T(8,128)(2,1)S(1)} %get-tuple-element.21), channel_id=1, source_target_pairs={{0,2},{1,3},{2,0},{3,1},{4,6},{5,7},{6,4},{7,5},{8,10},{9,11},{10,... | collective-permute-start | bytes 245768 | tf_op jit(solution)/shard_map/ppermute | solution.py:91
  10.1 5.5 %collective-permute-start = (bf16[64,896]{1,0:T(8,128)(2,1)S(1)}, bf16[64,896]{1,0:T(8,128)(2,1)S(1)}, u32[]{:S(2)}, u32[]{:S(2)}) collective-permute-start(bf16[64,896]{1,0:T(8,128)(2,1)S(1)} %get-tuple-element.17), channel_id=1, source_target_pairs={{0,1},{1,0},{2,3},{3,2},{4,5},{5,4},{6,7},{7,6},{8,9},{9,8},{10,11... | collective-permute-start | bytes 344072 | tf_op jit(solution)/shard_map/ppermute | solution.py:91
  12.0 9.2 %collective-permute-start.4 = (bf16[192,512]{1,0:T(8,128)(2,1)S(1)}, bf16[192,512]{1,0:T(8,128)(2,1)S(1)}, u32[]{:S(2)}, u32[]{:S(2)}) collective-permute-start(bf16[192,512]{1,0:T(8,128)(2,1)S(1)} %get-tuple-element.19), channel_id=1, source_target_pairs={{0,1},{1,0},{2,3},{3,2},{4,5},{5,4},{6,7},{7,6},{8,9},{9,8},{10,11... | collective-permute-start | bytes 589832 | tf_op jit(solution)/shard_map/ppermute | solution.py:91
  13.6 9.3 %collective-permute-start.10 = (bf16[256,512]{1,0:T(8,128)(2,1)S(1)}, bf16[256,512]{1,0:T(8,128)(2,1)S(1)}, u32[]{:S(2)}, u32[]{:S(2)}) collective-permute-start(bf16[256,512]{1,0:T(8,128)(2,1)S(1)} %get-tuple-element.26.refs_2_), channel_id=1, source_target_pairs={{0,2},{1,3},{2,0},{3,1},{4,6},{5,7},{6,4},{7,5},{8,10},{9,11},{10,... | collective-permute-start | bytes 786440 | tf_op jit(solution)/shard_map/ppermute | solution.py:91
  15.8 5.9 %collective-permute-start.7 = (bf16[80,256]{1,0:T(8,128)(2,1)S(1)}, bf16[80,256]{1,0:T(8,128)(2,1)S(1)}, u32[]{:S(2)}, u32[]{:S(2)}) collective-permute-start(bf16[80,256]{1,0:T(8,128)(2,1)S(1)} %get-tuple-element.23), channel_id=1, source_target_pairs={{0,8},{1,9},{2,10},{3,11},{4,12},{5,13},{6,14},{7,15},{8,16},{9,17... | collective-permute-start | bytes 122888 | tf_op jit(solution)/shard_map/ppermute | solution.py:91
  16.8 5.7 %collective-permute-start.8 = (bf16[80,256]{1,0:T(8,128)(2,1)S(1)}, bf16[80,256]{1,0:T(8,128)(2,1)S(1)}, u32[]{:S(2)}, u32[]{:S(2)}) collective-permute-start(bf16[80,256]{1,0:T(8,128)(2,1)S(1)} %get-tuple-element.24), channel_id=1, source_target_pairs={{0,16},{1,17},{2,18},{3,19},{4,20},{5,21},{6,22},{7,23},{8,24},{9,... | collective-permute-start | bytes 122888 | tf_op jit(solution)/shard_map/ppermute | solution.py:91
  18.9 4.1 %collective-permute-start.9 = (bf16[80,256]{1,0:T(8,128)(2,1)S(1)}, bf16[80,256]{1,0:T(8,128)(2,1)S(1)}, u32[]{:S(2)}, u32[]{:S(2)}) collective-permute-start(bf16[80,256]{1,0:T(8,128)(2,1)S(1)} %get-tuple-element.25), channel_id=1, source_target_pairs={{0,24},{1,25},{2,26},{3,27},{4,28},{5,29},{6,30},{7,31},{8,0},{9,1... | collective-permute-start | bytes 122888 | tf_op jit(solution)/shard_map/ppermute | solution.py:91
  21.3 6.5 %collective-permute-start.5 = (bf16[256,512]{1,0:T(8,128)(2,1)S(1)}, bf16[256,512]{1,0:T(8,128)(2,1)S(1)}, u32[]{:S(2)}, u32[]{:S(2)}) collective-permute-start(bf16[256,512]{1,0:T(8,128)(2,1)S(1)} %rows_to_y.1.refs_0_), channel_id=1, source_target_pairs={{0,2},{1,3},{2,0},{3,1},{4,6},{5,7},{6,4},{7,5},{8,10},{9,11},{10,... | collective-permute-start | bytes 786440 | tf_op jit(solution)/shard_map/ppermute | solution.py:91
  23.0 4.2 %collective-permute-start.11 = (bf16[48,512]{1,0:T(8,128)(2,1)S(1)}, bf16[48,512]{1,0:T(8,128)(2,1)S(1)}, u32[]{:S(2)}, u32[]{:S(2)}) collective-permute-start(bf16[48,512]{1,0:T(8,128)(2,1)S(1)} %columns_to_x.1.refs_1_), channel_id=1, source_target_pairs={{0,1},{1,0},{2,3},{3,2},{4,5},{5,4},{6,7},{7,6},{8,9},{9,8},{10,11... | collective-permute-start | bytes 147464 | tf_op jit(solution)/shard_map/ppermute | solution.py:91
  25.8 3.0 %collective-permute-start.12 = (bf16[768,512]{1,0:T(8,128)(2,1)S(1)}, bf16[768,512]{1,0:T(8,128)(2,1)S(1)}, u32[]{:S(2)}, u32[]{:S(2)}) collective-permute-start(bf16[768,512]{1,0:T(8,128)(2,1)S(1)} %get-tuple-element.28), channel_id=1, source_target_pairs={{0,4},{1,5},{2,6},{3,7},{4,0},{5,1},{6,2},{7,3},{8,12},{9,13},{10,... | collective-permute-start | bytes 2359304 | tf_op jit(solution)/shard_map/ppermute | solution.py:91
  27.8 2.1 %collective-permute-start.13 = (bf16[304,512]{1,0:T(8,128)(2,1)S(1)}, bf16[304,512]{1,0:T(8,128)(2,1)S(1)}, u32[]{:S(2)}, u32[]{:S(2)}) collective-permute-start(bf16[304,512]{1,0:T(8,128)(2,1)S(1)} %join.1.joined_ref), channel_id=1, source_target_pairs={{0,4},{1,5},{2,6},{3,7},{4,0},{5,1},{6,2},{7,3},{8,12},{9,13},{10,... | collective-permute-start | bytes 933896 | tf_op jit(solution)/shard_map/ppermute | solution.py:91

commit v18 on v17

--- a/solution.py
+++ b/solution.py
@@ -95,10 +95,10 @@
     return pl.CostEstimate(flops=flops, bytes_accessed=0, transcendentals=0)
 
 
-def pack_kernel(sizes, lists_hbm, masks_hbm, order_hbm, weights_hbm, panel_hbm, jac_hbm, *refs):
+def pack_kernel(sizes, lists_hbm, masks_hbm, order_hbm, weights_hbm, panel_hbm, jac_hbm, factor_hbm, *refs):
     layers, owners, per_owner, block_count, slot_count, block_rows, tile_width = sizes
-    weighted_ref, kept_ref, to_x_ref, to_y_ref = refs[:4]
-    lists_ref, masks_ref, order_ref, weights_ref, panel_ref, jac_ref, places_ref, turned_ref, sems = refs[4:]
+    weighted_ref, kept_ref, to_x_ref, to_y_ref, factor_ref = refs[:5]
+    lists_ref, masks_ref, order_ref, weights_ref, panel_ref, jac_ref, places_ref, turned_ref, sems = refs[5:]
     copies = [
         pltpu.make_async_copy(order_hbm, order_ref, sems.at[0]),
         pltpu.make_async_copy(lists_hbm, lists_ref, sems.at[1]),
@@ -109,6 +109,8 @@
     ]
     for copy in copies:
         copy.start()
+    factor_copy = pltpu.make_async_copy(factor_hbm, factor_ref, sems.at[6])
+    factor_copy.start()
     f32, bf16 = jnp.float32, jnp.bfloat16
     rows, width = panel_ref.shape
     lane_group = CAP * block_rows
@@ -125,7 +127,6 @@
     column = jnp.sum(jnp.where(row_ids == lane_ids, weights_ref[...], 0.0), axis=1, keepdims=True)
     weighted = (column * panel_ref[...].astype(f32)).astype(bf16)
     weighted_ref[...] = weighted
-    to_x_ref[:, :width] = weighted
 
     for b in range(block_count):
         block = jac_ref[b * block_rows : (b + 1) * block_rows, :].astype(f32)
@@ -146,7 +147,7 @@
     shape = (16, CAP * block_count * block_rows)
     lane, row = lax.broadcasted_iota(jnp.int32, shape, 1), lax.broadcasted_iota(jnp.int32, shape, 0)
     notes = []
-    spots = [(kept_ref, 0), (to_x_ref, width), (to_y_ref, 0), (to_y_ref, post)]
+    spots = [(kept_ref, 0), (to_x_ref, 0), (to_y_ref, 0), (to_y_ref, post)]
     for e, (parcel, start) in enumerate(spots):
         wanted = me_c ^ e
         found = jnp.int32(0)
@@ -177,8 +178,9 @@
                     to = start + k * lane_group + j * block_rows
                     parcel[u * part : (u + 1) * part, to : to + block_rows] = piece
     kept_ref[:16, post:] = notes[0].astype(f32).astype(bf16)
-    to_x_ref[:16, width + post :] = notes[1].astype(f32).astype(bf16)
+    to_x_ref[:16, post:] = notes[1].astype(f32).astype(bf16)
     to_y_ref[:16, 2 * post :] = jnp.where(row == 0, notes[2], notes[3]).astype(f32).astype(bf16)
+    factor_copy.wait()
 
 
 def row_of(block, i):
@@ -195,19 +197,17 @@
 
 
 def stack_kernel(*refs):
-    inputs, (rest_ref, all_ref) = refs[:-2], refs[-2:]
+    inputs, out_ref = refs[:-1], refs[-1]
     rows = inputs[0].shape[0]
     for i, ref in enumerate(reversed(inputs)):
-        all_ref[i * rows : (i + 1) * rows, :] = ref[...]
-        if i:
-            rest_ref[(i - 1) * rows : i * rows, :] = ref[...]
+        out_ref[i * rows : (i + 1) * rows, :] = ref[...]
 
 
 def sort_kernel(sizes, kept_ref, from_x_ref, from_y_ref, *posts):
     layers, width, lane_group, wide = sizes
     post = layers * lane_group
     rows = kept_ref.shape[0]
-    spots = [(kept_ref, 0), (from_x_ref, width), (from_y_ref, 0), (from_y_ref, post)]
+    spots = [(kept_ref, 0), (from_x_ref, 0), (from_y_ref, 0), (from_y_ref, post)]
     notes = [row_of(ref[:16, ref.shape[1] - wide :], int(e == 3)) for e, (ref, start) in enumerate(spots)]
     block = rows_from(notes)
     for k, out in enumerate(posts):
@@ -215,12 +215,6 @@
             piece = ref[:, start + k * lane_group : start + (k + 1) * lane_group]
             out[:rows, e * lane_group : (e + 1) * lane_group] = piece
         out[rows:, :wide] = block
-
-
-def rows_to_y_kernel(from_x_ref, by_x_ref, out_ref):
-    rows = from_x_ref.shape[0]
-    out_ref[:rows, :] = from_x_ref[:, : out_ref.shape[1]]
-    out_ref[rows:, :] = by_x_ref[...]
 
 
 def columns_to_x_kernel(sizes, *refs):
@@ -267,10 +261,7 @@
         low_ref[:, start:stop] = (total - high.astype(f32)).astype(bf16)
 
 
-def turn_kernel(factor_hbm, out_ref, factor_ref, sem):
-    copy = pltpu.make_async_copy(factor_hbm, factor_ref, sem)
-    copy.start()
-    copy.wait()
+def turn_kernel(factor_ref, out_ref):
     turned = factor_ref[...].T
     high = turned.astype(jnp.bfloat16)
     out_ref[0, :, :] = high
@@ -279,7 +270,7 @@
 
 def near_kernel(sizes, earlier, *refs):
     layers, owners, per_owner, block_count, block_rows = sizes
-    panels, posts, refs = refs[earlier : earlier + 4], refs[earlier + 4 : earlier + 4 + layers], refs[earlier + 4 + layers :]
+    panels, posts, refs = refs[earlier : earlier + 3], refs[earlier + 3 : earlier + 3 + layers], refs[earlier + 3 + layers :]
     own_ref, other_ref, placed_ref, rows_ref = refs
     f32, bf16 = jnp.float32, jnp.bfloat16
     rows = block_count * block_rows
@@ -383,14 +374,15 @@
     post = layers * lane_group
     wide = CAP * rows
     sizes = (layers, owners, per_owner, block_count, slot_count, block_rows, tile_width)
-    weighted, kept, to_x, to_y = pl.pallas_call(
+    weighted, kept, to_x, to_y, factor = pl.pallas_call(
         functools.partial(pack_kernel, sizes),
         out_shape=[
             shaped((rows, width), bf16)
-            for width in (panel_width, post + wide, panel_width + post + wide, 2 * post + wide)
-        ],
-        in_specs=[anywhere] * 6,
-        out_specs=[vmem] * 4,
+            for width in (panel_width, post + wide, post + wide, 2 * post + wide)
+        ]
+        + [shaped(factor_inverse.shape, f32)],
+        in_specs=[anywhere] * 7,
+        out_specs=[vmem] * 5,
         scratch_shapes=[
             pltpu.SMEM(tile_lists.shape, jnp.int32),
             pltpu.SMEM(tile_masks.shape, jnp.int32),
@@ -400,20 +392,20 @@
             pltpu.VMEM(jac.shape, bf16),
             pltpu.SMEM(tile_order.shape, jnp.int32),
             pltpu.VMEM((block_count * slot_count * tile_width, block_rows), f32),
-            pltpu.SemaphoreType.DMA((6,)),
+            pltpu.SemaphoreType.DMA((7,)),
         ],
         compiler_params=params,
         name="pack",
-    )(*map(in_hbm, (tile_lists, tile_masks, tile_order, weights.reshape(1, rows), panel_jac, jac)))
+    )(*map(in_hbm, (tile_lists, tile_masks, tile_order, weights.reshape(1, rows), panel_jac, jac, factor_inverse)))
     line = [shift(weighted, k, 0) for k in range(1, layers)]
     from_x, from_y = shift(to_x, 0, 1), shift(to_y, 0, 2)
 
     sizes = (layers, panel_width, lane_group, wide)
-    others, column = pl.pallas_call(
+    column = pl.pallas_call(
         stack_kernel,
-        out_shape=[shaped((height * rows, panel_width), bf16) for height in (layers - 1, layers)],
+        out_shape=shaped((layers * rows, panel_width), bf16),
         in_specs=[vmem] * layers,
-        out_specs=[vmem] * 2,
+        out_specs=vmem,
         compiler_params=params,
         cost_estimate=lasting(10**10),
         name="stack",
@@ -428,26 +420,17 @@
         name="sort",
     )(kept, from_x, from_y)
     posts = [posts[0]] + [shift(posts[k], k, 0) for k in range(1, layers)]
-    by_x, by_y = shift(others, 0, 1), shift(column, 0, 2)
-
-    rows_to_y = pl.pallas_call(
-        rows_to_y_kernel,
-        out_shape=shaped(column.shape, bf16),
-        in_specs=[vmem] * 2,
-        out_specs=vmem,
-        compiler_params=params,
-        name="rows_to_y",
-    )(from_x, by_x)
-    across_y = shift(rows_to_y, 0, 2)
+    by_x, by_y = shift(column, 0, 1), shift(column, 0, 2)
+
+    across_y = shift(by_x, 0, 2)
     turned = pl.pallas_call(
         turn_kernel,
         out_shape=shaped((2, *factor_inverse.shape), bf16),
-        in_specs=[anywhere],
+        in_specs=[vmem],
         out_specs=vmem,
-        scratch_shapes=[pltpu.VMEM(factor_inverse.shape, f32), pltpu.SemaphoreType.DMA],
         compiler_params=params,
         name="turn",
-    )(in_hbm(factor_inverse))
+    )(factor)
     columns_to_x = pl.pallas_call(
         functools.partial(columns_to_x_kernel, (layers, lane_group, wide)),
         out_shape=shaped((rows // 2 + 16, panel_width), bf16),
@@ -463,11 +446,11 @@
     depth = layers * rows
     sizes = (layers, owners, per_owner, block_count, block_rows)
     result = shaped((count, panel_width), f32)
-    panels = [column, from_x, by_x, by_y]
+    panels = [column, by_x, by_y]
     own, other = pl.pallas_call(
-        functools.partial(near_kernel, sizes, 2),
+        functools.partial(near_kernel, sizes, 1),
         out_shape=[result, shaped((count, panel_width), bf16)],
-        in_specs=[anywhere] * 2 + [vmem] * (len(panels) + layers),
+        in_specs=[anywhere] + [vmem] * (len(panels) + layers),
         out_specs=[vmem] * 2,
         scratch_shapes=[
             pltpu.VMEM((count, (owners - 1) * depth), bf16),
@@ -476,7 +459,7 @@
         compiler_params=params,
         cost_estimate=lasting(10**9),
         name="near",
-    )(rows_to_y, columns_to_x, *panels, *posts)
+    )(columns_to_x, *panels, *posts)
     other = shift(other, 0, 0, 1)
     joined = pl.pallas_call(
         join_kernel,

time: 32 us -> 31.3 us (0.978)
  Pallas kernels: 8.73 us -> 7.47 us
  starting transfers between devices: 18.7 us -> 19.1 us
    pallas_call x1, Pallas kernels: 1.57 us -> 0.34 us  [local(): pl.pallas_call(turn_kernel, out_shape=shaped((2, *factor_inverse.shape),...]
    ppermute x14, starting transfers between devices: 18.7 us -> 19.1 us  [shift(): return lax.ppermute(value, ('rows', 'cols'), pairs)]
    pallas_call x3 -> x2, Pallas kernels: 1.5 us -> 1.46 us  [the longest x1 1.45 us: local(): pl.pallas_call(functools.partial(near_kernel, sizes, 1), out_shape=[resul...]
  transfers between devices with their start and end apart: 14 -> 14, of which waited for: 8 -> 6; matrix products, arithmetic and copies ran while one was open for 0% -> 0% of each run, Pallas kernels for 17% -> 13%
where the time goes in v18:
time: 31.3 us; the launch traced here: 31.1 us
  starting transfers between devices  19.1 us (61%)
  Pallas kernels  7.47 us (24%)
  waiting for transfers between devices  4.41 us (14%)
    ppermute x14, starting transfers between devices, shift(): return lax.ppermute(value, ('rows', 'cols'), pairs)  19.1 us
    ppermute x14, waiting for transfers between devices, shift(): return lax.ppermute(value, ('rows', 'cols'), pairs)  4.41 us
    pallas_call x1, Pallas kernels, local(): pl.pallas_call(functools.partial(final_kernel, sizes), out_shape=result,...  1.87 us
    pallas_call x1, Pallas kernels, local(): pl.pallas_call(functools.partial(pack_kernel, sizes), out_shape=[shaped((...  1.58 us
    pallas_call x1, Pallas kernels, local(): pl.pallas_call(functools.partial(near_kernel, sizes, 1), out_shape=[resul...  1.45 us
    pallas_call x1, Pallas kernels, local(): pl.pallas_call(middle_kernel, out_shape=result, in_specs=[vmem] * 4, out_...  1.09 us
    pallas_call x1, Pallas kernels, local(): pl.pallas_call(functools.partial(far_kernel, sizes), out_shape=result, in...  0.9 us
  transfers between devices with their start and end apart: 14, of which 6 were waited for; matrix products, arithmetic and copies ran while one was open for 0% of the time, Pallas kernels for 13%

profile of v18, /device:TPU:0, one launch (start us, length us, event | category | flops | bytes accessed | tf_op | source)
XLA Modules:
  0.0 31.1 jit_solution(13051511209845729658)
XLA Ops:
  0.0 1.6 %pack.1 = (bf16[64,512]{1,0:T(8,128)(2,1)S(1)}, bf16[64,384]{1,0:T(8,128)(2,1)S(1)}, bf16[64,384]{1,0:T(8,128)(2,1)S(1)}, bf16[64,640]{1,0:T(8,128)(2,1)S(1)}, f32[512,512]{1,0:T(8,128)S(1)}) custom-call(s32[2,4]{1,0:T(2,128)} %lists_hbm.1, s32[2,4]{1,0:T(2,128)} %masks_hbm.1, s32[96]{0:T(128)} %order_hbm.1, f32[1,64]{1,0:T(1,128)} %bitcast.2, ...), custom_call_target="tpu_custom_call" | custom-call | tf_op jit(solution)/shard_map/pack/pallas_call | solution.py:377
  1.6 3.1 %collective-permute-start.2 = (bf16[64,512]{1,0:T(8,128)(2,1)S(1)}, bf16[64,512]{1,0:T(8,128)(2,1)S(1)}, u32[]{:S(2)}, u32[]{:S(2)}) collective-permute-start(bf16[64,512]{1,0:T(8,128)(2,1)S(1)} %get-tuple-element.16.refs_3_), channel_id=1, source_target_pairs={{0,8},{1,9},{2,10},{3,11},{4,12},{5,13},{6,14},{7,15},{8,16},{9,17... | collective-permute-start | bytes 196616 | tf_op jit(solution)/shard_map/ppermute | solution.py:91
  4.7 2.6 %collective-permute-start.1 = (bf16[64,512]{1,0:T(8,128)(2,1)S(1)}, bf16[64,512]{1,0:T(8,128)(2,1)S(1)}, u32[]{:S(2)}, u32[]{:S(2)}) collective-permute-start(bf16[64,512]{1,0:T(8,128)(2,1)S(1)} %get-tuple-element.16.refs_3_), channel_id=1, source_target_pairs={{0,16},{1,17},{2,18},{3,19},{4,20},{5,21},{6,22},{7,23},{8,24},{9,... | collective-permute-start | bytes 196616 | tf_op jit(solution)/shard_map/ppermute | solution.py:91
  7.3 1.3 %collective-permute-start = (bf16[64,512]{1,0:T(8,128)(2,1)S(1)}, bf16[64,512]{1,0:T(8,128)(2,1)S(1)}, u32[]{:S(2)}, u32[]{:S(2)}) collective-permute-start(bf16[64,512]{1,0:T(8,128)(2,1)S(1)} %get-tuple-element.16.refs_3_), channel_id=1, source_target_pairs={{0,24},{1,25},{2,26},{3,27},{4,28},{5,29},{6,30},{7,31},{8,0},{9,1... | collective-permute-start | bytes 196616 | tf_op jit(solution)/shard_map/ppermute | solution.py:91
  8.6 1.5 %collective-permute-start.5 = (bf16[64,384]{1,0:T(8,128)(2,1)S(1)}, bf16[64,384]{1,0:T(8,128)(2,1)S(1)}, u32[]{:S(2)}, u32[]{:S(2)}) collective-permute-start(bf16[64,384]{1,0:T(8,128)(2,1)S(1)} %get-tuple-element.18), channel_id=1, source_target_pairs={{0,1},{1,0},{2,3},{3,2},{4,5},{5,4},{6,7},{7,6},{8,9},{9,8},{10,11... | collective-permute-start | bytes 147464 | tf_op jit(solution)/shard_map/ppermute | solution.py:91
  10.1 1.5 %collective-permute-start.6 = (bf16[64,640]{1,0:T(8,128)(2,1)S(1)}, bf16[64,640]{1,0:T(8,128)(2,1)S(1)}, u32[]{:S(2)}, u32[]{:S(2)}) collective-permute-start(bf16[64,640]{1,0:T(8,128)(2,1)S(1)} %get-tuple-element.19), channel_id=1, source_target_pairs={{0,2},{1,3},{2,0},{3,1},{4,6},{5,7},{6,4},{7,5},{8,10},{9,11},{10,... | collective-permute-start | bytes 245768 | tf_op jit(solution)/shard_map/ppermute | solution.py:91
  11.6 0.1 collective-permute-done.1.refs_1_
  11.7 0.2 collective-permute-done.refs_0_
  12.0 1.6 %collective-permute-start.10 = (bf16[256,512]{1,0:T(8,128)(2,1)S(1)}, bf16[256,512]{1,0:T(8,128)(2,1)S(1)}, u32[]{:S(2)}, u32[]{:S(2)}) collective-permute-start(bf16[256,512]{1,0:T(8,128)(2,1)S(1)} %stack.1.refs_1_), channel_id=1, source_target_pairs={{0,2},{1,3},{2,0},{3,1},{4,6},{5,7},{6,4},{7,5},{8,10},{9,11},{10,... | collective-permute-start | bytes 786440 | tf_op jit(solution)/shard_map/ppermute | solution.py:91
  13.6 1.5 %collective-permute-start.3 = (bf16[256,512]{1,0:T(8,128)(2,1)S(1)}, bf16[256,512]{1,0:T(8,128)(2,1)S(1)}, u32[]{:S(2)}, u32[]{:S(2)}) collective-permute-start(bf16[256,512]{1,0:T(8,128)(2,1)S(1)} %stack.1.refs_1_), channel_id=1, source_target_pairs={{0,1},{1,0},{2,3},{3,2},{4,5},{5,4},{6,7},{7,6},{8,9},{9,8},{10,11... | collective-permute-start | bytes 786440 | tf_op jit(solution)/shard_map/ppermute | solution.py:91
  15.1 0.1 sort.1
  15.3 1.6 %collective-permute-start.7 = (bf16[80,256]{1,0:T(8,128)(2,1)S(1)}, bf16[80,256]{1,0:T(8,128)(2,1)S(1)}, u32[]{:S(2)}, u32[]{:S(2)}) collective-permute-start(bf16[80,256]{1,0:T(8,128)(2,1)S(1)} %get-tuple-element.21), channel_id=1, source_target_pairs={{0,8},{1,9},{2,10},{3,11},{4,12},{5,13},{6,14},{7,15},{8,16},{9,17... | collective-permute-start | bytes 122888 | tf_op jit(solution)/shard_map/ppermute | solution.py:91
  16.8 2.0 %collective-permute-start.8 = (bf16[80,256]{1,0:T(8,128)(2,1)S(1)}, bf16[80,256]{1,0:T(8,128)(2,1)S(1)}, u32[]{:S(2)}, u32[]{:S(2)}) collective-permute-start(bf16[80,256]{1,0:T(8,128)(2,1)S(1)} %get-tuple-element.22), channel_id=1, source_target_pairs={{0,16},{1,17},{2,18},{3,19},{4,20},{5,21},{6,22},{7,23},{8,24},{9,... | collective-permute-start | bytes 122888 | tf_op jit(solution)/shard_map/ppermute | solution.py:91
  18.9 0.4 %collective-permute-start.9 = (bf16[80,256]{1,0:T(8,128)(2,1)S(1)}, bf16[80,256]{1,0:T(8,128)(2,1)S(1)}, u32[]{:S(2)}, u32[]{:S(2)}) collective-permute-start(bf16[80,256]{1,0:T(8,128)(2,1)S(1)} %get-tuple-element.23), channel_id=1, source_target_pairs={{0,24},{1,25},{2,26},{3,27},{4,28},{5,29},{6,30},{7,31},{8,0},{9,1... | collective-permute-start | bytes 122888 | tf_op jit(solution)/shard_map/ppermute | solution.py:91
  19.3 0.3 %turn.1.refs_5_.turned_ref = bf16[2,512,512]{2,1,0:T(8,128)(2,1)S(1)} custom-call(f32[512,512]{1,0:T(8,128)S(1)} %get-tuple-element.24.factor_ref), custom_call_target="tpu_custom_call" | custom-call | tf_op jit(solution)/shard_map/turn/pallas_call | solution.py:426
  19.6 0.7 %collective-permute-done.3.refs_2_ = bf16[256,512]{1,0:T(8,128)(2,1)S(1)} collective-permute-done((bf16[256,512]{1,0:T(8,128)(2,1)S(1)}, bf16[256,512]{1,0:T(8,128)(2,1)S(1)}, u32[]{:S(2)}, u32[]{:S(2)}) %collective-permute-start.3) | collective-permute-done | bytes 262176 | tf_op jit(solution)/shard_map/ppermute | solution.py:91
  20.4 1.2 %collective-permute-start.4 = (bf16[256,512]{1,0:T(8,128)(2,1)S(1)}, bf16[256,512]{1,0:T(8,128)(2,1)S(1)}, u32[]{:S(2)}, u32[]{:S(2)}) collective-permute-start(bf16[256,512]{1,0:T(8,128)(2,1)S(1)} %collective-permute-done.3.refs_2_), channel_id=1, source_target_pairs={{0,2},{1,3},{2,0},{3,1},{4,6},{5,7},{6,4},{7,5},{8,10},{9,11},{10,... | collective-permute-start | bytes 786440 | tf_op jit(solution)/shard_map/ppermute | solution.py:91
  21.6 0.0 collective-permute-done.7.refs_1_.refs_5_
  21.6 0.5 %collective-permute-done.8.refs_2_.refs_6_ = bf16[80,256]{1,0:T(8,128)(2,1)S(1)} collective-permute-done((bf16[80,256]{1,0:T(8,128)(2,1)S(1)}, bf16[80,256]{1,0:T(8,128)(2,1)S(1)}, u32[]{:S(2)}, u32[]{:S(2)}) %collective-permute-start.8) | collective-permute-done | bytes 40992 | tf_op jit(solution)/shard_map/ppermute | solution.py:91
  22.1 0.7 %collective-permute-done.9.refs_3_.refs_7_ = bf16[80,256]{1,0:T(8,128)(2,1)S(1)} collective-permute-done((bf16[80,256]{1,0:T(8,128)(2,1)S(1)}, bf16[80,256]{1,0:T(8,128)(2,1)S(1)}, u32[]{:S(2)}, u32[]{:S(2)}) %collective-permute-start.9) | collective-permute-done | bytes 40992 | tf_op jit(solution)/shard_map/ppermute | solution.py:91
  22.9 0.0 collective-permute-done.10.refs_4_.refs_3_
  22.9 0.1 columns_to_x.1.refs_0_
  23.0 0.6 %collective-permute-start.11 = (bf16[48,512]{1,0:T(8,128)(2,1)S(1)}, bf16[48,512]{1,0:T(8,128)(2,1)S(1)}, u32[]{:S(2)}, u32[]{:S(2)}) collective-permute-start(bf16[48,512]{1,0:T(8,128)(2,1)S(1)} %columns_to_x.1.refs_0_), channel_id=1, source_target_pairs={{0,1},{1,0},{2,3},{3,2},{4,5},{5,4},{6,7},{7,6},{8,9},{9,8},{10,11... | collective-permute-start | bytes 147464 | tf_op jit(solution)/shard_map/ppermute | solution.py:91
  23.6 1.4 %near.1 = (f32[768,512]{1,0:T(8,128)S(1)}, bf16[768,512]{1,0:T(8,128)(2,1)S(1)}) custom-call(bf16[48,512]{1,0:T(8,128)(2,1)S(1)} %columns_to_x.1.refs_0_, bf16[256,512]{1,0:T(8,128)(2,1)S(1)} %stack.1.refs_1_, bf16[256,512]{1,0:T(8,128)(2,1)S(1)} %collective-permute-done.3.refs_2_, bf16[256,512]{1,0:T(8,128)(2,1)S(1)} %collective-permute-done.10.refs_4_.refs_3_, ...), custom_call_target="tpu_custom_call" | custom-call | flops 1000000000 | tf_op jit(solution)/shard_map/near/pallas_call | solution.py:450
  25.0 0.1 collective-permute-start.12
  25.1 2.0 %collective-permute-done.11.below_ref = bf16[48,512]{1,0:T(8,128)(2,1)S(1)} collective-permute-done((bf16[48,512]{1,0:T(8,128)(2,1)S(1)}, bf16[48,512]{1,0:T(8,128)(2,1)S(1)}, u32[]{:S(2)}, u32[]{:S(2)}) %collective-permute-start.11) | collective-permute-done | bytes 49184 | tf_op jit(solution)/shard_map/ppermute | solution.py:91
  27.1 0.1 collective-permute-start.13
  27.2 0.9 %far.1.far_ref = f32[768,512]{1,0:T(8,128)S(1)} custom-call(bf16[304,512]{1,0:T(8,128)(2,1)S(1)} %join.1.joined_ref, bf16[2,512,512]{2,1,0:T(8,128)(2,1)S(1)} %turn.1.refs_5_.turned_ref), custom_call_target="tpu_custom_call" | custom-call | tf_op jit(solution)/shard_map/far/pallas_call | solution.py:475
  28.1 0.0 collective-permute-done.12.other_ref
  28.1 1.1 %middle.1.middle_ref = f32[768,512]{1,0:T(8,128)S(1)} custom-call(f32[768,512]{1,0:T(8,128)S(1)} %far.1.far_ref, f32[768,512]{1,0:T(8,128)S(1)} %get-tuple-element.25.own_ref, bf16[768,512]{1,0:T(8,128)(2,1)S(1)} %collective-permute-done.12.other_ref, bf16[2,512,512]{2,1,0:T(8,128)(2,1)S(1)} %turn.1.refs_5_.turned_ref), custom_call_target="tpu_custom_call" | custom-call | tf_op jit(solution)/shard_map/middle/pallas_call | solution.py:484
  29.2 0.0 collective-permute-done.13.joined_ref
  29.3 1.9 %final.1 = f32[768,512]{1,0:T(8,128)} custom-call(f32[768,512]{1,0:T(8,128)S(1)} %middle.1.middle_ref, bf16[304,512]{1,0:T(8,128)(2,1)S(1)} %collective-permute-done.13.joined_ref, bf16[2,512,512]{2,1,0:T(8,128)(2,1)S(1)} %turn.1.refs_5_.turned_ref), custom_call_target="tpu_custom_call" | custom-call | tf_op jit(solution)/shard_map/final/pallas_call | solution.py:492
  (6 shorter events, 0.0 us)
Async XLA Ops:
  1.6 10.0 %collective-permute-start.2 = (bf16[64,512]{1,0:T(8,128)(2,1)S(1)}, bf16[64,512]{1,0:T(8,128)(2,1)S(1)}, u32[]{:S(2)}, u32[]{:S(2)}) collective-permute-start(bf16[64,512]{1,0:T(8,128)(2,1)S(1)} %get-tuple-element.16.refs_3_), channel_id=1, source_target_pairs={{0,8},{1,9},{2,10},{3,11},{4,12},{5,13},{6,14},{7,15},{8,16},{9,17... | collective-permute-start | bytes 196616 | tf_op jit(solution)/shard_map/ppermute | solution.py:91
  4.7 7.1 %collective-permute-start.1 = (bf16[64,512]{1,0:T(8,128)(2,1)S(1)}, bf16[64,512]{1,0:T(8,128)(2,1)S(1)}, u32[]{:S(2)}, u32[]{:S(2)}) collective-permute-start(bf16[64,512]{1,0:T(8,128)(2,1)S(1)} %get-tuple-element.16.refs_3_), channel_id=1, source_target_pairs={{0,16},{1,17},{2,18},{3,19},{4,20},{5,21},{6,22},{7,23},{8,24},{9,... | collective-permute-start | bytes 196616 | tf_op jit(solution)/shard_map/ppermute | solution.py:91
  7.3 4.7 %collective-permute-start = (bf16[64,512]{1,0:T(8,128)(2,1)S(1)}, bf16[64,512]{1,0:T(8,128)(2,1)S(1)}, u32[]{:S(2)}, u32[]{:S(2)}) collective-permute-start(bf16[64,512]{1,0:T(8,128)(2,1)S(1)} %get-tuple-element.16.refs_3_), channel_id=1, source_target_pairs={{0,24},{1,25},{2,26},{3,27},{4,28},{5,29},{6,30},{7,31},{8,0},{9,1... | collective-permute-start | bytes 196616 | tf_op jit(solution)/shard_map/ppermute | solution.py:91
  8.6 6.5 %collective-permute-start.5 = (bf16[64,384]{1,0:T(8,128)(2,1)S(1)}, bf16[64,384]{1,0:T(8,128)(2,1)S(1)}, u32[]{:S(2)}, u32[]{:S(2)}) collective-permute-start(bf16[64,384]{1,0:T(8,128)(2,1)S(1)} %get-tuple-element.18), channel_id=1, source_target_pairs={{0,1},{1,0},{2,3},{3,2},{4,5},{5,4},{6,7},{7,6},{8,9},{9,8},{10,11... | collective-permute-start | bytes 147464 | tf_op jit(solution)/shard_map/ppermute | solution.py:91
  10.1 5.0 %collective-permute-start.6 = (bf16[64,640]{1,0:T(8,128)(2,1)S(1)}, bf16[64,640]{1,0:T(8,128)(2,1)S(1)}, u32[]{:S(2)}, u32[]{:S(2)}) collective-permute-start(bf16[64,640]{1,0:T(8,128)(2,1)S(1)} %get-tuple-element.19), channel_id=1, source_target_pairs={{0,2},{1,3},{2,0},{3,1},{4,6},{5,7},{6,4},{7,5},{8,10},{9,11},{10,... | collective-permute-start | bytes 245768 | tf_op jit(solution)/shard_map/ppermute | solution.py:91
  12.0 10.9 %collective-permute-start.10 = (bf16[256,512]{1,0:T(8,128)(2,1)S(1)}, bf16[256,512]{1,0:T(8,128)(2,1)S(1)}, u32[]{:S(2)}, u32[]{:S(2)}) collective-permute-start(bf16[256,512]{1,0:T(8,128)(2,1)S(1)} %stack.1.refs_1_), channel_id=1, source_target_pairs={{0,2},{1,3},{2,0},{3,1},{4,6},{5,7},{6,4},{7,5},{8,10},{9,11},{10,... | collective-permute-start | bytes 786440 | tf_op jit(solution)/shard_map/ppermute | solution.py:91
  13.6 6.8 %collective-permute-start.3 = (bf16[256,512]{1,0:T(8,128)(2,1)S(1)}, bf16[256,512]{1,0:T(8,128)(2,1)S(1)}, u32[]{:S(2)}, u32[]{:S(2)}) collective-permute-start(bf16[256,512]{1,0:T(8,128)(2,1)S(1)} %stack.1.refs_1_), channel_id=1, source_target_pairs={{0,1},{1,0},{2,3},{3,2},{4,5},{5,4},{6,7},{7,6},{8,9},{9,8},{10,11... | collective-permute-start | bytes 786440 | tf_op jit(solution)/shard_map/ppermute | solution.py:91
  15.3 6.4 %collective-permute-start.7 = (bf16[80,256]{1,0:T(8,128)(2,1)S(1)}, bf16[80,256]{1,0:T(8,128)(2,1)S(1)}, u32[]{:S(2)}, u32[]{:S(2)}) collective-permute-start(bf16[80,256]{1,0:T(8,128)(2,1)S(1)} %get-tuple-element.21), channel_id=1, source_target_pairs={{0,8},{1,9},{2,10},{3,11},{4,12},{5,13},{6,14},{7,15},{8,16},{9,17... | collective-permute-start | bytes 122888 | tf_op jit(solution)/shard_map/ppermute | solution.py:91
  16.8 5.3 %collective-permute-start.8 = (bf16[80,256]{1,0:T(8,128)(2,1)S(1)}, bf16[80,256]{1,0:T(8,128)(2,1)S(1)}, u32[]{:S(2)}, u32[]{:S(2)}) collective-permute-start(bf16[80,256]{1,0:T(8,128)(2,1)S(1)} %get-tuple-element.22), channel_id=1, source_target_pairs={{0,16},{1,17},{2,18},{3,19},{4,20},{5,21},{6,22},{7,23},{8,24},{9,... | collective-permute-start | bytes 122888 | tf_op jit(solution)/shard_map/ppermute | solution.py:91
  18.9 4.0 %collective-permute-start.9 = (bf16[80,256]{1,0:T(8,128)(2,1)S(1)}, bf16[80,256]{1,0:T(8,128)(2,1)S(1)}, u32[]{:S(2)}, u32[]{:S(2)}) collective-permute-start(bf16[80,256]{1,0:T(8,128)(2,1)S(1)} %get-tuple-element.23), channel_id=1, source_target_pairs={{0,24},{1,25},{2,26},{3,27},{4,28},{5,29},{6,30},{7,31},{8,0},{9,1... | collective-permute-start | bytes 122888 | tf_op jit(solution)/shard_map/ppermute | solution.py:91
  20.4 6.7 %collective-permute-start.4 = (bf16[256,512]{1,0:T(8,128)(2,1)S(1)}, bf16[256,512]{1,0:T(8,128)(2,1)S(1)}, u32[]{:S(2)}, u32[]{:S(2)}) collective-permute-start(bf16[256,512]{1,0:T(8,128)(2,1)S(1)} %collective-permute-done.3.refs_2_), channel_id=1, source_target_pairs={{0,2},{1,3},{2,0},{3,1},{4,6},{5,7},{6,4},{7,5},{8,10},{9,11},{10,... | collective-permute-start | bytes 786440 | tf_op jit(solution)/shard_map/ppermute | solution.py:91
  23.0 4.2 %collective-permute-start.11 = (bf16[48,512]{1,0:T(8,128)(2,1)S(1)}, bf16[48,512]{1,0:T(8,128)(2,1)S(1)}, u32[]{:S(2)}, u32[]{:S(2)}) collective-permute-start(bf16[48,512]{1,0:T(8,128)(2,1)S(1)} %columns_to_x.1.refs_0_), channel_id=1, source_target_pairs={{0,1},{1,0},{2,3},{3,2},{4,5},{5,4},{6,7},{7,6},{8,9},{9,8},{10,11... | collective-permute-start | bytes 147464 | tf_op jit(solution)/shard_map/ppermute | solution.py:91
  25.0 3.1 %collective-permute-start.12 = (bf16[768,512]{1,0:T(8,128)(2,1)S(1)}, bf16[768,512]{1,0:T(8,128)(2,1)S(1)}, u32[]{:S(2)}, u32[]{:S(2)}) collective-permute-start(bf16[768,512]{1,0:T(8,128)(2,1)S(1)} %get-tuple-element.26), channel_id=1, source_target_pairs={{0,4},{1,5},{2,6},{3,7},{4,0},{5,1},{6,2},{7,3},{8,12},{9,13},{10,... | collective-permute-start | bytes 2359304 | tf_op jit(solution)/shard_map/ppermute | solution.py:91
  27.1 2.1 %collective-permute-start.13 = (bf16[304,512]{1,0:T(8,128)(2,1)S(1)}, bf16[304,512]{1,0:T(8,128)(2,1)S(1)}, u32[]{:S(2)}, u32[]{:S(2)}) collective-permute-start(bf16[304,512]{1,0:T(8,128)(2,1)S(1)} %join.1.joined_ref), channel_id=1, source_target_pairs={{0,4},{1,5},{2,6},{3,7},{4,0},{5,1},{6,2},{7,3},{8,12},{9,13},{10,... | collective-permute-start | bytes 933896 | tf_op jit(solution)/shard_map/ppermute | solution.py:91

commit v19 on v18

--- a/solution.py
+++ b/solution.py
@@ -131,7 +131,7 @@
     for b in range(block_count):
         block = jac_ref[b * block_rows : (b + 1) * block_rows, :].astype(f32)
         start = b * slot_count * tile_width
-        turned_ref[start : start + slot_count * tile_width, :] = block.T
+        turned_ref[start : start + slot_count * tile_width, :] = block.T.astype(bf16)
 
     for i in range(order_ref.shape[0]):
         places_ref[order_ref[i]] = i
@@ -168,15 +168,16 @@
                 code = jnp.where(chosen[j] // slot_count == b, codes[j], -1)
                 note = jnp.where(here, code, note)
         notes.append(note)
-        for k in range(layers):
-            z = lax.rem(me_z + k, layers)
-            for u in range(2):
-                core = me_core ^ u
-                for j in range(CAP):
-                    first = pl.multiple_of(chosen[j] * tile_width + z * slab + core * part, part)
-                    piece = turned_ref[pl.ds(first, part), :].astype(bf16)
-                    to = start + k * lane_group + j * block_rows
-                    parcel[u * part : (u + 1) * part, to : to + block_rows] = piece
+        for u in range(2):
+            core = me_core ^ u
+            for k in range(0, layers, 2):
+                pieces = []
+                for z in (lax.rem(me_z + k, layers), lax.rem(me_z + k + 1, layers)):
+                    for j in range(CAP):
+                        first = pl.multiple_of(chosen[j] * tile_width + z * slab + core * part, part)
+                        pieces.append(turned_ref[pl.ds(first, part), :])
+                lanes = slice(start + k * lane_group, start + (k + 2) * lane_group)
+                parcel[u * part : (u + 1) * part, lanes] = jnp.concatenate(pieces, axis=1)
     kept_ref[:16, post:] = notes[0].astype(f32).astype(bf16)
     to_x_ref[:16, post:] = notes[1].astype(f32).astype(bf16)
     to_y_ref[:16, 2 * post :] = jnp.where(row == 0, notes[2], notes[3]).astype(f32).astype(bf16)
@@ -293,7 +294,7 @@
         out_ref[...] = gram.astype(out_ref.dtype)
 
 
-def join_kernel(above_ref, below_ref, out_ref):
+def join_kernel(above_ref, below_ref, earlier_ref, out_ref):
     rows = above_ref.shape[0]
     out_ref[:rows, :] = above_ref[...]
     out_ref[rows:, :] = below_ref[...]
@@ -322,17 +323,23 @@
     out_ref[...] = total + jnp.dot(placed, low_ref[...], preferred_element_type=jnp.float32)
 
 
-def middle_kernel(far_ref, own_ref, other_ref, turned_ref, out_ref):
-    f32, bf16 = jnp.float32, jnp.bfloat16
-    width = own_ref.shape[1]
-    gram = own_ref[...] + other_ref[...].astype(f32)
-    high = gram.astype(bf16)
-    low = (gram - high.astype(f32)).astype(bf16)
+def times_inverse(out_ref, terms, turned_ref, added):
+    width = out_ref.shape[1]
     for start, stop in ((0, width // 2), (width // 2, width)):
-        a, b = turned_ref[0, :stop, start:stop], turned_ref[1, :stop, start:stop]
-        total = far_ref[:, start:stop] + jnp.dot(high[:, :stop], a, preferred_element_type=f32)
-        total += jnp.dot(high[:, :stop], b, preferred_element_type=f32)
-        out_ref[:, start:stop] = total + jnp.dot(low[:, :stop], a, preferred_element_type=f32)
+        total = sum(ref[:, start:stop] for ref in added)
+        for i, j in ((0, 0), (0, 1), (1, 0))[: len(terms) + 1]:
+            total += jnp.dot(terms[i][:, :stop], turned_ref[j, :stop, start:stop], preferred_element_type=jnp.float32)
+        out_ref[:, start:stop] = total
+
+
+def own_kernel(own_ref, turned_ref, out_ref):
+    high = own_ref[...].astype(jnp.bfloat16)
+    low = (own_ref[...] - high.astype(jnp.float32)).astype(jnp.bfloat16)
+    times_inverse(out_ref, (high, low), turned_ref, ())
+
+
+def middle_kernel(own_ref, other_ref, far_ref, turned_ref, out_ref):
+    times_inverse(out_ref, (other_ref[...],), turned_ref, (own_ref, far_ref))
 
 
 def final_kernel(sizes, middle_ref, joined_ref, turned_ref, out_hbm, sum_ref, placed_ref, high_ref, low_ref, sems):
@@ -391,7 +398,7 @@
             pltpu.VMEM(panel_jac.shape, bf16),
             pltpu.VMEM(jac.shape, bf16),
             pltpu.SMEM(tile_order.shape, jnp.int32),
-            pltpu.VMEM((block_count * slot_count * tile_width, block_rows), f32),
+            pltpu.VMEM((block_count * slot_count * tile_width, block_rows), bf16),
             pltpu.SemaphoreType.DMA((7,)),
         ],
         compiler_params=params,
@@ -461,15 +468,24 @@
         name="near",
     )(columns_to_x, *panels, *posts)
     other = shift(other, 0, 0, 1)
+    own = pl.pallas_call(
+        own_kernel,
+        out_shape=result,
+        in_specs=[vmem] * 2,
+        out_specs=vmem,
+        compiler_params=params,
+        cost_estimate=lasting(10**9),
+        name="own",
+    )(own, turned)
     joined = pl.pallas_call(
         join_kernel,
         out_shape=shaped((across_y.shape[0] + across_x.shape[0], panel_width), bf16),
-        in_specs=[vmem] * 2,
+        in_specs=[vmem] * 2 + [anywhere],
         out_specs=vmem,
         compiler_params=params,
         cost_estimate=lasting(10**10),
         name="join",
-    )(across_y, across_x)
+    )(across_y, across_x, own)
     other_joined = shift(joined, 0, 0, 1)
     far_scratch = [pltpu.VMEM((count, depth), bf16)] + [pltpu.VMEM((depth, panel_width), bf16)] * 2
     far = pl.pallas_call(
@@ -488,7 +504,7 @@
         out_specs=vmem,
         compiler_params=params,
         name="middle",
-    )(far, own, other, turned)
+    )(own, other, far, turned)
     out = pl.pallas_call(
         functools.partial(final_kernel, sizes),
         out_shape=result,

time: 31.3 us -> 31 us (level)
  Pallas kernels: 7.47 us -> 8.21 us
  waiting for transfers between devices: 4.41 us -> 3.74 us
  starting transfers between devices: 19.1 us -> 18.7 us
    pallas_call x0 -> x1, Pallas kernels: none -> 1.08 us  [local(): pl.pallas_call(own_kernel, out_shape=result, in_specs=[vmem] * 2, out_spe...]
    ppermute x14, waiting for transfers between devices: 4.41 us -> 3.74 us  [shift(): return lax.ppermute(value, ('rows', 'cols'), pairs)]
    ppermute x14, starting transfers between devices: 19.1 us -> 18.7 us  [shift(): return lax.ppermute(value, ('rows', 'cols'), pairs)]
    pallas_call x1, Pallas kernels: 1.09 us -> 0.77 us  [local(): pl.pallas_call(middle_kernel, out_shape=result, in_specs=[vmem] * 4, out_...]
  transfers between devices with their start and end apart: 14 -> 14, of which waited for: 6 -> 7; matrix products, arithmetic and copies ran while one was open for 0% -> 0% of each run, Pallas kernels for 13% -> 16%
where the time goes in v19:
time: 31 us; the launch traced here: 30.8 us
  starting transfers between devices  18.7 us (60%)
  Pallas kernels  8.21 us (26%)
  waiting for transfers between devices  3.74 us (12%)
    ppermute x14, starting transfers between devices, shift(): return lax.ppermute(value, ('rows', 'cols'), pairs)  18.7 us
    ppermute x14, waiting for transfers between devices, shift(): return lax.ppermute(value, ('rows', 'cols'), pairs)  3.74 us
    pallas_call x1, Pallas kernels, local(): pl.pallas_call(functools.partial(final_kernel, sizes), out_shape=result,...  1.86 us
    pallas_call x1, Pallas kernels, local(): pl.pallas_call(functools.partial(pack_kernel, sizes), out_shape=[shaped((...  1.56 us
    pallas_call x1, Pallas kernels, local(): pl.pallas_call(functools.partial(near_kernel, sizes, 1), out_shape=[resul...  1.45 us
    pallas_call x1, Pallas kernels, local(): pl.pallas_call(own_kernel, out_shape=result, in_specs=[vmem] * 2, out_spe...  1.08 us
    pallas_call x1, Pallas kernels, local(): pl.pallas_call(functools.partial(far_kernel, sizes), out_shape=result, in...  0.9 us
    pallas_call x1, Pallas kernels, local(): pl.pallas_call(middle_kernel, out_shape=result, in_specs=[vmem] * 4, out_...  0.77 us
  transfers between devices with their start and end apart: 14, of which 7 were waited for; matrix products, arithmetic and copies ran while one was open for 0% of the time, Pallas kernels for 16%

profile of v19, /device:TPU:0, one launch (start us, length us, event | category | flops | bytes accessed | tf_op | source)
XLA Modules:
  0.0 30.8 jit_solution(16686469455568508351)
XLA Ops:
  0.0 1.6 %pack.1 = (bf16[64,512]{1,0:T(8,128)(2,1)S(1)}, bf16[64,384]{1,0:T(8,128)(2,1)S(1)}, bf16[64,384]{1,0:T(8,128)(2,1)S(1)}, bf16[64,640]{1,0:T(8,128)(2,1)S(1)}, f32[512,512]{1,0:T(8,128)S(1)}) custom-call(s32[2,4]{1,0:T(2,128)} %lists_hbm.1, s32[2,4]{1,0:T(2,128)} %masks_hbm.1, s32[96]{0:T(128)} %order_hbm.1, f32[1,64]{1,0:T(1,128)} %bitcast.2, ...), custom_call_target="tpu_custom_call" | custom-call | tf_op jit(solution)/shard_map/pack/pallas_call | solution.py:384
  1.6 3.1 %collective-permute-start.7 = (bf16[64,512]{1,0:T(8,128)(2,1)S(1)}, bf16[64,512]{1,0:T(8,128)(2,1)S(1)}, u32[]{:S(2)}, u32[]{:S(2)}) collective-permute-start(bf16[64,512]{1,0:T(8,128)(2,1)S(1)} %get-tuple-element.23.refs_3_), channel_id=1, source_target_pairs={{0,8},{1,9},{2,10},{3,11},{4,12},{5,13},{6,14},{7,15},{8,16},{9,17... | collective-permute-start | bytes 196616 | tf_op jit(solution)/shard_map/ppermute | solution.py:91
  4.6 2.6 %collective-permute-start.6 = (bf16[64,512]{1,0:T(8,128)(2,1)S(1)}, bf16[64,512]{1,0:T(8,128)(2,1)S(1)}, u32[]{:S(2)}, u32[]{:S(2)}) collective-permute-start(bf16[64,512]{1,0:T(8,128)(2,1)S(1)} %get-tuple-element.23.refs_3_), channel_id=1, source_target_pairs={{0,16},{1,17},{2,18},{3,19},{4,20},{5,21},{6,22},{7,23},{8,24},{9,... | collective-permute-start | bytes 196616 | tf_op jit(solution)/shard_map/ppermute | solution.py:91
  7.2 1.3 %collective-permute-start.5 = (bf16[64,512]{1,0:T(8,128)(2,1)S(1)}, bf16[64,512]{1,0:T(8,128)(2,1)S(1)}, u32[]{:S(2)}, u32[]{:S(2)}) collective-permute-start(bf16[64,512]{1,0:T(8,128)(2,1)S(1)} %get-tuple-element.23.refs_3_), channel_id=1, source_target_pairs={{0,24},{1,25},{2,26},{3,27},{4,28},{5,29},{6,30},{7,31},{8,0},{9,1... | collective-permute-start | bytes 196616 | tf_op jit(solution)/shard_map/ppermute | solution.py:91
  8.6 1.5 %collective-permute-start = (bf16[64,384]{1,0:T(8,128)(2,1)S(1)}, bf16[64,384]{1,0:T(8,128)(2,1)S(1)}, u32[]{:S(2)}, u32[]{:S(2)}) collective-permute-start(bf16[64,384]{1,0:T(8,128)(2,1)S(1)} %get-tuple-element.17), channel_id=1, source_target_pairs={{0,1},{1,0},{2,3},{3,2},{4,5},{5,4},{6,7},{7,6},{8,9},{9,8},{10,11... | collective-permute-start | bytes 147464 | tf_op jit(solution)/shard_map/ppermute | solution.py:91
  10.1 1.5 %collective-permute-start.1 = (bf16[64,640]{1,0:T(8,128)(2,1)S(1)}, bf16[64,640]{1,0:T(8,128)(2,1)S(1)}, u32[]{:S(2)}, u32[]{:S(2)}) collective-permute-start(bf16[64,640]{1,0:T(8,128)(2,1)S(1)} %get-tuple-element.18), channel_id=1, source_target_pairs={{0,2},{1,3},{2,0},{3,1},{4,6},{5,7},{6,4},{7,5},{8,10},{9,11},{10,... | collective-permute-start | bytes 245768 | tf_op jit(solution)/shard_map/ppermute | solution.py:91
  11.6 0.0 collective-permute-done.7.refs_2_
  11.6 0.1 collective-permute-done.6.refs_1_
  11.7 0.2 collective-permute-done.5.refs_0_
  12.0 1.6 %collective-permute-start.9 = (bf16[256,512]{1,0:T(8,128)(2,1)S(1)}, bf16[256,512]{1,0:T(8,128)(2,1)S(1)}, u32[]{:S(2)}, u32[]{:S(2)}) collective-permute-start(bf16[256,512]{1,0:T(8,128)(2,1)S(1)} %stack.1.refs_1_), channel_id=1, source_target_pairs={{0,1},{1,0},{2,3},{3,2},{4,5},{5,4},{6,7},{7,6},{8,9},{9,8},{10,11... | collective-permute-start | bytes 786440 | tf_op jit(solution)/shard_map/ppermute | solution.py:91
  13.6 1.5 %collective-permute-start.8 = (bf16[256,512]{1,0:T(8,128)(2,1)S(1)}, bf16[256,512]{1,0:T(8,128)(2,1)S(1)}, u32[]{:S(2)}, u32[]{:S(2)}) collective-permute-start(bf16[256,512]{1,0:T(8,128)(2,1)S(1)} %stack.1.refs_1_), channel_id=1, source_target_pairs={{0,2},{1,3},{2,0},{3,1},{4,6},{5,7},{6,4},{7,5},{8,10},{9,11},{10,... | collective-permute-start | bytes 786440 | tf_op jit(solution)/shard_map/ppermute | solution.py:91
  15.1 0.0 collective-permute-done.from_x_ref
  15.1 0.1 sort.1
  15.2 1.6 %collective-permute-start.2 = (bf16[80,256]{1,0:T(8,128)(2,1)S(1)}, bf16[80,256]{1,0:T(8,128)(2,1)S(1)}, u32[]{:S(2)}, u32[]{:S(2)}) collective-permute-start(bf16[80,256]{1,0:T(8,128)(2,1)S(1)} %get-tuple-element.20), channel_id=1, source_target_pairs={{0,8},{1,9},{2,10},{3,11},{4,12},{5,13},{6,14},{7,15},{8,16},{9,17... | collective-permute-start | bytes 122888 | tf_op jit(solution)/shard_map/ppermute | solution.py:91
  16.8 2.0 %collective-permute-start.3 = (bf16[80,256]{1,0:T(8,128)(2,1)S(1)}, bf16[80,256]{1,0:T(8,128)(2,1)S(1)}, u32[]{:S(2)}, u32[]{:S(2)}) collective-permute-start(bf16[80,256]{1,0:T(8,128)(2,1)S(1)} %get-tuple-element.21), channel_id=1, source_target_pairs={{0,16},{1,17},{2,18},{3,19},{4,20},{5,21},{6,22},{7,23},{8,24},{9,... | collective-permute-start | bytes 122888 | tf_op jit(solution)/shard_map/ppermute | solution.py:91
  18.8 0.4 %collective-permute-start.4 = (bf16[80,256]{1,0:T(8,128)(2,1)S(1)}, bf16[80,256]{1,0:T(8,128)(2,1)S(1)}, u32[]{:S(2)}, u32[]{:S(2)}) collective-permute-start(bf16[80,256]{1,0:T(8,128)(2,1)S(1)} %get-tuple-element.22), channel_id=1, source_target_pairs={{0,24},{1,25},{2,26},{3,27},{4,28},{5,29},{6,30},{7,31},{8,0},{9,1... | collective-permute-start | bytes 122888 | tf_op jit(solution)/shard_map/ppermute | solution.py:91
  19.3 0.3 %turn.1.refs_5_.turned_ref = bf16[2,512,512]{2,1,0:T(8,128)(2,1)S(1)} custom-call(f32[512,512]{1,0:T(8,128)S(1)} %get-tuple-element.24.factor_ref), custom_call_target="tpu_custom_call" | custom-call | tf_op jit(solution)/shard_map/turn/pallas_call | solution.py:433
  19.6 0.2 collective-permute-done.9.refs_2_
  19.8 0.8 %collective-permute-start.11 = (bf16[256,512]{1,0:T(8,128)(2,1)S(1)}, bf16[256,512]{1,0:T(8,128)(2,1)S(1)}, u32[]{:S(2)}, u32[]{:S(2)}) collective-permute-start(bf16[256,512]{1,0:T(8,128)(2,1)S(1)} %collective-permute-done.9.refs_2_), channel_id=1, source_target_pairs={{0,2},{1,3},{2,0},{3,1},{4,6},{5,7},{6,4},{7,5},{8,10},{9,11},{10,... | collective-permute-start | bytes 786440 | tf_op jit(solution)/shard_map/ppermute | solution.py:91
  20.6 0.6 %collective-permute-done.2.refs_1_.refs_5_ = bf16[80,256]{1,0:T(8,128)(2,1)S(1)} collective-permute-done((bf16[80,256]{1,0:T(8,128)(2,1)S(1)}, bf16[80,256]{1,0:T(8,128)(2,1)S(1)}, u32[]{:S(2)}, u32[]{:S(2)}) %collective-permute-start.2) | collective-permute-done | bytes 40992 | tf_op jit(solution)/shard_map/ppermute | solution.py:91
  21.2 0.9 %collective-permute-done.3.refs_2_.refs_6_ = bf16[80,256]{1,0:T(8,128)(2,1)S(1)} collective-permute-done((bf16[80,256]{1,0:T(8,128)(2,1)S(1)}, bf16[80,256]{1,0:T(8,128)(2,1)S(1)}, u32[]{:S(2)}, u32[]{:S(2)}) %collective-permute-start.3) | collective-permute-done | bytes 40992 | tf_op jit(solution)/shard_map/ppermute | solution.py:91
  22.1 0.7 %collective-permute-done.4.refs_3_.refs_7_ = bf16[80,256]{1,0:T(8,128)(2,1)S(1)} collective-permute-done((bf16[80,256]{1,0:T(8,128)(2,1)S(1)}, bf16[80,256]{1,0:T(8,128)(2,1)S(1)}, u32[]{:S(2)}, u32[]{:S(2)}) %collective-permute-start.4) | collective-permute-done | bytes 40992 | tf_op jit(solution)/shard_map/ppermute | solution.py:91
  22.9 0.1 columns_to_x.1.refs_0_
  22.9 0.6 %collective-permute-start.12 = (bf16[48,512]{1,0:T(8,128)(2,1)S(1)}, bf16[48,512]{1,0:T(8,128)(2,1)S(1)}, u32[]{:S(2)}, u32[]{:S(2)}) collective-permute-start(bf16[48,512]{1,0:T(8,128)(2,1)S(1)} %columns_to_x.1.refs_0_), channel_id=1, source_target_pairs={{0,1},{1,0},{2,3},{3,2},{4,5},{5,4},{6,7},{7,6},{8,9},{9,8},{10,11... | collective-permute-start | bytes 147464 | tf_op jit(solution)/shard_map/ppermute | solution.py:91
  23.5 1.4 %near.1 = (f32[768,512]{1,0:T(8,128)S(1)}, bf16[768,512]{1,0:T(8,128)(2,1)S(1)}) custom-call(bf16[48,512]{1,0:T(8,128)(2,1)S(1)} %columns_to_x.1.refs_0_, bf16[256,512]{1,0:T(8,128)(2,1)S(1)} %stack.1.refs_1_, bf16[256,512]{1,0:T(8,128)(2,1)S(1)} %collective-permute-done.9.refs_2_, bf16[256,512]{1,0:T(8,128)(2,1)S(1)} %collective-permute-done.8.refs_4_.refs_3_, ...), custom_call_target="tpu_custom_call" | custom-call | flops 1000000000 | tf_op jit(solution)/shard_map/near/pallas_call | solution.py:457
  25.0 0.1 collective-permute-start.10
  25.1 1.1 %own.1.earlier_ref.own_ref = f32[768,512]{1,0:T(8,128)S(1)} custom-call(f32[768,512]{1,0:T(8,128)S(1)} %get-tuple-element.25.own_ref, bf16[2,512,512]{2,1,0:T(8,128)(2,1)S(1)} %turn.1.refs_5_.turned_ref), custom_call_target="tpu_custom_call" | custom-call | flops 1000000000 | tf_op jit(solution)/shard_map/own/pallas_call | solution.py:471
  26.2 0.9 %collective-permute-done.12.below_ref = bf16[48,512]{1,0:T(8,128)(2,1)S(1)} collective-permute-done((bf16[48,512]{1,0:T(8,128)(2,1)S(1)}, bf16[48,512]{1,0:T(8,128)(2,1)S(1)}, u32[]{:S(2)}, u32[]{:S(2)}) %collective-permute-start.12) | collective-permute-done | bytes 49184 | tf_op jit(solution)/shard_map/ppermute | solution.py:91
  27.1 0.1 collective-permute-start.13
  27.2 0.9 %far.1.far_ref = f32[768,512]{1,0:T(8,128)S(1)} custom-call(bf16[304,512]{1,0:T(8,128)(2,1)S(1)} %join.1.joined_ref, bf16[2,512,512]{2,1,0:T(8,128)(2,1)S(1)} %turn.1.refs_5_.turned_ref), custom_call_target="tpu_custom_call" | custom-call | tf_op jit(solution)/shard_map/far/pallas_call | solution.py:491
  28.1 0.8 %middle.1.middle_ref = f32[768,512]{1,0:T(8,128)S(1)} custom-call(f32[768,512]{1,0:T(8,128)S(1)} %own.1.earlier_ref.own_ref, bf16[768,512]{1,0:T(8,128)(2,1)S(1)} %collective-permute-done.10.other_ref, f32[768,512]{1,0:T(8,128)S(1)} %far.1.far_ref, bf16[2,512,512]{2,1,0:T(8,128)(2,1)S(1)} %turn.1.refs_5_.turned_ref), custom_call_target="tpu_custom_call" | custom-call | tf_op jit(solution)/shard_map/middle/pallas_call | solution.py:500
  28.9 1.9 %final.1 = f32[768,512]{1,0:T(8,128)} custom-call(f32[768,512]{1,0:T(8,128)S(1)} %middle.1.middle_ref, bf16[304,512]{1,0:T(8,128)(2,1)S(1)} %collective-permute-done.13.joined_ref, bf16[2,512,512]{2,1,0:T(8,128)(2,1)S(1)} %turn.1.refs_5_.turned_ref), custom_call_target="tpu_custom_call" | custom-call | tf_op jit(solution)/shard_map/final/pallas_call | solution.py:508
  (7 shorter events, 0.1 us)
Async XLA Ops:
  1.6 10.0 %collective-permute-start.7 = (bf16[64,512]{1,0:T(8,128)(2,1)S(1)}, bf16[64,512]{1,0:T(8,128)(2,1)S(1)}, u32[]{:S(2)}, u32[]{:S(2)}) collective-permute-start(bf16[64,512]{1,0:T(8,128)(2,1)S(1)} %get-tuple-element.23.refs_3_), channel_id=1, source_target_pairs={{0,8},{1,9},{2,10},{3,11},{4,12},{5,13},{6,14},{7,15},{8,16},{9,17... | collective-permute-start | bytes 196616 | tf_op jit(solution)/shard_map/ppermute | solution.py:91
  4.6 7.1 %collective-permute-start.6 = (bf16[64,512]{1,0:T(8,128)(2,1)S(1)}, bf16[64,512]{1,0:T(8,128)(2,1)S(1)}, u32[]{:S(2)}, u32[]{:S(2)}) collective-permute-start(bf16[64,512]{1,0:T(8,128)(2,1)S(1)} %get-tuple-element.23.refs_3_), channel_id=1, source_target_pairs={{0,16},{1,17},{2,18},{3,19},{4,20},{5,21},{6,22},{7,23},{8,24},{9,... | collective-permute-start | bytes 196616 | tf_op jit(solution)/shard_map/ppermute | solution.py:91
  7.2 4.7 %collective-permute-start.5 = (bf16[64,512]{1,0:T(8,128)(2,1)S(1)}, bf16[64,512]{1,0:T(8,128)(2,1)S(1)}, u32[]{:S(2)}, u32[]{:S(2)}) collective-permute-start(bf16[64,512]{1,0:T(8,128)(2,1)S(1)} %get-tuple-element.23.refs_3_), channel_id=1, source_target_pairs={{0,24},{1,25},{2,26},{3,27},{4,28},{5,29},{6,30},{7,31},{8,0},{9,1... | collective-permute-start | bytes 196616 | tf_op jit(solution)/shard_map/ppermute | solution.py:91
  8.6 6.5 %collective-permute-start = (bf16[64,384]{1,0:T(8,128)(2,1)S(1)}, bf16[64,384]{1,0:T(8,128)(2,1)S(1)}, u32[]{:S(2)}, u32[]{:S(2)}) collective-permute-start(bf16[64,384]{1,0:T(8,128)(2,1)S(1)} %get-tuple-element.17), channel_id=1, source_target_pairs={{0,1},{1,0},{2,3},{3,2},{4,5},{5,4},{6,7},{7,6},{8,9},{9,8},{10,11... | collective-permute-start | bytes 147464 | tf_op jit(solution)/shard_map/ppermute | solution.py:91
  10.1 5.0 %collective-permute-start.1 = (bf16[64,640]{1,0:T(8,128)(2,1)S(1)}, bf16[64,640]{1,0:T(8,128)(2,1)S(1)}, u32[]{:S(2)}, u32[]{:S(2)}) collective-permute-start(bf16[64,640]{1,0:T(8,128)(2,1)S(1)} %get-tuple-element.18), channel_id=1, source_target_pairs={{0,2},{1,3},{2,0},{3,1},{4,6},{5,7},{6,4},{7,5},{8,10},{9,11},{10,... | collective-permute-start | bytes 245768 | tf_op jit(solution)/shard_map/ppermute | solution.py:91
  12.0 7.9 %collective-permute-start.9 = (bf16[256,512]{1,0:T(8,128)(2,1)S(1)}, bf16[256,512]{1,0:T(8,128)(2,1)S(1)}, u32[]{:S(2)}, u32[]{:S(2)}) collective-permute-start(bf16[256,512]{1,0:T(8,128)(2,1)S(1)} %stack.1.refs_1_), channel_id=1, source_target_pairs={{0,1},{1,0},{2,3},{3,2},{4,5},{5,4},{6,7},{7,6},{8,9},{9,8},{10,11... | collective-permute-start | bytes 786440 | tf_op jit(solution)/shard_map/ppermute | solution.py:91
  13.6 9.3 %collective-permute-start.8 = (bf16[256,512]{1,0:T(8,128)(2,1)S(1)}, bf16[256,512]{1,0:T(8,128)(2,1)S(1)}, u32[]{:S(2)}, u32[]{:S(2)}) collective-permute-start(bf16[256,512]{1,0:T(8,128)(2,1)S(1)} %stack.1.refs_1_), channel_id=1, source_target_pairs={{0,2},{1,3},{2,0},{3,1},{4,6},{5,7},{6,4},{7,5},{8,10},{9,11},{10,... | collective-permute-start | bytes 786440 | tf_op jit(solution)/shard_map/ppermute | solution.py:91
  15.2 6.0 %collective-permute-start.2 = (bf16[80,256]{1,0:T(8,128)(2,1)S(1)}, bf16[80,256]{1,0:T(8,128)(2,1)S(1)}, u32[]{:S(2)}, u32[]{:S(2)}) collective-permute-start(bf16[80,256]{1,0:T(8,128)(2,1)S(1)} %get-tuple-element.20), channel_id=1, source_target_pairs={{0,8},{1,9},{2,10},{3,11},{4,12},{5,13},{6,14},{7,15},{8,16},{9,17... | collective-permute-start | bytes 122888 | tf_op jit(solution)/shard_map/ppermute | solution.py:91
  16.8 5.3 %collective-permute-start.3 = (bf16[80,256]{1,0:T(8,128)(2,1)S(1)}, bf16[80,256]{1,0:T(8,128)(2,1)S(1)}, u32[]{:S(2)}, u32[]{:S(2)}) collective-permute-start(bf16[80,256]{1,0:T(8,128)(2,1)S(1)} %get-tuple-element.21), channel_id=1, source_target_pairs={{0,16},{1,17},{2,18},{3,19},{4,20},{5,21},{6,22},{7,23},{8,24},{9,... | collective-permute-start | bytes 122888 | tf_op jit(solution)/shard_map/ppermute | solution.py:91
  18.8 4.0 %collective-permute-start.4 = (bf16[80,256]{1,0:T(8,128)(2,1)S(1)}, bf16[80,256]{1,0:T(8,128)(2,1)S(1)}, u32[]{:S(2)}, u32[]{:S(2)}) collective-permute-start(bf16[80,256]{1,0:T(8,128)(2,1)S(1)} %get-tuple-element.22), channel_id=1, source_target_pairs={{0,24},{1,25},{2,26},{3,27},{4,28},{5,29},{6,30},{7,31},{8,0},{9,1... | collective-permute-start | bytes 122888 | tf_op jit(solution)/shard_map/ppermute | solution.py:91
  19.8 7.3 %collective-permute-start.11 = (bf16[256,512]{1,0:T(8,128)(2,1)S(1)}, bf16[256,512]{1,0:T(8,128)(2,1)S(1)}, u32[]{:S(2)}, u32[]{:S(2)}) collective-permute-start(bf16[256,512]{1,0:T(8,128)(2,1)S(1)} %collective-permute-done.9.refs_2_), channel_id=1, source_target_pairs={{0,2},{1,3},{2,0},{3,1},{4,6},{5,7},{6,4},{7,5},{8,10},{9,11},{10,... | collective-permute-start | bytes 786440 | tf_op jit(solution)/shard_map/ppermute | solution.py:91
  22.9 4.2 %collective-permute-start.12 = (bf16[48,512]{1,0:T(8,128)(2,1)S(1)}, bf16[48,512]{1,0:T(8,128)(2,1)S(1)}, u32[]{:S(2)}, u32[]{:S(2)}) collective-permute-start(bf16[48,512]{1,0:T(8,128)(2,1)S(1)} %columns_to_x.1.refs_0_), channel_id=1, source_target_pairs={{0,1},{1,0},{2,3},{3,2},{4,5},{5,4},{6,7},{7,6},{8,9},{9,8},{10,11... | collective-permute-start | bytes 147464 | tf_op jit(solution)/shard_map/ppermute | solution.py:91
  25.0 3.1 %collective-permute-start.10 = (bf16[768,512]{1,0:T(8,128)(2,1)S(1)}, bf16[768,512]{1,0:T(8,128)(2,1)S(1)}, u32[]{:S(2)}, u32[]{:S(2)}) collective-permute-start(bf16[768,512]{1,0:T(8,128)(2,1)S(1)} %get-tuple-element.26), channel_id=1, source_target_pairs={{0,4},{1,5},{2,6},{3,7},{4,0},{5,1},{6,2},{7,3},{8,12},{9,13},{10,... | collective-permute-start | bytes 2359304 | tf_op jit(solution)/shard_map/ppermute | solution.py:91
  27.1 1.8 %collective-permute-start.13 = (bf16[304,512]{1,0:T(8,128)(2,1)S(1)}, bf16[304,512]{1,0:T(8,128)(2,1)S(1)}, u32[]{:S(2)}, u32[]{:S(2)}) collective-permute-start(bf16[304,512]{1,0:T(8,128)(2,1)S(1)} %join.1.joined_ref), channel_id=1, source_target_pairs={{0,4},{1,5},{2,6},{3,7},{4,0},{5,1},{6,2},{7,3},{8,12},{9,13},{10,... | collective-permute-start | bytes 933896 | tf_op jit(solution)/shard_map/ppermute | solution.py:91

commit v20 on v19

--- a/solution.py
+++ b/solution.py
@@ -97,8 +97,8 @@
 
 def pack_kernel(sizes, lists_hbm, masks_hbm, order_hbm, weights_hbm, panel_hbm, jac_hbm, factor_hbm, *refs):
     layers, owners, per_owner, block_count, slot_count, block_rows, tile_width = sizes
-    weighted_ref, kept_ref, to_x_ref, to_y_ref, factor_ref = refs[:5]
-    lists_ref, masks_ref, order_ref, weights_ref, panel_ref, jac_ref, places_ref, turned_ref, sems = refs[5:]
+    weighted_ref, parcels, factor_ref = refs[0], refs[1 : 1 + owners], refs[1 + owners]
+    lists_ref, masks_ref, order_ref, weights_ref, panel_ref, jac_ref, places_ref, turned_ref, sems = refs[2 + owners :]
     copies = [
         pltpu.make_async_copy(order_hbm, order_ref, sems.at[0]),
         pltpu.make_async_copy(lists_hbm, lists_ref, sems.at[1]),
@@ -145,10 +145,8 @@
         slots.append((place - owner * per_owner, jnp.where(masks_ref[b, k] == 1, owner, -1)))
 
     shape = (16, CAP * block_count * block_rows)
-    lane, row = lax.broadcasted_iota(jnp.int32, shape, 1), lax.broadcasted_iota(jnp.int32, shape, 0)
-    notes = []
-    spots = [(kept_ref, 0), (to_x_ref, 0), (to_y_ref, 0), (to_y_ref, post)]
-    for e, (parcel, start) in enumerate(spots):
+    lane = lax.broadcasted_iota(jnp.int32, shape, 1)
+    for e, parcel in enumerate(parcels):
         wanted = me_c ^ e
         found = jnp.int32(0)
         chosen = [jnp.int32(0)] * CAP
@@ -167,7 +165,7 @@
                 here = (lane >= at) & (lane < at + block_rows)
                 code = jnp.where(chosen[j] // slot_count == b, codes[j], -1)
                 note = jnp.where(here, code, note)
-        notes.append(note)
+        parcel[:16, post:] = note.astype(f32).astype(bf16)
         for u in range(2):
             core = me_core ^ u
             for k in range(0, layers, 2):
@@ -176,11 +174,8 @@
                     for j in range(CAP):
                         first = pl.multiple_of(chosen[j] * tile_width + z * slab + core * part, part)
                         pieces.append(turned_ref[pl.ds(first, part), :])
-                lanes = slice(start + k * lane_group, start + (k + 2) * lane_group)
+                lanes = slice(k * lane_group, (k + 2) * lane_group)
                 parcel[u * part : (u + 1) * part, lanes] = jnp.concatenate(pieces, axis=1)
-    kept_ref[:16, post:] = notes[0].astype(f32).astype(bf16)
-    to_x_ref[:16, post:] = notes[1].astype(f32).astype(bf16)
-    to_y_ref[:16, 2 * post :] = jnp.where(row == 0, notes[2], notes[3]).astype(f32).astype(bf16)
     factor_copy.wait()
 
 
@@ -204,31 +199,24 @@
         out_ref[i * rows : (i + 1) * rows, :] = ref[...]
 
 
-def sort_kernel(sizes, kept_ref, from_x_ref, from_y_ref, *posts):
-    layers, width, lane_group, wide = sizes
-    post = layers * lane_group
-    rows = kept_ref.shape[0]
-    spots = [(kept_ref, 0), (from_x_ref, 0), (from_y_ref, 0), (from_y_ref, post)]
-    notes = [row_of(ref[:16, ref.shape[1] - wide :], int(e == 3)) for e, (ref, start) in enumerate(spots)]
-    block = rows_from(notes)
+def sort_kernel(sizes, *refs):
+    layers, owners, lane_group = sizes
+    parcels, posts = refs[:owners], refs[owners:]
+    rows, codes_at = parcels[0].shape[0], layers * lane_group
+    block = rows_from([row_of(parcel[:16, codes_at:], 0) for parcel in parcels])
     for k, out in enumerate(posts):
-        for e, (ref, start) in enumerate(spots):
-            piece = ref[:, start + k * lane_group : start + (k + 1) * lane_group]
+        for e, parcel in enumerate(parcels):
+            piece = parcel[:, k * lane_group : (k + 1) * lane_group]
             out[:rows, e * lane_group : (e + 1) * lane_group] = piece
-        out[rows:, :wide] = block
-
-
-def columns_to_x_kernel(sizes, *refs):
-    layers, lane_group, wide = sizes
-    posts, out_ref = refs[:layers], refs[-1]
-    rows = posts[0].shape[0] - 16
-    part = rows // 2
-    for k, ref in enumerate(posts):
-        for u in range(2):
-            piece = ref[u * part : (u + 1) * part, 3 * lane_group : 4 * lane_group]
-            at = (u * layers + k) * lane_group
-            out_ref[:part, at : at + lane_group] = piece
-    out_ref[part:, :wide] = rows_from([row_of(ref[rows:, :wide], 3) for ref in posts])
+        out[rows:, : block.shape[1]] = block
+
+
+def first_kernel(in_ref, out_ref):
+    out_ref[...] = in_ref[: out_ref.shape[0], :]
+
+
+def last_kernel(in_ref, out_ref):
+    out_ref[...] = in_ref[in_ref.shape[0] - out_ref.shape[0] :, :]
 
 
 def place(out_ref, lanes, per_owner, pieces, notes, sizes):
@@ -294,10 +282,19 @@
         out_ref[...] = gram.astype(out_ref.dtype)
 
 
-def join_kernel(above_ref, below_ref, earlier_ref, out_ref):
-    rows = above_ref.shape[0]
-    out_ref[:rows, :] = above_ref[...]
-    out_ref[rows:, :] = below_ref[...]
+def join_kernel(sizes, above_ref, below_ref, *refs):
+    layers, lane_group, wide = sizes
+    posts, out_ref = refs[:layers], refs[-1]
+    half, rows = above_ref.shape[0], posts[0].shape[0] - 16
+    part, depth = rows // 2, 2 * half
+    out_ref[:half, :] = above_ref[...]
+    out_ref[half:depth, :] = below_ref[...]
+    for k, ref in enumerate(posts):
+        for u in range(2):
+            piece = ref[u * part : (u + 1) * part, 3 * lane_group : 4 * lane_group]
+            at = (u * layers + k) * lane_group
+            out_ref[depth : depth + part, at : at + lane_group] = piece
+    out_ref[depth + part :, :wide] = rows_from([row_of(ref[rows:, :wide], 3) for ref in posts])
 
 
 def place_far(sizes, u, ref, placed_ref):
@@ -381,15 +378,13 @@
     post = layers * lane_group
     wide = CAP * rows
     sizes = (layers, owners, per_owner, block_count, slot_count, block_rows, tile_width)
-    weighted, kept, to_x, to_y, factor = pl.pallas_call(
+    weighted, *parcels, factor = pl.pallas_call(
         functools.partial(pack_kernel, sizes),
-        out_shape=[
-            shaped((rows, width), bf16)
-            for width in (panel_width, post + wide, post + wide, 2 * post + wide)
-        ]
+        out_shape=[shaped((rows, panel_width), bf16)]
+        + [shaped((rows, post + wide), bf16)] * owners
         + [shaped(factor_inverse.shape, f32)],
         in_specs=[anywhere] * 7,
-        out_specs=[vmem] * 5,
+        out_specs=[vmem] * (owners + 2),
         scratch_shapes=[
             pltpu.SMEM(tile_lists.shape, jnp.int32),
             pltpu.SMEM(tile_masks.shape, jnp.int32),
@@ -405,9 +400,8 @@
         name="pack",
     )(*map(in_hbm, (tile_lists, tile_masks, tile_order, weights.reshape(1, rows), panel_jac, jac, factor_inverse)))
     line = [shift(weighted, k, 0) for k in range(1, layers)]
-    from_x, from_y = shift(to_x, 0, 1), shift(to_y, 0, 2)
-
-    sizes = (layers, panel_width, lane_group, wide)
+    parcels = [parcels[0]] + [shift(parcels[e], 0, e) for e in range(1, owners)]
+
     column = pl.pallas_call(
         stack_kernel,
         out_shape=shaped((layers * rows, panel_width), bf16),
@@ -418,18 +412,30 @@
         name="stack",
     )(*reversed(line), weighted)
     posts = pl.pallas_call(
-        functools.partial(sort_kernel, sizes),
+        functools.partial(sort_kernel, (layers, owners, lane_group)),
         out_shape=[shaped((rows + 16, owners * lane_group), bf16)] * layers,
-        in_specs=[vmem] * 3,
+        in_specs=[vmem] * owners,
         out_specs=[vmem] * layers,
         compiler_params=params,
         cost_estimate=lasting(10**10),
         name="sort",
-    )(kept, from_x, from_y)
+    )(*parcels)
     posts = [posts[0]] + [shift(posts[k], k, 0) for k in range(1, layers)]
     by_x, by_y = shift(column, 0, 1), shift(column, 0, 2)
 
-    across_y = shift(by_x, 0, 2)
+
+    def cut(kernel, value, name):
+        return pl.pallas_call(
+            kernel,
+            out_shape=shaped((value.shape[0] // 2, panel_width), bf16),
+            in_specs=[vmem],
+            out_specs=vmem,
+            compiler_params=params,
+            name=name,
+        )(value)
+
+    rows_to_y, rows_to_x = cut(first_kernel, by_x, "first"), cut(last_kernel, by_y, "last")
+    across_y, across_x = shift(rows_to_y, 0, 2), shift(rows_to_x, 0, 1)
     turned = pl.pallas_call(
         turn_kernel,
         out_shape=shaped((2, *factor_inverse.shape), bf16),
@@ -438,26 +444,15 @@
         compiler_params=params,
         name="turn",
     )(factor)
-    columns_to_x = pl.pallas_call(
-        functools.partial(columns_to_x_kernel, (layers, lane_group, wide)),
-        out_shape=shaped((rows // 2 + 16, panel_width), bf16),
-        in_specs=[vmem] * layers + [anywhere] * 2,
-        out_specs=vmem,
-        compiler_params=params,
-        cost_estimate=lasting(3 * 10**9),
-        name="columns_to_x",
-    )(*posts, by_y, turned)
-    across_x = shift(columns_to_x, 0, 1)
-
     count = per_owner * slab_width
     depth = layers * rows
     sizes = (layers, owners, per_owner, block_count, block_rows)
     result = shaped((count, panel_width), f32)
     panels = [column, by_x, by_y]
     own, other = pl.pallas_call(
-        functools.partial(near_kernel, sizes, 1),
+        functools.partial(near_kernel, sizes, 3),
         out_shape=[result, shaped((count, panel_width), bf16)],
-        in_specs=[anywhere] + [vmem] * (len(panels) + layers),
+        in_specs=[anywhere] * 3 + [vmem] * (len(panels) + layers),
         out_specs=[vmem] * 2,
         scratch_shapes=[
             pltpu.VMEM((count, (owners - 1) * depth), bf16),
@@ -466,7 +461,7 @@
         compiler_params=params,
         cost_estimate=lasting(10**9),
         name="near",
-    )(columns_to_x, *panels, *posts)
+    )(rows_to_y, rows_to_x, turned, *panels, *posts)
     other = shift(other, 0, 0, 1)
     own = pl.pallas_call(
         own_kernel,
@@ -478,14 +473,14 @@
         name="own",
     )(own, turned)
     joined = pl.pallas_call(
-        join_kernel,
-        out_shape=shaped((across_y.shape[0] + across_x.shape[0], panel_width), bf16),
-        in_specs=[vmem] * 2 + [anywhere],
+        functools.partial(join_kernel, (layers, lane_group, wide)),
+        out_shape=shaped((depth + rows // 2 + 16, panel_width), bf16),
+        in_specs=[vmem] * (2 + layers) + [anywhere],
         out_specs=vmem,
         compiler_params=params,
         cost_estimate=lasting(10**10),
         name="join",
-    )(across_y, across_x, own)
+    )(across_y, across_x, *posts, own)
     other_joined = shift(joined, 0, 0, 1)
     far_scratch = [pltpu.VMEM((count, depth), bf16)] + [pltpu.VMEM((depth, panel_width), bf16)] * 2
     far = pl.pallas_call(

time: 31 us -> 31 us (level)
  waiting for transfers between devices: 3.74 us -> 3.23 us
  starting transfers between devices: 18.7 us -> 19.2 us
    ppermute x14 -> x15, starting transfers between devices: 18.7 us -> 19.2 us  [shift(): return lax.ppermute(value, ('rows', 'cols'), pairs)]
    ppermute x14 -> x15, waiting for transfers between devices: 3.74 us -> 3.23 us  [shift(): return lax.ppermute(value, ('rows', 'cols'), pairs)]
    pallas_call x4 -> x5, Pallas kernels: 1.68 us -> 1.68 us  [the longest x1 1.45 us: local(): pl.pallas_call(functools.partial(near_kernel, sizes, 3), out_shape=[resul...]
  transfers between devices with their start and end apart: 14 -> 15, of which waited for: 7 -> 4; matrix products, arithmetic and copies ran while one was open for 0% -> 0% of each run, Pallas kernels for 16% -> 16%
where the time goes in v20:
time: 31 us; the launch traced here: 30.8 us
  starting transfers between devices  19.2 us (62%)
  Pallas kernels  8.21 us (26%)
  waiting for transfers between devices  3.23 us (10%)
    ppermute x15, starting transfers between devices, shift(): return lax.ppermute(value, ('rows', 'cols'), pairs)  19.2 us
    ppermute x15, waiting for transfers between devices, shift(): return lax.ppermute(value, ('rows', 'cols'), pairs)  3.23 us
    pallas_call x1, Pallas kernels, local(): pl.pallas_call(functools.partial(final_kernel, sizes), out_shape=result,...  1.87 us
    pallas_call x1, Pallas kernels, local(): pl.pallas_call(functools.partial(pack_kernel, sizes), out_shape=[shaped((...  1.55 us
    pallas_call x1, Pallas kernels, local(): pl.pallas_call(functools.partial(near_kernel, sizes, 3), out_shape=[resul...  1.45 us
    pallas_call x1, Pallas kernels, local(): pl.pallas_call(own_kernel, out_shape=result, in_specs=[vmem] * 2, out_spe...  1.08 us
    pallas_call x1, Pallas kernels, local(): pl.pallas_call(functools.partial(far_kernel, sizes), out_shape=result, in...  0.9 us
    pallas_call x1, Pallas kernels, local(): pl.pallas_call(middle_kernel, out_shape=result, in_specs=[vmem] * 4, out_...  0.77 us
  transfers between devices with their start and end apart: 15, of which 4 were waited for; matrix products, arithmetic and copies ran while one was open for 0% of the time, Pallas kernels for 16%

profile of v20, /device:TPU:0, one launch (start us, length us, event | category | flops | bytes accessed | tf_op | source)
XLA Modules:
  0.0 30.8 jit_solution(6253125139344533793)
XLA Ops:
  0.0 1.6 %pack.1 = (bf16[64,512]{1,0:T(8,128)(2,1)S(1)}, bf16[64,384]{1,0:T(8,128)(2,1)S(1)}, bf16[64,384]{1,0:T(8,128)(2,1)S(1)}, bf16[64,384]{1,0:T(8,128)(2,1)S(1)}, b...) custom-call(s32[2,4]{1,0:T(2,128)} %lists_hbm.1, s32[2,4]{1,0:T(2,128)} %masks_hbm.1, s32[96]{0:T(128)} %order_hbm.1, ...), custom_call_target="tpu_custom_call" | custom-call | tf_op jit(solution)/shard_map/pack/pallas_call | solution.py:381
  1.6 3.1 %collective-permute-start.2 = (bf16[64,512]{1,0:T(8,128)(2,1)S(1)}, bf16[64,512]{1,0:T(8,128)(2,1)S(1)}, u32[]{:S(2)}, u32[]{:S(2)}) collective-permute-start(bf16[64,512]{1,0:T(8,128)(2,1)S(1)} %get-tuple-element.17.refs_3_), channel_id=1, source_target_pairs={{0,8},{1,9},{2,10},{3,11},{4,12},{5,13},{6,14},{7,15},{8,16},{9,17... | collective-permute-start | bytes 196616 | tf_op jit(solution)/shard_map/ppermute | solution.py:91
  4.6 2.6 %collective-permute-start.1 = (bf16[64,512]{1,0:T(8,128)(2,1)S(1)}, bf16[64,512]{1,0:T(8,128)(2,1)S(1)}, u32[]{:S(2)}, u32[]{:S(2)}) collective-permute-start(bf16[64,512]{1,0:T(8,128)(2,1)S(1)} %get-tuple-element.17.refs_3_), channel_id=1, source_target_pairs={{0,16},{1,17},{2,18},{3,19},{4,20},{5,21},{6,22},{7,23},{8,24},{9,... | collective-permute-start | bytes 196616 | tf_op jit(solution)/shard_map/ppermute | solution.py:91
  7.2 1.3 %collective-permute-start = (bf16[64,512]{1,0:T(8,128)(2,1)S(1)}, bf16[64,512]{1,0:T(8,128)(2,1)S(1)}, u32[]{:S(2)}, u32[]{:S(2)}) collective-permute-start(bf16[64,512]{1,0:T(8,128)(2,1)S(1)} %get-tuple-element.17.refs_3_), channel_id=1, source_target_pairs={{0,24},{1,25},{2,26},{3,27},{4,28},{5,29},{6,30},{7,31},{8,0},{9,1... | collective-permute-start | bytes 196616 | tf_op jit(solution)/shard_map/ppermute | solution.py:91
  8.6 1.5 %collective-permute-start.5 = (bf16[64,384]{1,0:T(8,128)(2,1)S(1)}, bf16[64,384]{1,0:T(8,128)(2,1)S(1)}, u32[]{:S(2)}, u32[]{:S(2)}) collective-permute-start(bf16[64,384]{1,0:T(8,128)(2,1)S(1)} %get-tuple-element.20), channel_id=1, source_target_pairs={{0,1},{1,0},{2,3},{3,2},{4,5},{5,4},{6,7},{7,6},{8,9},{9,8},{10,11... | collective-permute-start | bytes 147464 | tf_op jit(solution)/shard_map/ppermute | solution.py:91
  10.1 1.5 %collective-permute-start.6 = (bf16[64,384]{1,0:T(8,128)(2,1)S(1)}, bf16[64,384]{1,0:T(8,128)(2,1)S(1)}, u32[]{:S(2)}, u32[]{:S(2)}) collective-permute-start(bf16[64,384]{1,0:T(8,128)(2,1)S(1)} %get-tuple-element.21), channel_id=1, source_target_pairs={{0,2},{1,3},{2,0},{3,1},{4,6},{5,7},{6,4},{7,5},{8,10},{9,11},{10,... | collective-permute-start | bytes 147464 | tf_op jit(solution)/shard_map/ppermute | solution.py:91
  11.6 0.0 collective-permute-done.2.refs_2_
  11.6 0.5 %collective-permute-start.7 = (bf16[64,384]{1,0:T(8,128)(2,1)S(1)}, bf16[64,384]{1,0:T(8,128)(2,1)S(1)}, u32[]{:S(2)}, u32[]{:S(2)}) collective-permute-start(bf16[64,384]{1,0:T(8,128)(2,1)S(1)} %get-tuple-element.22), channel_id=1, source_target_pairs={{0,3},{1,2},{2,1},{3,0},{4,7},{5,6},{6,5},{7,4},{8,11},{9,10},{10,... | collective-permute-start | bytes 147464 | tf_op jit(solution)/shard_map/ppermute | solution.py:91
  12.1 1.6 %collective-permute-start.4 = (bf16[256,512]{1,0:T(8,128)(2,1)S(1)}, bf16[256,512]{1,0:T(8,128)(2,1)S(1)}, u32[]{:S(2)}, u32[]{:S(2)}) collective-permute-start(bf16[256,512]{1,0:T(8,128)(2,1)S(1)} %stack.1.refs_3_), channel_id=1, source_target_pairs={{0,2},{1,3},{2,0},{3,1},{4,6},{5,7},{6,4},{7,5},{8,10},{9,11},{10,... | collective-permute-start | bytes 786440 | tf_op jit(solution)/shard_map/ppermute | solution.py:91
  13.7 1.5 %collective-permute-start.3 = (bf16[256,512]{1,0:T(8,128)(2,1)S(1)}, bf16[256,512]{1,0:T(8,128)(2,1)S(1)}, u32[]{:S(2)}, u32[]{:S(2)}) collective-permute-start(bf16[256,512]{1,0:T(8,128)(2,1)S(1)} %stack.1.refs_3_), channel_id=1, source_target_pairs={{0,1},{1,0},{2,3},{3,2},{4,5},{5,4},{6,7},{7,6},{8,9},{9,8},{10,11... | collective-permute-start | bytes 786440 | tf_op jit(solution)/shard_map/ppermute | solution.py:91
  15.2 1.9 %collective-permute-done.7.refs_3_ = bf16[64,384]{1,0:T(8,128)(2,1)S(1)} collective-permute-done((bf16[64,384]{1,0:T(8,128)(2,1)S(1)}, bf16[64,384]{1,0:T(8,128)(2,1)S(1)}, u32[]{:S(2)}, u32[]{:S(2)}) %collective-permute-start.7) | collective-permute-done | bytes 49184 | tf_op jit(solution)/shard_map/ppermute | solution.py:91
  17.1 0.1 sort.1
  17.2 0.4 %collective-permute-start.8 = (bf16[80,256]{1,0:T(8,128)(2,1)S(1)}, bf16[80,256]{1,0:T(8,128)(2,1)S(1)}, u32[]{:S(2)}, u32[]{:S(2)}) collective-permute-start(bf16[80,256]{1,0:T(8,128)(2,1)S(1)} %get-tuple-element.24), channel_id=1, source_target_pairs={{0,8},{1,9},{2,10},{3,11},{4,12},{5,13},{6,14},{7,15},{8,16},{9,17... | collective-permute-start | bytes 122888 | tf_op jit(solution)/shard_map/ppermute | solution.py:91
  17.6 1.3 %collective-permute-start.9 = (bf16[80,256]{1,0:T(8,128)(2,1)S(1)}, bf16[80,256]{1,0:T(8,128)(2,1)S(1)}, u32[]{:S(2)}, u32[]{:S(2)}) collective-permute-start(bf16[80,256]{1,0:T(8,128)(2,1)S(1)} %get-tuple-element.25), channel_id=1, source_target_pairs={{0,16},{1,17},{2,18},{3,19},{4,20},{5,21},{6,22},{7,23},{8,24},{9,... | collective-permute-start | bytes 122888 | tf_op jit(solution)/shard_map/ppermute | solution.py:91
  18.9 2.2 %collective-permute-start.10 = (bf16[80,256]{1,0:T(8,128)(2,1)S(1)}, bf16[80,256]{1,0:T(8,128)(2,1)S(1)}, u32[]{:S(2)}, u32[]{:S(2)}) collective-permute-start(bf16[80,256]{1,0:T(8,128)(2,1)S(1)} %get-tuple-element.26), channel_id=1, source_target_pairs={{0,24},{1,25},{2,26},{3,27},{4,28},{5,29},{6,30},{7,31},{8,0},{9,1... | collective-permute-start | bytes 122888 | tf_op jit(solution)/shard_map/ppermute | solution.py:91
  21.1 0.3 %turn.1.refs_2_.turned_ref = bf16[2,512,512]{2,1,0:T(8,128)(2,1)S(1)} custom-call(f32[512,512]{1,0:T(8,128)S(1)} %get-tuple-element.18.factor_ref), custom_call_target="tpu_custom_call" | custom-call | tf_op jit(solution)/shard_map/turn/pallas_call | solution.py:439
  21.4 0.0 collective-permute-done.4.in_ref.refs_5_
  21.4 0.6 %collective-permute-start.13 = (bf16[128,512]{1,0:T(8,128)(2,1)S(1)}, bf16[128,512]{1,0:T(8,128)(2,1)S(1)}, u32[]{:S(2)}, u32[]{:S(2)}) collective-permute-start(bf16[128,512]{1,0:T(8,128)(2,1)S(1)} %last.1.refs_1_), channel_id=1, source_target_pairs={{0,1},{1,0},{2,3},{3,2},{4,5},{5,4},{6,7},{7,6},{8,9},{9,8},{10,11... | collective-permute-start | bytes 393224 | tf_op jit(solution)/shard_map/ppermute | solution.py:91
  22.0 1.1 %collective-permute-start.12 = (bf16[128,512]{1,0:T(8,128)(2,1)S(1)}, bf16[128,512]{1,0:T(8,128)(2,1)S(1)}, u32[]{:S(2)}, u32[]{:S(2)}) collective-permute-start(bf16[128,512]{1,0:T(8,128)(2,1)S(1)} %first.1.refs_0_), channel_id=1, source_target_pairs={{0,2},{1,3},{2,0},{3,1},{4,6},{5,7},{6,4},{7,5},{8,10},{9,11},{10,... | collective-permute-start | bytes 393224 | tf_op jit(solution)/shard_map/ppermute | solution.py:91
  23.1 0.0 collective-permute-done.8.refs_7_.refs_1_
  23.1 0.0 collective-permute-done.9.refs_8_.refs_2_
  23.1 0.5 %collective-permute-done.10.refs_9_.refs_3_ = bf16[80,256]{1,0:T(8,128)(2,1)S(1)} collective-permute-done((bf16[80,256]{1,0:T(8,128)(2,1)S(1)}, bf16[80,256]{1,0:T(8,128)(2,1)S(1)}, u32[]{:S(2)}, u32[]{:S(2)}) %collective-permute-start.10) | collective-permute-done | bytes 40992 | tf_op jit(solution)/shard_map/ppermute | solution.py:91
  23.6 1.4 %near.1 = (f32[768,512]{1,0:T(8,128)S(1)}, bf16[768,512]{1,0:T(8,128)(2,1)S(1)}) custom-call(bf16[128,512]{1,0:T(8,128)(2,1)S(1)} %first.1.refs_0_, bf16[128,512]{1,0:T(8,128)(2,1)S(1)} %last.1.refs_1_, bf16[2,512,512]{2,1,0:T(8,128)(2,1)S(1)} %turn.1.refs_2_.turned_ref, bf16[256,512]{1,0:T(8,128)(2,1)S(1)} %stack.1.refs_3_, ...), custom_call_target="tpu_custom_call" | custom-call | flops 1000000000 | tf_op jit(solution)/shard_map/near/pallas_call | solution.py:452
  25.1 0.1 collective-permute-start.11
  25.1 1.1 %own.1.refs_4_.own_ref = f32[768,512]{1,0:T(8,128)S(1)} custom-call(f32[768,512]{1,0:T(8,128)S(1)} %get-tuple-element.27.own_ref, bf16[2,512,512]{2,1,0:T(8,128)(2,1)S(1)} %turn.1.refs_2_.turned_ref), custom_call_target="tpu_custom_call" | custom-call | flops 1000000000 | tf_op jit(solution)/shard_map/own/pallas_call | solution.py:466
  26.2 0.2 collective-permute-done.13.below_ref
  26.5 0.6 %collective-permute-done.12.above_ref = bf16[128,512]{1,0:T(8,128)(2,1)S(1)} collective-permute-done((bf16[128,512]{1,0:T(8,128)(2,1)S(1)}, bf16[128,512]{1,0:T(8,128)(2,1)S(1)}, u32[]{:S(2)}, u32[]{:S(2)}) %collective-permute-start.12) | collective-permute-done | bytes 131104 | tf_op jit(solution)/shard_map/ppermute | solution.py:91
  27.1 0.1 join.1.joined_ref
  27.2 0.1 collective-permute-start.14
  27.2 0.9 %far.1.far_ref = f32[768,512]{1,0:T(8,128)S(1)} custom-call(bf16[304,512]{1,0:T(8,128)(2,1)S(1)} %join.1.joined_ref, bf16[2,512,512]{2,1,0:T(8,128)(2,1)S(1)} %turn.1.refs_2_.turned_ref), custom_call_target="tpu_custom_call" | custom-call | tf_op jit(solution)/shard_map/far/pallas_call | solution.py:486
  28.1 0.8 %middle.1.middle_ref = f32[768,512]{1,0:T(8,128)S(1)} custom-call(f32[768,512]{1,0:T(8,128)S(1)} %own.1.refs_4_.own_ref, bf16[768,512]{1,0:T(8,128)(2,1)S(1)} %collective-permute-done.11.other_ref, f32[768,512]{1,0:T(8,128)S(1)} %far.1.far_ref, bf16[2,512,512]{2,1,0:T(8,128)(2,1)S(1)} %turn.1.refs_2_.turned_ref), custom_call_target="tpu_custom_call" | custom-call | tf_op jit(solution)/shard_map/middle/pallas_call | solution.py:495
  28.9 1.9 %final.1 = f32[768,512]{1,0:T(8,128)} custom-call(f32[768,512]{1,0:T(8,128)S(1)} %middle.1.middle_ref, bf16[304,512]{1,0:T(8,128)(2,1)S(1)} %collective-permute-done.14.joined_ref, bf16[2,512,512]{2,1,0:T(8,128)(2,1)S(1)} %turn.1.refs_2_.turned_ref), custom_call_target="tpu_custom_call" | custom-call | tf_op jit(solution)/shard_map/final/pallas_call | solution.py:503
  (10 shorter events, 0.1 us)
Async XLA Ops:
  1.6 10.0 %collective-permute-start.2 = (bf16[64,512]{1,0:T(8,128)(2,1)S(1)}, bf16[64,512]{1,0:T(8,128)(2,1)S(1)}, u32[]{:S(2)}, u32[]{:S(2)}) collective-permute-start(bf16[64,512]{1,0:T(8,128)(2,1)S(1)} %get-tuple-element.17.refs_3_), channel_id=1, source_target_pairs={{0,8},{1,9},{2,10},{3,11},{4,12},{5,13},{6,14},{7,15},{8,16},{9,17... | collective-permute-start | bytes 196616 | tf_op jit(solution)/shard_map/ppermute | solution.py:91
  4.6 7.4 %collective-permute-start.1 = (bf16[64,512]{1,0:T(8,128)(2,1)S(1)}, bf16[64,512]{1,0:T(8,128)(2,1)S(1)}, u32[]{:S(2)}, u32[]{:S(2)}) collective-permute-start(bf16[64,512]{1,0:T(8,128)(2,1)S(1)} %get-tuple-element.17.refs_3_), channel_id=1, source_target_pairs={{0,16},{1,17},{2,18},{3,19},{4,20},{5,21},{6,22},{7,23},{8,24},{9,... | collective-permute-start | bytes 196616 | tf_op jit(solution)/shard_map/ppermute | solution.py:91
  7.2 4.8 %collective-permute-start = (bf16[64,512]{1,0:T(8,128)(2,1)S(1)}, bf16[64,512]{1,0:T(8,128)(2,1)S(1)}, u32[]{:S(2)}, u32[]{:S(2)}) collective-permute-start(bf16[64,512]{1,0:T(8,128)(2,1)S(1)} %get-tuple-element.17.refs_3_), channel_id=1, source_target_pairs={{0,24},{1,25},{2,26},{3,27},{4,28},{5,29},{6,30},{7,31},{8,0},{9,1... | collective-permute-start | bytes 196616 | tf_op jit(solution)/shard_map/ppermute | solution.py:91
  8.6 6.6 %collective-permute-start.5 = (bf16[64,384]{1,0:T(8,128)(2,1)S(1)}, bf16[64,384]{1,0:T(8,128)(2,1)S(1)}, u32[]{:S(2)}, u32[]{:S(2)}) collective-permute-start(bf16[64,384]{1,0:T(8,128)(2,1)S(1)} %get-tuple-element.20), channel_id=1, source_target_pairs={{0,1},{1,0},{2,3},{3,2},{4,5},{5,4},{6,7},{7,6},{8,9},{9,8},{10,11... | collective-permute-start | bytes 147464 | tf_op jit(solution)/shard_map/ppermute | solution.py:91
  10.1 5.1 %collective-permute-start.6 = (bf16[64,384]{1,0:T(8,128)(2,1)S(1)}, bf16[64,384]{1,0:T(8,128)(2,1)S(1)}, u32[]{:S(2)}, u32[]{:S(2)}) collective-permute-start(bf16[64,384]{1,0:T(8,128)(2,1)S(1)} %get-tuple-element.21), channel_id=1, source_target_pairs={{0,2},{1,3},{2,0},{3,1},{4,6},{5,7},{6,4},{7,5},{8,10},{9,11},{10,... | collective-permute-start | bytes 147464 | tf_op jit(solution)/shard_map/ppermute | solution.py:91
  11.6 5.5 %collective-permute-start.7 = (bf16[64,384]{1,0:T(8,128)(2,1)S(1)}, bf16[64,384]{1,0:T(8,128)(2,1)S(1)}, u32[]{:S(2)}, u32[]{:S(2)}) collective-permute-start(bf16[64,384]{1,0:T(8,128)(2,1)S(1)} %get-tuple-element.22), channel_id=1, source_target_pairs={{0,3},{1,2},{2,1},{3,0},{4,7},{5,6},{6,5},{7,4},{8,11},{9,10},{10,... | collective-permute-start | bytes 147464 | tf_op jit(solution)/shard_map/ppermute | solution.py:91
  12.1 9.3 %collective-permute-start.4 = (bf16[256,512]{1,0:T(8,128)(2,1)S(1)}, bf16[256,512]{1,0:T(8,128)(2,1)S(1)}, u32[]{:S(2)}, u32[]{:S(2)}) collective-permute-start(bf16[256,512]{1,0:T(8,128)(2,1)S(1)} %stack.1.refs_3_), channel_id=1, source_target_pairs={{0,2},{1,3},{2,0},{3,1},{4,6},{5,7},{6,4},{7,5},{8,10},{9,11},{10,... | collective-permute-start | bytes 786440 | tf_op jit(solution)/shard_map/ppermute | solution.py:91
  13.7 8.3 %collective-permute-start.3 = (bf16[256,512]{1,0:T(8,128)(2,1)S(1)}, bf16[256,512]{1,0:T(8,128)(2,1)S(1)}, u32[]{:S(2)}, u32[]{:S(2)}) collective-permute-start(bf16[256,512]{1,0:T(8,128)(2,1)S(1)} %stack.1.refs_3_), channel_id=1, source_target_pairs={{0,1},{1,0},{2,3},{3,2},{4,5},{5,4},{6,7},{7,6},{8,9},{9,8},{10,11... | collective-permute-start | bytes 786440 | tf_op jit(solution)/shard_map/ppermute | solution.py:91
  17.2 5.9 %collective-permute-start.8 = (bf16[80,256]{1,0:T(8,128)(2,1)S(1)}, bf16[80,256]{1,0:T(8,128)(2,1)S(1)}, u32[]{:S(2)}, u32[]{:S(2)}) collective-permute-start(bf16[80,256]{1,0:T(8,128)(2,1)S(1)} %get-tuple-element.24), channel_id=1, source_target_pairs={{0,8},{1,9},{2,10},{3,11},{4,12},{5,13},{6,14},{7,15},{8,16},{9,17... | collective-permute-start | bytes 122888 | tf_op jit(solution)/shard_map/ppermute | solution.py:91
  17.6 5.6 %collective-permute-start.9 = (bf16[80,256]{1,0:T(8,128)(2,1)S(1)}, bf16[80,256]{1,0:T(8,128)(2,1)S(1)}, u32[]{:S(2)}, u32[]{:S(2)}) collective-permute-start(bf16[80,256]{1,0:T(8,128)(2,1)S(1)} %get-tuple-element.25), channel_id=1, source_target_pairs={{0,16},{1,17},{2,18},{3,19},{4,20},{5,21},{6,22},{7,23},{8,24},{9,... | collective-permute-start | bytes 122888 | tf_op jit(solution)/shard_map/ppermute | solution.py:91
  18.9 4.8 %collective-permute-start.10 = (bf16[80,256]{1,0:T(8,128)(2,1)S(1)}, bf16[80,256]{1,0:T(8,128)(2,1)S(1)}, u32[]{:S(2)}, u32[]{:S(2)}) collective-permute-start(bf16[80,256]{1,0:T(8,128)(2,1)S(1)} %get-tuple-element.26), channel_id=1, source_target_pairs={{0,24},{1,25},{2,26},{3,27},{4,28},{5,29},{6,30},{7,31},{8,0},{9,1... | collective-permute-start | bytes 122888 | tf_op jit(solution)/shard_map/ppermute | solution.py:91
  21.4 5.0 %collective-permute-start.13 = (bf16[128,512]{1,0:T(8,128)(2,1)S(1)}, bf16[128,512]{1,0:T(8,128)(2,1)S(1)}, u32[]{:S(2)}, u32[]{:S(2)}) collective-permute-start(bf16[128,512]{1,0:T(8,128)(2,1)S(1)} %last.1.refs_1_), channel_id=1, source_target_pairs={{0,1},{1,0},{2,3},{3,2},{4,5},{5,4},{6,7},{7,6},{8,9},{9,8},{10,11... | collective-permute-start | bytes 393224 | tf_op jit(solution)/shard_map/ppermute | solution.py:91
  22.0 5.0 %collective-permute-start.12 = (bf16[128,512]{1,0:T(8,128)(2,1)S(1)}, bf16[128,512]{1,0:T(8,128)(2,1)S(1)}, u32[]{:S(2)}, u32[]{:S(2)}) collective-permute-start(bf16[128,512]{1,0:T(8,128)(2,1)S(1)} %first.1.refs_0_), channel_id=1, source_target_pairs={{0,2},{1,3},{2,0},{3,1},{4,6},{5,7},{6,4},{7,5},{8,10},{9,11},{10,... | collective-permute-start | bytes 393224 | tf_op jit(solution)/shard_map/ppermute | solution.py:91
  25.1 3.1 %collective-permute-start.11 = (bf16[768,512]{1,0:T(8,128)(2,1)S(1)}, bf16[768,512]{1,0:T(8,128)(2,1)S(1)}, u32[]{:S(2)}, u32[]{:S(2)}) collective-permute-start(bf16[768,512]{1,0:T(8,128)(2,1)S(1)} %get-tuple-element.28), channel_id=1, source_target_pairs={{0,4},{1,5},{2,6},{3,7},{4,0},{5,1},{6,2},{7,3},{8,12},{9,13},{10,... | collective-permute-start | bytes 2359304 | tf_op jit(solution)/shard_map/ppermute | solution.py:91
  27.2 1.8 %collective-permute-start.14 = (bf16[304,512]{1,0:T(8,128)(2,1)S(1)}, bf16[304,512]{1,0:T(8,128)(2,1)S(1)}, u32[]{:S(2)}, u32[]{:S(2)}) collective-permute-start(bf16[304,512]{1,0:T(8,128)(2,1)S(1)} %join.1.joined_ref), channel_id=1, source_target_pairs={{0,4},{1,5},{2,6},{3,7},{4,0},{5,1},{6,2},{7,3},{8,12},{9,13},{10,... | collective-permute-start | bytes 933896 | tf_op jit(solution)/shard_map/ppermute | solution.py:91

commit v21 on v20

--- a/solution.py
+++ b/solution.py
@@ -201,7 +201,7 @@
 
 def sort_kernel(sizes, *refs):
     layers, owners, lane_group = sizes
-    parcels, posts = refs[:owners], refs[owners:]
+    parcels, posts = (refs[0], refs[3], refs[2], refs[1]), refs[owners:]
     rows, codes_at = parcels[0].shape[0], layers * lane_group
     block = rows_from([row_of(parcel[:16, codes_at:], 0) for parcel in parcels])
     for k, out in enumerate(posts):
@@ -419,7 +419,7 @@
         compiler_params=params,
         cost_estimate=lasting(10**10),
         name="sort",
-    )(*parcels)
+    )(parcels[0], parcels[3], parcels[2], parcels[1])
     posts = [posts[0]] + [shift(posts[k], k, 0) for k in range(1, layers)]
     by_x, by_y = shift(column, 0, 1), shift(column, 0, 2)
 

time: 31 us -> 30.3 us (0.977)
  waiting for transfers between devices: 3.23 us -> 1.99 us
  starting transfers between devices: 19.2 us -> 19.8 us
    ppermute x15, waiting for transfers between devices: 3.23 us -> 1.99 us  [shift(): return lax.ppermute(value, ('rows', 'cols'), pairs)]
    ppermute x15, starting transfers between devices: 19.2 us -> 19.8 us  [shift(): return lax.ppermute(value, ('rows', 'cols'), pairs)]
  transfers between devices with their start and end apart: 15 -> 15, of which waited for: 4 -> 5; matrix products, arithmetic and copies ran while one was open for 0% -> 0% of each run, Pallas kernels for 16% -> 16%
where the time goes in v21:
time: 30.3 us; the launch traced here: 30.1 us
  starting transfers between devices  19.8 us (65%)
  Pallas kernels  8.21 us (27%)
  waiting for transfers between devices  1.99 us (7%)
    ppermute x15, starting transfers between devices, shift(): return lax.ppermute(value, ('rows', 'cols'), pairs)  19.8 us
    ppermute x15, waiting for transfers between devices, shift(): return lax.ppermute(value, ('rows', 'cols'), pairs)  1.99 us
    pallas_call x1, Pallas kernels, local(): pl.pallas_call(functools.partial(final_kernel, sizes), out_shape=result,...  1.86 us
    pallas_call x1, Pallas kernels, local(): pl.pallas_call(functools.partial(pack_kernel, sizes), out_shape=[shaped((...  1.55 us
    pallas_call x1, Pallas kernels, local(): pl.pallas_call(functools.partial(near_kernel, sizes, 3), out_shape=[resul...  1.45 us
    pallas_call x1, Pallas kernels, local(): pl.pallas_call(own_kernel, out_shape=result, in_specs=[vmem] * 2, out_spe...  1.08 us
    pallas_call x1, Pallas kernels, local(): pl.pallas_call(functools.partial(far_kernel, sizes), out_shape=result, in...  0.9 us
    pallas_call x1, Pallas kernels, local(): pl.pallas_call(middle_kernel, out_shape=result, in_specs=[vmem] * 4, out_...  0.77 us
  transfers between devices with their start and end apart: 15, of which 5 were waited for; matrix products, arithmetic and copies ran while one was open for 0% of the time, Pallas kernels for 16%

profile of v21, /device:TPU:0, one launch (start us, length us, event | category | flops | bytes accessed | tf_op | source)
XLA Modules:
  0.0 30.1 jit_solution(7120511146579407430)
XLA Ops:
  0.0 1.6 %pack.1 = (bf16[64,512]{1,0:T(8,128)(2,1)S(1)}, bf16[64,384]{1,0:T(8,128)(2,1)S(1)}, bf16[64,384]{1,0:T(8,128)(2,1)S(1)}, bf16[64,384]{1,0:T(8,128)(2,1)S(1)}, b...) custom-call(s32[2,4]{1,0:T(2,128)} %lists_hbm.1, s32[2,4]{1,0:T(2,128)} %masks_hbm.1, s32[96]{0:T(128)} %order_hbm.1, ...), custom_call_target="tpu_custom_call" | custom-call | tf_op jit(solution)/shard_map/pack/pallas_call | solution.py:381
  1.6 3.1 %collective-permute-start.2 = (bf16[64,512]{1,0:T(8,128)(2,1)S(1)}, bf16[64,512]{1,0:T(8,128)(2,1)S(1)}, u32[]{:S(2)}, u32[]{:S(2)}) collective-permute-start(bf16[64,512]{1,0:T(8,128)(2,1)S(1)} %get-tuple-element.17.refs_3_), channel_id=1, source_target_pairs={{0,8},{1,9},{2,10},{3,11},{4,12},{5,13},{6,14},{7,15},{8,16},{9,17... | collective-permute-start | bytes 196616 | tf_op jit(solution)/shard_map/ppermute | solution.py:91
  4.6 2.6 %collective-permute-start.1 = (bf16[64,512]{1,0:T(8,128)(2,1)S(1)}, bf16[64,512]{1,0:T(8,128)(2,1)S(1)}, u32[]{:S(2)}, u32[]{:S(2)}) collective-permute-start(bf16[64,512]{1,0:T(8,128)(2,1)S(1)} %get-tuple-element.17.refs_3_), channel_id=1, source_target_pairs={{0,16},{1,17},{2,18},{3,19},{4,20},{5,21},{6,22},{7,23},{8,24},{9,... | collective-permute-start | bytes 196616 | tf_op jit(solution)/shard_map/ppermute | solution.py:91
  7.2 1.3 %collective-permute-start = (bf16[64,512]{1,0:T(8,128)(2,1)S(1)}, bf16[64,512]{1,0:T(8,128)(2,1)S(1)}, u32[]{:S(2)}, u32[]{:S(2)}) collective-permute-start(bf16[64,512]{1,0:T(8,128)(2,1)S(1)} %get-tuple-element.17.refs_3_), channel_id=1, source_target_pairs={{0,24},{1,25},{2,26},{3,27},{4,28},{5,29},{6,30},{7,31},{8,0},{9,1... | collective-permute-start | bytes 196616 | tf_op jit(solution)/shard_map/ppermute | solution.py:91
  8.6 2.4 %collective-permute-start.5 = (bf16[64,384]{1,0:T(8,128)(2,1)S(1)}, bf16[64,384]{1,0:T(8,128)(2,1)S(1)}, u32[]{:S(2)}, u32[]{:S(2)}) collective-permute-start(bf16[64,384]{1,0:T(8,128)(2,1)S(1)} %get-tuple-element.20), channel_id=1, source_target_pairs={{0,3},{1,2},{2,1},{3,0},{4,7},{5,6},{6,5},{7,4},{8,11},{9,10},{10,... | collective-permute-start | bytes 147464 | tf_op jit(solution)/shard_map/ppermute | solution.py:91
  11.0 0.5 %collective-permute-start.6 = (bf16[64,384]{1,0:T(8,128)(2,1)S(1)}, bf16[64,384]{1,0:T(8,128)(2,1)S(1)}, u32[]{:S(2)}, u32[]{:S(2)}) collective-permute-start(bf16[64,384]{1,0:T(8,128)(2,1)S(1)} %get-tuple-element.21), channel_id=1, source_target_pairs={{0,2},{1,3},{2,0},{3,1},{4,6},{5,7},{6,4},{7,5},{8,10},{9,11},{10,... | collective-permute-start | bytes 147464 | tf_op jit(solution)/shard_map/ppermute | solution.py:91
  11.5 0.0 collective-permute-done.2.refs_2_
  11.5 0.5 %collective-permute-start.7 = (bf16[64,384]{1,0:T(8,128)(2,1)S(1)}, bf16[64,384]{1,0:T(8,128)(2,1)S(1)}, u32[]{:S(2)}, u32[]{:S(2)}) collective-permute-start(bf16[64,384]{1,0:T(8,128)(2,1)S(1)} %get-tuple-element.22), channel_id=1, source_target_pairs={{0,1},{1,0},{2,3},{3,2},{4,5},{5,4},{6,7},{7,6},{8,9},{9,8},{10,11... | collective-permute-start | bytes 147464 | tf_op jit(solution)/shard_map/ppermute | solution.py:91
  12.1 1.6 %collective-permute-start.4 = (bf16[256,512]{1,0:T(8,128)(2,1)S(1)}, bf16[256,512]{1,0:T(8,128)(2,1)S(1)}, u32[]{:S(2)}, u32[]{:S(2)}) collective-permute-start(bf16[256,512]{1,0:T(8,128)(2,1)S(1)} %stack.1.refs_3_), channel_id=1, source_target_pairs={{0,2},{1,3},{2,0},{3,1},{4,6},{5,7},{6,4},{7,5},{8,10},{9,11},{10,... | collective-permute-start | bytes 786440 | tf_op jit(solution)/shard_map/ppermute | solution.py:91
  13.7 1.5 %collective-permute-start.3 = (bf16[256,512]{1,0:T(8,128)(2,1)S(1)}, bf16[256,512]{1,0:T(8,128)(2,1)S(1)}, u32[]{:S(2)}, u32[]{:S(2)}) collective-permute-start(bf16[256,512]{1,0:T(8,128)(2,1)S(1)} %stack.1.refs_3_), channel_id=1, source_target_pairs={{0,1},{1,0},{2,3},{3,2},{4,5},{5,4},{6,7},{7,6},{8,9},{9,8},{10,11... | collective-permute-start | bytes 786440 | tf_op jit(solution)/shard_map/ppermute | solution.py:91
  15.2 0.0 collective-permute-done.5.refs_1_
  15.2 0.4 %collective-permute-done.6.refs_2_ = bf16[64,384]{1,0:T(8,128)(2,1)S(1)} collective-permute-done((bf16[64,384]{1,0:T(8,128)(2,1)S(1)}, bf16[64,384]{1,0:T(8,128)(2,1)S(1)}, u32[]{:S(2)}, u32[]{:S(2)}) %collective-permute-start.6) | collective-permute-done | bytes 49184 | tf_op jit(solution)/shard_map/ppermute | solution.py:91
  15.6 0.5 %collective-permute-done.7.refs_3_ = bf16[64,384]{1,0:T(8,128)(2,1)S(1)} collective-permute-done((bf16[64,384]{1,0:T(8,128)(2,1)S(1)}, bf16[64,384]{1,0:T(8,128)(2,1)S(1)}, u32[]{:S(2)}, u32[]{:S(2)}) %collective-permute-start.7) | collective-permute-done | bytes 49184 | tf_op jit(solution)/shard_map/ppermute | solution.py:91
  16.1 0.1 sort.1
  16.2 0.6 %collective-permute-start.8 = (bf16[80,256]{1,0:T(8,128)(2,1)S(1)}, bf16[80,256]{1,0:T(8,128)(2,1)S(1)}, u32[]{:S(2)}, u32[]{:S(2)}) collective-permute-start(bf16[80,256]{1,0:T(8,128)(2,1)S(1)} %get-tuple-element.24), channel_id=1, source_target_pairs={{0,8},{1,9},{2,10},{3,11},{4,12},{5,13},{6,14},{7,15},{8,16},{9,17... | collective-permute-start | bytes 122888 | tf_op jit(solution)/shard_map/ppermute | solution.py:91
  16.8 2.0 %collective-permute-start.9 = (bf16[80,256]{1,0:T(8,128)(2,1)S(1)}, bf16[80,256]{1,0:T(8,128)(2,1)S(1)}, u32[]{:S(2)}, u32[]{:S(2)}) collective-permute-start(bf16[80,256]{1,0:T(8,128)(2,1)S(1)} %get-tuple-element.25), channel_id=1, source_target_pairs={{0,16},{1,17},{2,18},{3,19},{4,20},{5,21},{6,22},{7,23},{8,24},{9,... | collective-permute-start | bytes 122888 | tf_op jit(solution)/shard_map/ppermute | solution.py:91
  18.9 1.2 %collective-permute-start.10 = (bf16[80,256]{1,0:T(8,128)(2,1)S(1)}, bf16[80,256]{1,0:T(8,128)(2,1)S(1)}, u32[]{:S(2)}, u32[]{:S(2)}) collective-permute-start(bf16[80,256]{1,0:T(8,128)(2,1)S(1)} %get-tuple-element.26), channel_id=1, source_target_pairs={{0,24},{1,25},{2,26},{3,27},{4,28},{5,29},{6,30},{7,31},{8,0},{9,1... | collective-permute-start | bytes 122888 | tf_op jit(solution)/shard_map/ppermute | solution.py:91
  20.1 0.3 %turn.1.refs_2_.turned_ref = bf16[2,512,512]{2,1,0:T(8,128)(2,1)S(1)} custom-call(f32[512,512]{1,0:T(8,128)S(1)} %get-tuple-element.18.factor_ref), custom_call_target="tpu_custom_call" | custom-call | tf_op jit(solution)/shard_map/turn/pallas_call | solution.py:439
  20.4 0.0 collective-permute-done.4.in_ref.refs_5_
  20.4 0.9 %collective-permute-start.13 = (bf16[128,512]{1,0:T(8,128)(2,1)S(1)}, bf16[128,512]{1,0:T(8,128)(2,1)S(1)}, u32[]{:S(2)}, u32[]{:S(2)}) collective-permute-start(bf16[128,512]{1,0:T(8,128)(2,1)S(1)} %last.1.refs_1_), channel_id=1, source_target_pairs={{0,1},{1,0},{2,3},{3,2},{4,5},{5,4},{6,7},{7,6},{8,9},{9,8},{10,11... | collective-permute-start | bytes 393224 | tf_op jit(solution)/shard_map/ppermute | solution.py:91
  21.4 1.3 %collective-permute-start.12 = (bf16[128,512]{1,0:T(8,128)(2,1)S(1)}, bf16[128,512]{1,0:T(8,128)(2,1)S(1)}, u32[]{:S(2)}, u32[]{:S(2)}) collective-permute-start(bf16[128,512]{1,0:T(8,128)(2,1)S(1)} %first.1.refs_0_), channel_id=1, source_target_pairs={{0,2},{1,3},{2,0},{3,1},{4,6},{5,7},{6,4},{7,5},{8,10},{9,11},{10,... | collective-permute-start | bytes 393224 | tf_op jit(solution)/shard_map/ppermute | solution.py:91
  22.7 0.1 collective-permute-done.9.refs_8_.refs_2_
  22.7 0.2 collective-permute-done.10.refs_9_.refs_3_
  22.9 1.4 %near.1 = (f32[768,512]{1,0:T(8,128)S(1)}, bf16[768,512]{1,0:T(8,128)(2,1)S(1)}) custom-call(bf16[128,512]{1,0:T(8,128)(2,1)S(1)} %first.1.refs_0_, bf16[128,512]{1,0:T(8,128)(2,1)S(1)} %last.1.refs_1_, bf16[2,512,512]{2,1,0:T(8,128)(2,1)S(1)} %turn.1.refs_2_.turned_ref, bf16[256,512]{1,0:T(8,128)(2,1)S(1)} %stack.1.refs_3_, ...), custom_call_target="tpu_custom_call" | custom-call | flops 1000000000 | tf_op jit(solution)/shard_map/near/pallas_call | solution.py:452
  24.3 0.1 collective-permute-start.11
  24.4 1.1 %own.1.refs_4_.own_ref = f32[768,512]{1,0:T(8,128)S(1)} custom-call(f32[768,512]{1,0:T(8,128)S(1)} %get-tuple-element.27.own_ref, bf16[2,512,512]{2,1,0:T(8,128)(2,1)S(1)} %turn.1.refs_2_.turned_ref), custom_call_target="tpu_custom_call" | custom-call | flops 1000000000 | tf_op jit(solution)/shard_map/own/pallas_call | solution.py:466
  25.5 0.9 %collective-permute-done.12.above_ref = bf16[128,512]{1,0:T(8,128)(2,1)S(1)} collective-permute-done((bf16[128,512]{1,0:T(8,128)(2,1)S(1)}, bf16[128,512]{1,0:T(8,128)(2,1)S(1)}, u32[]{:S(2)}, u32[]{:S(2)}) %collective-permute-start.12) | collective-permute-done | bytes 131104 | tf_op jit(solution)/shard_map/ppermute | solution.py:91
  26.4 0.1 join.1.joined_ref
  26.5 0.1 collective-permute-start.14
  26.5 0.9 %far.1.far_ref = f32[768,512]{1,0:T(8,128)S(1)} custom-call(bf16[304,512]{1,0:T(8,128)(2,1)S(1)} %join.1.joined_ref, bf16[2,512,512]{2,1,0:T(8,128)(2,1)S(1)} %turn.1.refs_2_.turned_ref), custom_call_target="tpu_custom_call" | custom-call | tf_op jit(solution)/shard_map/far/pallas_call | solution.py:486
  27.5 0.8 %middle.1.middle_ref = f32[768,512]{1,0:T(8,128)S(1)} custom-call(f32[768,512]{1,0:T(8,128)S(1)} %own.1.refs_4_.own_ref, bf16[768,512]{1,0:T(8,128)(2,1)S(1)} %collective-permute-done.11.other_ref, f32[768,512]{1,0:T(8,128)S(1)} %far.1.far_ref, bf16[2,512,512]{2,1,0:T(8,128)(2,1)S(1)} %turn.1.refs_2_.turned_ref), custom_call_target="tpu_custom_call" | custom-call | tf_op jit(solution)/shard_map/middle/pallas_call | solution.py:495
  28.3 1.9 %final.1 = f32[768,512]{1,0:T(8,128)} custom-call(f32[768,512]{1,0:T(8,128)S(1)} %middle.1.middle_ref, bf16[304,512]{1,0:T(8,128)(2,1)S(1)} %collective-permute-done.14.joined_ref, bf16[2,512,512]{2,1,0:T(8,128)(2,1)S(1)} %turn.1.refs_2_.turned_ref), custom_call_target="tpu_custom_call" | custom-call | tf_op jit(solution)/shard_map/final/pallas_call | solution.py:503
  (10 shorter events, 0.1 us)
Async XLA Ops:
  1.6 10.0 %collective-permute-start.2 = (bf16[64,512]{1,0:T(8,128)(2,1)S(1)}, bf16[64,512]{1,0:T(8,128)(2,1)S(1)}, u32[]{:S(2)}, u32[]{:S(2)}) collective-permute-start(bf16[64,512]{1,0:T(8,128)(2,1)S(1)} %get-tuple-element.17.refs_3_), channel_id=1, source_target_pairs={{0,8},{1,9},{2,10},{3,11},{4,12},{5,13},{6,14},{7,15},{8,16},{9,17... | collective-permute-start | bytes 196616 | tf_op jit(solution)/shard_map/ppermute | solution.py:91
  4.6 7.4 %collective-permute-start.1 = (bf16[64,512]{1,0:T(8,128)(2,1)S(1)}, bf16[64,512]{1,0:T(8,128)(2,1)S(1)}, u32[]{:S(2)}, u32[]{:S(2)}) collective-permute-start(bf16[64,512]{1,0:T(8,128)(2,1)S(1)} %get-tuple-element.17.refs_3_), channel_id=1, source_target_pairs={{0,16},{1,17},{2,18},{3,19},{4,20},{5,21},{6,22},{7,23},{8,24},{9,... | collective-permute-start | bytes 196616 | tf_op jit(solution)/shard_map/ppermute | solution.py:91
  7.2 4.8 %collective-permute-start = (bf16[64,512]{1,0:T(8,128)(2,1)S(1)}, bf16[64,512]{1,0:T(8,128)(2,1)S(1)}, u32[]{:S(2)}, u32[]{:S(2)}) collective-permute-start(bf16[64,512]{1,0:T(8,128)(2,1)S(1)} %get-tuple-element.17.refs_3_), channel_id=1, source_target_pairs={{0,24},{1,25},{2,26},{3,27},{4,28},{5,29},{6,30},{7,31},{8,0},{9,1... | collective-permute-start | bytes 196616 | tf_op jit(solution)/shard_map/ppermute | solution.py:91
  8.6 6.6 %collective-permute-start.5 = (bf16[64,384]{1,0:T(8,128)(2,1)S(1)}, bf16[64,384]{1,0:T(8,128)(2,1)S(1)}, u32[]{:S(2)}, u32[]{:S(2)}) collective-permute-start(bf16[64,384]{1,0:T(8,128)(2,1)S(1)} %get-tuple-element.20), channel_id=1, source_target_pairs={{0,3},{1,2},{2,1},{3,0},{4,7},{5,6},{6,5},{7,4},{8,11},{9,10},{10,... | collective-permute-start | bytes 147464 | tf_op jit(solution)/shard_map/ppermute | solution.py:91
  11.0 4.5 %collective-permute-start.6 = (bf16[64,384]{1,0:T(8,128)(2,1)S(1)}, bf16[64,384]{1,0:T(8,128)(2,1)S(1)}, u32[]{:S(2)}, u32[]{:S(2)}) collective-permute-start(bf16[64,384]{1,0:T(8,128)(2,1)S(1)} %get-tuple-element.21), channel_id=1, source_target_pairs={{0,2},{1,3},{2,0},{3,1},{4,6},{5,7},{6,4},{7,5},{8,10},{9,11},{10,... | collective-permute-start | bytes 147464 | tf_op jit(solution)/shard_map/ppermute | solution.py:91
  11.5 4.5 %collective-permute-start.7 = (bf16[64,384]{1,0:T(8,128)(2,1)S(1)}, bf16[64,384]{1,0:T(8,128)(2,1)S(1)}, u32[]{:S(2)}, u32[]{:S(2)}) collective-permute-start(bf16[64,384]{1,0:T(8,128)(2,1)S(1)} %get-tuple-element.22), channel_id=1, source_target_pairs={{0,1},{1,0},{2,3},{3,2},{4,5},{5,4},{6,7},{7,6},{8,9},{9,8},{10,11... | collective-permute-start | bytes 147464 | tf_op jit(solution)/shard_map/ppermute | solution.py:91
  12.1 8.3 %collective-permute-start.4 = (bf16[256,512]{1,0:T(8,128)(2,1)S(1)}, bf16[256,512]{1,0:T(8,128)(2,1)S(1)}, u32[]{:S(2)}, u32[]{:S(2)}) collective-permute-start(bf16[256,512]{1,0:T(8,128)(2,1)S(1)} %stack.1.refs_3_), channel_id=1, source_target_pairs={{0,2},{1,3},{2,0},{3,1},{4,6},{5,7},{6,4},{7,5},{8,10},{9,11},{10,... | collective-permute-start | bytes 786440 | tf_op jit(solution)/shard_map/ppermute | solution.py:91
  13.7 7.6 %collective-permute-start.3 = (bf16[256,512]{1,0:T(8,128)(2,1)S(1)}, bf16[256,512]{1,0:T(8,128)(2,1)S(1)}, u32[]{:S(2)}, u32[]{:S(2)}) collective-permute-start(bf16[256,512]{1,0:T(8,128)(2,1)S(1)} %stack.1.refs_3_), channel_id=1, source_target_pairs={{0,1},{1,0},{2,3},{3,2},{4,5},{5,4},{6,7},{7,6},{8,9},{9,8},{10,11... | collective-permute-start | bytes 786440 | tf_op jit(solution)/shard_map/ppermute | solution.py:91
  16.2 6.5 %collective-permute-start.8 = (bf16[80,256]{1,0:T(8,128)(2,1)S(1)}, bf16[80,256]{1,0:T(8,128)(2,1)S(1)}, u32[]{:S(2)}, u32[]{:S(2)}) collective-permute-start(bf16[80,256]{1,0:T(8,128)(2,1)S(1)} %get-tuple-element.24), channel_id=1, source_target_pairs={{0,8},{1,9},{2,10},{3,11},{4,12},{5,13},{6,14},{7,15},{8,16},{9,17... | collective-permute-start | bytes 122888 | tf_op jit(solution)/shard_map/ppermute | solution.py:91
  16.8 5.9 %collective-permute-start.9 = (bf16[80,256]{1,0:T(8,128)(2,1)S(1)}, bf16[80,256]{1,0:T(8,128)(2,1)S(1)}, u32[]{:S(2)}, u32[]{:S(2)}) collective-permute-start(bf16[80,256]{1,0:T(8,128)(2,1)S(1)} %get-tuple-element.25), channel_id=1, source_target_pairs={{0,16},{1,17},{2,18},{3,19},{4,20},{5,21},{6,22},{7,23},{8,24},{9,... | collective-permute-start | bytes 122888 | tf_op jit(solution)/shard_map/ppermute | solution.py:91
  18.9 4.0 %collective-permute-start.10 = (bf16[80,256]{1,0:T(8,128)(2,1)S(1)}, bf16[80,256]{1,0:T(8,128)(2,1)S(1)}, u32[]{:S(2)}, u32[]{:S(2)}) collective-permute-start(bf16[80,256]{1,0:T(8,128)(2,1)S(1)} %get-tuple-element.26), channel_id=1, source_target_pairs={{0,24},{1,25},{2,26},{3,27},{4,28},{5,29},{6,30},{7,31},{8,0},{9,1... | collective-permute-start | bytes 122888 | tf_op jit(solution)/shard_map/ppermute | solution.py:91
  20.4 5.1 %collective-permute-start.13 = (bf16[128,512]{1,0:T(8,128)(2,1)S(1)}, bf16[128,512]{1,0:T(8,128)(2,1)S(1)}, u32[]{:S(2)}, u32[]{:S(2)}) collective-permute-start(bf16[128,512]{1,0:T(8,128)(2,1)S(1)} %last.1.refs_1_), channel_id=1, source_target_pairs={{0,1},{1,0},{2,3},{3,2},{4,5},{5,4},{6,7},{7,6},{8,9},{9,8},{10,11... | collective-permute-start | bytes 393224 | tf_op jit(solution)/shard_map/ppermute | solution.py:91
  21.4 5.0 %collective-permute-start.12 = (bf16[128,512]{1,0:T(8,128)(2,1)S(1)}, bf16[128,512]{1,0:T(8,128)(2,1)S(1)}, u32[]{:S(2)}, u32[]{:S(2)}) collective-permute-start(bf16[128,512]{1,0:T(8,128)(2,1)S(1)} %first.1.refs_0_), channel_id=1, source_target_pairs={{0,2},{1,3},{2,0},{3,1},{4,6},{5,7},{6,4},{7,5},{8,10},{9,11},{10,... | collective-permute-start | bytes 393224 | tf_op jit(solution)/shard_map/ppermute | solution.py:91
  24.3 3.1 %collective-permute-start.11 = (bf16[768,512]{1,0:T(8,128)(2,1)S(1)}, bf16[768,512]{1,0:T(8,128)(2,1)S(1)}, u32[]{:S(2)}, u32[]{:S(2)}) collective-permute-start(bf16[768,512]{1,0:T(8,128)(2,1)S(1)} %get-tuple-element.28), channel_id=1, source_target_pairs={{0,4},{1,5},{2,6},{3,7},{4,0},{5,1},{6,2},{7,3},{8,12},{9,13},{10,... | collective-permute-start | bytes 2359304 | tf_op jit(solution)/shard_map/ppermute | solution.py:91
  26.5 1.8 %collective-permute-start.14 = (bf16[304,512]{1,0:T(8,128)(2,1)S(1)}, bf16[304,512]{1,0:T(8,128)(2,1)S(1)}, u32[]{:S(2)}, u32[]{:S(2)}) collective-permute-start(bf16[304,512]{1,0:T(8,128)(2,1)S(1)} %join.1.joined_ref), channel_id=1, source_target_pairs={{0,4},{1,5},{2,6},{3,7},{4,0},{5,1},{6,2},{7,3},{8,12},{9,13},{10,... | collective-permute-start | bytes 933896 | tf_op jit(solution)/shard_map/ppermute | solution.py:91

commit v22 on v21

--- a/solution.py
+++ b/solution.py
@@ -119,20 +119,8 @@
     part = slab // 2
     me_r, me_c = lax.axis_index("rows"), lax.axis_index("cols")
     me_z, me_core = me_r // 2, lax.rem(me_r, 2)
-    for copy in copies:
+    for copy in copies[:3]:
         copy.wait()
-
-    row_ids = lax.broadcasted_iota(jnp.int32, (rows, rows), 0)
-    lane_ids = lax.broadcasted_iota(jnp.int32, (rows, rows), 1)
-    column = jnp.sum(jnp.where(row_ids == lane_ids, weights_ref[...], 0.0), axis=1, keepdims=True)
-    weighted = (column * panel_ref[...].astype(f32)).astype(bf16)
-    weighted_ref[...] = weighted
-
-    for b in range(block_count):
-        block = jac_ref[b * block_rows : (b + 1) * block_rows, :].astype(f32)
-        start = b * slot_count * tile_width
-        turned_ref[start : start + slot_count * tile_width, :] = block.T.astype(bf16)
-
     for i in range(order_ref.shape[0]):
         places_ref[order_ref[i]] = i
     slots = []
@@ -144,9 +132,8 @@
             owner += (place >= c * per_owner).astype(jnp.int32)
         slots.append((place - owner * per_owner, jnp.where(masks_ref[b, k] == 1, owner, -1)))
 
-    shape = (16, CAP * block_count * block_rows)
-    lane = lax.broadcasted_iota(jnp.int32, shape, 1)
-    for e, parcel in enumerate(parcels):
+    found_slots = []
+    for e in range(owners):
         wanted = me_c ^ e
         found = jnp.int32(0)
         chosen = [jnp.int32(0)] * CAP
@@ -158,6 +145,25 @@
                 chosen[j] = jnp.where(take, s, chosen[j])
                 codes[j] = jnp.where(take, place, codes[j])
             found += hit.astype(jnp.int32)
+        found_slots.append((chosen, codes))
+
+    for copy in copies[3:]:
+        copy.wait()
+
+    row_ids = lax.broadcasted_iota(jnp.int32, (rows, rows), 0)
+    lane_ids = lax.broadcasted_iota(jnp.int32, (rows, rows), 1)
+    column = jnp.sum(jnp.where(row_ids == lane_ids, weights_ref[...], 0.0), axis=1, keepdims=True)
+    weighted = (column * panel_ref[...].astype(f32)).astype(bf16)
+    weighted_ref[...] = weighted
+
+    for b in range(block_count):
+        block = jac_ref[b * block_rows : (b + 1) * block_rows, :].astype(f32)
+        start = b * slot_count * tile_width
+        turned_ref[start : start + slot_count * tile_width, :] = block.T.astype(bf16)
+
+    shape = (16, CAP * block_count * block_rows)
+    lane = lax.broadcasted_iota(jnp.int32, shape, 1)
+    for parcel, (chosen, codes) in zip(parcels, found_slots):
         note = jnp.full(shape, -1, jnp.int32)
         for j in range(CAP):
             for b in range(block_count):

time: 30.3 us -> 30.2 us (level)
  no operation moved by 1% of the time
where the time goes in v22:
time: 30.2 us; the launch traced here: 30 us
  starting transfers between devices  19.8 us (66%)
  Pallas kernels  8.08 us (27%)
  waiting for transfers between devices  1.99 us (7%)
    ppermute x15, starting transfers between devices, shift(): return lax.ppermute(value, ('rows', 'cols'), pairs)  19.8 us
    ppermute x15, waiting for transfers between devices, shift(): return lax.ppermute(value, ('rows', 'cols'), pairs)  1.99 us
    pallas_call x1, Pallas kernels, local(): pl.pallas_call(functools.partial(final_kernel, sizes), out_shape=result,...  1.87 us
    pallas_call x1, Pallas kernels, local(): pl.pallas_call(functools.partial(near_kernel, sizes, 3), out_shape=[resul...  1.45 us
    pallas_call x1, Pallas kernels, local(): pl.pallas_call(functools.partial(pack_kernel, sizes), out_shape=[shaped((...  1.42 us
    pallas_call x1, Pallas kernels, local(): pl.pallas_call(own_kernel, out_shape=result, in_specs=[vmem] * 2, out_spe...  1.08 us
    pallas_call x1, Pallas kernels, local(): pl.pallas_call(functools.partial(far_kernel, sizes), out_shape=result, in...  0.9 us
    pallas_call x1, Pallas kernels, local(): pl.pallas_call(middle_kernel, out_shape=result, in_specs=[vmem] * 4, out_...  0.78 us
  transfers between devices with their start and end apart: 15, of which 5 were waited for; matrix products, arithmetic and copies ran while one was open for 0% of the time, Pallas kernels for 16%

profile of v22, /device:TPU:0, one launch (start us, length us, event | category | flops | bytes accessed | tf_op | source)
XLA Modules:
  0.0 30.0 jit_solution(14071014350863754501)
XLA Ops:
  0.0 1.4 %pack.1 = (bf16[64,512]{1,0:T(8,128)(2,1)S(1)}, bf16[64,384]{1,0:T(8,128)(2,1)S(1)}, bf16[64,384]{1,0:T(8,128)(2,1)S(1)}, bf16[64,384]{1,0:T(8,128)(2,1)S(1)}, b...) custom-call(s32[2,4]{1,0:T(2,128)} %lists_hbm.1, s32[2,4]{1,0:T(2,128)} %masks_hbm.1, s32[96]{0:T(128)} %order_hbm.1, ...), custom_call_target="tpu_custom_call" | custom-call | tf_op jit(solution)/shard_map/pack/pallas_call | solution.py:387
  1.4 3.1 %collective-permute-start.2 = (bf16[64,512]{1,0:T(8,128)(2,1)S(1)}, bf16[64,512]{1,0:T(8,128)(2,1)S(1)}, u32[]{:S(2)}, u32[]{:S(2)}) collective-permute-start(bf16[64,512]{1,0:T(8,128)(2,1)S(1)} %get-tuple-element.17.refs_3_), channel_id=1, source_target_pairs={{0,8},{1,9},{2,10},{3,11},{4,12},{5,13},{6,14},{7,15},{8,16},{9,17... | collective-permute-start | bytes 196616 | tf_op jit(solution)/shard_map/ppermute | solution.py:91
  4.5 2.6 %collective-permute-start.1 = (bf16[64,512]{1,0:T(8,128)(2,1)S(1)}, bf16[64,512]{1,0:T(8,128)(2,1)S(1)}, u32[]{:S(2)}, u32[]{:S(2)}) collective-permute-start(bf16[64,512]{1,0:T(8,128)(2,1)S(1)} %get-tuple-element.17.refs_3_), channel_id=1, source_target_pairs={{0,16},{1,17},{2,18},{3,19},{4,20},{5,21},{6,22},{7,23},{8,24},{9,... | collective-permute-start | bytes 196616 | tf_op jit(solution)/shard_map/ppermute | solution.py:91
  7.1 1.3 %collective-permute-start = (bf16[64,512]{1,0:T(8,128)(2,1)S(1)}, bf16[64,512]{1,0:T(8,128)(2,1)S(1)}, u32[]{:S(2)}, u32[]{:S(2)}) collective-permute-start(bf16[64,512]{1,0:T(8,128)(2,1)S(1)} %get-tuple-element.17.refs_3_), channel_id=1, source_target_pairs={{0,24},{1,25},{2,26},{3,27},{4,28},{5,29},{6,30},{7,31},{8,0},{9,1... | collective-permute-start | bytes 196616 | tf_op jit(solution)/shard_map/ppermute | solution.py:91
  8.4 2.4 %collective-permute-start.5 = (bf16[64,384]{1,0:T(8,128)(2,1)S(1)}, bf16[64,384]{1,0:T(8,128)(2,1)S(1)}, u32[]{:S(2)}, u32[]{:S(2)}) collective-permute-start(bf16[64,384]{1,0:T(8,128)(2,1)S(1)} %get-tuple-element.20), channel_id=1, source_target_pairs={{0,3},{1,2},{2,1},{3,0},{4,7},{5,6},{6,5},{7,4},{8,11},{9,10},{10,... | collective-permute-start | bytes 147464 | tf_op jit(solution)/shard_map/ppermute | solution.py:91
  10.9 0.5 %collective-permute-start.6 = (bf16[64,384]{1,0:T(8,128)(2,1)S(1)}, bf16[64,384]{1,0:T(8,128)(2,1)S(1)}, u32[]{:S(2)}, u32[]{:S(2)}) collective-permute-start(bf16[64,384]{1,0:T(8,128)(2,1)S(1)} %get-tuple-element.21), channel_id=1, source_target_pairs={{0,2},{1,3},{2,0},{3,1},{4,6},{5,7},{6,4},{7,5},{8,10},{9,11},{10,... | collective-permute-start | bytes 147464 | tf_op jit(solution)/shard_map/ppermute | solution.py:91
  11.4 0.0 collective-permute-done.2.refs_2_
  11.4 0.5 %collective-permute-start.7 = (bf16[64,384]{1,0:T(8,128)(2,1)S(1)}, bf16[64,384]{1,0:T(8,128)(2,1)S(1)}, u32[]{:S(2)}, u32[]{:S(2)}) collective-permute-start(bf16[64,384]{1,0:T(8,128)(2,1)S(1)} %get-tuple-element.22), channel_id=1, source_target_pairs={{0,1},{1,0},{2,3},{3,2},{4,5},{5,4},{6,7},{7,6},{8,9},{9,8},{10,11... | collective-permute-start | bytes 147464 | tf_op jit(solution)/shard_map/ppermute | solution.py:91
  11.9 0.0 collective-permute-done.1.refs_1_
  11.9 0.0 collective-permute-done.refs_0_
  12.0 1.6 %collective-permute-start.4 = (bf16[256,512]{1,0:T(8,128)(2,1)S(1)}, bf16[256,512]{1,0:T(8,128)(2,1)S(1)}, u32[]{:S(2)}, u32[]{:S(2)}) collective-permute-start(bf16[256,512]{1,0:T(8,128)(2,1)S(1)} %stack.1.refs_3_), channel_id=1, source_target_pairs={{0,2},{1,3},{2,0},{3,1},{4,6},{5,7},{6,4},{7,5},{8,10},{9,11},{10,... | collective-permute-start | bytes 786440 | tf_op jit(solution)/shard_map/ppermute | solution.py:91
  13.6 1.5 %collective-permute-start.3 = (bf16[256,512]{1,0:T(8,128)(2,1)S(1)}, bf16[256,512]{1,0:T(8,128)(2,1)S(1)}, u32[]{:S(2)}, u32[]{:S(2)}) collective-permute-start(bf16[256,512]{1,0:T(8,128)(2,1)S(1)} %stack.1.refs_3_), channel_id=1, source_target_pairs={{0,1},{1,0},{2,3},{3,2},{4,5},{5,4},{6,7},{7,6},{8,9},{9,8},{10,11... | collective-permute-start | bytes 786440 | tf_op jit(solution)/shard_map/ppermute | solution.py:91
  15.0 0.4 %collective-permute-done.6.refs_2_ = bf16[64,384]{1,0:T(8,128)(2,1)S(1)} collective-permute-done((bf16[64,384]{1,0:T(8,128)(2,1)S(1)}, bf16[64,384]{1,0:T(8,128)(2,1)S(1)}, u32[]{:S(2)}, u32[]{:S(2)}) %collective-permute-start.6) | collective-permute-done | bytes 49184 | tf_op jit(solution)/shard_map/ppermute | solution.py:91
  15.4 0.5 %collective-permute-done.7.refs_3_ = bf16[64,384]{1,0:T(8,128)(2,1)S(1)} collective-permute-done((bf16[64,384]{1,0:T(8,128)(2,1)S(1)}, bf16[64,384]{1,0:T(8,128)(2,1)S(1)}, u32[]{:S(2)}, u32[]{:S(2)}) %collective-permute-start.7) | collective-permute-done | bytes 49184 | tf_op jit(solution)/shard_map/ppermute | solution.py:91
  15.9 0.1 sort.1
  16.1 0.6 %collective-permute-start.8 = (bf16[80,256]{1,0:T(8,128)(2,1)S(1)}, bf16[80,256]{1,0:T(8,128)(2,1)S(1)}, u32[]{:S(2)}, u32[]{:S(2)}) collective-permute-start(bf16[80,256]{1,0:T(8,128)(2,1)S(1)} %get-tuple-element.24), channel_id=1, source_target_pairs={{0,8},{1,9},{2,10},{3,11},{4,12},{5,13},{6,14},{7,15},{8,16},{9,17... | collective-permute-start | bytes 122888 | tf_op jit(solution)/shard_map/ppermute | solution.py:91
  16.7 2.0 %collective-permute-start.9 = (bf16[80,256]{1,0:T(8,128)(2,1)S(1)}, bf16[80,256]{1,0:T(8,128)(2,1)S(1)}, u32[]{:S(2)}, u32[]{:S(2)}) collective-permute-start(bf16[80,256]{1,0:T(8,128)(2,1)S(1)} %get-tuple-element.25), channel_id=1, source_target_pairs={{0,16},{1,17},{2,18},{3,19},{4,20},{5,21},{6,22},{7,23},{8,24},{9,... | collective-permute-start | bytes 122888 | tf_op jit(solution)/shard_map/ppermute | solution.py:91
  18.7 1.2 %collective-permute-start.10 = (bf16[80,256]{1,0:T(8,128)(2,1)S(1)}, bf16[80,256]{1,0:T(8,128)(2,1)S(1)}, u32[]{:S(2)}, u32[]{:S(2)}) collective-permute-start(bf16[80,256]{1,0:T(8,128)(2,1)S(1)} %get-tuple-element.26), channel_id=1, source_target_pairs={{0,24},{1,25},{2,26},{3,27},{4,28},{5,29},{6,30},{7,31},{8,0},{9,1... | collective-permute-start | bytes 122888 | tf_op jit(solution)/shard_map/ppermute | solution.py:91
  19.9 0.3 %turn.1.refs_2_.turned_ref = bf16[2,512,512]{2,1,0:T(8,128)(2,1)S(1)} custom-call(f32[512,512]{1,0:T(8,128)S(1)} %get-tuple-element.18.factor_ref), custom_call_target="tpu_custom_call" | custom-call | tf_op jit(solution)/shard_map/turn/pallas_call | solution.py:445
  20.3 0.9 %collective-permute-start.13 = (bf16[128,512]{1,0:T(8,128)(2,1)S(1)}, bf16[128,512]{1,0:T(8,128)(2,1)S(1)}, u32[]{:S(2)}, u32[]{:S(2)}) collective-permute-start(bf16[128,512]{1,0:T(8,128)(2,1)S(1)} %last.1.refs_1_), channel_id=1, source_target_pairs={{0,1},{1,0},{2,3},{3,2},{4,5},{5,4},{6,7},{7,6},{8,9},{9,8},{10,11... | collective-permute-start | bytes 393224 | tf_op jit(solution)/shard_map/ppermute | solution.py:91
  21.2 1.3 %collective-permute-start.12 = (bf16[128,512]{1,0:T(8,128)(2,1)S(1)}, bf16[128,512]{1,0:T(8,128)(2,1)S(1)}, u32[]{:S(2)}, u32[]{:S(2)}) collective-permute-start(bf16[128,512]{1,0:T(8,128)(2,1)S(1)} %first.1.refs_0_), channel_id=1, source_target_pairs={{0,2},{1,3},{2,0},{3,1},{4,6},{5,7},{6,4},{7,5},{8,10},{9,11},{10,... | collective-permute-start | bytes 393224 | tf_op jit(solution)/shard_map/ppermute | solution.py:91
  22.5 0.1 collective-permute-done.9.refs_8_.refs_2_
  22.6 0.2 collective-permute-done.10.refs_9_.refs_3_
  22.7 1.4 %near.1 = (f32[768,512]{1,0:T(8,128)S(1)}, bf16[768,512]{1,0:T(8,128)(2,1)S(1)}) custom-call(bf16[128,512]{1,0:T(8,128)(2,1)S(1)} %first.1.refs_0_, bf16[128,512]{1,0:T(8,128)(2,1)S(1)} %last.1.refs_1_, bf16[2,512,512]{2,1,0:T(8,128)(2,1)S(1)} %turn.1.refs_2_.turned_ref, bf16[256,512]{1,0:T(8,128)(2,1)S(1)} %stack.1.refs_3_, ...), custom_call_target="tpu_custom_call" | custom-call | flops 1000000000 | tf_op jit(solution)/shard_map/near/pallas_call | solution.py:458
  24.2 0.1 collective-permute-start.11
  24.3 1.1 %own.1.refs_4_.own_ref = f32[768,512]{1,0:T(8,128)S(1)} custom-call(f32[768,512]{1,0:T(8,128)S(1)} %get-tuple-element.27.own_ref, bf16[2,512,512]{2,1,0:T(8,128)(2,1)S(1)} %turn.1.refs_2_.turned_ref), custom_call_target="tpu_custom_call" | custom-call | flops 1000000000 | tf_op jit(solution)/shard_map/own/pallas_call | solution.py:472
  25.4 0.9 %collective-permute-done.12.above_ref = bf16[128,512]{1,0:T(8,128)(2,1)S(1)} collective-permute-done((bf16[128,512]{1,0:T(8,128)(2,1)S(1)}, bf16[128,512]{1,0:T(8,128)(2,1)S(1)}, u32[]{:S(2)}, u32[]{:S(2)}) %collective-permute-start.12) | collective-permute-done | bytes 131104 | tf_op jit(solution)/shard_map/ppermute | solution.py:91
  26.2 0.1 join.1.joined_ref
  26.3 0.1 collective-permute-start.14
  26.4 0.9 %far.1.far_ref = f32[768,512]{1,0:T(8,128)S(1)} custom-call(bf16[304,512]{1,0:T(8,128)(2,1)S(1)} %join.1.joined_ref, bf16[2,512,512]{2,1,0:T(8,128)(2,1)S(1)} %turn.1.refs_2_.turned_ref), custom_call_target="tpu_custom_call" | custom-call | tf_op jit(solution)/shard_map/far/pallas_call | solution.py:492
  27.3 0.8 %middle.1.middle_ref = f32[768,512]{1,0:T(8,128)S(1)} custom-call(f32[768,512]{1,0:T(8,128)S(1)} %own.1.refs_4_.own_ref, bf16[768,512]{1,0:T(8,128)(2,1)S(1)} %collective-permute-done.11.other_ref, f32[768,512]{1,0:T(8,128)S(1)} %far.1.far_ref, bf16[2,512,512]{2,1,0:T(8,128)(2,1)S(1)} %turn.1.refs_2_.turned_ref), custom_call_target="tpu_custom_call" | custom-call | tf_op jit(solution)/shard_map/middle/pallas_call | solution.py:501
  28.1 1.9 %final.1 = f32[768,512]{1,0:T(8,128)} custom-call(f32[768,512]{1,0:T(8,128)S(1)} %middle.1.middle_ref, bf16[304,512]{1,0:T(8,128)(2,1)S(1)} %collective-permute-done.14.joined_ref, bf16[2,512,512]{2,1,0:T(8,128)(2,1)S(1)} %turn.1.refs_2_.turned_ref), custom_call_target="tpu_custom_call" | custom-call | tf_op jit(solution)/shard_map/final/pallas_call | solution.py:509
  (10 shorter events, 0.1 us)
Async XLA Ops:
  1.4 10.0 %collective-permute-start.2 = (bf16[64,512]{1,0:T(8,128)(2,1)S(1)}, bf16[64,512]{1,0:T(8,128)(2,1)S(1)}, u32[]{:S(2)}, u32[]{:S(2)}) collective-permute-start(bf16[64,512]{1,0:T(8,128)(2,1)S(1)} %get-tuple-element.17.refs_3_), channel_id=1, source_target_pairs={{0,8},{1,9},{2,10},{3,11},{4,12},{5,13},{6,14},{7,15},{8,16},{9,17... | collective-permute-start | bytes 196616 | tf_op jit(solution)/shard_map/ppermute | solution.py:91
  4.5 7.4 %collective-permute-start.1 = (bf16[64,512]{1,0:T(8,128)(2,1)S(1)}, bf16[64,512]{1,0:T(8,128)(2,1)S(1)}, u32[]{:S(2)}, u32[]{:S(2)}) collective-permute-start(bf16[64,512]{1,0:T(8,128)(2,1)S(1)} %get-tuple-element.17.refs_3_), channel_id=1, source_target_pairs={{0,16},{1,17},{2,18},{3,19},{4,20},{5,21},{6,22},{7,23},{8,24},{9,... | collective-permute-start | bytes 196616 | tf_op jit(solution)/shard_map/ppermute | solution.py:91
  7.1 4.8 %collective-permute-start = (bf16[64,512]{1,0:T(8,128)(2,1)S(1)}, bf16[64,512]{1,0:T(8,128)(2,1)S(1)}, u32[]{:S(2)}, u32[]{:S(2)}) collective-permute-start(bf16[64,512]{1,0:T(8,128)(2,1)S(1)} %get-tuple-element.17.refs_3_), channel_id=1, source_target_pairs={{0,24},{1,25},{2,26},{3,27},{4,28},{5,29},{6,30},{7,31},{8,0},{9,1... | collective-permute-start | bytes 196616 | tf_op jit(solution)/shard_map/ppermute | solution.py:91
  8.4 6.6 %collective-permute-start.5 = (bf16[64,384]{1,0:T(8,128)(2,1)S(1)}, bf16[64,384]{1,0:T(8,128)(2,1)S(1)}, u32[]{:S(2)}, u32[]{:S(2)}) collective-permute-start(bf16[64,384]{1,0:T(8,128)(2,1)S(1)} %get-tuple-element.20), channel_id=1, source_target_pairs={{0,3},{1,2},{2,1},{3,0},{4,7},{5,6},{6,5},{7,4},{8,11},{9,10},{10,... | collective-permute-start | bytes 147464 | tf_op jit(solution)/shard_map/ppermute | solution.py:91
  10.9 4.5 %collective-permute-start.6 = (bf16[64,384]{1,0:T(8,128)(2,1)S(1)}, bf16[64,384]{1,0:T(8,128)(2,1)S(1)}, u32[]{:S(2)}, u32[]{:S(2)}) collective-permute-start(bf16[64,384]{1,0:T(8,128)(2,1)S(1)} %get-tuple-element.21), channel_id=1, source_target_pairs={{0,2},{1,3},{2,0},{3,1},{4,6},{5,7},{6,4},{7,5},{8,10},{9,11},{10,... | collective-permute-start | bytes 147464 | tf_op jit(solution)/shard_map/ppermute | solution.py:91
  11.4 4.5 %collective-permute-start.7 = (bf16[64,384]{1,0:T(8,128)(2,1)S(1)}, bf16[64,384]{1,0:T(8,128)(2,1)S(1)}, u32[]{:S(2)}, u32[]{:S(2)}) collective-permute-start(bf16[64,384]{1,0:T(8,128)(2,1)S(1)} %get-tuple-element.22), channel_id=1, source_target_pairs={{0,1},{1,0},{2,3},{3,2},{4,5},{5,4},{6,7},{7,6},{8,9},{9,8},{10,11... | collective-permute-start | bytes 147464 | tf_op jit(solution)/shard_map/ppermute | solution.py:91
  12.0 8.3 %collective-permute-start.4 = (bf16[256,512]{1,0:T(8,128)(2,1)S(1)}, bf16[256,512]{1,0:T(8,128)(2,1)S(1)}, u32[]{:S(2)}, u32[]{:S(2)}) collective-permute-start(bf16[256,512]{1,0:T(8,128)(2,1)S(1)} %stack.1.refs_3_), channel_id=1, source_target_pairs={{0,2},{1,3},{2,0},{3,1},{4,6},{5,7},{6,4},{7,5},{8,10},{9,11},{10,... | collective-permute-start | bytes 786440 | tf_op jit(solution)/shard_map/ppermute | solution.py:91
  13.6 7.6 %collective-permute-start.3 = (bf16[256,512]{1,0:T(8,128)(2,1)S(1)}, bf16[256,512]{1,0:T(8,128)(2,1)S(1)}, u32[]{:S(2)}, u32[]{:S(2)}) collective-permute-start(bf16[256,512]{1,0:T(8,128)(2,1)S(1)} %stack.1.refs_3_), channel_id=1, source_target_pairs={{0,1},{1,0},{2,3},{3,2},{4,5},{5,4},{6,7},{7,6},{8,9},{9,8},{10,11... | collective-permute-start | bytes 786440 | tf_op jit(solution)/shard_map/ppermute | solution.py:91
  16.1 6.5 %collective-permute-start.8 = (bf16[80,256]{1,0:T(8,128)(2,1)S(1)}, bf16[80,256]{1,0:T(8,128)(2,1)S(1)}, u32[]{:S(2)}, u32[]{:S(2)}) collective-permute-start(bf16[80,256]{1,0:T(8,128)(2,1)S(1)} %get-tuple-element.24), channel_id=1, source_target_pairs={{0,8},{1,9},{2,10},{3,11},{4,12},{5,13},{6,14},{7,15},{8,16},{9,17... | collective-permute-start | bytes 122888 | tf_op jit(solution)/shard_map/ppermute | solution.py:91
  16.7 5.9 %collective-permute-start.9 = (bf16[80,256]{1,0:T(8,128)(2,1)S(1)}, bf16[80,256]{1,0:T(8,128)(2,1)S(1)}, u32[]{:S(2)}, u32[]{:S(2)}) collective-permute-start(bf16[80,256]{1,0:T(8,128)(2,1)S(1)} %get-tuple-element.25), channel_id=1, source_target_pairs={{0,16},{1,17},{2,18},{3,19},{4,20},{5,21},{6,22},{7,23},{8,24},{9,... | collective-permute-start | bytes 122888 | tf_op jit(solution)/shard_map/ppermute | solution.py:91
  18.7 4.0 %collective-permute-start.10 = (bf16[80,256]{1,0:T(8,128)(2,1)S(1)}, bf16[80,256]{1,0:T(8,128)(2,1)S(1)}, u32[]{:S(2)}, u32[]{:S(2)}) collective-permute-start(bf16[80,256]{1,0:T(8,128)(2,1)S(1)} %get-tuple-element.26), channel_id=1, source_target_pairs={{0,24},{1,25},{2,26},{3,27},{4,28},{5,29},{6,30},{7,31},{8,0},{9,1... | collective-permute-start | bytes 122888 | tf_op jit(solution)/shard_map/ppermute | solution.py:91
  20.3 5.1 %collective-permute-start.13 = (bf16[128,512]{1,0:T(8,128)(2,1)S(1)}, bf16[128,512]{1,0:T(8,128)(2,1)S(1)}, u32[]{:S(2)}, u32[]{:S(2)}) collective-permute-start(bf16[128,512]{1,0:T(8,128)(2,1)S(1)} %last.1.refs_1_), channel_id=1, source_target_pairs={{0,1},{1,0},{2,3},{3,2},{4,5},{5,4},{6,7},{7,6},{8,9},{9,8},{10,11... | collective-permute-start | bytes 393224 | tf_op jit(solution)/shard_map/ppermute | solution.py:91
  21.2 5.0 %collective-permute-start.12 = (bf16[128,512]{1,0:T(8,128)(2,1)S(1)}, bf16[128,512]{1,0:T(8,128)(2,1)S(1)}, u32[]{:S(2)}, u32[]{:S(2)}) collective-permute-start(bf16[128,512]{1,0:T(8,128)(2,1)S(1)} %first.1.refs_0_), channel_id=1, source_target_pairs={{0,2},{1,3},{2,0},{3,1},{4,6},{5,7},{6,4},{7,5},{8,10},{9,11},{10,... | collective-permute-start | bytes 393224 | tf_op jit(solution)/shard_map/ppermute | solution.py:91
  24.2 3.1 %collective-permute-start.11 = (bf16[768,512]{1,0:T(8,128)(2,1)S(1)}, bf16[768,512]{1,0:T(8,128)(2,1)S(1)}, u32[]{:S(2)}, u32[]{:S(2)}) collective-permute-start(bf16[768,512]{1,0:T(8,128)(2,1)S(1)} %get-tuple-element.28), channel_id=1, source_target_pairs={{0,4},{1,5},{2,6},{3,7},{4,0},{5,1},{6,2},{7,3},{8,12},{9,13},{10,... | collective-permute-start | bytes 2359304 | tf_op jit(solution)/shard_map/ppermute | solution.py:91
  26.3 1.8 %collective-permute-start.14 = (bf16[304,512]{1,0:T(8,128)(2,1)S(1)}, bf16[304,512]{1,0:T(8,128)(2,1)S(1)}, u32[]{:S(2)}, u32[]{:S(2)}) collective-permute-start(bf16[304,512]{1,0:T(8,128)(2,1)S(1)} %join.1.joined_ref), channel_id=1, source_target_pairs={{0,4},{1,5},{2,6},{3,7},{4,0},{5,1},{6,2},{7,3},{8,12},{9,13},{10,... | collective-permute-start | bytes 933896 | tf_op jit(solution)/shard_map/ppermute | solution.py:91

commit v23 on v22

--- a/solution.py
+++ b/solution.py
@@ -256,7 +256,7 @@
         low_ref[:, start:stop] = (total - high.astype(f32)).astype(bf16)
 
 
-def turn_kernel(factor_ref, out_ref):
+def turn_kernel(factor_ref, earlier_ref, out_ref):
     turned = factor_ref[...].T
     high = turned.astype(jnp.bfloat16)
     out_ref[0, :, :] = high
@@ -442,23 +442,15 @@
 
     rows_to_y, rows_to_x = cut(first_kernel, by_x, "first"), cut(last_kernel, by_y, "last")
     across_y, across_x = shift(rows_to_y, 0, 2), shift(rows_to_x, 0, 1)
-    turned = pl.pallas_call(
-        turn_kernel,
-        out_shape=shaped((2, *factor_inverse.shape), bf16),
-        in_specs=[vmem],
-        out_specs=vmem,
-        compiler_params=params,
-        name="turn",
-    )(factor)
     count = per_owner * slab_width
     depth = layers * rows
     sizes = (layers, owners, per_owner, block_count, block_rows)
     result = shaped((count, panel_width), f32)
     panels = [column, by_x, by_y]
     own, other = pl.pallas_call(
-        functools.partial(near_kernel, sizes, 3),
+        functools.partial(near_kernel, sizes, 2),
         out_shape=[result, shaped((count, panel_width), bf16)],
-        in_specs=[anywhere] * 3 + [vmem] * (len(panels) + layers),
+        in_specs=[anywhere] * 2 + [vmem] * (len(panels) + layers),
         out_specs=[vmem] * 2,
         scratch_shapes=[
             pltpu.VMEM((count, (owners - 1) * depth), bf16),
@@ -467,8 +459,16 @@
         compiler_params=params,
         cost_estimate=lasting(10**9),
         name="near",
-    )(rows_to_y, rows_to_x, turned, *panels, *posts)
+    )(rows_to_y, rows_to_x, *panels, *posts)
     other = shift(other, 0, 0, 1)
+    turned = pl.pallas_call(
+        turn_kernel,
+        out_shape=shaped((2, *factor_inverse.shape), bf16),
+        in_specs=[vmem, anywhere],
+        out_specs=vmem,
+        compiler_params=params,
+        name="turn",
+    )(factor, own)
     own = pl.pallas_call(
         own_kernel,
         out_shape=result,

time: 30.2 us -> 30.2 us (level)
  transfers between devices with their start and end apart: 15 -> 15, of which waited for: 5 -> 6; matrix products, arithmetic and copies ran while one was open for 0% -> 0% of each run, Pallas kernels for 16% -> 16%
where the time goes in v23:
time: 30.2 us; the launch traced here: 30 us
  starting transfers between devices  19.7 us (65%)
  Pallas kernels  8.08 us (27%)
  waiting for transfers between devices  2.13 us (7%)
    ppermute x15, starting transfers between devices, shift(): return lax.ppermute(value, ('rows', 'cols'), pairs)  19.7 us
    ppermute x15, waiting for transfers between devices, shift(): return lax.ppermute(value, ('rows', 'cols'), pairs)  2.13 us
    pallas_call x1, Pallas kernels, local(): pl.pallas_call(functools.partial(final_kernel, sizes), out_shape=result,...  1.87 us
    pallas_call x1, Pallas kernels, local(): pl.pallas_call(functools.partial(near_kernel, sizes, 2), out_shape=[resul...  1.45 us
    pallas_call x1, Pallas kernels, local(): pl.pallas_call(functools.partial(pack_kernel, sizes), out_shape=[shaped((...  1.42 us
    pallas_call x1, Pallas kernels, local(): pl.pallas_call(own_kernel, out_shape=result, in_specs=[vmem] * 2, out_spe...  1.08 us
    pallas_call x1, Pallas kernels, local(): pl.pallas_call(functools.partial(far_kernel, sizes), out_shape=result, in...  0.9 us
    pallas_call x1, Pallas kernels, local(): pl.pallas_call(middle_kernel, out_shape=result, in_specs=[vmem] * 4, out_...  0.78 us
  transfers between devices with their start and end apart: 15, of which 6 were waited for; matrix products, arithmetic and copies ran while one was open for 0% of the time, Pallas kernels for 16%

profile of v23, /device:TPU:0, one launch (start us, length us, event | category | flops | bytes accessed | tf_op | source)
XLA Modules:
  0.0 30.0 jit_solution(13791506342572293276)
XLA Ops:
  0.0 1.4 %pack.1 = (bf16[64,512]{1,0:T(8,128)(2,1)S(1)}, bf16[64,384]{1,0:T(8,128)(2,1)S(1)}, bf16[64,384]{1,0:T(8,128)(2,1)S(1)}, bf16[64,384]{1,0:T(8,128)(2,1)S(1)}, b...) custom-call(s32[2,4]{1,0:T(2,128)} %lists_hbm.1, s32[2,4]{1,0:T(2,128)} %masks_hbm.1, s32[96]{0:T(128)} %order_hbm.1, ...), custom_call_target="tpu_custom_call" | custom-call | tf_op jit(solution)/shard_map/pack/pallas_call | solution.py:387
  1.4 3.1 %collective-permute-start.2 = (bf16[64,512]{1,0:T(8,128)(2,1)S(1)}, bf16[64,512]{1,0:T(8,128)(2,1)S(1)}, u32[]{:S(2)}, u32[]{:S(2)}) collective-permute-start(bf16[64,512]{1,0:T(8,128)(2,1)S(1)} %get-tuple-element.17.refs_3_), channel_id=1, source_target_pairs={{0,8},{1,9},{2,10},{3,11},{4,12},{5,13},{6,14},{7,15},{8,16},{9,17... | collective-permute-start | bytes 196616 | tf_op jit(solution)/shard_map/ppermute | solution.py:91
  4.5 2.6 %collective-permute-start.1 = (bf16[64,512]{1,0:T(8,128)(2,1)S(1)}, bf16[64,512]{1,0:T(8,128)(2,1)S(1)}, u32[]{:S(2)}, u32[]{:S(2)}) collective-permute-start(bf16[64,512]{1,0:T(8,128)(2,1)S(1)} %get-tuple-element.17.refs_3_), channel_id=1, source_target_pairs={{0,16},{1,17},{2,18},{3,19},{4,20},{5,21},{6,22},{7,23},{8,24},{9,... | collective-permute-start | bytes 196616 | tf_op jit(solution)/shard_map/ppermute | solution.py:91
  7.1 1.3 %collective-permute-start = (bf16[64,512]{1,0:T(8,128)(2,1)S(1)}, bf16[64,512]{1,0:T(8,128)(2,1)S(1)}, u32[]{:S(2)}, u32[]{:S(2)}) collective-permute-start(bf16[64,512]{1,0:T(8,128)(2,1)S(1)} %get-tuple-element.17.refs_3_), channel_id=1, source_target_pairs={{0,24},{1,25},{2,26},{3,27},{4,28},{5,29},{6,30},{7,31},{8,0},{9,1... | collective-permute-start | bytes 196616 | tf_op jit(solution)/shard_map/ppermute | solution.py:91
  8.4 2.4 %collective-permute-start.5 = (bf16[64,384]{1,0:T(8,128)(2,1)S(1)}, bf16[64,384]{1,0:T(8,128)(2,1)S(1)}, u32[]{:S(2)}, u32[]{:S(2)}) collective-permute-start(bf16[64,384]{1,0:T(8,128)(2,1)S(1)} %get-tuple-element.19), channel_id=1, source_target_pairs={{0,3},{1,2},{2,1},{3,0},{4,7},{5,6},{6,5},{7,4},{8,11},{9,10},{10,... | collective-permute-start | bytes 147464 | tf_op jit(solution)/shard_map/ppermute | solution.py:91
  10.9 0.5 %collective-permute-start.6 = (bf16[64,384]{1,0:T(8,128)(2,1)S(1)}, bf16[64,384]{1,0:T(8,128)(2,1)S(1)}, u32[]{:S(2)}, u32[]{:S(2)}) collective-permute-start(bf16[64,384]{1,0:T(8,128)(2,1)S(1)} %get-tuple-element.20), channel_id=1, source_target_pairs={{0,2},{1,3},{2,0},{3,1},{4,6},{5,7},{6,4},{7,5},{8,10},{9,11},{10,... | collective-permute-start | bytes 147464 | tf_op jit(solution)/shard_map/ppermute | solution.py:91
  11.4 0.5 %collective-permute-start.7 = (bf16[64,384]{1,0:T(8,128)(2,1)S(1)}, bf16[64,384]{1,0:T(8,128)(2,1)S(1)}, u32[]{:S(2)}, u32[]{:S(2)}) collective-permute-start(bf16[64,384]{1,0:T(8,128)(2,1)S(1)} %get-tuple-element.21), channel_id=1, source_target_pairs={{0,1},{1,0},{2,3},{3,2},{4,5},{5,4},{6,7},{7,6},{8,9},{9,8},{10,11... | collective-permute-start | bytes 147464 | tf_op jit(solution)/shard_map/ppermute | solution.py:91
  11.9 0.0 collective-permute-done.1.refs_1_
  11.9 0.0 collective-permute-done.refs_0_
  12.0 1.6 %collective-permute-start.4 = (bf16[256,512]{1,0:T(8,128)(2,1)S(1)}, bf16[256,512]{1,0:T(8,128)(2,1)S(1)}, u32[]{:S(2)}, u32[]{:S(2)}) collective-permute-start(bf16[256,512]{1,0:T(8,128)(2,1)S(1)} %stack.1.refs_2_), channel_id=1, source_target_pairs={{0,2},{1,3},{2,0},{3,1},{4,6},{5,7},{6,4},{7,5},{8,10},{9,11},{10,... | collective-permute-start | bytes 786440 | tf_op jit(solution)/shard_map/ppermute | solution.py:91
  13.6 1.5 %collective-permute-start.3 = (bf16[256,512]{1,0:T(8,128)(2,1)S(1)}, bf16[256,512]{1,0:T(8,128)(2,1)S(1)}, u32[]{:S(2)}, u32[]{:S(2)}) collective-permute-start(bf16[256,512]{1,0:T(8,128)(2,1)S(1)} %stack.1.refs_2_), channel_id=1, source_target_pairs={{0,1},{1,0},{2,3},{3,2},{4,5},{5,4},{6,7},{7,6},{8,9},{9,8},{10,11... | collective-permute-start | bytes 786440 | tf_op jit(solution)/shard_map/ppermute | solution.py:91
  15.0 0.4 %collective-permute-done.6.refs_2_ = bf16[64,384]{1,0:T(8,128)(2,1)S(1)} collective-permute-done((bf16[64,384]{1,0:T(8,128)(2,1)S(1)}, bf16[64,384]{1,0:T(8,128)(2,1)S(1)}, u32[]{:S(2)}, u32[]{:S(2)}) %collective-permute-start.6) | collective-permute-done | bytes 49184 | tf_op jit(solution)/shard_map/ppermute | solution.py:91
  15.4 0.5 %collective-permute-done.7.refs_3_ = bf16[64,384]{1,0:T(8,128)(2,1)S(1)} collective-permute-done((bf16[64,384]{1,0:T(8,128)(2,1)S(1)}, bf16[64,384]{1,0:T(8,128)(2,1)S(1)}, u32[]{:S(2)}, u32[]{:S(2)}) %collective-permute-start.7) | collective-permute-done | bytes 49184 | tf_op jit(solution)/shard_map/ppermute | solution.py:91
  15.9 0.1 sort.1
  16.1 0.6 %collective-permute-start.8 = (bf16[80,256]{1,0:T(8,128)(2,1)S(1)}, bf16[80,256]{1,0:T(8,128)(2,1)S(1)}, u32[]{:S(2)}, u32[]{:S(2)}) collective-permute-start(bf16[80,256]{1,0:T(8,128)(2,1)S(1)} %get-tuple-element.23), channel_id=1, source_target_pairs={{0,8},{1,9},{2,10},{3,11},{4,12},{5,13},{6,14},{7,15},{8,16},{9,17... | collective-permute-start | bytes 122888 | tf_op jit(solution)/shard_map/ppermute | solution.py:91
  16.7 2.0 %collective-permute-start.9 = (bf16[80,256]{1,0:T(8,128)(2,1)S(1)}, bf16[80,256]{1,0:T(8,128)(2,1)S(1)}, u32[]{:S(2)}, u32[]{:S(2)}) collective-permute-start(bf16[80,256]{1,0:T(8,128)(2,1)S(1)} %get-tuple-element.24), channel_id=1, source_target_pairs={{0,16},{1,17},{2,18},{3,19},{4,20},{5,21},{6,22},{7,23},{8,24},{9,... | collective-permute-start | bytes 122888 | tf_op jit(solution)/shard_map/ppermute | solution.py:91
  18.7 1.2 %collective-permute-start.10 = (bf16[80,256]{1,0:T(8,128)(2,1)S(1)}, bf16[80,256]{1,0:T(8,128)(2,1)S(1)}, u32[]{:S(2)}, u32[]{:S(2)}) collective-permute-start(bf16[80,256]{1,0:T(8,128)(2,1)S(1)} %get-tuple-element.25), channel_id=1, source_target_pairs={{0,24},{1,25},{2,26},{3,27},{4,28},{5,29},{6,30},{7,31},{8,0},{9,1... | collective-permute-start | bytes 122888 | tf_op jit(solution)/shard_map/ppermute | solution.py:91
  19.9 0.3 collective-permute-done.4.in_ref.refs_4_
  20.2 1.0 %collective-permute-start.13 = (bf16[128,512]{1,0:T(8,128)(2,1)S(1)}, bf16[128,512]{1,0:T(8,128)(2,1)S(1)}, u32[]{:S(2)}, u32[]{:S(2)}) collective-permute-start(bf16[128,512]{1,0:T(8,128)(2,1)S(1)} %last.1.refs_1_), channel_id=1, source_target_pairs={{0,1},{1,0},{2,3},{3,2},{4,5},{5,4},{6,7},{7,6},{8,9},{9,8},{10,11... | collective-permute-start | bytes 393224 | tf_op jit(solution)/shard_map/ppermute | solution.py:91
  21.2 1.1 %collective-permute-start.12 = (bf16[128,512]{1,0:T(8,128)(2,1)S(1)}, bf16[128,512]{1,0:T(8,128)(2,1)S(1)}, u32[]{:S(2)}, u32[]{:S(2)}) collective-permute-start(bf16[128,512]{1,0:T(8,128)(2,1)S(1)} %first.1.refs_0_), channel_id=1, source_target_pairs={{0,2},{1,3},{2,0},{3,1},{4,6},{5,7},{6,4},{7,5},{8,10},{9,11},{10,... | collective-permute-start | bytes 393224 | tf_op jit(solution)/shard_map/ppermute | solution.py:91
  22.3 0.2 collective-permute-done.9.refs_7_.refs_2_
  22.6 0.2 collective-permute-done.10.refs_8_.refs_3_
  22.7 1.4 %near.1 = (f32[768,512]{1,0:T(8,128)S(1)}, bf16[768,512]{1,0:T(8,128)(2,1)S(1)}) custom-call(bf16[128,512]{1,0:T(8,128)(2,1)S(1)} %first.1.refs_0_, bf16[128,512]{1,0:T(8,128)(2,1)S(1)} %last.1.refs_1_, bf16[256,512]{1,0:T(8,128)(2,1)S(1)} %stack.1.refs_2_, bf16[256,512]{1,0:T(8,128)(2,1)S(1)} %collective-permute-done.3.in_ref.refs_3_, ...), custom_call_target="tpu_custom_call" | custom-call | flops 1000000000 | tf_op jit(solution)/shard_map/near/pallas_call | solution.py:450
  24.2 0.1 collective-permute-start.11
  24.3 0.3 %turn.1.turned_ref = bf16[2,512,512]{2,1,0:T(8,128)(2,1)S(1)} custom-call(f32[512,512]{1,0:T(8,128)S(1)} %get-tuple-element.27.factor_ref, f32[768,512]{1,0:T(8,128)S(1)} %get-tuple-element.26.earlier_ref.own_ref), custom_call_target="tpu_custom_call" | custom-call | tf_op jit(solution)/shard_map/turn/pallas_call | solution.py:464
  24.6 1.1 %own.1.refs_4_.own_ref = f32[768,512]{1,0:T(8,128)S(1)} custom-call(f32[768,512]{1,0:T(8,128)S(1)} %get-tuple-element.26.earlier_ref.own_ref, bf16[2,512,512]{2,1,0:T(8,128)(2,1)S(1)} %turn.1.turned_ref), custom_call_target="tpu_custom_call" | custom-call | flops 1000000000 | tf_op jit(solution)/shard_map/own/pallas_call | solution.py:472
  25.7 0.5 %collective-permute-done.12.above_ref = bf16[128,512]{1,0:T(8,128)(2,1)S(1)} collective-permute-done((bf16[128,512]{1,0:T(8,128)(2,1)S(1)}, bf16[128,512]{1,0:T(8,128)(2,1)S(1)}, u32[]{:S(2)}, u32[]{:S(2)}) %collective-permute-start.12) | collective-permute-done | bytes 131104 | tf_op jit(solution)/shard_map/ppermute | solution.py:91
  26.2 0.1 join.1.joined_ref
  26.3 0.1 collective-permute-start.14
  26.4 0.9 %far.1.far_ref = f32[768,512]{1,0:T(8,128)S(1)} custom-call(bf16[304,512]{1,0:T(8,128)(2,1)S(1)} %join.1.joined_ref, bf16[2,512,512]{2,1,0:T(8,128)(2,1)S(1)} %turn.1.turned_ref), custom_call_target="tpu_custom_call" | custom-call | tf_op jit(solution)/shard_map/far/pallas_call | solution.py:492
  27.3 0.8 %middle.1.middle_ref = f32[768,512]{1,0:T(8,128)S(1)} custom-call(f32[768,512]{1,0:T(8,128)S(1)} %own.1.refs_4_.own_ref, bf16[768,512]{1,0:T(8,128)(2,1)S(1)} %collective-permute-done.11.other_ref, f32[768,512]{1,0:T(8,128)S(1)} %far.1.far_ref, bf16[2,512,512]{2,1,0:T(8,128)(2,1)S(1)} %turn.1.turned_ref), custom_call_target="tpu_custom_call" | custom-call | tf_op jit(solution)/shard_map/middle/pallas_call | solution.py:501
  28.1 1.9 %final.1 = f32[768,512]{1,0:T(8,128)} custom-call(f32[768,512]{1,0:T(8,128)S(1)} %middle.1.middle_ref, bf16[304,512]{1,0:T(8,128)(2,1)S(1)} %collective-permute-done.14.joined_ref, bf16[2,512,512]{2,1,0:T(8,128)(2,1)S(1)} %turn.1.turned_ref), custom_call_target="tpu_custom_call" | custom-call | tf_op jit(solution)/shard_map/final/pallas_call | solution.py:509
  (10 shorter events, 0.1 us)
Async XLA Ops:
  1.4 10.0 %collective-permute-start.2 = (bf16[64,512]{1,0:T(8,128)(2,1)S(1)}, bf16[64,512]{1,0:T(8,128)(2,1)S(1)}, u32[]{:S(2)}, u32[]{:S(2)}) collective-permute-start(bf16[64,512]{1,0:T(8,128)(2,1)S(1)} %get-tuple-element.17.refs_3_), channel_id=1, source_target_pairs={{0,8},{1,9},{2,10},{3,11},{4,12},{5,13},{6,14},{7,15},{8,16},{9,17... | collective-permute-start | bytes 196616 | tf_op jit(solution)/shard_map/ppermute | solution.py:91
  4.5 7.4 %collective-permute-start.1 = (bf16[64,512]{1,0:T(8,128)(2,1)S(1)}, bf16[64,512]{1,0:T(8,128)(2,1)S(1)}, u32[]{:S(2)}, u32[]{:S(2)}) collective-permute-start(bf16[64,512]{1,0:T(8,128)(2,1)S(1)} %get-tuple-element.17.refs_3_), channel_id=1, source_target_pairs={{0,16},{1,17},{2,18},{3,19},{4,20},{5,21},{6,22},{7,23},{8,24},{9,... | collective-permute-start | bytes 196616 | tf_op jit(solution)/shard_map/ppermute | solution.py:91
  7.1 4.8 %collective-permute-start = (bf16[64,512]{1,0:T(8,128)(2,1)S(1)}, bf16[64,512]{1,0:T(8,128)(2,1)S(1)}, u32[]{:S(2)}, u32[]{:S(2)}) collective-permute-start(bf16[64,512]{1,0:T(8,128)(2,1)S(1)} %get-tuple-element.17.refs_3_), channel_id=1, source_target_pairs={{0,24},{1,25},{2,26},{3,27},{4,28},{5,29},{6,30},{7,31},{8,0},{9,1... | collective-permute-start | bytes 196616 | tf_op jit(solution)/shard_map/ppermute | solution.py:91
  8.4 6.6 %collective-permute-start.5 = (bf16[64,384]{1,0:T(8,128)(2,1)S(1)}, bf16[64,384]{1,0:T(8,128)(2,1)S(1)}, u32[]{:S(2)}, u32[]{:S(2)}) collective-permute-start(bf16[64,384]{1,0:T(8,128)(2,1)S(1)} %get-tuple-element.19), channel_id=1, source_target_pairs={{0,3},{1,2},{2,1},{3,0},{4,7},{5,6},{6,5},{7,4},{8,11},{9,10},{10,... | collective-permute-start | bytes 147464 | tf_op jit(solution)/shard_map/ppermute | solution.py:91
  10.9 4.5 %collective-permute-start.6 = (bf16[64,384]{1,0:T(8,128)(2,1)S(1)}, bf16[64,384]{1,0:T(8,128)(2,1)S(1)}, u32[]{:S(2)}, u32[]{:S(2)}) collective-permute-start(bf16[64,384]{1,0:T(8,128)(2,1)S(1)} %get-tuple-element.20), channel_id=1, source_target_pairs={{0,2},{1,3},{2,0},{3,1},{4,6},{5,7},{6,4},{7,5},{8,10},{9,11},{10,... | collective-permute-start | bytes 147464 | tf_op jit(solution)/shard_map/ppermute | solution.py:91
  11.4 4.5 %collective-permute-start.7 = (bf16[64,384]{1,0:T(8,128)(2,1)S(1)}, bf16[64,384]{1,0:T(8,128)(2,1)S(1)}, u32[]{:S(2)}, u32[]{:S(2)}) collective-permute-start(bf16[64,384]{1,0:T(8,128)(2,1)S(1)} %get-tuple-element.21), channel_id=1, source_target_pairs={{0,1},{1,0},{2,3},{3,2},{4,5},{5,4},{6,7},{7,6},{8,9},{9,8},{10,11... | collective-permute-start | bytes 147464 | tf_op jit(solution)/shard_map/ppermute | solution.py:91
  12.0 8.3 %collective-permute-start.4 = (bf16[256,512]{1,0:T(8,128)(2,1)S(1)}, bf16[256,512]{1,0:T(8,128)(2,1)S(1)}, u32[]{:S(2)}, u32[]{:S(2)}) collective-permute-start(bf16[256,512]{1,0:T(8,128)(2,1)S(1)} %stack.1.refs_2_), channel_id=1, source_target_pairs={{0,2},{1,3},{2,0},{3,1},{4,6},{5,7},{6,4},{7,5},{8,10},{9,11},{10,... | collective-permute-start | bytes 786440 | tf_op jit(solution)/shard_map/ppermute | solution.py:91
  13.6 7.6 %collective-permute-start.3 = (bf16[256,512]{1,0:T(8,128)(2,1)S(1)}, bf16[256,512]{1,0:T(8,128)(2,1)S(1)}, u32[]{:S(2)}, u32[]{:S(2)}) collective-permute-start(bf16[256,512]{1,0:T(8,128)(2,1)S(1)} %stack.1.refs_2_), channel_id=1, source_target_pairs={{0,1},{1,0},{2,3},{3,2},{4,5},{5,4},{6,7},{7,6},{8,9},{9,8},{10,11... | collective-permute-start | bytes 786440 | tf_op jit(solution)/shard_map/ppermute | solution.py:91
  16.1 6.3 %collective-permute-start.8 = (bf16[80,256]{1,0:T(8,128)(2,1)S(1)}, bf16[80,256]{1,0:T(8,128)(2,1)S(1)}, u32[]{:S(2)}, u32[]{:S(2)}) collective-permute-start(bf16[80,256]{1,0:T(8,128)(2,1)S(1)} %get-tuple-element.23), channel_id=1, source_target_pairs={{0,8},{1,9},{2,10},{3,11},{4,12},{5,13},{6,14},{7,15},{8,16},{9,17... | collective-permute-start | bytes 122888 | tf_op jit(solution)/shard_map/ppermute | solution.py:91
  16.7 5.9 %collective-permute-start.9 = (bf16[80,256]{1,0:T(8,128)(2,1)S(1)}, bf16[80,256]{1,0:T(8,128)(2,1)S(1)}, u32[]{:S(2)}, u32[]{:S(2)}) collective-permute-start(bf16[80,256]{1,0:T(8,128)(2,1)S(1)} %get-tuple-element.24), channel_id=1, source_target_pairs={{0,16},{1,17},{2,18},{3,19},{4,20},{5,21},{6,22},{7,23},{8,24},{9,... | collective-permute-start | bytes 122888 | tf_op jit(solution)/shard_map/ppermute | solution.py:91
  18.7 4.0 %collective-permute-start.10 = (bf16[80,256]{1,0:T(8,128)(2,1)S(1)}, bf16[80,256]{1,0:T(8,128)(2,1)S(1)}, u32[]{:S(2)}, u32[]{:S(2)}) collective-permute-start(bf16[80,256]{1,0:T(8,128)(2,1)S(1)} %get-tuple-element.25), channel_id=1, source_target_pairs={{0,24},{1,25},{2,26},{3,27},{4,28},{5,29},{6,30},{7,31},{8,0},{9,1... | collective-permute-start | bytes 122888 | tf_op jit(solution)/shard_map/ppermute | solution.py:91
  20.2 5.5 %collective-permute-start.13 = (bf16[128,512]{1,0:T(8,128)(2,1)S(1)}, bf16[128,512]{1,0:T(8,128)(2,1)S(1)}, u32[]{:S(2)}, u32[]{:S(2)}) collective-permute-start(bf16[128,512]{1,0:T(8,128)(2,1)S(1)} %last.1.refs_1_), channel_id=1, source_target_pairs={{0,1},{1,0},{2,3},{3,2},{4,5},{5,4},{6,7},{7,6},{8,9},{9,8},{10,11... | collective-permute-start | bytes 393224 | tf_op jit(solution)/shard_map/ppermute | solution.py:91
  21.2 5.0 %collective-permute-start.12 = (bf16[128,512]{1,0:T(8,128)(2,1)S(1)}, bf16[128,512]{1,0:T(8,128)(2,1)S(1)}, u32[]{:S(2)}, u32[]{:S(2)}) collective-permute-start(bf16[128,512]{1,0:T(8,128)(2,1)S(1)} %first.1.refs_0_), channel_id=1, source_target_pairs={{0,2},{1,3},{2,0},{3,1},{4,6},{5,7},{6,4},{7,5},{8,10},{9,11},{10,... | collective-permute-start | bytes 393224 | tf_op jit(solution)/shard_map/ppermute | solution.py:91
  24.2 3.1 %collective-permute-start.11 = (bf16[768,512]{1,0:T(8,128)(2,1)S(1)}, bf16[768,512]{1,0:T(8,128)(2,1)S(1)}, u32[]{:S(2)}, u32[]{:S(2)}) collective-permute-start(bf16[768,512]{1,0:T(8,128)(2,1)S(1)} %get-tuple-element.28), channel_id=1, source_target_pairs={{0,4},{1,5},{2,6},{3,7},{4,0},{5,1},{6,2},{7,3},{8,12},{9,13},{10,... | collective-permute-start | bytes 2359304 | tf_op jit(solution)/shard_map/ppermute | solution.py:91
  26.3 1.8 %collective-permute-start.14 = (bf16[304,512]{1,0:T(8,128)(2,1)S(1)}, bf16[304,512]{1,0:T(8,128)(2,1)S(1)}, u32[]{:S(2)}, u32[]{:S(2)}) collective-permute-start(bf16[304,512]{1,0:T(8,128)(2,1)S(1)} %join.1.joined_ref), channel_id=1, source_target_pairs={{0,4},{1,5},{2,6},{3,7},{4,0},{5,1},{6,2},{7,3},{8,12},{9,13},{10,... | collective-permute-start | bytes 933896 | tf_op jit(solution)/shard_map/ppermute | solution.py:91

commit v24 on v22

--- a/solution.py
+++ b/solution.py
@@ -511,7 +511,7 @@
         out_shape=result,
         in_specs=[vmem] * 3,
         out_specs=anywhere,
-        scratch_shapes=[pltpu.VMEM((count, panel_width), f32)] + far_scratch + [pltpu.SemaphoreType.DMA((4,))],
+        scratch_shapes=[pltpu.VMEM((count, panel_width), f32)] + far_scratch + [pltpu.SemaphoreType.DMA((6,))],
         compiler_params=params,
         name="final",
     )(middle, other_joined, turned)

time: 30.2 us -> 30.2 us (level)
  no operation moved by 1% of the time
where the time goes in v24:
time: 30.2 us; the launch traced here: 30 us
  starting transfers between devices  19.8 us (66%)
  Pallas kernels  8.09 us (27%)
  waiting for transfers between devices  2 us (7%)
    ppermute x15, starting transfers between devices, shift(): return lax.ppermute(value, ('rows', 'cols'), pairs)  19.8 us
    ppermute x15, waiting for transfers between devices, shift(): return lax.ppermute(value, ('rows', 'cols'), pairs)  2 us
    pallas_call x1, Pallas kernels, local(): pl.pallas_call(functools.partial(final_kernel, sizes), out_shape=result,...  1.88 us
    pallas_call x1, Pallas kernels, local(): pl.pallas_call(functools.partial(near_kernel, sizes, 3), out_shape=[resul...  1.45 us
    pallas_call x1, Pallas kernels, local(): pl.pallas_call(functools.partial(pack_kernel, sizes), out_shape=[shaped((...  1.42 us
    pallas_call x1, Pallas kernels, local(): pl.pallas_call(own_kernel, out_shape=result, in_specs=[vmem] * 2, out_spe...  1.08 us
    pallas_call x1, Pallas kernels, local(): pl.pallas_call(functools.partial(far_kernel, sizes), out_shape=result, in...  0.9 us
    pallas_call x1, Pallas kernels, local(): pl.pallas_call(middle_kernel, out_shape=result, in_specs=[vmem] * 4, out_...  0.77 us
  transfers between devices with their start and end apart: 15, of which 5 were waited for; matrix products, arithmetic and copies ran while one was open for 0% of the time, Pallas kernels for 16%

profile of v24, /device:TPU:0, one launch (start us, length us, event | category | flops | bytes accessed | tf_op | source)
XLA Modules:
  0.0 30.0 jit_solution(9754062868664863722)
XLA Ops:
  0.0 1.4 %pack.1 = (bf16[64,512]{1,0:T(8,128)(2,1)S(1)}, bf16[64,384]{1,0:T(8,128)(2,1)S(1)}, bf16[64,384]{1,0:T(8,128)(2,1)S(1)}, bf16[64,384]{1,0:T(8,128)(2,1)S(1)}, b...) custom-call(s32[2,4]{1,0:T(2,128)} %lists_hbm.1, s32[2,4]{1,0:T(2,128)} %masks_hbm.1, s32[96]{0:T(128)} %order_hbm.1, ...), custom_call_target="tpu_custom_call" | custom-call | tf_op jit(solution)/shard_map/pack/pallas_call | solution.py:387
  1.4 3.1 %collective-permute-start.2 = (bf16[64,512]{1,0:T(8,128)(2,1)S(1)}, bf16[64,512]{1,0:T(8,128)(2,1)S(1)}, u32[]{:S(2)}, u32[]{:S(2)}) collective-permute-start(bf16[64,512]{1,0:T(8,128)(2,1)S(1)} %get-tuple-element.17.refs_3_), channel_id=1, source_target_pairs={{0,8},{1,9},{2,10},{3,11},{4,12},{5,13},{6,14},{7,15},{8,16},{9,17... | collective-permute-start | bytes 196616 | tf_op jit(solution)/shard_map/ppermute | solution.py:91
  4.5 2.6 %collective-permute-start.1 = (bf16[64,512]{1,0:T(8,128)(2,1)S(1)}, bf16[64,512]{1,0:T(8,128)(2,1)S(1)}, u32[]{:S(2)}, u32[]{:S(2)}) collective-permute-start(bf16[64,512]{1,0:T(8,128)(2,1)S(1)} %get-tuple-element.17.refs_3_), channel_id=1, source_target_pairs={{0,16},{1,17},{2,18},{3,19},{4,20},{5,21},{6,22},{7,23},{8,24},{9,... | collective-permute-start | bytes 196616 | tf_op jit(solution)/shard_map/ppermute | solution.py:91
  7.1 1.3 %collective-permute-start = (bf16[64,512]{1,0:T(8,128)(2,1)S(1)}, bf16[64,512]{1,0:T(8,128)(2,1)S(1)}, u32[]{:S(2)}, u32[]{:S(2)}) collective-permute-start(bf16[64,512]{1,0:T(8,128)(2,1)S(1)} %get-tuple-element.17.refs_3_), channel_id=1, source_target_pairs={{0,24},{1,25},{2,26},{3,27},{4,28},{5,29},{6,30},{7,31},{8,0},{9,1... | collective-permute-start | bytes 196616 | tf_op jit(solution)/shard_map/ppermute | solution.py:91
  8.4 2.4 %collective-permute-start.5 = (bf16[64,384]{1,0:T(8,128)(2,1)S(1)}, bf16[64,384]{1,0:T(8,128)(2,1)S(1)}, u32[]{:S(2)}, u32[]{:S(2)}) collective-permute-start(bf16[64,384]{1,0:T(8,128)(2,1)S(1)} %get-tuple-element.20), channel_id=1, source_target_pairs={{0,3},{1,2},{2,1},{3,0},{4,7},{5,6},{6,5},{7,4},{8,11},{9,10},{10,... | collective-permute-start | bytes 147464 | tf_op jit(solution)/shard_map/ppermute | solution.py:91
  10.9 0.5 %collective-permute-start.6 = (bf16[64,384]{1,0:T(8,128)(2,1)S(1)}, bf16[64,384]{1,0:T(8,128)(2,1)S(1)}, u32[]{:S(2)}, u32[]{:S(2)}) collective-permute-start(bf16[64,384]{1,0:T(8,128)(2,1)S(1)} %get-tuple-element.21), channel_id=1, source_target_pairs={{0,2},{1,3},{2,0},{3,1},{4,6},{5,7},{6,4},{7,5},{8,10},{9,11},{10,... | collective-permute-start | bytes 147464 | tf_op jit(solution)/shard_map/ppermute | solution.py:91
  11.4 0.5 %collective-permute-start.7 = (bf16[64,384]{1,0:T(8,128)(2,1)S(1)}, bf16[64,384]{1,0:T(8,128)(2,1)S(1)}, u32[]{:S(2)}, u32[]{:S(2)}) collective-permute-start(bf16[64,384]{1,0:T(8,128)(2,1)S(1)} %get-tuple-element.22), channel_id=1, source_target_pairs={{0,1},{1,0},{2,3},{3,2},{4,5},{5,4},{6,7},{7,6},{8,9},{9,8},{10,11... | collective-permute-start | bytes 147464 | tf_op jit(solution)/shard_map/ppermute | solution.py:91
  11.9 0.0 collective-permute-done.1.refs_1_
  11.9 0.0 collective-permute-done.refs_0_
  12.0 1.6 %collective-permute-start.4 = (bf16[256,512]{1,0:T(8,128)(2,1)S(1)}, bf16[256,512]{1,0:T(8,128)(2,1)S(1)}, u32[]{:S(2)}, u32[]{:S(2)}) collective-permute-start(bf16[256,512]{1,0:T(8,128)(2,1)S(1)} %stack.1.refs_3_), channel_id=1, source_target_pairs={{0,2},{1,3},{2,0},{3,1},{4,6},{5,7},{6,4},{7,5},{8,10},{9,11},{10,... | collective-permute-start | bytes 786440 | tf_op jit(solution)/shard_map/ppermute | solution.py:91
  13.6 1.5 %collective-permute-start.3 = (bf16[256,512]{1,0:T(8,128)(2,1)S(1)}, bf16[256,512]{1,0:T(8,128)(2,1)S(1)}, u32[]{:S(2)}, u32[]{:S(2)}) collective-permute-start(bf16[256,512]{1,0:T(8,128)(2,1)S(1)} %stack.1.refs_3_), channel_id=1, source_target_pairs={{0,1},{1,0},{2,3},{3,2},{4,5},{5,4},{6,7},{7,6},{8,9},{9,8},{10,11... | collective-permute-start | bytes 786440 | tf_op jit(solution)/shard_map/ppermute | solution.py:91
  15.0 0.4 %collective-permute-done.6.refs_2_ = bf16[64,384]{1,0:T(8,128)(2,1)S(1)} collective-permute-done((bf16[64,384]{1,0:T(8,128)(2,1)S(1)}, bf16[64,384]{1,0:T(8,128)(2,1)S(1)}, u32[]{:S(2)}, u32[]{:S(2)}) %collective-permute-start.6) | collective-permute-done | bytes 49184 | tf_op jit(solution)/shard_map/ppermute | solution.py:91
  15.4 0.5 %collective-permute-done.7.refs_3_ = bf16[64,384]{1,0:T(8,128)(2,1)S(1)} collective-permute-done((bf16[64,384]{1,0:T(8,128)(2,1)S(1)}, bf16[64,384]{1,0:T(8,128)(2,1)S(1)}, u32[]{:S(2)}, u32[]{:S(2)}) %collective-permute-start.7) | collective-permute-done | bytes 49184 | tf_op jit(solution)/shard_map/ppermute | solution.py:91
  15.9 0.1 sort.1
  16.1 0.6 %collective-permute-start.8 = (bf16[80,256]{1,0:T(8,128)(2,1)S(1)}, bf16[80,256]{1,0:T(8,128)(2,1)S(1)}, u32[]{:S(2)}, u32[]{:S(2)}) collective-permute-start(bf16[80,256]{1,0:T(8,128)(2,1)S(1)} %get-tuple-element.24), channel_id=1, source_target_pairs={{0,8},{1,9},{2,10},{3,11},{4,12},{5,13},{6,14},{7,15},{8,16},{9,17... | collective-permute-start | bytes 122888 | tf_op jit(solution)/shard_map/ppermute | solution.py:91
  16.7 2.0 %collective-permute-start.9 = (bf16[80,256]{1,0:T(8,128)(2,1)S(1)}, bf16[80,256]{1,0:T(8,128)(2,1)S(1)}, u32[]{:S(2)}, u32[]{:S(2)}) collective-permute-start(bf16[80,256]{1,0:T(8,128)(2,1)S(1)} %get-tuple-element.25), channel_id=1, source_target_pairs={{0,16},{1,17},{2,18},{3,19},{4,20},{5,21},{6,22},{7,23},{8,24},{9,... | collective-permute-start | bytes 122888 | tf_op jit(solution)/shard_map/ppermute | solution.py:91
  18.7 1.2 %collective-permute-start.10 = (bf16[80,256]{1,0:T(8,128)(2,1)S(1)}, bf16[80,256]{1,0:T(8,128)(2,1)S(1)}, u32[]{:S(2)}, u32[]{:S(2)}) collective-permute-start(bf16[80,256]{1,0:T(8,128)(2,1)S(1)} %get-tuple-element.26), channel_id=1, source_target_pairs={{0,24},{1,25},{2,26},{3,27},{4,28},{5,29},{6,30},{7,31},{8,0},{9,1... | collective-permute-start | bytes 122888 | tf_op jit(solution)/shard_map/ppermute | solution.py:91
  19.9 0.3 %turn.1.refs_2_.turned_ref = bf16[2,512,512]{2,1,0:T(8,128)(2,1)S(1)} custom-call(f32[512,512]{1,0:T(8,128)S(1)} %get-tuple-element.18.factor_ref), custom_call_target="tpu_custom_call" | custom-call | tf_op jit(solution)/shard_map/turn/pallas_call | solution.py:445
  20.3 0.0 collective-permute-done.4.in_ref.refs_5_
  20.3 0.9 %collective-permute-start.13 = (bf16[128,512]{1,0:T(8,128)(2,1)S(1)}, bf16[128,512]{1,0:T(8,128)(2,1)S(1)}, u32[]{:S(2)}, u32[]{:S(2)}) collective-permute-start(bf16[128,512]{1,0:T(8,128)(2,1)S(1)} %last.1.refs_1_), channel_id=1, source_target_pairs={{0,1},{1,0},{2,3},{3,2},{4,5},{5,4},{6,7},{7,6},{8,9},{9,8},{10,11... | collective-permute-start | bytes 393224 | tf_op jit(solution)/shard_map/ppermute | solution.py:91
  21.2 1.3 %collective-permute-start.12 = (bf16[128,512]{1,0:T(8,128)(2,1)S(1)}, bf16[128,512]{1,0:T(8,128)(2,1)S(1)}, u32[]{:S(2)}, u32[]{:S(2)}) collective-permute-start(bf16[128,512]{1,0:T(8,128)(2,1)S(1)} %first.1.refs_0_), channel_id=1, source_target_pairs={{0,2},{1,3},{2,0},{3,1},{4,6},{5,7},{6,4},{7,5},{8,10},{9,11},{10,... | collective-permute-start | bytes 393224 | tf_op jit(solution)/shard_map/ppermute | solution.py:91
  22.5 0.1 collective-permute-done.9.refs_8_.refs_2_
  22.6 0.2 collective-permute-done.10.refs_9_.refs_3_
  22.7 1.4 %near.1 = (f32[768,512]{1,0:T(8,128)S(1)}, bf16[768,512]{1,0:T(8,128)(2,1)S(1)}) custom-call(bf16[128,512]{1,0:T(8,128)(2,1)S(1)} %first.1.refs_0_, bf16[128,512]{1,0:T(8,128)(2,1)S(1)} %last.1.refs_1_, bf16[2,512,512]{2,1,0:T(8,128)(2,1)S(1)} %turn.1.refs_2_.turned_ref, bf16[256,512]{1,0:T(8,128)(2,1)S(1)} %stack.1.refs_3_, ...), custom_call_target="tpu_custom_call" | custom-call | flops 1000000000 | tf_op jit(solution)/shard_map/near/pallas_call | solution.py:458
  24.2 0.1 collective-permute-start.11
  24.3 1.1 %own.1.refs_4_.own_ref = f32[768,512]{1,0:T(8,128)S(1)} custom-call(f32[768,512]{1,0:T(8,128)S(1)} %get-tuple-element.27.own_ref, bf16[2,512,512]{2,1,0:T(8,128)(2,1)S(1)} %turn.1.refs_2_.turned_ref), custom_call_target="tpu_custom_call" | custom-call | flops 1000000000 | tf_op jit(solution)/shard_map/own/pallas_call | solution.py:472
  25.4 0.9 %collective-permute-done.12.above_ref = bf16[128,512]{1,0:T(8,128)(2,1)S(1)} collective-permute-done((bf16[128,512]{1,0:T(8,128)(2,1)S(1)}, bf16[128,512]{1,0:T(8,128)(2,1)S(1)}, u32[]{:S(2)}, u32[]{:S(2)}) %collective-permute-start.12) | collective-permute-done | bytes 131104 | tf_op jit(solution)/shard_map/ppermute | solution.py:91
  26.2 0.1 join.1.joined_ref
  26.3 0.1 collective-permute-start.14
  26.4 0.9 %far.1.far_ref = f32[768,512]{1,0:T(8,128)S(1)} custom-call(bf16[304,512]{1,0:T(8,128)(2,1)S(1)} %join.1.joined_ref, bf16[2,512,512]{2,1,0:T(8,128)(2,1)S(1)} %turn.1.refs_2_.turned_ref), custom_call_target="tpu_custom_call" | custom-call | tf_op jit(solution)/shard_map/far/pallas_call | solution.py:492
  27.3 0.8 %middle.1.middle_ref = f32[768,512]{1,0:T(8,128)S(1)} custom-call(f32[768,512]{1,0:T(8,128)S(1)} %own.1.refs_4_.own_ref, bf16[768,512]{1,0:T(8,128)(2,1)S(1)} %collective-permute-done.11.other_ref, f32[768,512]{1,0:T(8,128)S(1)} %far.1.far_ref, bf16[2,512,512]{2,1,0:T(8,128)(2,1)S(1)} %turn.1.refs_2_.turned_ref), custom_call_target="tpu_custom_call" | custom-call | tf_op jit(solution)/shard_map/middle/pallas_call | solution.py:501
  28.1 1.9 %final.1 = f32[768,512]{1,0:T(8,128)} custom-call(f32[768,512]{1,0:T(8,128)S(1)} %middle.1.middle_ref, bf16[304,512]{1,0:T(8,128)(2,1)S(1)} %collective-permute-done.14.joined_ref, bf16[2,512,512]{2,1,0:T(8,128)(2,1)S(1)} %turn.1.refs_2_.turned_ref), custom_call_target="tpu_custom_call" | custom-call | tf_op jit(solution)/shard_map/final/pallas_call | solution.py:509
  (10 shorter events, 0.1 us)
Async XLA Ops:
  1.4 10.0 %collective-permute-start.2 = (bf16[64,512]{1,0:T(8,128)(2,1)S(1)}, bf16[64,512]{1,0:T(8,128)(2,1)S(1)}, u32[]{:S(2)}, u32[]{:S(2)}) collective-permute-start(bf16[64,512]{1,0:T(8,128)(2,1)S(1)} %get-tuple-element.17.refs_3_), channel_id=1, source_target_pairs={{0,8},{1,9},{2,10},{3,11},{4,12},{5,13},{6,14},{7,15},{8,16},{9,17... | collective-permute-start | bytes 196616 | tf_op jit(solution)/shard_map/ppermute | solution.py:91
  4.5 7.4 %collective-permute-start.1 = (bf16[64,512]{1,0:T(8,128)(2,1)S(1)}, bf16[64,512]{1,0:T(8,128)(2,1)S(1)}, u32[]{:S(2)}, u32[]{:S(2)}) collective-permute-start(bf16[64,512]{1,0:T(8,128)(2,1)S(1)} %get-tuple-element.17.refs_3_), channel_id=1, source_target_pairs={{0,16},{1,17},{2,18},{3,19},{4,20},{5,21},{6,22},{7,23},{8,24},{9,... | collective-permute-start | bytes 196616 | tf_op jit(solution)/shard_map/ppermute | solution.py:91
  7.1 4.8 %collective-permute-start = (bf16[64,512]{1,0:T(8,128)(2,1)S(1)}, bf16[64,512]{1,0:T(8,128)(2,1)S(1)}, u32[]{:S(2)}, u32[]{:S(2)}) collective-permute-start(bf16[64,512]{1,0:T(8,128)(2,1)S(1)} %get-tuple-element.17.refs_3_), channel_id=1, source_target_pairs={{0,24},{1,25},{2,26},{3,27},{4,28},{5,29},{6,30},{7,31},{8,0},{9,1... | collective-permute-start | bytes 196616 | tf_op jit(solution)/shard_map/ppermute | solution.py:91
  8.4 6.6 %collective-permute-start.5 = (bf16[64,384]{1,0:T(8,128)(2,1)S(1)}, bf16[64,384]{1,0:T(8,128)(2,1)S(1)}, u32[]{:S(2)}, u32[]{:S(2)}) collective-permute-start(bf16[64,384]{1,0:T(8,128)(2,1)S(1)} %get-tuple-element.20), channel_id=1, source_target_pairs={{0,3},{1,2},{2,1},{3,0},{4,7},{5,6},{6,5},{7,4},{8,11},{9,10},{10,... | collective-permute-start | bytes 147464 | tf_op jit(solution)/shard_map/ppermute | solution.py:91
  10.9 4.5 %collective-permute-start.6 = (bf16[64,384]{1,0:T(8,128)(2,1)S(1)}, bf16[64,384]{1,0:T(8,128)(2,1)S(1)}, u32[]{:S(2)}, u32[]{:S(2)}) collective-permute-start(bf16[64,384]{1,0:T(8,128)(2,1)S(1)} %get-tuple-element.21), channel_id=1, source_target_pairs={{0,2},{1,3},{2,0},{3,1},{4,6},{5,7},{6,4},{7,5},{8,10},{9,11},{10,... | collective-permute-start | bytes 147464 | tf_op jit(solution)/shard_map/ppermute | solution.py:91
  11.4 4.5 %collective-permute-start.7 = (bf16[64,384]{1,0:T(8,128)(2,1)S(1)}, bf16[64,384]{1,0:T(8,128)(2,1)S(1)}, u32[]{:S(2)}, u32[]{:S(2)}) collective-permute-start(bf16[64,384]{1,0:T(8,128)(2,1)S(1)} %get-tuple-element.22), channel_id=1, source_target_pairs={{0,1},{1,0},{2,3},{3,2},{4,5},{5,4},{6,7},{7,6},{8,9},{9,8},{10,11... | collective-permute-start | bytes 147464 | tf_op jit(solution)/shard_map/ppermute | solution.py:91
  12.0 8.3 %collective-permute-start.4 = (bf16[256,512]{1,0:T(8,128)(2,1)S(1)}, bf16[256,512]{1,0:T(8,128)(2,1)S(1)}, u32[]{:S(2)}, u32[]{:S(2)}) collective-permute-start(bf16[256,512]{1,0:T(8,128)(2,1)S(1)} %stack.1.refs_3_), channel_id=1, source_target_pairs={{0,2},{1,3},{2,0},{3,1},{4,6},{5,7},{6,4},{7,5},{8,10},{9,11},{10,... | collective-permute-start | bytes 786440 | tf_op jit(solution)/shard_map/ppermute | solution.py:91
  13.6 7.7 %collective-permute-start.3 = (bf16[256,512]{1,0:T(8,128)(2,1)S(1)}, bf16[256,512]{1,0:T(8,128)(2,1)S(1)}, u32[]{:S(2)}, u32[]{:S(2)}) collective-permute-start(bf16[256,512]{1,0:T(8,128)(2,1)S(1)} %stack.1.refs_3_), channel_id=1, source_target_pairs={{0,1},{1,0},{2,3},{3,2},{4,5},{5,4},{6,7},{7,6},{8,9},{9,8},{10,11... | collective-permute-start | bytes 786440 | tf_op jit(solution)/shard_map/ppermute | solution.py:91
  16.1 6.5 %collective-permute-start.8 = (bf16[80,256]{1,0:T(8,128)(2,1)S(1)}, bf16[80,256]{1,0:T(8,128)(2,1)S(1)}, u32[]{:S(2)}, u32[]{:S(2)}) collective-permute-start(bf16[80,256]{1,0:T(8,128)(2,1)S(1)} %get-tuple-element.24), channel_id=1, source_target_pairs={{0,8},{1,9},{2,10},{3,11},{4,12},{5,13},{6,14},{7,15},{8,16},{9,17... | collective-permute-start | bytes 122888 | tf_op jit(solution)/shard_map/ppermute | solution.py:91
  16.7 5.9 %collective-permute-start.9 = (bf16[80,256]{1,0:T(8,128)(2,1)S(1)}, bf16[80,256]{1,0:T(8,128)(2,1)S(1)}, u32[]{:S(2)}, u32[]{:S(2)}) collective-permute-start(bf16[80,256]{1,0:T(8,128)(2,1)S(1)} %get-tuple-element.25), channel_id=1, source_target_pairs={{0,16},{1,17},{2,18},{3,19},{4,20},{5,21},{6,22},{7,23},{8,24},{9,... | collective-permute-start | bytes 122888 | tf_op jit(solution)/shard_map/ppermute | solution.py:91
  18.7 4.0 %collective-permute-start.10 = (bf16[80,256]{1,0:T(8,128)(2,1)S(1)}, bf16[80,256]{1,0:T(8,128)(2,1)S(1)}, u32[]{:S(2)}, u32[]{:S(2)}) collective-permute-start(bf16[80,256]{1,0:T(8,128)(2,1)S(1)} %get-tuple-element.26), channel_id=1, source_target_pairs={{0,24},{1,25},{2,26},{3,27},{4,28},{5,29},{6,30},{7,31},{8,0},{9,1... | collective-permute-start | bytes 122888 | tf_op jit(solution)/shard_map/ppermute | solution.py:91
  20.3 5.1 %collective-permute-start.13 = (bf16[128,512]{1,0:T(8,128)(2,1)S(1)}, bf16[128,512]{1,0:T(8,128)(2,1)S(1)}, u32[]{:S(2)}, u32[]{:S(2)}) collective-permute-start(bf16[128,512]{1,0:T(8,128)(2,1)S(1)} %last.1.refs_1_), channel_id=1, source_target_pairs={{0,1},{1,0},{2,3},{3,2},{4,5},{5,4},{6,7},{7,6},{8,9},{9,8},{10,11... | collective-permute-start | bytes 393224 | tf_op jit(solution)/shard_map/ppermute | solution.py:91
  21.2 5.0 %collective-permute-start.12 = (bf16[128,512]{1,0:T(8,128)(2,1)S(1)}, bf16[128,512]{1,0:T(8,128)(2,1)S(1)}, u32[]{:S(2)}, u32[]{:S(2)}) collective-permute-start(bf16[128,512]{1,0:T(8,128)(2,1)S(1)} %first.1.refs_0_), channel_id=1, source_target_pairs={{0,2},{1,3},{2,0},{3,1},{4,6},{5,7},{6,4},{7,5},{8,10},{9,11},{10,... | collective-permute-start | bytes 393224 | tf_op jit(solution)/shard_map/ppermute | solution.py:91
  24.2 3.1 %collective-permute-start.11 = (bf16[768,512]{1,0:T(8,128)(2,1)S(1)}, bf16[768,512]{1,0:T(8,128)(2,1)S(1)}, u32[]{:S(2)}, u32[]{:S(2)}) collective-permute-start(bf16[768,512]{1,0:T(8,128)(2,1)S(1)} %get-tuple-element.28), channel_id=1, source_target_pairs={{0,4},{1,5},{2,6},{3,7},{4,0},{5,1},{6,2},{7,3},{8,12},{9,13},{10,... | collective-permute-start | bytes 2359304 | tf_op jit(solution)/shard_map/ppermute | solution.py:91
  26.3 1.8 %collective-permute-start.14 = (bf16[304,512]{1,0:T(8,128)(2,1)S(1)}, bf16[304,512]{1,0:T(8,128)(2,1)S(1)}, u32[]{:S(2)}, u32[]{:S(2)}) collective-permute-start(bf16[304,512]{1,0:T(8,128)(2,1)S(1)} %join.1.joined_ref), channel_id=1, source_target_pairs={{0,4},{1,5},{2,6},{3,7},{4,0},{5,1},{6,2},{7,3},{8,12},{9,13},{10,... | collective-permute-start | bytes 933896 | tf_op jit(solution)/shard_map/ppermute | solution.py:91

commit v25 on v22

--- a/solution.py
+++ b/solution.py
@@ -198,11 +198,11 @@
     return block.astype(jnp.bfloat16)
 
 
-def stack_kernel(*refs):
-    inputs, out_ref = refs[:-1], refs[-1]
-    rows = inputs[0].shape[0]
-    for i, ref in enumerate(reversed(inputs)):
-        out_ref[i * rows : (i + 1) * rows, :] = ref[...]
+def stack_kernel(places, *refs):
+    out_ref = refs[-1]
+    for place_of, ref in zip(places, refs):
+        rows = ref.shape[0]
+        out_ref[place_of * rows : (place_of + 1) * rows, :] = ref[...]
 
 
 def sort_kernel(sizes, *refs):
@@ -409,14 +409,14 @@
     parcels = [parcels[0]] + [shift(parcels[e], 0, e) for e in range(1, owners)]
 
     column = pl.pallas_call(
-        stack_kernel,
+        functools.partial(stack_kernel, (3, 1, 2, 0)),
         out_shape=shaped((layers * rows, panel_width), bf16),
         in_specs=[vmem] * layers,
         out_specs=vmem,
         compiler_params=params,
         cost_estimate=lasting(10**10),
         name="stack",
-    )(*reversed(line), weighted)
+    )(line[2], line[0], line[1], weighted)
     posts = pl.pallas_call(
         functools.partial(sort_kernel, (layers, owners, lane_group)),
         out_shape=[shaped((rows + 16, owners * lane_group), bf16)] * layers,

time: 30.2 us -> 30.9 us (1.023)
  starting transfers between devices: 19.8 us -> 20.7 us
    ppermute x15, starting transfers between devices: 19.8 us -> 20.7 us  [shift(): return lax.ppermute(value, ('rows', 'cols'), pairs)]
  transfers between devices with their start and end apart: 15 -> 15, of which waited for: 5 -> 4; matrix products, arithmetic and copies ran while one was open for 0% -> 0% of each run, Pallas kernels for 16% -> 16%
where the time goes in v25:
time: 30.9 us; the launch traced here: 30.7 us
  starting transfers between devices  20.7 us (67%)
  Pallas kernels  8.07 us (26%)
  waiting for transfers between devices  1.82 us (6%)
    ppermute x15, starting transfers between devices, shift(): return lax.ppermute(value, ('rows', 'cols'), pairs)  20.7 us
    pallas_call x1, Pallas kernels, local(): pl.pallas_call(functools.partial(final_kernel, sizes), out_shape=result,...  1.86 us
    ppermute x15, waiting for transfers between devices, shift(): return lax.ppermute(value, ('rows', 'cols'), pairs)  1.82 us
    pallas_call x1, Pallas kernels, local(): pl.pallas_call(functools.partial(near_kernel, sizes, 3), out_shape=[resul...  1.45 us
    pallas_call x1, Pallas kernels, local(): pl.pallas_call(functools.partial(pack_kernel, sizes), out_shape=[shaped((...  1.42 us
    pallas_call x1, Pallas kernels, local(): pl.pallas_call(own_kernel, out_shape=result, in_specs=[vmem] * 2, out_spe...  1.08 us
    pallas_call x1, Pallas kernels, local(): pl.pallas_call(functools.partial(far_kernel, sizes), out_shape=result, in...  0.9 us
    pallas_call x1, Pallas kernels, local(): pl.pallas_call(middle_kernel, out_shape=result, in_specs=[vmem] * 4, out_...  0.77 us
  transfers between devices with their start and end apart: 15, of which 4 were waited for; matrix products, arithmetic and copies ran while one was open for 0% of the time, Pallas kernels for 16%

profile of v25, /device:TPU:0, one launch (start us, length us, event | category | flops | bytes accessed | tf_op | source)
XLA Modules:
  0.0 30.7 jit_solution(1444242935279748953)
XLA Ops:
  0.0 1.4 %pack.1 = (bf16[64,512]{1,0:T(8,128)(2,1)S(1)}, bf16[64,384]{1,0:T(8,128)(2,1)S(1)}, bf16[64,384]{1,0:T(8,128)(2,1)S(1)}, bf16[64,384]{1,0:T(8,128)(2,1)S(1)}, b...) custom-call(s32[2,4]{1,0:T(2,128)} %lists_hbm.1, s32[2,4]{1,0:T(2,128)} %masks_hbm.1, s32[96]{0:T(128)} %order_hbm.1, ...), custom_call_target="tpu_custom_call" | custom-call | tf_op jit(solution)/shard_map/pack/pallas_call | solution.py:387
  1.4 4.1 %collective-permute-start.2 = (bf16[64,512]{1,0:T(8,128)(2,1)S(1)}, bf16[64,512]{1,0:T(8,128)(2,1)S(1)}, u32[]{:S(2)}, u32[]{:S(2)}) collective-permute-start(bf16[64,512]{1,0:T(8,128)(2,1)S(1)} %get-tuple-element.17.refs_3_), channel_id=1, source_target_pairs={{0,16},{1,17},{2,18},{3,19},{4,20},{5,21},{6,22},{7,23},{8,24},{9,... | collective-permute-start | bytes 196616 | tf_op jit(solution)/shard_map/ppermute | solution.py:91
  5.5 1.6 %collective-permute-start.1 = (bf16[64,512]{1,0:T(8,128)(2,1)S(1)}, bf16[64,512]{1,0:T(8,128)(2,1)S(1)}, u32[]{:S(2)}, u32[]{:S(2)}) collective-permute-start(bf16[64,512]{1,0:T(8,128)(2,1)S(1)} %get-tuple-element.17.refs_3_), channel_id=1, source_target_pairs={{0,8},{1,9},{2,10},{3,11},{4,12},{5,13},{6,14},{7,15},{8,16},{9,17... | collective-permute-start | bytes 196616 | tf_op jit(solution)/shard_map/ppermute | solution.py:91
  7.1 2.2 %collective-permute-start = (bf16[64,512]{1,0:T(8,128)(2,1)S(1)}, bf16[64,512]{1,0:T(8,128)(2,1)S(1)}, u32[]{:S(2)}, u32[]{:S(2)}) collective-permute-start(bf16[64,512]{1,0:T(8,128)(2,1)S(1)} %get-tuple-element.17.refs_3_), channel_id=1, source_target_pairs={{0,24},{1,25},{2,26},{3,27},{4,28},{5,29},{6,30},{7,31},{8,0},{9,1... | collective-permute-start | bytes 196616 | tf_op jit(solution)/shard_map/ppermute | solution.py:91
  9.4 2.4 %collective-permute-start.5 = (bf16[64,384]{1,0:T(8,128)(2,1)S(1)}, bf16[64,384]{1,0:T(8,128)(2,1)S(1)}, u32[]{:S(2)}, u32[]{:S(2)}) collective-permute-start(bf16[64,384]{1,0:T(8,128)(2,1)S(1)} %get-tuple-element.20), channel_id=1, source_target_pairs={{0,3},{1,2},{2,1},{3,0},{4,7},{5,6},{6,5},{7,4},{8,11},{9,10},{10,... | collective-permute-start | bytes 147464 | tf_op jit(solution)/shard_map/ppermute | solution.py:91
  11.8 0.5 %collective-permute-start.6 = (bf16[64,384]{1,0:T(8,128)(2,1)S(1)}, bf16[64,384]{1,0:T(8,128)(2,1)S(1)}, u32[]{:S(2)}, u32[]{:S(2)}) collective-permute-start(bf16[64,384]{1,0:T(8,128)(2,1)S(1)} %get-tuple-element.21), channel_id=1, source_target_pairs={{0,2},{1,3},{2,0},{3,1},{4,6},{5,7},{6,4},{7,5},{8,10},{9,11},{10,... | collective-permute-start | bytes 147464 | tf_op jit(solution)/shard_map/ppermute | solution.py:91
  12.3 0.0 collective-permute-done.2.refs_2_
  12.3 0.5 %collective-permute-start.7 = (bf16[64,384]{1,0:T(8,128)(2,1)S(1)}, bf16[64,384]{1,0:T(8,128)(2,1)S(1)}, u32[]{:S(2)}, u32[]{:S(2)}) collective-permute-start(bf16[64,384]{1,0:T(8,128)(2,1)S(1)} %get-tuple-element.22), channel_id=1, source_target_pairs={{0,1},{1,0},{2,3},{3,2},{4,5},{5,4},{6,7},{7,6},{8,9},{9,8},{10,11... | collective-permute-start | bytes 147464 | tf_op jit(solution)/shard_map/ppermute | solution.py:91
  12.9 1.6 %collective-permute-start.4 = (bf16[256,512]{1,0:T(8,128)(2,1)S(1)}, bf16[256,512]{1,0:T(8,128)(2,1)S(1)}, u32[]{:S(2)}, u32[]{:S(2)}) collective-permute-start(bf16[256,512]{1,0:T(8,128)(2,1)S(1)} %stack.1.refs_3_), channel_id=1, source_target_pairs={{0,2},{1,3},{2,0},{3,1},{4,6},{5,7},{6,4},{7,5},{8,10},{9,11},{10,... | collective-permute-start | bytes 786440 | tf_op jit(solution)/shard_map/ppermute | solution.py:91
  14.5 1.5 %collective-permute-start.3 = (bf16[256,512]{1,0:T(8,128)(2,1)S(1)}, bf16[256,512]{1,0:T(8,128)(2,1)S(1)}, u32[]{:S(2)}, u32[]{:S(2)}) collective-permute-start(bf16[256,512]{1,0:T(8,128)(2,1)S(1)} %stack.1.refs_3_), channel_id=1, source_target_pairs={{0,1},{1,0},{2,3},{3,2},{4,5},{5,4},{6,7},{7,6},{8,9},{9,8},{10,11... | collective-permute-start | bytes 786440 | tf_op jit(solution)/shard_map/ppermute | solution.py:91
  16.0 0.0 collective-permute-done.5.refs_1_
  16.0 0.5 %collective-permute-done.6.refs_2_ = bf16[64,384]{1,0:T(8,128)(2,1)S(1)} collective-permute-done((bf16[64,384]{1,0:T(8,128)(2,1)S(1)}, bf16[64,384]{1,0:T(8,128)(2,1)S(1)}, u32[]{:S(2)}, u32[]{:S(2)}) %collective-permute-start.6) | collective-permute-done | bytes 49184 | tf_op jit(solution)/shard_map/ppermute | solution.py:91
  16.5 0.4 %collective-permute-done.7.refs_3_ = bf16[64,384]{1,0:T(8,128)(2,1)S(1)} collective-permute-done((bf16[64,384]{1,0:T(8,128)(2,1)S(1)}, bf16[64,384]{1,0:T(8,128)(2,1)S(1)}, u32[]{:S(2)}, u32[]{:S(2)}) %collective-permute-start.7) | collective-permute-done | bytes 49184 | tf_op jit(solution)/shard_map/ppermute | solution.py:91
  16.9 0.1 sort.1
  17.0 0.1 collective-permute-start.8
  17.1 2.2 %collective-permute-start.9 = (bf16[80,256]{1,0:T(8,128)(2,1)S(1)}, bf16[80,256]{1,0:T(8,128)(2,1)S(1)}, u32[]{:S(2)}, u32[]{:S(2)}) collective-permute-start(bf16[80,256]{1,0:T(8,128)(2,1)S(1)} %get-tuple-element.25), channel_id=1, source_target_pairs={{0,16},{1,17},{2,18},{3,19},{4,20},{5,21},{6,22},{7,23},{8,24},{9,... | collective-permute-start | bytes 122888 | tf_op jit(solution)/shard_map/ppermute | solution.py:91
  19.3 1.6 %collective-permute-start.10 = (bf16[80,256]{1,0:T(8,128)(2,1)S(1)}, bf16[80,256]{1,0:T(8,128)(2,1)S(1)}, u32[]{:S(2)}, u32[]{:S(2)}) collective-permute-start(bf16[80,256]{1,0:T(8,128)(2,1)S(1)} %get-tuple-element.26), channel_id=1, source_target_pairs={{0,24},{1,25},{2,26},{3,27},{4,28},{5,29},{6,30},{7,31},{8,0},{9,1... | collective-permute-start | bytes 122888 | tf_op jit(solution)/shard_map/ppermute | solution.py:91
  20.9 0.3 %turn.1.refs_2_.turned_ref = bf16[2,512,512]{2,1,0:T(8,128)(2,1)S(1)} custom-call(f32[512,512]{1,0:T(8,128)S(1)} %get-tuple-element.18.factor_ref), custom_call_target="tpu_custom_call" | custom-call | tf_op jit(solution)/shard_map/turn/pallas_call | solution.py:445
  21.3 0.0 collective-permute-done.4.in_ref.refs_5_
  21.3 0.6 %collective-permute-start.13 = (bf16[128,512]{1,0:T(8,128)(2,1)S(1)}, bf16[128,512]{1,0:T(8,128)(2,1)S(1)}, u32[]{:S(2)}, u32[]{:S(2)}) collective-permute-start(bf16[128,512]{1,0:T(8,128)(2,1)S(1)} %last.1.refs_1_), channel_id=1, source_target_pairs={{0,1},{1,0},{2,3},{3,2},{4,5},{5,4},{6,7},{7,6},{8,9},{9,8},{10,11... | collective-permute-start | bytes 393224 | tf_op jit(solution)/shard_map/ppermute | solution.py:91
  21.9 0.0 collective-permute-done.3.in_ref.refs_4_
  21.9 1.6 %collective-permute-start.12 = (bf16[128,512]{1,0:T(8,128)(2,1)S(1)}, bf16[128,512]{1,0:T(8,128)(2,1)S(1)}, u32[]{:S(2)}, u32[]{:S(2)}) collective-permute-start(bf16[128,512]{1,0:T(8,128)(2,1)S(1)} %first.1.refs_0_), channel_id=1, source_target_pairs={{0,2},{1,3},{2,0},{3,1},{4,6},{5,7},{6,4},{7,5},{8,10},{9,11},{10,... | collective-permute-start | bytes 393224 | tf_op jit(solution)/shard_map/ppermute | solution.py:91
  23.5 1.5 %near.1 = (f32[768,512]{1,0:T(8,128)S(1)}, bf16[768,512]{1,0:T(8,128)(2,1)S(1)}) custom-call(bf16[128,512]{1,0:T(8,128)(2,1)S(1)} %first.1.refs_0_, bf16[128,512]{1,0:T(8,128)(2,1)S(1)} %last.1.refs_1_, bf16[2,512,512]{2,1,0:T(8,128)(2,1)S(1)} %turn.1.refs_2_.turned_ref, bf16[256,512]{1,0:T(8,128)(2,1)S(1)} %stack.1.refs_3_, ...), custom_call_target="tpu_custom_call" | custom-call | flops 1000000000 | tf_op jit(solution)/shard_map/near/pallas_call | solution.py:458
  25.0 0.1 collective-permute-start.11
  25.1 1.1 %own.1.refs_4_.own_ref = f32[768,512]{1,0:T(8,128)S(1)} custom-call(f32[768,512]{1,0:T(8,128)S(1)} %get-tuple-element.27.own_ref, bf16[2,512,512]{2,1,0:T(8,128)(2,1)S(1)} %turn.1.refs_2_.turned_ref), custom_call_target="tpu_custom_call" | custom-call | flops 1000000000 | tf_op jit(solution)/shard_map/own/pallas_call | solution.py:472
  26.1 0.2 collective-permute-done.13.below_ref
  26.3 0.6 %collective-permute-done.12.above_ref = bf16[128,512]{1,0:T(8,128)(2,1)S(1)} collective-permute-done((bf16[128,512]{1,0:T(8,128)(2,1)S(1)}, bf16[128,512]{1,0:T(8,128)(2,1)S(1)}, u32[]{:S(2)}, u32[]{:S(2)}) %collective-permute-start.12) | collective-permute-done | bytes 131104 | tf_op jit(solution)/shard_map/ppermute | solution.py:91
  27.0 0.1 join.1.joined_ref
  27.1 0.1 collective-permute-start.14
  27.1 0.9 %far.1.far_ref = f32[768,512]{1,0:T(8,128)S(1)} custom-call(bf16[304,512]{1,0:T(8,128)(2,1)S(1)} %join.1.joined_ref, bf16[2,512,512]{2,1,0:T(8,128)(2,1)S(1)} %turn.1.refs_2_.turned_ref), custom_call_target="tpu_custom_call" | custom-call | tf_op jit(solution)/shard_map/far/pallas_call | solution.py:492
  28.1 0.8 %middle.1.middle_ref = f32[768,512]{1,0:T(8,128)S(1)} custom-call(f32[768,512]{1,0:T(8,128)S(1)} %own.1.refs_4_.own_ref, bf16[768,512]{1,0:T(8,128)(2,1)S(1)} %collective-permute-done.11.other_ref, f32[768,512]{1,0:T(8,128)S(1)} %far.1.far_ref, bf16[2,512,512]{2,1,0:T(8,128)(2,1)S(1)} %turn.1.refs_2_.turned_ref), custom_call_target="tpu_custom_call" | custom-call | tf_op jit(solution)/shard_map/middle/pallas_call | solution.py:501
  28.9 1.9 %final.1 = f32[768,512]{1,0:T(8,128)} custom-call(f32[768,512]{1,0:T(8,128)S(1)} %middle.1.middle_ref, bf16[304,512]{1,0:T(8,128)(2,1)S(1)} %collective-permute-done.14.joined_ref, bf16[2,512,512]{2,1,0:T(8,128)(2,1)S(1)} %turn.1.refs_2_.turned_ref), custom_call_target="tpu_custom_call" | custom-call | tf_op jit(solution)/shard_map/final/pallas_call | solution.py:509
  (10 shorter events, 0.1 us)
Async XLA Ops:
  1.4 10.9 %collective-permute-start.2 = (bf16[64,512]{1,0:T(8,128)(2,1)S(1)}, bf16[64,512]{1,0:T(8,128)(2,1)S(1)}, u32[]{:S(2)}, u32[]{:S(2)}) collective-permute-start(bf16[64,512]{1,0:T(8,128)(2,1)S(1)} %get-tuple-element.17.refs_3_), channel_id=1, source_target_pairs={{0,16},{1,17},{2,18},{3,19},{4,20},{5,21},{6,22},{7,23},{8,24},{9,... | collective-permute-start | bytes 196616 | tf_op jit(solution)/shard_map/ppermute | solution.py:91
  5.5 7.3 %collective-permute-start.1 = (bf16[64,512]{1,0:T(8,128)(2,1)S(1)}, bf16[64,512]{1,0:T(8,128)(2,1)S(1)}, u32[]{:S(2)}, u32[]{:S(2)}) collective-permute-start(bf16[64,512]{1,0:T(8,128)(2,1)S(1)} %get-tuple-element.17.refs_3_), channel_id=1, source_target_pairs={{0,8},{1,9},{2,10},{3,11},{4,12},{5,13},{6,14},{7,15},{8,16},{9,17... | collective-permute-start | bytes 196616 | tf_op jit(solution)/shard_map/ppermute | solution.py:91
  7.1 5.7 %collective-permute-start = (bf16[64,512]{1,0:T(8,128)(2,1)S(1)}, bf16[64,512]{1,0:T(8,128)(2,1)S(1)}, u32[]{:S(2)}, u32[]{:S(2)}) collective-permute-start(bf16[64,512]{1,0:T(8,128)(2,1)S(1)} %get-tuple-element.17.refs_3_), channel_id=1, source_target_pairs={{0,24},{1,25},{2,26},{3,27},{4,28},{5,29},{6,30},{7,31},{8,0},{9,1... | collective-permute-start | bytes 196616 | tf_op jit(solution)/shard_map/ppermute | solution.py:91
  9.4 6.6 %collective-permute-start.5 = (bf16[64,384]{1,0:T(8,128)(2,1)S(1)}, bf16[64,384]{1,0:T(8,128)(2,1)S(1)}, u32[]{:S(2)}, u32[]{:S(2)}) collective-permute-start(bf16[64,384]{1,0:T(8,128)(2,1)S(1)} %get-tuple-element.20), channel_id=1, source_target_pairs={{0,3},{1,2},{2,1},{3,0},{4,7},{5,6},{6,5},{7,4},{8,11},{9,10},{10,... | collective-permute-start | bytes 147464 | tf_op jit(solution)/shard_map/ppermute | solution.py:91
  11.8 4.7 %collective-permute-start.6 = (bf16[64,384]{1,0:T(8,128)(2,1)S(1)}, bf16[64,384]{1,0:T(8,128)(2,1)S(1)}, u32[]{:S(2)}, u32[]{:S(2)}) collective-permute-start(bf16[64,384]{1,0:T(8,128)(2,1)S(1)} %get-tuple-element.21), channel_id=1, source_target_pairs={{0,2},{1,3},{2,0},{3,1},{4,6},{5,7},{6,4},{7,5},{8,10},{9,11},{10,... | collective-permute-start | bytes 147464 | tf_op jit(solution)/shard_map/ppermute | solution.py:91
  12.3 4.6 %collective-permute-start.7 = (bf16[64,384]{1,0:T(8,128)(2,1)S(1)}, bf16[64,384]{1,0:T(8,128)(2,1)S(1)}, u32[]{:S(2)}, u32[]{:S(2)}) collective-permute-start(bf16[64,384]{1,0:T(8,128)(2,1)S(1)} %get-tuple-element.22), channel_id=1, source_target_pairs={{0,1},{1,0},{2,3},{3,2},{4,5},{5,4},{6,7},{7,6},{8,9},{9,8},{10,11... | collective-permute-start | bytes 147464 | tf_op jit(solution)/shard_map/ppermute | solution.py:91
  12.9 8.4 %collective-permute-start.4 = (bf16[256,512]{1,0:T(8,128)(2,1)S(1)}, bf16[256,512]{1,0:T(8,128)(2,1)S(1)}, u32[]{:S(2)}, u32[]{:S(2)}) collective-permute-start(bf16[256,512]{1,0:T(8,128)(2,1)S(1)} %stack.1.refs_3_), channel_id=1, source_target_pairs={{0,2},{1,3},{2,0},{3,1},{4,6},{5,7},{6,4},{7,5},{8,10},{9,11},{10,... | collective-permute-start | bytes 786440 | tf_op jit(solution)/shard_map/ppermute | solution.py:91
  14.5 7.5 %collective-permute-start.3 = (bf16[256,512]{1,0:T(8,128)(2,1)S(1)}, bf16[256,512]{1,0:T(8,128)(2,1)S(1)}, u32[]{:S(2)}, u32[]{:S(2)}) collective-permute-start(bf16[256,512]{1,0:T(8,128)(2,1)S(1)} %stack.1.refs_3_), channel_id=1, source_target_pairs={{0,1},{1,0},{2,3},{3,2},{4,5},{5,4},{6,7},{7,6},{8,9},{9,8},{10,11... | collective-permute-start | bytes 786440 | tf_op jit(solution)/shard_map/ppermute | solution.py:91
  17.0 6.5 %collective-permute-start.8 = (bf16[80,256]{1,0:T(8,128)(2,1)S(1)}, bf16[80,256]{1,0:T(8,128)(2,1)S(1)}, u32[]{:S(2)}, u32[]{:S(2)}) collective-permute-start(bf16[80,256]{1,0:T(8,128)(2,1)S(1)} %get-tuple-element.24), channel_id=1, source_target_pairs={{0,8},{1,9},{2,10},{3,11},{4,12},{5,13},{6,14},{7,15},{8,16},{9,17... | collective-permute-start | bytes 122888 | tf_op jit(solution)/shard_map/ppermute | solution.py:91
  17.1 6.4 %collective-permute-start.9 = (bf16[80,256]{1,0:T(8,128)(2,1)S(1)}, bf16[80,256]{1,0:T(8,128)(2,1)S(1)}, u32[]{:S(2)}, u32[]{:S(2)}) collective-permute-start(bf16[80,256]{1,0:T(8,128)(2,1)S(1)} %get-tuple-element.25), channel_id=1, source_target_pairs={{0,16},{1,17},{2,18},{3,19},{4,20},{5,21},{6,22},{7,23},{8,24},{9,... | collective-permute-start | bytes 122888 | tf_op jit(solution)/shard_map/ppermute | solution.py:91
  19.3 4.2 %collective-permute-start.10 = (bf16[80,256]{1,0:T(8,128)(2,1)S(1)}, bf16[80,256]{1,0:T(8,128)(2,1)S(1)}, u32[]{:S(2)}, u32[]{:S(2)}) collective-permute-start(bf16[80,256]{1,0:T(8,128)(2,1)S(1)} %get-tuple-element.26), channel_id=1, source_target_pairs={{0,24},{1,25},{2,26},{3,27},{4,28},{5,29},{6,30},{7,31},{8,0},{9,1... | collective-permute-start | bytes 122888 | tf_op jit(solution)/shard_map/ppermute | solution.py:91
  21.3 5.0 %collective-permute-start.13 = (bf16[128,512]{1,0:T(8,128)(2,1)S(1)}, bf16[128,512]{1,0:T(8,128)(2,1)S(1)}, u32[]{:S(2)}, u32[]{:S(2)}) collective-permute-start(bf16[128,512]{1,0:T(8,128)(2,1)S(1)} %last.1.refs_1_), channel_id=1, source_target_pairs={{0,1},{1,0},{2,3},{3,2},{4,5},{5,4},{6,7},{7,6},{8,9},{9,8},{10,11... | collective-permute-start | bytes 393224 | tf_op jit(solution)/shard_map/ppermute | solution.py:91
  21.9 5.0 %collective-permute-start.12 = (bf16[128,512]{1,0:T(8,128)(2,1)S(1)}, bf16[128,512]{1,0:T(8,128)(2,1)S(1)}, u32[]{:S(2)}, u32[]{:S(2)}) collective-permute-start(bf16[128,512]{1,0:T(8,128)(2,1)S(1)} %first.1.refs_0_), channel_id=1, source_target_pairs={{0,2},{1,3},{2,0},{3,1},{4,6},{5,7},{6,4},{7,5},{8,10},{9,11},{10,... | collective-permute-start | bytes 393224 | tf_op jit(solution)/shard_map/ppermute | solution.py:91
  25.0 3.1 %collective-permute-start.11 = (bf16[768,512]{1,0:T(8,128)(2,1)S(1)}, bf16[768,512]{1,0:T(8,128)(2,1)S(1)}, u32[]{:S(2)}, u32[]{:S(2)}) collective-permute-start(bf16[768,512]{1,0:T(8,128)(2,1)S(1)} %get-tuple-element.28), channel_id=1, source_target_pairs={{0,4},{1,5},{2,6},{3,7},{4,0},{5,1},{6,2},{7,3},{8,12},{9,13},{10,... | collective-permute-start | bytes 2359304 | tf_op jit(solution)/shard_map/ppermute | solution.py:91
  27.1 1.8 %collective-permute-start.14 = (bf16[304,512]{1,0:T(8,128)(2,1)S(1)}, bf16[304,512]{1,0:T(8,128)(2,1)S(1)}, u32[]{:S(2)}, u32[]{:S(2)}) collective-permute-start(bf16[304,512]{1,0:T(8,128)(2,1)S(1)} %join.1.joined_ref), channel_id=1, source_target_pairs={{0,4},{1,5},{2,6},{3,7},{4,0},{5,1},{6,2},{7,3},{8,12},{9,13},{10,... | collective-permute-start | bytes 933896 | tf_op jit(solution)/shard_map/ppermute | solution.py:91
